TPU v7x, 32 devices: a whole 2x2x4 slice. The times are simulated.
32 devices in a mesh: tx: 4 (over z), ty: 2 (over x), mode: 4 (over y, core).
Axes of the slice: x: 2, y: 2, z: 4, core: 2. Of those that a mesh axis runs over, the one named last changes fastest.
Arguments:
- object_field: float32 [2, 512, 512], P(None, 'tx', 'ty'), may hold values from -5 to 5
- probe: float32 [2, 8, 256, 256], P(None, 'mode'), may hold values from -1.5 to 1.5
- amplitudes: bfloat16 [4, 2, 2, 256, 256], P('tx', 'ty'), may hold values from 0.29882812 to 2.5
- centers: int32 [4, 2, 2, 2], P('tx', 'ty'), may hold values from 0 to 255, as said below
- live: int32 [4, 2], P('tx', 'ty'), may hold values from 1 to 2, as said below
Outputs:
- updated: float32 [2, 512, 512], P(None, 'tx', 'ty')
Inputs may be any that keep to these rules, and one draw needn't show every extreme that they name: `centers`: the first component is under 128, the second under 256; some live slot sits at offsets (127, 255) and some at (0, 0). A tile's positions fill its slots 0 to live - 1; some tile has all 2 slots live and some only one.
All inputs are finite; a program needn't handle non-finite values.
Results may differ from a plain program's by a relative error of at most 0.006.
Values may be sent and summed in bfloat16 or wider, within the bound.
No kernel may reach another device: no remote copies, remote signals or barrier semaphores. Data moves between devices by JAX's collectives and lax.ppermute only.
A program may use at most 64 MiB of HBM per device.

v0:
```python
import math

import jax
import jax.numpy as jnp
from jax import lax
from jax.sharding import PartitionSpec as P

power_floor = 0.01
regularizer = 0.1


def padded_2(block, sides, width):
    for axis, dim in sides:
        count = lax.axis_size(axis)
        forward = [(i, i + 1) for i in range(count - 1)]
        backward = [(target, source) for source, target in forward]
        low = lax.ppermute(
            lax.slice_in_dim(block, block.shape[dim] - width, None, axis=dim), axis, forward
        )
        high = lax.ppermute(lax.slice_in_dim(block, 0, width, axis=dim), axis, backward)
        block = jnp.concatenate([low, block, high], axis=dim)
    return block


def dft_tables(pattern_side):
    index_line = jnp.arange(pattern_side, dtype=jnp.int32)
    product_table = index_line[:, None] * index_line[None, :] % pattern_side
    angle_table = product_table.astype(jnp.float32) * (2.0 * math.pi / pattern_side)
    scaling = 1.0 / math.sqrt(pattern_side)
    table_real = (jnp.cos(angle_table) * scaling).astype(jnp.bfloat16)
    table_imaginary = (-jnp.sin(angle_table) * scaling).astype(jnp.bfloat16)
    return (table_real, table_imaginary)


def left_mult(matrix, signal):
    return jnp.einsum("uv,kvw->kuw", matrix, signal, preferred_element_type=jnp.float32)


def right_mult(signal, matrix):
    return jnp.einsum("kuv,vw->kuw", signal, matrix, preferred_element_type=jnp.float32)


def left_apply(matrix_real, matrix_imaginary, signal_real, signal_imaginary):
    return (
        left_mult(matrix_real, signal_real) - left_mult(matrix_imaginary, signal_imaginary),
        left_mult(matrix_real, signal_imaginary) + left_mult(matrix_imaginary, signal_real),
    )


def right_apply(matrix_real, matrix_imaginary, signal_real, signal_imaginary):
    return (
        right_mult(signal_real, matrix_real) - right_mult(signal_imaginary, matrix_imaginary),
        right_mult(signal_real, matrix_imaginary) + right_mult(signal_imaginary, matrix_real),
    )


def forward_wave(patch, probe_real, probe_imaginary, table_real, table_imaginary):
    patch_real = patch[0].astype(jnp.float32)
    patch_imaginary = patch[1].astype(jnp.float32)
    exit_real = (probe_real * patch_real - probe_imaginary * patch_imaginary).astype(jnp.bfloat16)
    exit_imaginary = (probe_real * patch_imaginary + probe_imaginary * patch_real).astype(
        jnp.bfloat16
    )
    half_real, half_imaginary = left_apply(table_real, table_imaginary, exit_real, exit_imaginary)
    far_real, far_imaginary = right_apply(
        table_real,
        table_imaginary,
        half_real.astype(jnp.bfloat16),
        half_imaginary.astype(jnp.bfloat16),
    )
    return (exit_real, exit_imaginary, far_real, far_imaginary)


def backward_wave(
    far_real,
    far_imaginary,
    power,
    amplitude,
    exit_real,
    exit_imaginary,
    probe_real,
    probe_imaginary,
    table_real,
    table_imaginary,
):
    factor = amplitude.astype(jnp.float32) / jnp.sqrt(power + power_floor)
    fixed_real = (far_real * factor).astype(jnp.bfloat16)
    fixed_imaginary = (far_imaginary * factor).astype(jnp.bfloat16)
    back_half_real, back_half_imaginary = left_apply(
        table_real, -table_imaginary, fixed_real, fixed_imaginary
    )
    back_real, back_imaginary = right_apply(
        table_real,
        -table_imaginary,
        back_half_real.astype(jnp.bfloat16),
        back_half_imaginary.astype(jnp.bfloat16),
    )
    diff_real = back_real - exit_real.astype(jnp.float32)
    diff_imaginary = back_imaginary - exit_imaginary.astype(jnp.float32)
    grad_real = jnp.sum(probe_real * diff_real + probe_imaginary * diff_imaginary, axis=0)
    grad_imaginary = jnp.sum(probe_real * diff_imaginary - probe_imaginary * diff_real, axis=0)
    return (grad_real, grad_imaginary)


def on_device(object_field, probe, amplitudes, centers, live):
    pattern_side = probe.shape[2]
    half_width = pattern_side // 2
    tile_rows = object_field.shape[1]
    tile_cols = object_field.shape[2]
    channels = 3
    table_real, table_imaginary = dft_tables(pattern_side)
    object_low = object_field.astype(jnp.bfloat16)
    padded = padded_2(object_low, (("tx", 1), ("ty", 2)), half_width)
    live_count = live[0, 0]
    anchor = jnp.zeros((), jnp.int32)
    extended = jnp.zeros(
        (channels, tile_rows + pattern_side, tile_cols + pattern_side), jnp.float32
    )

    def place_of(slot_index):
        return (centers[0, 0, slot_index, 0], centers[0, 0, slot_index, 1])

    def patch_of(row_at, col_at):
        return lax.dynamic_slice(padded, (anchor, row_at, col_at), (2, pattern_side, pattern_side))

    def deposit(extended, row_at, col_at, grad_real, grad_imaginary, weight):
        block = jnp.stack([grad_real, grad_imaginary, weight])
        current = lax.dynamic_slice(
            extended, (anchor, row_at, col_at), (channels, pattern_side, pattern_side)
        )
        return lax.dynamic_update_slice(extended, current + block, (anchor, row_at, col_at))

    gathered = lax.all_gather(probe.astype(jnp.bfloat16), "mode", axis=1, tiled=True).astype(
        probe.dtype
    )
    probe_real = gathered[0]
    probe_imaginary = gathered[1]
    weight = jnp.sum(probe_real * probe_real + probe_imaginary * probe_imaginary, axis=0)
    group_size = lax.axis_size("mode")
    member_index = lax.axis_index("mode")
    turn_count = jnp.maximum((live_count - member_index + group_size - 1) // group_size, 0)

    def visit(turn, extended):
        slot_index = member_index + turn * group_size
        row_at, col_at = place_of(slot_index)
        exit_real, exit_imaginary, far_real, far_imaginary = forward_wave(
            patch_of(row_at, col_at), probe_real, probe_imaginary, table_real, table_imaginary
        )
        power = jnp.sum(far_real * far_real + far_imaginary * far_imaginary, axis=0)
        amplitude = lax.dynamic_index_in_dim(amplitudes[0, 0], slot_index, 0, keepdims=False)
        grad_real, grad_imaginary = backward_wave(
            far_real,
            far_imaginary,
            power,
            amplitude,
            exit_real,
            exit_imaginary,
            probe_real,
            probe_imaginary,
            table_real,
            table_imaginary,
        )
        return deposit(extended, row_at, col_at, grad_real, grad_imaginary, weight)

    extended = lax.fori_loop(0, turn_count, visit, extended)
    rows_out = jnp.concatenate(
        [extended[:, :half_width, :], extended[:, tile_rows + half_width :, :]], axis=1
    )
    rows_back = padded_2(rows_out.astype(jnp.bfloat16), (("tx", 1),), half_width).astype(
        rows_out.dtype
    )
    inner = extended[:, half_width : half_width + tile_rows, :]
    inner = inner.at[:, :half_width, :].add(rows_back[:, :half_width, :])
    inner = inner.at[:, tile_rows - half_width :, :].add(rows_back[:, 3 * half_width :, :])
    cols_out = jnp.concatenate(
        [inner[:, :, :half_width], inner[:, :, tile_cols + half_width :]], axis=2
    )
    cols_back = padded_2(cols_out.astype(jnp.bfloat16), (("ty", 2),), half_width).astype(
        cols_out.dtype
    )
    core = inner[:, :, half_width : half_width + tile_cols]
    core = core.at[:, :, :half_width].add(cols_back[:, :, :half_width])
    core = core.at[:, :, tile_cols - half_width :].add(cols_back[:, :, 3 * half_width :])
    summed = lax.psum(core.astype(jnp.bfloat16), "mode").astype(jnp.float32)
    return object_field + summed[:2] / (summed[2] + regularizer)


def solution(mesh):
    return jax.shard_map(
        on_device,
        mesh=mesh,
        in_specs=(
            P(None, "tx", "ty"),
            P(None, "mode", None, None),
            P("tx", "ty", None, None, None),
            P("tx", "ty", None, None),
            P("tx", "ty"),
        ),
        out_specs=P(None, "tx", "ty"),
        check_vma=False,
    )
```

profile of v0, /device:TPU:0, one launch (start us, length us, event | category | flops | bytes accessed | tf_op | source)
XLA Modules:
  0.0 148.6 jit_solution(1797770230737860651)
XLA Ops:
  6.5 2.1 %convert_element_type.160 = bf16[2,2,256,256]{3,2,1,0:T(8,128)(2,1)} convert(f32[2,2,256,256]{3,2,1,0:T(8,128)} %param.20) | non-fusion elementwise | flops 262144 | bytes 1572864 | tf_op jit(solution)/shard_map/convert_element_type | solution.py:133
  10.1 5.6 %collective-permute-start = (bf16[2,128,256]{2,1,0:T(8,128)(2,1)S(1)}, bf16[2,128,256]{2,1,0:T(8,128)(2,1)S(1)}, u32[]{:S(2)}, u32[]{:S(2)}) collective-permute-start(bf16[2,128,256]{2,1,0:T(8,128)(2,1)S(1)} %convert_element_type.159), channel_id=1, source_target_pairs={{0,8},{8,16},{16,24},{1,9},{9,17},{17,25},{2,10},{10,18},{18,26},{... | collective-permute-start | bytes 393224 | tf_op jit(solution)/shard_map/ppermute | solution.py:17
  15.6 1.5 %collective-permute-done.1 = bf16[2,128,256]{2,1,0:T(8,128)(2,1)S(1)} collective-permute-done((bf16[2,128,256]{2,1,0:T(8,128)(2,1)S(1)}, bf16[2,128,256]{2,1,0:T(8,128)(2,1)S(1)}, u32[]{:S(2)}, u32[]{:S(2)}) %collective-permute-start.1) | collective-permute-done | bytes 131104 | tf_op jit(solution)/shard_map/ppermute | solution.py:20
  18.5 3.6 %collective-permute-start.2 = (bf16[2,384,128]{2,1,0:T(8,128)(2,1)S(1)}, bf16[2,384,128]{2,1,0:T(8,128)(2,1)S(1)}, u32[]{:S(2)}, u32[]{:S(2)}) collective-permute-start(bf16[2,384,128]{2,1,0:T(8,128)(2,1)S(1)} %get-tuple-element.336), channel_id=1, source_target_pairs={{0,4},{1,5},{2,6},{3,7},{8,12},{9,13},{10,14},{11,15},{16,20},{17,... | collective-permute-start | bytes 589832 | tf_op jit(solution)/shard_map/ppermute | solution.py:17
  25.3 4.4 %collective-permute-done.3 = bf16[2,384,128]{2,1,0:T(8,128)(2,1)S(1)} collective-permute-done((bf16[2,384,128]{2,1,0:T(8,128)(2,1)S(1)}, bf16[2,384,128]{2,1,0:T(8,128)(2,1)S(1)}, u32[]{:S(2)}, u32[]{:S(2)}) %collective-permute-start.3) | collective-permute-done | bytes 196640 | tf_op jit(solution)/shard_map/ppermute | solution.py:20
  30.6 3.6 %all-gather.2.cloned.1.call-done = bf16[2,8,256,256]{3,2,1,0:T(8,128)(2,1)} async-done(((bf16[2,2,256,256]{3,2,1,0:T(8,128)(2,1)}), bf16[2,8,256,256]{3,2,1,0:T(8,128)(2,1)}) %all-gather.2.cloned.1.call-update) | async-done | bytes 2097168 | tf_op jit(solution)/shard_map/all_gather | solution.py:133
  34.2 2.0 %convert_element_type.161 = f32[2,8,256,256]{3,2,1,0:T(8,128)S(1)} convert(bf16[2,8,256,256]{3,2,1,0:T(8,128)(2,1)} %all-gather.2.cloned.1.call-done) | non-fusion elementwise | flops 1048576 | bytes 6291456 | tf_op jit(solution)/shard_map/convert_element_type | solution.py:133
  36.6 1.7 %slice_bitcast_fusion = (f32[8,256,256]{2,1,0:T(8,128)S(1)}, f32[8,256,256]{2,1,0:T(8,128)}) fusion(f32[2,8,256,256]{3,2,1,0:T(8,128)S(1)} %convert_element_type.161), kind=kLoop, calls=%fused_computation.139 | loop fusion | bytes 8388608 | tf_op jit(solution)/shard_map/squeeze | solution.py:137
  38.3 1.7 %broadcast_in_dim.2 = f32[3,384,512]{2,1,0:T(8,128)} broadcast(f32[]{:T(128)} %constant.186.clone.1), dimensions={} | broadcast | bytes 2359300 | tf_op jit(solution)/shard_map/broadcast_in_dim | solution.py:116
  40.0 42.5 %while.19 = (s32[]{:T(128)}, f32[3,384,512]{2,1,0:T(8,128)}, s32[]{:T(128)}, s32[]{:T(128)}, s32[1,1,2,2]{3,2,1,0:T(2,128)S(1)}, /*index=5*/bf16[2,384,512]{2,1,...) while((s32[]{:T(128)}, f32[3,384,512]{2,1,0:T(8,128)}, ...), condition=%wide.region_5.6_spmd.clone.clone, body=%wide.region_1.5_spmd.clone.clone.sunk | while | flops 4336844800 | bytes 97911152 | solution.py:165
  45.6 2.2 %subtract_convert_fusion.4 = (bf16[8,256,256]{2,1,0:T(8,128)(2,1)S(1)}, bf16[8,256,256]{2,1,0:T(8,128)(2,1)S(1)}) fusion(f32[8,256,256]{2,1,0:T(8,128)S(1)} %get-tuple-element.461, f32[8,256,256]{2,1,0:T(8,128)} %get-tuple-element.460, f32[256,256]{1,0:T(8,128)S(1)} %get-tuple-element.412, f32[256,256]{1,0:T(8,128)S(1)} %get-tuple-element.413), kind=kLoop, calls=%fused_computation.15.clone.1 | loop fusion | flops 4194304 | bytes 6815744 | tf_op jit(solution)/shard_map/while/body/convert_element_type | solution.py:60
  49.2 1.4 fusion.217
  50.6 1.4 fusion.221
  54.8 1.4 fusion.220
  56.2 1.4 convolution_subtract_fusion.2
  57.6 1.7 %add_reduce_fusion.5 = (f32[256,256]{1,0:T(8,128)S(1)}, f32[8,256,256]{2,1,0:T(8,128)S(1)}) fusion(f32[8,256,256]{2,1,0:T(8,128)S(1)} %convolution_subtract_fusion.2, f32[8,256,256]{2,1,0:T(8,128)S(1)} %fusion.221, bf16[8,256,256]{1,2,0:T(8,128)(2,1)S(1)} %fusion.220), kind=kOutput, calls=%fused_computation.11.clone.1 | convolution fusion | flops 272039936 | bytes 7602176 | tf_op jit(solution)/shard_map/while/body/kuv,vw->kuw/dot_general | solution.py:40
  59.3 1.4 fusion.225
  60.8 1.4 fusion.226
  62.2 1.4 fusion.222
  63.7 1.4 fusion.223
  65.1 1.4 fusion.227
  67.9 1.4 convert_subtract_fusion.3
  69.5 2.5 %add_reduce_fusion.6 = (f32[256,256]{1,0:T(8,128)S(1)}, f32[256,256]{1,0:T(8,128)S(1)}) fusion(f32[8,256,256]{2,1,0:T(8,128)S(1)} %get-tuple-element.461, f32[8,256,256]{2,1,0:T(8,128)S(1)} %copy-done, f32[8,256,256]{2,1,0:T(8,128)S(1)} %convert_subtract_fusion.3, bf16[8,256,256]{2,1,0:T(8,128)(2,1)S(1)} %get-tuple-element.415, ...), kind=kOutput, calls=%fused_computation.4.clone.1 | convolution fusion | flops 275120128 | bytes 11010048 | tf_op jit(solution)/shard_map/while/body/kuv,vw->kuw/dot_general | solution.py:40
  72.0 1.6 %maximum_add_fusion.2 = f32[3,256,256]{2,1,0:T(8,128)S(1)} fusion(f32[1,256,256]{2,1,0:T(8,128)S(1)} %bitcast.162, f32[1,256,256]{2,1,0:T(8,128)S(1)} %bitcast.161, f32[1,256,256]{2,1,0:T(8,128)S(1)} %bitcast.160, f32[3,384,512]{2,1,0:T(8,128)} %get-tuple-element.438, s32[]{:T(128)S(6)} %select_n.163, s32[]{:T(128)S(6)} %select_n.164), kind=kLoop, calls=%fused_computation.22.clone.1 | loop fusion | flops 589824 | bytes 2359304 | tf_op jit(solution)/shard_map/while/body/add | solution.py:131
  73.6 8.9 %dynamic_update_slice.7 = f32[3,384,512]{2,1,0:T(8,128)} dynamic-update-slice(f32[3,384,512]{2,1,0:T(8,128)} %get-tuple-element.438, f32[3,256,256]{2,1,0:T(8,128)S(1)} %maximum_add_fusion.2, s32[]{:T(128)} %constant.185.clone.1..sunk, s32[]{:T(128)S(6)} %select_n.163, s32[]{:T(128)S(6)} %select_n.164) | dynamic-update-slice | bytes 1572868 | tf_op jit(solution)/shard_map/while/body/dynamic_update_slice | solution.py:131
  82.6 1.8 %convert.15 = bf16[3,384,512]{2,1,0:T(8,128)(2,1)S(1)} convert(f32[3,384,512]{2,1,0:T(8,128)} %get-tuple-element.225) | non-fusion elementwise | flops 589824 | bytes 3538944 | tf_op jit(solution)/shard_map/convert.9
  84.4 3.3 %collective-permute-start.4 = (bf16[3,128,512]{2,1,0:T(8,128)(2,1)S(1)}, bf16[3,128,512]{2,1,0:T(8,128)(2,1)S(1)}, u32[]{:S(2)}, u32[]{:S(2)}) collective-permute-start(bf16[3,128,512]{2,1,0:T(8,128)(2,1)S(1)} %get-tuple-element.332), channel_id=1, source_target_pairs={{0,8},{8,16},{16,24},{1,9},{9,17},{17,25},{2,10},{10,18},{18,26},{... | collective-permute-start | bytes 1179656 | tf_op jit(solution)/shard_map/ppermute | solution.py:17
  89.0 4.0 %collective-permute-done.4 = bf16[3,128,512]{2,1,0:T(8,128)(2,1)S(1)} collective-permute-done((bf16[3,128,512]{2,1,0:T(8,128)(2,1)S(1)}, bf16[3,128,512]{2,1,0:T(8,128)(2,1)S(1)}, u32[]{:S(2)}, u32[]{:S(2)}) %collective-permute-start.4) | collective-permute-done | bytes 393248 | tf_op jit(solution)/shard_map/ppermute | solution.py:17
  93.0 4.4 %collective-permute-done.5 = bf16[3,128,512]{2,1,0:T(8,128)(2,1)S(1)} collective-permute-done((bf16[3,128,512]{2,1,0:T(8,128)(2,1)S(1)}, bf16[3,128,512]{2,1,0:T(8,128)(2,1)S(1)}, u32[]{:S(2)}, u32[]{:S(2)}) %collective-permute-start.5) | collective-permute-done | bytes 393248 | tf_op jit(solution)/shard_map/ppermute | solution.py:20
  98.7 5.1 %collective-permute-start.6 = (bf16[3,128,128]{2,1,0:T(8,128)(2,1)S(1)}, bf16[3,128,128]{2,1,0:T(8,128)(2,1)S(1)}, u32[]{:S(2)}, u32[]{:S(2)}) collective-permute-start(bf16[3,128,128]{2,1,0:T(8,128)(2,1)S(1)} %get-tuple-element.334), channel_id=1, source_target_pairs={{0,4},{1,5},{2,6},{3,7},{8,12},{9,13},{10,14},{11,15},{16,20},{17,... | collective-permute-start | bytes 294920 | tf_op jit(solution)/shard_map/ppermute | solution.py:17
  106.0 4.3 %collective-permute-done.7 = bf16[3,128,128]{2,1,0:T(8,128)(2,1)S(1)} collective-permute-done((bf16[3,128,128]{2,1,0:T(8,128)(2,1)S(1)}, bf16[3,128,128]{2,1,0:T(8,128)(2,1)S(1)}, u32[]{:S(2)}, u32[]{:S(2)}) %collective-permute-start.7) | collective-permute-done | bytes 98336 | tf_op jit(solution)/shard_map/ppermute | solution.py:20
  111.2 28.9 %all-reduce.2.cloned.1.call-done = bf16[3,128,256]{2,1,0:T(8,128)(2,1)} async-done(((bf16[3,128,256]{2,1,0:T(8,128)(2,1)}), bf16[3,128,256]{2,1,0:T(8,128)(2,1)}) %all-reduce.2.cloned.1.call-update) | async-done | bytes 196624 | tf_op jit(solution)/shard_map/psum | solution.py:184
  (43 shorter events, 21.4 us)
Async XLA Ops:
  6.5 2.2 %copy-start.2 = (f32[2,128,256]{2,1,0:T(8,128)S(1)}, f32[2,128,256]{2,1,0:T(8,128)}, u32[]{:S(2)}) copy-start(f32[2,128,256]{2,1,0:T(8,128)} %param.19) | copy-start | bytes 786436
  6.5 27.7 %all-gather.2.cloned.1.call-start = ((), (), s32[]{:S(2)}) async-start(), calls=%async_computation | async-start | bytes 2621440 | tf_op jit(solution)/shard_map/all_gather | solution.py:133
  8.7 131.4 %all-reduce.2.cloned.1.call-start = ((), (), s32[]{:S(2)}) async-start(), calls=%async_computation.1 | async-start | bytes 393216 | tf_op jit(solution)/shard_map/psum | solution.py:184
  8.8 8.4 %collective-permute-start.1 = (bf16[2,128,256]{2,1,0:T(8,128)(2,1)S(1)}, bf16[2,128,256]{2,1,0:T(8,128)(2,1)S(1)}, u32[]{:S(2)}, u32[]{:S(2)}) collective-permute-start(bf16[2,128,256]{2,1,0:T(8,128)(2,1)S(1)} %convert_element_type.159), channel_id=1, source_target_pairs={{8,0},{16,8},{24,16},{9,1},{17,9},{25,17},{10,2},{18,10},{26,18},{... | collective-permute-start | bytes 393224 | tf_op jit(solution)/shard_map/ppermute | solution.py:20
  10.1 8.3 %collective-permute-start = (bf16[2,128,256]{2,1,0:T(8,128)(2,1)S(1)}, bf16[2,128,256]{2,1,0:T(8,128)(2,1)S(1)}, u32[]{:S(2)}, u32[]{:S(2)}) collective-permute-start(bf16[2,128,256]{2,1,0:T(8,128)(2,1)S(1)} %convert_element_type.159), channel_id=1, source_target_pairs={{0,8},{8,16},{16,24},{1,9},{9,17},{17,25},{2,10},{10,18},{18,26},{... | collective-permute-start | bytes 393224 | tf_op jit(solution)/shard_map/ppermute | solution.py:17
  18.5 6.8 %collective-permute-start.2 = (bf16[2,384,128]{2,1,0:T(8,128)(2,1)S(1)}, bf16[2,384,128]{2,1,0:T(8,128)(2,1)S(1)}, u32[]{:S(2)}, u32[]{:S(2)}) collective-permute-start(bf16[2,384,128]{2,1,0:T(8,128)(2,1)S(1)} %get-tuple-element.336), channel_id=1, source_target_pairs={{0,4},{1,5},{2,6},{3,7},{8,12},{9,13},{10,14},{11,15},{16,20},{17,... | collective-permute-start | bytes 589832 | tf_op jit(solution)/shard_map/ppermute | solution.py:17
  22.1 7.6 %collective-permute-start.3 = (bf16[2,384,128]{2,1,0:T(8,128)(2,1)S(1)}, bf16[2,384,128]{2,1,0:T(8,128)(2,1)S(1)}, u32[]{:S(2)}, u32[]{:S(2)}) collective-permute-start(bf16[2,384,128]{2,1,0:T(8,128)(2,1)S(1)} %get-tuple-element.337), channel_id=1, source_target_pairs={{4,0},{5,1},{6,2},{7,3},{12,8},{13,9},{14,10},{15,11},{20,16},{21,... | collective-permute-start | bytes 589832 | tf_op jit(solution)/shard_map/ppermute | solution.py:20
  38.3 1.7 %copy-start.1 = (bf16[1,1,2,256,256]{4,3,2,1,0:T(8,128)(2,1)S(1)}, bf16[1,1,2,256,256]{4,3,2,1,0:T(8,128)(2,1)}, u32[]{:S(2)}) copy-start(bf16[1,1,2,256,256]{4,3,2,1,0:T(8,128)(2,1)} %param.21) | copy-start | bytes 786436
  38.3 1.7 %copy-start.4 = (s32[1,1,2,2]{3,2,1,0:T(2,128)S(1)}, s32[1,1,2,2]{3,2,1,0:T(2,128)}, u32[]{:S(2)}) copy-start(s32[1,1,2,2]{3,2,1,0:T(2,128)} %param.22) | copy-start | bytes 52
  67.9 1.6 %copy-start = (f32[8,256,256]{2,1,0:T(8,128)S(1)}, f32[8,256,256]{2,1,0:T(8,128)}, u32[]{:S(2)}) copy-start(f32[8,256,256]{2,1,0:T(8,128)} %get-tuple-element.460) | copy-start | bytes 6291460 | tf_op jit(solution)/shard_map/while
  84.4 8.5 %collective-permute-start.4 = (bf16[3,128,512]{2,1,0:T(8,128)(2,1)S(1)}, bf16[3,128,512]{2,1,0:T(8,128)(2,1)S(1)}, u32[]{:S(2)}, u32[]{:S(2)}) collective-permute-start(bf16[3,128,512]{2,1,0:T(8,128)(2,1)S(1)} %get-tuple-element.332), channel_id=1, source_target_pairs={{0,8},{8,16},{16,24},{1,9},{9,17},{17,25},{2,10},{10,18},{18,26},{... | collective-permute-start | bytes 1179656 | tf_op jit(solution)/shard_map/ppermute | solution.py:17
  87.7 9.7 %collective-permute-start.5 = (bf16[3,128,512]{2,1,0:T(8,128)(2,1)S(1)}, bf16[3,128,512]{2,1,0:T(8,128)(2,1)S(1)}, u32[]{:S(2)}, u32[]{:S(2)}) collective-permute-start(bf16[3,128,512]{2,1,0:T(8,128)(2,1)S(1)} %get-tuple-element.333), channel_id=1, source_target_pairs={{8,0},{16,8},{24,16},{9,1},{17,9},{25,17},{10,2},{18,10},{26,18},{... | collective-permute-start | bytes 1179656 | tf_op jit(solution)/shard_map/ppermute | solution.py:20
  98.7 42.3 %copy-start.3 = (f32[2,128,256]{2,1,0:T(8,128)S(1)}, f32[2,128,256]{2,1,0:T(8,128)}, u32[]{:S(2)}) copy-start(f32[2,128,256]{2,1,0:T(8,128)} %param.19) | copy-start | bytes 786436
  98.7 7.3 %collective-permute-start.6 = (bf16[3,128,128]{2,1,0:T(8,128)(2,1)S(1)}, bf16[3,128,128]{2,1,0:T(8,128)(2,1)S(1)}, u32[]{:S(2)}, u32[]{:S(2)}) collective-permute-start(bf16[3,128,128]{2,1,0:T(8,128)(2,1)S(1)} %get-tuple-element.334), channel_id=1, source_target_pairs={{0,4},{1,5},{2,6},{3,7},{8,12},{9,13},{10,14},{11,15},{16,20},{17,... | collective-permute-start | bytes 294920 | tf_op jit(solution)/shard_map/ppermute | solution.py:17
  103.8 6.5 %collective-permute-start.7 = (bf16[3,128,128]{2,1,0:T(8,128)(2,1)S(1)}, bf16[3,128,128]{2,1,0:T(8,128)(2,1)S(1)}, u32[]{:S(2)}, u32[]{:S(2)}) collective-permute-start(bf16[3,128,128]{2,1,0:T(8,128)(2,1)S(1)} %get-tuple-element.335), channel_id=1, source_target_pairs={{4,0},{5,1},{6,2},{7,3},{12,8},{13,9},{14,10},{15,11},{20,16},{21,... | collective-permute-start | bytes 294920 | tf_op jit(solution)/shard_map/ppermute | solution.py:20
Sparse Core Ops, SparseCore 0:
  8.9 25.2 all-gather.1
  111.3 28.7 all-reduce.1
where the time goes:
time: 151 us; the launch traced here: 149 us
  waiting for transfers between devices  54.4 us (36%)
  matrix products  24 us (16%)
  starting transfers between devices  22.7 us (15%)
  other arithmetic  16.1 us (11%)
  between operations  14.3 us (9%)
  local copies, waits for them, and re-layouts  13.3 us (9%)
  loops' own time  3.83 us (3%)
    psum x1, waiting for transfers between devices, on_device(): summed = lax.psum(core.astype(jnp.bfloat16), 'mode').astype(jnp.float32)  28.9 us
    ppermute x4, starting transfers between devices, padded_2(): lax.ppermute(lax.slice_in_dim(block, block.shape[dim] - width, None, axis...  17.5 us
    ppermute x4, waiting for transfers between devices, padded_2(): lax.ppermute(lax.slice_in_dim(block, 0, width, axis=dim), axis, backward)  14.7 us
    dot_general x8, matrix products, right_mult(): jnp.einsum('kuv,vw->kuw', signal, matrix, preferred_element_type=jnp.floa...  12.6 us
    dot_general x8, matrix products, left_mult(): jnp.einsum('uv,kvw->kuw', matrix, signal, preferred_element_type=jnp.floa...  11.4 us
    dynamic_update_slice x1, local copies, waits for them, and re-layouts, deposit(): lax.dynamic_update_slice(extended, current + block, (anchor, row_at, col_...  8.93 us
    ppermute x4, waiting for transfers between devices, padded_2(): lax.ppermute(lax.slice_in_dim(block, block.shape[dim] - width, None, axis...  7.17 us
    ppermute x4, starting transfers between devices, padded_2(): lax.ppermute(lax.slice_in_dim(block, 0, width, axis=dim), axis, backward)  5.17 us
  transfers between devices with their start and end apart: 10, of which 10 were waited for; matrix products, arithmetic and copies ran while one was open for 1% of the time, Pallas kernels for 0%

commit v1 on v0

v1 whole, which is shorter than its diff:
```python
import functools
import math

import jax
import jax.numpy as jnp
import numpy as np
from jax import lax
from jax.experimental import pallas as pl
from jax.experimental.pallas import tpu as pltpu
from jax.sharding import PartitionSpec as P

power_floor = 0.01
regularizer = 0.1
nowhere = -(1 << 20)


def dft_matrices(side):
    line = np.arange(side, dtype=np.int32)
    angle = (line[:, None] * line[None, :] % side).astype(np.float32) * np.float32(
        2.0 * math.pi / side
    )
    scaling = np.float32(1.0 / math.sqrt(side))
    real = (np.cos(angle) * scaling).astype(jnp.bfloat16)
    imag = (-np.sin(angle) * scaling).astype(jnp.bfloat16)
    direct = np.block([[real, -imag], [imag, real]])
    swapped = np.block([[real, imag], [-imag, real]])
    return direct, swapped


def dot(left, right):
    return jnp.dot(left, right, preferred_element_type=jnp.float32)


def iota(shape, dim):
    return lax.broadcasted_iota(jnp.int32, shape, dim)


def column_coordinate(at, tile_cols, half, sides, x_index, x_count):
    own = at + half
    if sides == 1:
        side = at - tile_cols + jnp.where(x_index == 0, half + tile_cols, 0)
        return jnp.where(at < tile_cols, own, side)
    left = jnp.where(x_index > 0, at - tile_cols, nowhere)
    right = jnp.where(x_index < x_count - 1, at, nowhere)
    return jnp.where(at < tile_cols, own, jnp.where(at < tile_cols + half, left, right))


def wave_kernel(
    sides,
    slots,
    z_count,
    x_count,
    place_ref,
    *refs,
):
    n_pieces = 3 + 3 * sides
    pieces = refs[:n_pieces]
    groups = refs[n_pieces : n_pieces + 4]
    amplitude_ref, direct_ref, swapped_ref = refs[n_pieces + 4 : n_pieces + 7]
    outs = refs[n_pieces + 7 : n_pieces + 7 + n_pieces + 1]
    ext_ref, exit_ref, far_ref, grad_ref = refs[n_pieces + 7 + n_pieces + 1 :]
    row_at, col_at, is_live = place_ref[0], place_ref[1], place_ref[2]
    z_index, x_index, parity = place_ref[3], place_ref[4], place_ref[5]
    own_ref, rows_a, rows_b = pieces[:3]
    tile_rows, tile_cols = own_ref.shape[1:]
    side = groups[0].shape[2]
    half = side // 2
    ext_rows = tile_rows + side
    ext_cols = tile_cols + sides * half
    a_at = pl.multiple_of(jnp.where(parity == 0, 0, half + tile_rows), half)
    b_at = pl.multiple_of(jnp.where(parity == 0, half + tile_rows, 0), half)

    for channel in range(2):
        base = channel * ext_rows
        own_rows = pl.ds(base + half, tile_rows)
        ext_ref[own_rows, :tile_cols] = own_ref[channel]
        ext_ref[pl.ds(base + a_at, half), :tile_cols] = rows_a[channel]
        ext_ref[pl.ds(base + b_at, half), :tile_cols] = rows_b[channel]
        for index in range(sides):
            level, corner_a, corner_b = pieces[3 + 3 * index : 6 + 3 * index]
            columns = slice(tile_cols + index * half, tile_cols + (index + 1) * half)
            ext_ref[own_rows, columns] = level[channel]
            ext_ref[pl.ds(base + a_at, half), columns] = corner_a[channel]
            ext_ref[pl.ds(base + b_at, half), columns] = corner_b[channel]

    def column_of(at):
        return column_coordinate(at, tile_cols, half, sides, x_index, x_count)

    def row_of(at):
        first = jnp.where(z_index > 0, 0, half)
        last = jnp.where(z_index < z_count - 1, ext_rows, half + tile_rows)
        return jnp.where((at >= first) & (at < last), at, nowhere)

    pick_cols = (
        column_of(iota((ext_cols, side), 0)) == iota((ext_cols, side), 1) + col_at
    ).astype(jnp.bfloat16)
    pick_rows = (row_of(iota((side, ext_rows), 1)) == iota((side, ext_rows), 0) + row_at).astype(
        jnp.bfloat16
    )
    narrow = dot(ext_ref[...], pick_cols).astype(jnp.bfloat16)
    patch_real = dot(pick_rows, narrow[:ext_rows])
    patch_imag = dot(pick_rows, narrow[ext_rows:])

    direct = direct_ref[...]
    swapped = swapped_ref[...]
    modes = groups[0].shape[1]

    def wide(tall):
        return jnp.concatenate([tall[:side], tall[side:]], axis=1)

    def tall(wide):
        return jnp.concatenate([wide[:, :side], wide[:, side:]], axis=0)

    def forward(group, slot):
        power = jnp.zeros((side, side), jnp.float32)
        weight = jnp.zeros((side, side), jnp.float32)
        for k in range(modes):
            real = group[0, k].astype(jnp.float32)
            imag = group[1, k].astype(jnp.float32)
            exit_wave = jnp.concatenate(
                [
                    (real * patch_real - imag * patch_imag).astype(jnp.bfloat16),
                    (real * patch_imag + imag * patch_real).astype(jnp.bfloat16),
                ],
                axis=0,
            )
            exit_ref[slot + k] = exit_wave
            half_wave = dot(direct, exit_wave).astype(jnp.bfloat16)
            far = dot(wide(half_wave), swapped)
            far_ref[slot + k] = far
            power = power + (far[:, :side] * far[:, :side] + far[:, side:] * far[:, side:])
            weight = weight + (real * real + imag * imag)
        return power, weight

    sums = [forward(group, index * modes) for index, group in enumerate(groups)]
    power = (sums[0][0] + sums[1][0]) + (sums[2][0] + sums[3][0])
    weight = (sums[0][1] + sums[1][1]) + (sums[2][1] + sums[3][1])
    outs[-1][...] = weight.astype(jnp.bfloat16)
    factor = amplitude_ref[0].astype(jnp.float32) / jnp.sqrt(power + power_floor)
    factor = jnp.concatenate([factor, factor], axis=1)

    def backward(group, slot):
        grad_real = jnp.zeros((side, side), jnp.float32)
        grad_imag = jnp.zeros((side, side), jnp.float32)
        for k in range(modes):
            fixed = (far_ref[slot + k] * factor).astype(jnp.bfloat16)
            back_half = dot(swapped, tall(fixed)).astype(jnp.bfloat16)
            back = dot(wide(back_half), direct)
            exit_wave = exit_ref[slot + k].astype(jnp.float32)
            real = group[0, k].astype(jnp.float32)
            imag = group[1, k].astype(jnp.float32)
            diff_real = back[:, :side] - exit_wave[:side]
            diff_imag = back[:, side:] - exit_wave[side:]
            grad_real = grad_real + (real * diff_real + imag * diff_imag)
            grad_imag = grad_imag + (real * diff_imag - imag * diff_real)
        return grad_real, grad_imag

    grads = [backward(group, index * modes) for index, group in enumerate(groups)]
    put_cols = (
        (column_of(iota((side, ext_cols), 1)) == iota((side, ext_cols), 0) + col_at)
        & (is_live > 0)
    ).astype(jnp.bfloat16)
    put_rows = (iota((ext_rows, side), 0) == iota((ext_rows, side), 1) + row_at).astype(
        jnp.bfloat16
    )
    for channel in range(2):
        gradient = (grads[0][channel] + grads[1][channel]) + (grads[2][channel] + grads[3][channel])
        placed = dot(put_rows, gradient.astype(jnp.bfloat16)).astype(jnp.bfloat16)
        grad_ref[...] = dot(placed, put_cols).astype(jnp.bfloat16)
        outs[0][channel] = grad_ref[half : half + tile_rows, :tile_cols]
        outs[1][channel] = grad_ref[pl.ds(b_at, half), :tile_cols]
        outs[2][channel] = grad_ref[pl.ds(a_at, half), :tile_cols]
        for index in range(sides):
            columns = slice(tile_cols + index * half, tile_cols + (index + 1) * half)
            outs[3 + 3 * index][channel] = grad_ref[half : half + tile_rows, columns]
            outs[4 + 3 * index][channel] = grad_ref[pl.ds(b_at, half), columns]
            outs[5 + 3 * index][channel] = grad_ref[pl.ds(a_at, half), columns]


def weight_kernel(slots, z_count, x_count, place_ref, table_ref, weight_ref, out_ref):
    tile_rows, tile_cols = out_ref.shape
    side = weight_ref.shape[0]
    half = side // 2
    z_index, x_index = place_ref[3], place_ref[4]
    x_tiles = (
        [(x, x - x_index) for x in range(x_count)]
        if x_count <= 3
        else [(x_index + step, step) for step in (-1, 0, 1)]
    )
    weight = weight_ref[...]
    total = jnp.zeros((tile_rows, tile_cols), jnp.float32)
    for z_step in (-1, 0, 1):
        z_tile = z_index + z_step
        z_held = jnp.clip(z_tile, 0, z_count - 1)
        for x_tile, x_step in x_tiles:
            x_held = jnp.clip(x_tile, 0, x_count - 1)
            inside = (z_held == z_tile) & (x_held == x_tile)
            record = z_held * x_count + x_held
            for slot in range(slots):
                shown = inside & (slot < table_ref[record, 2 * slots])
                row = table_ref[record, 2 * slot] + z_step * tile_rows - half
                col = table_ref[record, 2 * slot + 1] + x_step * tile_cols - half
                row = jnp.where(shown, row, nowhere)
                put_rows = (
                    iota((tile_rows, side), 0) == iota((tile_rows, side), 1) + row
                ).astype(jnp.bfloat16)
                put_cols = (
                    iota((side, tile_cols), 1) == iota((side, tile_cols), 0) + col
                ).astype(jnp.bfloat16)
                placed = dot(put_rows, weight).astype(jnp.bfloat16)
                total = total + dot(placed, put_cols)
    out_ref[...] = total


def sum_kernel(sides, z_count, x_count, place_ref, *refs):
    pieces, out_ref = refs[:-1], refs[-1]
    own_ref, rows_a, rows_b = pieces[:3]
    tile_cols = own_ref.shape[2]
    half = pieces[3].shape[2]
    z_index, x_index, parity = place_ref[3], place_ref[4], place_ref[5]
    below = z_index > 0
    above = z_index < z_count - 1
    a_on = jnp.where(parity == 0, below, above)
    b_on = jnp.where(parity == 0, above, below)

    def gate(on, ref, channel):
        return jnp.where(on, ref[channel].astype(jnp.float32), 0.0)

    for channel in range(2):
        total = own_ref[channel].astype(jnp.float32)
        total = total + gate(a_on, rows_a, channel) + gate(b_on, rows_b, channel)
        first = jnp.zeros((total.shape[0], half), jnp.float32)
        last = first
        for index in range(sides):
            level, corner_a, corner_b = pieces[3 + 3 * index : 6 + 3 * index]
            edge = level[channel].astype(jnp.float32)
            edge = edge + gate(a_on, corner_a, channel) + gate(b_on, corner_b, channel)
            if sides == 1:
                first = jnp.where(x_index == 1, edge, 0.0)
                last = jnp.where(x_index == 0, edge, 0.0)
            elif index == 0:
                last = jnp.where(x_index < x_count - 1, edge, 0.0)
            else:
                first = jnp.where(x_index > 0, edge, 0.0)
        zero = jnp.zeros((total.shape[0], tile_cols - 2 * half), jnp.float32)
        parts = [first, zero, last] if tile_cols > 2 * half else [first, last]
        total = total + jnp.concatenate(parts, axis=1)
        out_ref[channel] = total.astype(jnp.bfloat16)


def smem():
    return pl.BlockSpec(memory_space=pltpu.SMEM)


def vmem():
    return pl.BlockSpec(memory_space=pltpu.VMEM)


def on_device(object_field, probe, amplitudes, centers, live):
    side = probe.shape[2]
    half = side // 2
    _, tile_rows, tile_cols = object_field.shape
    slots = centers.shape[2]
    z_count = lax.axis_size("tx")
    x_count = lax.axis_size("ty")
    m_count = lax.axis_size("mode")
    if tile_rows != half or slots != 2 or m_count != 4 or x_count < 2:
        raise ValueError("unsupported sizes")
    z_index = lax.axis_index("tx")
    x_index = lax.axis_index("ty")
    member = lax.axis_index("mode")
    parity = member % 2
    sides = 1 if x_count == 2 else 2
    axes = ("tx", "ty", "mode")

    def zigzag(flip, x_step):
        def moved(z, m):
            down = (m % 2 == 0) != flip
            if down:
                return (z + 1, m) if z < z_count - 1 else (z, m ^ 1)
            return (z - 1, m) if z > 0 else (z, m ^ 1)

        pairs = []
        for z in range(z_count):
            for x in range(x_count):
                for m in range(m_count):
                    z_to, m_to = moved(z, m)
                    x_to = (x + x_step) % x_count
                    pairs.append(
                        (
                            (z * x_count + x) * m_count + m,
                            (z_to * x_count + x_to) * m_count + m_to,
                        )
                    )
        return pairs

    def level(step):
        return [(x, (x + step) % x_count) for x in range(x_count)]

    def exchange(array, flip):
        return lax.ppermute(array, "mode", [(m, m ^ flip) for m in range(m_count)])

    probe_low = probe.astype(jnp.bfloat16)
    probe_y = exchange(probe_low, 2)
    probe_core = exchange(probe_low, 1)
    object_low = object_field.astype(jnp.bfloat16)
    x_steps = [1] if sides == 1 else [1, -1]
    if sides == 1:
        edges = [
            lax.dynamic_slice_in_dim(object_low, (tile_cols - half) * (1 - x_index), half, axis=2)
        ]
    else:
        edges = [object_low[:, :, tile_cols - half :], object_low[:, :, :half]]
    pieces = [object_low]
    pieces += [lax.ppermute(object_low, axes, zigzag(flip, 0)) for flip in (False, True)]
    for step, edge in zip(x_steps, edges):
        pieces.append(lax.ppermute(edge, "ty", level(step)))
        pieces += [lax.ppermute(edge, axes, zigzag(flip, step)) for flip in (False, True)]
    probe_diagonal = exchange(probe_y, 1)

    slot = parity
    place = jnp.stack(
        [
            centers[0, 0, slot, 0],
            centers[0, 0, slot, 1],
            (slot < live[0, 0]).astype(jnp.int32),
            z_index,
            x_index,
            parity,
        ]
    )
    record = jnp.concatenate([centers.reshape(1, 2 * slots), live.reshape(1, 1)], axis=1)
    table = lax.all_gather(record, ("tx", "ty"), axis=0, tiled=True)
    amplitude = lax.dynamic_slice_in_dim(amplitudes[0, 0], slot, 1, axis=0)
    direct, swapped = dft_matrices(side)
    ext_rows = tile_rows + side
    ext_cols = tile_cols + sides * half
    n_pieces = len(pieces)
    results = pl.pallas_call(
        functools.partial(wave_kernel, sides, slots, z_count, x_count),
        out_shape=[jax.ShapeDtypeStruct(piece.shape, jnp.bfloat16) for piece in pieces]
        + [jax.ShapeDtypeStruct((side, side), jnp.bfloat16)],
        in_specs=[smem()] + [vmem()] * (n_pieces + 7),
        out_specs=[vmem()] * (n_pieces + 1),
        scratch_shapes=[
            pltpu.VMEM((2 * ext_rows, ext_cols), jnp.bfloat16),
            pltpu.VMEM((4 * probe.shape[1], 2 * side, side), jnp.bfloat16),
            pltpu.VMEM((4 * probe.shape[1], side, 2 * side), jnp.float32),
            pltpu.VMEM((ext_rows, ext_cols), jnp.bfloat16),
        ],
        compiler_params=pltpu.CompilerParams(vmem_limit_bytes=48 * 1024 * 1024),
        name="waves",
    )(
        place,
        *pieces,
        probe_low,
        probe_core,
        probe_y,
        probe_diagonal,
        amplitude,
        jnp.asarray(direct),
        jnp.asarray(swapped),
    )
    weight = pl.pallas_call(
        functools.partial(weight_kernel, slots, z_count, x_count),
        out_shape=jax.ShapeDtypeStruct((tile_rows, tile_cols), jnp.float32),
        in_specs=[smem(), smem(), vmem()],
        out_specs=vmem(),
        name="weights",
    )(place, table, results[-1])
    received = [results[0]]
    received += [
        lax.ppermute(results[1 + index], axes, zigzag(flip, 0))
        for index, flip in enumerate((False, True))
    ]
    for index, step in enumerate(x_steps):
        back_step = -step
        received.append(lax.ppermute(results[3 + 3 * index], "ty", level(back_step)))
        received += [
            lax.ppermute(results[4 + 3 * index + turn], axes, zigzag(flip, back_step))
            for turn, flip in enumerate((False, True))
        ]
    summed = pl.pallas_call(
        functools.partial(sum_kernel, sides, z_count, x_count),
        out_shape=jax.ShapeDtypeStruct(object_field.shape, jnp.bfloat16),
        in_specs=[smem()] + [vmem()] * n_pieces,
        out_specs=vmem(),
        name="sums",
    )(place, *received)
    other = exchange(summed, 1)
    gradient = summed.astype(jnp.float32) + other.astype(jnp.float32)
    return object_field + gradient / (weight + regularizer)


def solution(mesh):
    return jax.shard_map(
        on_device,
        mesh=mesh,
        in_specs=(
            P(None, "tx", "ty"),
            P(None, "mode", None, None),
            P("tx", "ty", None, None, None),
            P("tx", "ty", None, None),
            P("tx", "ty"),
        ),
        out_specs=P(None, "tx", "ty"),
        check_vma=False,
    )
```

time: 151 us -> 80.7 us (0.53); the launches traced: 149 us -> 80.4 us
  waiting for transfers between devices: 54.4 us -> 18 us
  matrix products: 24 us -> 0 us
  blocking collectives: 0 us -> 20.5 us
  Pallas kernels: 0 us -> 13.7 us
  between operations: 14.3 us -> 0.83 us
  other arithmetic: 16.1 us -> 4.06 us
  starting transfers between devices: 22.7 us -> 15.4 us
  local copies, waits for them, and re-layouts: 13.3 us -> 7.9 us
  loops' own time: 3.83 us -> 0 us
    psum x1 -> x0, waiting for transfers between devices: 28.9 us -> none  [on_device(): summed = lax.psum(core.astype(jnp.bfloat16), 'mode').astype(jnp.float32)]
    dot_general x16 -> x0, matrix products: 24 us -> none  [the longest x8 12.6 us: right_mult(): jnp.einsum('kuv,vw->kuw', signal, matrix, preferred_element_type=jnp.floa...]
    all_gather x0 -> x1, blocking collectives: none -> 20.5 us  [on_device(): table = lax.all_gather(record, ('tx', 'ty'), axis=0, tiled=True)]
    pallas_call x0 -> x3, Pallas kernels: none -> 13.7 us  [the longest x1 9.5 us: on_device(): pl.pallas_call(functools.partial(wave_kernel, sides, slots, z_count, x_co...]
    dynamic_update_slice x1 -> x0, local copies, waits for them, and re-layouts: 8.93 us -> none  [deposit(): lax.dynamic_update_slice(extended, current + block, (anchor, row_at, col_...]
    ppermute x8 -> x14, starting transfers between devices: 22.7 us -> 15.4 us  [the longest x2 3.66 us: on_device(): lax.ppermute(edge, axes, zigzag(flip, step))]
    convert_element_type x5 -> x1, other arithmetic: 7.98 us -> 1.35 us  [on_device(): probe_low = probe.astype(jnp.bfloat16)]
    unnamed x8 -> x38, local copies, waits for them, and re-layouts: 0.02 us -> 5.19 us
  transfers between devices with their start and end apart: 10 -> 14, of which waited for: 10 -> 4; matrix products, arithmetic and copies ran while one was open for 1% -> 5% of each run, Pallas kernels for 0% -> 3%
where the time goes in v1:
time: 80.7 us; the launch traced here: 80.4 us
  blocking collectives  20.5 us (25%)
  waiting for transfers between devices  18 us (22%)
  starting transfers between devices  15.4 us (19%)
  Pallas kernels  13.7 us (17%)
  local copies, waits for them, and re-layouts  7.9 us (10%)
  other arithmetic  4.06 us (5%)
  between operations  0.83 us (1%)
    all_gather x1, blocking collectives, on_device(): table = lax.all_gather(record, ('tx', 'ty'), axis=0, tiled=True)  20.5 us
    ppermute x4, waiting for transfers between devices, exchange(): return lax.ppermute(array, 'mode', [(m, m ^ flip) for m in range(m_count)])  13.5 us
    pallas_call x1, Pallas kernels, on_device(): pl.pallas_call(functools.partial(wave_kernel, sides, slots, z_count, x_co...  9.5 us
    unnamed x38, local copies, waits for them, and re-layouts  5.19 us
    ppermute x2, waiting for transfers between devices, on_device(): lax.ppermute(edge, axes, zigzag(flip, step))  4.36 us
    ppermute x2, starting transfers between devices, on_device(): lax.ppermute(edge, axes, zigzag(flip, step))  3.66 us
    ppermute x4, starting transfers between devices, exchange(): return lax.ppermute(array, 'mode', [(m, m ^ flip) for m in range(m_count)])  3.04 us
    pallas_call x1, Pallas kernels, on_device(): pl.pallas_call(functools.partial(weight_kernel, slots, z_count, x_count),...  2.27 us
  transfers between devices with their start and end apart: 14, of which 4 were waited for; matrix products, arithmetic and copies ran while one was open for 5% of the time, Pallas kernels for 3%

profile of v1, /device:TPU:0, one launch (start us, length us, event | category | flops | bytes accessed | tf_op | source)
XLA Modules:
  0.0 80.4 jit_solution(7330701629664538439)
XLA Ops:
  0.0 1.4 %convert_element_type.14.refs_6_ = bf16[2,2,256,256]{3,2,1,0:T(8,128)(2,1)S(1)} convert(f32[2,2,256,256]{3,2,1,0:T(8,128)} %param.8) | non-fusion elementwise | flops 262144 | bytes 1572864 | tf_op jit(solution)/shard_map/convert_element_type | solution.py:303
  1.4 3.0 %collective-permute-start.6 = (bf16[2,2,256,256]{3,2,1,0:T(8,128)(2,1)S(1)}, bf16[2,2,256,256]{3,2,1,0:T(8,128)(2,1)S(1)}, u32[]{:S(2)}, u32[]{:S(2)}) collective-permute-start(bf16[2,2,256,256]{3,2,1,0:T(8,128)(2,1)S(1)} %convert_element_type.14.refs_6_), channel_id=1, source_target_pairs={{0,2},{1,3},{2,0},{3,1},{4,6},{5,7},{6,4},{7,5},{8,10},{9,11},{10,... | collective-permute-start | bytes 1572872 | tf_op jit(solution)/shard_map/ppermute | solution.py:301
  4.4 11.9 %collective-permute-done.6.refs_8_ = bf16[2,2,256,256]{3,2,1,0:T(8,128)(2,1)S(1)} collective-permute-done((bf16[2,2,256,256]{3,2,1,0:T(8,128)(2,1)S(1)}, bf16[2,2,256,256]{3,2,1,0:T(8,128)(2,1)S(1)}, u32[]{:S(2)}, u32[]{:S(2)}) %collective-permute-start.6) | collective-permute-done | bytes 524320 | tf_op jit(solution)/shard_map/ppermute | solution.py:301
  16.3 1.0 %convert_element_type.13.refs_0_ = bf16[2,128,256]{2,1,0:T(8,128)(2,1)S(1)} convert(f32[2,128,256]{2,1,0:T(8,128)} %param.7) | non-fusion elementwise | flops 65536 | bytes 393216 | tf_op jit(solution)/shard_map/convert_element_type | solution.py:306
  17.3 0.6 constant_dynamic-slice_fusion
  17.9 1.7 %collective-permute-start.2 = (bf16[2,128,128]{2,1,0:T(8,128)(2,1)}, bf16[2,128,128]{2,1,0:T(8,128)(2,1)S(1)}, u32[]{:S(2)}, u32[]{:S(2)}) collective-permute-start(bf16[2,128,128]{2,1,0:T(8,128)(2,1)} %constant_dynamic-slice_fusion), channel_id=1, source_target_pairs={{0,4},{4,0},{1,5},{5,1},{2,6},{6,2},{3,7},{7,3},{8,12},{12,8},{9,1... | collective-permute-start | bytes 196616 | tf_op jit(solution)/shard_map/ppermute | solution.py:317
  19.7 1.5 %collective-permute-start.3 = (bf16[2,128,128]{2,1,0:T(8,128)(2,1)}, bf16[2,128,128]{2,1,0:T(8,128)(2,1)}, u32[]{:S(2)}, u32[]{:S(2)}) collective-permute-start(bf16[2,128,128]{2,1,0:T(8,128)(2,1)} %constant_dynamic-slice_fusion), channel_id=1, source_target_pairs={{0,12},{1,4},{2,14},{3,6},{4,8},{5,0},{6,10},{7,2},{8,20},{9,5},{1... | collective-permute-start | bytes 196616 | tf_op jit(solution)/shard_map/ppermute | solution.py:318
  21.2 1.6 %collective-permute-start = (bf16[2,128,256]{2,1,0:T(8,128)(2,1)S(1)}, bf16[2,128,256]{2,1,0:T(8,128)(2,1)}, u32[]{:S(2)}, u32[]{:S(2)}) collective-permute-start(bf16[2,128,256]{2,1,0:T(8,128)(2,1)S(1)} %convert_element_type.13.refs_0_), channel_id=1, source_target_pairs={{0,8},{1,0},{2,10},{3,2},{4,12},{5,4},{6,14},{7,6},{8,16},{9,1},{1... | collective-permute-start | bytes 393224 | tf_op jit(solution)/shard_map/ppermute | solution.py:315
  22.8 0.2 collective-permute-done.2.refs_3_
  22.9 0.6 copy-done.5
  24.2 0.7 copy-done.18
  24.9 0.6 constant_dynamic-slice_fusion.1
  25.5 1.3 %stack.23.place_ref = s32[6]{0:T(128)S(1)} concatenate(s32[1]{0:T(128)} %bitcast, s32[1]{0:T(128)} %bitcast.1, s32[1]{0:T(128)} %bitcast.3, s32[1]{0:T(128)} %bitcast.4, s32[1]{0:T(128)} %bitcast.5, s32[1]{0:T(128)} %bitcast.6), dimensions={0} | concatenate | bytes 48 | tf_op jit(solution)/shard_map/stack | solution.py:322
  26.9 2.1 %collective-permute-start.4 = (bf16[2,128,128]{2,1,0:T(8,128)(2,1)}, bf16[2,128,128]{2,1,0:T(8,128)(2,1)S(1)}, u32[]{:S(2)}, u32[]{:S(2)}) collective-permute-start(bf16[2,128,128]{2,1,0:T(8,128)(2,1)} %constant_dynamic-slice_fusion), channel_id=1, source_target_pairs={{0,5},{1,13},{2,7},{3,15},{4,1},{5,9},{6,3},{7,11},{8,4},{9,21},{1... | collective-permute-start | bytes 196616 | tf_op jit(solution)/shard_map/ppermute | solution.py:318
  29.0 4.4 %collective-permute-done.4.refs_5_ = bf16[2,128,128]{2,1,0:T(8,128)(2,1)S(1)} collective-permute-done((bf16[2,128,128]{2,1,0:T(8,128)(2,1)}, bf16[2,128,128]{2,1,0:T(8,128)(2,1)S(1)}, u32[]{:S(2)}, u32[]{:S(2)}) %collective-permute-start.4) | collective-permute-done | bytes 65568 | tf_op jit(solution)/shard_map/ppermute | solution.py:318
  33.4 9.5 %waves.1 = (bf16[2,128,256]{2,1,0:T(8,128)(2,1)S(1)}, bf16[2,128,256]{2,1,0:T(8,128)(2,1)}, bf16[2,128,256]{2,1,0:T(8,128)(2,1)}, bf16[2,128,128]{2,1,0:T(8,128)...) custom-call(s32[6]{0:T(128)S(1)} %stack.23.place_ref, ...), custom_call_target="tpu_custom_call" | custom-call | tf_op jit(solution)/shard_map/waves/pallas_call | solution.py:339
  42.9 0.6 copy-done.3
  43.6 0.7 copy-done.4
  44.2 0.6 copy-done.8
  44.9 0.6 copy-done.9
  45.5 0.6 copy-done.10
  46.1 1.9 %collective-permute-start.8 = (bf16[2,128,256]{2,1,0:T(8,128)(2,1)}, bf16[2,128,256]{2,1,0:T(8,128)(2,1)S(1)}, u32[]{:S(2)}, u32[]{:S(2)}) collective-permute-start(bf16[2,128,256]{2,1,0:T(8,128)(2,1)} %get-tuple-element.13), channel_id=1, source_target_pairs={{0,8},{1,0},{2,10},{3,2},{4,12},{5,4},{6,14},{7,6},{8,16},{9,1},{1... | collective-permute-start | bytes 393224 | tf_op jit(solution)/shard_map/ppermute | solution.py:373
  48.0 0.1 reshape.5
  48.1 1.6 %collective-permute-start.10 = (bf16[2,128,128]{2,1,0:T(8,128)(2,1)}, bf16[2,128,128]{2,1,0:T(8,128)(2,1)S(1)}, u32[]{:S(2)}, u32[]{:S(2)}) collective-permute-start(bf16[2,128,128]{2,1,0:T(8,128)(2,1)} %copy-done.10), channel_id=1, source_target_pairs={{0,4},{4,0},{1,5},{5,1},{2,6},{6,2},{3,7},{7,3},{8,12},{12,8},{9,1... | collective-permute-start | bytes 196616 | tf_op jit(solution)/shard_map/ppermute | solution.py:378
  49.7 1.9 %collective-permute-start.11 = (bf16[2,128,128]{2,1,0:T(8,128)(2,1)}, bf16[2,128,128]{2,1,0:T(8,128)(2,1)S(1)}, u32[]{:S(2)}, u32[]{:S(2)}) collective-permute-start(bf16[2,128,128]{2,1,0:T(8,128)(2,1)} %copy-done.9), channel_id=1, source_target_pairs={{0,12},{1,4},{2,14},{3,6},{4,8},{5,0},{6,10},{7,2},{8,20},{9,5},{1... | collective-permute-start | bytes 196616 | tf_op jit(solution)/shard_map/ppermute | solution.py:380
  51.6 0.1 add_bitcast_fusion
  51.7 20.5 %all-gather = s32[8,1,5]{2,1,0:T(1,128)} all-gather(s32[1,1,5]{2,1,0:T(1,128)S(1)} %add_bitcast_fusion), channel_id=1, replica_groups=mesh['tx'=4,'ty'=2,'mode'=4] {'tx','ty'}, dimensions={0}, use_global_device_ids=true | all-gather | bytes 180 | tf_op jit(solution)/shard_map/all_gather | solution.py:333
  72.2 2.3 %weights.1 = f32[128,256]{1,0:T(8,128)} custom-call(s32[6]{0:T(128)} %copy-done.7, s32[8,5]{1,0:T(8,128)} %bitcast.13, bf16[256,256]{1,0:T(8,128)(2,1)} %copy-done.4), custom_call_target="tpu_custom_call" | custom-call | tf_op jit(solution)/shard_map/weights/pallas_call | solution.py:364
  74.6 0.5 copy-done.15
  75.3 1.9 %sums.1 = bf16[2,128,256]{2,1,0:T(8,128)(2,1)} custom-call(s32[6]{0:T(128)} %copy-done.7, bf16[2,128,256]{2,1,0:T(8,128)(2,1)} %copy-done.3, bf16[2,128,256]{2,1,0:T(8,128)(2,1)} %copy-done.13, bf16[2,128,256]{2,1,0:T(8,128)(2,1)} %copy-done.14, bf16[2,128,128]{2,1,0:T(8,128)(2,1)} %copy-done.15, bf16[2,128,128]{2,1,0:T(8,128)(2,1)} %copy-done.16, ...), custom_call_target="tpu_custom_call" | custom-call | tf_op jit(solution)/shard_map/sums/pallas_call | solution.py:383
  77.2 1.5 %collective-permute-done.13 = bf16[2,128,256]{2,1,0:T(8,128)(2,1)S(1)} collective-permute-done((bf16[2,128,256]{2,1,0:T(8,128)(2,1)}, bf16[2,128,256]{2,1,0:T(8,128)(2,1)S(1)}, u32[]{:S(2)}, u32[]{:S(2)}) %collective-permute-start.13) | collective-permute-done | bytes 131104 | tf_op jit(solution)/shard_map/ppermute | solution.py:301
  78.7 1.7 %divide_add_fusion = f32[2,128,256]{2,1,0:T(8,128)} fusion(f32[2,128,256]{2,1,0:T(8,128)S(1)} %copy-done.11, bf16[2,128,256]{2,1,0:T(8,128)(2,1)S(1)} %collective-permute-done.13, bf16[2,128,256]{2,1,0:T(8,128)(2,1)} %sums.1, f32[128,256]{1,0:T(8,128)S(1)} %broadcast_add_fusion), kind=kLoop, calls=%fused_computation | loop fusion | flops 327680 | bytes 917504 | tf_op jit(solution)/shard_map/add | solution.py:392
  (48 shorter events, 0.3 us)
Async XLA Ops:
  0.0 29.0 %copy-start = (bf16[1,1,2,256,256]{4,3,2,1,0:T(8,128)(2,1)S(1)}, bf16[1,1,2,256,256]{4,3,2,1,0:T(8,128)(2,1)}, u32[]{:S(2)}) copy-start(bf16[1,1,2,256,256]{4,3,2,1,0:T(8,128)(2,1)} %param.9) | copy-start | bytes 786436
  0.0 33.4 %copy-start.2 = (bf16[512,512]{1,0:T(8,128)(2,1)S(1)}, bf16[512,512]{1,0:T(8,128)(2,1)}, u32[]{:S(2)}) copy-start(bf16[512,512]{1,0:T(8,128)(2,1)} %constant.39.clone.refs_12_) | copy-start | bytes 1572868
  1.4 32.1 %copy-start.1 = (bf16[512,512]{1,0:T(8,128)(2,1)S(1)}, bf16[512,512]{1,0:T(8,128)(2,1)}, u32[]{:S(2)}) copy-start(bf16[512,512]{1,0:T(8,128)(2,1)} %constant.38.clone.refs_11_) | copy-start | bytes 1572868
  1.4 15.0 %collective-permute-start.6 = (bf16[2,2,256,256]{3,2,1,0:T(8,128)(2,1)S(1)}, bf16[2,2,256,256]{3,2,1,0:T(8,128)(2,1)S(1)}, u32[]{:S(2)}, u32[]{:S(2)}) collective-permute-start(bf16[2,2,256,256]{3,2,1,0:T(8,128)(2,1)S(1)} %convert_element_type.14.refs_6_), channel_id=1, source_target_pairs={{0,2},{1,3},{2,0},{3,1},{4,6},{5,7},{6,4},{7,5},{8,10},{9,11},{10,... | collective-permute-start | bytes 1572872 | tf_op jit(solution)/shard_map/ppermute | solution.py:301
  4.4 29.0 %collective-permute-start.5 = (bf16[2,2,256,256]{3,2,1,0:T(8,128)(2,1)S(1)}, bf16[2,2,256,256]{3,2,1,0:T(8,128)(2,1)S(1)}, u32[]{:S(2)}, u32[]{:S(2)}) collective-permute-start(bf16[2,2,256,256]{3,2,1,0:T(8,128)(2,1)S(1)} %convert_element_type.14.refs_6_), channel_id=1, source_target_pairs={{0,1},{1,0},{2,3},{3,2},{4,5},{5,4},{6,7},{7,6},{8,9},{9,8},{10,11... | collective-permute-start | bytes 1572872 | tf_op jit(solution)/shard_map/ppermute | solution.py:301
  16.3 17.1 %collective-permute-start.7 = (bf16[2,2,256,256]{3,2,1,0:T(8,128)(2,1)S(1)}, bf16[2,2,256,256]{3,2,1,0:T(8,128)(2,1)S(1)}, u32[]{:S(2)}, u32[]{:S(2)}) collective-permute-start(bf16[2,2,256,256]{3,2,1,0:T(8,128)(2,1)S(1)} %collective-permute-done.6.refs_8_), channel_id=1, source_target_pairs={{0,1},{1,0},{2,3},{3,2},{4,5},{5,4},{6,7},{7,6},{8,9},{9,8},{10,11... | collective-permute-start | bytes 1572872 | tf_op jit(solution)/shard_map/ppermute | solution.py:301
  17.9 5.0 %collective-permute-start.2 = (bf16[2,128,128]{2,1,0:T(8,128)(2,1)}, bf16[2,128,128]{2,1,0:T(8,128)(2,1)S(1)}, u32[]{:S(2)}, u32[]{:S(2)}) collective-permute-start(bf16[2,128,128]{2,1,0:T(8,128)(2,1)} %constant_dynamic-slice_fusion), channel_id=1, source_target_pairs={{0,4},{4,0},{1,5},{5,1},{2,6},{6,2},{3,7},{7,3},{8,12},{12,8},{9,1... | collective-permute-start | bytes 196616 | tf_op jit(solution)/shard_map/ppermute | solution.py:317
  19.7 7.2 %collective-permute-start.3 = (bf16[2,128,128]{2,1,0:T(8,128)(2,1)}, bf16[2,128,128]{2,1,0:T(8,128)(2,1)}, u32[]{:S(2)}, u32[]{:S(2)}) collective-permute-start(bf16[2,128,128]{2,1,0:T(8,128)(2,1)} %constant_dynamic-slice_fusion), channel_id=1, source_target_pairs={{0,12},{1,4},{2,14},{3,6},{4,8},{5,0},{6,10},{7,2},{8,20},{9,5},{1... | collective-permute-start | bytes 196616 | tf_op jit(solution)/shard_map/ppermute | solution.py:318
  21.2 12.2 %collective-permute-start = (bf16[2,128,256]{2,1,0:T(8,128)(2,1)S(1)}, bf16[2,128,256]{2,1,0:T(8,128)(2,1)}, u32[]{:S(2)}, u32[]{:S(2)}) collective-permute-start(bf16[2,128,256]{2,1,0:T(8,128)(2,1)S(1)} %convert_element_type.13.refs_0_), channel_id=1, source_target_pairs={{0,8},{1,0},{2,10},{3,2},{4,12},{5,4},{6,14},{7,6},{8,16},{9,1},{1... | collective-permute-start | bytes 393224 | tf_op jit(solution)/shard_map/ppermute | solution.py:315
  22.9 0.6 copy-start.5
  23.6 9.8 %collective-permute-start.1 = (bf16[2,128,256]{2,1,0:T(8,128)(2,1)S(1)}, bf16[2,128,256]{2,1,0:T(8,128)(2,1)}, u32[]{:S(2)}, u32[]{:S(2)}) collective-permute-start(bf16[2,128,256]{2,1,0:T(8,128)(2,1)S(1)} %convert_element_type.13.refs_0_), channel_id=1, source_target_pairs={{0,1},{1,9},{2,3},{3,11},{4,5},{5,13},{6,7},{7,15},{8,0},{9,17},{1... | collective-permute-start | bytes 393224 | tf_op jit(solution)/shard_map/ppermute | solution.py:315
  24.2 0.7 copy-start.18
  26.9 6.5 %copy-start.7 = (s32[6]{0:T(128)}, s32[6]{0:T(128)S(1)}, u32[]{:S(2)}) copy-start(s32[6]{0:T(128)S(1)} %stack.23.place_ref) | copy-start | bytes 76
  26.9 6.6 %copy-start.6 = (bf16[2,128,128]{2,1,0:T(8,128)(2,1)S(1)}, bf16[2,128,128]{2,1,0:T(8,128)(2,1)}, u32[]{:S(2)}) copy-start(bf16[2,128,128]{2,1,0:T(8,128)(2,1)} %copy-done.5) | copy-start | bytes 196612
  26.9 6.5 %collective-permute-start.4 = (bf16[2,128,128]{2,1,0:T(8,128)(2,1)}, bf16[2,128,128]{2,1,0:T(8,128)(2,1)S(1)}, u32[]{:S(2)}, u32[]{:S(2)}) collective-permute-start(bf16[2,128,128]{2,1,0:T(8,128)(2,1)} %constant_dynamic-slice_fusion), channel_id=1, source_target_pairs={{0,5},{1,13},{2,7},{3,15},{4,1},{5,9},{6,3},{7,11},{8,4},{9,21},{1... | collective-permute-start | bytes 196616 | tf_op jit(solution)/shard_map/ppermute | solution.py:318
  42.9 0.6 copy-start.3
  43.6 0.7 copy-start.4
  44.9 0.6 copy-start.9
  45.5 0.6 copy-start.10
  46.1 28.4 %collective-permute-start.8 = (bf16[2,128,256]{2,1,0:T(8,128)(2,1)}, bf16[2,128,256]{2,1,0:T(8,128)(2,1)S(1)}, u32[]{:S(2)}, u32[]{:S(2)}) collective-permute-start(bf16[2,128,256]{2,1,0:T(8,128)(2,1)} %get-tuple-element.13), channel_id=1, source_target_pairs={{0,8},{1,0},{2,10},{3,2},{4,12},{5,4},{6,14},{7,6},{8,16},{9,1},{1... | collective-permute-start | bytes 393224 | tf_op jit(solution)/shard_map/ppermute | solution.py:373
  48.0 26.5 %collective-permute-start.9 = (bf16[2,128,256]{2,1,0:T(8,128)(2,1)}, bf16[2,128,256]{2,1,0:T(8,128)(2,1)S(1)}, u32[]{:S(2)}, u32[]{:S(2)}) collective-permute-start(bf16[2,128,256]{2,1,0:T(8,128)(2,1)} %get-tuple-element.14), channel_id=1, source_target_pairs={{0,1},{1,9},{2,3},{3,11},{4,5},{5,13},{6,7},{7,15},{8,0},{9,17},{1... | collective-permute-start | bytes 393224 | tf_op jit(solution)/shard_map/ppermute | solution.py:373
  48.1 26.4 %collective-permute-start.10 = (bf16[2,128,128]{2,1,0:T(8,128)(2,1)}, bf16[2,128,128]{2,1,0:T(8,128)(2,1)S(1)}, u32[]{:S(2)}, u32[]{:S(2)}) collective-permute-start(bf16[2,128,128]{2,1,0:T(8,128)(2,1)} %copy-done.10), channel_id=1, source_target_pairs={{0,4},{4,0},{1,5},{5,1},{2,6},{6,2},{3,7},{7,3},{8,12},{12,8},{9,1... | collective-permute-start | bytes 196616 | tf_op jit(solution)/shard_map/ppermute | solution.py:378
  49.7 24.8 %collective-permute-start.11 = (bf16[2,128,128]{2,1,0:T(8,128)(2,1)}, bf16[2,128,128]{2,1,0:T(8,128)(2,1)S(1)}, u32[]{:S(2)}, u32[]{:S(2)}) collective-permute-start(bf16[2,128,128]{2,1,0:T(8,128)(2,1)} %copy-done.9), channel_id=1, source_target_pairs={{0,12},{1,4},{2,14},{3,6},{4,8},{5,0},{6,10},{7,2},{8,20},{9,5},{1... | collective-permute-start | bytes 196616 | tf_op jit(solution)/shard_map/ppermute | solution.py:380
  51.6 22.9 %collective-permute-start.12 = (bf16[2,128,128]{2,1,0:T(8,128)(2,1)}, bf16[2,128,128]{2,1,0:T(8,128)(2,1)S(1)}, u32[]{:S(2)}, u32[]{:S(2)}) collective-permute-start(bf16[2,128,128]{2,1,0:T(8,128)(2,1)} %copy-done.8), channel_id=1, source_target_pairs={{0,5},{1,13},{2,7},{3,15},{4,1},{5,9},{6,3},{7,11},{8,4},{9,21},{1... | collective-permute-start | bytes 196616 | tf_op jit(solution)/shard_map/ppermute | solution.py:380
  74.5 0.6 copy-start.15
  74.5 0.6 copy-start.16
  74.5 0.7 copy-start.17
  74.5 0.7 copy-start.13
  74.6 0.7 copy-start.14
  75.3 1.9 %copy-start.12 = (f32[128,256]{1,0:T(8,128)S(1)}, f32[128,256]{1,0:T(8,128)}, u32[]{:S(2)}) copy-start(f32[128,256]{1,0:T(8,128)} %weights.1) | copy-start | bytes 393220
  77.2 1.6 %copy-start.11 = (f32[2,128,256]{2,1,0:T(8,128)S(1)}, f32[2,128,256]{2,1,0:T(8,128)}, u32[]{:S(2)}) copy-start(f32[2,128,256]{2,1,0:T(8,128)} %param.7) | copy-start | bytes 786436
  77.2 1.6 %collective-permute-start.13 = (bf16[2,128,256]{2,1,0:T(8,128)(2,1)}, bf16[2,128,256]{2,1,0:T(8,128)(2,1)S(1)}, u32[]{:S(2)}, u32[]{:S(2)}) collective-permute-start(bf16[2,128,256]{2,1,0:T(8,128)(2,1)} %sums.1), channel_id=1, source_target_pairs={{0,1},{1,0},{2,3},{3,2},{4,5},{5,4},{6,7},{7,6},{8,9},{9,8},{10,11... | collective-permute-start | bytes 393224 | tf_op jit(solution)/shard_map/ppermute | solution.py:301
  (1 other events, 0.6 us)

commit v2 on v1

v2 whole, which is shorter than its diff:
```python
import functools
import math

import jax
import jax.numpy as jnp
import numpy as np
from jax import lax
from jax.experimental import pallas as pl
from jax.experimental.pallas import tpu as pltpu
from jax.sharding import PartitionSpec as P

power_floor = 0.01
regularizer = 0.1
nowhere = -(1 << 20)
record_rows = 16
vmem_bytes = 40 * 1024 * 1024


def dft_matrices(side):
    line = np.arange(side, dtype=np.int32)
    angle = (line[:, None] * line[None, :] % side).astype(np.float32) * np.float32(
        2.0 * math.pi / side
    )
    scaling = np.float32(1.0 / math.sqrt(side))
    real = (np.cos(angle) * scaling).astype(jnp.bfloat16)
    imag = (-np.sin(angle) * scaling).astype(jnp.bfloat16)
    direct = np.block([[real, -imag], [imag, real]])
    swapped = np.block([[real, imag], [-imag, real]])
    return direct, swapped


def dot(left, right):
    return jnp.dot(left, right, preferred_element_type=jnp.float32)


def iota(shape, dim):
    return lax.broadcasted_iota(jnp.int32, shape, dim)


def column_coordinate(at, tile_cols, half, sides, x_index, x_count):
    own = at + half
    if sides == 1:
        side = at - tile_cols + jnp.where(x_index == 0, half + tile_cols, 0)
        return jnp.where(at < tile_cols, own, side)
    left = jnp.where(x_index > 0, at - tile_cols, nowhere)
    right = jnp.where(x_index < x_count - 1, at, nowhere)
    return jnp.where(at < tile_cols, own, jnp.where(at < tile_cols + half, left, right))


def wide(tall):
    side = tall.shape[0] // 2
    return jnp.concatenate([tall[:side], tall[side:]], axis=1)


def tall(wide):
    side = wide.shape[1] // 2
    return jnp.concatenate([wide[:, :side], wide[:, side:]], axis=0)


def here():
    return (lax.axis_index("tx"), lax.axis_index("ty"), lax.axis_index("mode") % 2)


def pack_kernel(sides, slots, centers_ref, live_ref, object_ref, *outs):
    _, tile_rows, tile_cols = object_ref.shape
    half = outs[1].shape[1]
    _, x_index, _ = here()
    record = jnp.zeros((record_rows, tile_cols), jnp.float32)
    line = iota((record_rows, tile_cols), 0)
    for slot in range(slots):
        for axis in range(2):
            value = centers_ref[0, 0, slot, axis].astype(jnp.float32)
            record = jnp.where(line == 2 * slot + axis, value, record)
    record = jnp.where(line == 2 * slots, live_ref[0, 0].astype(jnp.float32), record)
    record = record.astype(jnp.bfloat16)
    first, last = slice(0, half), slice(tile_cols - half, tile_cols)
    for channel in range(2):
        rows = slice(channel * tile_rows, (channel + 1) * tile_rows)
        values = object_ref[channel].astype(jnp.bfloat16)
        outs[0][rows] = values
        if sides == 1:
            outs[1][rows] = jnp.where(x_index == 0, values[:, last], values[:, first])
        else:
            outs[1][rows] = values[:, last]
            outs[2][rows] = values[:, first]
    rows = slice(2 * tile_rows, 2 * tile_rows + record_rows)
    outs[0][rows] = record
    for out in outs[1:]:
        out[rows] = record[:, :half]


def row_starts(half, tile_rows, parity):
    low, high = 0, half + tile_rows
    return (
        pl.multiple_of(jnp.where(parity == 0, low, high), half),
        pl.multiple_of(jnp.where(parity == 0, high, low), half),
    )


def patch_of(sides, z_count, x_count, tile_rows, side, centers_ref, pieces, ext_ref):
    z_index, x_index, parity = here()
    row_at = centers_ref[0, 0, parity, 0]
    col_at = centers_ref[0, 0, parity, 1]
    half = side // 2
    tile_cols = pieces[0].shape[1]
    ext_rows = tile_rows + side
    ext_cols = tile_cols + sides * half
    a_at, b_at = row_starts(half, tile_rows, parity)
    for channel in range(2):
        base = channel * ext_rows
        rows = slice(channel * tile_rows, (channel + 1) * tile_rows)
        for index in range(1 + sides):
            columns = (
                slice(0, tile_cols)
                if index == 0
                else slice(tile_cols + (index - 1) * half, tile_cols + index * half)
            )
            level, turn_a, turn_b = pieces[3 * index : 3 * index + 3]
            ext_ref[pl.ds(base + half, tile_rows), columns] = level[rows]
            ext_ref[pl.ds(base + a_at, half), columns] = turn_a[rows]
            ext_ref[pl.ds(base + b_at, half), columns] = turn_b[rows]
    at = iota((ext_cols, side), 0)
    column = column_coordinate(at, tile_cols, half, sides, x_index, x_count)
    pick_cols = (column == iota((ext_cols, side), 1) + col_at).astype(jnp.bfloat16)
    at = iota((side, ext_rows), 1)
    first = jnp.where(z_index > 0, 0, half)
    last = jnp.where(z_index < z_count - 1, ext_rows, half + tile_rows)
    row = jnp.where((at >= first) & (at < last), at, nowhere)
    pick_rows = (row == iota((side, ext_rows), 0) + row_at).astype(jnp.bfloat16)
    narrow = dot(ext_ref[...], pick_cols).astype(jnp.bfloat16)
    return dot(pick_rows, narrow[:ext_rows]), dot(pick_rows, narrow[ext_rows:])


def forward(groups, patch, direct, swapped, far_ref, exit_ref, at):
    patch_real, patch_imag = patch
    side = patch_real.shape[0]
    sums = []
    for group in groups:
        modes = group.shape[1]
        power = jnp.zeros((side, side), jnp.float32)
        weight = jnp.zeros((side, side), jnp.float32)
        halves = []
        for k in range(modes):
            real = group[0, k].astype(jnp.float32)
            imag = group[1, k].astype(jnp.float32)
            exit_wave = jnp.concatenate(
                [
                    (real * patch_real - imag * patch_imag).astype(jnp.bfloat16),
                    (real * patch_imag + imag * patch_real).astype(jnp.bfloat16),
                ],
                axis=0,
            )
            exit_ref[at + k] = exit_wave
            halves.append(wide(dot(direct, exit_wave).astype(jnp.bfloat16)))
            weight = weight + (real * real + imag * imag)
        far_both = dot(jnp.concatenate(halves, axis=0), swapped)
        for k in range(modes):
            far = far_both[k * side : (k + 1) * side]
            far_ref[at + k] = far
            power = power + (far[:, :side] * far[:, :side] + far[:, side:] * far[:, side:])
        sums.append((power, weight))
        at += modes
    return sums


def backward(groups, factor, direct, swapped, far_ref, exit_ref):
    side = factor.shape[0]
    grads = []
    at = 0
    for group in groups:
        modes = group.shape[1]
        grad_real = jnp.zeros((side, side), jnp.float32)
        grad_imag = jnp.zeros((side, side), jnp.float32)
        halves = []
        for k in range(modes):
            fixed = (far_ref[at + k] * factor).astype(jnp.bfloat16)
            halves.append(wide(dot(swapped, tall(fixed)).astype(jnp.bfloat16)))
        back_both = dot(jnp.concatenate(halves, axis=0), direct)
        for k in range(modes):
            back = back_both[k * side : (k + 1) * side]
            exit_wave = exit_ref[at + k].astype(jnp.float32)
            real = group[0, k].astype(jnp.float32)
            imag = group[1, k].astype(jnp.float32)
            diff_real = back[:, :side] - exit_wave[:side]
            diff_imag = back[:, side:] - exit_wave[side:]
            grad_real = grad_real + (real * diff_real + imag * diff_imag)
            grad_imag = grad_imag + (real * diff_imag - imag * diff_real)
        grads.append((grad_real, grad_imag))
        at += modes
    return grads


def near_kernel(sides, z_count, x_count, tile_rows, centers_ref, *refs):
    n_pieces = 3 + 3 * sides
    pieces = refs[:n_pieces]
    own, core, direct, swapped = refs[n_pieces : n_pieces + 4]
    patch_ref, far_ref, exit_ref, sum_ref, ext_ref = refs[n_pieces + 4 :]
    side = own.shape[2]
    patch = patch_of(sides, z_count, x_count, tile_rows, side, centers_ref, pieces, ext_ref)
    patch_ref[0], patch_ref[1] = patch
    sums = forward((own, core), patch, direct[...], swapped[...], far_ref, exit_ref, 0)
    sum_ref[0] = sums[0][0] + sums[1][0]
    sum_ref[1] = sums[0][1] + sums[1][1]


def far_kernel(patch_ref, group, direct, swapped, far_ref, exit_ref, sum_ref):
    patch = (patch_ref[0], patch_ref[1])
    ((power, weight),) = forward((group,), patch, direct[...], swapped[...], far_ref, exit_ref, 0)
    sum_ref[0] = power
    sum_ref[1] = weight


def back_kernel(sides, x_count, tile_rows, tile_cols, centers_ref, live_ref, *refs):
    n_pieces = 3 + 3 * sides
    amplitude_ref, patch_ref, own, core, over, last, direct_ref, swapped_ref = refs[:8]
    near_far, near_exit, near_sum, over_far, over_exit, over_sum = refs[8:14]
    outs = refs[14 : 14 + n_pieces + 1]
    last_far, last_exit, grad_ref = refs[14 + n_pieces + 1 :]
    side = own.shape[2]
    half = side // 2
    modes = own.shape[1]
    ext_rows = tile_rows + side
    ext_cols = tile_cols + sides * half
    _, x_index, parity = here()
    row_at = centers_ref[0, 0, parity, 0]
    col_at = centers_ref[0, 0, parity, 1]
    is_live = parity < live_ref[0, 0]
    direct = direct_ref[...]
    swapped = swapped_ref[...]
    patch = (patch_ref[0], patch_ref[1])
    ((power, weight),) = forward((last,), patch, direct, swapped, last_far, last_exit, 0)
    power = near_sum[0] + (over_sum[0] + power)
    weight = near_sum[1] + (over_sum[1] + weight)
    outs[-1][...] = weight.astype(jnp.bfloat16)
    amplitude = amplitude_ref[0, 0, parity].astype(jnp.float32)
    factor = amplitude / jnp.sqrt(power + power_floor)
    factor = jnp.concatenate([factor, factor], axis=1)
    near = backward((own, core), factor, direct, swapped, near_far, near_exit)
    (beyond,) = backward((over,), factor, direct, swapped, over_far, over_exit)
    (final,) = backward((last,), factor, direct, swapped, last_far, last_exit)
    at = iota((side, ext_cols), 1)
    column = column_coordinate(at, tile_cols, half, sides, x_index, x_count)
    put_cols = ((column == iota((side, ext_cols), 0) + col_at) & is_live).astype(jnp.bfloat16)
    put_rows = (iota((ext_rows, side), 0) == iota((ext_rows, side), 1) + row_at).astype(
        jnp.bfloat16
    )
    a_at, b_at = row_starts(half, tile_rows, parity)
    for channel in range(2):
        gradient = (near[0][channel] + near[1][channel]) + (beyond[channel] + final[channel])
        placed = dot(put_rows, gradient.astype(jnp.bfloat16)).astype(jnp.bfloat16)
        grad_ref[...] = dot(placed, put_cols).astype(jnp.bfloat16)
        for index in range(1 + sides):
            columns = (
                slice(0, tile_cols)
                if index == 0
                else slice(tile_cols + (index - 1) * half, tile_cols + index * half)
            )
            outs[3 * index][channel] = grad_ref[half : half + tile_rows, columns]
            outs[3 * index + 1][channel] = grad_ref[pl.ds(b_at, half), columns]
            outs[3 * index + 2][channel] = grad_ref[pl.ds(a_at, half), columns]


def weight_kernel(sides, slots, z_count, x_count, weight_ref, *refs):
    pieces, out_ref = refs[:-1], refs[-1]
    tile_rows, tile_cols = out_ref.shape
    side = weight_ref.shape[0]
    half = side // 2
    z_index, x_index, parity = here()
    z_step_a = jnp.where(parity == 0, -1, 1)
    if sides == 1:
        x_steps = [0, jnp.where(x_index == 0, 1, -1)]
        x_shown = [True, True]
    else:
        x_steps = [0, -1, 1]
        x_shown = [True, x_index > 0, x_index < x_count - 1]
    weight = weight_ref[...]
    total = jnp.zeros((tile_rows, tile_cols), jnp.float32)
    for index, x_step in enumerate(x_steps):
        turns = []
        for turn, z_step in enumerate((0, z_step_a, -z_step_a)):
            part = jnp.zeros((tile_rows, tile_cols), jnp.float32)
            z_tile = z_index + z_step
            shown = (z_tile >= 0) & (z_tile < z_count) & x_shown[index]
            record = pieces[3 * index + turn][2 * tile_rows :].astype(jnp.float32)
            record = record.astype(jnp.int32)
            if record.shape[1] < side:
                record = jnp.concatenate([record] * (side // record.shape[1]), axis=1)
            count = record[2 * slots : 2 * slots + 1, :side]
            for slot in range(slots):
                row = record[2 * slot : 2 * slot + 1, :side] + (z_step * tile_rows - half)
                col = record[2 * slot + 1 : 2 * slot + 2, :side] + (x_step * tile_cols - half)
                row = jnp.where((count > slot) & shown, row, nowhere)
                put_rows = (
                    iota((tile_rows, side), 0) == iota((tile_rows, side), 1) + row
                ).astype(jnp.bfloat16)
                put_cols = (
                    iota((side, tile_cols), 1) == iota((side, tile_cols), 0) + col[:, :1]
                ).astype(jnp.bfloat16)
                placed = dot(put_rows, weight).astype(jnp.bfloat16)
                part = part + dot(placed, put_cols)
            turns.append(part)
        total = total + (turns[0] + (turns[1] + turns[2]))
    out_ref[...] = total


def sum_kernel(sides, z_count, x_count, *refs):
    pieces, out_ref = refs[:-1], refs[-1]
    own_ref, rows_a, rows_b = pieces[:3]
    tile_cols = own_ref.shape[2]
    half = pieces[3].shape[2]
    z_index, x_index, parity = here()
    below = z_index > 0
    above = z_index < z_count - 1
    a_on = jnp.where(parity == 0, below, above)
    b_on = jnp.where(parity == 0, above, below)

    def gate(on, ref, channel):
        return jnp.where(on, ref[channel].astype(jnp.float32), 0.0)

    for channel in range(2):
        total = own_ref[channel].astype(jnp.float32)
        total = total + gate(a_on, rows_a, channel) + gate(b_on, rows_b, channel)
        first = jnp.zeros((total.shape[0], half), jnp.float32)
        last = first
        for index in range(sides):
            level, corner_a, corner_b = pieces[3 + 3 * index : 6 + 3 * index]
            edge = level[channel].astype(jnp.float32)
            edge = edge + gate(a_on, corner_a, channel) + gate(b_on, corner_b, channel)
            if sides == 1:
                first = jnp.where(x_index == 1, edge, 0.0)
                last = jnp.where(x_index == 0, edge, 0.0)
            elif index == 0:
                last = jnp.where(x_index < x_count - 1, edge, 0.0)
            else:
                first = jnp.where(x_index > 0, edge, 0.0)
        zero = jnp.zeros((total.shape[0], tile_cols - 2 * half), jnp.float32)
        parts = [first, zero, last] if tile_cols > 2 * half else [first, last]
        total = total + jnp.concatenate(parts, axis=1)
        out_ref[channel] = total.astype(jnp.bfloat16)


def smem():
    return pl.BlockSpec(memory_space=pltpu.SMEM)


def vmem():
    return pl.BlockSpec(memory_space=pltpu.VMEM)


def on_device(object_field, probe, amplitudes, centers, live):
    side = probe.shape[2]
    half = side // 2
    _, tile_rows, tile_cols = object_field.shape
    slots = centers.shape[2]
    z_count = lax.axis_size("tx")
    x_count = lax.axis_size("ty")
    m_count = lax.axis_size("mode")
    if tile_rows != half or slots != 2 or m_count != 4 or x_count < 2:
        raise ValueError("unsupported sizes")
    sides = 1 if x_count == 2 else 2
    axes = ("tx", "ty", "mode")

    def zigzag(flip, x_step):
        def moved(z, m):
            down = (m % 2 == 0) != flip
            if down:
                return (z + 1, m) if z < z_count - 1 else (z, m ^ 1)
            return (z - 1, m) if z > 0 else (z, m ^ 1)

        pairs = []
        for z in range(z_count):
            for x in range(x_count):
                for m in range(m_count):
                    z_to, m_to = moved(z, m)
                    x_to = (x + x_step) % x_count
                    pairs.append(
                        (
                            (z * x_count + x) * m_count + m,
                            (z_to * x_count + x_to) * m_count + m_to,
                        )
                    )
        return pairs

    def level(step):
        return [(x, (x + step) % x_count) for x in range(x_count)]

    def exchange(array, flip):
        return lax.ppermute(array, "mode", [(m, m ^ flip) for m in range(m_count)])

    probe_low = probe.astype(jnp.bfloat16)
    probe_y = exchange(probe_low, 2)
    probe_core = exchange(probe_low, 1)
    packed_rows = 2 * tile_rows + record_rows
    packed = pl.pallas_call(
        functools.partial(pack_kernel, sides, slots),
        out_shape=[jax.ShapeDtypeStruct((packed_rows, tile_cols), jnp.bfloat16)]
        + [jax.ShapeDtypeStruct((packed_rows, half), jnp.bfloat16)] * sides,
        in_specs=[smem(), smem(), vmem()],
        out_specs=[vmem()] * (1 + sides),
        name="pack",
    )(centers, live, object_field)
    x_steps = [1] if sides == 1 else [1, -1]
    pieces = [packed[0]]
    pieces += [lax.ppermute(packed[0], axes, zigzag(flip, 0)) for flip in (False, True)]
    for step, edge in zip(x_steps, packed[1:]):
        pieces.append(lax.ppermute(edge, "ty", level(step)))
        pieces += [lax.ppermute(edge, axes, zigzag(flip, step)) for flip in (False, True)]
    probe_y, probe_core, *pieces = lax.optimization_barrier((probe_y, probe_core, *pieces))
    probe_diagonal = exchange(probe_y, 1)

    n_pieces = len(pieces)
    modes = probe.shape[1]
    ext_rows = tile_rows + side
    ext_cols = tile_cols + sides * half
    direct, swapped = (jnp.asarray(matrix) for matrix in dft_matrices(side))

    def waves(count):
        return [
            jax.ShapeDtypeStruct((count, side, 2 * side), jnp.float32),
            jax.ShapeDtypeStruct((count, 2 * side, side), jnp.bfloat16),
            jax.ShapeDtypeStruct((2, side, side), jnp.float32),
        ]

    patch, *near = pl.pallas_call(
        functools.partial(near_kernel, sides, z_count, x_count, tile_rows),
        out_shape=[jax.ShapeDtypeStruct((2, side, side), jnp.float32)] + waves(2 * modes),
        in_specs=[smem()] + [vmem()] * (n_pieces + 4),
        out_specs=[vmem()] * 4,
        scratch_shapes=[pltpu.VMEM((2 * ext_rows, ext_cols), jnp.bfloat16)],
        compiler_params=pltpu.CompilerParams(vmem_limit_bytes=vmem_bytes),
        name="near",
    )(centers, *pieces, probe_low, probe_core, direct, swapped)
    over = pl.pallas_call(
        far_kernel,
        out_shape=waves(modes),
        in_specs=[vmem()] * 4,
        out_specs=[vmem()] * 3,
        compiler_params=pltpu.CompilerParams(vmem_limit_bytes=vmem_bytes),
        name="over",
    )(patch, probe_y, direct, swapped)
    shapes = [(2, tile_rows, tile_cols)] + [(2, half, tile_cols)] * 2
    shapes += ([(2, tile_rows, half)] + [(2, half, half)] * 2) * sides
    results = pl.pallas_call(
        functools.partial(back_kernel, sides, x_count, tile_rows, tile_cols),
        out_shape=[jax.ShapeDtypeStruct(shape, jnp.bfloat16) for shape in shapes]
        + [jax.ShapeDtypeStruct((side, side), jnp.bfloat16)],
        in_specs=[smem(), smem()] + [vmem()] * 14,
        out_specs=[vmem()] * (n_pieces + 1),
        scratch_shapes=[
            pltpu.VMEM((modes, side, 2 * side), jnp.float32),
            pltpu.VMEM((modes, 2 * side, side), jnp.bfloat16),
            pltpu.VMEM((ext_rows, ext_cols), jnp.bfloat16),
        ],
        compiler_params=pltpu.CompilerParams(vmem_limit_bytes=vmem_bytes),
        name="back",
    )(
        centers,
        live,
        amplitudes,
        patch,
        probe_low,
        probe_core,
        probe_y,
        probe_diagonal,
        direct,
        swapped,
        *near,
        *over,
    )
    weight = pl.pallas_call(
        functools.partial(weight_kernel, sides, slots, z_count, x_count),
        out_shape=jax.ShapeDtypeStruct((tile_rows, tile_cols), jnp.float32),
        in_specs=[vmem()] * (n_pieces + 1),
        out_specs=vmem(),
        name="weights",
    )(results[-1], *pieces)
    received = [results[0]]
    received += [
        lax.ppermute(results[1 + index], axes, zigzag(flip, 0))
        for index, flip in enumerate((False, True))
    ]
    for index, step in enumerate(x_steps):
        back_step = -step
        received.append(lax.ppermute(results[3 + 3 * index], "ty", level(back_step)))
        received += [
            lax.ppermute(results[4 + 3 * index + turn], axes, zigzag(flip, back_step))
            for turn, flip in enumerate((False, True))
        ]
    summed = pl.pallas_call(
        functools.partial(sum_kernel, sides, z_count, x_count),
        out_shape=jax.ShapeDtypeStruct(object_field.shape, jnp.bfloat16),
        in_specs=[vmem()] * n_pieces,
        out_specs=vmem(),
        name="sums",
    )(*received)
    other = exchange(summed, 1)
    gradient = summed.astype(jnp.float32) + other.astype(jnp.float32)
    return object_field + gradient / (weight + regularizer)


def solution(mesh):
    return jax.shard_map(
        on_device,
        mesh=mesh,
        in_specs=(
            P(None, "tx", "ty"),
            P(None, "mode", None, None),
            P("tx", "ty", None, None, None),
            P("tx", "ty", None, None),
            P("tx", "ty"),
        ),
        out_specs=P(None, "tx", "ty"),
        check_vma=False,
    )
```

time: 80.7 us -> 47.3 us (0.59)
  blocking collectives: 20.5 us -> 0 us
  waiting for transfers between devices: 18 us -> 8.25 us
  local copies, waits for them, and re-layouts: 7.9 us -> 3.59 us
  Pallas kernels: 13.7 us -> 15 us
    all_gather x1 -> x0, blocking collectives: 20.5 us -> none  [on_device(): table = lax.all_gather(record, ('tx', 'ty'), axis=0, tiled=True)]
    ppermute x4, waiting for transfers between devices: 13.5 us -> 0.64 us  [exchange(): return lax.ppermute(array, 'mode', [(m, m ^ flip) for m in range(m_count)])]
    ppermute x2, waiting for transfers between devices: 0.01 us -> 2.49 us  [on_device(): lax.ppermute(results[4 + 3 * index + turn], axes, zigzag(flip, back_step))]
    ppermute x1, waiting for transfers between devices: 0.16 us -> 2.5 us  [on_device(): pieces.append(lax.ppermute(edge, 'ty', level(step)))]
    ppermute x2, waiting for transfers between devices: 4.36 us -> 2.6 us  [on_device(): lax.ppermute(edge, axes, zigzag(flip, step))]
    unnamed x38 -> x34, local copies, waits for them, and re-layouts: 5.19 us -> 3.59 us
    pallas_call x2 -> x5, Pallas kernels: 11.8 us -> 13.2 us  [the longest x1 5.13 us: on_device(): pl.pallas_call(functools.partial(back_kernel, sides, x_count, tile_rows,...]
    another operation x1 -> x0, local copies, waits for them, and re-layouts: 1.34 us -> none  [on_device(): jnp.stack([centers[0, 0, slot, 0], centers[0, 0, slot, 1], (slot < live[0...]
  transfers between devices with their start and end apart: 14 -> 14, of which waited for: 4 -> 4; matrix products, arithmetic and copies ran while one was open for 5% -> 2% of each run, Pallas kernels for 3% -> 17%
where the time goes in v2:
time: 47.3 us; the launch traced here: 47 us
  starting transfers between devices  15.3 us (32%)
  Pallas kernels  15 us (32%)
  waiting for transfers between devices  8.25 us (17%)
  other arithmetic  4.02 us (8%)
  local copies, waits for them, and re-layouts  3.59 us (8%)
  between operations  0.87 us (2%)
    pallas_call x1, Pallas kernels, on_device(): pl.pallas_call(functools.partial(back_kernel, sides, x_count, tile_rows,...  5.13 us
    unnamed x34, local copies, waits for them, and re-layouts  3.59 us
    ppermute x4, starting transfers between devices, exchange(): return lax.ppermute(array, 'mode', [(m, m ^ flip) for m in range(m_count)])  3.18 us
    ppermute x2, starting transfers between devices, on_device(): lax.ppermute(edge, axes, zigzag(flip, step))  2.92 us
    pallas_call x1, Pallas kernels, on_device(): pl.pallas_call(functools.partial(near_kernel, sides, z_count, x_count, ti...  2.86 us
    add x2, other arithmetic, on_device(): return object_field + gradient / (weight + regularizer)  2.65 us
    pallas_call x1, Pallas kernels, on_device(): pl.pallas_call(functools.partial(weight_kernel, sides, slots, z_count, x_...  2.61 us
    ppermute x2, waiting for transfers between devices, on_device(): lax.ppermute(edge, axes, zigzag(flip, step))  2.6 us
  transfers between devices with their start and end apart: 14, of which 4 were waited for; matrix products, arithmetic and copies ran while one was open for 2% of the time, Pallas kernels for 17%

profile of v2, /device:TPU:0, one launch (start us, length us, event | category | flops | bytes accessed | tf_op | source)
XLA Modules:
  0.0 47.0 jit_solution(13161605908953990441)
XLA Ops:
  0.0 1.4 %convert_element_type.9.refs_6_.refs_2_ = bf16[2,2,256,256]{3,2,1,0:T(8,128)(2,1)S(1)} convert(f32[2,2,256,256]{3,2,1,0:T(8,128)} %param.8) | non-fusion elementwise | flops 262144 | bytes 1572864 | tf_op jit(solution)/shard_map/convert_element_type | solution.py:390
  1.4 0.5 %collective-permute-start.1 = (bf16[2,2,256,256]{3,2,1,0:T(8,128)(2,1)S(1)}, bf16[2,2,256,256]{3,2,1,0:T(8,128)(2,1)S(1)}, u32[]{:S(2)}, u32[]{:S(2)}) collective-permute-start(bf16[2,2,256,256]{3,2,1,0:T(8,128)(2,1)S(1)} %convert_element_type.9.refs_6_.refs_2_), channel_id=1, source_target_pairs={{0,1},{1,0},{2,3},{3,2},{4,5},{5,4},{6,7},{7,6},{8,9},{9,8},{10,11... | collective-permute-start | bytes 1572872 | tf_op jit(solution)/shard_map/ppermute | solution.py:388
  1.9 2.6 %collective-permute-start = (bf16[2,2,256,256]{3,2,1,0:T(8,128)(2,1)S(1)}, bf16[2,2,256,256]{3,2,1,0:T(8,128)(2,1)S(1)}, u32[]{:S(2)}, u32[]{:S(2)}) collective-permute-start(bf16[2,2,256,256]{3,2,1,0:T(8,128)(2,1)S(1)} %convert_element_type.9.refs_6_.refs_2_), channel_id=1, source_target_pairs={{0,2},{1,3},{2,0},{3,1},{4,6},{5,7},{6,4},{7,5},{8,10},{9,11},{10,... | collective-permute-start | bytes 1572872 | tf_op jit(solution)/shard_map/ppermute | solution.py:388
  5.1 0.0 copy-start.8
  5.1 1.7 %pack.1 = (bf16[272,256]{1,0:T(8,128)(2,1)}, bf16[272,128]{1,0:T(8,128)(2,1)}) custom-call(s32[1,1,2,2]{3,2,1,0:T(2,128)} %centers_ref.5, s32[1,1]{1,0:T(1,128)S(6)} %copy.8.live_ref, f32[2,128,256]{2,1,0:T(8,128)} %object_ref.1), custom_call_target="tpu_custom_call" | custom-call | tf_op jit(solution)/shard_map/pack/pallas_call | solution.py:394
  6.8 1.3 %collective-permute-start.6 = (bf16[272,128]{1,0:T(8,128)(2,1)}, bf16[272,128]{1,0:T(8,128)(2,1)S(1)}, u32[]{:S(2)}, u32[]{:S(2)}) collective-permute-start(bf16[272,128]{1,0:T(8,128)(2,1)} %get-tuple-element.30), channel_id=1, source_target_pairs={{0,5},{1,13},{2,7},{3,15},{4,1},{5,9},{6,3},{7,11},{8,4},{9,21},{1... | collective-permute-start | bytes 208904 | tf_op jit(solution)/shard_map/ppermute | solution.py:407
  8.1 1.7 %collective-permute-start.5 = (bf16[272,128]{1,0:T(8,128)(2,1)}, bf16[272,128]{1,0:T(8,128)(2,1)S(1)}, u32[]{:S(2)}, u32[]{:S(2)}) collective-permute-start(bf16[272,128]{1,0:T(8,128)(2,1)} %get-tuple-element.30), channel_id=1, source_target_pairs={{0,12},{1,4},{2,14},{3,6},{4,8},{5,0},{6,10},{7,2},{8,20},{9,5},{1... | collective-permute-start | bytes 208904 | tf_op jit(solution)/shard_map/ppermute | solution.py:407
  9.8 2.6 %collective-permute-done.6.refs_5_ = bf16[272,128]{1,0:T(8,128)(2,1)S(1)} collective-permute-done((bf16[272,128]{1,0:T(8,128)(2,1)}, bf16[272,128]{1,0:T(8,128)(2,1)S(1)}, u32[]{:S(2)}, u32[]{:S(2)}) %collective-permute-start.6) | collective-permute-done | bytes 69664 | tf_op jit(solution)/shard_map/ppermute | solution.py:407
  12.4 1.5 %collective-permute-start.2 = (bf16[272,256]{1,0:T(8,128)(2,1)}, bf16[272,256]{1,0:T(8,128)(2,1)S(1)}, u32[]{:S(2)}, u32[]{:S(2)}) collective-permute-start(bf16[272,256]{1,0:T(8,128)(2,1)} %get-tuple-element.31.refs_0_), channel_id=1, source_target_pairs={{0,8},{1,0},{2,10},{3,2},{4,12},{5,4},{6,14},{7,6},{8,16},{9,1},{1... | collective-permute-start | bytes 417800 | tf_op jit(solution)/shard_map/ppermute | solution.py:404
  13.9 2.3 %collective-permute-start.4 = (bf16[272,128]{1,0:T(8,128)(2,1)}, bf16[272,128]{1,0:T(8,128)(2,1)S(1)}, u32[]{:S(2)}, u32[]{:S(2)}) collective-permute-start(bf16[272,128]{1,0:T(8,128)(2,1)} %get-tuple-element.30), channel_id=1, source_target_pairs={{0,4},{4,0},{1,5},{5,1},{2,6},{6,2},{3,7},{7,3},{8,12},{12,8},{9,1... | collective-permute-start | bytes 208904 | tf_op jit(solution)/shard_map/ppermute | solution.py:406
  16.1 2.5 %collective-permute-done.4.refs_3_ = bf16[272,128]{1,0:T(8,128)(2,1)S(1)} collective-permute-done((bf16[272,128]{1,0:T(8,128)(2,1)}, bf16[272,128]{1,0:T(8,128)(2,1)S(1)}, u32[]{:S(2)}, u32[]{:S(2)}) %collective-permute-start.4) | collective-permute-done | bytes 69664 | tf_op jit(solution)/shard_map/ppermute | solution.py:406
  18.7 0.1 collective-permute-start.7
  18.8 0.9 %copy-done.2 = bf16[272,256]{1,0:T(8,128)(2,1)S(1)} copy-done((bf16[272,256]{1,0:T(8,128)(2,1)S(1)}, bf16[272,256]{1,0:T(8,128)(2,1)}, u32[]{:S(2)}) %copy-start.2) | copy-done | bytes 139288
  19.7 0.7 %copy-done.11 = s32[1,1,2,2]{3,2,1,0:T(2,128)S(1)} copy-done((s32[1,1,2,2]{3,2,1,0:T(2,128)S(1)}, s32[1,1,2,2]{3,2,1,0:T(2,128)}, u32[]{:S(2)}) %copy-start.11) | copy-done | bytes 40
  20.4 2.9 %near.1 = (f32[2,256,256]{2,1,0:T(8,128)S(1)}, f32[4,256,512]{2,1,0:T(8,128)S(1)}, bf16[4,512,256]{2,1,0:T(8,128)(2,1)S(1)}, f32[2,256,256]{2,1,0:T(8,128)S(1)}) custom-call(s32[1,1,2,2]{3,2,1,0:T(2,128)S(1)} %copy-done.11, bf16[272,256]{1,0:T(8,128)(2,1)S(1)} %copy-done.2, bf16[272,256]{1,0:T(8,128)(2,1)S(1)} %collective-permute-done.2.refs_1_, ...), custom_call_target="tpu_custom_call" | custom-call | tf_op jit(solution)/shard_map/near/pallas_call | solution.py:424
  23.2 0.9 %over.1 = (f32[2,256,512]{2,1,0:T(8,128)S(1)}, bf16[2,512,256]{2,1,0:T(8,128)(2,1)S(1)}, f32[2,256,256]{2,1,0:T(8,128)S(1)}) custom-call(f32[2,256,256]{2,1,0:T(8,128)S(1)} %get-tuple-element.38.patch_ref.refs_1_, bf16[2,2,256,256]{3,2,1,0:T(8,128)(2,1)S(1)} %collective-permute-done.group.refs_4_, bf16[512,512]{1,0:T(8,128)(2,1)S(1)} %copy-done.1, ...), custom_call_target="tpu_custom_call" | custom-call | tf_op jit(solution)/shard_map/over/pallas_call | solution.py:433
  24.2 5.1 %back.1 = (bf16[2,128,256]{2,1,0:T(8,128)(2,1)S(1)}, bf16[2,128,256]{2,1,0:T(8,128)(2,1)S(1)}, bf16[2,128,256]{2,1,0:T(8,128)(2,1)S(1)}, bf16[2,128,128]{2,1,0:T...) custom-call(s32[1,1,2,2]{3,2,1,0:T(2,128)S(1)} %copy-done.11, ...), custom_call_target="tpu_custom_call" | custom-call | tf_op jit(solution)/shard_map/back/pallas_call | solution.py:443
  29.3 0.6 %copy-done.9 = bf16[256,256]{1,0:T(8,128)(2,1)} copy-done((bf16[256,256]{1,0:T(8,128)(2,1)}, bf16[256,256]{1,0:T(8,128)(2,1)S(1)}, u32[]{:S(2)}) %copy-start.9) | copy-done | bytes 131096
  30.0 0.7 %copy-done.10 = bf16[2,128,256]{2,1,0:T(8,128)(2,1)} copy-done((bf16[2,128,256]{2,1,0:T(8,128)(2,1)}, bf16[2,128,256]{2,1,0:T(8,128)(2,1)S(1)}, u32[]{:S(2)}) %copy-start.10) | copy-done | bytes 131096
  30.6 1.9 %collective-permute-start.8 = (bf16[2,128,256]{2,1,0:T(8,128)(2,1)S(1)}, bf16[2,128,256]{2,1,0:T(8,128)(2,1)S(1)}, u32[]{:S(2)}, u32[]{:S(2)}) collective-permute-start(bf16[2,128,256]{2,1,0:T(8,128)(2,1)S(1)} %get-tuple-element.47), channel_id=1, source_target_pairs={{0,8},{1,0},{2,10},{3,2},{4,12},{5,4},{6,14},{7,6},{8,16},{9,1},{1... | collective-permute-start | bytes 393224 | tf_op jit(solution)/shard_map/ppermute | solution.py:479
  32.5 1.8 %collective-permute-start.10 = (bf16[2,128,128]{2,1,0:T(8,128)(2,1)S(1)}, bf16[2,128,128]{2,1,0:T(8,128)(2,1)S(1)}, u32[]{:S(2)}, u32[]{:S(2)}) collective-permute-start(bf16[2,128,128]{2,1,0:T(8,128)(2,1)S(1)} %get-tuple-element.49), channel_id=1, source_target_pairs={{0,4},{4,0},{1,5},{5,1},{2,6},{6,2},{3,7},{7,3},{8,12},{12,8},{9,1... | collective-permute-start | bytes 196616 | tf_op jit(solution)/shard_map/ppermute | solution.py:484
  34.3 1.7 %collective-permute-start.11 = (bf16[2,128,128]{2,1,0:T(8,128)(2,1)S(1)}, bf16[2,128,128]{2,1,0:T(8,128)(2,1)S(1)}, u32[]{:S(2)}, u32[]{:S(2)}) collective-permute-start(bf16[2,128,128]{2,1,0:T(8,128)(2,1)S(1)} %get-tuple-element.50), channel_id=1, source_target_pairs={{0,12},{1,4},{2,14},{3,6},{4,8},{5,0},{6,10},{7,2},{8,20},{9,5},{1... | collective-permute-start | bytes 196616 | tf_op jit(solution)/shard_map/ppermute | solution.py:486
  36.0 0.0 collective-permute-start.12
  36.0 2.6 %weights.1 = f32[128,256]{1,0:T(8,128)} custom-call(bf16[256,256]{1,0:T(8,128)(2,1)} %copy-done.9, bf16[272,256]{1,0:T(8,128)(2,1)} %get-tuple-element.31.refs_0_, bf16[272,256]{1,0:T(8,128)(2,1)} %copy-done.4, bf16[272,256]{1,0:T(8,128)(2,1)} %copy-done.3, bf16[272,128]{1,0:T(8,128)(2,1)} %copy-done.7, bf16[272,128]{1,0:T(8,128)(2,1)} %copy-done.6, ...), custom_call_target="tpu_custom_call" | custom-call | tf_op jit(solution)/shard_map/weights/pallas_call | solution.py:470
  38.7 2.5 %collective-permute-done.12.refs_5_ = bf16[2,128,128]{2,1,0:T(8,128)(2,1)S(1)} collective-permute-done((bf16[2,128,128]{2,1,0:T(8,128)(2,1)S(1)}, bf16[2,128,128]{2,1,0:T(8,128)(2,1)S(1)}, u32[]{:S(2)}, u32[]{:S(2)}) %collective-permute-start.12) | collective-permute-done | bytes 65568 | tf_op jit(solution)/shard_map/ppermute | solution.py:486
  41.2 0.6 %copy-done.16 = bf16[2,128,128]{2,1,0:T(8,128)(2,1)} copy-done((bf16[2,128,128]{2,1,0:T(8,128)(2,1)}, bf16[2,128,128]{2,1,0:T(8,128)(2,1)S(1)}, u32[]{:S(2)}) %copy-start.16) | copy-done | bytes 65560
  41.8 0.0 copy-done.12
  41.8 0.0 copy-done.13
  41.9 1.9 %sums.1 = bf16[2,128,256]{2,1,0:T(8,128)(2,1)} custom-call(bf16[2,128,256]{2,1,0:T(8,128)(2,1)} %copy-done.10, bf16[2,128,256]{2,1,0:T(8,128)(2,1)} %copy-done.12, bf16[2,128,256]{2,1,0:T(8,128)(2,1)} %copy-done.13, bf16[2,128,128]{2,1,0:T(8,128)(2,1)} %copy-done.14, bf16[2,128,128]{2,1,0:T(8,128)(2,1)} %copy-done.15, bf16[2,128,128]{2,1,0:T(8,128)(2,1)} %copy-done.16), custom_call_target="tpu_custom_call" | custom-call | tf_op jit(solution)/shard_map/sums/pallas_call | solution.py:489
  43.7 0.9 %broadcast_add_fusion = f32[128,256]{1,0:T(8,128)S(1)} fusion(f32[128,256]{1,0:T(8,128)} %weights.1), kind=kLoop, calls=%fused_computation.1 | loop fusion | flops 32768 | bytes 262144 | tf_op jit(solution)/shard_map/add | solution.py:498
  44.6 0.6 %collective-permute-done.13 = bf16[2,128,256]{2,1,0:T(8,128)(2,1)S(1)} collective-permute-done((bf16[2,128,256]{2,1,0:T(8,128)(2,1)}, bf16[2,128,256]{2,1,0:T(8,128)(2,1)S(1)}, u32[]{:S(2)}, u32[]{:S(2)}) %collective-permute-start.13) | collective-permute-done | bytes 131104 | tf_op jit(solution)/shard_map/ppermute | solution.py:388
  45.3 1.7 %divide_add_fusion = f32[2,128,256]{2,1,0:T(8,128)} fusion(f32[2,128,256]{2,1,0:T(8,128)} %object_ref.1, bf16[2,128,256]{2,1,0:T(8,128)(2,1)S(1)} %collective-permute-done.13, bf16[2,128,256]{2,1,0:T(8,128)(2,1)} %sums.1, f32[128,256]{1,0:T(8,128)S(1)} %broadcast_add_fusion), kind=kLoop, calls=%fused_computation | loop fusion | flops 327680 | bytes 917504 | tf_op jit(solution)/shard_map/add | solution.py:498
  (39 shorter events, 0.1 us)
Async XLA Ops:
  0.0 18.8 %copy-start = (bf16[512,512]{1,0:T(8,128)(2,1)S(1)}, bf16[512,512]{1,0:T(8,128)(2,1)}, u32[]{:S(2)}) copy-start(bf16[512,512]{1,0:T(8,128)(2,1)} %constant.7.clone.refs_9_.swapped.refs_7_) | copy-start | bytes 1572868
  0.0 18.8 %copy-start.1 = (bf16[512,512]{1,0:T(8,128)(2,1)S(1)}, bf16[512,512]{1,0:T(8,128)(2,1)}, u32[]{:S(2)}) copy-start(bf16[512,512]{1,0:T(8,128)(2,1)} %constant.6.clone.refs_8_.direct.refs_6_) | copy-start | bytes 1572868
  1.4 17.3 %collective-permute-start.1 = (bf16[2,2,256,256]{3,2,1,0:T(8,128)(2,1)S(1)}, bf16[2,2,256,256]{3,2,1,0:T(8,128)(2,1)S(1)}, u32[]{:S(2)}, u32[]{:S(2)}) collective-permute-start(bf16[2,2,256,256]{3,2,1,0:T(8,128)(2,1)S(1)} %convert_element_type.9.refs_6_.refs_2_), channel_id=1, source_target_pairs={{0,1},{1,0},{2,3},{3,2},{4,5},{5,4},{6,7},{7,6},{8,9},{9,8},{10,11... | collective-permute-start | bytes 1572872 | tf_op jit(solution)/shard_map/ppermute | solution.py:388
  1.9 16.8 %collective-permute-start = (bf16[2,2,256,256]{3,2,1,0:T(8,128)(2,1)S(1)}, bf16[2,2,256,256]{3,2,1,0:T(8,128)(2,1)S(1)}, u32[]{:S(2)}, u32[]{:S(2)}) collective-permute-start(bf16[2,2,256,256]{3,2,1,0:T(8,128)(2,1)S(1)} %convert_element_type.9.refs_6_.refs_2_), channel_id=1, source_target_pairs={{0,2},{1,3},{2,0},{3,1},{4,6},{5,7},{6,4},{7,5},{8,10},{9,11},{10,... | collective-permute-start | bytes 1572872 | tf_op jit(solution)/shard_map/ppermute | solution.py:388
  5.1 19.1 %copy-start.8 = (bf16[1,1,2,256,256]{4,3,2,1,0:T(8,128)(2,1)S(1)}, bf16[1,1,2,256,256]{4,3,2,1,0:T(8,128)(2,1)}, u32[]{:S(2)}) copy-start(bf16[1,1,2,256,256]{4,3,2,1,0:T(8,128)(2,1)} %refs_0_.1) | copy-start | bytes 786436
  6.8 5.5 %collective-permute-start.6 = (bf16[272,128]{1,0:T(8,128)(2,1)}, bf16[272,128]{1,0:T(8,128)(2,1)S(1)}, u32[]{:S(2)}, u32[]{:S(2)}) collective-permute-start(bf16[272,128]{1,0:T(8,128)(2,1)} %get-tuple-element.30), channel_id=1, source_target_pairs={{0,5},{1,13},{2,7},{3,15},{4,1},{5,9},{6,3},{7,11},{8,4},{9,21},{1... | collective-permute-start | bytes 208904 | tf_op jit(solution)/shard_map/ppermute | solution.py:407
  8.1 5.7 %collective-permute-start.5 = (bf16[272,128]{1,0:T(8,128)(2,1)}, bf16[272,128]{1,0:T(8,128)(2,1)S(1)}, u32[]{:S(2)}, u32[]{:S(2)}) collective-permute-start(bf16[272,128]{1,0:T(8,128)(2,1)} %get-tuple-element.30), channel_id=1, source_target_pairs={{0,12},{1,4},{2,14},{3,6},{4,8},{5,0},{6,10},{7,2},{8,20},{9,5},{1... | collective-permute-start | bytes 208904 | tf_op jit(solution)/shard_map/ppermute | solution.py:407
  9.8 8.9 %collective-permute-start.3 = (bf16[272,256]{1,0:T(8,128)(2,1)}, bf16[272,256]{1,0:T(8,128)(2,1)S(1)}, u32[]{:S(2)}, u32[]{:S(2)}) collective-permute-start(bf16[272,256]{1,0:T(8,128)(2,1)} %get-tuple-element.31.refs_0_), channel_id=1, source_target_pairs={{0,1},{1,9},{2,3},{3,11},{4,5},{5,13},{6,7},{7,15},{8,0},{9,17},{1... | collective-permute-start | bytes 417800 | tf_op jit(solution)/shard_map/ppermute | solution.py:404
  12.4 11.8 %copy-start.5 = (bf16[272,128]{1,0:T(8,128)(2,1)}, bf16[272,128]{1,0:T(8,128)(2,1)S(1)}, u32[]{:S(2)}) copy-start(bf16[272,128]{1,0:T(8,128)(2,1)S(1)} %collective-permute-done.6.refs_5_) | copy-start | bytes 208900
  12.4 6.3 %collective-permute-start.2 = (bf16[272,256]{1,0:T(8,128)(2,1)}, bf16[272,256]{1,0:T(8,128)(2,1)S(1)}, u32[]{:S(2)}, u32[]{:S(2)}) collective-permute-start(bf16[272,256]{1,0:T(8,128)(2,1)} %get-tuple-element.31.refs_0_), channel_id=1, source_target_pairs={{0,8},{1,0},{2,10},{3,2},{4,12},{5,4},{6,14},{7,6},{8,16},{9,1},{1... | collective-permute-start | bytes 417800 | tf_op jit(solution)/shard_map/ppermute | solution.py:404
  13.9 10.3 %copy-start.6 = (bf16[272,128]{1,0:T(8,128)(2,1)}, bf16[272,128]{1,0:T(8,128)(2,1)S(1)}, u32[]{:S(2)}) copy-start(bf16[272,128]{1,0:T(8,128)(2,1)S(1)} %collective-permute-done.5.refs_4_) | copy-start | bytes 208900
  13.9 4.8 %collective-permute-start.4 = (bf16[272,128]{1,0:T(8,128)(2,1)}, bf16[272,128]{1,0:T(8,128)(2,1)S(1)}, u32[]{:S(2)}, u32[]{:S(2)}) collective-permute-start(bf16[272,128]{1,0:T(8,128)(2,1)} %get-tuple-element.30), channel_id=1, source_target_pairs={{0,4},{4,0},{1,5},{5,1},{2,6},{6,2},{3,7},{7,3},{8,12},{12,8},{9,1... | collective-permute-start | bytes 208904 | tf_op jit(solution)/shard_map/ppermute | solution.py:406
  18.6 5.5 %copy-start.7 = (bf16[272,128]{1,0:T(8,128)(2,1)}, bf16[272,128]{1,0:T(8,128)(2,1)S(1)}, u32[]{:S(2)}) copy-start(bf16[272,128]{1,0:T(8,128)(2,1)S(1)} %collective-permute-done.4.refs_3_) | copy-start | bytes 208900
  18.6 5.5 %copy-start.3 = (bf16[272,256]{1,0:T(8,128)(2,1)}, bf16[272,256]{1,0:T(8,128)(2,1)S(1)}, u32[]{:S(2)}) copy-start(bf16[272,256]{1,0:T(8,128)(2,1)S(1)} %collective-permute-done.3.refs_2_) | copy-start | bytes 417796
  18.7 5.5 %copy-start.4 = (bf16[272,256]{1,0:T(8,128)(2,1)}, bf16[272,256]{1,0:T(8,128)(2,1)S(1)}, u32[]{:S(2)}) copy-start(bf16[272,256]{1,0:T(8,128)(2,1)S(1)} %collective-permute-done.2.refs_1_) | copy-start | bytes 417796
  18.7 5.5 %collective-permute-start.7 = (bf16[2,2,256,256]{3,2,1,0:T(8,128)(2,1)S(1)}, bf16[2,2,256,256]{3,2,1,0:T(8,128)(2,1)S(1)}, u32[]{:S(2)}, u32[]{:S(2)}) collective-permute-start(bf16[2,2,256,256]{3,2,1,0:T(8,128)(2,1)S(1)} %collective-permute-done.group.refs_4_), channel_id=1, source_target_pairs={{0,1},{1,0},{2,3},{3,2},{4,5},{5,4},{6,7},{7,6},{8,9},{9,8},{10,11... | collective-permute-start | bytes 1572872 | tf_op jit(solution)/shard_map/ppermute | solution.py:388
  18.8 0.9 %copy-start.2 = (bf16[272,256]{1,0:T(8,128)(2,1)S(1)}, bf16[272,256]{1,0:T(8,128)(2,1)}, u32[]{:S(2)}) copy-start(bf16[272,256]{1,0:T(8,128)(2,1)} %get-tuple-element.31.refs_0_) | copy-start | bytes 417796
  19.7 0.7 %copy-start.11 = (s32[1,1,2,2]{3,2,1,0:T(2,128)S(1)}, s32[1,1,2,2]{3,2,1,0:T(2,128)}, u32[]{:S(2)}) copy-start(s32[1,1,2,2]{3,2,1,0:T(2,128)} %centers_ref.5) | copy-start | bytes 52
  29.3 0.7 %copy-start.9 = (bf16[256,256]{1,0:T(8,128)(2,1)}, bf16[256,256]{1,0:T(8,128)(2,1)S(1)}, u32[]{:S(2)}) copy-start(bf16[256,256]{1,0:T(8,128)(2,1)S(1)} %get-tuple-element.52.weight_ref) | copy-start | bytes 393220
  30.0 0.7 %copy-start.10 = (bf16[2,128,256]{2,1,0:T(8,128)(2,1)}, bf16[2,128,256]{2,1,0:T(8,128)(2,1)S(1)}, u32[]{:S(2)}) copy-start(bf16[2,128,256]{2,1,0:T(8,128)(2,1)S(1)} %get-tuple-element.46.refs_0_) | copy-start | bytes 393220
  30.6 10.5 %collective-permute-start.8 = (bf16[2,128,256]{2,1,0:T(8,128)(2,1)S(1)}, bf16[2,128,256]{2,1,0:T(8,128)(2,1)S(1)}, u32[]{:S(2)}, u32[]{:S(2)}) collective-permute-start(bf16[2,128,256]{2,1,0:T(8,128)(2,1)S(1)} %get-tuple-element.47), channel_id=1, source_target_pairs={{0,8},{1,0},{2,10},{3,2},{4,12},{5,4},{6,14},{7,6},{8,16},{9,1},{1... | collective-permute-start | bytes 393224 | tf_op jit(solution)/shard_map/ppermute | solution.py:479
  32.5 8.7 %collective-permute-start.9 = (bf16[2,128,256]{2,1,0:T(8,128)(2,1)S(1)}, bf16[2,128,256]{2,1,0:T(8,128)(2,1)S(1)}, u32[]{:S(2)}, u32[]{:S(2)}) collective-permute-start(bf16[2,128,256]{2,1,0:T(8,128)(2,1)S(1)} %get-tuple-element.48), channel_id=1, source_target_pairs={{0,1},{1,9},{2,3},{3,11},{4,5},{5,13},{6,7},{7,15},{8,0},{9,17},{1... | collective-permute-start | bytes 393224 | tf_op jit(solution)/shard_map/ppermute | solution.py:479
  32.5 6.1 %collective-permute-start.10 = (bf16[2,128,128]{2,1,0:T(8,128)(2,1)S(1)}, bf16[2,128,128]{2,1,0:T(8,128)(2,1)S(1)}, u32[]{:S(2)}, u32[]{:S(2)}) collective-permute-start(bf16[2,128,128]{2,1,0:T(8,128)(2,1)S(1)} %get-tuple-element.49), channel_id=1, source_target_pairs={{0,4},{4,0},{1,5},{5,1},{2,6},{6,2},{3,7},{7,3},{8,12},{12,8},{9,1... | collective-permute-start | bytes 196616 | tf_op jit(solution)/shard_map/ppermute | solution.py:484
  34.3 4.4 %collective-permute-start.11 = (bf16[2,128,128]{2,1,0:T(8,128)(2,1)S(1)}, bf16[2,128,128]{2,1,0:T(8,128)(2,1)S(1)}, u32[]{:S(2)}, u32[]{:S(2)}) collective-permute-start(bf16[2,128,128]{2,1,0:T(8,128)(2,1)S(1)} %get-tuple-element.50), channel_id=1, source_target_pairs={{0,12},{1,4},{2,14},{3,6},{4,8},{5,0},{6,10},{7,2},{8,20},{9,5},{1... | collective-permute-start | bytes 196616 | tf_op jit(solution)/shard_map/ppermute | solution.py:486
  36.0 5.2 %collective-permute-start.12 = (bf16[2,128,128]{2,1,0:T(8,128)(2,1)S(1)}, bf16[2,128,128]{2,1,0:T(8,128)(2,1)S(1)}, u32[]{:S(2)}, u32[]{:S(2)}) collective-permute-start(bf16[2,128,128]{2,1,0:T(8,128)(2,1)S(1)} %get-tuple-element.51), channel_id=1, source_target_pairs={{0,5},{1,13},{2,7},{3,15},{4,1},{5,9},{6,3},{7,11},{8,4},{9,21},{1... | collective-permute-start | bytes 196616 | tf_op jit(solution)/shard_map/ppermute | solution.py:486
  38.6 2.5 %copy-start.14 = (bf16[2,128,128]{2,1,0:T(8,128)(2,1)}, bf16[2,128,128]{2,1,0:T(8,128)(2,1)S(1)}, u32[]{:S(2)}) copy-start(bf16[2,128,128]{2,1,0:T(8,128)(2,1)S(1)} %collective-permute-done.10.refs_3_) | copy-start | bytes 196612
  38.6 2.5 %copy-start.15 = (bf16[2,128,128]{2,1,0:T(8,128)(2,1)}, bf16[2,128,128]{2,1,0:T(8,128)(2,1)S(1)}, u32[]{:S(2)}) copy-start(bf16[2,128,128]{2,1,0:T(8,128)(2,1)S(1)} %collective-permute-done.11.refs_4_) | copy-start | bytes 196612
  41.1 0.6 %copy-start.16 = (bf16[2,128,128]{2,1,0:T(8,128)(2,1)}, bf16[2,128,128]{2,1,0:T(8,128)(2,1)S(1)}, u32[]{:S(2)}) copy-start(bf16[2,128,128]{2,1,0:T(8,128)(2,1)S(1)} %collective-permute-done.12.refs_5_) | copy-start | bytes 196612
  41.2 0.7 %copy-start.12 = (bf16[2,128,256]{2,1,0:T(8,128)(2,1)}, bf16[2,128,256]{2,1,0:T(8,128)(2,1)S(1)}, u32[]{:S(2)}) copy-start(bf16[2,128,256]{2,1,0:T(8,128)(2,1)S(1)} %collective-permute-done.8.refs_1_) | copy-start | bytes 393220
  41.2 0.7 %copy-start.13 = (bf16[2,128,256]{2,1,0:T(8,128)(2,1)}, bf16[2,128,256]{2,1,0:T(8,128)(2,1)S(1)}, u32[]{:S(2)}) copy-start(bf16[2,128,256]{2,1,0:T(8,128)(2,1)S(1)} %collective-permute-done.9.refs_2_) | copy-start | bytes 393220
  43.7 1.6 %collective-permute-start.13 = (bf16[2,128,256]{2,1,0:T(8,128)(2,1)}, bf16[2,128,256]{2,1,0:T(8,128)(2,1)S(1)}, u32[]{:S(2)}, u32[]{:S(2)}) collective-permute-start(bf16[2,128,256]{2,1,0:T(8,128)(2,1)} %sums.1), channel_id=1, source_target_pairs={{0,1},{1,0},{2,3},{3,2},{4,5},{5,4},{6,7},{7,6},{8,9},{9,8},{10,11... | collective-permute-start | bytes 393224 | tf_op jit(solution)/shard_map/ppermute | solution.py:388

commit v3 on v2

--- a/solution.py
+++ b/solution.py
@@ -13,7 +13,8 @@
 regularizer = 0.1
 nowhere = -(1 << 20)
 record_rows = 16
-vmem_bytes = 40 * 1024 * 1024
+wave_bytes = 32 * 1024 * 1024
+small_bytes = 8 * 1024 * 1024
 
 
 def dft_matrices(side):
@@ -300,7 +301,7 @@
                 part = part + dot(placed, put_cols)
             turns.append(part)
         total = total + (turns[0] + (turns[1] + turns[2]))
-    out_ref[...] = total
+    out_ref[...] = total + regularizer
 
 
 def sum_kernel(sides, z_count, x_count, *refs):
@@ -339,6 +340,12 @@
         out_ref[channel] = total.astype(jnp.bfloat16)
 
 
+def update_kernel(object_ref, own_ref, other_ref, weight_ref, out_ref):
+    for channel in range(2):
+        gradient = own_ref[channel].astype(jnp.float32) + other_ref[channel].astype(jnp.float32)
+        out_ref[channel] = object_ref[channel] + gradient / weight_ref[...]
+
+
 def smem():
     return pl.BlockSpec(memory_space=pltpu.SMEM)
 
@@ -397,16 +404,16 @@
         + [jax.ShapeDtypeStruct((packed_rows, half), jnp.bfloat16)] * sides,
         in_specs=[smem(), smem(), vmem()],
         out_specs=[vmem()] * (1 + sides),
+        compiler_params=pltpu.CompilerParams(vmem_limit_bytes=small_bytes),
         name="pack",
     )(centers, live, object_field)
+    probe_core, *packed = lax.optimization_barrier((probe_core, *packed))
     x_steps = [1] if sides == 1 else [1, -1]
     pieces = [packed[0]]
     pieces += [lax.ppermute(packed[0], axes, zigzag(flip, 0)) for flip in (False, True)]
     for step, edge in zip(x_steps, packed[1:]):
         pieces.append(lax.ppermute(edge, "ty", level(step)))
         pieces += [lax.ppermute(edge, axes, zigzag(flip, step)) for flip in (False, True)]
-    probe_y, probe_core, *pieces = lax.optimization_barrier((probe_y, probe_core, *pieces))
-    probe_diagonal = exchange(probe_y, 1)
 
     n_pieces = len(pieces)
     modes = probe.shape[1]
@@ -427,15 +434,17 @@
         in_specs=[smem()] + [vmem()] * (n_pieces + 4),
         out_specs=[vmem()] * 4,
         scratch_shapes=[pltpu.VMEM((2 * ext_rows, ext_cols), jnp.bfloat16)],
-        compiler_params=pltpu.CompilerParams(vmem_limit_bytes=vmem_bytes),
+        compiler_params=pltpu.CompilerParams(vmem_limit_bytes=wave_bytes),
         name="near",
     )(centers, *pieces, probe_low, probe_core, direct, swapped)
+    probe_y, patch = lax.optimization_barrier((probe_y, patch))
+    probe_diagonal = exchange(probe_y, 1)
     over = pl.pallas_call(
         far_kernel,
         out_shape=waves(modes),
         in_specs=[vmem()] * 4,
         out_specs=[vmem()] * 3,
-        compiler_params=pltpu.CompilerParams(vmem_limit_bytes=vmem_bytes),
+        compiler_params=pltpu.CompilerParams(vmem_limit_bytes=wave_bytes),
         name="over",
     )(patch, probe_y, direct, swapped)
     shapes = [(2, tile_rows, tile_cols)] + [(2, half, tile_cols)] * 2
@@ -451,7 +460,7 @@
             pltpu.VMEM((modes, 2 * side, side), jnp.bfloat16),
             pltpu.VMEM((ext_rows, ext_cols), jnp.bfloat16),
         ],
-        compiler_params=pltpu.CompilerParams(vmem_limit_bytes=vmem_bytes),
+        compiler_params=pltpu.CompilerParams(vmem_limit_bytes=wave_bytes),
         name="back",
     )(
         centers,
@@ -472,6 +481,7 @@
         out_shape=jax.ShapeDtypeStruct((tile_rows, tile_cols), jnp.float32),
         in_specs=[vmem()] * (n_pieces + 1),
         out_specs=vmem(),
+        compiler_params=pltpu.CompilerParams(vmem_limit_bytes=small_bytes),
         name="weights",
     )(results[-1], *pieces)
     received = [results[0]]
@@ -486,16 +496,24 @@
             lax.ppermute(results[4 + 3 * index + turn], axes, zigzag(flip, back_step))
             for turn, flip in enumerate((False, True))
         ]
+    weight, *received = lax.optimization_barrier((weight, *received))
     summed = pl.pallas_call(
         functools.partial(sum_kernel, sides, z_count, x_count),
         out_shape=jax.ShapeDtypeStruct(object_field.shape, jnp.bfloat16),
         in_specs=[vmem()] * n_pieces,
         out_specs=vmem(),
+        compiler_params=pltpu.CompilerParams(vmem_limit_bytes=small_bytes),
         name="sums",
     )(*received)
     other = exchange(summed, 1)
-    gradient = summed.astype(jnp.float32) + other.astype(jnp.float32)
-    return object_field + gradient / (weight + regularizer)
+    return pl.pallas_call(
+        update_kernel,
+        out_shape=jax.ShapeDtypeStruct(object_field.shape, jnp.float32),
+        in_specs=[vmem()] * 4,
+        out_specs=vmem(),
+        compiler_params=pltpu.CompilerParams(vmem_limit_bytes=small_bytes),
+        name="update",
+    )(object_field, summed, other, weight)
 
 
 def solution(mesh):

time: 47.3 us -> 41.3 us (0.87)
  Pallas kernels: 15 us -> 11.3 us
  other arithmetic: 4.02 us -> 1.37 us
  waiting for transfers between devices: 8.25 us -> 10 us
  local copies, waits for them, and re-layouts: 3.59 us -> 2.32 us
    add x2 -> x0, other arithmetic: 2.65 us -> none  [on_device(): return object_field + gradient / (weight + regularizer)]
    pallas_call x1, Pallas kernels: 2.61 us -> 0.74 us  [on_device(): pl.pallas_call(functools.partial(weight_kernel, sides, slots, z_count, x_...]
    pallas_call x1, Pallas kernels: 1.87 us -> 0.14 us  [on_device(): pl.pallas_call(functools.partial(sum_kernel, sides, z_count, x_count), ou...]
    ppermute x4, waiting for transfers between devices: 0.64 us -> 2.34 us  [exchange(): return lax.ppermute(array, 'mode', [(m, m ^ flip) for m in range(m_count)])]
    ppermute x2, waiting for transfers between devices: 2.49 us -> 3.98 us  [on_device(): lax.ppermute(results[4 + 3 * index + turn], axes, zigzag(flip, back_step))]
    unnamed x34 -> x14, local copies, waits for them, and re-layouts: 3.59 us -> 2.32 us
    ppermute x2, waiting for transfers between devices: 2.6 us -> 1.36 us  [on_device(): lax.ppermute(edge, axes, zigzag(flip, step))]
    pallas_call x1, Pallas kernels: 1.7 us -> 0.58 us  [on_device(): pl.pallas_call(functools.partial(pack_kernel, sides, slots), out_shape=[j...]
  transfers between devices with their start and end apart: 14 -> 14, of which waited for: 4 -> 8; matrix products, arithmetic and copies ran while one was open for 2% -> 0% of each run, Pallas kernels for 17% -> 13%
where the time goes in v3:
time: 41.3 us; the launch traced here: 41.1 us
  starting transfers between devices  15.3 us (37%)
  Pallas kernels  11.3 us (27%)
  waiting for transfers between devices  10 us (24%)
  local copies, waits for them, and re-layouts  2.32 us (6%)
  other arithmetic  1.37 us (3%)
  between operations  0.78 us (2%)
    pallas_call x1, Pallas kernels, on_device(): pl.pallas_call(functools.partial(back_kernel, sides, x_count, tile_rows,...  5.23 us
    ppermute x2, waiting for transfers between devices, on_device(): lax.ppermute(results[4 + 3 * index + turn], axes, zigzag(flip, back_step))  3.98 us
    ppermute x4, starting transfers between devices, exchange(): return lax.ppermute(array, 'mode', [(m, m ^ flip) for m in range(m_count)])  3.25 us
    ppermute x2, starting transfers between devices, on_device(): lax.ppermute(edge, axes, zigzag(flip, step))  2.98 us
    pallas_call x1, Pallas kernels, on_device(): pl.pallas_call(functools.partial(near_kernel, sides, z_count, x_count, ti...  2.95 us
    ppermute x4, waiting for transfers between devices, exchange(): return lax.ppermute(array, 'mode', [(m, m ^ flip) for m in range(m_count)])  2.34 us
    unnamed x14, local copies, waits for them, and re-layouts  2.32 us
    ppermute x2, starting transfers between devices, on_device(): lax.ppermute(results[1 + index], axes, zigzag(flip, 0))  2.09 us
  transfers between devices with their start and end apart: 14, of which 8 were waited for; matrix products, arithmetic and copies ran while one was open for 0% of the time, Pallas kernels for 13%

profile of v3, /device:TPU:0, one launch (start us, length us, event | category | flops | bytes accessed | tf_op | source)
XLA Modules:
  0.0 41.1 jit_solution(16382255129027687790)
XLA Ops:
  0.0 1.4 %convert_element_type.3.refs_6_.refs_2_ = bf16[2,2,256,256]{3,2,1,0:T(8,128)(2,1)S(1)} convert(f32[2,2,256,256]{3,2,1,0:T(8,128)} %param.8) | non-fusion elementwise | flops 262144 | bytes 1572864 | tf_op jit(solution)/shard_map/convert_element_type | solution.py:397
  1.4 0.5 %collective-permute-start.1 = (bf16[2,2,256,256]{3,2,1,0:T(8,128)(2,1)S(1)}, bf16[2,2,256,256]{3,2,1,0:T(8,128)(2,1)S(1)}, u32[]{:S(2)}, u32[]{:S(2)}) collective-permute-start(bf16[2,2,256,256]{3,2,1,0:T(8,128)(2,1)S(1)} %convert_element_type.3.refs_6_.refs_2_), channel_id=1, source_target_pairs={{0,1},{1,0},{2,3},{3,2},{4,5},{5,4},{6,7},{7,6},{8,9},{9,8},{10,11... | collective-permute-start | bytes 1572872 | tf_op jit(solution)/shard_map/ppermute | solution.py:395
  1.9 2.6 %collective-permute-start = (bf16[2,2,256,256]{3,2,1,0:T(8,128)(2,1)S(1)}, bf16[2,2,256,256]{3,2,1,0:T(8,128)(2,1)S(1)}, u32[]{:S(2)}, u32[]{:S(2)}) collective-permute-start(bf16[2,2,256,256]{3,2,1,0:T(8,128)(2,1)S(1)} %convert_element_type.3.refs_6_.refs_2_), channel_id=1, source_target_pairs={{0,2},{1,3},{2,0},{3,1},{4,6},{5,7},{6,4},{7,5},{8,10},{9,11},{10,... | collective-permute-start | bytes 1572872 | tf_op jit(solution)/shard_map/ppermute | solution.py:395
  5.1 0.0 copy-start.2
  5.1 0.9 %copy-done.2 = f32[2,128,256]{2,1,0:T(8,128)S(1)} copy-done((f32[2,128,256]{2,1,0:T(8,128)S(1)}, f32[2,128,256]{2,1,0:T(8,128)}, u32[]{:S(2)}) %copy-start.2) | copy-done | bytes 262168
  6.1 0.7 %copy-done.5 = s32[1,1,2,2]{3,2,1,0:T(2,128)S(1)} copy-done((s32[1,1,2,2]{3,2,1,0:T(2,128)S(1)}, s32[1,1,2,2]{3,2,1,0:T(2,128)}, u32[]{:S(2)}) %copy-start.5) | copy-done | bytes 40
  6.8 0.6 %pack.1 = (bf16[272,256]{1,0:T(8,128)(2,1)S(1)}, bf16[272,128]{1,0:T(8,128)(2,1)S(1)}) custom-call(s32[1,1,2,2]{3,2,1,0:T(2,128)S(1)} %copy-done.5, s32[1,1]{1,0:T(1,128)S(6)} %copy.8.live_ref, f32[2,128,256]{2,1,0:T(8,128)S(1)} %copy-done.2), custom_call_target="tpu_custom_call" | custom-call | tf_op jit(solution)/shard_map/pack/pallas_call | solution.py:401
  7.4 1.3 %collective-permute-start.6 = (bf16[272,128]{1,0:T(8,128)(2,1)S(1)}, bf16[272,128]{1,0:T(8,128)(2,1)S(1)}, u32[]{:S(2)}, u32[]{:S(2)}) collective-permute-start(bf16[272,128]{1,0:T(8,128)(2,1)S(1)} %get-tuple-element.36), channel_id=1, source_target_pairs={{0,5},{1,13},{2,7},{3,15},{4,1},{5,9},{6,3},{7,11},{8,4},{9,21},{1... | collective-permute-start | bytes 208904 | tf_op jit(solution)/shard_map/ppermute | solution.py:416
  8.7 1.1 %collective-permute-start.3 = (bf16[272,256]{1,0:T(8,128)(2,1)S(1)}, bf16[272,256]{1,0:T(8,128)(2,1)S(1)}, u32[]{:S(2)}, u32[]{:S(2)}) collective-permute-start(bf16[272,256]{1,0:T(8,128)(2,1)S(1)} %get-tuple-element.35.refs_0_), channel_id=1, source_target_pairs={{0,1},{1,9},{2,3},{3,11},{4,5},{5,13},{6,7},{7,15},{8,0},{9,17},{1... | collective-permute-start | bytes 417800 | tf_op jit(solution)/shard_map/ppermute | solution.py:413
  9.8 0.9 %collective-permute-start.2 = (bf16[272,256]{1,0:T(8,128)(2,1)S(1)}, bf16[272,256]{1,0:T(8,128)(2,1)S(1)}, u32[]{:S(2)}, u32[]{:S(2)}) collective-permute-start(bf16[272,256]{1,0:T(8,128)(2,1)S(1)} %get-tuple-element.35.refs_0_), channel_id=1, source_target_pairs={{0,8},{1,0},{2,10},{3,2},{4,12},{5,4},{6,14},{7,6},{8,16},{9,1},{1... | collective-permute-start | bytes 417800 | tf_op jit(solution)/shard_map/ppermute | solution.py:413
  10.7 1.7 %collective-permute-start.5 = (bf16[272,128]{1,0:T(8,128)(2,1)S(1)}, bf16[272,128]{1,0:T(8,128)(2,1)S(1)}, u32[]{:S(2)}, u32[]{:S(2)}) collective-permute-start(bf16[272,128]{1,0:T(8,128)(2,1)S(1)} %get-tuple-element.36), channel_id=1, source_target_pairs={{0,12},{1,4},{2,14},{3,6},{4,8},{5,0},{6,10},{7,2},{8,20},{9,5},{1... | collective-permute-start | bytes 208904 | tf_op jit(solution)/shard_map/ppermute | solution.py:416
  12.4 0.3 collective-permute-done.6.refs_5_
  12.6 1.5 %collective-permute-start.4 = (bf16[272,128]{1,0:T(8,128)(2,1)S(1)}, bf16[272,128]{1,0:T(8,128)(2,1)S(1)}, u32[]{:S(2)}, u32[]{:S(2)}) collective-permute-start(bf16[272,128]{1,0:T(8,128)(2,1)S(1)} %get-tuple-element.36), channel_id=1, source_target_pairs={{0,4},{4,0},{1,5},{5,1},{2,6},{6,2},{3,7},{7,3},{8,12},{12,8},{9,1... | collective-permute-start | bytes 208904 | tf_op jit(solution)/shard_map/ppermute | solution.py:415
  14.1 1.1 %collective-permute-done.5.refs_4_ = bf16[272,128]{1,0:T(8,128)(2,1)S(1)} collective-permute-done((bf16[272,128]{1,0:T(8,128)(2,1)S(1)}, bf16[272,128]{1,0:T(8,128)(2,1)S(1)}, u32[]{:S(2)}, u32[]{:S(2)}) %collective-permute-start.5) | collective-permute-done | bytes 69664 | tf_op jit(solution)/shard_map/ppermute | solution.py:416
  15.2 1.9 %collective-permute-done.4.refs_3_ = bf16[272,128]{1,0:T(8,128)(2,1)S(1)} collective-permute-done((bf16[272,128]{1,0:T(8,128)(2,1)S(1)}, bf16[272,128]{1,0:T(8,128)(2,1)S(1)}, u32[]{:S(2)}, u32[]{:S(2)}) %collective-permute-start.4) | collective-permute-done | bytes 69664 | tf_op jit(solution)/shard_map/ppermute | solution.py:415
  17.2 0.7 %copy-done.6 = s32[1,1,2,2]{3,2,1,0:T(2,128)S(1)} copy-done((s32[1,1,2,2]{3,2,1,0:T(2,128)S(1)}, s32[1,1,2,2]{3,2,1,0:T(2,128)}, u32[]{:S(2)}) %copy-start.6) | copy-done | bytes 40
  17.8 3.0 %near.1 = (f32[2,256,256]{2,1,0:T(8,128)S(1)}, f32[4,256,512]{2,1,0:T(8,128)S(1)}, bf16[4,512,256]{2,1,0:T(8,128)(2,1)S(1)}, f32[2,256,256]{2,1,0:T(8,128)S(1)}) custom-call(s32[1,1,2,2]{3,2,1,0:T(2,128)S(1)} %copy-done.6, bf16[272,256]{1,0:T(8,128)(2,1)S(1)} %get-tuple-element.35.refs_0_, bf16[272,256]{1,0:T(8,128)(2,1)S(1)} %collective-permute-done.2.refs_1_, ...), custom_call_target="tpu_custom_call" | custom-call | tf_op jit(solution)/shard_map/near/pallas_call | solution.py:431
  20.8 0.1 collective-permute-start.7
  20.9 0.9 %over.1 = (f32[2,256,512]{2,1,0:T(8,128)S(1)}, bf16[2,512,256]{2,1,0:T(8,128)(2,1)S(1)}, f32[2,256,256]{2,1,0:T(8,128)S(1)}) custom-call(f32[2,256,256]{2,1,0:T(8,128)S(1)} %get-tuple-element.39.patch_ref.refs_1_, bf16[2,2,256,256]{3,2,1,0:T(8,128)(2,1)S(1)} %collective-permute-done.group.refs_4_, bf16[512,512]{1,0:T(8,128)(2,1)S(1)} %copy-done.1, ...), custom_call_target="tpu_custom_call" | custom-call | tf_op jit(solution)/shard_map/over/pallas_call | solution.py:442
  21.8 1.0 %collective-permute-done.7.refs_5_ = bf16[2,2,256,256]{3,2,1,0:T(8,128)(2,1)S(1)} collective-permute-done((bf16[2,2,256,256]{3,2,1,0:T(8,128)(2,1)S(1)}, bf16[2,2,256,256]{3,2,1,0:T(8,128)(2,1)S(1)}, u32[]{:S(2)}, u32[]{:S(2)}) %collective-permute-start.7) | collective-permute-done | bytes 524320 | tf_op jit(solution)/shard_map/ppermute | solution.py:395
  22.8 5.2 %back.1 = (bf16[2,128,256]{2,1,0:T(8,128)(2,1)S(1)}, bf16[2,128,256]{2,1,0:T(8,128)(2,1)S(1)}, bf16[2,128,256]{2,1,0:T(8,128)(2,1)S(1)}, bf16[2,128,128]{2,1,0:T...) custom-call(s32[1,1,2,2]{3,2,1,0:T(2,128)S(1)} %copy-done.6, ...), custom_call_target="tpu_custom_call" | custom-call | tf_op jit(solution)/shard_map/back/pallas_call | solution.py:452
  28.0 2.1 %collective-permute-start.8 = (bf16[2,128,256]{2,1,0:T(8,128)(2,1)S(1)}, bf16[2,128,256]{2,1,0:T(8,128)(2,1)S(1)}, u32[]{:S(2)}, u32[]{:S(2)}) collective-permute-start(bf16[2,128,256]{2,1,0:T(8,128)(2,1)S(1)} %get-tuple-element.49), channel_id=1, source_target_pairs={{0,8},{1,0},{2,10},{3,2},{4,12},{5,4},{6,14},{7,6},{8,16},{9,1},{1... | collective-permute-start | bytes 393224 | tf_op jit(solution)/shard_map/ppermute | solution.py:489
  30.1 1.5 %collective-permute-start.10 = (bf16[2,128,128]{2,1,0:T(8,128)(2,1)S(1)}, bf16[2,128,128]{2,1,0:T(8,128)(2,1)S(1)}, u32[]{:S(2)}, u32[]{:S(2)}) collective-permute-start(bf16[2,128,128]{2,1,0:T(8,128)(2,1)S(1)} %get-tuple-element.51), channel_id=1, source_target_pairs={{0,4},{4,0},{1,5},{5,1},{2,6},{6,2},{3,7},{7,3},{8,12},{12,8},{9,1... | collective-permute-start | bytes 196616 | tf_op jit(solution)/shard_map/ppermute | solution.py:494
  31.6 2.0 %collective-permute-start.11 = (bf16[2,128,128]{2,1,0:T(8,128)(2,1)S(1)}, bf16[2,128,128]{2,1,0:T(8,128)(2,1)S(1)}, u32[]{:S(2)}, u32[]{:S(2)}) collective-permute-start(bf16[2,128,128]{2,1,0:T(8,128)(2,1)S(1)} %get-tuple-element.52), channel_id=1, source_target_pairs={{0,12},{1,4},{2,14},{3,6},{4,8},{5,0},{6,10},{7,2},{8,20},{9,5},{1... | collective-permute-start | bytes 196616 | tf_op jit(solution)/shard_map/ppermute | solution.py:496
  33.6 0.7 %weights.1.weight_ref = f32[128,256]{1,0:T(8,128)S(1)} custom-call(bf16[256,256]{1,0:T(8,128)(2,1)S(1)} %get-tuple-element.47.weight_ref, bf16[272,256]{1,0:T(8,128)(2,1)S(1)} %get-tuple-element.35.refs_0_, bf16[272,256]{1,0:T(8,128)(2,1)S(1)} %collective-permute-done.2.refs_1_, bf16[272,256]{1,0:T(8,128)(2,1)S(1)} %collective-permute-done.3.refs_2_, ...), custom_call_target="tpu_custom_call" | custom-call | tf_op jit(solution)/shard_map/weights/pallas_call | solution.py:479
  34.3 0.4 %collective-permute-done.10.refs_3_ = bf16[2,128,128]{2,1,0:T(8,128)(2,1)S(1)} collective-permute-done((bf16[2,128,128]{2,1,0:T(8,128)(2,1)S(1)}, bf16[2,128,128]{2,1,0:T(8,128)(2,1)S(1)}, u32[]{:S(2)}, u32[]{:S(2)}) %collective-permute-start.10) | collective-permute-done | bytes 65568 | tf_op jit(solution)/shard_map/ppermute | solution.py:494
  34.8 1.1 %collective-permute-done.11.refs_4_ = bf16[2,128,128]{2,1,0:T(8,128)(2,1)S(1)} collective-permute-done((bf16[2,128,128]{2,1,0:T(8,128)(2,1)S(1)}, bf16[2,128,128]{2,1,0:T(8,128)(2,1)S(1)}, u32[]{:S(2)}, u32[]{:S(2)}) %collective-permute-start.11) | collective-permute-done | bytes 65568 | tf_op jit(solution)/shard_map/ppermute | solution.py:496
  35.9 2.9 %collective-permute-done.12.refs_5_ = bf16[2,128,128]{2,1,0:T(8,128)(2,1)S(1)} collective-permute-done((bf16[2,128,128]{2,1,0:T(8,128)(2,1)S(1)}, bf16[2,128,128]{2,1,0:T(8,128)(2,1)S(1)}, u32[]{:S(2)}, u32[]{:S(2)}) %collective-permute-start.12) | collective-permute-done | bytes 65568 | tf_op jit(solution)/shard_map/ppermute | solution.py:496
  38.8 0.1 sums.1.own_ref
  38.9 0.1 collective-permute-start.13
  39.0 1.3 %collective-permute-done.13.other_ref = bf16[2,128,256]{2,1,0:T(8,128)(2,1)S(1)} collective-permute-done((bf16[2,128,256]{2,1,0:T(8,128)(2,1)S(1)}, bf16[2,128,256]{2,1,0:T(8,128)(2,1)S(1)}, u32[]{:S(2)}, u32[]{:S(2)}) %collective-permute-start.13) | collective-permute-done | bytes 131104 | tf_op jit(solution)/shard_map/ppermute | solution.py:395
  40.3 0.8 %update.1 = f32[2,128,256]{2,1,0:T(8,128)} custom-call(f32[2,128,256]{2,1,0:T(8,128)S(1)} %copy-done.3, bf16[2,128,256]{2,1,0:T(8,128)(2,1)S(1)} %sums.1.own_ref, bf16[2,128,256]{2,1,0:T(8,128)(2,1)S(1)} %collective-permute-done.13.other_ref, f32[128,256]{1,0:T(8,128)S(1)} %weights.1.weight_ref), custom_call_target="tpu_custom_call" | custom-call | tf_op jit(solution)/shard_map/update/pallas_call | solution.py:509
  (18 shorter events, 0.0 us)
Async XLA Ops:
  0.0 17.1 %copy-start = (bf16[512,512]{1,0:T(8,128)(2,1)S(1)}, bf16[512,512]{1,0:T(8,128)(2,1)}, u32[]{:S(2)}) copy-start(bf16[512,512]{1,0:T(8,128)(2,1)} %constant.5.clone.refs_9_.swapped.refs_7_) | copy-start | bytes 1572868
  0.0 17.1 %copy-start.1 = (bf16[512,512]{1,0:T(8,128)(2,1)S(1)}, bf16[512,512]{1,0:T(8,128)(2,1)}, u32[]{:S(2)}) copy-start(bf16[512,512]{1,0:T(8,128)(2,1)} %constant.4.clone.refs_8_.direct.refs_6_) | copy-start | bytes 1572868
  1.4 6.0 %collective-permute-start.1 = (bf16[2,2,256,256]{3,2,1,0:T(8,128)(2,1)S(1)}, bf16[2,2,256,256]{3,2,1,0:T(8,128)(2,1)S(1)}, u32[]{:S(2)}, u32[]{:S(2)}) collective-permute-start(bf16[2,2,256,256]{3,2,1,0:T(8,128)(2,1)S(1)} %convert_element_type.3.refs_6_.refs_2_), channel_id=1, source_target_pairs={{0,1},{1,0},{2,3},{3,2},{4,5},{5,4},{6,7},{7,6},{8,9},{9,8},{10,11... | collective-permute-start | bytes 1572872 | tf_op jit(solution)/shard_map/ppermute | solution.py:395
  1.9 18.9 %collective-permute-start = (bf16[2,2,256,256]{3,2,1,0:T(8,128)(2,1)S(1)}, bf16[2,2,256,256]{3,2,1,0:T(8,128)(2,1)S(1)}, u32[]{:S(2)}, u32[]{:S(2)}) collective-permute-start(bf16[2,2,256,256]{3,2,1,0:T(8,128)(2,1)S(1)} %convert_element_type.3.refs_6_.refs_2_), channel_id=1, source_target_pairs={{0,2},{1,3},{2,0},{3,1},{4,6},{5,7},{6,4},{7,5},{8,10},{9,11},{10,... | collective-permute-start | bytes 1572872 | tf_op jit(solution)/shard_map/ppermute | solution.py:395
  5.1 1.0 %copy-start.2 = (f32[2,128,256]{2,1,0:T(8,128)S(1)}, f32[2,128,256]{2,1,0:T(8,128)}, u32[]{:S(2)}) copy-start(f32[2,128,256]{2,1,0:T(8,128)} %object_ref.3) | copy-start | bytes 786436
  6.1 0.7 %copy-start.5 = (s32[1,1,2,2]{3,2,1,0:T(2,128)S(1)}, s32[1,1,2,2]{3,2,1,0:T(2,128)}, u32[]{:S(2)}) copy-start(s32[1,1,2,2]{3,2,1,0:T(2,128)} %centers_ref.5) | copy-start | bytes 52
  7.4 15.4 %copy-start.4 = (bf16[1,1,2,256,256]{4,3,2,1,0:T(8,128)(2,1)S(1)}, bf16[1,1,2,256,256]{4,3,2,1,0:T(8,128)(2,1)}, u32[]{:S(2)}) copy-start(bf16[1,1,2,256,256]{4,3,2,1,0:T(8,128)(2,1)} %refs_0_.1) | copy-start | bytes 786436
  7.4 5.3 %collective-permute-start.6 = (bf16[272,128]{1,0:T(8,128)(2,1)S(1)}, bf16[272,128]{1,0:T(8,128)(2,1)S(1)}, u32[]{:S(2)}, u32[]{:S(2)}) collective-permute-start(bf16[272,128]{1,0:T(8,128)(2,1)S(1)} %get-tuple-element.36), channel_id=1, source_target_pairs={{0,5},{1,13},{2,7},{3,15},{4,1},{5,9},{6,3},{7,11},{8,4},{9,21},{1... | collective-permute-start | bytes 208904 | tf_op jit(solution)/shard_map/ppermute | solution.py:416
  8.7 8.4 %collective-permute-start.3 = (bf16[272,256]{1,0:T(8,128)(2,1)S(1)}, bf16[272,256]{1,0:T(8,128)(2,1)S(1)}, u32[]{:S(2)}, u32[]{:S(2)}) collective-permute-start(bf16[272,256]{1,0:T(8,128)(2,1)S(1)} %get-tuple-element.35.refs_0_), channel_id=1, source_target_pairs={{0,1},{1,9},{2,3},{3,11},{4,5},{5,13},{6,7},{7,15},{8,0},{9,17},{1... | collective-permute-start | bytes 417800 | tf_op jit(solution)/shard_map/ppermute | solution.py:413
  9.8 7.3 %collective-permute-start.2 = (bf16[272,256]{1,0:T(8,128)(2,1)S(1)}, bf16[272,256]{1,0:T(8,128)(2,1)S(1)}, u32[]{:S(2)}, u32[]{:S(2)}) collective-permute-start(bf16[272,256]{1,0:T(8,128)(2,1)S(1)} %get-tuple-element.35.refs_0_), channel_id=1, source_target_pairs={{0,8},{1,0},{2,10},{3,2},{4,12},{5,4},{6,14},{7,6},{8,16},{9,1},{1... | collective-permute-start | bytes 417800 | tf_op jit(solution)/shard_map/ppermute | solution.py:413
  10.7 4.5 %collective-permute-start.5 = (bf16[272,128]{1,0:T(8,128)(2,1)S(1)}, bf16[272,128]{1,0:T(8,128)(2,1)S(1)}, u32[]{:S(2)}, u32[]{:S(2)}) collective-permute-start(bf16[272,128]{1,0:T(8,128)(2,1)S(1)} %get-tuple-element.36), channel_id=1, source_target_pairs={{0,12},{1,4},{2,14},{3,6},{4,8},{5,0},{6,10},{7,2},{8,20},{9,5},{1... | collective-permute-start | bytes 208904 | tf_op jit(solution)/shard_map/ppermute | solution.py:416
  12.6 4.5 %collective-permute-start.4 = (bf16[272,128]{1,0:T(8,128)(2,1)S(1)}, bf16[272,128]{1,0:T(8,128)(2,1)S(1)}, u32[]{:S(2)}, u32[]{:S(2)}) collective-permute-start(bf16[272,128]{1,0:T(8,128)(2,1)S(1)} %get-tuple-element.36), channel_id=1, source_target_pairs={{0,4},{4,0},{1,5},{5,1},{2,6},{6,2},{3,7},{7,3},{8,12},{12,8},{9,1... | collective-permute-start | bytes 208904 | tf_op jit(solution)/shard_map/ppermute | solution.py:415
  17.1 0.7 %copy-start.6 = (s32[1,1,2,2]{3,2,1,0:T(2,128)S(1)}, s32[1,1,2,2]{3,2,1,0:T(2,128)}, u32[]{:S(2)}) copy-start(s32[1,1,2,2]{3,2,1,0:T(2,128)} %centers_ref.5) | copy-start | bytes 52
  20.8 2.0 %collective-permute-start.7 = (bf16[2,2,256,256]{3,2,1,0:T(8,128)(2,1)S(1)}, bf16[2,2,256,256]{3,2,1,0:T(8,128)(2,1)S(1)}, u32[]{:S(2)}, u32[]{:S(2)}) collective-permute-start(bf16[2,2,256,256]{3,2,1,0:T(8,128)(2,1)S(1)} %collective-permute-done.group.refs_4_), channel_id=1, source_target_pairs={{0,1},{1,0},{2,3},{3,2},{4,5},{5,4},{6,7},{7,6},{8,9},{9,8},{10,11... | collective-permute-start | bytes 1572872 | tf_op jit(solution)/shard_map/ppermute | solution.py:395
  22.8 17.5 %copy-start.3 = (f32[2,128,256]{2,1,0:T(8,128)S(1)}, f32[2,128,256]{2,1,0:T(8,128)}, u32[]{:S(2)}) copy-start(f32[2,128,256]{2,1,0:T(8,128)} %object_ref.3) | copy-start | bytes 786436
  28.0 10.7 %collective-permute-start.8 = (bf16[2,128,256]{2,1,0:T(8,128)(2,1)S(1)}, bf16[2,128,256]{2,1,0:T(8,128)(2,1)S(1)}, u32[]{:S(2)}, u32[]{:S(2)}) collective-permute-start(bf16[2,128,256]{2,1,0:T(8,128)(2,1)S(1)} %get-tuple-element.49), channel_id=1, source_target_pairs={{0,8},{1,0},{2,10},{3,2},{4,12},{5,4},{6,14},{7,6},{8,16},{9,1},{1... | collective-permute-start | bytes 393224 | tf_op jit(solution)/shard_map/ppermute | solution.py:489
  30.1 8.7 %collective-permute-start.9 = (bf16[2,128,256]{2,1,0:T(8,128)(2,1)S(1)}, bf16[2,128,256]{2,1,0:T(8,128)(2,1)S(1)}, u32[]{:S(2)}, u32[]{:S(2)}) collective-permute-start(bf16[2,128,256]{2,1,0:T(8,128)(2,1)S(1)} %get-tuple-element.50), channel_id=1, source_target_pairs={{0,1},{1,9},{2,3},{3,11},{4,5},{5,13},{6,7},{7,15},{8,0},{9,17},{1... | collective-permute-start | bytes 393224 | tf_op jit(solution)/shard_map/ppermute | solution.py:489
  30.1 4.7 %collective-permute-start.10 = (bf16[2,128,128]{2,1,0:T(8,128)(2,1)S(1)}, bf16[2,128,128]{2,1,0:T(8,128)(2,1)S(1)}, u32[]{:S(2)}, u32[]{:S(2)}) collective-permute-start(bf16[2,128,128]{2,1,0:T(8,128)(2,1)S(1)} %get-tuple-element.51), channel_id=1, source_target_pairs={{0,4},{4,0},{1,5},{5,1},{2,6},{6,2},{3,7},{7,3},{8,12},{12,8},{9,1... | collective-permute-start | bytes 196616 | tf_op jit(solution)/shard_map/ppermute | solution.py:494
  31.6 4.3 %collective-permute-start.11 = (bf16[2,128,128]{2,1,0:T(8,128)(2,1)S(1)}, bf16[2,128,128]{2,1,0:T(8,128)(2,1)S(1)}, u32[]{:S(2)}, u32[]{:S(2)}) collective-permute-start(bf16[2,128,128]{2,1,0:T(8,128)(2,1)S(1)} %get-tuple-element.52), channel_id=1, source_target_pairs={{0,12},{1,4},{2,14},{3,6},{4,8},{5,0},{6,10},{7,2},{8,20},{9,5},{1... | collective-permute-start | bytes 196616 | tf_op jit(solution)/shard_map/ppermute | solution.py:496
  33.6 5.2 %collective-permute-start.12 = (bf16[2,128,128]{2,1,0:T(8,128)(2,1)S(1)}, bf16[2,128,128]{2,1,0:T(8,128)(2,1)S(1)}, u32[]{:S(2)}, u32[]{:S(2)}) collective-permute-start(bf16[2,128,128]{2,1,0:T(8,128)(2,1)S(1)} %get-tuple-element.53), channel_id=1, source_target_pairs={{0,5},{1,13},{2,7},{3,15},{4,1},{5,9},{6,3},{7,11},{8,4},{9,21},{1... | collective-permute-start | bytes 196616 | tf_op jit(solution)/shard_map/ppermute | solution.py:496
  38.9 1.4 %collective-permute-start.13 = (bf16[2,128,256]{2,1,0:T(8,128)(2,1)S(1)}, bf16[2,128,256]{2,1,0:T(8,128)(2,1)S(1)}, u32[]{:S(2)}, u32[]{:S(2)}) collective-permute-start(bf16[2,128,256]{2,1,0:T(8,128)(2,1)S(1)} %sums.1.own_ref), channel_id=1, source_target_pairs={{0,1},{1,0},{2,3},{3,2},{4,5},{5,4},{6,7},{7,6},{8,9},{9,8},{10,11... | collective-permute-start | bytes 393224 | tf_op jit(solution)/shard_map/ppermute | solution.py:395

commit v4 on v3

--- a/solution.py
+++ b/solution.py
@@ -62,32 +62,56 @@
     return (lax.axis_index("tx"), lax.axis_index("ty"), lax.axis_index("mode") % 2)
 
 
-def pack_kernel(sides, slots, centers_ref, live_ref, object_ref, *outs):
-    _, tile_rows, tile_cols = object_ref.shape
-    half = outs[1].shape[1]
+def start_kernel(sides, object_hbm, probe_hbm, low_ref, packed_ref, *rest):
+    edges = rest[:sides]
+    object_ref, probe_ref, sems = rest[sides:]
+    copies = [
+        pltpu.make_async_copy(source, target, sems.at[index])
+        for index, (source, target) in enumerate(
+            ((probe_hbm, probe_ref), (object_hbm, object_ref))
+        )
+    ]
+    for copy in copies:
+        copy.start()
+    tile_cols = object_ref.shape[2]
+    half = edges[0].shape[2]
     _, x_index, _ = here()
-    record = jnp.zeros((record_rows, tile_cols), jnp.float32)
-    line = iota((record_rows, tile_cols), 0)
+    copies[0].wait()
+    low_ref[...] = probe_ref[...].astype(jnp.bfloat16)
+    copies[1].wait()
+    first, last = slice(0, half), slice(tile_cols - half, tile_cols)
+    for channel in range(2):
+        values = object_ref[channel].astype(jnp.bfloat16)
+        packed_ref[channel] = values
+        if sides == 1:
+            edges[0][channel] = jnp.where(x_index == 0, values[:, last], values[:, first])
+        else:
+            edges[0][channel] = values[:, last]
+            edges[1][channel] = values[:, first]
+
+
+def record_kernel(slots, centers_ref, live_ref, out_ref):
+    record = jnp.zeros(out_ref.shape, jnp.float32)
+    line = iota(out_ref.shape, 0)
     for slot in range(slots):
         for axis in range(2):
             value = centers_ref[0, 0, slot, axis].astype(jnp.float32)
             record = jnp.where(line == 2 * slot + axis, value, record)
     record = jnp.where(line == 2 * slots, live_ref[0, 0].astype(jnp.float32), record)
-    record = record.astype(jnp.bfloat16)
-    first, last = slice(0, half), slice(tile_cols - half, tile_cols)
-    for channel in range(2):
-        rows = slice(channel * tile_rows, (channel + 1) * tile_rows)
-        values = object_ref[channel].astype(jnp.bfloat16)
-        outs[0][rows] = values
-        if sides == 1:
-            outs[1][rows] = jnp.where(x_index == 0, values[:, last], values[:, first])
-        else:
-            outs[1][rows] = values[:, last]
-            outs[2][rows] = values[:, first]
-    rows = slice(2 * tile_rows, 2 * tile_rows + record_rows)
-    outs[0][rows] = record
-    for out in outs[1:]:
-        out[rows] = record[:, :half]
+    out_ref[...] = record.astype(jnp.bfloat16)
+
+
+def positions(record_ref, slots):
+    _, _, parity = here()
+    record = record_ref[:, :128].astype(jnp.float32).astype(jnp.int32)[:, :1]
+
+    def of_slot(axis):
+        value = record[axis : axis + 1]
+        for slot in range(1, slots):
+            value = jnp.where(parity == slot, record[2 * slot + axis : 2 * slot + axis + 1], value)
+        return value
+
+    return of_slot(0), of_slot(1), record[2 * slots : 2 * slots + 1] > parity
 
 
 def row_starts(half, tile_rows, parity):
@@ -98,18 +122,16 @@
     )
 
 
-def patch_of(sides, z_count, x_count, tile_rows, side, centers_ref, pieces, ext_ref):
+def patch_of(sides, slots, z_count, x_count, side, record_ref, pieces, ext_ref):
     z_index, x_index, parity = here()
-    row_at = centers_ref[0, 0, parity, 0]
-    col_at = centers_ref[0, 0, parity, 1]
+    row_at, col_at, _ = positions(record_ref, slots)
     half = side // 2
-    tile_cols = pieces[0].shape[1]
+    _, tile_rows, tile_cols = pieces[0].shape
     ext_rows = tile_rows + side
     ext_cols = tile_cols + sides * half
     a_at, b_at = row_starts(half, tile_rows, parity)
     for channel in range(2):
         base = channel * ext_rows
-        rows = slice(channel * tile_rows, (channel + 1) * tile_rows)
         for index in range(1 + sides):
             columns = (
                 slice(0, tile_cols)
@@ -117,9 +139,9 @@
                 else slice(tile_cols + (index - 1) * half, tile_cols + index * half)
             )
             level, turn_a, turn_b = pieces[3 * index : 3 * index + 3]
-            ext_ref[pl.ds(base + half, tile_rows), columns] = level[rows]
-            ext_ref[pl.ds(base + a_at, half), columns] = turn_a[rows]
-            ext_ref[pl.ds(base + b_at, half), columns] = turn_b[rows]
+            ext_ref[pl.ds(base + half, tile_rows), columns] = level[channel]
+            ext_ref[pl.ds(base + a_at, half), columns] = turn_a[channel]
+            ext_ref[pl.ds(base + b_at, half), columns] = turn_b[channel]
     at = iota((ext_cols, side), 0)
     column = column_coordinate(at, tile_cols, half, sides, x_index, x_count)
     pick_cols = (column == iota((ext_cols, side), 1) + col_at).astype(jnp.bfloat16)
@@ -191,13 +213,13 @@
     return grads
 
 
-def near_kernel(sides, z_count, x_count, tile_rows, centers_ref, *refs):
+def near_kernel(sides, slots, z_count, x_count, record_ref, *refs):
     n_pieces = 3 + 3 * sides
     pieces = refs[:n_pieces]
     own, core, direct, swapped = refs[n_pieces : n_pieces + 4]
     patch_ref, far_ref, exit_ref, sum_ref, ext_ref = refs[n_pieces + 4 :]
     side = own.shape[2]
-    patch = patch_of(sides, z_count, x_count, tile_rows, side, centers_ref, pieces, ext_ref)
+    patch = patch_of(sides, slots, z_count, x_count, side, record_ref, pieces, ext_ref)
     patch_ref[0], patch_ref[1] = patch
     sums = forward((own, core), patch, direct[...], swapped[...], far_ref, exit_ref, 0)
     sum_ref[0] = sums[0][0] + sums[1][0]
@@ -211,7 +233,7 @@
     sum_ref[1] = weight
 
 
-def back_kernel(sides, x_count, tile_rows, tile_cols, centers_ref, live_ref, *refs):
+def back_kernel(sides, slots, x_count, tile_rows, tile_cols, record_ref, *refs):
     n_pieces = 3 + 3 * sides
     amplitude_ref, patch_ref, own, core, over, last, direct_ref, swapped_ref = refs[:8]
     near_far, near_exit, near_sum, over_far, over_exit, over_sum = refs[8:14]
@@ -223,9 +245,7 @@
     ext_rows = tile_rows + side
     ext_cols = tile_cols + sides * half
     _, x_index, parity = here()
-    row_at = centers_ref[0, 0, parity, 0]
-    col_at = centers_ref[0, 0, parity, 1]
-    is_live = parity < live_ref[0, 0]
+    row_at, col_at, is_live = positions(record_ref, slots)
     direct = direct_ref[...]
     swapped = swapped_ref[...]
     patch = (patch_ref[0], patch_ref[1])
@@ -250,15 +270,18 @@
         gradient = (near[0][channel] + near[1][channel]) + (beyond[channel] + final[channel])
         placed = dot(put_rows, gradient.astype(jnp.bfloat16)).astype(jnp.bfloat16)
         grad_ref[...] = dot(placed, put_cols).astype(jnp.bfloat16)
+        rows = slice(channel * half, (channel + 1) * half)
         for index in range(1 + sides):
             columns = (
                 slice(0, tile_cols)
                 if index == 0
                 else slice(tile_cols + (index - 1) * half, tile_cols + index * half)
             )
-            outs[3 * index][channel] = grad_ref[half : half + tile_rows, columns]
-            outs[3 * index + 1][channel] = grad_ref[pl.ds(b_at, half), columns]
-            outs[3 * index + 2][channel] = grad_ref[pl.ds(a_at, half), columns]
+            outs[3 * index][rows] = grad_ref[half : half + tile_rows, columns]
+            outs[3 * index + 1][rows] = grad_ref[pl.ds(b_at, half), columns]
+            outs[3 * index + 2][rows] = grad_ref[pl.ds(a_at, half), columns]
+    for out in outs[:n_pieces]:
+        out[2 * half :] = record_ref[:, : out.shape[1]]
 
 
 def weight_kernel(sides, slots, z_count, x_count, weight_ref, *refs):
@@ -272,8 +295,8 @@
         x_steps = [0, jnp.where(x_index == 0, 1, -1)]
         x_shown = [True, True]
     else:
-        x_steps = [0, -1, 1]
-        x_shown = [True, x_index > 0, x_index < x_count - 1]
+        x_steps = [0, 1, -1]
+        x_shown = [True, x_index < x_count - 1, x_index > 0]
     weight = weight_ref[...]
     total = jnp.zeros((tile_rows, tile_cols), jnp.float32)
     for index, x_step in enumerate(x_steps):
@@ -282,7 +305,7 @@
             part = jnp.zeros((tile_rows, tile_cols), jnp.float32)
             z_tile = z_index + z_step
             shown = (z_tile >= 0) & (z_tile < z_count) & x_shown[index]
-            record = pieces[3 * index + turn][2 * tile_rows :].astype(jnp.float32)
+            record = pieces[3 * index + turn][2 * half :].astype(jnp.float32)
             record = record.astype(jnp.int32)
             if record.shape[1] < side:
                 record = jnp.concatenate([record] * (side // record.shape[1]), axis=1)
@@ -307,26 +330,28 @@
 def sum_kernel(sides, z_count, x_count, *refs):
     pieces, out_ref = refs[:-1], refs[-1]
     own_ref, rows_a, rows_b = pieces[:3]
-    tile_cols = own_ref.shape[2]
-    half = pieces[3].shape[2]
+    _, tile_rows, tile_cols = out_ref.shape
+    half = pieces[3].shape[1]
     z_index, x_index, parity = here()
     below = z_index > 0
     above = z_index < z_count - 1
     a_on = jnp.where(parity == 0, below, above)
     b_on = jnp.where(parity == 0, above, below)
 
-    def gate(on, ref, channel):
-        return jnp.where(on, ref[channel].astype(jnp.float32), 0.0)
-
     for channel in range(2):
-        total = own_ref[channel].astype(jnp.float32)
-        total = total + gate(a_on, rows_a, channel) + gate(b_on, rows_b, channel)
-        first = jnp.zeros((total.shape[0], half), jnp.float32)
+        rows = slice(channel * tile_rows, (channel + 1) * tile_rows)
+
+        def gate(on, ref, rows=rows):
+            return jnp.where(on, ref[rows].astype(jnp.float32), 0.0)
+
+        total = own_ref[rows].astype(jnp.float32)
+        total = total + gate(a_on, rows_a) + gate(b_on, rows_b)
+        first = jnp.zeros((tile_rows, half), jnp.float32)
         last = first
         for index in range(sides):
             level, corner_a, corner_b = pieces[3 + 3 * index : 6 + 3 * index]
-            edge = level[channel].astype(jnp.float32)
-            edge = edge + gate(a_on, corner_a, channel) + gate(b_on, corner_b, channel)
+            edge = level[rows].astype(jnp.float32)
+            edge = edge + gate(a_on, corner_a) + gate(b_on, corner_b)
             if sides == 1:
                 first = jnp.where(x_index == 1, edge, 0.0)
                 last = jnp.where(x_index == 0, edge, 0.0)
@@ -334,7 +359,7 @@
                 last = jnp.where(x_index < x_count - 1, edge, 0.0)
             else:
                 first = jnp.where(x_index > 0, edge, 0.0)
-        zero = jnp.zeros((total.shape[0], tile_cols - 2 * half), jnp.float32)
+        zero = jnp.zeros((tile_rows, tile_cols - 2 * half), jnp.float32)
         parts = [first, zero, last] if tile_cols > 2 * half else [first, last]
         total = total + jnp.concatenate(parts, axis=1)
         out_ref[channel] = total.astype(jnp.bfloat16)
@@ -346,8 +371,16 @@
         out_ref[channel] = object_ref[channel] + gradient / weight_ref[...]
 
 
+def in_hbm(array):
+    return pltpu.with_memory_space_constraint(array, pltpu.HBM)
+
+
 def smem():
     return pl.BlockSpec(memory_space=pltpu.SMEM)
+
+
+def hbm():
+    return pl.BlockSpec(memory_space=pltpu.HBM)
 
 
 def vmem():
@@ -394,19 +427,25 @@
     def exchange(array, flip):
         return lax.ppermute(array, "mode", [(m, m ^ flip) for m in range(m_count)])
 
-    probe_low = probe.astype(jnp.bfloat16)
+    probe_low, *packed = pl.pallas_call(
+        functools.partial(start_kernel, sides),
+        out_shape=[
+            jax.ShapeDtypeStruct(probe.shape, jnp.bfloat16),
+            jax.ShapeDtypeStruct(object_field.shape, jnp.bfloat16),
+        ]
+        + [jax.ShapeDtypeStruct((2, tile_rows, half), jnp.bfloat16)] * sides,
+        in_specs=[hbm()] * 2,
+        out_specs=[vmem()] * (2 + sides),
+        scratch_shapes=[
+            pltpu.VMEM(object_field.shape, jnp.float32),
+            pltpu.VMEM(probe.shape, jnp.float32),
+            pltpu.SemaphoreType.DMA((2,)),
+        ],
+        compiler_params=pltpu.CompilerParams(vmem_limit_bytes=small_bytes),
+        name="start",
+    )(in_hbm(object_field), in_hbm(probe))
     probe_y = exchange(probe_low, 2)
     probe_core = exchange(probe_low, 1)
-    packed_rows = 2 * tile_rows + record_rows
-    packed = pl.pallas_call(
-        functools.partial(pack_kernel, sides, slots),
-        out_shape=[jax.ShapeDtypeStruct((packed_rows, tile_cols), jnp.bfloat16)]
-        + [jax.ShapeDtypeStruct((packed_rows, half), jnp.bfloat16)] * sides,
-        in_specs=[smem(), smem(), vmem()],
-        out_specs=[vmem()] * (1 + sides),
-        compiler_params=pltpu.CompilerParams(vmem_limit_bytes=small_bytes),
-        name="pack",
-    )(centers, live, object_field)
     probe_core, *packed = lax.optimization_barrier((probe_core, *packed))
     x_steps = [1] if sides == 1 else [1, -1]
     pieces = [packed[0]]
@@ -415,6 +454,15 @@
         pieces.append(lax.ppermute(edge, "ty", level(step)))
         pieces += [lax.ppermute(edge, axes, zigzag(flip, step)) for flip in (False, True)]
 
+    centers, live, pieces[3] = lax.optimization_barrier((centers, live, pieces[3]))
+    record = pl.pallas_call(
+        functools.partial(record_kernel, slots),
+        out_shape=jax.ShapeDtypeStruct((record_rows, tile_cols), jnp.bfloat16),
+        in_specs=[smem(), smem()],
+        out_specs=vmem(),
+        compiler_params=pltpu.CompilerParams(vmem_limit_bytes=small_bytes),
+        name="record",
+    )(centers, live)
     n_pieces = len(pieces)
     modes = probe.shape[1]
     ext_rows = tile_rows + side
@@ -429,14 +477,14 @@
         ]
 
     patch, *near = pl.pallas_call(
-        functools.partial(near_kernel, sides, z_count, x_count, tile_rows),
+        functools.partial(near_kernel, sides, slots, z_count, x_count),
         out_shape=[jax.ShapeDtypeStruct((2, side, side), jnp.float32)] + waves(2 * modes),
-        in_specs=[smem()] + [vmem()] * (n_pieces + 4),
+        in_specs=[vmem()] * (n_pieces + 5),
         out_specs=[vmem()] * 4,
         scratch_shapes=[pltpu.VMEM((2 * ext_rows, ext_cols), jnp.bfloat16)],
         compiler_params=pltpu.CompilerParams(vmem_limit_bytes=wave_bytes),
         name="near",
-    )(centers, *pieces, probe_low, probe_core, direct, swapped)
+    )(record, *pieces, probe_low, probe_core, direct, swapped)
     probe_y, patch = lax.optimization_barrier((probe_y, patch))
     probe_diagonal = exchange(probe_y, 1)
     over = pl.pallas_call(
@@ -447,13 +495,13 @@
         compiler_params=pltpu.CompilerParams(vmem_limit_bytes=wave_bytes),
         name="over",
     )(patch, probe_y, direct, swapped)
-    shapes = [(2, tile_rows, tile_cols)] + [(2, half, tile_cols)] * 2
-    shapes += ([(2, tile_rows, half)] + [(2, half, half)] * 2) * sides
+    shapes = [(2 * half + record_rows, tile_cols)] * 3
+    shapes += [(2 * half + record_rows, half)] * (3 * sides)
     results = pl.pallas_call(
-        functools.partial(back_kernel, sides, x_count, tile_rows, tile_cols),
+        functools.partial(back_kernel, sides, slots, x_count, tile_rows, tile_cols),
         out_shape=[jax.ShapeDtypeStruct(shape, jnp.bfloat16) for shape in shapes]
         + [jax.ShapeDtypeStruct((side, side), jnp.bfloat16)],
-        in_specs=[smem(), smem()] + [vmem()] * 14,
+        in_specs=[vmem()] * 15,
         out_specs=[vmem()] * (n_pieces + 1),
         scratch_shapes=[
             pltpu.VMEM((modes, side, 2 * side), jnp.float32),
@@ -463,8 +511,7 @@
         compiler_params=pltpu.CompilerParams(vmem_limit_bytes=wave_bytes),
         name="back",
     )(
-        centers,
-        live,
+        record,
         amplitudes,
         patch,
         probe_low,
@@ -476,14 +523,6 @@
         *near,
         *over,
     )
-    weight = pl.pallas_call(
-        functools.partial(weight_kernel, sides, slots, z_count, x_count),
-        out_shape=jax.ShapeDtypeStruct((tile_rows, tile_cols), jnp.float32),
-        in_specs=[vmem()] * (n_pieces + 1),
-        out_specs=vmem(),
-        compiler_params=pltpu.CompilerParams(vmem_limit_bytes=small_bytes),
-        name="weights",
-    )(results[-1], *pieces)
     received = [results[0]]
     received += [
         lax.ppermute(results[1 + index], axes, zigzag(flip, 0))
@@ -496,7 +535,6 @@
             lax.ppermute(results[4 + 3 * index + turn], axes, zigzag(flip, back_step))
             for turn, flip in enumerate((False, True))
         ]
-    weight, *received = lax.optimization_barrier((weight, *received))
     summed = pl.pallas_call(
         functools.partial(sum_kernel, sides, z_count, x_count),
         out_shape=jax.ShapeDtypeStruct(object_field.shape, jnp.bfloat16),
@@ -505,6 +543,14 @@
         compiler_params=pltpu.CompilerParams(vmem_limit_bytes=small_bytes),
         name="sums",
     )(*received)
+    weight = pl.pallas_call(
+        functools.partial(weight_kernel, sides, slots, z_count, x_count),
+        out_shape=jax.ShapeDtypeStruct((tile_rows, tile_cols), jnp.float32),
+        in_specs=[vmem()] * (n_pieces + 1),
+        out_specs=vmem(),
+        compiler_params=pltpu.CompilerParams(vmem_limit_bytes=small_bytes),
+        name="weights",
+    )(results[-1], *received)
     other = exchange(summed, 1)
     return pl.pallas_call(
         update_kernel,

time: 41.3 us -> 38.8 us (0.939)
  waiting for transfers between devices: 10 us -> 7.6 us
  other arithmetic: 1.37 us -> 0 us
  starting transfers between devices: 15.3 us -> 15.9 us
  local copies, waits for them, and re-layouts: 2.32 us -> 2.77 us
    ppermute x1, waiting for transfers between devices: 1.88 us -> 0.44 us  [on_device(): pieces.append(lax.ppermute(edge, 'ty', level(step)))]
    convert_element_type x1 -> x0, other arithmetic: 1.37 us -> none  [on_device(): probe_low = probe.astype(jnp.bfloat16)]
    ppermute x2, waiting for transfers between devices: 1.36 us -> 0.39 us  [on_device(): lax.ppermute(edge, axes, zigzag(flip, step))]
    ppermute x1, waiting for transfers between devices: 0.43 us -> 1.32 us  [on_device(): lax.ppermute(results[3 + 3 * index], 'ty', level(back_step))]
    ppermute x4, waiting for transfers between devices: 2.34 us -> 1.57 us  [exchange(): return lax.ppermute(array, 'mode', [(m, m ^ flip) for m in range(m_count)])]
    unnamed x14, local copies, waits for them, and re-layouts: 2.32 us -> 2.77 us
    pallas_call x3 -> x4, Pallas kernels: 8.76 us -> 9.03 us  [the longest x1 4.71 us: on_device(): pl.pallas_call(functools.partial(back_kernel, sides, slots, x_count, tile...]
  transfers between devices with their start and end apart: 14 -> 14, of which waited for: 8 -> 7; matrix products, arithmetic and copies ran while one was open for 0% -> 0% of each run, Pallas kernels for 13% -> 12%
where the time goes in v4:
time: 38.8 us; the launch traced here: 38.6 us
  starting transfers between devices  15.9 us (41%)
  Pallas kernels  11.6 us (30%)
  waiting for transfers between devices  7.6 us (20%)
  local copies, waits for them, and re-layouts  2.77 us (7%)
  between operations  0.77 us (2%)
    pallas_call x1, Pallas kernels, on_device(): pl.pallas_call(functools.partial(back_kernel, sides, slots, x_count, tile...  4.71 us
    ppermute x2, waiting for transfers between devices, on_device(): lax.ppermute(results[4 + 3 * index + turn], axes, zigzag(flip, back_step))  3.89 us
    ppermute x4, starting transfers between devices, exchange(): return lax.ppermute(array, 'mode', [(m, m ^ flip) for m in range(m_count)])  3.25 us
    ppermute x2, starting transfers between devices, on_device(): lax.ppermute(edge, axes, zigzag(flip, step))  2.81 us
    unnamed x14, local copies, waits for them, and re-layouts  2.77 us
    ppermute x2, starting transfers between devices, on_device(): lax.ppermute(results[1 + index], axes, zigzag(flip, 0))  2.48 us
    pallas_call x1, Pallas kernels, on_device(): pl.pallas_call(functools.partial(near_kernel, sides, slots, z_count, x_co...  2.35 us
    ppermute x2, starting transfers between devices, on_device(): lax.ppermute(packed[0], axes, zigzag(flip, 0))  2.03 us
  transfers between devices with their start and end apart: 14, of which 7 were waited for; matrix products, arithmetic and copies ran while one was open for 0% of the time, Pallas kernels for 12%

profile of v4, /device:TPU:0, one launch (start us, length us, event | category | flops | bytes accessed | tf_op | source)
XLA Modules:
  0.0 38.6 jit_solution(7309886828256175171)
XLA Ops:
  0.0 1.4 %start.1 = (bf16[2,2,256,256]{3,2,1,0:T(8,128)(2,1)S(1)}, bf16[2,128,256]{2,1,0:T(8,128)(2,1)S(1)}, bf16[2,128,128]{2,1,0:T(8,128)(2,1)S(1)}) custom-call(f32[2,128,256]{2,1,0:T(8,128)} %object_ref.1, f32[2,2,256,256]{3,2,1,0:T(8,128)} %probe_hbm.1), custom_call_target="tpu_custom_call" | custom-call | tf_op jit(solution)/shard_map/start/pallas_call | solution.py:430
  1.4 0.5 %collective-permute-start = (bf16[2,2,256,256]{3,2,1,0:T(8,128)(2,1)S(1)}, bf16[2,2,256,256]{3,2,1,0:T(8,128)(2,1)S(1)}, u32[]{:S(2)}, u32[]{:S(2)}) collective-permute-start(bf16[2,2,256,256]{3,2,1,0:T(8,128)(2,1)S(1)} %get-tuple-element.30.refs_6_.refs_2_), channel_id=1, source_target_pairs={{0,1},{1,0},{2,3},{3,2},{4,5},{5,4},{6,7},{7,6},{8,9},{9,8},{10,11... | collective-permute-start | bytes 1572872 | tf_op jit(solution)/shard_map/ppermute | solution.py:428
  1.9 2.6 %collective-permute-start.2 = (bf16[2,2,256,256]{3,2,1,0:T(8,128)(2,1)S(1)}, bf16[2,2,256,256]{3,2,1,0:T(8,128)(2,1)S(1)}, u32[]{:S(2)}, u32[]{:S(2)}) collective-permute-start(bf16[2,2,256,256]{3,2,1,0:T(8,128)(2,1)S(1)} %get-tuple-element.30.refs_6_.refs_2_), channel_id=1, source_target_pairs={{0,2},{1,3},{2,0},{3,1},{4,6},{5,7},{6,4},{7,5},{8,10},{9,11},{10,... | collective-permute-start | bytes 1572872 | tf_op jit(solution)/shard_map/ppermute | solution.py:428
  4.5 1.8 %collective-permute-start.1 = (bf16[2,128,128]{2,1,0:T(8,128)(2,1)S(1)}, bf16[2,128,128]{2,1,0:T(8,128)(2,1)S(1)}, u32[]{:S(2)}, u32[]{:S(2)}) collective-permute-start(bf16[2,128,128]{2,1,0:T(8,128)(2,1)S(1)} %get-tuple-element.33), channel_id=1, source_target_pairs={{0,4},{4,0},{1,5},{5,1},{2,6},{6,2},{3,7},{7,3},{8,12},{12,8},{9,1... | collective-permute-start | bytes 196616 | tf_op jit(solution)/shard_map/ppermute | solution.py:454
  6.3 2.0 %collective-permute-start.3 = (bf16[2,128,256]{2,1,0:T(8,128)(2,1)S(1)}, bf16[2,128,256]{2,1,0:T(8,128)(2,1)S(1)}, u32[]{:S(2)}, u32[]{:S(2)}) collective-permute-start(bf16[2,128,256]{2,1,0:T(8,128)(2,1)S(1)} %get-tuple-element.36.refs_0_), channel_id=1, source_target_pairs={{0,8},{1,0},{2,10},{3,2},{4,12},{5,4},{6,14},{7,6},{8,16},{9,1},{1... | collective-permute-start | bytes 393224 | tf_op jit(solution)/shard_map/ppermute | solution.py:452
  8.4 0.0 collective-permute-start.6
  8.4 0.4 %collective-permute-done.1.refs_3_ = bf16[2,128,128]{2,1,0:T(8,128)(2,1)S(1)} collective-permute-done((bf16[2,128,128]{2,1,0:T(8,128)(2,1)S(1)}, bf16[2,128,128]{2,1,0:T(8,128)(2,1)S(1)}, u32[]{:S(2)}, u32[]{:S(2)}) %collective-permute-start.1) | collective-permute-done | bytes 65568 | tf_op jit(solution)/shard_map/ppermute | solution.py:454
  8.8 2.8 %collective-permute-start.5 = (bf16[2,128,128]{2,1,0:T(8,128)(2,1)S(1)}, bf16[2,128,128]{2,1,0:T(8,128)(2,1)S(1)}, u32[]{:S(2)}, u32[]{:S(2)}) collective-permute-start(bf16[2,128,128]{2,1,0:T(8,128)(2,1)S(1)} %get-tuple-element.33), channel_id=1, source_target_pairs={{0,12},{1,4},{2,14},{3,6},{4,8},{5,0},{6,10},{7,2},{8,20},{9,5},{1... | collective-permute-start | bytes 196616 | tf_op jit(solution)/shard_map/ppermute | solution.py:455
  12.3 0.0 copy-start.6
  12.3 0.7 %copy-done.6 = s32[1,1,2,2]{3,2,1,0:T(2,128)S(1)} copy-done((s32[1,1,2,2]{3,2,1,0:T(2,128)S(1)}, s32[1,1,2,2]{3,2,1,0:T(2,128)}, u32[]{:S(2)}) %copy-start.6) | copy-done | bytes 40
  12.9 0.6 %record.1.record_ref = bf16[16,256]{1,0:T(8,128)(2,1)S(1)} custom-call(s32[1,1,2,2]{3,2,1,0:T(2,128)S(1)} %copy-done.6, s32[1,1]{1,0:T(1,128)S(6)} %copy.8.live_ref), custom_call_target="tpu_custom_call" | custom-call | tf_op jit(solution)/shard_map/record/pallas_call | solution.py:458
  13.5 0.4 collective-permute-done.6.refs_5_
  13.9 0.0 collective-permute-done.5.refs_4_
  13.9 0.0 copy-start
  13.9 1.0 %copy-done = bf16[512,512]{1,0:T(8,128)(2,1)S(1)} copy-done((bf16[512,512]{1,0:T(8,128)(2,1)S(1)}, bf16[512,512]{1,0:T(8,128)(2,1)}, u32[]{:S(2)}) %copy-start) | copy-done | bytes 524312
  15.0 1.0 %copy-done.2 = bf16[512,512]{1,0:T(8,128)(2,1)S(1)} copy-done((bf16[512,512]{1,0:T(8,128)(2,1)S(1)}, bf16[512,512]{1,0:T(8,128)(2,1)}, u32[]{:S(2)}) %copy-start.2) | copy-done | bytes 524312
  16.0 2.4 %near.1 = (f32[2,256,256]{2,1,0:T(8,128)S(1)}, f32[4,256,512]{2,1,0:T(8,128)S(1)}, bf16[4,512,256]{2,1,0:T(8,128)(2,1)S(1)}, f32[2,256,256]{2,1,0:T(8,128)S(1)}) custom-call(bf16[16,256]{1,0:T(8,128)(2,1)S(1)} %record.1.record_ref, bf16[2,128,256]{2,1,0:T(8,128)(2,1)S(1)} %get-tuple-element.36.refs_0_, ...), custom_call_target="tpu_custom_call" | custom-call | tf_op jit(solution)/shard_map/near/pallas_call | solution.py:479
  18.4 0.1 collective-permute-start.7
  18.5 0.9 %over.1 = (f32[2,256,512]{2,1,0:T(8,128)S(1)}, bf16[2,512,256]{2,1,0:T(8,128)(2,1)S(1)}, f32[2,256,256]{2,1,0:T(8,128)S(1)}) custom-call(f32[2,256,256]{2,1,0:T(8,128)S(1)} %get-tuple-element.40.patch_ref.refs_1_, bf16[2,2,256,256]{3,2,1,0:T(8,128)(2,1)S(1)} %collective-permute-done.2.group.refs_4_, bf16[512,512]{1,0:T(8,128)(2,1)S(1)} %copy-done.3, ...), custom_call_target="tpu_custom_call" | custom-call | tf_op jit(solution)/shard_map/over/pallas_call | solution.py:490
  19.4 1.0 %collective-permute-done.7.refs_5_ = bf16[2,2,256,256]{3,2,1,0:T(8,128)(2,1)S(1)} collective-permute-done((bf16[2,2,256,256]{3,2,1,0:T(8,128)(2,1)S(1)}, bf16[2,2,256,256]{3,2,1,0:T(8,128)(2,1)S(1)}, u32[]{:S(2)}, u32[]{:S(2)}) %collective-permute-start.7) | collective-permute-done | bytes 524320 | tf_op jit(solution)/shard_map/ppermute | solution.py:428
  20.3 4.7 %back.1 = (bf16[272,256]{1,0:T(8,128)(2,1)S(1)}, bf16[272,256]{1,0:T(8,128)(2,1)S(1)}, bf16[272,256]{1,0:T(8,128)(2,1)S(1)}, bf16[272,128]{1,0:T(8,128)(2,1)S(1)...) custom-call(bf16[16,256]{1,0:T(8,128)(2,1)S(1)} %record.1.record_ref, ...), custom_call_target="tpu_custom_call" | custom-call | tf_op jit(solution)/shard_map/back/pallas_call | solution.py:500
  25.1 2.5 %collective-permute-start.8 = (bf16[272,256]{1,0:T(8,128)(2,1)S(1)}, bf16[272,256]{1,0:T(8,128)(2,1)S(1)}, u32[]{:S(2)}, u32[]{:S(2)}) collective-permute-start(bf16[272,256]{1,0:T(8,128)(2,1)S(1)} %get-tuple-element.49), channel_id=1, source_target_pairs={{0,8},{1,0},{2,10},{3,2},{4,12},{5,4},{6,14},{7,6},{8,16},{9,1},{1... | collective-permute-start | bytes 417800 | tf_op jit(solution)/shard_map/ppermute | solution.py:528
  27.5 1.5 %collective-permute-start.10 = (bf16[272,128]{1,0:T(8,128)(2,1)S(1)}, bf16[272,128]{1,0:T(8,128)(2,1)S(1)}, u32[]{:S(2)}, u32[]{:S(2)}) collective-permute-start(bf16[272,128]{1,0:T(8,128)(2,1)S(1)} %get-tuple-element.51), channel_id=1, source_target_pairs={{0,4},{4,0},{1,5},{5,1},{2,6},{6,2},{3,7},{7,3},{8,12},{12,8},{9,1... | collective-permute-start | bytes 208904 | tf_op jit(solution)/shard_map/ppermute | solution.py:533
  29.0 2.0 %collective-permute-start.11 = (bf16[272,128]{1,0:T(8,128)(2,1)S(1)}, bf16[272,128]{1,0:T(8,128)(2,1)S(1)}, u32[]{:S(2)}, u32[]{:S(2)}) collective-permute-start(bf16[272,128]{1,0:T(8,128)(2,1)S(1)} %get-tuple-element.52), channel_id=1, source_target_pairs={{0,12},{1,4},{2,14},{3,6},{4,8},{5,0},{6,10},{7,2},{8,20},{9,5},{1... | collective-permute-start | bytes 208904 | tf_op jit(solution)/shard_map/ppermute | solution.py:535
  31.0 1.3 %collective-permute-done.10.refs_3_ = bf16[272,128]{1,0:T(8,128)(2,1)S(1)} collective-permute-done((bf16[272,128]{1,0:T(8,128)(2,1)S(1)}, bf16[272,128]{1,0:T(8,128)(2,1)S(1)}, u32[]{:S(2)}, u32[]{:S(2)}) %collective-permute-start.10) | collective-permute-done | bytes 69664 | tf_op jit(solution)/shard_map/ppermute | solution.py:533
  32.3 1.0 %collective-permute-done.11.refs_4_ = bf16[272,128]{1,0:T(8,128)(2,1)S(1)} collective-permute-done((bf16[272,128]{1,0:T(8,128)(2,1)S(1)}, bf16[272,128]{1,0:T(8,128)(2,1)S(1)}, u32[]{:S(2)}, u32[]{:S(2)}) %collective-permute-start.11) | collective-permute-done | bytes 69664 | tf_op jit(solution)/shard_map/ppermute | solution.py:535
  33.4 2.8 %collective-permute-done.12.refs_5_ = bf16[272,128]{1,0:T(8,128)(2,1)S(1)} collective-permute-done((bf16[272,128]{1,0:T(8,128)(2,1)S(1)}, bf16[272,128]{1,0:T(8,128)(2,1)S(1)}, u32[]{:S(2)}, u32[]{:S(2)}) %collective-permute-start.12) | collective-permute-done | bytes 69664 | tf_op jit(solution)/shard_map/ppermute | solution.py:535
  36.2 0.1 sums.1.own_ref
  36.4 0.1 collective-permute-start.13
  36.5 0.7 %weights.1.weight_ref = f32[128,256]{1,0:T(8,128)S(1)} custom-call(bf16[256,256]{1,0:T(8,128)(2,1)S(1)} %get-tuple-element.54.weight_ref, bf16[272,256]{1,0:T(8,128)(2,1)S(1)} %get-tuple-element.48.refs_0_, bf16[272,256]{1,0:T(8,128)(2,1)S(1)} %collective-permute-done.8.refs_1_, bf16[272,256]{1,0:T(8,128)(2,1)S(1)} %collective-permute-done.9.refs_2_, ...), custom_call_target="tpu_custom_call" | custom-call | tf_op jit(solution)/shard_map/weights/pallas_call | solution.py:546
  37.2 0.6 %collective-permute-done.13.other_ref = bf16[2,128,256]{2,1,0:T(8,128)(2,1)S(1)} collective-permute-done((bf16[2,128,256]{2,1,0:T(8,128)(2,1)S(1)}, bf16[2,128,256]{2,1,0:T(8,128)(2,1)S(1)}, u32[]{:S(2)}, u32[]{:S(2)}) %collective-permute-start.13) | collective-permute-done | bytes 131104 | tf_op jit(solution)/shard_map/ppermute | solution.py:428
  37.8 0.8 %update.1 = f32[2,128,256]{2,1,0:T(8,128)} custom-call(f32[2,128,256]{2,1,0:T(8,128)S(1)} %copy-done.4, bf16[2,128,256]{2,1,0:T(8,128)(2,1)S(1)} %sums.1.own_ref, bf16[2,128,256]{2,1,0:T(8,128)(2,1)S(1)} %collective-permute-done.13.other_ref, f32[128,256]{1,0:T(8,128)S(1)} %weights.1.weight_ref), custom_call_target="tpu_custom_call" | custom-call | tf_op jit(solution)/shard_map/update/pallas_call | solution.py:555
  (18 shorter events, 0.0 us)
Async XLA Ops:
  0.0 18.4 %copy-start.1 = (bf16[512,512]{1,0:T(8,128)(2,1)S(1)}, bf16[512,512]{1,0:T(8,128)(2,1)}, u32[]{:S(2)}) copy-start(bf16[512,512]{1,0:T(8,128)(2,1)} %constant.5.clone.refs_9_.swapped.refs_7_) | copy-start | bytes 1572868
  0.0 18.5 %copy-start.3 = (bf16[512,512]{1,0:T(8,128)(2,1)S(1)}, bf16[512,512]{1,0:T(8,128)(2,1)}, u32[]{:S(2)}) copy-start(bf16[512,512]{1,0:T(8,128)(2,1)} %constant.4.clone.refs_8_.direct.refs_6_) | copy-start | bytes 1572868
  1.4 3.1 %collective-permute-start = (bf16[2,2,256,256]{3,2,1,0:T(8,128)(2,1)S(1)}, bf16[2,2,256,256]{3,2,1,0:T(8,128)(2,1)S(1)}, u32[]{:S(2)}, u32[]{:S(2)}) collective-permute-start(bf16[2,2,256,256]{3,2,1,0:T(8,128)(2,1)S(1)} %get-tuple-element.30.refs_6_.refs_2_), channel_id=1, source_target_pairs={{0,1},{1,0},{2,3},{3,2},{4,5},{5,4},{6,7},{7,6},{8,9},{9,8},{10,11... | collective-permute-start | bytes 1572872 | tf_op jit(solution)/shard_map/ppermute | solution.py:428
  1.9 16.4 %collective-permute-start.2 = (bf16[2,2,256,256]{3,2,1,0:T(8,128)(2,1)S(1)}, bf16[2,2,256,256]{3,2,1,0:T(8,128)(2,1)S(1)}, u32[]{:S(2)}, u32[]{:S(2)}) collective-permute-start(bf16[2,2,256,256]{3,2,1,0:T(8,128)(2,1)S(1)} %get-tuple-element.30.refs_6_.refs_2_), channel_id=1, source_target_pairs={{0,2},{1,3},{2,0},{3,1},{4,6},{5,7},{6,4},{7,5},{8,10},{9,11},{10,... | collective-permute-start | bytes 1572872 | tf_op jit(solution)/shard_map/ppermute | solution.py:428
  4.5 4.3 %collective-permute-start.1 = (bf16[2,128,128]{2,1,0:T(8,128)(2,1)S(1)}, bf16[2,128,128]{2,1,0:T(8,128)(2,1)S(1)}, u32[]{:S(2)}, u32[]{:S(2)}) collective-permute-start(bf16[2,128,128]{2,1,0:T(8,128)(2,1)S(1)} %get-tuple-element.33), channel_id=1, source_target_pairs={{0,4},{4,0},{1,5},{5,1},{2,6},{6,2},{3,7},{7,3},{8,12},{12,8},{9,1... | collective-permute-start | bytes 196616 | tf_op jit(solution)/shard_map/ppermute | solution.py:454
  6.3 7.6 %collective-permute-start.4 = (bf16[2,128,256]{2,1,0:T(8,128)(2,1)S(1)}, bf16[2,128,256]{2,1,0:T(8,128)(2,1)S(1)}, u32[]{:S(2)}, u32[]{:S(2)}) collective-permute-start(bf16[2,128,256]{2,1,0:T(8,128)(2,1)S(1)} %get-tuple-element.36.refs_0_), channel_id=1, source_target_pairs={{0,1},{1,9},{2,3},{3,11},{4,5},{5,13},{6,7},{7,15},{8,0},{9,17},{1... | collective-permute-start | bytes 393224 | tf_op jit(solution)/shard_map/ppermute | solution.py:452
  6.3 7.6 %collective-permute-start.3 = (bf16[2,128,256]{2,1,0:T(8,128)(2,1)S(1)}, bf16[2,128,256]{2,1,0:T(8,128)(2,1)S(1)}, u32[]{:S(2)}, u32[]{:S(2)}) collective-permute-start(bf16[2,128,256]{2,1,0:T(8,128)(2,1)S(1)} %get-tuple-element.36.refs_0_), channel_id=1, source_target_pairs={{0,8},{1,0},{2,10},{3,2},{4,12},{5,4},{6,14},{7,6},{8,16},{9,1},{1... | collective-permute-start | bytes 393224 | tf_op jit(solution)/shard_map/ppermute | solution.py:452
  8.4 5.5 %collective-permute-start.6 = (bf16[2,128,128]{2,1,0:T(8,128)(2,1)S(1)}, bf16[2,128,128]{2,1,0:T(8,128)(2,1)S(1)}, u32[]{:S(2)}, u32[]{:S(2)}) collective-permute-start(bf16[2,128,128]{2,1,0:T(8,128)(2,1)S(1)} %get-tuple-element.33), channel_id=1, source_target_pairs={{0,5},{1,13},{2,7},{3,15},{4,1},{5,9},{6,3},{7,11},{8,4},{9,21},{1... | collective-permute-start | bytes 196616 | tf_op jit(solution)/shard_map/ppermute | solution.py:455
  8.8 5.1 %collective-permute-start.5 = (bf16[2,128,128]{2,1,0:T(8,128)(2,1)S(1)}, bf16[2,128,128]{2,1,0:T(8,128)(2,1)S(1)}, u32[]{:S(2)}, u32[]{:S(2)}) collective-permute-start(bf16[2,128,128]{2,1,0:T(8,128)(2,1)S(1)} %get-tuple-element.33), channel_id=1, source_target_pairs={{0,12},{1,4},{2,14},{3,6},{4,8},{5,0},{6,10},{7,2},{8,20},{9,5},{1... | collective-permute-start | bytes 196616 | tf_op jit(solution)/shard_map/ppermute | solution.py:455
  12.3 0.7 %copy-start.6 = (s32[1,1,2,2]{3,2,1,0:T(2,128)S(1)}, s32[1,1,2,2]{3,2,1,0:T(2,128)}, u32[]{:S(2)}) copy-start(s32[1,1,2,2]{3,2,1,0:T(2,128)} %centers_ref) | copy-start | bytes 52
  13.9 1.0 %copy-start = (bf16[512,512]{1,0:T(8,128)(2,1)S(1)}, bf16[512,512]{1,0:T(8,128)(2,1)}, u32[]{:S(2)}) copy-start(bf16[512,512]{1,0:T(8,128)(2,1)} %constant.5.clone.refs_9_.swapped.refs_7_) | copy-start | bytes 1572868
  15.0 1.0 %copy-start.2 = (bf16[512,512]{1,0:T(8,128)(2,1)S(1)}, bf16[512,512]{1,0:T(8,128)(2,1)}, u32[]{:S(2)}) copy-start(bf16[512,512]{1,0:T(8,128)(2,1)} %constant.4.clone.refs_8_.direct.refs_6_) | copy-start | bytes 1572868
  16.0 4.4 %copy-start.5 = (bf16[1,1,2,256,256]{4,3,2,1,0:T(8,128)(2,1)S(1)}, bf16[1,1,2,256,256]{4,3,2,1,0:T(8,128)(2,1)}, u32[]{:S(2)}) copy-start(bf16[1,1,2,256,256]{4,3,2,1,0:T(8,128)(2,1)} %refs_0_.1) | copy-start | bytes 786436
  18.4 2.0 %collective-permute-start.7 = (bf16[2,2,256,256]{3,2,1,0:T(8,128)(2,1)S(1)}, bf16[2,2,256,256]{3,2,1,0:T(8,128)(2,1)S(1)}, u32[]{:S(2)}, u32[]{:S(2)}) collective-permute-start(bf16[2,2,256,256]{3,2,1,0:T(8,128)(2,1)S(1)} %collective-permute-done.2.group.refs_4_), channel_id=1, source_target_pairs={{0,1},{1,0},{2,3},{3,2},{4,5},{5,4},{6,7},{7,6},{8,9},{9,8},{10,11... | collective-permute-start | bytes 1572872 | tf_op jit(solution)/shard_map/ppermute | solution.py:428
  20.3 17.5 %copy-start.4 = (f32[2,128,256]{2,1,0:T(8,128)S(1)}, f32[2,128,256]{2,1,0:T(8,128)}, u32[]{:S(2)}) copy-start(f32[2,128,256]{2,1,0:T(8,128)} %object_ref.1) | copy-start | bytes 786436
  25.1 11.2 %collective-permute-start.8 = (bf16[272,256]{1,0:T(8,128)(2,1)S(1)}, bf16[272,256]{1,0:T(8,128)(2,1)S(1)}, u32[]{:S(2)}, u32[]{:S(2)}) collective-permute-start(bf16[272,256]{1,0:T(8,128)(2,1)S(1)} %get-tuple-element.49), channel_id=1, source_target_pairs={{0,8},{1,0},{2,10},{3,2},{4,12},{5,4},{6,14},{7,6},{8,16},{9,1},{1... | collective-permute-start | bytes 417800 | tf_op jit(solution)/shard_map/ppermute | solution.py:528
  27.5 8.7 %collective-permute-start.9 = (bf16[272,256]{1,0:T(8,128)(2,1)S(1)}, bf16[272,256]{1,0:T(8,128)(2,1)S(1)}, u32[]{:S(2)}, u32[]{:S(2)}) collective-permute-start(bf16[272,256]{1,0:T(8,128)(2,1)S(1)} %get-tuple-element.50), channel_id=1, source_target_pairs={{0,1},{1,9},{2,3},{3,11},{4,5},{5,13},{6,7},{7,15},{8,0},{9,17},{1... | collective-permute-start | bytes 417800 | tf_op jit(solution)/shard_map/ppermute | solution.py:528
  27.5 4.8 %collective-permute-start.10 = (bf16[272,128]{1,0:T(8,128)(2,1)S(1)}, bf16[272,128]{1,0:T(8,128)(2,1)S(1)}, u32[]{:S(2)}, u32[]{:S(2)}) collective-permute-start(bf16[272,128]{1,0:T(8,128)(2,1)S(1)} %get-tuple-element.51), channel_id=1, source_target_pairs={{0,4},{4,0},{1,5},{5,1},{2,6},{6,2},{3,7},{7,3},{8,12},{12,8},{9,1... | collective-permute-start | bytes 208904 | tf_op jit(solution)/shard_map/ppermute | solution.py:533
  29.0 4.4 %collective-permute-start.11 = (bf16[272,128]{1,0:T(8,128)(2,1)S(1)}, bf16[272,128]{1,0:T(8,128)(2,1)S(1)}, u32[]{:S(2)}, u32[]{:S(2)}) collective-permute-start(bf16[272,128]{1,0:T(8,128)(2,1)S(1)} %get-tuple-element.52), channel_id=1, source_target_pairs={{0,12},{1,4},{2,14},{3,6},{4,8},{5,0},{6,10},{7,2},{8,20},{9,5},{1... | collective-permute-start | bytes 208904 | tf_op jit(solution)/shard_map/ppermute | solution.py:535
  31.0 5.2 %collective-permute-start.12 = (bf16[272,128]{1,0:T(8,128)(2,1)S(1)}, bf16[272,128]{1,0:T(8,128)(2,1)S(1)}, u32[]{:S(2)}, u32[]{:S(2)}) collective-permute-start(bf16[272,128]{1,0:T(8,128)(2,1)S(1)} %get-tuple-element.53), channel_id=1, source_target_pairs={{0,5},{1,13},{2,7},{3,15},{4,1},{5,9},{6,3},{7,11},{8,4},{9,21},{1... | collective-permute-start | bytes 208904 | tf_op jit(solution)/shard_map/ppermute | solution.py:535
  36.4 1.4 %collective-permute-start.13 = (bf16[2,128,256]{2,1,0:T(8,128)(2,1)S(1)}, bf16[2,128,256]{2,1,0:T(8,128)(2,1)S(1)}, u32[]{:S(2)}, u32[]{:S(2)}) collective-permute-start(bf16[2,128,256]{2,1,0:T(8,128)(2,1)S(1)} %sums.1.own_ref), channel_id=1, source_target_pairs={{0,1},{1,0},{2,3},{3,2},{4,5},{5,4},{6,7},{7,6},{8,9},{9,8},{10,11... | collective-permute-start | bytes 393224 | tf_op jit(solution)/shard_map/ppermute | solution.py:428

commit v5 on v4

--- a/solution.py
+++ b/solution.py
@@ -46,6 +46,20 @@
     left = jnp.where(x_index > 0, at - tile_cols, nowhere)
     right = jnp.where(x_index < x_count - 1, at, nowhere)
     return jnp.where(at < tile_cols, own, jnp.where(at < tile_cols + half, left, right))
+
+
+def sent_order(sides):
+    corners = [at for index in range(sides) for at in (4 + 3 * index, 5 + 3 * index)]
+    return [0] + corners + [1, 2] + [3 + 3 * index for index in range(sides)]
+
+
+def in_sent_order(pieces):
+    return [pieces[at] for at in sent_order(len(pieces) // 3 - 1)]
+
+
+def from_sent_order(pieces):
+    order = sent_order(len(pieces) // 3 - 1)
+    return [pieces[order.index(at)] for at in range(len(pieces))]
 
 
 def wide(tall):
@@ -90,7 +104,15 @@
             edges[1][channel] = values[:, first]
 
 
-def record_kernel(slots, centers_ref, live_ref, out_ref):
+def record_kernel(
+    slots, centers_ref, live_ref, direct_hbm, swapped_hbm, out_ref, direct_ref, swapped_ref, sems
+):
+    copies = [
+        pltpu.make_async_copy(direct_hbm, direct_ref, sems.at[0]),
+        pltpu.make_async_copy(swapped_hbm, swapped_ref, sems.at[1]),
+    ]
+    for copy in copies:
+        copy.start()
     record = jnp.zeros(out_ref.shape, jnp.float32)
     line = iota(out_ref.shape, 0)
     for slot in range(slots):
@@ -99,6 +121,8 @@
             record = jnp.where(line == 2 * slot + axis, value, record)
     record = jnp.where(line == 2 * slots, live_ref[0, 0].astype(jnp.float32), record)
     out_ref[...] = record.astype(jnp.bfloat16)
+    for copy in copies:
+        copy.wait()
 
 
 def positions(record_ref, slots):
@@ -215,7 +239,7 @@
 
 def near_kernel(sides, slots, z_count, x_count, record_ref, *refs):
     n_pieces = 3 + 3 * sides
-    pieces = refs[:n_pieces]
+    pieces = from_sent_order(refs[:n_pieces])
     own, core, direct, swapped = refs[n_pieces : n_pieces + 4]
     patch_ref, far_ref, exit_ref, sum_ref, ext_ref = refs[n_pieces + 4 :]
     side = own.shape[2]
@@ -285,7 +309,7 @@
 
 
 def weight_kernel(sides, slots, z_count, x_count, weight_ref, *refs):
-    pieces, out_ref = refs[:-1], refs[-1]
+    pieces, out_ref = from_sent_order(refs[:-1]), refs[-1]
     tile_rows, tile_cols = out_ref.shape
     side = weight_ref.shape[0]
     half = side // 2
@@ -328,7 +352,7 @@
 
 
 def sum_kernel(sides, z_count, x_count, *refs):
-    pieces, out_ref = refs[:-1], refs[-1]
+    pieces, out_ref = from_sent_order(refs[:-1]), refs[-1]
     own_ref, rows_a, rows_b = pieces[:3]
     _, tile_rows, tile_cols = out_ref.shape
     half = pieces[3].shape[1]
@@ -400,7 +424,7 @@
     sides = 1 if x_count == 2 else 2
     axes = ("tx", "ty", "mode")
 
-    def zigzag(flip, x_step):
+    def zigzag(x_step, flip=False):
         def moved(z, m):
             down = (m % 2 == 0) != flip
             if down:
@@ -448,27 +472,30 @@
     probe_core = exchange(probe_low, 1)
     probe_core, *packed = lax.optimization_barrier((probe_core, *packed))
     x_steps = [1] if sides == 1 else [1, -1]
-    pieces = [packed[0]]
-    pieces += [lax.ppermute(packed[0], axes, zigzag(flip, 0)) for flip in (False, True)]
+    moved = [lax.ppermute(packed[0], axes, zigzag(0))]
+    levels = []
     for step, edge in zip(x_steps, packed[1:]):
-        pieces.append(lax.ppermute(edge, "ty", level(step)))
-        pieces += [lax.ppermute(edge, axes, zigzag(flip, step)) for flip in (False, True)]
-
+        moved.append(lax.ppermute(edge, axes, zigzag(step)))
+        levels.append(lax.ppermute(edge, "ty", level(step)))
+    pieces = [packed[0], moved[0], exchange(moved[0], 1)]
+    for here_level, corner in zip(levels, moved[1:]):
+        pieces += [here_level, corner, exchange(corner, 1)]
+    tables = [in_hbm(jnp.asarray(matrix)) for matrix in dft_matrices(side)]
     centers, live, pieces[3] = lax.optimization_barrier((centers, live, pieces[3]))
-    record = pl.pallas_call(
+    record, direct, swapped = pl.pallas_call(
         functools.partial(record_kernel, slots),
-        out_shape=jax.ShapeDtypeStruct((record_rows, tile_cols), jnp.bfloat16),
-        in_specs=[smem(), smem()],
-        out_specs=vmem(),
+        out_shape=[jax.ShapeDtypeStruct((record_rows, tile_cols), jnp.bfloat16)]
+        + [jax.ShapeDtypeStruct((2 * side, 2 * side), jnp.bfloat16)] * 2,
+        in_specs=[smem(), smem(), hbm(), hbm()],
+        out_specs=[vmem()] * 3,
+        scratch_shapes=[pltpu.SemaphoreType.DMA((2,))],
         compiler_params=pltpu.CompilerParams(vmem_limit_bytes=small_bytes),
         name="record",
-    )(centers, live)
+    )(centers, live, *tables)
     n_pieces = len(pieces)
     modes = probe.shape[1]
     ext_rows = tile_rows + side
     ext_cols = tile_cols + sides * half
-    direct, swapped = (jnp.asarray(matrix) for matrix in dft_matrices(side))
-
     def waves(count):
         return [
             jax.ShapeDtypeStruct((count, side, 2 * side), jnp.float32),
@@ -484,7 +511,7 @@
         scratch_shapes=[pltpu.VMEM((2 * ext_rows, ext_cols), jnp.bfloat16)],
         compiler_params=pltpu.CompilerParams(vmem_limit_bytes=wave_bytes),
         name="near",
-    )(record, *pieces, probe_low, probe_core, direct, swapped)
+    )(record, *in_sent_order(pieces), probe_low, probe_core, direct, swapped)
     probe_y, patch = lax.optimization_barrier((probe_y, patch))
     probe_diagonal = exchange(probe_y, 1)
     over = pl.pallas_call(
@@ -523,18 +550,15 @@
         *near,
         *over,
     )
-    received = [results[0]]
-    received += [
-        lax.ppermute(results[1 + index], axes, zigzag(flip, 0))
-        for index, flip in enumerate((False, True))
-    ]
+    received = [results[0]] + [None] * (n_pieces - 1)
     for index, step in enumerate(x_steps):
-        back_step = -step
-        received.append(lax.ppermute(results[3 + 3 * index], "ty", level(back_step)))
-        received += [
-            lax.ppermute(results[4 + 3 * index + turn], axes, zigzag(flip, back_step))
-            for turn, flip in enumerate((False, True))
-        ]
+        at = 3 + 3 * index
+        for turn, flip in enumerate((False, True)):
+            received[at + 1 + turn] = lax.ppermute(results[at + 1 + turn], axes, zigzag(-step, flip))
+    for turn, flip in enumerate((False, True)):
+        received[1 + turn] = lax.ppermute(results[1 + turn], axes, zigzag(0, flip))
+    for index, step in enumerate(x_steps):
+        received[3 + 3 * index] = lax.ppermute(results[3 + 3 * index], "ty", level(-step))
     summed = pl.pallas_call(
         functools.partial(sum_kernel, sides, z_count, x_count),
         out_shape=jax.ShapeDtypeStruct(object_field.shape, jnp.bfloat16),
@@ -542,7 +566,7 @@
         out_specs=vmem(),
         compiler_params=pltpu.CompilerParams(vmem_limit_bytes=small_bytes),
         name="sums",
-    )(*received)
+    )(*in_sent_order(received))
     weight = pl.pallas_call(
         functools.partial(weight_kernel, sides, slots, z_count, x_count),
         out_shape=jax.ShapeDtypeStruct((tile_rows, tile_cols), jnp.float32),
@@ -550,7 +574,7 @@
         out_specs=vmem(),
         compiler_params=pltpu.CompilerParams(vmem_limit_bytes=small_bytes),
         name="weights",
-    )(results[-1], *received)
+    )(results[-1], *in_sent_order(received))
     other = exchange(summed, 1)
     return pl.pallas_call(
         update_kernel,

time: 38.8 us -> 38.1 us (0.982)
  local copies, waits for them, and re-layouts: 2.77 us -> 0.69 us
  Pallas kernels: 11.6 us -> 12.8 us
  waiting for transfers between devices: 7.6 us -> 8.48 us
  starting transfers between devices: 15.9 us -> 15.3 us
    unnamed x14 -> x6, local copies, waits for them, and re-layouts: 2.77 us -> 0.69 us
    pallas_call x1, Pallas kernels: 0.56 us -> 1.76 us  [on_device(): pl.pallas_call(functools.partial(record_kernel, slots), out_shape=[jax.Sh...]
    ppermute x10 -> x8, waiting for transfers between devices: 6.04 us -> 6.89 us  [the longest x2 4.67 us: on_device(): lax.ppermute(results[at + 1 + turn], axes, zigzag(-step, flip))]
    ppermute x10 -> x8, starting transfers between devices: 12.6 us -> 12 us  [the longest x2 2.95 us: on_device(): lax.ppermute(results[at + 1 + turn], axes, zigzag(-step, flip))]
    ppermute x4 -> x6, waiting for transfers between devices: 1.57 us -> 1.59 us  [exchange(): return lax.ppermute(array, 'mode', [(m, m ^ flip) for m in range(m_count)])]
    ppermute x4 -> x6, starting transfers between devices: 3.25 us -> 3.26 us  [exchange(): return lax.ppermute(array, 'mode', [(m, m ^ flip) for m in range(m_count)])]
  transfers between devices with their start and end apart: 14 -> 14, of which waited for: 7 -> 6; matrix products, arithmetic and copies ran while one was open for 0% -> 0% of each run, Pallas kernels for 12% -> 15%
where the time goes in v5:
time: 38.1 us; the launch traced here: 37.9 us
  starting transfers between devices  15.3 us (40%)
  Pallas kernels  12.8 us (34%)
  waiting for transfers between devices  8.48 us (22%)
  between operations  0.76 us (2%)
  local copies, waits for them, and re-layouts  0.69 us (2%)
    pallas_call x1, Pallas kernels, on_device(): pl.pallas_call(functools.partial(back_kernel, sides, slots, x_count, tile...  4.71 us
    ppermute x2, waiting for transfers between devices, on_device(): lax.ppermute(results[at + 1 + turn], axes, zigzag(-step, flip))  4.67 us
    ppermute x6, starting transfers between devices, exchange(): return lax.ppermute(array, 'mode', [(m, m ^ flip) for m in range(m_count)])  3.26 us
    ppermute x2, starting transfers between devices, on_device(): lax.ppermute(results[at + 1 + turn], axes, zigzag(-step, flip))  2.95 us
    ppermute x1, starting transfers between devices, on_device(): moved.append(lax.ppermute(edge, axes, zigzag(step)))  2.5 us
    ppermute x2, starting transfers between devices, on_device(): received[1 + turn] = lax.ppermute(results[1 + turn], axes, zigzag(0, flip))  2.46 us
    pallas_call x1, Pallas kernels, on_device(): pl.pallas_call(functools.partial(near_kernel, sides, slots, z_count, x_co...  2.44 us
    ppermute x1, waiting for transfers between devices, on_device(): levels.append(lax.ppermute(edge, 'ty', level(step)))  1.97 us
  transfers between devices with their start and end apart: 14, of which 6 were waited for; matrix products, arithmetic and copies ran while one was open for 0% of the time, Pallas kernels for 15%

profile of v5, /device:TPU:0, one launch (start us, length us, event | category | flops | bytes accessed | tf_op | source)
XLA Modules:
  0.0 37.9 jit_solution(3217058287195537207)
XLA Ops:
  0.0 1.3 %start.1 = (bf16[2,2,256,256]{3,2,1,0:T(8,128)(2,1)S(1)}, bf16[2,128,256]{2,1,0:T(8,128)(2,1)S(1)}, bf16[2,128,128]{2,1,0:T(8,128)(2,1)S(1)}) custom-call(f32[2,128,256]{2,1,0:T(8,128)} %object_ref.1, f32[2,2,256,256]{3,2,1,0:T(8,128)} %probe_hbm.1), custom_call_target="tpu_custom_call" | custom-call | tf_op jit(solution)/shard_map/start/pallas_call | solution.py:454
  1.3 0.5 %collective-permute-start = (bf16[2,2,256,256]{3,2,1,0:T(8,128)(2,1)S(1)}, bf16[2,2,256,256]{3,2,1,0:T(8,128)(2,1)S(1)}, u32[]{:S(2)}, u32[]{:S(2)}) collective-permute-start(bf16[2,2,256,256]{3,2,1,0:T(8,128)(2,1)S(1)} %get-tuple-element.33.refs_6_.refs_2_), channel_id=1, source_target_pairs={{0,1},{1,0},{2,3},{3,2},{4,5},{5,4},{6,7},{7,6},{8,9},{9,8},{10,11... | collective-permute-start | bytes 1572872 | tf_op jit(solution)/shard_map/ppermute | solution.py:452
  1.8 2.6 %collective-permute-start.2 = (bf16[2,2,256,256]{3,2,1,0:T(8,128)(2,1)S(1)}, bf16[2,2,256,256]{3,2,1,0:T(8,128)(2,1)S(1)}, u32[]{:S(2)}, u32[]{:S(2)}) collective-permute-start(bf16[2,2,256,256]{3,2,1,0:T(8,128)(2,1)S(1)} %get-tuple-element.33.refs_6_.refs_2_), channel_id=1, source_target_pairs={{0,2},{1,3},{2,0},{3,1},{4,6},{5,7},{6,4},{7,5},{8,10},{9,11},{10,... | collective-permute-start | bytes 1572872 | tf_op jit(solution)/shard_map/ppermute | solution.py:452
  4.4 1.9 %collective-permute-start.5 = (bf16[2,128,256]{2,1,0:T(8,128)(2,1)S(1)}, bf16[2,128,256]{2,1,0:T(8,128)(2,1)S(1)}, u32[]{:S(2)}, u32[]{:S(2)}) collective-permute-start(bf16[2,128,256]{2,1,0:T(8,128)(2,1)S(1)} %get-tuple-element.40.refs_0_), channel_id=1, source_target_pairs={{0,8},{1,0},{2,10},{3,2},{4,12},{5,4},{6,14},{7,6},{8,16},{9,1},{1... | collective-permute-start | bytes 393224 | tf_op jit(solution)/shard_map/ppermute | solution.py:475
  6.3 2.5 %collective-permute-start.3 = (bf16[2,128,128]{2,1,0:T(8,128)(2,1)S(1)}, bf16[2,128,128]{2,1,0:T(8,128)(2,1)S(1)}, u32[]{:S(2)}, u32[]{:S(2)}) collective-permute-start(bf16[2,128,128]{2,1,0:T(8,128)(2,1)S(1)} %get-tuple-element.36), channel_id=1, source_target_pairs={{0,12},{1,4},{2,14},{3,6},{4,8},{5,0},{6,10},{7,2},{8,20},{9,5},{1... | collective-permute-start | bytes 196616 | tf_op jit(solution)/shard_map/ppermute | solution.py:478
  8.8 0.0 collective-permute-done.5.refs_3_
  8.8 0.0 collective-permute-start.6
  8.8 1.7 %collective-permute-start.1 = (bf16[2,128,128]{2,1,0:T(8,128)(2,1)S(1)}, bf16[2,128,128]{2,1,0:T(8,128)(2,1)S(1)}, u32[]{:S(2)}, u32[]{:S(2)}) collective-permute-start(bf16[2,128,128]{2,1,0:T(8,128)(2,1)S(1)} %get-tuple-element.36), channel_id=1, source_target_pairs={{0,4},{4,0},{1,5},{5,1},{2,6},{6,2},{3,7},{7,3},{8,12},{12,8},{9,1... | collective-permute-start | bytes 196616 | tf_op jit(solution)/shard_map/ppermute | solution.py:479
  10.5 0.2 collective-permute-done.3.refs_1_
  10.7 0.0 collective-permute-start.4
  11.4 2.0 %collective-permute-done.1.refs_5_ = bf16[2,128,128]{2,1,0:T(8,128)(2,1)S(1)} collective-permute-done((bf16[2,128,128]{2,1,0:T(8,128)(2,1)S(1)}, bf16[2,128,128]{2,1,0:T(8,128)(2,1)S(1)}, u32[]{:S(2)}, u32[]{:S(2)}) %collective-permute-start.1) | collective-permute-done | bytes 65568 | tf_op jit(solution)/shard_map/ppermute | solution.py:479
  13.4 0.7 %copy-done.2 = s32[1,1,2,2]{3,2,1,0:T(2,128)S(1)} copy-done((s32[1,1,2,2]{3,2,1,0:T(2,128)S(1)}, s32[1,1,2,2]{3,2,1,0:T(2,128)}, u32[]{:S(2)}) %copy-start.2) | copy-done | bytes 40
  14.0 1.8 %record.1 = (bf16[16,256]{1,0:T(8,128)(2,1)S(1)}, bf16[512,512]{1,0:T(8,128)(2,1)S(1)}, bf16[512,512]{1,0:T(8,128)(2,1)S(1)}) custom-call(s32[1,1,2,2]{3,2,1,0:T(2,128)S(1)} %copy-done.2, s32[1,1]{1,0:T(1,128)S(6)} %copy.8.live_ref, bf16[512,512]{1,0:T(8,128)(2,1)} %constant.4.clone.direct_hbm, bf16[512,512]{1,0:T(8,128)(2,1)} %constant.5.clone.swapped_hbm), custom_call_target="tpu_custom_call" | custom-call | tf_op jit(solution)/shard_map/record/pallas_call | solution.py:485
  15.8 0.0 collective-permute-done.6.refs_4_
  15.8 0.0 copy-start.1
  15.8 2.4 %near.1 = (f32[2,256,256]{2,1,0:T(8,128)S(1)}, f32[4,256,512]{2,1,0:T(8,128)S(1)}, bf16[4,512,256]{2,1,0:T(8,128)(2,1)S(1)}, f32[2,256,256]{2,1,0:T(8,128)S(1)}) custom-call(bf16[16,256]{1,0:T(8,128)(2,1)S(1)} %get-tuple-element.39.record_ref, bf16[2,128,256]{2,1,0:T(8,128)(2,1)S(1)} %get-tuple-element.40.refs_0_, ...), custom_call_target="tpu_custom_call" | custom-call | tf_op jit(solution)/shard_map/near/pallas_call | solution.py:506
  18.3 0.0 collective-permute-done.2.group.refs_4_
  18.3 0.1 collective-permute-start.7
  18.4 0.9 %over.1 = (f32[2,256,512]{2,1,0:T(8,128)S(1)}, bf16[2,512,256]{2,1,0:T(8,128)(2,1)S(1)}, f32[2,256,256]{2,1,0:T(8,128)S(1)}) custom-call(f32[2,256,256]{2,1,0:T(8,128)S(1)} %get-tuple-element.46.patch_ref.refs_1_, bf16[2,2,256,256]{3,2,1,0:T(8,128)(2,1)S(1)} %collective-permute-done.2.group.refs_4_, ...), custom_call_target="tpu_custom_call" | custom-call | tf_op jit(solution)/shard_map/over/pallas_call | solution.py:517
  19.3 1.0 %collective-permute-done.7.refs_5_ = bf16[2,2,256,256]{3,2,1,0:T(8,128)(2,1)S(1)} collective-permute-done((bf16[2,2,256,256]{3,2,1,0:T(8,128)(2,1)S(1)}, bf16[2,2,256,256]{3,2,1,0:T(8,128)(2,1)S(1)}, u32[]{:S(2)}, u32[]{:S(2)}) %collective-permute-start.7) | collective-permute-done | bytes 524320 | tf_op jit(solution)/shard_map/ppermute | solution.py:452
  20.3 4.7 %back.1 = (bf16[272,256]{1,0:T(8,128)(2,1)S(1)}, bf16[272,256]{1,0:T(8,128)(2,1)S(1)}, bf16[272,256]{1,0:T(8,128)(2,1)S(1)}, bf16[272,128]{1,0:T(8,128)(2,1)S(1)...) custom-call(bf16[16,256]{1,0:T(8,128)(2,1)S(1)} %get-tuple-element.39.record_ref, ...), custom_call_target="tpu_custom_call" | custom-call | tf_op jit(solution)/shard_map/back/pallas_call | solution.py:527
  25.0 2.5 %collective-permute-start.10 = (bf16[272,256]{1,0:T(8,128)(2,1)S(1)}, bf16[272,256]{1,0:T(8,128)(2,1)S(1)}, u32[]{:S(2)}, u32[]{:S(2)}) collective-permute-start(bf16[272,256]{1,0:T(8,128)(2,1)S(1)} %get-tuple-element.57), channel_id=1, source_target_pairs={{0,8},{1,0},{2,10},{3,2},{4,12},{5,4},{6,14},{7,6},{8,16},{9,1},{1... | collective-permute-start | bytes 417800 | tf_op jit(solution)/shard_map/ppermute | solution.py:559
  27.4 2.9 %collective-permute-start.8 = (bf16[272,128]{1,0:T(8,128)(2,1)S(1)}, bf16[272,128]{1,0:T(8,128)(2,1)S(1)}, u32[]{:S(2)}, u32[]{:S(2)}) collective-permute-start(bf16[272,128]{1,0:T(8,128)(2,1)S(1)} %get-tuple-element.55), channel_id=1, source_target_pairs={{0,12},{1,4},{2,14},{3,6},{4,8},{5,0},{6,10},{7,2},{8,20},{9,5},{1... | collective-permute-start | bytes 208904 | tf_op jit(solution)/shard_map/ppermute | solution.py:557
  30.4 0.0 collective-permute-start.9
  30.4 0.5 %collective-permute-start.12 = (bf16[272,128]{1,0:T(8,128)(2,1)S(1)}, bf16[272,128]{1,0:T(8,128)(2,1)S(1)}, u32[]{:S(2)}, u32[]{:S(2)}) collective-permute-start(bf16[272,128]{1,0:T(8,128)(2,1)S(1)} %get-tuple-element.59), channel_id=1, source_target_pairs={{0,4},{4,0},{1,5},{5,1},{2,6},{6,2},{3,7},{7,3},{8,12},{12,8},{9,1... | collective-permute-start | bytes 208904 | tf_op jit(solution)/shard_map/ppermute | solution.py:561
  30.9 1.4 %collective-permute-done.8.refs_1_ = bf16[272,128]{1,0:T(8,128)(2,1)S(1)} collective-permute-done((bf16[272,128]{1,0:T(8,128)(2,1)S(1)}, bf16[272,128]{1,0:T(8,128)(2,1)S(1)}, u32[]{:S(2)}, u32[]{:S(2)}) %collective-permute-start.8) | collective-permute-done | bytes 69664 | tf_op jit(solution)/shard_map/ppermute | solution.py:557
  32.3 3.3 %collective-permute-done.9.refs_2_ = bf16[272,128]{1,0:T(8,128)(2,1)S(1)} collective-permute-done((bf16[272,128]{1,0:T(8,128)(2,1)S(1)}, bf16[272,128]{1,0:T(8,128)(2,1)S(1)}, u32[]{:S(2)}, u32[]{:S(2)}) %collective-permute-start.9) | collective-permute-done | bytes 69664 | tf_op jit(solution)/shard_map/ppermute | solution.py:557
  35.6 0.1 sums.1.own_ref
  35.8 0.1 collective-permute-start.13
  35.8 0.7 %weights.1.weight_ref = f32[128,256]{1,0:T(8,128)S(1)} custom-call(bf16[256,256]{1,0:T(8,128)(2,1)S(1)} %get-tuple-element.60.weight_ref, bf16[272,256]{1,0:T(8,128)(2,1)S(1)} %get-tuple-element.54.refs_0_, bf16[272,128]{1,0:T(8,128)(2,1)S(1)} %collective-permute-done.8.refs_1_, bf16[272,128]{1,0:T(8,128)(2,1)S(1)} %collective-permute-done.9.refs_2_, ...), custom_call_target="tpu_custom_call" | custom-call | tf_op jit(solution)/shard_map/weights/pallas_call | solution.py:570
  36.6 0.6 %collective-permute-done.13.other_ref = bf16[2,128,256]{2,1,0:T(8,128)(2,1)S(1)} collective-permute-done((bf16[2,128,256]{2,1,0:T(8,128)(2,1)S(1)}, bf16[2,128,256]{2,1,0:T(8,128)(2,1)S(1)}, u32[]{:S(2)}, u32[]{:S(2)}) %collective-permute-start.13) | collective-permute-done | bytes 131104 | tf_op jit(solution)/shard_map/ppermute | solution.py:452
  37.2 0.8 %update.1 = f32[2,128,256]{2,1,0:T(8,128)} custom-call(f32[2,128,256]{2,1,0:T(8,128)S(1)} %copy-done, bf16[2,128,256]{2,1,0:T(8,128)(2,1)S(1)} %sums.1.own_ref, bf16[2,128,256]{2,1,0:T(8,128)(2,1)S(1)} %collective-permute-done.13.other_ref, f32[128,256]{1,0:T(8,128)S(1)} %weights.1.weight_ref), custom_call_target="tpu_custom_call" | custom-call | tf_op jit(solution)/shard_map/update/pallas_call | solution.py:579
  (10 shorter events, 0.0 us)
Async XLA Ops:
  1.3 3.1 %collective-permute-start = (bf16[2,2,256,256]{3,2,1,0:T(8,128)(2,1)S(1)}, bf16[2,2,256,256]{3,2,1,0:T(8,128)(2,1)S(1)}, u32[]{:S(2)}, u32[]{:S(2)}) collective-permute-start(bf16[2,2,256,256]{3,2,1,0:T(8,128)(2,1)S(1)} %get-tuple-element.33.refs_6_.refs_2_), channel_id=1, source_target_pairs={{0,1},{1,0},{2,3},{3,2},{4,5},{5,4},{6,7},{7,6},{8,9},{9,8},{10,11... | collective-permute-start | bytes 1572872 | tf_op jit(solution)/shard_map/ppermute | solution.py:452
  1.8 16.4 %collective-permute-start.2 = (bf16[2,2,256,256]{3,2,1,0:T(8,128)(2,1)S(1)}, bf16[2,2,256,256]{3,2,1,0:T(8,128)(2,1)S(1)}, u32[]{:S(2)}, u32[]{:S(2)}) collective-permute-start(bf16[2,2,256,256]{3,2,1,0:T(8,128)(2,1)S(1)} %get-tuple-element.33.refs_6_.refs_2_), channel_id=1, source_target_pairs={{0,2},{1,3},{2,0},{3,1},{4,6},{5,7},{6,4},{7,5},{8,10},{9,11},{10,... | collective-permute-start | bytes 1572872 | tf_op jit(solution)/shard_map/ppermute | solution.py:452
  4.4 4.4 %collective-permute-start.5 = (bf16[2,128,256]{2,1,0:T(8,128)(2,1)S(1)}, bf16[2,128,256]{2,1,0:T(8,128)(2,1)S(1)}, u32[]{:S(2)}, u32[]{:S(2)}) collective-permute-start(bf16[2,128,256]{2,1,0:T(8,128)(2,1)S(1)} %get-tuple-element.40.refs_0_), channel_id=1, source_target_pairs={{0,8},{1,0},{2,10},{3,2},{4,12},{5,4},{6,14},{7,6},{8,16},{9,1},{1... | collective-permute-start | bytes 393224 | tf_op jit(solution)/shard_map/ppermute | solution.py:475
  6.3 4.4 %collective-permute-start.3 = (bf16[2,128,128]{2,1,0:T(8,128)(2,1)S(1)}, bf16[2,128,128]{2,1,0:T(8,128)(2,1)S(1)}, u32[]{:S(2)}, u32[]{:S(2)}) collective-permute-start(bf16[2,128,128]{2,1,0:T(8,128)(2,1)S(1)} %get-tuple-element.36), channel_id=1, source_target_pairs={{0,12},{1,4},{2,14},{3,6},{4,8},{5,0},{6,10},{7,2},{8,20},{9,5},{1... | collective-permute-start | bytes 196616 | tf_op jit(solution)/shard_map/ppermute | solution.py:478
  8.8 7.0 %collective-permute-start.6 = (bf16[2,128,256]{2,1,0:T(8,128)(2,1)S(1)}, bf16[2,128,256]{2,1,0:T(8,128)(2,1)S(1)}, u32[]{:S(2)}, u32[]{:S(2)}) collective-permute-start(bf16[2,128,256]{2,1,0:T(8,128)(2,1)S(1)} %collective-permute-done.5.refs_3_), channel_id=1, source_target_pairs={{0,1},{1,0},{2,3},{3,2},{4,5},{5,4},{6,7},{7,6},{8,9},{9,8},{10,11... | collective-permute-start | bytes 393224 | tf_op jit(solution)/shard_map/ppermute | solution.py:452
  8.8 4.5 %collective-permute-start.1 = (bf16[2,128,128]{2,1,0:T(8,128)(2,1)S(1)}, bf16[2,128,128]{2,1,0:T(8,128)(2,1)S(1)}, u32[]{:S(2)}, u32[]{:S(2)}) collective-permute-start(bf16[2,128,128]{2,1,0:T(8,128)(2,1)S(1)} %get-tuple-element.36), channel_id=1, source_target_pairs={{0,4},{4,0},{1,5},{5,1},{2,6},{6,2},{3,7},{7,3},{8,12},{12,8},{9,1... | collective-permute-start | bytes 196616 | tf_op jit(solution)/shard_map/ppermute | solution.py:479
  10.7 5.1 %collective-permute-start.4 = (bf16[2,128,128]{2,1,0:T(8,128)(2,1)S(1)}, bf16[2,128,128]{2,1,0:T(8,128)(2,1)S(1)}, u32[]{:S(2)}, u32[]{:S(2)}) collective-permute-start(bf16[2,128,128]{2,1,0:T(8,128)(2,1)S(1)} %collective-permute-done.3.refs_1_), channel_id=1, source_target_pairs={{0,1},{1,0},{2,3},{3,2},{4,5},{5,4},{6,7},{7,6},{8,9},{9,8},{10,11... | collective-permute-start | bytes 196616 | tf_op jit(solution)/shard_map/ppermute | solution.py:452
  13.4 0.7 %copy-start.2 = (s32[1,1,2,2]{3,2,1,0:T(2,128)S(1)}, s32[1,1,2,2]{3,2,1,0:T(2,128)}, u32[]{:S(2)}) copy-start(s32[1,1,2,2]{3,2,1,0:T(2,128)} %centers_ref) | copy-start | bytes 52
  15.8 4.4 %copy-start.1 = (bf16[1,1,2,256,256]{4,3,2,1,0:T(8,128)(2,1)S(1)}, bf16[1,1,2,256,256]{4,3,2,1,0:T(8,128)(2,1)}, u32[]{:S(2)}) copy-start(bf16[1,1,2,256,256]{4,3,2,1,0:T(8,128)(2,1)} %refs_0_.1) | copy-start | bytes 786436
  18.3 2.0 %collective-permute-start.7 = (bf16[2,2,256,256]{3,2,1,0:T(8,128)(2,1)S(1)}, bf16[2,2,256,256]{3,2,1,0:T(8,128)(2,1)S(1)}, u32[]{:S(2)}, u32[]{:S(2)}) collective-permute-start(bf16[2,2,256,256]{3,2,1,0:T(8,128)(2,1)S(1)} %collective-permute-done.2.group.refs_4_), channel_id=1, source_target_pairs={{0,1},{1,0},{2,3},{3,2},{4,5},{5,4},{6,7},{7,6},{8,9},{9,8},{10,11... | collective-permute-start | bytes 1572872 | tf_op jit(solution)/shard_map/ppermute | solution.py:452
  20.3 16.9 %copy-start = (f32[2,128,256]{2,1,0:T(8,128)S(1)}, f32[2,128,256]{2,1,0:T(8,128)}, u32[]{:S(2)}) copy-start(f32[2,128,256]{2,1,0:T(8,128)} %object_ref.1) | copy-start | bytes 786436
  25.0 10.6 %collective-permute-start.10 = (bf16[272,256]{1,0:T(8,128)(2,1)S(1)}, bf16[272,256]{1,0:T(8,128)(2,1)S(1)}, u32[]{:S(2)}, u32[]{:S(2)}) collective-permute-start(bf16[272,256]{1,0:T(8,128)(2,1)S(1)} %get-tuple-element.57), channel_id=1, source_target_pairs={{0,8},{1,0},{2,10},{3,2},{4,12},{5,4},{6,14},{7,6},{8,16},{9,1},{1... | collective-permute-start | bytes 417800 | tf_op jit(solution)/shard_map/ppermute | solution.py:559
  27.4 8.2 %collective-permute-start.11 = (bf16[272,256]{1,0:T(8,128)(2,1)S(1)}, bf16[272,256]{1,0:T(8,128)(2,1)S(1)}, u32[]{:S(2)}, u32[]{:S(2)}) collective-permute-start(bf16[272,256]{1,0:T(8,128)(2,1)S(1)} %get-tuple-element.58), channel_id=1, source_target_pairs={{0,1},{1,9},{2,3},{3,11},{4,5},{5,13},{6,7},{7,15},{8,0},{9,17},{1... | collective-permute-start | bytes 417800 | tf_op jit(solution)/shard_map/ppermute | solution.py:559
  27.4 4.9 %collective-permute-start.8 = (bf16[272,128]{1,0:T(8,128)(2,1)S(1)}, bf16[272,128]{1,0:T(8,128)(2,1)S(1)}, u32[]{:S(2)}, u32[]{:S(2)}) collective-permute-start(bf16[272,128]{1,0:T(8,128)(2,1)S(1)} %get-tuple-element.55), channel_id=1, source_target_pairs={{0,12},{1,4},{2,14},{3,6},{4,8},{5,0},{6,10},{7,2},{8,20},{9,5},{1... | collective-permute-start | bytes 208904 | tf_op jit(solution)/shard_map/ppermute | solution.py:557
  30.4 5.2 %collective-permute-start.9 = (bf16[272,128]{1,0:T(8,128)(2,1)S(1)}, bf16[272,128]{1,0:T(8,128)(2,1)S(1)}, u32[]{:S(2)}, u32[]{:S(2)}) collective-permute-start(bf16[272,128]{1,0:T(8,128)(2,1)S(1)} %get-tuple-element.56), channel_id=1, source_target_pairs={{0,5},{1,13},{2,7},{3,15},{4,1},{5,9},{6,3},{7,11},{8,4},{9,21},{1... | collective-permute-start | bytes 208904 | tf_op jit(solution)/shard_map/ppermute | solution.py:557
  30.4 5.2 %collective-permute-start.12 = (bf16[272,128]{1,0:T(8,128)(2,1)S(1)}, bf16[272,128]{1,0:T(8,128)(2,1)S(1)}, u32[]{:S(2)}, u32[]{:S(2)}) collective-permute-start(bf16[272,128]{1,0:T(8,128)(2,1)S(1)} %get-tuple-element.59), channel_id=1, source_target_pairs={{0,4},{4,0},{1,5},{5,1},{2,6},{6,2},{3,7},{7,3},{8,12},{12,8},{9,1... | collective-permute-start | bytes 208904 | tf_op jit(solution)/shard_map/ppermute | solution.py:561
  35.8 1.4 %collective-permute-start.13 = (bf16[2,128,256]{2,1,0:T(8,128)(2,1)S(1)}, bf16[2,128,256]{2,1,0:T(8,128)(2,1)S(1)}, u32[]{:S(2)}, u32[]{:S(2)}) collective-permute-start(bf16[2,128,256]{2,1,0:T(8,128)(2,1)S(1)} %sums.1.own_ref), channel_id=1, source_target_pairs={{0,1},{1,0},{2,3},{3,2},{4,5},{5,4},{6,7},{7,6},{8,9},{9,8},{10,11... | collective-permute-start | bytes 393224 | tf_op jit(solution)/shard_map/ppermute | solution.py:452

commit v6 on v5

--- a/solution.py
+++ b/solution.py
@@ -481,7 +481,7 @@
     for here_level, corner in zip(levels, moved[1:]):
         pieces += [here_level, corner, exchange(corner, 1)]
     tables = [in_hbm(jnp.asarray(matrix)) for matrix in dft_matrices(side)]
-    centers, live, pieces[3] = lax.optimization_barrier((centers, live, pieces[3]))
+    centers, live, moved[0] = lax.optimization_barrier((centers, live, moved[0]))
     record, direct, swapped = pl.pallas_call(
         functools.partial(record_kernel, slots),
         out_shape=[jax.ShapeDtypeStruct((record_rows, tile_cols), jnp.bfloat16)]

time: 38.1 us -> 36.2 us (0.950)
  waiting for transfers between devices: 8.48 us -> 7.15 us
  starting transfers between devices: 15.3 us -> 14.7 us
    ppermute x1, waiting for transfers between devices: 1.97 us -> 0.01 us  [on_device(): levels.append(lax.ppermute(edge, 'ty', level(step)))]
    ppermute x6, waiting for transfers between devices: 1.59 us -> 2.22 us  [exchange(): return lax.ppermute(array, 'mode', [(m, m ^ flip) for m in range(m_count)])]
    ppermute x2, starting transfers between devices: 2.46 us -> 1.94 us  [on_device(): received[1 + turn] = lax.ppermute(results[1 + turn], axes, zigzag(0, flip))]
  transfers between devices with their start and end apart: 14 -> 14, of which waited for: 6 -> 6; matrix products, arithmetic and copies ran while one was open for 0% -> 0% of each run, Pallas kernels for 15% -> 16%
where the time goes in v6:
time: 36.2 us; the launch traced here: 36 us
  starting transfers between devices  14.7 us (41%)
  Pallas kernels  12.7 us (35%)
  waiting for transfers between devices  7.15 us (20%)
  between operations  0.76 us (2%)
  local copies, waits for them, and re-layouts  0.68 us (2%)
    pallas_call x1, Pallas kernels, on_device(): pl.pallas_call(functools.partial(back_kernel, sides, slots, x_count, tile...  4.7 us
    ppermute x2, waiting for transfers between devices, on_device(): lax.ppermute(results[at + 1 + turn], axes, zigzag(-step, flip))  4.67 us
    ppermute x6, starting transfers between devices, exchange(): return lax.ppermute(array, 'mode', [(m, m ^ flip) for m in range(m_count)])  3.19 us
    ppermute x2, starting transfers between devices, on_device(): lax.ppermute(results[at + 1 + turn], axes, zigzag(-step, flip))  2.96 us
    ppermute x1, starting transfers between devices, on_device(): moved.append(lax.ppermute(edge, axes, zigzag(step)))  2.5 us
    pallas_call x1, Pallas kernels, on_device(): pl.pallas_call(functools.partial(near_kernel, sides, slots, z_count, x_co...  2.44 us
    ppermute x6, waiting for transfers between devices, exchange(): return lax.ppermute(array, 'mode', [(m, m ^ flip) for m in range(m_count)])  2.22 us
    ppermute x2, starting transfers between devices, on_device(): received[1 + turn] = lax.ppermute(results[1 + turn], axes, zigzag(0, flip))  1.94 us
  transfers between devices with their start and end apart: 14, of which 6 were waited for; matrix products, arithmetic and copies ran while one was open for 0% of the time, Pallas kernels for 16%

profile of v6, /device:TPU:0, one launch (start us, length us, event | category | flops | bytes accessed | tf_op | source)
XLA Modules:
  0.0 36.0 jit_solution(3399700853574988102)
XLA Ops:
  0.0 1.3 %start.1 = (bf16[2,2,256,256]{3,2,1,0:T(8,128)(2,1)S(1)}, bf16[2,128,256]{2,1,0:T(8,128)(2,1)S(1)}, bf16[2,128,128]{2,1,0:T(8,128)(2,1)S(1)}) custom-call(f32[2,128,256]{2,1,0:T(8,128)} %object_ref.1, f32[2,2,256,256]{3,2,1,0:T(8,128)} %probe_hbm.1), custom_call_target="tpu_custom_call" | custom-call | tf_op jit(solution)/shard_map/start/pallas_call | solution.py:454
  1.3 0.5 %collective-permute-start = (bf16[2,2,256,256]{3,2,1,0:T(8,128)(2,1)S(1)}, bf16[2,2,256,256]{3,2,1,0:T(8,128)(2,1)S(1)}, u32[]{:S(2)}, u32[]{:S(2)}) collective-permute-start(bf16[2,2,256,256]{3,2,1,0:T(8,128)(2,1)S(1)} %get-tuple-element.32.refs_6_.refs_2_), channel_id=1, source_target_pairs={{0,1},{1,0},{2,3},{3,2},{4,5},{5,4},{6,7},{7,6},{8,9},{9,8},{10,11... | collective-permute-start | bytes 1572872 | tf_op jit(solution)/shard_map/ppermute | solution.py:452
  1.8 2.6 %collective-permute-start.2 = (bf16[2,2,256,256]{3,2,1,0:T(8,128)(2,1)S(1)}, bf16[2,2,256,256]{3,2,1,0:T(8,128)(2,1)S(1)}, u32[]{:S(2)}, u32[]{:S(2)}) collective-permute-start(bf16[2,2,256,256]{3,2,1,0:T(8,128)(2,1)S(1)} %get-tuple-element.32.refs_6_.refs_2_), channel_id=1, source_target_pairs={{0,2},{1,3},{2,0},{3,1},{4,6},{5,7},{6,4},{7,5},{8,10},{9,11},{10,... | collective-permute-start | bytes 1572872 | tf_op jit(solution)/shard_map/ppermute | solution.py:452
  4.4 0.0 collective-permute-done.refs_7_.refs_3_
  4.4 1.9 %collective-permute-start.1 = (bf16[2,128,256]{2,1,0:T(8,128)(2,1)S(1)}, bf16[2,128,256]{2,1,0:T(8,128)(2,1)S(1)}, u32[]{:S(2)}, u32[]{:S(2)}) collective-permute-start(bf16[2,128,256]{2,1,0:T(8,128)(2,1)S(1)} %get-tuple-element.35.refs_0_), channel_id=1, source_target_pairs={{0,8},{1,0},{2,10},{3,2},{4,12},{5,4},{6,14},{7,6},{8,16},{9,1},{1... | collective-permute-start | bytes 393224 | tf_op jit(solution)/shard_map/ppermute | solution.py:475
  6.3 2.5 %collective-permute-start.3 = (bf16[2,128,128]{2,1,0:T(8,128)(2,1)S(1)}, bf16[2,128,128]{2,1,0:T(8,128)(2,1)S(1)}, u32[]{:S(2)}, u32[]{:S(2)}) collective-permute-start(bf16[2,128,128]{2,1,0:T(8,128)(2,1)S(1)} %get-tuple-element.39), channel_id=1, source_target_pairs={{0,12},{1,4},{2,14},{3,6},{4,8},{5,0},{6,10},{7,2},{8,20},{9,5},{1... | collective-permute-start | bytes 196616 | tf_op jit(solution)/shard_map/ppermute | solution.py:478
  8.8 0.0 collective-permute-done.1.refs_3_
  8.8 1.7 %collective-permute-start.6 = (bf16[2,128,128]{2,1,0:T(8,128)(2,1)S(1)}, bf16[2,128,128]{2,1,0:T(8,128)(2,1)S(1)}, u32[]{:S(2)}, u32[]{:S(2)}) collective-permute-start(bf16[2,128,128]{2,1,0:T(8,128)(2,1)S(1)} %get-tuple-element.39), channel_id=1, source_target_pairs={{0,4},{4,0},{1,5},{5,1},{2,6},{6,2},{3,7},{7,3},{8,12},{12,8},{9,1... | collective-permute-start | bytes 196616 | tf_op jit(solution)/shard_map/ppermute | solution.py:479
  10.5 0.2 collective-permute-done.3.refs_1_
  10.7 0.0 collective-permute-start.4
  11.4 0.0 copy-start.2
  11.4 0.7 %copy-done.2 = s32[1,1,2,2]{3,2,1,0:T(2,128)S(1)} copy-done((s32[1,1,2,2]{3,2,1,0:T(2,128)S(1)}, s32[1,1,2,2]{3,2,1,0:T(2,128)}, u32[]{:S(2)}) %copy-start.2) | copy-done | bytes 40
  12.1 1.8 %record.1 = (bf16[16,256]{1,0:T(8,128)(2,1)S(1)}, bf16[512,512]{1,0:T(8,128)(2,1)S(1)}, bf16[512,512]{1,0:T(8,128)(2,1)S(1)}) custom-call(s32[1,1,2,2]{3,2,1,0:T(2,128)S(1)} %copy-done.2, s32[1,1]{1,0:T(1,128)S(6)} %copy.8.live_ref, bf16[512,512]{1,0:T(8,128)(2,1)} %constant.4.clone.direct_hbm, bf16[512,512]{1,0:T(8,128)(2,1)} %constant.5.clone.swapped_hbm), custom_call_target="tpu_custom_call" | custom-call | tf_op jit(solution)/shard_map/record/pallas_call | solution.py:485
  13.8 0.0 collective-permute-done.6.refs_5_
  13.9 0.0 collective-permute-done.5.refs_4_
  13.9 0.0 copy-start.1
  13.9 2.4 %near.1 = (f32[2,256,256]{2,1,0:T(8,128)S(1)}, f32[4,256,512]{2,1,0:T(8,128)S(1)}, bf16[4,512,256]{2,1,0:T(8,128)(2,1)S(1)}, f32[2,256,256]{2,1,0:T(8,128)S(1)}) custom-call(bf16[16,256]{1,0:T(8,128)(2,1)S(1)} %get-tuple-element.38.record_ref, bf16[2,128,256]{2,1,0:T(8,128)(2,1)S(1)} %get-tuple-element.35.refs_0_, ...), custom_call_target="tpu_custom_call" | custom-call | tf_op jit(solution)/shard_map/near/pallas_call | solution.py:506
  16.3 0.6 %collective-permute-done.2.group.refs_4_ = bf16[2,2,256,256]{3,2,1,0:T(8,128)(2,1)S(1)} collective-permute-done((bf16[2,2,256,256]{3,2,1,0:T(8,128)(2,1)S(1)}, bf16[2,2,256,256]{3,2,1,0:T(8,128)(2,1)S(1)}, u32[]{:S(2)}, u32[]{:S(2)}) %collective-permute-start.2) | collective-permute-done | bytes 524320 | tf_op jit(solution)/shard_map/ppermute | solution.py:452
  17.0 0.9 %over.1 = (f32[2,256,512]{2,1,0:T(8,128)S(1)}, bf16[2,512,256]{2,1,0:T(8,128)(2,1)S(1)}, f32[2,256,256]{2,1,0:T(8,128)S(1)}) custom-call(f32[2,256,256]{2,1,0:T(8,128)S(1)} %get-tuple-element.44.patch_ref.refs_1_, bf16[2,2,256,256]{3,2,1,0:T(8,128)(2,1)S(1)} %collective-permute-done.2.group.refs_4_, ...), custom_call_target="tpu_custom_call" | custom-call | tf_op jit(solution)/shard_map/over/pallas_call | solution.py:517
  17.9 1.0 %collective-permute-done.7.refs_5_ = bf16[2,2,256,256]{3,2,1,0:T(8,128)(2,1)S(1)} collective-permute-done((bf16[2,2,256,256]{3,2,1,0:T(8,128)(2,1)S(1)}, bf16[2,2,256,256]{3,2,1,0:T(8,128)(2,1)S(1)}, u32[]{:S(2)}, u32[]{:S(2)}) %collective-permute-start.7) | collective-permute-done | bytes 524320 | tf_op jit(solution)/shard_map/ppermute | solution.py:452
  18.9 4.7 %back.1 = (bf16[272,256]{1,0:T(8,128)(2,1)S(1)}, bf16[272,256]{1,0:T(8,128)(2,1)S(1)}, bf16[272,256]{1,0:T(8,128)(2,1)S(1)}, bf16[272,128]{1,0:T(8,128)(2,1)S(1)...) custom-call(bf16[16,256]{1,0:T(8,128)(2,1)S(1)} %get-tuple-element.38.record_ref, ...), custom_call_target="tpu_custom_call" | custom-call | tf_op jit(solution)/shard_map/back/pallas_call | solution.py:527
  23.6 1.9 %collective-permute-start.10 = (bf16[272,256]{1,0:T(8,128)(2,1)S(1)}, bf16[272,256]{1,0:T(8,128)(2,1)S(1)}, u32[]{:S(2)}, u32[]{:S(2)}) collective-permute-start(bf16[272,256]{1,0:T(8,128)(2,1)S(1)} %get-tuple-element.55), channel_id=1, source_target_pairs={{0,8},{1,0},{2,10},{3,2},{4,12},{5,4},{6,14},{7,6},{8,16},{9,1},{1... | collective-permute-start | bytes 417800 | tf_op jit(solution)/shard_map/ppermute | solution.py:559
  25.5 3.0 %collective-permute-start.8 = (bf16[272,128]{1,0:T(8,128)(2,1)S(1)}, bf16[272,128]{1,0:T(8,128)(2,1)S(1)}, u32[]{:S(2)}, u32[]{:S(2)}) collective-permute-start(bf16[272,128]{1,0:T(8,128)(2,1)S(1)} %get-tuple-element.53), channel_id=1, source_target_pairs={{0,12},{1,4},{2,14},{3,6},{4,8},{5,0},{6,10},{7,2},{8,20},{9,5},{1... | collective-permute-start | bytes 208904 | tf_op jit(solution)/shard_map/ppermute | solution.py:557
  28.5 0.0 collective-permute-start.9
  28.5 0.5 %collective-permute-start.12 = (bf16[272,128]{1,0:T(8,128)(2,1)S(1)}, bf16[272,128]{1,0:T(8,128)(2,1)S(1)}, u32[]{:S(2)}, u32[]{:S(2)}) collective-permute-start(bf16[272,128]{1,0:T(8,128)(2,1)S(1)} %get-tuple-element.57), channel_id=1, source_target_pairs={{0,4},{4,0},{1,5},{5,1},{2,6},{6,2},{3,7},{7,3},{8,12},{12,8},{9,1... | collective-permute-start | bytes 208904 | tf_op jit(solution)/shard_map/ppermute | solution.py:561
  29.0 1.5 %collective-permute-done.8.refs_1_ = bf16[272,128]{1,0:T(8,128)(2,1)S(1)} collective-permute-done((bf16[272,128]{1,0:T(8,128)(2,1)S(1)}, bf16[272,128]{1,0:T(8,128)(2,1)S(1)}, u32[]{:S(2)}, u32[]{:S(2)}) %collective-permute-start.8) | collective-permute-done | bytes 69664 | tf_op jit(solution)/shard_map/ppermute | solution.py:557
  30.5 3.1 %collective-permute-done.9.refs_2_ = bf16[272,128]{1,0:T(8,128)(2,1)S(1)} collective-permute-done((bf16[272,128]{1,0:T(8,128)(2,1)S(1)}, bf16[272,128]{1,0:T(8,128)(2,1)S(1)}, u32[]{:S(2)}, u32[]{:S(2)}) %collective-permute-start.9) | collective-permute-done | bytes 69664 | tf_op jit(solution)/shard_map/ppermute | solution.py:557
  33.7 0.1 sums.1.own_ref
  33.8 0.1 collective-permute-start.13
  33.9 0.7 %weights.1.weight_ref = f32[128,256]{1,0:T(8,128)S(1)} custom-call(bf16[256,256]{1,0:T(8,128)(2,1)S(1)} %get-tuple-element.58.weight_ref, bf16[272,256]{1,0:T(8,128)(2,1)S(1)} %get-tuple-element.52.refs_0_, bf16[272,128]{1,0:T(8,128)(2,1)S(1)} %collective-permute-done.8.refs_1_, bf16[272,128]{1,0:T(8,128)(2,1)S(1)} %collective-permute-done.9.refs_2_, ...), custom_call_target="tpu_custom_call" | custom-call | tf_op jit(solution)/shard_map/weights/pallas_call | solution.py:570
  34.7 0.6 %collective-permute-done.13.other_ref = bf16[2,128,256]{2,1,0:T(8,128)(2,1)S(1)} collective-permute-done((bf16[2,128,256]{2,1,0:T(8,128)(2,1)S(1)}, bf16[2,128,256]{2,1,0:T(8,128)(2,1)S(1)}, u32[]{:S(2)}, u32[]{:S(2)}) %collective-permute-start.13) | collective-permute-done | bytes 131104 | tf_op jit(solution)/shard_map/ppermute | solution.py:452
  35.3 0.8 %update.1 = f32[2,128,256]{2,1,0:T(8,128)} custom-call(f32[2,128,256]{2,1,0:T(8,128)S(1)} %copy-done, bf16[2,128,256]{2,1,0:T(8,128)(2,1)S(1)} %sums.1.own_ref, bf16[2,128,256]{2,1,0:T(8,128)(2,1)S(1)} %collective-permute-done.13.other_ref, f32[128,256]{1,0:T(8,128)S(1)} %weights.1.weight_ref), custom_call_target="tpu_custom_call" | custom-call | tf_op jit(solution)/shard_map/update/pallas_call | solution.py:579
  (10 shorter events, 0.0 us)
Async XLA Ops:
  1.3 3.1 %collective-permute-start = (bf16[2,2,256,256]{3,2,1,0:T(8,128)(2,1)S(1)}, bf16[2,2,256,256]{3,2,1,0:T(8,128)(2,1)S(1)}, u32[]{:S(2)}, u32[]{:S(2)}) collective-permute-start(bf16[2,2,256,256]{3,2,1,0:T(8,128)(2,1)S(1)} %get-tuple-element.32.refs_6_.refs_2_), channel_id=1, source_target_pairs={{0,1},{1,0},{2,3},{3,2},{4,5},{5,4},{6,7},{7,6},{8,9},{9,8},{10,11... | collective-permute-start | bytes 1572872 | tf_op jit(solution)/shard_map/ppermute | solution.py:452
  1.8 15.1 %collective-permute-start.2 = (bf16[2,2,256,256]{3,2,1,0:T(8,128)(2,1)S(1)}, bf16[2,2,256,256]{3,2,1,0:T(8,128)(2,1)S(1)}, u32[]{:S(2)}, u32[]{:S(2)}) collective-permute-start(bf16[2,2,256,256]{3,2,1,0:T(8,128)(2,1)S(1)} %get-tuple-element.32.refs_6_.refs_2_), channel_id=1, source_target_pairs={{0,2},{1,3},{2,0},{3,1},{4,6},{5,7},{6,4},{7,5},{8,10},{9,11},{10,... | collective-permute-start | bytes 1572872 | tf_op jit(solution)/shard_map/ppermute | solution.py:452
  4.4 4.4 %collective-permute-start.1 = (bf16[2,128,256]{2,1,0:T(8,128)(2,1)S(1)}, bf16[2,128,256]{2,1,0:T(8,128)(2,1)S(1)}, u32[]{:S(2)}, u32[]{:S(2)}) collective-permute-start(bf16[2,128,256]{2,1,0:T(8,128)(2,1)S(1)} %get-tuple-element.35.refs_0_), channel_id=1, source_target_pairs={{0,8},{1,0},{2,10},{3,2},{4,12},{5,4},{6,14},{7,6},{8,16},{9,1},{1... | collective-permute-start | bytes 393224 | tf_op jit(solution)/shard_map/ppermute | solution.py:475
  6.3 4.4 %collective-permute-start.3 = (bf16[2,128,128]{2,1,0:T(8,128)(2,1)S(1)}, bf16[2,128,128]{2,1,0:T(8,128)(2,1)S(1)}, u32[]{:S(2)}, u32[]{:S(2)}) collective-permute-start(bf16[2,128,128]{2,1,0:T(8,128)(2,1)S(1)} %get-tuple-element.39), channel_id=1, source_target_pairs={{0,12},{1,4},{2,14},{3,6},{4,8},{5,0},{6,10},{7,2},{8,20},{9,5},{1... | collective-permute-start | bytes 196616 | tf_op jit(solution)/shard_map/ppermute | solution.py:478
  8.8 5.0 %collective-permute-start.5 = (bf16[2,128,256]{2,1,0:T(8,128)(2,1)S(1)}, bf16[2,128,256]{2,1,0:T(8,128)(2,1)S(1)}, u32[]{:S(2)}, u32[]{:S(2)}) collective-permute-start(bf16[2,128,256]{2,1,0:T(8,128)(2,1)S(1)} %collective-permute-done.1.refs_3_), channel_id=1, source_target_pairs={{0,1},{1,0},{2,3},{3,2},{4,5},{5,4},{6,7},{7,6},{8,9},{9,8},{10,11... | collective-permute-start | bytes 393224 | tf_op jit(solution)/shard_map/ppermute | solution.py:452
  8.8 5.0 %collective-permute-start.6 = (bf16[2,128,128]{2,1,0:T(8,128)(2,1)S(1)}, bf16[2,128,128]{2,1,0:T(8,128)(2,1)S(1)}, u32[]{:S(2)}, u32[]{:S(2)}) collective-permute-start(bf16[2,128,128]{2,1,0:T(8,128)(2,1)S(1)} %get-tuple-element.39), channel_id=1, source_target_pairs={{0,4},{4,0},{1,5},{5,1},{2,6},{6,2},{3,7},{7,3},{8,12},{12,8},{9,1... | collective-permute-start | bytes 196616 | tf_op jit(solution)/shard_map/ppermute | solution.py:479
  10.7 3.1 %collective-permute-start.4 = (bf16[2,128,128]{2,1,0:T(8,128)(2,1)S(1)}, bf16[2,128,128]{2,1,0:T(8,128)(2,1)S(1)}, u32[]{:S(2)}, u32[]{:S(2)}) collective-permute-start(bf16[2,128,128]{2,1,0:T(8,128)(2,1)S(1)} %collective-permute-done.3.refs_1_), channel_id=1, source_target_pairs={{0,1},{1,0},{2,3},{3,2},{4,5},{5,4},{6,7},{7,6},{8,9},{9,8},{10,11... | collective-permute-start | bytes 196616 | tf_op jit(solution)/shard_map/ppermute | solution.py:452
  11.4 0.7 %copy-start.2 = (s32[1,1,2,2]{3,2,1,0:T(2,128)S(1)}, s32[1,1,2,2]{3,2,1,0:T(2,128)}, u32[]{:S(2)}) copy-start(s32[1,1,2,2]{3,2,1,0:T(2,128)} %centers_ref) | copy-start | bytes 52
  13.9 5.0 %copy-start.1 = (bf16[1,1,2,256,256]{4,3,2,1,0:T(8,128)(2,1)S(1)}, bf16[1,1,2,256,256]{4,3,2,1,0:T(8,128)(2,1)}, u32[]{:S(2)}) copy-start(bf16[1,1,2,256,256]{4,3,2,1,0:T(8,128)(2,1)} %refs_0_.1) | copy-start | bytes 786436
  17.0 1.9 %collective-permute-start.7 = (bf16[2,2,256,256]{3,2,1,0:T(8,128)(2,1)S(1)}, bf16[2,2,256,256]{3,2,1,0:T(8,128)(2,1)S(1)}, u32[]{:S(2)}, u32[]{:S(2)}) collective-permute-start(bf16[2,2,256,256]{3,2,1,0:T(8,128)(2,1)S(1)} %collective-permute-done.2.group.refs_4_), channel_id=1, source_target_pairs={{0,1},{1,0},{2,3},{3,2},{4,5},{5,4},{6,7},{7,6},{8,9},{9,8},{10,11... | collective-permute-start | bytes 1572872 | tf_op jit(solution)/shard_map/ppermute | solution.py:452
  18.9 16.4 %copy-start = (f32[2,128,256]{2,1,0:T(8,128)S(1)}, f32[2,128,256]{2,1,0:T(8,128)}, u32[]{:S(2)}) copy-start(f32[2,128,256]{2,1,0:T(8,128)} %object_ref.1) | copy-start | bytes 786436
  23.6 10.1 %collective-permute-start.10 = (bf16[272,256]{1,0:T(8,128)(2,1)S(1)}, bf16[272,256]{1,0:T(8,128)(2,1)S(1)}, u32[]{:S(2)}, u32[]{:S(2)}) collective-permute-start(bf16[272,256]{1,0:T(8,128)(2,1)S(1)} %get-tuple-element.55), channel_id=1, source_target_pairs={{0,8},{1,0},{2,10},{3,2},{4,12},{5,4},{6,14},{7,6},{8,16},{9,1},{1... | collective-permute-start | bytes 417800 | tf_op jit(solution)/shard_map/ppermute | solution.py:559
  25.5 8.2 %collective-permute-start.11 = (bf16[272,256]{1,0:T(8,128)(2,1)S(1)}, bf16[272,256]{1,0:T(8,128)(2,1)S(1)}, u32[]{:S(2)}, u32[]{:S(2)}) collective-permute-start(bf16[272,256]{1,0:T(8,128)(2,1)S(1)} %get-tuple-element.56), channel_id=1, source_target_pairs={{0,1},{1,9},{2,3},{3,11},{4,5},{5,13},{6,7},{7,15},{8,0},{9,17},{1... | collective-permute-start | bytes 417800 | tf_op jit(solution)/shard_map/ppermute | solution.py:559
  25.5 5.0 %collective-permute-start.8 = (bf16[272,128]{1,0:T(8,128)(2,1)S(1)}, bf16[272,128]{1,0:T(8,128)(2,1)S(1)}, u32[]{:S(2)}, u32[]{:S(2)}) collective-permute-start(bf16[272,128]{1,0:T(8,128)(2,1)S(1)} %get-tuple-element.53), channel_id=1, source_target_pairs={{0,12},{1,4},{2,14},{3,6},{4,8},{5,0},{6,10},{7,2},{8,20},{9,5},{1... | collective-permute-start | bytes 208904 | tf_op jit(solution)/shard_map/ppermute | solution.py:557
  28.5 5.2 %collective-permute-start.9 = (bf16[272,128]{1,0:T(8,128)(2,1)S(1)}, bf16[272,128]{1,0:T(8,128)(2,1)S(1)}, u32[]{:S(2)}, u32[]{:S(2)}) collective-permute-start(bf16[272,128]{1,0:T(8,128)(2,1)S(1)} %get-tuple-element.54), channel_id=1, source_target_pairs={{0,5},{1,13},{2,7},{3,15},{4,1},{5,9},{6,3},{7,11},{8,4},{9,21},{1... | collective-permute-start | bytes 208904 | tf_op jit(solution)/shard_map/ppermute | solution.py:557
  28.5 5.2 %collective-permute-start.12 = (bf16[272,128]{1,0:T(8,128)(2,1)S(1)}, bf16[272,128]{1,0:T(8,128)(2,1)S(1)}, u32[]{:S(2)}, u32[]{:S(2)}) collective-permute-start(bf16[272,128]{1,0:T(8,128)(2,1)S(1)} %get-tuple-element.57), channel_id=1, source_target_pairs={{0,4},{4,0},{1,5},{5,1},{2,6},{6,2},{3,7},{7,3},{8,12},{12,8},{9,1... | collective-permute-start | bytes 208904 | tf_op jit(solution)/shard_map/ppermute | solution.py:561
  33.8 1.4 %collective-permute-start.13 = (bf16[2,128,256]{2,1,0:T(8,128)(2,1)S(1)}, bf16[2,128,256]{2,1,0:T(8,128)(2,1)S(1)}, u32[]{:S(2)}, u32[]{:S(2)}) collective-permute-start(bf16[2,128,256]{2,1,0:T(8,128)(2,1)S(1)} %sums.1.own_ref), channel_id=1, source_target_pairs={{0,1},{1,0},{2,3},{3,2},{4,5},{5,4},{6,7},{7,6},{8,9},{9,8},{10,11... | collective-permute-start | bytes 393224 | tf_op jit(solution)/shard_map/ppermute | solution.py:452

commit v7 on v6

--- a/solution.py
+++ b/solution.py
@@ -76,7 +76,7 @@
     return (lax.axis_index("tx"), lax.axis_index("ty"), lax.axis_index("mode") % 2)
 
 
-def start_kernel(sides, object_hbm, probe_hbm, low_ref, packed_ref, *rest):
+def start_kernel(sides, object_hbm, probe_hbm, low_ref, shared_ref, rest_ref, packed_ref, *rest):
     edges = rest[:sides]
     object_ref, probe_ref, sems = rest[sides:]
     copies = [
@@ -92,6 +92,8 @@
     _, x_index, _ = here()
     copies[0].wait()
     low_ref[...] = probe_ref[...].astype(jnp.bfloat16)
+    shared_ref[...] = jnp.where(x_index % 2 == 0, low_ref[0, 0], low_ref[1, 0])
+    rest_ref[...] = low_ref[:, 1:]
     copies[1].wait()
     first, last = slice(0, half), slice(tile_cols - half, tile_cols)
     for channel in range(2):
@@ -178,63 +180,71 @@
     return dot(pick_rows, narrow[:ext_rows]), dot(pick_rows, narrow[ext_rows:])
 
 
-def forward(groups, patch, direct, swapped, far_ref, exit_ref, at):
+def modes_of(group):
+    def reader(k):
+        return lambda: (group[0, k].astype(jnp.float32), group[1, k].astype(jnp.float32))
+
+    return [reader(k) for k in range(group.shape[1])]
+
+
+def shared_mode(over_y, over_x):
+    def read():
+        _, x_index, _ = here()
+        even = x_index % 2 == 0
+        over_y_values = over_y[...].astype(jnp.float32)
+        over_x_values = over_x[...].astype(jnp.float32)
+        return (
+            jnp.where(even, over_y_values, over_x_values),
+            jnp.where(even, over_x_values, over_y_values),
+        )
+
+    return read
+
+
+def forward(modes, patch, direct, swapped, far_ref, exit_ref, at):
     patch_real, patch_imag = patch
     side = patch_real.shape[0]
-    sums = []
-    for group in groups:
-        modes = group.shape[1]
-        power = jnp.zeros((side, side), jnp.float32)
-        weight = jnp.zeros((side, side), jnp.float32)
-        halves = []
-        for k in range(modes):
-            real = group[0, k].astype(jnp.float32)
-            imag = group[1, k].astype(jnp.float32)
-            exit_wave = jnp.concatenate(
-                [
-                    (real * patch_real - imag * patch_imag).astype(jnp.bfloat16),
-                    (real * patch_imag + imag * patch_real).astype(jnp.bfloat16),
-                ],
-                axis=0,
-            )
-            exit_ref[at + k] = exit_wave
-            halves.append(wide(dot(direct, exit_wave).astype(jnp.bfloat16)))
-            weight = weight + (real * real + imag * imag)
-        far_both = dot(jnp.concatenate(halves, axis=0), swapped)
-        for k in range(modes):
-            far = far_both[k * side : (k + 1) * side]
-            far_ref[at + k] = far
-            power = power + (far[:, :side] * far[:, :side] + far[:, side:] * far[:, side:])
-        sums.append((power, weight))
-        at += modes
-    return sums
-
-
-def backward(groups, factor, direct, swapped, far_ref, exit_ref):
+    power = jnp.zeros((side, side), jnp.float32)
+    weight = jnp.zeros((side, side), jnp.float32)
+    halves = []
+    for k, mode in enumerate(modes):
+        real, imag = mode()
+        exit_wave = jnp.concatenate(
+            [
+                (real * patch_real - imag * patch_imag).astype(jnp.bfloat16),
+                (real * patch_imag + imag * patch_real).astype(jnp.bfloat16),
+            ],
+            axis=0,
+        )
+        exit_ref[at + k] = exit_wave
+        halves.append(wide(dot(direct, exit_wave).astype(jnp.bfloat16)))
+        weight = weight + (real * real + imag * imag)
+    far_all = dot(jnp.concatenate(halves, axis=0), swapped)
+    for k in range(len(modes)):
+        far = far_all[k * side : (k + 1) * side]
+        far_ref[at + k] = far
+        power = power + (far[:, :side] * far[:, :side] + far[:, side:] * far[:, side:])
+    return power, weight
+
+
+def backward(modes, factor, direct, swapped, far_ref, exit_ref, at):
     side = factor.shape[0]
-    grads = []
-    at = 0
-    for group in groups:
-        modes = group.shape[1]
-        grad_real = jnp.zeros((side, side), jnp.float32)
-        grad_imag = jnp.zeros((side, side), jnp.float32)
-        halves = []
-        for k in range(modes):
-            fixed = (far_ref[at + k] * factor).astype(jnp.bfloat16)
-            halves.append(wide(dot(swapped, tall(fixed)).astype(jnp.bfloat16)))
-        back_both = dot(jnp.concatenate(halves, axis=0), direct)
-        for k in range(modes):
-            back = back_both[k * side : (k + 1) * side]
-            exit_wave = exit_ref[at + k].astype(jnp.float32)
-            real = group[0, k].astype(jnp.float32)
-            imag = group[1, k].astype(jnp.float32)
-            diff_real = back[:, :side] - exit_wave[:side]
-            diff_imag = back[:, side:] - exit_wave[side:]
-            grad_real = grad_real + (real * diff_real + imag * diff_imag)
-            grad_imag = grad_imag + (real * diff_imag - imag * diff_real)
-        grads.append((grad_real, grad_imag))
-        at += modes
-    return grads
+    grad_real = jnp.zeros((side, side), jnp.float32)
+    grad_imag = jnp.zeros((side, side), jnp.float32)
+    halves = []
+    for k in range(len(modes)):
+        fixed = (far_ref[at + k] * factor).astype(jnp.bfloat16)
+        halves.append(wide(dot(swapped, tall(fixed)).astype(jnp.bfloat16)))
+    back_all = dot(jnp.concatenate(halves, axis=0), direct)
+    for k, mode in enumerate(modes):
+        back = back_all[k * side : (k + 1) * side]
+        exit_wave = exit_ref[at + k].astype(jnp.float32)
+        real, imag = mode()
+        diff_real = back[:, :side] - exit_wave[:side]
+        diff_imag = back[:, side:] - exit_wave[side:]
+        grad_real = grad_real + (real * diff_real + imag * diff_imag)
+        grad_imag = grad_imag + (real * diff_imag - imag * diff_real)
+    return grad_real, grad_imag
 
 
 def near_kernel(sides, slots, z_count, x_count, record_ref, *refs):
@@ -245,24 +255,30 @@
     side = own.shape[2]
     patch = patch_of(sides, slots, z_count, x_count, side, record_ref, pieces, ext_ref)
     patch_ref[0], patch_ref[1] = patch
-    sums = forward((own, core), patch, direct[...], swapped[...], far_ref, exit_ref, 0)
-    sum_ref[0] = sums[0][0] + sums[1][0]
-    sum_ref[1] = sums[0][1] + sums[1][1]
-
-
-def far_kernel(patch_ref, group, direct, swapped, far_ref, exit_ref, sum_ref):
+    tables = (direct[...], swapped[...], far_ref, exit_ref)
+    first = forward(modes_of(own), patch, *tables, 0)
+    second = forward(modes_of(core), patch, *tables, own.shape[1])
+    sum_ref[0] = first[0] + second[0]
+    sum_ref[1] = first[1] + second[1]
+
+
+def over_kernel(patch_ref, over_y, over_x, rest, direct, swapped, far_ref, exit_ref, sum_ref):
     patch = (patch_ref[0], patch_ref[1])
-    ((power, weight),) = forward((group,), patch, direct[...], swapped[...], far_ref, exit_ref, 0)
-    sum_ref[0] = power
-    sum_ref[1] = weight
+    modes = [shared_mode(over_y, over_x)] + modes_of(rest)
+    sum_ref[0], sum_ref[1] = forward(
+        modes, patch, direct[...], swapped[...], far_ref, exit_ref, 0
+    )
 
 
 def back_kernel(sides, slots, x_count, tile_rows, tile_cols, record_ref, *refs):
     n_pieces = 3 + 3 * sides
-    amplitude_ref, patch_ref, own, core, over, last, direct_ref, swapped_ref = refs[:8]
-    near_far, near_exit, near_sum, over_far, over_exit, over_sum = refs[8:14]
-    outs = refs[14 : 14 + n_pieces + 1]
-    last_far, last_exit, grad_ref = refs[14 + n_pieces + 1 :]
+    amplitude_ref, patch_ref, own, core = refs[:4]
+    over_modes = [shared_mode(*refs[4:6])] + modes_of(refs[6])
+    last_modes = [shared_mode(*refs[7:9])] + modes_of(refs[9])
+    direct_ref, swapped_ref = refs[10:12]
+    near_far, near_exit, near_sum, over_far, over_exit, over_sum = refs[12:18]
+    outs = refs[18 : 18 + n_pieces + 1]
+    last_far, last_exit, grad_ref = refs[18 + n_pieces + 1 :]
     side = own.shape[2]
     half = side // 2
     modes = own.shape[1]
@@ -273,16 +289,20 @@
     direct = direct_ref[...]
     swapped = swapped_ref[...]
     patch = (patch_ref[0], patch_ref[1])
-    ((power, weight),) = forward((last,), patch, direct, swapped, last_far, last_exit, 0)
+    power, weight = forward(last_modes, patch, direct, swapped, last_far, last_exit, 0)
     power = near_sum[0] + (over_sum[0] + power)
     weight = near_sum[1] + (over_sum[1] + weight)
     outs[-1][...] = weight.astype(jnp.bfloat16)
     amplitude = amplitude_ref[0, 0, parity].astype(jnp.float32)
     factor = amplitude / jnp.sqrt(power + power_floor)
     factor = jnp.concatenate([factor, factor], axis=1)
-    near = backward((own, core), factor, direct, swapped, near_far, near_exit)
-    (beyond,) = backward((over,), factor, direct, swapped, over_far, over_exit)
-    (final,) = backward((last,), factor, direct, swapped, last_far, last_exit)
+    tables = (factor, direct, swapped)
+    grads = [
+        backward(modes_of(own), *tables, near_far, near_exit, 0),
+        backward(modes_of(core), *tables, near_far, near_exit, modes),
+        backward(over_modes, *tables, over_far, over_exit, 0),
+        backward(last_modes, *tables, last_far, last_exit, 0),
+    ]
     at = iota((side, ext_cols), 1)
     column = column_coordinate(at, tile_cols, half, sides, x_index, x_count)
     put_cols = ((column == iota((side, ext_cols), 0) + col_at) & is_live).astype(jnp.bfloat16)
@@ -291,7 +311,7 @@
     )
     a_at, b_at = row_starts(half, tile_rows, parity)
     for channel in range(2):
-        gradient = (near[0][channel] + near[1][channel]) + (beyond[channel] + final[channel])
+        gradient = (grads[0][channel] + grads[1][channel]) + (grads[2][channel] + grads[3][channel])
         placed = dot(put_rows, gradient.astype(jnp.bfloat16)).astype(jnp.bfloat16)
         grad_ref[...] = dot(placed, put_cols).astype(jnp.bfloat16)
         rows = slice(channel * half, (channel + 1) * half)
@@ -419,7 +439,8 @@
     z_count = lax.axis_size("tx")
     x_count = lax.axis_size("ty")
     m_count = lax.axis_size("mode")
-    if tile_rows != half or slots != 2 or m_count != 4 or x_count < 2:
+    modes = probe.shape[1]
+    if tile_rows != half or slots != 2 or m_count != 4 or x_count % 2 or modes < 2:
         raise ValueError("unsupported sizes")
     sides = 1 if x_count == 2 else 2
     axes = ("tx", "ty", "mode")
@@ -451,15 +472,17 @@
     def exchange(array, flip):
         return lax.ppermute(array, "mode", [(m, m ^ flip) for m in range(m_count)])
 
-    probe_low, *packed = pl.pallas_call(
+    probe_low, shared, rest, *packed = pl.pallas_call(
         functools.partial(start_kernel, sides),
         out_shape=[
             jax.ShapeDtypeStruct(probe.shape, jnp.bfloat16),
+            jax.ShapeDtypeStruct((side, side), jnp.bfloat16),
+            jax.ShapeDtypeStruct((2, modes - 1, side, side), jnp.bfloat16),
             jax.ShapeDtypeStruct(object_field.shape, jnp.bfloat16),
         ]
         + [jax.ShapeDtypeStruct((2, tile_rows, half), jnp.bfloat16)] * sides,
         in_specs=[hbm()] * 2,
-        out_specs=[vmem()] * (2 + sides),
+        out_specs=[vmem()] * (4 + sides),
         scratch_shapes=[
             pltpu.VMEM(object_field.shape, jnp.float32),
             pltpu.VMEM(probe.shape, jnp.float32),
@@ -468,9 +491,11 @@
         compiler_params=pltpu.CompilerParams(vmem_limit_bytes=small_bytes),
         name="start",
     )(in_hbm(object_field), in_hbm(probe))
-    probe_y = exchange(probe_low, 2)
+    over_y = exchange(shared, 2)
     probe_core = exchange(probe_low, 1)
-    probe_core, *packed = lax.optimization_barrier((probe_core, *packed))
+    probe_core, rest = lax.optimization_barrier((probe_core, rest))
+    rest = exchange(rest, 2)
+    over_x = lax.ppermute(over_y, "ty", [(x, x ^ 1) for x in range(x_count)])
     x_steps = [1] if sides == 1 else [1, -1]
     moved = [lax.ppermute(packed[0], axes, zigzag(0))]
     levels = []
@@ -493,9 +518,9 @@
         name="record",
     )(centers, live, *tables)
     n_pieces = len(pieces)
-    modes = probe.shape[1]
     ext_rows = tile_rows + side
     ext_cols = tile_cols + sides * half
+
     def waves(count):
         return [
             jax.ShapeDtypeStruct((count, side, 2 * side), jnp.float32),
@@ -512,23 +537,24 @@
         compiler_params=pltpu.CompilerParams(vmem_limit_bytes=wave_bytes),
         name="near",
     )(record, *in_sent_order(pieces), probe_low, probe_core, direct, swapped)
-    probe_y, patch = lax.optimization_barrier((probe_y, patch))
-    probe_diagonal = exchange(probe_y, 1)
+    over_x, rest, patch = lax.optimization_barrier((over_x, rest, patch))
+    over_group = (over_y, over_x, rest)
+    last_group = [exchange(part, 1) for part in over_group]
     over = pl.pallas_call(
-        far_kernel,
+        over_kernel,
         out_shape=waves(modes),
-        in_specs=[vmem()] * 4,
+        in_specs=[vmem()] * 6,
         out_specs=[vmem()] * 3,
         compiler_params=pltpu.CompilerParams(vmem_limit_bytes=wave_bytes),
         name="over",
-    )(patch, probe_y, direct, swapped)
+    )(patch, *over_group, direct, swapped)
     shapes = [(2 * half + record_rows, tile_cols)] * 3
     shapes += [(2 * half + record_rows, half)] * (3 * sides)
     results = pl.pallas_call(
         functools.partial(back_kernel, sides, slots, x_count, tile_rows, tile_cols),
         out_shape=[jax.ShapeDtypeStruct(shape, jnp.bfloat16) for shape in shapes]
         + [jax.ShapeDtypeStruct((side, side), jnp.bfloat16)],
-        in_specs=[vmem()] * 15,
+        in_specs=[vmem()] * 19,
         out_specs=[vmem()] * (n_pieces + 1),
         scratch_shapes=[
             pltpu.VMEM((modes, side, 2 * side), jnp.float32),
@@ -543,8 +569,8 @@
         patch,
         probe_low,
         probe_core,
-        probe_y,
-        probe_diagonal,
+        *over_group,
+        *last_group,
         direct,
         swapped,
         *near,

time: 36.2 us -> 38 us (1.050)
  starting transfers between devices: 14.7 us -> 15.6 us
  waiting for transfers between devices: 7.15 us -> 7.96 us
    ppermute x0 -> x1, starting transfers between devices: none -> 1.46 us  [on_device(): over_x = lax.ppermute(over_y, 'ty', [(x, x ^ 1) for x in range(x_count)])]
    ppermute x1, starting transfers between devices: 1.65 us -> 0.56 us  [on_device(): levels.append(lax.ppermute(edge, 'ty', level(step)))]
    ppermute x1, starting transfers between devices: 1.89 us -> 2.6 us  [on_device(): moved = [lax.ppermute(packed[0], axes, zigzag(0))]]
    ppermute x1, waiting for transfers between devices: 0.01 us -> 0.59 us  [on_device(): levels.append(lax.ppermute(edge, 'ty', level(step)))]
    ppermute x6 -> x9, waiting for transfers between devices: 2.22 us -> 2.78 us  [exchange(): return lax.ppermute(array, 'mode', [(m, m ^ flip) for m in range(m_count)])]
    ppermute x6 -> x9, starting transfers between devices: 3.19 us -> 3.27 us  [exchange(): return lax.ppermute(array, 'mode', [(m, m ^ flip) for m in range(m_count)])]
  transfers between devices with their start and end apart: 14 -> 18, of which waited for: 6 -> 7; matrix products, arithmetic and copies ran while one was open for 0% -> 0% of each run, Pallas kernels for 16% -> 16%
where the time goes in v7:
time: 38 us; the launch traced here: 37.8 us
  starting transfers between devices  15.6 us (41%)
  Pallas kernels  12.8 us (34%)
  waiting for transfers between devices  7.96 us (21%)
  between operations  0.76 us (2%)
  local copies, waits for them, and re-layouts  0.68 us (2%)
    pallas_call x1, Pallas kernels, on_device(): pl.pallas_call(functools.partial(back_kernel, sides, slots, x_count, tile...  4.69 us
    ppermute x2, waiting for transfers between devices, on_device(): lax.ppermute(results[at + 1 + turn], axes, zigzag(-step, flip))  4.58 us
    ppermute x9, starting transfers between devices, exchange(): return lax.ppermute(array, 'mode', [(m, m ^ flip) for m in range(m_count)])  3.27 us
    ppermute x2, starting transfers between devices, on_device(): lax.ppermute(results[at + 1 + turn], axes, zigzag(-step, flip))  2.86 us
    ppermute x9, waiting for transfers between devices, exchange(): return lax.ppermute(array, 'mode', [(m, m ^ flip) for m in range(m_count)])  2.78 us
    ppermute x1, starting transfers between devices, on_device(): moved = [lax.ppermute(packed[0], axes, zigzag(0))]  2.6 us
    ppermute x1, starting transfers between devices, on_device(): moved.append(lax.ppermute(edge, axes, zigzag(step)))  2.5 us
    pallas_call x1, Pallas kernels, on_device(): pl.pallas_call(functools.partial(near_kernel, sides, slots, z_count, x_co...  2.44 us
  transfers between devices with their start and end apart: 18, of which 7 were waited for; matrix products, arithmetic and copies ran while one was open for 0% of the time, Pallas kernels for 16%

profile of v7, /device:TPU:0, one launch (start us, length us, event | category | flops | bytes accessed | tf_op | source)
XLA Modules:
  0.0 37.8 jit_solution(16533696504031778843)
XLA Ops:
  0.0 1.3 %start.1 = (bf16[2,2,256,256]{3,2,1,0:T(8,128)(2,1)S(1)}, bf16[256,256]{1,0:T(8,128)(2,1)S(1)}, bf16[2,1,256,256]{3,2,1,0:T(8,128)(2,1)S(1)}, bf16[2,128,256]{2,1,0:T(8,128)(2,1)S(1)}, bf16[2,128,128]{2,1,0:T(8,128)(2,1)S(1)}) custom-call(f32[2,128,256]{2,1,0:T(8,128)} %object_ref.1, f32[2,2,256,256]{3,2,1,0:T(8,128)} %probe_hbm.1), custom_call_target="tpu_custom_call" | custom-call | tf_op jit(solution)/shard_map/start/pallas_call | solution.py:475
  1.3 0.5 %collective-permute-start.3 = (bf16[2,2,256,256]{3,2,1,0:T(8,128)(2,1)S(1)}, bf16[2,2,256,256]{3,2,1,0:T(8,128)(2,1)S(1)}, u32[]{:S(2)}, u32[]{:S(2)}) collective-permute-start(bf16[2,2,256,256]{3,2,1,0:T(8,128)(2,1)S(1)} %get-tuple-element.39.refs_6_.refs_2_), channel_id=1, source_target_pairs={{0,1},{1,0},{2,3},{3,2},{4,5},{5,4},{6,7},{7,6},{8,9},{9,8},{10,11... | collective-permute-start | bytes 1572872 | tf_op jit(solution)/shard_map/ppermute | solution.py:473
  1.9 2.6 %collective-permute-start = (bf16[2,128,256]{2,1,0:T(8,128)(2,1)S(1)}, bf16[2,128,256]{2,1,0:T(8,128)(2,1)S(1)}, u32[]{:S(2)}, u32[]{:S(2)}) collective-permute-start(bf16[2,128,256]{2,1,0:T(8,128)(2,1)S(1)} %get-tuple-element.34.refs_0_), channel_id=1, source_target_pairs={{0,8},{1,0},{2,10},{3,2},{4,12},{5,4},{6,14},{7,6},{8,16},{9,1},{1... | collective-permute-start | bytes 393224 | tf_op jit(solution)/shard_map/ppermute | solution.py:500
  4.5 1.5 %collective-permute-start.1 = (bf16[256,256]{1,0:T(8,128)(2,1)S(1)}, bf16[256,256]{1,0:T(8,128)(2,1)S(1)}, u32[]{:S(2)}, u32[]{:S(2)}) collective-permute-start(bf16[256,256]{1,0:T(8,128)(2,1)S(1)} %get-tuple-element.38), channel_id=1, source_target_pairs={{0,2},{1,3},{2,0},{3,1},{4,6},{5,7},{6,4},{7,5},{8,10},{9,11},{10,... | collective-permute-start | bytes 393224 | tf_op jit(solution)/shard_map/ppermute | solution.py:473
  6.0 0.5 %collective-permute-start.4 = (bf16[2,1,256,256]{3,2,1,0:T(8,128)(2,1)S(1)}, bf16[2,1,256,256]{3,2,1,0:T(8,128)(2,1)S(1)}, u32[]{:S(2)}, u32[]{:S(2)}) collective-permute-start(bf16[2,1,256,256]{3,2,1,0:T(8,128)(2,1)S(1)} %get-tuple-element.41), channel_id=1, source_target_pairs={{0,2},{1,3},{2,0},{3,1},{4,6},{5,7},{6,4},{7,5},{8,10},{9,11},{10,... | collective-permute-start | bytes 786440 | tf_op jit(solution)/shard_map/ppermute | solution.py:473
  6.5 2.5 %collective-permute-start.5 = (bf16[2,128,128]{2,1,0:T(8,128)(2,1)S(1)}, bf16[2,128,128]{2,1,0:T(8,128)(2,1)S(1)}, u32[]{:S(2)}, u32[]{:S(2)}) collective-permute-start(bf16[2,128,128]{2,1,0:T(8,128)(2,1)S(1)} %get-tuple-element.42), channel_id=1, source_target_pairs={{0,12},{1,4},{2,14},{3,6},{4,8},{5,0},{6,10},{7,2},{8,20},{9,5},{1... | collective-permute-start | bytes 196616 | tf_op jit(solution)/shard_map/ppermute | solution.py:503
  9.0 1.8 %collective-permute-done.1.over_y.refs_4_ = bf16[256,256]{1,0:T(8,128)(2,1)S(1)} collective-permute-done((bf16[256,256]{1,0:T(8,128)(2,1)S(1)}, bf16[256,256]{1,0:T(8,128)(2,1)S(1)}, u32[]{:S(2)}, u32[]{:S(2)}) %collective-permute-start.1) | collective-permute-done | bytes 131104 | tf_op jit(solution)/shard_map/ppermute | solution.py:473
  10.8 1.5 %collective-permute-start.2 = (bf16[256,256]{1,0:T(8,128)(2,1)S(1)}, bf16[256,256]{1,0:T(8,128)(2,1)S(1)}, u32[]{:S(2)}, u32[]{:S(2)}) collective-permute-start(bf16[256,256]{1,0:T(8,128)(2,1)S(1)} %collective-permute-done.1.over_y.refs_4_), channel_id=1, source_target_pairs={{0,4},{4,0},{1,5},{5,1},{2,6},{6,2},{3,7},{7,3},{8,12},{12,8},{9,1... | collective-permute-start | bytes 393224 | tf_op jit(solution)/shard_map/ppermute | solution.py:498
  12.3 0.6 %collective-permute-start.8 = (bf16[2,128,128]{2,1,0:T(8,128)(2,1)S(1)}, bf16[2,128,128]{2,1,0:T(8,128)(2,1)S(1)}, u32[]{:S(2)}, u32[]{:S(2)}) collective-permute-start(bf16[2,128,128]{2,1,0:T(8,128)(2,1)S(1)} %get-tuple-element.42), channel_id=1, source_target_pairs={{0,4},{4,0},{1,5},{5,1},{2,6},{6,2},{3,7},{7,3},{8,12},{12,8},{9,1... | collective-permute-start | bytes 196616 | tf_op jit(solution)/shard_map/ppermute | solution.py:504
  13.5 0.0 copy-start.2
  13.5 0.7 %copy-done.2 = s32[1,1,2,2]{3,2,1,0:T(2,128)S(1)} copy-done((s32[1,1,2,2]{3,2,1,0:T(2,128)S(1)}, s32[1,1,2,2]{3,2,1,0:T(2,128)}, u32[]{:S(2)}) %copy-start.2) | copy-done | bytes 40
  14.2 1.8 %record.1 = (bf16[16,256]{1,0:T(8,128)(2,1)S(1)}, bf16[512,512]{1,0:T(8,128)(2,1)S(1)}, bf16[512,512]{1,0:T(8,128)(2,1)S(1)}) custom-call(s32[1,1,2,2]{3,2,1,0:T(2,128)S(1)} %copy-done.2, s32[1,1]{1,0:T(1,128)S(6)} %copy.8.live_ref, bf16[512,512]{1,0:T(8,128)(2,1)} %constant.4.clone.direct_hbm, bf16[512,512]{1,0:T(8,128)(2,1)} %constant.5.clone.swapped_hbm), custom_call_target="tpu_custom_call" | custom-call | tf_op jit(solution)/shard_map/record/pallas_call | solution.py:510
  15.9 0.6 %collective-permute-done.8.refs_5_ = bf16[2,128,128]{2,1,0:T(8,128)(2,1)S(1)} collective-permute-done((bf16[2,128,128]{2,1,0:T(8,128)(2,1)S(1)}, bf16[2,128,128]{2,1,0:T(8,128)(2,1)S(1)}, u32[]{:S(2)}, u32[]{:S(2)}) %collective-permute-start.8) | collective-permute-done | bytes 65568 | tf_op jit(solution)/shard_map/ppermute | solution.py:504
  16.5 0.0 collective-permute-done.6.refs_2_
  16.5 2.4 %near.1 = (f32[2,256,256]{2,1,0:T(8,128)S(1)}, f32[4,256,512]{2,1,0:T(8,128)S(1)}, bf16[4,512,256]{2,1,0:T(8,128)(2,1)S(1)}, f32[2,256,256]{2,1,0:T(8,128)S(1)}) custom-call(bf16[16,256]{1,0:T(8,128)(2,1)S(1)} %get-tuple-element.37.record_ref, bf16[2,128,256]{2,1,0:T(8,128)(2,1)S(1)} %get-tuple-element.34.refs_0_, ...), custom_call_target="tpu_custom_call" | custom-call | tf_op jit(solution)/shard_map/near/pallas_call | solution.py:531
  19.0 0.1 collective-permute-start.11
  19.1 0.5 %collective-permute-start.9 = (bf16[256,256]{1,0:T(8,128)(2,1)S(1)}, bf16[256,256]{1,0:T(8,128)(2,1)S(1)}, u32[]{:S(2)}, u32[]{:S(2)}) collective-permute-start(bf16[256,256]{1,0:T(8,128)(2,1)S(1)} %collective-permute-done.1.over_y.refs_4_), channel_id=1, source_target_pairs={{0,1},{1,0},{2,3},{3,2},{4,5},{5,4},{6,7},{7,6},{8,9},{9,8},{10,11... | collective-permute-start | bytes 393224 | tf_op jit(solution)/shard_map/ppermute | solution.py:473
  19.6 0.1 collective-permute-start.10
  19.7 0.9 %over.1 = (f32[2,256,512]{2,1,0:T(8,128)S(1)}, bf16[2,512,256]{2,1,0:T(8,128)(2,1)S(1)}, f32[2,256,256]{2,1,0:T(8,128)S(1)}) custom-call(f32[2,256,256]{2,1,0:T(8,128)S(1)} %get-tuple-element.47.patch_ref.refs_1_, bf16[256,256]{1,0:T(8,128)(2,1)S(1)} %collective-permute-done.1.over_y.refs_4_, bf16[256,256]{1,0:T(8,128)(2,1)S(1)} %collective-permute-done.2.over_x.refs_5_, ...), custom_call_target="tpu_custom_call" | custom-call | tf_op jit(solution)/shard_map/over/pallas_call | solution.py:543
  20.6 0.2 collective-permute-done.9.refs_7_
  20.8 0.2 collective-permute-done.10.refs_8_
  21.0 4.7 %back.1 = (bf16[272,256]{1,0:T(8,128)(2,1)S(1)}, bf16[272,256]{1,0:T(8,128)(2,1)S(1)}, bf16[272,256]{1,0:T(8,128)(2,1)S(1)}, bf16[272,128]{1,0:T(8,128)(2,1)S(1)...) custom-call(bf16[16,256]{1,0:T(8,128)(2,1)S(1)} %get-tuple-element.37.record_ref, ...), custom_call_target="tpu_custom_call" | custom-call | tf_op jit(solution)/shard_map/back/pallas_call | solution.py:553
  25.7 1.7 %collective-permute-start.14 = (bf16[272,256]{1,0:T(8,128)(2,1)S(1)}, bf16[272,256]{1,0:T(8,128)(2,1)S(1)}, u32[]{:S(2)}, u32[]{:S(2)}) collective-permute-start(bf16[272,256]{1,0:T(8,128)(2,1)S(1)} %get-tuple-element.59), channel_id=1, source_target_pairs={{0,8},{1,0},{2,10},{3,2},{4,12},{5,4},{6,14},{7,6},{8,16},{9,1},{1... | collective-permute-start | bytes 417800 | tf_op jit(solution)/shard_map/ppermute | solution.py:585
  27.4 2.9 %collective-permute-start.12 = (bf16[272,128]{1,0:T(8,128)(2,1)S(1)}, bf16[272,128]{1,0:T(8,128)(2,1)S(1)}, u32[]{:S(2)}, u32[]{:S(2)}) collective-permute-start(bf16[272,128]{1,0:T(8,128)(2,1)S(1)} %get-tuple-element.57), channel_id=1, source_target_pairs={{0,12},{1,4},{2,14},{3,6},{4,8},{5,0},{6,10},{7,2},{8,20},{9,5},{1... | collective-permute-start | bytes 208904 | tf_op jit(solution)/shard_map/ppermute | solution.py:583
  30.3 0.6 %collective-permute-start.16 = (bf16[272,128]{1,0:T(8,128)(2,1)S(1)}, bf16[272,128]{1,0:T(8,128)(2,1)S(1)}, u32[]{:S(2)}, u32[]{:S(2)}) collective-permute-start(bf16[272,128]{1,0:T(8,128)(2,1)S(1)} %get-tuple-element.61), channel_id=1, source_target_pairs={{0,4},{4,0},{1,5},{5,1},{2,6},{6,2},{3,7},{7,3},{8,12},{12,8},{9,1... | collective-permute-start | bytes 208904 | tf_op jit(solution)/shard_map/ppermute | solution.py:587
  30.9 1.3 %collective-permute-done.12.refs_1_ = bf16[272,128]{1,0:T(8,128)(2,1)S(1)} collective-permute-done((bf16[272,128]{1,0:T(8,128)(2,1)S(1)}, bf16[272,128]{1,0:T(8,128)(2,1)S(1)}, u32[]{:S(2)}, u32[]{:S(2)}) %collective-permute-start.12) | collective-permute-done | bytes 69664 | tf_op jit(solution)/shard_map/ppermute | solution.py:583
  32.2 3.3 %collective-permute-done.13.refs_2_ = bf16[272,128]{1,0:T(8,128)(2,1)S(1)} collective-permute-done((bf16[272,128]{1,0:T(8,128)(2,1)S(1)}, bf16[272,128]{1,0:T(8,128)(2,1)S(1)}, u32[]{:S(2)}, u32[]{:S(2)}) %collective-permute-start.13) | collective-permute-done | bytes 69664 | tf_op jit(solution)/shard_map/ppermute | solution.py:583
  35.5 0.1 sums.1.own_ref
  35.6 0.1 collective-permute-start.17
  35.7 0.7 %weights.1.weight_ref = f32[128,256]{1,0:T(8,128)S(1)} custom-call(bf16[256,256]{1,0:T(8,128)(2,1)S(1)} %get-tuple-element.62.weight_ref, bf16[272,256]{1,0:T(8,128)(2,1)S(1)} %get-tuple-element.56.refs_0_, bf16[272,128]{1,0:T(8,128)(2,1)S(1)} %collective-permute-done.12.refs_1_, bf16[272,128]{1,0:T(8,128)(2,1)S(1)} %collective-permute-done.13.refs_2_, ...), custom_call_target="tpu_custom_call" | custom-call | tf_op jit(solution)/shard_map/weights/pallas_call | solution.py:596
  36.5 0.6 %collective-permute-done.17.other_ref = bf16[2,128,256]{2,1,0:T(8,128)(2,1)S(1)} collective-permute-done((bf16[2,128,256]{2,1,0:T(8,128)(2,1)S(1)}, bf16[2,128,256]{2,1,0:T(8,128)(2,1)S(1)}, u32[]{:S(2)}, u32[]{:S(2)}) %collective-permute-start.17) | collective-permute-done | bytes 131104 | tf_op jit(solution)/shard_map/ppermute | solution.py:473
  37.1 0.8 %update.1 = f32[2,128,256]{2,1,0:T(8,128)} custom-call(f32[2,128,256]{2,1,0:T(8,128)S(1)} %copy-done, bf16[2,128,256]{2,1,0:T(8,128)(2,1)S(1)} %sums.1.own_ref, bf16[2,128,256]{2,1,0:T(8,128)(2,1)S(1)} %collective-permute-done.17.other_ref, f32[128,256]{1,0:T(8,128)S(1)} %weights.1.weight_ref), custom_call_target="tpu_custom_call" | custom-call | tf_op jit(solution)/shard_map/update/pallas_call | solution.py:605
  (18 shorter events, 0.0 us)
Async XLA Ops:
  1.3 4.6 %collective-permute-start.3 = (bf16[2,2,256,256]{3,2,1,0:T(8,128)(2,1)S(1)}, bf16[2,2,256,256]{3,2,1,0:T(8,128)(2,1)S(1)}, u32[]{:S(2)}, u32[]{:S(2)}) collective-permute-start(bf16[2,2,256,256]{3,2,1,0:T(8,128)(2,1)S(1)} %get-tuple-element.39.refs_6_.refs_2_), channel_id=1, source_target_pairs={{0,1},{1,0},{2,3},{3,2},{4,5},{5,4},{6,7},{7,6},{8,9},{9,8},{10,11... | collective-permute-start | bytes 1572872 | tf_op jit(solution)/shard_map/ppermute | solution.py:473
  1.9 7.1 %collective-permute-start = (bf16[2,128,256]{2,1,0:T(8,128)(2,1)S(1)}, bf16[2,128,256]{2,1,0:T(8,128)(2,1)S(1)}, u32[]{:S(2)}, u32[]{:S(2)}) collective-permute-start(bf16[2,128,256]{2,1,0:T(8,128)(2,1)S(1)} %get-tuple-element.34.refs_0_), channel_id=1, source_target_pairs={{0,8},{1,0},{2,10},{3,2},{4,12},{5,4},{6,14},{7,6},{8,16},{9,1},{1... | collective-permute-start | bytes 393224 | tf_op jit(solution)/shard_map/ppermute | solution.py:500
  4.5 6.3 %collective-permute-start.1 = (bf16[256,256]{1,0:T(8,128)(2,1)S(1)}, bf16[256,256]{1,0:T(8,128)(2,1)S(1)}, u32[]{:S(2)}, u32[]{:S(2)}) collective-permute-start(bf16[256,256]{1,0:T(8,128)(2,1)S(1)} %get-tuple-element.38), channel_id=1, source_target_pairs={{0,2},{1,3},{2,0},{3,1},{4,6},{5,7},{6,4},{7,5},{8,10},{9,11},{10,... | collective-permute-start | bytes 393224 | tf_op jit(solution)/shard_map/ppermute | solution.py:473
  6.0 13.0 %collective-permute-start.4 = (bf16[2,1,256,256]{3,2,1,0:T(8,128)(2,1)S(1)}, bf16[2,1,256,256]{3,2,1,0:T(8,128)(2,1)S(1)}, u32[]{:S(2)}, u32[]{:S(2)}) collective-permute-start(bf16[2,1,256,256]{3,2,1,0:T(8,128)(2,1)S(1)} %get-tuple-element.41), channel_id=1, source_target_pairs={{0,2},{1,3},{2,0},{3,1},{4,6},{5,7},{6,4},{7,5},{8,10},{9,11},{10,... | collective-permute-start | bytes 786440 | tf_op jit(solution)/shard_map/ppermute | solution.py:473
  6.5 6.3 %collective-permute-start.5 = (bf16[2,128,128]{2,1,0:T(8,128)(2,1)S(1)}, bf16[2,128,128]{2,1,0:T(8,128)(2,1)S(1)}, u32[]{:S(2)}, u32[]{:S(2)}) collective-permute-start(bf16[2,128,128]{2,1,0:T(8,128)(2,1)S(1)} %get-tuple-element.42), channel_id=1, source_target_pairs={{0,12},{1,4},{2,14},{3,6},{4,8},{5,0},{6,10},{7,2},{8,20},{9,5},{1... | collective-permute-start | bytes 196616 | tf_op jit(solution)/shard_map/ppermute | solution.py:503
  9.0 7.5 %collective-permute-start.7 = (bf16[2,128,256]{2,1,0:T(8,128)(2,1)S(1)}, bf16[2,128,256]{2,1,0:T(8,128)(2,1)S(1)}, u32[]{:S(2)}, u32[]{:S(2)}) collective-permute-start(bf16[2,128,256]{2,1,0:T(8,128)(2,1)S(1)} %collective-permute-done.refs_3_), channel_id=1, source_target_pairs={{0,1},{1,0},{2,3},{3,2},{4,5},{5,4},{6,7},{7,6},{8,9},{9,8},{10,11... | collective-permute-start | bytes 393224 | tf_op jit(solution)/shard_map/ppermute | solution.py:473
  10.8 8.2 %collective-permute-start.2 = (bf16[256,256]{1,0:T(8,128)(2,1)S(1)}, bf16[256,256]{1,0:T(8,128)(2,1)S(1)}, u32[]{:S(2)}, u32[]{:S(2)}) collective-permute-start(bf16[256,256]{1,0:T(8,128)(2,1)S(1)} %collective-permute-done.1.over_y.refs_4_), channel_id=1, source_target_pairs={{0,4},{4,0},{1,5},{5,1},{2,6},{6,2},{3,7},{7,3},{8,12},{12,8},{9,1... | collective-permute-start | bytes 393224 | tf_op jit(solution)/shard_map/ppermute | solution.py:498
  12.3 4.3 %collective-permute-start.8 = (bf16[2,128,128]{2,1,0:T(8,128)(2,1)S(1)}, bf16[2,128,128]{2,1,0:T(8,128)(2,1)S(1)}, u32[]{:S(2)}, u32[]{:S(2)}) collective-permute-start(bf16[2,128,128]{2,1,0:T(8,128)(2,1)S(1)} %get-tuple-element.42), channel_id=1, source_target_pairs={{0,4},{4,0},{1,5},{5,1},{2,6},{6,2},{3,7},{7,3},{8,12},{12,8},{9,1... | collective-permute-start | bytes 196616 | tf_op jit(solution)/shard_map/ppermute | solution.py:504
  12.8 3.7 %collective-permute-start.6 = (bf16[2,128,128]{2,1,0:T(8,128)(2,1)S(1)}, bf16[2,128,128]{2,1,0:T(8,128)(2,1)S(1)}, u32[]{:S(2)}, u32[]{:S(2)}) collective-permute-start(bf16[2,128,128]{2,1,0:T(8,128)(2,1)S(1)} %collective-permute-done.5.refs_1_), channel_id=1, source_target_pairs={{0,1},{1,0},{2,3},{3,2},{4,5},{5,4},{6,7},{7,6},{8,9},{9,8},{10,11... | collective-permute-start | bytes 196616 | tf_op jit(solution)/shard_map/ppermute | solution.py:473
  13.5 0.7 %copy-start.2 = (s32[1,1,2,2]{3,2,1,0:T(2,128)S(1)}, s32[1,1,2,2]{3,2,1,0:T(2,128)}, u32[]{:S(2)}) copy-start(s32[1,1,2,2]{3,2,1,0:T(2,128)} %centers_ref) | copy-start | bytes 52
  16.5 4.5 %copy-start.1 = (bf16[1,1,2,256,256]{4,3,2,1,0:T(8,128)(2,1)S(1)}, bf16[1,1,2,256,256]{4,3,2,1,0:T(8,128)(2,1)}, u32[]{:S(2)}) copy-start(bf16[1,1,2,256,256]{4,3,2,1,0:T(8,128)(2,1)} %refs_0_.1) | copy-start | bytes 786436
  19.0 2.0 %collective-permute-start.11 = (bf16[2,1,256,256]{3,2,1,0:T(8,128)(2,1)S(1)}, bf16[2,1,256,256]{3,2,1,0:T(8,128)(2,1)S(1)}, u32[]{:S(2)}, u32[]{:S(2)}) collective-permute-start(bf16[2,1,256,256]{3,2,1,0:T(8,128)(2,1)S(1)} %collective-permute-done.4.rest.refs_6_), channel_id=1, source_target_pairs={{0,1},{1,0},{2,3},{3,2},{4,5},{5,4},{6,7},{7,6},{8,9},{9,8},{10,11... | collective-permute-start | bytes 786440 | tf_op jit(solution)/shard_map/ppermute | solution.py:473
  19.1 1.7 %collective-permute-start.9 = (bf16[256,256]{1,0:T(8,128)(2,1)S(1)}, bf16[256,256]{1,0:T(8,128)(2,1)S(1)}, u32[]{:S(2)}, u32[]{:S(2)}) collective-permute-start(bf16[256,256]{1,0:T(8,128)(2,1)S(1)} %collective-permute-done.1.over_y.refs_4_), channel_id=1, source_target_pairs={{0,1},{1,0},{2,3},{3,2},{4,5},{5,4},{6,7},{7,6},{8,9},{9,8},{10,11... | collective-permute-start | bytes 393224 | tf_op jit(solution)/shard_map/ppermute | solution.py:473
  19.6 1.4 %collective-permute-start.10 = (bf16[256,256]{1,0:T(8,128)(2,1)S(1)}, bf16[256,256]{1,0:T(8,128)(2,1)S(1)}, u32[]{:S(2)}, u32[]{:S(2)}) collective-permute-start(bf16[256,256]{1,0:T(8,128)(2,1)S(1)} %collective-permute-done.2.over_x.refs_5_), channel_id=1, source_target_pairs={{0,1},{1,0},{2,3},{3,2},{4,5},{5,4},{6,7},{7,6},{8,9},{9,8},{10,11... | collective-permute-start | bytes 393224 | tf_op jit(solution)/shard_map/ppermute | solution.py:473
  21.0 16.1 %copy-start = (f32[2,128,256]{2,1,0:T(8,128)S(1)}, f32[2,128,256]{2,1,0:T(8,128)}, u32[]{:S(2)}) copy-start(f32[2,128,256]{2,1,0:T(8,128)} %object_ref.1) | copy-start | bytes 786436
  25.7 9.8 %collective-permute-start.14 = (bf16[272,256]{1,0:T(8,128)(2,1)S(1)}, bf16[272,256]{1,0:T(8,128)(2,1)S(1)}, u32[]{:S(2)}, u32[]{:S(2)}) collective-permute-start(bf16[272,256]{1,0:T(8,128)(2,1)S(1)} %get-tuple-element.59), channel_id=1, source_target_pairs={{0,8},{1,0},{2,10},{3,2},{4,12},{5,4},{6,14},{7,6},{8,16},{9,1},{1... | collective-permute-start | bytes 417800 | tf_op jit(solution)/shard_map/ppermute | solution.py:585
  27.4 8.1 %collective-permute-start.15 = (bf16[272,256]{1,0:T(8,128)(2,1)S(1)}, bf16[272,256]{1,0:T(8,128)(2,1)S(1)}, u32[]{:S(2)}, u32[]{:S(2)}) collective-permute-start(bf16[272,256]{1,0:T(8,128)(2,1)S(1)} %get-tuple-element.60), channel_id=1, source_target_pairs={{0,1},{1,9},{2,3},{3,11},{4,5},{5,13},{6,7},{7,15},{8,0},{9,17},{1... | collective-permute-start | bytes 417800 | tf_op jit(solution)/shard_map/ppermute | solution.py:585
  27.4 4.8 %collective-permute-start.12 = (bf16[272,128]{1,0:T(8,128)(2,1)S(1)}, bf16[272,128]{1,0:T(8,128)(2,1)S(1)}, u32[]{:S(2)}, u32[]{:S(2)}) collective-permute-start(bf16[272,128]{1,0:T(8,128)(2,1)S(1)} %get-tuple-element.57), channel_id=1, source_target_pairs={{0,12},{1,4},{2,14},{3,6},{4,8},{5,0},{6,10},{7,2},{8,20},{9,5},{1... | collective-permute-start | bytes 208904 | tf_op jit(solution)/shard_map/ppermute | solution.py:583
  30.3 5.2 %collective-permute-start.13 = (bf16[272,128]{1,0:T(8,128)(2,1)S(1)}, bf16[272,128]{1,0:T(8,128)(2,1)S(1)}, u32[]{:S(2)}, u32[]{:S(2)}) collective-permute-start(bf16[272,128]{1,0:T(8,128)(2,1)S(1)} %get-tuple-element.58), channel_id=1, source_target_pairs={{0,5},{1,13},{2,7},{3,15},{4,1},{5,9},{6,3},{7,11},{8,4},{9,21},{1... | collective-permute-start | bytes 208904 | tf_op jit(solution)/shard_map/ppermute | solution.py:583
  30.3 5.2 %collective-permute-start.16 = (bf16[272,128]{1,0:T(8,128)(2,1)S(1)}, bf16[272,128]{1,0:T(8,128)(2,1)S(1)}, u32[]{:S(2)}, u32[]{:S(2)}) collective-permute-start(bf16[272,128]{1,0:T(8,128)(2,1)S(1)} %get-tuple-element.61), channel_id=1, source_target_pairs={{0,4},{4,0},{1,5},{5,1},{2,6},{6,2},{3,7},{7,3},{8,12},{12,8},{9,1... | collective-permute-start | bytes 208904 | tf_op jit(solution)/shard_map/ppermute | solution.py:587
  35.6 1.4 %collective-permute-start.17 = (bf16[2,128,256]{2,1,0:T(8,128)(2,1)S(1)}, bf16[2,128,256]{2,1,0:T(8,128)(2,1)S(1)}, u32[]{:S(2)}, u32[]{:S(2)}) collective-permute-start(bf16[2,128,256]{2,1,0:T(8,128)(2,1)S(1)} %sums.1.own_ref), channel_id=1, source_target_pairs={{0,1},{1,0},{2,3},{3,2},{4,5},{5,4},{6,7},{7,6},{8,9},{9,8},{10,11... | collective-permute-start | bytes 393224 | tf_op jit(solution)/shard_map/ppermute | solution.py:473

commit v8 on v7

--- a/solution.py
+++ b/solution.py
@@ -76,13 +76,35 @@
     return (lax.axis_index("tx"), lax.axis_index("ty"), lax.axis_index("mode") % 2)
 
 
-def start_kernel(sides, object_hbm, probe_hbm, low_ref, shared_ref, rest_ref, packed_ref, *rest):
-    edges = rest[:sides]
-    object_ref, probe_ref, sems = rest[sides:]
+def start_kernel(
+    sides,
+    slots,
+    object_hbm,
+    probe_hbm,
+    centers_hbm,
+    direct_hbm,
+    swapped_hbm,
+    low_ref,
+    shared_ref,
+    rest_ref,
+    record_ref,
+    direct_ref,
+    swapped_ref,
+    packed_ref,
+    *refs,
+):
+    edges = refs[:sides]
+    object_ref, probe_ref, centers_ref, sems = refs[sides:]
     copies = [
         pltpu.make_async_copy(source, target, sems.at[index])
         for index, (source, target) in enumerate(
-            ((probe_hbm, probe_ref), (object_hbm, object_ref))
+            (
+                (probe_hbm, probe_ref),
+                (object_hbm, object_ref),
+                (centers_hbm, centers_ref),
+                (direct_hbm, direct_ref),
+                (swapped_hbm, swapped_ref),
+            )
         )
     ]
     for copy in copies:
@@ -104,27 +126,23 @@
         else:
             edges[0][channel] = values[:, last]
             edges[1][channel] = values[:, first]
-
-
-def record_kernel(
-    slots, centers_ref, live_ref, direct_hbm, swapped_hbm, out_ref, direct_ref, swapped_ref, sems
-):
-    copies = [
-        pltpu.make_async_copy(direct_hbm, direct_ref, sems.at[0]),
-        pltpu.make_async_copy(swapped_hbm, swapped_ref, sems.at[1]),
-    ]
-    for copy in copies:
-        copy.start()
-    record = jnp.zeros(out_ref.shape, jnp.float32)
-    line = iota(out_ref.shape, 0)
+    copies[2].wait()
+    record = jnp.zeros(record_ref.shape, jnp.float32)
+    line = iota(record_ref.shape, 0)
     for slot in range(slots):
         for axis in range(2):
             value = centers_ref[0, 0, slot, axis].astype(jnp.float32)
             record = jnp.where(line == 2 * slot + axis, value, record)
+    record_ref[...] = record.astype(jnp.bfloat16)
+    copies[3].wait()
+    copies[4].wait()
+
+
+def live_kernel(slots, record_ref, live_ref, out_ref):
+    line = iota(record_ref.shape, 0)
+    record = record_ref[...].astype(jnp.float32)
     record = jnp.where(line == 2 * slots, live_ref[0, 0].astype(jnp.float32), record)
     out_ref[...] = record.astype(jnp.bfloat16)
-    for copy in copies:
-        copy.wait()
 
 
 def positions(record_ref, slots):
@@ -472,51 +490,51 @@
     def exchange(array, flip):
         return lax.ppermute(array, "mode", [(m, m ^ flip) for m in range(m_count)])
 
-    probe_low, shared, rest, *packed = pl.pallas_call(
-        functools.partial(start_kernel, sides),
+    tables = [jnp.asarray(matrix) for matrix in dft_matrices(side)]
+    probe_low, shared, rest, record, direct, swapped, *packed = pl.pallas_call(
+        functools.partial(start_kernel, sides, slots),
         out_shape=[
             jax.ShapeDtypeStruct(probe.shape, jnp.bfloat16),
             jax.ShapeDtypeStruct((side, side), jnp.bfloat16),
             jax.ShapeDtypeStruct((2, modes - 1, side, side), jnp.bfloat16),
+            jax.ShapeDtypeStruct((record_rows, tile_cols), jnp.bfloat16),
+            jax.ShapeDtypeStruct((2 * side, 2 * side), jnp.bfloat16),
+            jax.ShapeDtypeStruct((2 * side, 2 * side), jnp.bfloat16),
             jax.ShapeDtypeStruct(object_field.shape, jnp.bfloat16),
         ]
         + [jax.ShapeDtypeStruct((2, tile_rows, half), jnp.bfloat16)] * sides,
-        in_specs=[hbm()] * 2,
-        out_specs=[vmem()] * (4 + sides),
+        in_specs=[hbm()] * 5,
+        out_specs=[vmem()] * (7 + sides),
         scratch_shapes=[
             pltpu.VMEM(object_field.shape, jnp.float32),
             pltpu.VMEM(probe.shape, jnp.float32),
-            pltpu.SemaphoreType.DMA((2,)),
+            pltpu.SMEM(centers.shape, jnp.int32),
+            pltpu.SemaphoreType.DMA((5,)),
         ],
         compiler_params=pltpu.CompilerParams(vmem_limit_bytes=small_bytes),
         name="start",
-    )(in_hbm(object_field), in_hbm(probe))
+    )(*(in_hbm(array) for array in (object_field, probe, centers, *tables)))
     over_y = exchange(shared, 2)
     probe_core = exchange(probe_low, 1)
-    probe_core, rest = lax.optimization_barrier((probe_core, rest))
+    probe_core, rest, live = lax.optimization_barrier((probe_core, rest, live))
     rest = exchange(rest, 2)
     over_x = lax.ppermute(over_y, "ty", [(x, x ^ 1) for x in range(x_count)])
     x_steps = [1] if sides == 1 else [1, -1]
-    moved = [lax.ppermute(packed[0], axes, zigzag(0))]
-    levels = []
-    for step, edge in zip(x_steps, packed[1:]):
-        moved.append(lax.ppermute(edge, axes, zigzag(step)))
-        levels.append(lax.ppermute(edge, "ty", level(step)))
-    pieces = [packed[0], moved[0], exchange(moved[0], 1)]
-    for here_level, corner in zip(levels, moved[1:]):
-        pieces += [here_level, corner, exchange(corner, 1)]
-    tables = [in_hbm(jnp.asarray(matrix)) for matrix in dft_matrices(side)]
-    centers, live, moved[0] = lax.optimization_barrier((centers, live, moved[0]))
-    record, direct, swapped = pl.pallas_call(
-        functools.partial(record_kernel, slots),
-        out_shape=[jax.ShapeDtypeStruct((record_rows, tile_cols), jnp.bfloat16)]
-        + [jax.ShapeDtypeStruct((2 * side, 2 * side), jnp.bfloat16)] * 2,
-        in_specs=[smem(), smem(), hbm(), hbm()],
-        out_specs=[vmem()] * 3,
-        scratch_shapes=[pltpu.SemaphoreType.DMA((2,))],
+    rows = lax.ppermute(packed[0], axes, zigzag(0))
+    corners = [lax.ppermute(edge, axes, zigzag(step)) for step, edge in zip(x_steps, packed[1:])]
+    levels = [lax.ppermute(edge, "ty", level(step)) for step, edge in zip(x_steps, packed[1:])]
+    record = pl.pallas_call(
+        functools.partial(live_kernel, slots),
+        out_shape=jax.ShapeDtypeStruct(record.shape, jnp.bfloat16),
+        in_specs=[vmem(), smem()],
+        out_specs=vmem(),
         compiler_params=pltpu.CompilerParams(vmem_limit_bytes=small_bytes),
-        name="record",
-    )(centers, live, *tables)
+        name="live",
+    )(record, live)
+    rows, record, *levels = lax.optimization_barrier((rows, record, *levels))
+    pieces = [packed[0], rows, exchange(rows, 1)]
+    for at_level, corner in zip(levels, corners):
+        pieces += [at_level, corner, exchange(corner, 1)]
     n_pieces = len(pieces)
     ext_rows = tile_rows + side
     ext_cols = tile_cols + sides * half

time: 38 us -> 36.4 us (0.958)
  Pallas kernels: 12.8 us -> 11.3 us
  local copies, waits for them, and re-layouts: 0.68 us -> 0.01 us
  waiting for transfers between devices: 7.96 us -> 8.38 us
    pallas_call x2, Pallas kernels: 3.09 us -> 1.64 us  [the longest x1 1.64 us: on_device(): pl.pallas_call(functools.partial(start_kernel, sides, slots), out_shape=[...]
    ppermute x1, starting transfers between devices: 1.46 us -> 2.55 us  [on_device(): over_x = lax.ppermute(over_y, 'ty', [(x, x ^ 1) for x in range(x_count)])]
    ppermute x2, starting transfers between devices: 1.73 us -> 0.9 us  [on_device(): received[1 + turn] = lax.ppermute(results[1 + turn], axes, zigzag(0, flip))]
    unnamed x6 -> x4, local copies, waits for them, and re-layouts: 0.68 us -> 0.01 us
    ppermute x9, waiting for transfers between devices: 2.78 us -> 2.19 us  [exchange(): return lax.ppermute(array, 'mode', [(m, m ^ flip) for m in range(m_count)])]
    ppermute x1, waiting for transfers between devices: 0.01 us -> 0.45 us  [on_device(): over_x = lax.ppermute(over_y, 'ty', [(x, x ^ 1) for x in range(x_count)])]
  transfers between devices with their start and end apart: 18 -> 18, of which waited for: 7 -> 8; matrix products, arithmetic and copies ran while one was open for 0% -> 0% of each run, Pallas kernels for 16% -> 11%
where the time goes in v8:
time: 36.4 us; the launch traced here: 36.2 us
  starting transfers between devices  15.9 us (44%)
  Pallas kernels  11.3 us (31%)
  waiting for transfers between devices  8.38 us (23%)
  between operations  0.73 us (2%)
    ppermute x2, waiting for transfers between devices, on_device(): lax.ppermute(results[at + 1 + turn], axes, zigzag(-step, flip))  4.92 us
    pallas_call x1, Pallas kernels, on_device(): pl.pallas_call(functools.partial(back_kernel, sides, slots, x_count, tile...  4.71 us
    ppermute x9, starting transfers between devices, exchange(): return lax.ppermute(array, 'mode', [(m, m ^ flip) for m in range(m_count)])  3.29 us
    ppermute x2, starting transfers between devices, on_device(): lax.ppermute(results[at + 1 + turn], axes, zigzag(-step, flip))  3.2 us
    ppermute x1, starting transfers between devices, on_device(): rows = lax.ppermute(packed[0], axes, zigzag(0))  2.6 us
    ppermute x1, starting transfers between devices, on_device(): over_x = lax.ppermute(over_y, 'ty', [(x, x ^ 1) for x in range(x_count)])  2.55 us
    pallas_call x1, Pallas kernels, on_device(): pl.pallas_call(functools.partial(near_kernel, sides, slots, z_count, x_co...  2.38 us
    ppermute x9, waiting for transfers between devices, exchange(): return lax.ppermute(array, 'mode', [(m, m ^ flip) for m in range(m_count)])  2.19 us
  transfers between devices with their start and end apart: 18, of which 8 were waited for; matrix products, arithmetic and copies ran while one was open for 0% of the time, Pallas kernels for 11%

profile of v8, /device:TPU:0, one launch (start us, length us, event | category | flops | bytes accessed | tf_op | source)
XLA Modules:
  0.0 36.2 jit_solution(8646865621415151889)
XLA Ops:
  0.0 1.6 %start.1 = (bf16[2,2,256,256]{3,2,1,0:T(8,128)(2,1)S(1)}, bf16[256,256]{1,0:T(8,128)(2,1)S(1)}, bf16[2,1,256,256]{3,2,1,0:T(8,128)(2,1)S(1)}, bf16[16,256]{1,0:T...) custom-call(f32[2,128,256]{2,1,0:T(8,128)} %object_ref.1, ...), custom_call_target="tpu_custom_call" | custom-call | tf_op jit(solution)/shard_map/start/pallas_call | solution.py:494
  1.6 0.5 %collective-permute-start.1 = (bf16[2,2,256,256]{3,2,1,0:T(8,128)(2,1)S(1)}, bf16[2,2,256,256]{3,2,1,0:T(8,128)(2,1)S(1)}, u32[]{:S(2)}, u32[]{:S(2)}) collective-permute-start(bf16[2,2,256,256]{3,2,1,0:T(8,128)(2,1)S(1)} %get-tuple-element.38.refs_6_.refs_2_), channel_id=1, source_target_pairs={{0,1},{1,0},{2,3},{3,2},{4,5},{5,4},{6,7},{7,6},{8,9},{9,8},{10,11... | collective-permute-start | bytes 1572872 | tf_op jit(solution)/shard_map/ppermute | solution.py:491
  2.2 2.6 %collective-permute-start = (bf16[2,128,256]{2,1,0:T(8,128)(2,1)S(1)}, bf16[2,128,256]{2,1,0:T(8,128)(2,1)S(1)}, u32[]{:S(2)}, u32[]{:S(2)}) collective-permute-start(bf16[2,128,256]{2,1,0:T(8,128)(2,1)S(1)} %get-tuple-element.36.refs_0_), channel_id=1, source_target_pairs={{0,8},{1,0},{2,10},{3,2},{4,12},{5,4},{6,14},{7,6},{8,16},{9,1},{1... | collective-permute-start | bytes 393224 | tf_op jit(solution)/shard_map/ppermute | solution.py:523
  4.8 1.5 %collective-permute-start.3 = (bf16[256,256]{1,0:T(8,128)(2,1)S(1)}, bf16[256,256]{1,0:T(8,128)(2,1)S(1)}, u32[]{:S(2)}, u32[]{:S(2)}) collective-permute-start(bf16[256,256]{1,0:T(8,128)(2,1)S(1)} %get-tuple-element.43), channel_id=1, source_target_pairs={{0,2},{1,3},{2,0},{3,1},{4,6},{5,7},{6,4},{7,5},{8,10},{9,11},{10,... | collective-permute-start | bytes 393224 | tf_op jit(solution)/shard_map/ppermute | solution.py:491
  6.3 0.5 %collective-permute-start.5 = (bf16[2,1,256,256]{3,2,1,0:T(8,128)(2,1)S(1)}, bf16[2,1,256,256]{3,2,1,0:T(8,128)(2,1)S(1)}, u32[]{:S(2)}, u32[]{:S(2)}) collective-permute-start(bf16[2,1,256,256]{3,2,1,0:T(8,128)(2,1)S(1)} %get-tuple-element.44), channel_id=1, source_target_pairs={{0,2},{1,3},{2,0},{3,1},{4,6},{5,7},{6,4},{7,5},{8,10},{9,11},{10,... | collective-permute-start | bytes 786440 | tf_op jit(solution)/shard_map/ppermute | solution.py:491
  6.8 1.5 %collective-permute-start.2 = (bf16[2,128,128]{2,1,0:T(8,128)(2,1)S(1)}, bf16[2,128,128]{2,1,0:T(8,128)(2,1)S(1)}, u32[]{:S(2)}, u32[]{:S(2)}) collective-permute-start(bf16[2,128,128]{2,1,0:T(8,128)(2,1)S(1)} %get-tuple-element.41), channel_id=1, source_target_pairs={{0,4},{4,0},{1,5},{5,1},{2,6},{6,2},{3,7},{7,3},{8,12},{12,8},{9,1... | collective-permute-start | bytes 196616 | tf_op jit(solution)/shard_map/ppermute | solution.py:525
  8.3 1.5 %collective-permute-start.6 = (bf16[2,128,128]{2,1,0:T(8,128)(2,1)S(1)}, bf16[2,128,128]{2,1,0:T(8,128)(2,1)S(1)}, u32[]{:S(2)}, u32[]{:S(2)}) collective-permute-start(bf16[2,128,128]{2,1,0:T(8,128)(2,1)S(1)} %get-tuple-element.41), channel_id=1, source_target_pairs={{0,12},{1,4},{2,14},{3,6},{4,8},{5,0},{6,10},{7,2},{8,20},{9,5},{1... | collective-permute-start | bytes 196616 | tf_op jit(solution)/shard_map/ppermute | solution.py:524
  10.5 0.8 %collective-permute-done.2.refs_5_ = bf16[2,128,128]{2,1,0:T(8,128)(2,1)S(1)} collective-permute-done((bf16[2,128,128]{2,1,0:T(8,128)(2,1)S(1)}, bf16[2,128,128]{2,1,0:T(8,128)(2,1)S(1)}, u32[]{:S(2)}, u32[]{:S(2)}) %collective-permute-start.2) | collective-permute-done | bytes 65568 | tf_op jit(solution)/shard_map/ppermute | solution.py:525
  11.3 0.0 collective-permute-start.8
  11.3 0.0 collective-permute-done.3.over_y.refs_4_
  11.3 2.5 %collective-permute-start.4 = (bf16[256,256]{1,0:T(8,128)(2,1)S(1)}, bf16[256,256]{1,0:T(8,128)(2,1)S(1)}, u32[]{:S(2)}, u32[]{:S(2)}) collective-permute-start(bf16[256,256]{1,0:T(8,128)(2,1)S(1)} %collective-permute-done.3.over_y.refs_4_), channel_id=1, source_target_pairs={{0,4},{4,0},{1,5},{5,1},{2,6},{6,2},{3,7},{7,3},{8,12},{12,8},{9,1... | collective-permute-start | bytes 393224 | tf_op jit(solution)/shard_map/ppermute | solution.py:521
  13.9 0.0 collective-permute-done.6.refs_1_
  13.9 0.2 collective-permute-start.7
  14.0 1.1 %collective-permute-done.7.refs_2_ = bf16[2,128,128]{2,1,0:T(8,128)(2,1)S(1)} collective-permute-done((bf16[2,128,128]{2,1,0:T(8,128)(2,1)S(1)}, bf16[2,128,128]{2,1,0:T(8,128)(2,1)S(1)}, u32[]{:S(2)}, u32[]{:S(2)}) %collective-permute-start.7) | collective-permute-done | bytes 65568 | tf_op jit(solution)/shard_map/ppermute | solution.py:491
  15.1 2.4 %near.1 = (f32[2,256,256]{2,1,0:T(8,128)S(1)}, f32[4,256,512]{2,1,0:T(8,128)S(1)}, bf16[4,512,256]{2,1,0:T(8,128)(2,1)S(1)}, f32[2,256,256]{2,1,0:T(8,128)S(1)}) custom-call(bf16[16,256]{1,0:T(8,128)(2,1)S(1)} %live.1.record_ref, bf16[2,128,256]{2,1,0:T(8,128)(2,1)S(1)} %get-tuple-element.36.refs_0_, ...), custom_call_target="tpu_custom_call" | custom-call | tf_op jit(solution)/shard_map/near/pallas_call | solution.py:549
  17.5 0.5 %collective-permute-done.4.over_x.refs_5_ = bf16[256,256]{1,0:T(8,128)(2,1)S(1)} collective-permute-done((bf16[256,256]{1,0:T(8,128)(2,1)S(1)}, bf16[256,256]{1,0:T(8,128)(2,1)S(1)}, u32[]{:S(2)}, u32[]{:S(2)}) %collective-permute-start.4) | collective-permute-done | bytes 131104 | tf_op jit(solution)/shard_map/ppermute | solution.py:521
  18.0 0.5 %collective-permute-start.9 = (bf16[256,256]{1,0:T(8,128)(2,1)S(1)}, bf16[256,256]{1,0:T(8,128)(2,1)S(1)}, u32[]{:S(2)}, u32[]{:S(2)}) collective-permute-start(bf16[256,256]{1,0:T(8,128)(2,1)S(1)} %collective-permute-done.3.over_y.refs_4_), channel_id=1, source_target_pairs={{0,1},{1,0},{2,3},{3,2},{4,5},{5,4},{6,7},{7,6},{8,9},{9,8},{10,11... | collective-permute-start | bytes 393224 | tf_op jit(solution)/shard_map/ppermute | solution.py:491
  18.5 0.0 collective-permute-start.10
  18.5 0.9 %over.1 = (f32[2,256,512]{2,1,0:T(8,128)S(1)}, bf16[2,512,256]{2,1,0:T(8,128)(2,1)S(1)}, f32[2,256,256]{2,1,0:T(8,128)S(1)}) custom-call(f32[2,256,256]{2,1,0:T(8,128)S(1)} %get-tuple-element.51.patch_ref.refs_1_, bf16[256,256]{1,0:T(8,128)(2,1)S(1)} %collective-permute-done.3.over_y.refs_4_, bf16[256,256]{1,0:T(8,128)(2,1)S(1)} %collective-permute-done.4.over_x.refs_5_, ...), custom_call_target="tpu_custom_call" | custom-call | tf_op jit(solution)/shard_map/over/pallas_call | solution.py:561
  19.4 0.3 collective-permute-done.9.refs_7_
  19.7 0.2 collective-permute-done.10.refs_8_
  19.9 4.7 %back.1 = (bf16[272,256]{1,0:T(8,128)(2,1)S(1)}, bf16[272,256]{1,0:T(8,128)(2,1)S(1)}, bf16[272,256]{1,0:T(8,128)(2,1)S(1)}, bf16[272,128]{1,0:T(8,128)(2,1)S(1)...) custom-call(bf16[16,256]{1,0:T(8,128)(2,1)S(1)} %live.1.record_ref, ...), custom_call_target="tpu_custom_call" | custom-call | tf_op jit(solution)/shard_map/back/pallas_call | solution.py:571
  24.6 0.9 %collective-permute-start.14 = (bf16[272,256]{1,0:T(8,128)(2,1)S(1)}, bf16[272,256]{1,0:T(8,128)(2,1)S(1)}, u32[]{:S(2)}, u32[]{:S(2)}) collective-permute-start(bf16[272,256]{1,0:T(8,128)(2,1)S(1)} %get-tuple-element.63), channel_id=1, source_target_pairs={{0,8},{1,0},{2,10},{3,2},{4,12},{5,4},{6,14},{7,6},{8,16},{9,1},{1... | collective-permute-start | bytes 417800 | tf_op jit(solution)/shard_map/ppermute | solution.py:603
  25.5 3.2 %collective-permute-start.12 = (bf16[272,128]{1,0:T(8,128)(2,1)S(1)}, bf16[272,128]{1,0:T(8,128)(2,1)S(1)}, u32[]{:S(2)}, u32[]{:S(2)}) collective-permute-start(bf16[272,128]{1,0:T(8,128)(2,1)S(1)} %get-tuple-element.61), channel_id=1, source_target_pairs={{0,12},{1,4},{2,14},{3,6},{4,8},{5,0},{6,10},{7,2},{8,20},{9,5},{1... | collective-permute-start | bytes 208904 | tf_op jit(solution)/shard_map/ppermute | solution.py:601
  28.7 0.3 collective-permute-start.16
  29.0 2.2 %collective-permute-done.12.refs_1_ = bf16[272,128]{1,0:T(8,128)(2,1)S(1)} collective-permute-done((bf16[272,128]{1,0:T(8,128)(2,1)S(1)}, bf16[272,128]{1,0:T(8,128)(2,1)S(1)}, u32[]{:S(2)}, u32[]{:S(2)}) %collective-permute-start.12) | collective-permute-done | bytes 69664 | tf_op jit(solution)/shard_map/ppermute | solution.py:601
  31.2 2.7 %collective-permute-done.13.refs_2_ = bf16[272,128]{1,0:T(8,128)(2,1)S(1)} collective-permute-done((bf16[272,128]{1,0:T(8,128)(2,1)S(1)}, bf16[272,128]{1,0:T(8,128)(2,1)S(1)}, u32[]{:S(2)}, u32[]{:S(2)}) %collective-permute-start.13) | collective-permute-done | bytes 69664 | tf_op jit(solution)/shard_map/ppermute | solution.py:601
  33.9 0.1 sums.1.own_ref
  34.1 0.1 collective-permute-start.17
  34.1 0.7 %weights.1.weight_ref = f32[128,256]{1,0:T(8,128)S(1)} custom-call(bf16[256,256]{1,0:T(8,128)(2,1)S(1)} %get-tuple-element.66.weight_ref, bf16[272,256]{1,0:T(8,128)(2,1)S(1)} %get-tuple-element.60.refs_0_, bf16[272,128]{1,0:T(8,128)(2,1)S(1)} %collective-permute-done.12.refs_1_, bf16[272,128]{1,0:T(8,128)(2,1)S(1)} %collective-permute-done.13.refs_2_, ...), custom_call_target="tpu_custom_call" | custom-call | tf_op jit(solution)/shard_map/weights/pallas_call | solution.py:614
  34.9 0.6 %collective-permute-done.17.other_ref = bf16[2,128,256]{2,1,0:T(8,128)(2,1)S(1)} collective-permute-done((bf16[2,128,256]{2,1,0:T(8,128)(2,1)S(1)}, bf16[2,128,256]{2,1,0:T(8,128)(2,1)S(1)}, u32[]{:S(2)}, u32[]{:S(2)}) %collective-permute-start.17) | collective-permute-done | bytes 131104 | tf_op jit(solution)/shard_map/ppermute | solution.py:491
  35.5 0.8 %update.1 = f32[2,128,256]{2,1,0:T(8,128)} custom-call(f32[2,128,256]{2,1,0:T(8,128)S(1)} %copy-done, bf16[2,128,256]{2,1,0:T(8,128)(2,1)S(1)} %sums.1.own_ref, bf16[2,128,256]{2,1,0:T(8,128)(2,1)S(1)} %collective-permute-done.17.other_ref, f32[128,256]{1,0:T(8,128)S(1)} %weights.1.weight_ref), custom_call_target="tpu_custom_call" | custom-call | tf_op jit(solution)/shard_map/update/pallas_call | solution.py:623
  (16 shorter events, 0.0 us)
Async XLA Ops:
  1.6 4.6 %collective-permute-start.1 = (bf16[2,2,256,256]{3,2,1,0:T(8,128)(2,1)S(1)}, bf16[2,2,256,256]{3,2,1,0:T(8,128)(2,1)S(1)}, u32[]{:S(2)}, u32[]{:S(2)}) collective-permute-start(bf16[2,2,256,256]{3,2,1,0:T(8,128)(2,1)S(1)} %get-tuple-element.38.refs_6_.refs_2_), channel_id=1, source_target_pairs={{0,1},{1,0},{2,3},{3,2},{4,5},{5,4},{6,7},{7,6},{8,9},{9,8},{10,11... | collective-permute-start | bytes 1572872 | tf_op jit(solution)/shard_map/ppermute | solution.py:491
  2.2 9.1 %collective-permute-start = (bf16[2,128,256]{2,1,0:T(8,128)(2,1)S(1)}, bf16[2,128,256]{2,1,0:T(8,128)(2,1)S(1)}, u32[]{:S(2)}, u32[]{:S(2)}) collective-permute-start(bf16[2,128,256]{2,1,0:T(8,128)(2,1)S(1)} %get-tuple-element.36.refs_0_), channel_id=1, source_target_pairs={{0,8},{1,0},{2,10},{3,2},{4,12},{5,4},{6,14},{7,6},{8,16},{9,1},{1... | collective-permute-start | bytes 393224 | tf_op jit(solution)/shard_map/ppermute | solution.py:523
  4.8 6.5 %collective-permute-start.3 = (bf16[256,256]{1,0:T(8,128)(2,1)S(1)}, bf16[256,256]{1,0:T(8,128)(2,1)S(1)}, u32[]{:S(2)}, u32[]{:S(2)}) collective-permute-start(bf16[256,256]{1,0:T(8,128)(2,1)S(1)} %get-tuple-element.43), channel_id=1, source_target_pairs={{0,2},{1,3},{2,0},{3,1},{4,6},{5,7},{6,4},{7,5},{8,10},{9,11},{10,... | collective-permute-start | bytes 393224 | tf_op jit(solution)/shard_map/ppermute | solution.py:491
  6.3 11.7 %collective-permute-start.5 = (bf16[2,1,256,256]{3,2,1,0:T(8,128)(2,1)S(1)}, bf16[2,1,256,256]{3,2,1,0:T(8,128)(2,1)S(1)}, u32[]{:S(2)}, u32[]{:S(2)}) collective-permute-start(bf16[2,1,256,256]{3,2,1,0:T(8,128)(2,1)S(1)} %get-tuple-element.44), channel_id=1, source_target_pairs={{0,2},{1,3},{2,0},{3,1},{4,6},{5,7},{6,4},{7,5},{8,10},{9,11},{10,... | collective-permute-start | bytes 786440 | tf_op jit(solution)/shard_map/ppermute | solution.py:491
  6.8 4.5 %collective-permute-start.2 = (bf16[2,128,128]{2,1,0:T(8,128)(2,1)S(1)}, bf16[2,128,128]{2,1,0:T(8,128)(2,1)S(1)}, u32[]{:S(2)}, u32[]{:S(2)}) collective-permute-start(bf16[2,128,128]{2,1,0:T(8,128)(2,1)S(1)} %get-tuple-element.41), channel_id=1, source_target_pairs={{0,4},{4,0},{1,5},{5,1},{2,6},{6,2},{3,7},{7,3},{8,12},{12,8},{9,1... | collective-permute-start | bytes 196616 | tf_op jit(solution)/shard_map/ppermute | solution.py:525
  8.3 5.6 %collective-permute-start.6 = (bf16[2,128,128]{2,1,0:T(8,128)(2,1)S(1)}, bf16[2,128,128]{2,1,0:T(8,128)(2,1)S(1)}, u32[]{:S(2)}, u32[]{:S(2)}) collective-permute-start(bf16[2,128,128]{2,1,0:T(8,128)(2,1)S(1)} %get-tuple-element.41), channel_id=1, source_target_pairs={{0,12},{1,4},{2,14},{3,6},{4,8},{5,0},{6,10},{7,2},{8,20},{9,5},{1... | collective-permute-start | bytes 196616 | tf_op jit(solution)/shard_map/ppermute | solution.py:524
  11.3 3.8 %collective-permute-start.8 = (bf16[2,128,256]{2,1,0:T(8,128)(2,1)S(1)}, bf16[2,128,256]{2,1,0:T(8,128)(2,1)S(1)}, u32[]{:S(2)}, u32[]{:S(2)}) collective-permute-start(bf16[2,128,256]{2,1,0:T(8,128)(2,1)S(1)} %collective-permute-done.refs_3_), channel_id=1, source_target_pairs={{0,1},{1,0},{2,3},{3,2},{4,5},{5,4},{6,7},{7,6},{8,9},{9,8},{10,11... | collective-permute-start | bytes 393224 | tf_op jit(solution)/shard_map/ppermute | solution.py:491
  11.3 6.6 %collective-permute-start.4 = (bf16[256,256]{1,0:T(8,128)(2,1)S(1)}, bf16[256,256]{1,0:T(8,128)(2,1)S(1)}, u32[]{:S(2)}, u32[]{:S(2)}) collective-permute-start(bf16[256,256]{1,0:T(8,128)(2,1)S(1)} %collective-permute-done.3.over_y.refs_4_), channel_id=1, source_target_pairs={{0,4},{4,0},{1,5},{5,1},{2,6},{6,2},{3,7},{7,3},{8,12},{12,8},{9,1... | collective-permute-start | bytes 393224 | tf_op jit(solution)/shard_map/ppermute | solution.py:521
  13.9 1.3 %collective-permute-start.7 = (bf16[2,128,128]{2,1,0:T(8,128)(2,1)S(1)}, bf16[2,128,128]{2,1,0:T(8,128)(2,1)S(1)}, u32[]{:S(2)}, u32[]{:S(2)}) collective-permute-start(bf16[2,128,128]{2,1,0:T(8,128)(2,1)S(1)} %collective-permute-done.6.refs_1_), channel_id=1, source_target_pairs={{0,1},{1,0},{2,3},{3,2},{4,5},{5,4},{6,7},{7,6},{8,9},{9,8},{10,11... | collective-permute-start | bytes 196616 | tf_op jit(solution)/shard_map/ppermute | solution.py:491
  15.1 4.8 %copy-start.1 = (bf16[1,1,2,256,256]{4,3,2,1,0:T(8,128)(2,1)S(1)}, bf16[1,1,2,256,256]{4,3,2,1,0:T(8,128)(2,1)}, u32[]{:S(2)}) copy-start(bf16[1,1,2,256,256]{4,3,2,1,0:T(8,128)(2,1)} %refs_0_.1) | copy-start | bytes 786436
  18.0 1.9 %collective-permute-start.11 = (bf16[2,1,256,256]{3,2,1,0:T(8,128)(2,1)S(1)}, bf16[2,1,256,256]{3,2,1,0:T(8,128)(2,1)S(1)}, u32[]{:S(2)}, u32[]{:S(2)}) collective-permute-start(bf16[2,1,256,256]{3,2,1,0:T(8,128)(2,1)S(1)} %collective-permute-done.5.rest.refs_6_), channel_id=1, source_target_pairs={{0,1},{1,0},{2,3},{3,2},{4,5},{5,4},{6,7},{7,6},{8,9},{9,8},{10,11... | collective-permute-start | bytes 786440 | tf_op jit(solution)/shard_map/ppermute | solution.py:491
  18.0 1.7 %collective-permute-start.9 = (bf16[256,256]{1,0:T(8,128)(2,1)S(1)}, bf16[256,256]{1,0:T(8,128)(2,1)S(1)}, u32[]{:S(2)}, u32[]{:S(2)}) collective-permute-start(bf16[256,256]{1,0:T(8,128)(2,1)S(1)} %collective-permute-done.3.over_y.refs_4_), channel_id=1, source_target_pairs={{0,1},{1,0},{2,3},{3,2},{4,5},{5,4},{6,7},{7,6},{8,9},{9,8},{10,11... | collective-permute-start | bytes 393224 | tf_op jit(solution)/shard_map/ppermute | solution.py:491
  18.5 1.4 %collective-permute-start.10 = (bf16[256,256]{1,0:T(8,128)(2,1)S(1)}, bf16[256,256]{1,0:T(8,128)(2,1)S(1)}, u32[]{:S(2)}, u32[]{:S(2)}) collective-permute-start(bf16[256,256]{1,0:T(8,128)(2,1)S(1)} %collective-permute-done.4.over_x.refs_5_), channel_id=1, source_target_pairs={{0,1},{1,0},{2,3},{3,2},{4,5},{5,4},{6,7},{7,6},{8,9},{9,8},{10,11... | collective-permute-start | bytes 393224 | tf_op jit(solution)/shard_map/ppermute | solution.py:491
  19.9 15.6 %copy-start = (f32[2,128,256]{2,1,0:T(8,128)S(1)}, f32[2,128,256]{2,1,0:T(8,128)}, u32[]{:S(2)}) copy-start(f32[2,128,256]{2,1,0:T(8,128)} %object_ref.1) | copy-start | bytes 786436
  24.6 9.3 %collective-permute-start.14 = (bf16[272,256]{1,0:T(8,128)(2,1)S(1)}, bf16[272,256]{1,0:T(8,128)(2,1)S(1)}, u32[]{:S(2)}, u32[]{:S(2)}) collective-permute-start(bf16[272,256]{1,0:T(8,128)(2,1)S(1)} %get-tuple-element.63), channel_id=1, source_target_pairs={{0,8},{1,0},{2,10},{3,2},{4,12},{5,4},{6,14},{7,6},{8,16},{9,1},{1... | collective-permute-start | bytes 417800 | tf_op jit(solution)/shard_map/ppermute | solution.py:603
  25.5 8.4 %collective-permute-start.15 = (bf16[272,256]{1,0:T(8,128)(2,1)S(1)}, bf16[272,256]{1,0:T(8,128)(2,1)S(1)}, u32[]{:S(2)}, u32[]{:S(2)}) collective-permute-start(bf16[272,256]{1,0:T(8,128)(2,1)S(1)} %get-tuple-element.64), channel_id=1, source_target_pairs={{0,1},{1,9},{2,3},{3,11},{4,5},{5,13},{6,7},{7,15},{8,0},{9,17},{1... | collective-permute-start | bytes 417800 | tf_op jit(solution)/shard_map/ppermute | solution.py:603
  25.5 5.7 %collective-permute-start.12 = (bf16[272,128]{1,0:T(8,128)(2,1)S(1)}, bf16[272,128]{1,0:T(8,128)(2,1)S(1)}, u32[]{:S(2)}, u32[]{:S(2)}) collective-permute-start(bf16[272,128]{1,0:T(8,128)(2,1)S(1)} %get-tuple-element.61), channel_id=1, source_target_pairs={{0,12},{1,4},{2,14},{3,6},{4,8},{5,0},{6,10},{7,2},{8,20},{9,5},{1... | collective-permute-start | bytes 208904 | tf_op jit(solution)/shard_map/ppermute | solution.py:601
  28.7 5.2 %collective-permute-start.13 = (bf16[272,128]{1,0:T(8,128)(2,1)S(1)}, bf16[272,128]{1,0:T(8,128)(2,1)S(1)}, u32[]{:S(2)}, u32[]{:S(2)}) collective-permute-start(bf16[272,128]{1,0:T(8,128)(2,1)S(1)} %get-tuple-element.62), channel_id=1, source_target_pairs={{0,5},{1,13},{2,7},{3,15},{4,1},{5,9},{6,3},{7,11},{8,4},{9,21},{1... | collective-permute-start | bytes 208904 | tf_op jit(solution)/shard_map/ppermute | solution.py:601
  28.7 5.2 %collective-permute-start.16 = (bf16[272,128]{1,0:T(8,128)(2,1)S(1)}, bf16[272,128]{1,0:T(8,128)(2,1)S(1)}, u32[]{:S(2)}, u32[]{:S(2)}) collective-permute-start(bf16[272,128]{1,0:T(8,128)(2,1)S(1)} %get-tuple-element.65), channel_id=1, source_target_pairs={{0,4},{4,0},{1,5},{5,1},{2,6},{6,2},{3,7},{7,3},{8,12},{12,8},{9,1... | collective-permute-start | bytes 208904 | tf_op jit(solution)/shard_map/ppermute | solution.py:605
  34.1 1.4 %collective-permute-start.17 = (bf16[2,128,256]{2,1,0:T(8,128)(2,1)S(1)}, bf16[2,128,256]{2,1,0:T(8,128)(2,1)S(1)}, u32[]{:S(2)}, u32[]{:S(2)}) collective-permute-start(bf16[2,128,256]{2,1,0:T(8,128)(2,1)S(1)} %sums.1.own_ref), channel_id=1, source_target_pairs={{0,1},{1,0},{2,3},{3,2},{4,5},{5,4},{6,7},{7,6},{8,9},{9,8},{10,11... | collective-permute-start | bytes 393224 | tf_op jit(solution)/shard_map/ppermute | solution.py:491

commit v9 on v8

--- a/solution.py
+++ b/solution.py
@@ -145,17 +145,16 @@
     out_ref[...] = record.astype(jnp.bfloat16)
 
 
-def positions(record_ref, slots):
-    _, _, parity = here()
-    record = record_ref[:, :128].astype(jnp.float32).astype(jnp.int32)[:, :1]
+def position_of(record, slots, wanted):
+    record = record[:, :128].astype(jnp.float32).astype(jnp.int32)[:, :1]
 
     def of_slot(axis):
         value = record[axis : axis + 1]
         for slot in range(1, slots):
-            value = jnp.where(parity == slot, record[2 * slot + axis : 2 * slot + axis + 1], value)
+            value = jnp.where(wanted == slot, record[2 * slot + axis : 2 * slot + axis + 1], value)
         return value
 
-    return of_slot(0), of_slot(1), record[2 * slots : 2 * slots + 1] > parity
+    return of_slot(0), of_slot(1), record[2 * slots : 2 * slots + 1] > wanted
 
 
 def row_starts(half, tile_rows, parity):
@@ -168,7 +167,7 @@
 
 def patch_of(sides, slots, z_count, x_count, side, record_ref, pieces, ext_ref):
     z_index, x_index, parity = here()
-    row_at, col_at, _ = positions(record_ref, slots)
+    row_at, col_at, _ = position_of(record_ref, slots, parity)
     half = side // 2
     _, tile_rows, tile_cols = pieces[0].shape
     ext_rows = tile_rows + side
@@ -289,28 +288,28 @@
 
 
 def back_kernel(sides, slots, x_count, tile_rows, tile_cols, record_ref, *refs):
-    n_pieces = 3 + 3 * sides
     amplitude_ref, patch_ref, own, core = refs[:4]
     over_modes = [shared_mode(*refs[4:6])] + modes_of(refs[6])
     last_modes = [shared_mode(*refs[7:9])] + modes_of(refs[9])
     direct_ref, swapped_ref = refs[10:12]
     near_far, near_exit, near_sum, over_far, over_exit, over_sum = refs[12:18]
-    outs = refs[18 : 18 + n_pieces + 1]
-    last_far, last_exit, grad_ref = refs[18 + n_pieces + 1 :]
+    weight_out, own_out, keep_out, swap_out = refs[18:22]
+    side_outs = refs[22 : 22 + sides]
+    last_far, last_exit, grad_ref = refs[22 + sides :]
     side = own.shape[2]
     half = side // 2
     modes = own.shape[1]
     ext_rows = tile_rows + side
     ext_cols = tile_cols + sides * half
     _, x_index, parity = here()
-    row_at, col_at, is_live = positions(record_ref, slots)
+    row_at, col_at, is_live = position_of(record_ref, slots, parity)
     direct = direct_ref[...]
     swapped = swapped_ref[...]
     patch = (patch_ref[0], patch_ref[1])
     power, weight = forward(last_modes, patch, direct, swapped, last_far, last_exit, 0)
     power = near_sum[0] + (over_sum[0] + power)
     weight = near_sum[1] + (over_sum[1] + weight)
-    outs[-1][...] = weight.astype(jnp.bfloat16)
+    weight_out[...] = weight.astype(jnp.bfloat16)
     amplitude = amplitude_ref[0, 0, parity].astype(jnp.float32)
     factor = amplitude / jnp.sqrt(power + power_floor)
     factor = jnp.concatenate([factor, factor], axis=1)
@@ -333,104 +332,99 @@
         placed = dot(put_rows, gradient.astype(jnp.bfloat16)).astype(jnp.bfloat16)
         grad_ref[...] = dot(placed, put_cols).astype(jnp.bfloat16)
         rows = slice(channel * half, (channel + 1) * half)
-        for index in range(1 + sides):
-            columns = (
-                slice(0, tile_cols)
-                if index == 0
-                else slice(tile_cols + (index - 1) * half, tile_cols + index * half)
-            )
-            outs[3 * index][rows] = grad_ref[half : half + tile_rows, columns]
-            outs[3 * index + 1][rows] = grad_ref[pl.ds(b_at, half), columns]
-            outs[3 * index + 2][rows] = grad_ref[pl.ds(a_at, half), columns]
-    for out in outs[:n_pieces]:
-        out[2 * half :] = record_ref[:, : out.shape[1]]
-
-
-def weight_kernel(sides, slots, z_count, x_count, weight_ref, *refs):
-    pieces, out_ref = from_sent_order(refs[:-1]), refs[-1]
-    tile_rows, tile_cols = out_ref.shape
+        own_out[rows] = grad_ref[half : half + tile_rows, :tile_cols]
+        keep_out[rows] = grad_ref[pl.ds(b_at, half), :]
+        swap_out[rows] = grad_ref[pl.ds(a_at, half), :]
+        for index, out in enumerate(side_outs):
+            columns = slice(tile_cols + index * half, tile_cols + (index + 1) * half)
+            out[rows] = grad_ref[half : half + tile_rows, columns]
+    for out in side_outs:
+        out[2 * half :] = record_ref[:, :half]
+
+
+def meet_kernel(record_ref, keep_ref, swap_ref, rows_out, *corner_outs):
+    total = keep_ref[...].astype(jnp.float32) + swap_ref[...].astype(jnp.float32)
+    total = total.astype(jnp.bfloat16)
+    height = total.shape[0]
+    tile_cols = rows_out.shape[1]
+    rows_out[:height] = total[:, :tile_cols]
+    rows_out[height:] = record_ref[...]
+    for index, out in enumerate(corner_outs):
+        half = out.shape[1]
+        out[:height] = total[:, tile_cols + index * half : tile_cols + (index + 1) * half]
+        out[height:] = record_ref[:, :half]
+
+
+def sum_kernel(sides, slots, z_count, x_count, weight_ref, record_ref, own_ref, rows_ref, *refs):
+    corners, levels, out_ref = refs[:sides], refs[sides:-1], refs[-1]
+    _, tile_rows, tile_cols = out_ref.shape
     side = weight_ref.shape[0]
     half = side // 2
     z_index, x_index, parity = here()
-    z_step_a = jnp.where(parity == 0, -1, 1)
+    z_step = jnp.where(parity == 0, -1, 1)
+    z_shown = jnp.where(parity == 0, z_index > 0, z_index < z_count - 1)
     if sides == 1:
-        x_steps = [0, jnp.where(x_index == 0, 1, -1)]
-        x_shown = [True, True]
+        x_steps = [jnp.where(x_index == 0, 1, -1)]
+        x_shown = [z_index >= 0]
     else:
-        x_steps = [0, 1, -1]
-        x_shown = [True, x_index < x_count - 1, x_index > 0]
+        x_steps = [1, -1]
+        x_shown = [x_index < x_count - 1, x_index > 0]
     weight = weight_ref[...]
-    total = jnp.zeros((tile_rows, tile_cols), jnp.float32)
-    for index, x_step in enumerate(x_steps):
-        turns = []
-        for turn, z_step in enumerate((0, z_step_a, -z_step_a)):
-            part = jnp.zeros((tile_rows, tile_cols), jnp.float32)
-            z_tile = z_index + z_step
-            shown = (z_tile >= 0) & (z_tile < z_count) & x_shown[index]
-            record = pieces[3 * index + turn][2 * half :].astype(jnp.float32)
-            record = record.astype(jnp.int32)
-            if record.shape[1] < side:
-                record = jnp.concatenate([record] * (side // record.shape[1]), axis=1)
-            count = record[2 * slots : 2 * slots + 1, :side]
-            for slot in range(slots):
-                row = record[2 * slot : 2 * slot + 1, :side] + (z_step * tile_rows - half)
-                col = record[2 * slot + 1 : 2 * slot + 2, :side] + (x_step * tile_cols - half)
-                row = jnp.where((count > slot) & shown, row, nowhere)
-                put_rows = (
-                    iota((tile_rows, side), 0) == iota((tile_rows, side), 1) + row
-                ).astype(jnp.bfloat16)
-                put_cols = (
-                    iota((side, tile_cols), 1) == iota((side, tile_cols), 0) + col[:, :1]
-                ).astype(jnp.bfloat16)
-                placed = dot(put_rows, weight).astype(jnp.bfloat16)
-                part = part + dot(placed, put_cols)
-            turns.append(part)
-        total = total + (turns[0] + (turns[1] + turns[2]))
-    out_ref[...] = total + regularizer
-
-
-def sum_kernel(sides, z_count, x_count, *refs):
-    pieces, out_ref = from_sent_order(refs[:-1]), refs[-1]
-    own_ref, rows_a, rows_b = pieces[:3]
-    _, tile_rows, tile_cols = out_ref.shape
-    half = pieces[3].shape[1]
-    z_index, x_index, parity = here()
-    below = z_index > 0
-    above = z_index < z_count - 1
-    a_on = jnp.where(parity == 0, below, above)
-    b_on = jnp.where(parity == 0, above, below)
+
+    def placed(position, z_step, x_step, shown):
+        row, col, is_live = position
+        row = jnp.where(is_live & shown, row + (z_step * tile_rows - half), nowhere)
+        col = col + (x_step * tile_cols - half)
+        put_rows = (iota((tile_rows, side), 0) == iota((tile_rows, side), 1) + row).astype(
+            jnp.bfloat16
+        )
+        put_cols = (iota((side, tile_cols), 1) == iota((side, tile_cols), 0) + col).astype(
+            jnp.bfloat16
+        )
+        return dot(dot(put_rows, weight).astype(jnp.bfloat16), put_cols)
+
+    total = placed(position_of(record_ref, slots, parity), 0, 0, z_index >= 0)
+    for level, x_step, shown in zip(levels, x_steps, x_shown):
+        record = level[2 * half :]
+        total = total + placed(position_of(record, slots, parity), 0, x_step, shown)
+    for piece, x_step, shown in zip(
+        (rows_ref,) + corners, [0] + x_steps, [z_index >= 0] + x_shown
+    ):
+        record = piece[2 * half :]
+        for slot in range(slots):
+            position = position_of(record, slots, slot)
+            total = total + placed(position, z_step, x_step, shown & z_shown)
+    out_ref[2] = total.astype(jnp.bfloat16)
 
     for channel in range(2):
         rows = slice(channel * tile_rows, (channel + 1) * tile_rows)
 
-        def gate(on, ref, rows=rows):
-            return jnp.where(on, ref[rows].astype(jnp.float32), 0.0)
-
-        total = own_ref[rows].astype(jnp.float32)
-        total = total + gate(a_on, rows_a) + gate(b_on, rows_b)
+        def values(ref, rows=rows):
+            return ref[rows].astype(jnp.float32)
+
+        total = values(own_ref) + jnp.where(z_shown, values(rows_ref), 0.0)
         first = jnp.zeros((tile_rows, half), jnp.float32)
         last = first
         for index in range(sides):
-            level, corner_a, corner_b = pieces[3 + 3 * index : 6 + 3 * index]
-            edge = level[rows].astype(jnp.float32)
-            edge = edge + gate(a_on, corner_a) + gate(b_on, corner_b)
+            edge = values(levels[index]) + jnp.where(z_shown, values(corners[index]), 0.0)
             if sides == 1:
                 first = jnp.where(x_index == 1, edge, 0.0)
                 last = jnp.where(x_index == 0, edge, 0.0)
             elif index == 0:
-                last = jnp.where(x_index < x_count - 1, edge, 0.0)
+                last = jnp.where(x_shown[0], edge, 0.0)
             else:
-                first = jnp.where(x_index > 0, edge, 0.0)
+                first = jnp.where(x_shown[1], edge, 0.0)
         zero = jnp.zeros((tile_rows, tile_cols - 2 * half), jnp.float32)
         parts = [first, zero, last] if tile_cols > 2 * half else [first, last]
         total = total + jnp.concatenate(parts, axis=1)
         out_ref[channel] = total.astype(jnp.bfloat16)
 
 
-def update_kernel(object_ref, own_ref, other_ref, weight_ref, out_ref):
+def update_kernel(object_ref, own_ref, other_ref, out_ref):
+    weight = own_ref[2].astype(jnp.float32) + other_ref[2].astype(jnp.float32) + regularizer
     for channel in range(2):
         gradient = own_ref[channel].astype(jnp.float32) + other_ref[channel].astype(jnp.float32)
-        out_ref[channel] = object_ref[channel] + gradient / weight_ref[...]
+        out_ref[channel] = object_ref[channel] + gradient / weight
 
 
 def in_hbm(array):
@@ -463,10 +457,9 @@
     sides = 1 if x_count == 2 else 2
     axes = ("tx", "ty", "mode")
 
-    def zigzag(x_step, flip=False):
+    def zigzag(x_step):
         def moved(z, m):
-            down = (m % 2 == 0) != flip
-            if down:
+            if m % 2 == 0:
                 return (z + 1, m) if z < z_count - 1 else (z, m ^ 1)
             return (z - 1, m) if z > 0 else (z, m ^ 1)
 
@@ -566,14 +559,14 @@
         compiler_params=pltpu.CompilerParams(vmem_limit_bytes=wave_bytes),
         name="over",
     )(patch, *over_group, direct, swapped)
-    shapes = [(2 * half + record_rows, tile_cols)] * 3
-    shapes += [(2 * half + record_rows, half)] * (3 * sides)
-    results = pl.pallas_call(
+    piece_rows = 2 * half + record_rows
+    shapes = [(side, side), (2 * half, tile_cols)] + [(2 * half, ext_cols)] * 2
+    shapes += [(piece_rows, half)] * sides
+    weight, own, keep, swap, *levels = pl.pallas_call(
         functools.partial(back_kernel, sides, slots, x_count, tile_rows, tile_cols),
-        out_shape=[jax.ShapeDtypeStruct(shape, jnp.bfloat16) for shape in shapes]
-        + [jax.ShapeDtypeStruct((side, side), jnp.bfloat16)],
+        out_shape=[jax.ShapeDtypeStruct(shape, jnp.bfloat16) for shape in shapes],
         in_specs=[vmem()] * 19,
-        out_specs=[vmem()] * (n_pieces + 1),
+        out_specs=[vmem()] * (4 + sides),
         scratch_shapes=[
             pltpu.VMEM((modes, side, 2 * side), jnp.float32),
             pltpu.VMEM((modes, 2 * side, side), jnp.bfloat16),
@@ -594,40 +587,36 @@
         *near,
         *over,
     )
-    received = [results[0]] + [None] * (n_pieces - 1)
-    for index, step in enumerate(x_steps):
-        at = 3 + 3 * index
-        for turn, flip in enumerate((False, True)):
-            received[at + 1 + turn] = lax.ppermute(results[at + 1 + turn], axes, zigzag(-step, flip))
-    for turn, flip in enumerate((False, True)):
-        received[1 + turn] = lax.ppermute(results[1 + turn], axes, zigzag(0, flip))
-    for index, step in enumerate(x_steps):
-        received[3 + 3 * index] = lax.ppermute(results[3 + 3 * index], "ty", level(-step))
+    levels = [lax.ppermute(piece, "ty", level(-step)) for piece, step in zip(levels, x_steps)]
+    rows, *corners = pl.pallas_call(
+        meet_kernel,
+        out_shape=[jax.ShapeDtypeStruct((piece_rows, tile_cols), jnp.bfloat16)]
+        + [jax.ShapeDtypeStruct((piece_rows, half), jnp.bfloat16)] * sides,
+        in_specs=[vmem()] * 3,
+        out_specs=[vmem()] * (1 + sides),
+        compiler_params=pltpu.CompilerParams(vmem_limit_bytes=small_bytes),
+        name="meet",
+    )(record, keep, exchange(swap, 1))
+    corners = [
+        lax.ppermute(piece, axes, zigzag(-step)) for piece, step in zip(corners, x_steps)
+    ]
+    rows = lax.ppermute(rows, axes, zigzag(0))
     summed = pl.pallas_call(
-        functools.partial(sum_kernel, sides, z_count, x_count),
-        out_shape=jax.ShapeDtypeStruct(object_field.shape, jnp.bfloat16),
-        in_specs=[vmem()] * n_pieces,
+        functools.partial(sum_kernel, sides, slots, z_count, x_count),
+        out_shape=jax.ShapeDtypeStruct((3, tile_rows, tile_cols), jnp.bfloat16),
+        in_specs=[vmem()] * (4 + 2 * sides),
         out_specs=vmem(),
         compiler_params=pltpu.CompilerParams(vmem_limit_bytes=small_bytes),
         name="sums",
-    )(*in_sent_order(received))
-    weight = pl.pallas_call(
-        functools.partial(weight_kernel, sides, slots, z_count, x_count),
-        out_shape=jax.ShapeDtypeStruct((tile_rows, tile_cols), jnp.float32),
-        in_specs=[vmem()] * (n_pieces + 1),
-        out_specs=vmem(),
-        compiler_params=pltpu.CompilerParams(vmem_limit_bytes=small_bytes),
-        name="weights",
-    )(results[-1], *in_sent_order(received))
-    other = exchange(summed, 1)
+    )(weight, record, own, rows, *corners, *levels)
     return pl.pallas_call(
         update_kernel,
         out_shape=jax.ShapeDtypeStruct(object_field.shape, jnp.float32),
-        in_specs=[vmem()] * 4,
+        in_specs=[vmem()] * 3,
         out_specs=vmem(),
         compiler_params=pltpu.CompilerParams(vmem_limit_bytes=small_bytes),
         name="update",
-    )(object_field, summed, other, weight)
+    )(object_field, summed, exchange(summed, 1))
 
 
 def solution(mesh):

time: 36.4 us -> 36.2 us (level)
    ppermute x9 -> x10, waiting for transfers between devices: 2.19 us -> 4.34 us  [exchange(): return lax.ppermute(array, 'mode', [(m, m ^ flip) for m in range(m_count)])]
    ppermute x5 -> x3, waiting for transfers between devices: 4.93 us -> 3.04 us  [the longest x1 1.61 us: on_device(): lax.ppermute(piece, 'ty', level(-step))]
    ppermute x5 -> x3, starting transfers between devices: 4.39 us -> 3.93 us  [the longest x1 1.75 us: on_device(): lax.ppermute(piece, 'ty', level(-step))]
    ppermute x9 -> x10, starting transfers between devices: 3.29 us -> 3.5 us  [exchange(): return lax.ppermute(array, 'mode', [(m, m ^ flip) for m in range(m_count)])]
  transfers between devices with their start and end apart: 18 -> 17, of which waited for: 8 -> 9; matrix products, arithmetic and copies ran while one was open for 0% -> 0% of each run, Pallas kernels for 11% -> 9%
where the time goes in v9:
time: 36.2 us; the launch traced here: 36 us
  starting transfers between devices  15.6 us (43%)
  Pallas kernels  11 us (30%)
  waiting for transfers between devices  8.64 us (24%)
  between operations  0.73 us (2%)
    pallas_call x1, Pallas kernels, on_device(): pl.pallas_call(functools.partial(back_kernel, sides, slots, x_count, tile...  4.7 us
    ppermute x10, waiting for transfers between devices, exchange(): return lax.ppermute(array, 'mode', [(m, m ^ flip) for m in range(m_count)])  4.34 us
    ppermute x10, starting transfers between devices, exchange(): return lax.ppermute(array, 'mode', [(m, m ^ flip) for m in range(m_count)])  3.5 us
    ppermute x1, starting transfers between devices, on_device(): rows = lax.ppermute(packed[0], axes, zigzag(0))  2.6 us
    ppermute x1, starting transfers between devices, on_device(): over_x = lax.ppermute(over_y, 'ty', [(x, x ^ 1) for x in range(x_count)])  2.55 us
    pallas_call x1, Pallas kernels, on_device(): pl.pallas_call(functools.partial(near_kernel, sides, slots, z_count, x_co...  2.38 us
    ppermute x1, starting transfers between devices, on_device(): lax.ppermute(piece, 'ty', level(-step))  1.75 us
    pallas_call x1, Pallas kernels, on_device(): pl.pallas_call(functools.partial(start_kernel, sides, slots), out_shape=[...  1.64 us
  transfers between devices with their start and end apart: 17, of which 9 were waited for; matrix products, arithmetic and copies ran while one was open for 0% of the time, Pallas kernels for 9%

profile of v9, /device:TPU:0, one launch (start us, length us, event | category | flops | bytes accessed | tf_op | source)
XLA Modules:
  0.0 36.0 jit_solution(5407808567119093450)
XLA Ops:
  0.0 1.6 %start.1 = (bf16[2,2,256,256]{3,2,1,0:T(8,128)(2,1)S(1)}, bf16[256,256]{1,0:T(8,128)(2,1)S(1)}, bf16[2,1,256,256]{3,2,1,0:T(8,128)(2,1)S(1)}, bf16[16,256]{1,0:T...) custom-call(f32[2,128,256]{2,1,0:T(8,128)} %object_ref.1, ...), custom_call_target="tpu_custom_call" | custom-call | tf_op jit(solution)/shard_map/start/pallas_call | solution.py:487
  1.6 0.5 %collective-permute-start.1 = (bf16[2,2,256,256]{3,2,1,0:T(8,128)(2,1)S(1)}, bf16[2,2,256,256]{3,2,1,0:T(8,128)(2,1)S(1)}, u32[]{:S(2)}, u32[]{:S(2)}) collective-permute-start(bf16[2,2,256,256]{3,2,1,0:T(8,128)(2,1)S(1)} %get-tuple-element.38.refs_6_.refs_2_), channel_id=1, source_target_pairs={{0,1},{1,0},{2,3},{3,2},{4,5},{5,4},{6,7},{7,6},{8,9},{9,8},{10,11... | collective-permute-start | bytes 1572872 | tf_op jit(solution)/shard_map/ppermute | solution.py:484
  2.2 2.6 %collective-permute-start = (bf16[2,128,256]{2,1,0:T(8,128)(2,1)S(1)}, bf16[2,128,256]{2,1,0:T(8,128)(2,1)S(1)}, u32[]{:S(2)}, u32[]{:S(2)}) collective-permute-start(bf16[2,128,256]{2,1,0:T(8,128)(2,1)S(1)} %get-tuple-element.36.refs_0_), channel_id=1, source_target_pairs={{0,8},{1,0},{2,10},{3,2},{4,12},{5,4},{6,14},{7,6},{8,16},{9,1},{1... | collective-permute-start | bytes 393224 | tf_op jit(solution)/shard_map/ppermute | solution.py:516
  4.8 1.5 %collective-permute-start.3 = (bf16[256,256]{1,0:T(8,128)(2,1)S(1)}, bf16[256,256]{1,0:T(8,128)(2,1)S(1)}, u32[]{:S(2)}, u32[]{:S(2)}) collective-permute-start(bf16[256,256]{1,0:T(8,128)(2,1)S(1)} %get-tuple-element.43), channel_id=1, source_target_pairs={{0,2},{1,3},{2,0},{3,1},{4,6},{5,7},{6,4},{7,5},{8,10},{9,11},{10,... | collective-permute-start | bytes 393224 | tf_op jit(solution)/shard_map/ppermute | solution.py:484
  6.3 0.0 collective-permute-done.1.refs_7_.refs_3_
  6.3 0.5 %collective-permute-start.5 = (bf16[2,1,256,256]{3,2,1,0:T(8,128)(2,1)S(1)}, bf16[2,1,256,256]{3,2,1,0:T(8,128)(2,1)S(1)}, u32[]{:S(2)}, u32[]{:S(2)}) collective-permute-start(bf16[2,1,256,256]{3,2,1,0:T(8,128)(2,1)S(1)} %get-tuple-element.44), channel_id=1, source_target_pairs={{0,2},{1,3},{2,0},{3,1},{4,6},{5,7},{6,4},{7,5},{8,10},{9,11},{10,... | collective-permute-start | bytes 786440 | tf_op jit(solution)/shard_map/ppermute | solution.py:484
  6.8 1.5 %collective-permute-start.2 = (bf16[2,128,128]{2,1,0:T(8,128)(2,1)S(1)}, bf16[2,128,128]{2,1,0:T(8,128)(2,1)S(1)}, u32[]{:S(2)}, u32[]{:S(2)}) collective-permute-start(bf16[2,128,128]{2,1,0:T(8,128)(2,1)S(1)} %get-tuple-element.41), channel_id=1, source_target_pairs={{0,4},{4,0},{1,5},{5,1},{2,6},{6,2},{3,7},{7,3},{8,12},{12,8},{9,1... | collective-permute-start | bytes 196616 | tf_op jit(solution)/shard_map/ppermute | solution.py:518
  8.3 1.5 %collective-permute-start.6 = (bf16[2,128,128]{2,1,0:T(8,128)(2,1)S(1)}, bf16[2,128,128]{2,1,0:T(8,128)(2,1)S(1)}, u32[]{:S(2)}, u32[]{:S(2)}) collective-permute-start(bf16[2,128,128]{2,1,0:T(8,128)(2,1)S(1)} %get-tuple-element.41), channel_id=1, source_target_pairs={{0,12},{1,4},{2,14},{3,6},{4,8},{5,0},{6,10},{7,2},{8,20},{9,5},{1... | collective-permute-start | bytes 196616 | tf_op jit(solution)/shard_map/ppermute | solution.py:517
  10.5 0.8 %collective-permute-done.2.refs_5_ = bf16[2,128,128]{2,1,0:T(8,128)(2,1)S(1)} collective-permute-done((bf16[2,128,128]{2,1,0:T(8,128)(2,1)S(1)}, bf16[2,128,128]{2,1,0:T(8,128)(2,1)S(1)}, u32[]{:S(2)}, u32[]{:S(2)}) %collective-permute-start.2) | collective-permute-done | bytes 65568 | tf_op jit(solution)/shard_map/ppermute | solution.py:518
  11.3 2.5 %collective-permute-start.4 = (bf16[256,256]{1,0:T(8,128)(2,1)S(1)}, bf16[256,256]{1,0:T(8,128)(2,1)S(1)}, u32[]{:S(2)}, u32[]{:S(2)}) collective-permute-start(bf16[256,256]{1,0:T(8,128)(2,1)S(1)} %collective-permute-done.3.over_y.refs_4_), channel_id=1, source_target_pairs={{0,4},{4,0},{1,5},{5,1},{2,6},{6,2},{3,7},{7,3},{8,12},{12,8},{9,1... | collective-permute-start | bytes 393224 | tf_op jit(solution)/shard_map/ppermute | solution.py:514
  13.9 0.2 collective-permute-start.7
  14.0 1.1 %collective-permute-done.7.refs_2_ = bf16[2,128,128]{2,1,0:T(8,128)(2,1)S(1)} collective-permute-done((bf16[2,128,128]{2,1,0:T(8,128)(2,1)S(1)}, bf16[2,128,128]{2,1,0:T(8,128)(2,1)S(1)}, u32[]{:S(2)}, u32[]{:S(2)}) %collective-permute-start.7) | collective-permute-done | bytes 65568 | tf_op jit(solution)/shard_map/ppermute | solution.py:484
  15.1 2.4 %near.1 = (f32[2,256,256]{2,1,0:T(8,128)S(1)}, f32[4,256,512]{2,1,0:T(8,128)S(1)}, bf16[4,512,256]{2,1,0:T(8,128)(2,1)S(1)}, f32[2,256,256]{2,1,0:T(8,128)S(1)}) custom-call(bf16[16,256]{1,0:T(8,128)(2,1)S(1)} %live.1.record_ref, bf16[2,128,256]{2,1,0:T(8,128)(2,1)S(1)} %get-tuple-element.36.refs_0_, ...), custom_call_target="tpu_custom_call" | custom-call | tf_op jit(solution)/shard_map/near/pallas_call | solution.py:542
  17.5 0.5 %collective-permute-done.4.over_x.refs_5_ = bf16[256,256]{1,0:T(8,128)(2,1)S(1)} collective-permute-done((bf16[256,256]{1,0:T(8,128)(2,1)S(1)}, bf16[256,256]{1,0:T(8,128)(2,1)S(1)}, u32[]{:S(2)}, u32[]{:S(2)}) %collective-permute-start.4) | collective-permute-done | bytes 131104 | tf_op jit(solution)/shard_map/ppermute | solution.py:514
  18.0 0.5 %collective-permute-start.9 = (bf16[256,256]{1,0:T(8,128)(2,1)S(1)}, bf16[256,256]{1,0:T(8,128)(2,1)S(1)}, u32[]{:S(2)}, u32[]{:S(2)}) collective-permute-start(bf16[256,256]{1,0:T(8,128)(2,1)S(1)} %collective-permute-done.3.over_y.refs_4_), channel_id=1, source_target_pairs={{0,1},{1,0},{2,3},{3,2},{4,5},{5,4},{6,7},{7,6},{8,9},{9,8},{10,11... | collective-permute-start | bytes 393224 | tf_op jit(solution)/shard_map/ppermute | solution.py:484
  18.5 0.0 collective-permute-start.10
  18.5 0.9 %over.1 = (f32[2,256,512]{2,1,0:T(8,128)S(1)}, bf16[2,512,256]{2,1,0:T(8,128)(2,1)S(1)}, f32[2,256,256]{2,1,0:T(8,128)S(1)}) custom-call(f32[2,256,256]{2,1,0:T(8,128)S(1)} %get-tuple-element.51.patch_ref.refs_1_, bf16[256,256]{1,0:T(8,128)(2,1)S(1)} %collective-permute-done.3.over_y.refs_4_, bf16[256,256]{1,0:T(8,128)(2,1)S(1)} %collective-permute-done.4.over_x.refs_5_, ...), custom_call_target="tpu_custom_call" | custom-call | tf_op jit(solution)/shard_map/over/pallas_call | solution.py:554
  19.4 0.3 collective-permute-done.9.refs_7_
  19.7 0.2 collective-permute-done.10.refs_8_
  19.9 4.7 %back.1 = (bf16[256,256]{1,0:T(8,128)(2,1)S(1)}, bf16[256,256]{1,0:T(8,128)(2,1)S(1)}, bf16[256,384]{1,0:T(8,128)(2,1)S(1)}, bf16[256,384]{1,0:T(8,128)(2,1)S(1)}, bf16[272,128]{1,0:T(8,128)(2,1)S(1)}) custom-call(bf16[16,256]{1,0:T(8,128)(2,1)S(1)} %live.1.record_ref, bf16[1,1,2,256,256]{4,3,2,1,0:T(8,128)(2,1)S(1)} %copy-done.1, ...), custom_call_target="tpu_custom_call" | custom-call | tf_op jit(solution)/shard_map/back/pallas_call | solution.py:565
  24.6 0.2 collective-permute-start.12
  24.8 1.3 %collective-permute-done.12.swap_ref = bf16[256,384]{1,0:T(8,128)(2,1)S(1)} collective-permute-done((bf16[256,384]{1,0:T(8,128)(2,1)S(1)}, bf16[256,384]{1,0:T(8,128)(2,1)S(1)}, u32[]{:S(2)}, u32[]{:S(2)}) %collective-permute-start.12) | collective-permute-done | bytes 196640 | tf_op jit(solution)/shard_map/ppermute | solution.py:484
  26.1 0.1 meet.1
  26.2 0.9 %collective-permute-start.13 = (bf16[272,256]{1,0:T(8,128)(2,1)S(1)}, bf16[272,256]{1,0:T(8,128)(2,1)S(1)}, u32[]{:S(2)}, u32[]{:S(2)}) collective-permute-start(bf16[272,256]{1,0:T(8,128)(2,1)S(1)} %get-tuple-element.64), channel_id=1, source_target_pairs={{0,8},{1,0},{2,10},{3,2},{4,12},{5,4},{6,14},{7,6},{8,16},{9,1},{1... | collective-permute-start | bytes 417800 | tf_op jit(solution)/shard_map/ppermute | solution.py:603
  27.1 1.8 %collective-permute-start.15 = (bf16[272,128]{1,0:T(8,128)(2,1)S(1)}, bf16[272,128]{1,0:T(8,128)(2,1)S(1)}, u32[]{:S(2)}, u32[]{:S(2)}) collective-permute-start(bf16[272,128]{1,0:T(8,128)(2,1)S(1)} %get-tuple-element.66), channel_id=1, source_target_pairs={{0,4},{4,0},{1,5},{5,1},{2,6},{6,2},{3,7},{7,3},{8,12},{12,8},{9,1... | collective-permute-start | bytes 208904 | tf_op jit(solution)/shard_map/ppermute | solution.py:590
  28.8 1.3 %collective-permute-start.14 = (bf16[272,128]{1,0:T(8,128)(2,1)S(1)}, bf16[272,128]{1,0:T(8,128)(2,1)S(1)}, u32[]{:S(2)}, u32[]{:S(2)}) collective-permute-start(bf16[272,128]{1,0:T(8,128)(2,1)S(1)} %get-tuple-element.65), channel_id=1, source_target_pairs={{0,12},{1,4},{2,14},{3,6},{4,8},{5,0},{6,10},{7,2},{8,20},{9,5},{1... | collective-permute-start | bytes 208904 | tf_op jit(solution)/shard_map/ppermute | solution.py:601
  30.1 1.6 %collective-permute-done.15.refs_1_ = bf16[272,128]{1,0:T(8,128)(2,1)S(1)} collective-permute-done((bf16[272,128]{1,0:T(8,128)(2,1)S(1)}, bf16[272,128]{1,0:T(8,128)(2,1)S(1)}, u32[]{:S(2)}, u32[]{:S(2)}) %collective-permute-start.15) | collective-permute-done | bytes 69664 | tf_op jit(solution)/shard_map/ppermute | solution.py:590
  31.7 1.4 %collective-permute-done.14.refs_0_ = bf16[272,128]{1,0:T(8,128)(2,1)S(1)} collective-permute-done((bf16[272,128]{1,0:T(8,128)(2,1)S(1)}, bf16[272,128]{1,0:T(8,128)(2,1)S(1)}, u32[]{:S(2)}, u32[]{:S(2)}) %collective-permute-start.14) | collective-permute-done | bytes 69664 | tf_op jit(solution)/shard_map/ppermute | solution.py:601
  33.1 0.6 %sums.1.own_ref = bf16[3,128,256]{2,1,0:T(8,128)(2,1)S(1)} custom-call(bf16[256,256]{1,0:T(8,128)(2,1)S(1)} %get-tuple-element.60.weight_ref, bf16[16,256]{1,0:T(8,128)(2,1)S(1)} %live.1.record_ref, bf16[256,256]{1,0:T(8,128)(2,1)S(1)} %get-tuple-element.61.own_ref, bf16[272,256]{1,0:T(8,128)(2,1)S(1)} %collective-permute-done.13.rows_ref, ...), custom_call_target="tpu_custom_call" | custom-call | tf_op jit(solution)/shard_map/sums/pallas_call | solution.py:604
  33.7 0.1 collective-permute-start.16
  33.8 1.4 %collective-permute-done.16.other_ref = bf16[3,128,256]{2,1,0:T(8,128)(2,1)S(1)} collective-permute-done((bf16[3,128,256]{2,1,0:T(8,128)(2,1)S(1)}, bf16[3,128,256]{2,1,0:T(8,128)(2,1)S(1)}, u32[]{:S(2)}, u32[]{:S(2)}) %collective-permute-start.16) | collective-permute-done | bytes 196640 | tf_op jit(solution)/shard_map/ppermute | solution.py:484
  35.2 0.8 %update.1 = f32[2,128,256]{2,1,0:T(8,128)} custom-call(f32[2,128,256]{2,1,0:T(8,128)S(1)} %copy-done, bf16[3,128,256]{2,1,0:T(8,128)(2,1)S(1)} %sums.1.own_ref, bf16[3,128,256]{2,1,0:T(8,128)(2,1)S(1)} %collective-permute-done.16.other_ref), custom_call_target="tpu_custom_call" | custom-call | tf_op jit(solution)/shard_map/update/pallas_call | solution.py:612
  (14 shorter events, 0.0 us)
Async XLA Ops:
  1.6 4.6 %collective-permute-start.1 = (bf16[2,2,256,256]{3,2,1,0:T(8,128)(2,1)S(1)}, bf16[2,2,256,256]{3,2,1,0:T(8,128)(2,1)S(1)}, u32[]{:S(2)}, u32[]{:S(2)}) collective-permute-start(bf16[2,2,256,256]{3,2,1,0:T(8,128)(2,1)S(1)} %get-tuple-element.38.refs_6_.refs_2_), channel_id=1, source_target_pairs={{0,1},{1,0},{2,3},{3,2},{4,5},{5,4},{6,7},{7,6},{8,9},{9,8},{10,11... | collective-permute-start | bytes 1572872 | tf_op jit(solution)/shard_map/ppermute | solution.py:484
  2.2 9.1 %collective-permute-start = (bf16[2,128,256]{2,1,0:T(8,128)(2,1)S(1)}, bf16[2,128,256]{2,1,0:T(8,128)(2,1)S(1)}, u32[]{:S(2)}, u32[]{:S(2)}) collective-permute-start(bf16[2,128,256]{2,1,0:T(8,128)(2,1)S(1)} %get-tuple-element.36.refs_0_), channel_id=1, source_target_pairs={{0,8},{1,0},{2,10},{3,2},{4,12},{5,4},{6,14},{7,6},{8,16},{9,1},{1... | collective-permute-start | bytes 393224 | tf_op jit(solution)/shard_map/ppermute | solution.py:516
  4.8 6.5 %collective-permute-start.3 = (bf16[256,256]{1,0:T(8,128)(2,1)S(1)}, bf16[256,256]{1,0:T(8,128)(2,1)S(1)}, u32[]{:S(2)}, u32[]{:S(2)}) collective-permute-start(bf16[256,256]{1,0:T(8,128)(2,1)S(1)} %get-tuple-element.43), channel_id=1, source_target_pairs={{0,2},{1,3},{2,0},{3,1},{4,6},{5,7},{6,4},{7,5},{8,10},{9,11},{10,... | collective-permute-start | bytes 393224 | tf_op jit(solution)/shard_map/ppermute | solution.py:484
  6.3 11.7 %collective-permute-start.5 = (bf16[2,1,256,256]{3,2,1,0:T(8,128)(2,1)S(1)}, bf16[2,1,256,256]{3,2,1,0:T(8,128)(2,1)S(1)}, u32[]{:S(2)}, u32[]{:S(2)}) collective-permute-start(bf16[2,1,256,256]{3,2,1,0:T(8,128)(2,1)S(1)} %get-tuple-element.44), channel_id=1, source_target_pairs={{0,2},{1,3},{2,0},{3,1},{4,6},{5,7},{6,4},{7,5},{8,10},{9,11},{10,... | collective-permute-start | bytes 786440 | tf_op jit(solution)/shard_map/ppermute | solution.py:484
  6.8 4.5 %collective-permute-start.2 = (bf16[2,128,128]{2,1,0:T(8,128)(2,1)S(1)}, bf16[2,128,128]{2,1,0:T(8,128)(2,1)S(1)}, u32[]{:S(2)}, u32[]{:S(2)}) collective-permute-start(bf16[2,128,128]{2,1,0:T(8,128)(2,1)S(1)} %get-tuple-element.41), channel_id=1, source_target_pairs={{0,4},{4,0},{1,5},{5,1},{2,6},{6,2},{3,7},{7,3},{8,12},{12,8},{9,1... | collective-permute-start | bytes 196616 | tf_op jit(solution)/shard_map/ppermute | solution.py:518
  8.3 5.6 %collective-permute-start.6 = (bf16[2,128,128]{2,1,0:T(8,128)(2,1)S(1)}, bf16[2,128,128]{2,1,0:T(8,128)(2,1)S(1)}, u32[]{:S(2)}, u32[]{:S(2)}) collective-permute-start(bf16[2,128,128]{2,1,0:T(8,128)(2,1)S(1)} %get-tuple-element.41), channel_id=1, source_target_pairs={{0,12},{1,4},{2,14},{3,6},{4,8},{5,0},{6,10},{7,2},{8,20},{9,5},{1... | collective-permute-start | bytes 196616 | tf_op jit(solution)/shard_map/ppermute | solution.py:517
  11.3 3.8 %collective-permute-start.8 = (bf16[2,128,256]{2,1,0:T(8,128)(2,1)S(1)}, bf16[2,128,256]{2,1,0:T(8,128)(2,1)S(1)}, u32[]{:S(2)}, u32[]{:S(2)}) collective-permute-start(bf16[2,128,256]{2,1,0:T(8,128)(2,1)S(1)} %collective-permute-done.refs_3_), channel_id=1, source_target_pairs={{0,1},{1,0},{2,3},{3,2},{4,5},{5,4},{6,7},{7,6},{8,9},{9,8},{10,11... | collective-permute-start | bytes 393224 | tf_op jit(solution)/shard_map/ppermute | solution.py:484
  11.3 6.6 %collective-permute-start.4 = (bf16[256,256]{1,0:T(8,128)(2,1)S(1)}, bf16[256,256]{1,0:T(8,128)(2,1)S(1)}, u32[]{:S(2)}, u32[]{:S(2)}) collective-permute-start(bf16[256,256]{1,0:T(8,128)(2,1)S(1)} %collective-permute-done.3.over_y.refs_4_), channel_id=1, source_target_pairs={{0,4},{4,0},{1,5},{5,1},{2,6},{6,2},{3,7},{7,3},{8,12},{12,8},{9,1... | collective-permute-start | bytes 393224 | tf_op jit(solution)/shard_map/ppermute | solution.py:514
  13.9 1.3 %collective-permute-start.7 = (bf16[2,128,128]{2,1,0:T(8,128)(2,1)S(1)}, bf16[2,128,128]{2,1,0:T(8,128)(2,1)S(1)}, u32[]{:S(2)}, u32[]{:S(2)}) collective-permute-start(bf16[2,128,128]{2,1,0:T(8,128)(2,1)S(1)} %collective-permute-done.6.refs_1_), channel_id=1, source_target_pairs={{0,1},{1,0},{2,3},{3,2},{4,5},{5,4},{6,7},{7,6},{8,9},{9,8},{10,11... | collective-permute-start | bytes 196616 | tf_op jit(solution)/shard_map/ppermute | solution.py:484
  15.1 4.8 %copy-start.1 = (bf16[1,1,2,256,256]{4,3,2,1,0:T(8,128)(2,1)S(1)}, bf16[1,1,2,256,256]{4,3,2,1,0:T(8,128)(2,1)}, u32[]{:S(2)}) copy-start(bf16[1,1,2,256,256]{4,3,2,1,0:T(8,128)(2,1)} %refs_0_.1) | copy-start | bytes 786436
  18.0 1.9 %collective-permute-start.11 = (bf16[2,1,256,256]{3,2,1,0:T(8,128)(2,1)S(1)}, bf16[2,1,256,256]{3,2,1,0:T(8,128)(2,1)S(1)}, u32[]{:S(2)}, u32[]{:S(2)}) collective-permute-start(bf16[2,1,256,256]{3,2,1,0:T(8,128)(2,1)S(1)} %collective-permute-done.5.rest.refs_6_), channel_id=1, source_target_pairs={{0,1},{1,0},{2,3},{3,2},{4,5},{5,4},{6,7},{7,6},{8,9},{9,8},{10,11... | collective-permute-start | bytes 786440 | tf_op jit(solution)/shard_map/ppermute | solution.py:484
  18.0 1.7 %collective-permute-start.9 = (bf16[256,256]{1,0:T(8,128)(2,1)S(1)}, bf16[256,256]{1,0:T(8,128)(2,1)S(1)}, u32[]{:S(2)}, u32[]{:S(2)}) collective-permute-start(bf16[256,256]{1,0:T(8,128)(2,1)S(1)} %collective-permute-done.3.over_y.refs_4_), channel_id=1, source_target_pairs={{0,1},{1,0},{2,3},{3,2},{4,5},{5,4},{6,7},{7,6},{8,9},{9,8},{10,11... | collective-permute-start | bytes 393224 | tf_op jit(solution)/shard_map/ppermute | solution.py:484
  18.5 1.4 %collective-permute-start.10 = (bf16[256,256]{1,0:T(8,128)(2,1)S(1)}, bf16[256,256]{1,0:T(8,128)(2,1)S(1)}, u32[]{:S(2)}, u32[]{:S(2)}) collective-permute-start(bf16[256,256]{1,0:T(8,128)(2,1)S(1)} %collective-permute-done.4.over_x.refs_5_), channel_id=1, source_target_pairs={{0,1},{1,0},{2,3},{3,2},{4,5},{5,4},{6,7},{7,6},{8,9},{9,8},{10,11... | collective-permute-start | bytes 393224 | tf_op jit(solution)/shard_map/ppermute | solution.py:484
  19.9 15.4 %copy-start = (f32[2,128,256]{2,1,0:T(8,128)S(1)}, f32[2,128,256]{2,1,0:T(8,128)}, u32[]{:S(2)}) copy-start(f32[2,128,256]{2,1,0:T(8,128)} %object_ref.1) | copy-start | bytes 786436
  24.6 1.5 %collective-permute-start.12 = (bf16[256,384]{1,0:T(8,128)(2,1)S(1)}, bf16[256,384]{1,0:T(8,128)(2,1)S(1)}, u32[]{:S(2)}, u32[]{:S(2)}) collective-permute-start(bf16[256,384]{1,0:T(8,128)(2,1)S(1)} %get-tuple-element.63), channel_id=1, source_target_pairs={{0,1},{1,0},{2,3},{3,2},{4,5},{5,4},{6,7},{7,6},{8,9},{9,8},{10,11... | collective-permute-start | bytes 589832 | tf_op jit(solution)/shard_map/ppermute | solution.py:484
  26.2 7.0 %collective-permute-start.13 = (bf16[272,256]{1,0:T(8,128)(2,1)S(1)}, bf16[272,256]{1,0:T(8,128)(2,1)S(1)}, u32[]{:S(2)}, u32[]{:S(2)}) collective-permute-start(bf16[272,256]{1,0:T(8,128)(2,1)S(1)} %get-tuple-element.64), channel_id=1, source_target_pairs={{0,8},{1,0},{2,10},{3,2},{4,12},{5,4},{6,14},{7,6},{8,16},{9,1},{1... | collective-permute-start | bytes 417800 | tf_op jit(solution)/shard_map/ppermute | solution.py:603
  27.1 4.6 %collective-permute-start.15 = (bf16[272,128]{1,0:T(8,128)(2,1)S(1)}, bf16[272,128]{1,0:T(8,128)(2,1)S(1)}, u32[]{:S(2)}, u32[]{:S(2)}) collective-permute-start(bf16[272,128]{1,0:T(8,128)(2,1)S(1)} %get-tuple-element.66), channel_id=1, source_target_pairs={{0,4},{4,0},{1,5},{5,1},{2,6},{6,2},{3,7},{7,3},{8,12},{12,8},{9,1... | collective-permute-start | bytes 208904 | tf_op jit(solution)/shard_map/ppermute | solution.py:590
  28.8 4.3 %collective-permute-start.14 = (bf16[272,128]{1,0:T(8,128)(2,1)S(1)}, bf16[272,128]{1,0:T(8,128)(2,1)S(1)}, u32[]{:S(2)}, u32[]{:S(2)}) collective-permute-start(bf16[272,128]{1,0:T(8,128)(2,1)S(1)} %get-tuple-element.65), channel_id=1, source_target_pairs={{0,12},{1,4},{2,14},{3,6},{4,8},{5,0},{6,10},{7,2},{8,20},{9,5},{1... | collective-permute-start | bytes 208904 | tf_op jit(solution)/shard_map/ppermute | solution.py:601
  33.7 1.5 %collective-permute-start.16 = (bf16[3,128,256]{2,1,0:T(8,128)(2,1)S(1)}, bf16[3,128,256]{2,1,0:T(8,128)(2,1)S(1)}, u32[]{:S(2)}, u32[]{:S(2)}) collective-permute-start(bf16[3,128,256]{2,1,0:T(8,128)(2,1)S(1)} %sums.1.own_ref), channel_id=1, source_target_pairs={{0,1},{1,0},{2,3},{3,2},{4,5},{5,4},{6,7},{7,6},{8,9},{9,8},{10,11... | collective-permute-start | bytes 589832 | tf_op jit(solution)/shard_map/ppermute | solution.py:484

commit v10 on v9

--- a/solution.py
+++ b/solution.py
@@ -36,16 +36,6 @@
 
 def iota(shape, dim):
     return lax.broadcasted_iota(jnp.int32, shape, dim)
-
-
-def column_coordinate(at, tile_cols, half, sides, x_index, x_count):
-    own = at + half
-    if sides == 1:
-        side = at - tile_cols + jnp.where(x_index == 0, half + tile_cols, 0)
-        return jnp.where(at < tile_cols, own, side)
-    left = jnp.where(x_index > 0, at - tile_cols, nowhere)
-    right = jnp.where(x_index < x_count - 1, at, nowhere)
-    return jnp.where(at < tile_cols, own, jnp.where(at < tile_cols + half, left, right))
 
 
 def sent_order(sides):
@@ -88,6 +78,7 @@
     shared_ref,
     rest_ref,
     record_ref,
+    spot_ref,
     direct_ref,
     swapped_ref,
     packed_ref,
@@ -111,10 +102,10 @@
         copy.start()
     tile_cols = object_ref.shape[2]
     half = edges[0].shape[2]
-    _, x_index, _ = here()
+    z_index, x_index, parity = here()
     copies[0].wait()
     low_ref[...] = probe_ref[...].astype(jnp.bfloat16)
-    shared_ref[...] = jnp.where(x_index % 2 == 0, low_ref[0, 0], low_ref[1, 0])
+    shared_ref[...] = jnp.where(z_index % 2 == 0, low_ref[0, 0], low_ref[1, 0])
     rest_ref[...] = low_ref[:, 1:]
     copies[1].wait()
     first, last = slice(0, half), slice(tile_cols - half, tile_cols)
@@ -127,6 +118,9 @@
             edges[0][channel] = values[:, last]
             edges[1][channel] = values[:, first]
     copies[2].wait()
+    spot_ref[...] = jnp.where(
+        iota(spot_ref.shape, 0) == 0, centers_ref[0, 0, parity, 0], centers_ref[0, 0, parity, 1]
+    )
     record = jnp.zeros(record_ref.shape, jnp.float32)
     line = iota(record_ref.shape, 0)
     for slot in range(slots):
@@ -157,44 +151,50 @@
     return of_slot(0), of_slot(1), record[2 * slots : 2 * slots + 1] > wanted
 
 
-def row_starts(half, tile_rows, parity):
-    low, high = 0, half + tile_rows
-    return (
-        pl.multiple_of(jnp.where(parity == 0, low, high), half),
-        pl.multiple_of(jnp.where(parity == 0, high, low), half),
-    )
-
-
-def patch_of(sides, slots, z_count, x_count, side, record_ref, pieces, ext_ref):
+def turned_back(value, side):
+    return jnp.where(value == 0, 0, side - value)
+
+
+def patch_of(sides, z_count, x_count, side, spot_ref, pieces):
     z_index, x_index, parity = here()
-    row_at, col_at, _ = position_of(record_ref, slots, parity)
+    row_at, col_at = spot_ref[0, 0], spot_ref[1, 0]
     half = side // 2
-    _, tile_rows, tile_cols = pieces[0].shape
-    ext_rows = tile_rows + side
-    ext_cols = tile_cols + sides * half
-    a_at, b_at = row_starts(half, tile_rows, parity)
+    even = parity == 0
+    low_shown = z_index > 0
+    high_shown = z_index < z_count - 1
+
+    def joined(piece, a, b, channel):
+        level = piece[channel].astype(jnp.float32)
+        turn_a = a[channel].astype(jnp.float32)
+        turn_b = b[channel].astype(jnp.float32)
+        low = jnp.where(even & low_shown, turn_a, jnp.where(low_shown, turn_b, 0.0))
+        high = jnp.where(even & high_shown, turn_b, jnp.where(high_shown, turn_a, 0.0))
+        first = jnp.where(iota(low.shape, 0) >= row_at, low, high)
+        return jnp.concatenate([first, level], axis=0)
+
+    out = []
     for channel in range(2):
-        base = channel * ext_rows
-        for index in range(1 + sides):
-            columns = (
-                slice(0, tile_cols)
-                if index == 0
-                else slice(tile_cols + (index - 1) * half, tile_cols + index * half)
-            )
-            level, turn_a, turn_b = pieces[3 * index : 3 * index + 3]
-            ext_ref[pl.ds(base + half, tile_rows), columns] = level[channel]
-            ext_ref[pl.ds(base + a_at, half), columns] = turn_a[channel]
-            ext_ref[pl.ds(base + b_at, half), columns] = turn_b[channel]
-    at = iota((ext_cols, side), 0)
-    column = column_coordinate(at, tile_cols, half, sides, x_index, x_count)
-    pick_cols = (column == iota((ext_cols, side), 1) + col_at).astype(jnp.bfloat16)
-    at = iota((side, ext_rows), 1)
-    first = jnp.where(z_index > 0, 0, half)
-    last = jnp.where(z_index < z_count - 1, ext_rows, half + tile_rows)
-    row = jnp.where((at >= first) & (at < last), at, nowhere)
-    pick_rows = (row == iota((side, ext_rows), 0) + row_at).astype(jnp.bfloat16)
-    narrow = dot(ext_ref[...], pick_cols).astype(jnp.bfloat16)
-    return dot(pick_rows, narrow[:ext_rows]), dot(pick_rows, narrow[ext_rows:])
+        own = joined(*pieces[:3], channel)
+        sides_joined = [
+            joined(*pieces[3 + 3 * index : 6 + 3 * index], channel) for index in range(sides)
+        ]
+        if sides == 1:
+            left = jnp.where(x_index == 1, sides_joined[0], 0.0)
+            right = jnp.where(x_index == 0, sides_joined[0], 0.0)
+        else:
+            left = jnp.where(x_index > 0, sides_joined[0], 0.0)
+            right = jnp.where(x_index < x_count - 1, sides_joined[1], 0.0)
+        at = iota(left.shape, 1)
+        window = jnp.concatenate(
+            [
+                jnp.where(at >= col_at, left, own[:, half:]),
+                jnp.where(at + half >= col_at, own[:, :half], right),
+            ],
+            axis=1,
+        )
+        window = pltpu.roll(window, turned_back(row_at, side), 0)
+        out.append(pltpu.roll(window, turned_back(col_at, side), 1))
+    return out
 
 
 def modes_of(group):
@@ -204,15 +204,15 @@
     return [reader(k) for k in range(group.shape[1])]
 
 
-def shared_mode(over_y, over_x):
+def shared_mode(over_y, over_z):
     def read():
-        _, x_index, _ = here()
-        even = x_index % 2 == 0
+        z_index, _, _ = here()
+        even = z_index % 2 == 0
         over_y_values = over_y[...].astype(jnp.float32)
-        over_x_values = over_x[...].astype(jnp.float32)
+        over_z_values = over_z[...].astype(jnp.float32)
         return (
-            jnp.where(even, over_y_values, over_x_values),
-            jnp.where(even, over_x_values, over_y_values),
+            jnp.where(even, over_y_values, over_z_values),
+            jnp.where(even, over_z_values, over_y_values),
         )
 
     return read
@@ -264,13 +264,13 @@
     return grad_real, grad_imag
 
 
-def near_kernel(sides, slots, z_count, x_count, record_ref, *refs):
+def near_kernel(sides, z_count, x_count, spot_ref, *refs):
     n_pieces = 3 + 3 * sides
     pieces = from_sent_order(refs[:n_pieces])
     own, core, direct, swapped = refs[n_pieces : n_pieces + 4]
-    patch_ref, far_ref, exit_ref, sum_ref, ext_ref = refs[n_pieces + 4 :]
+    patch_ref, far_ref, exit_ref, sum_ref = refs[n_pieces + 4 :]
     side = own.shape[2]
-    patch = patch_of(sides, slots, z_count, x_count, side, record_ref, pieces, ext_ref)
+    patch = patch_of(sides, z_count, x_count, side, spot_ref, pieces)
     patch_ref[0], patch_ref[1] = patch
     tables = (direct[...], swapped[...], far_ref, exit_ref)
     first = forward(modes_of(own), patch, *tables, 0)
@@ -279,15 +279,15 @@
     sum_ref[1] = first[1] + second[1]
 
 
-def over_kernel(patch_ref, over_y, over_x, rest, direct, swapped, far_ref, exit_ref, sum_ref):
+def over_kernel(patch_ref, over_y, over_z, rest, direct, swapped, far_ref, exit_ref, sum_ref):
     patch = (patch_ref[0], patch_ref[1])
-    modes = [shared_mode(over_y, over_x)] + modes_of(rest)
+    modes = [shared_mode(over_y, over_z)] + modes_of(rest)
     sum_ref[0], sum_ref[1] = forward(
         modes, patch, direct[...], swapped[...], far_ref, exit_ref, 0
     )
 
 
-def back_kernel(sides, slots, x_count, tile_rows, tile_cols, record_ref, *refs):
+def back_kernel(sides, slots, tile_cols, record_ref, spot_ref, *refs):
     amplitude_ref, patch_ref, own, core = refs[:4]
     over_modes = [shared_mode(*refs[4:6])] + modes_of(refs[6])
     last_modes = [shared_mode(*refs[7:9])] + modes_of(refs[9])
@@ -295,14 +295,13 @@
     near_far, near_exit, near_sum, over_far, over_exit, over_sum = refs[12:18]
     weight_out, own_out, keep_out, swap_out = refs[18:22]
     side_outs = refs[22 : 22 + sides]
-    last_far, last_exit, grad_ref = refs[22 + sides :]
+    last_far, last_exit = refs[22 + sides :]
     side = own.shape[2]
     half = side // 2
     modes = own.shape[1]
-    ext_rows = tile_rows + side
-    ext_cols = tile_cols + sides * half
     _, x_index, parity = here()
-    row_at, col_at, is_live = position_of(record_ref, slots, parity)
+    row_at, col_at = spot_ref[0, 0], spot_ref[1, 0]
+    _, _, is_live = position_of(record_ref, slots, parity)
     direct = direct_ref[...]
     swapped = swapped_ref[...]
     patch = (patch_ref[0], patch_ref[1])
@@ -320,39 +319,47 @@
         backward(over_modes, *tables, over_far, over_exit, 0),
         backward(last_modes, *tables, last_far, last_exit, 0),
     ]
-    at = iota((side, ext_cols), 1)
-    column = column_coordinate(at, tile_cols, half, sides, x_index, x_count)
-    put_cols = ((column == iota((side, ext_cols), 0) + col_at) & is_live).astype(jnp.bfloat16)
-    put_rows = (iota((ext_rows, side), 0) == iota((ext_rows, side), 1) + row_at).astype(
-        jnp.bfloat16
-    )
-    a_at, b_at = row_starts(half, tile_rows, parity)
+    even = parity == 0
     for channel in range(2):
         gradient = (grads[0][channel] + grads[1][channel]) + (grads[2][channel] + grads[3][channel])
-        placed = dot(put_rows, gradient.astype(jnp.bfloat16)).astype(jnp.bfloat16)
-        grad_ref[...] = dot(placed, put_cols).astype(jnp.bfloat16)
+        gradient = jnp.where(is_live, gradient, 0.0)
+        gradient = pltpu.roll(pltpu.roll(gradient, col_at, 1), row_at, 0)
+        first, second = gradient[:, :half], gradient[:, half:]
+        at = iota(first.shape, 1)
+        left = jnp.where(at >= col_at, first, 0.0)
+        own = [
+            jnp.where(at + half >= col_at, second, 0.0),
+            jnp.where(at < col_at, first, 0.0),
+        ]
+        right = jnp.where(at + half < col_at, second, 0.0)
+        if sides == 1:
+            beside = [jnp.where(x_index == 0, right, left)]
+        else:
+            beside = [left, right]
+        placed = jnp.concatenate(own + beside, axis=1)
+        row = iota((half, placed.shape[1]), 0)
+        low = jnp.where(row >= row_at, placed[:half], 0.0).astype(jnp.bfloat16)
+        high = jnp.where(row < row_at, placed[:half], 0.0).astype(jnp.bfloat16)
+        inner = placed[half:].astype(jnp.bfloat16)
         rows = slice(channel * half, (channel + 1) * half)
-        own_out[rows] = grad_ref[half : half + tile_rows, :tile_cols]
-        keep_out[rows] = grad_ref[pl.ds(b_at, half), :]
-        swap_out[rows] = grad_ref[pl.ds(a_at, half), :]
+        own_out[rows] = inner[:, :tile_cols]
+        keep_out[rows] = jnp.where(even, high, low)
+        swap_out[rows] = jnp.where(even, low, high)
         for index, out in enumerate(side_outs):
-            columns = slice(tile_cols + index * half, tile_cols + (index + 1) * half)
-            out[rows] = grad_ref[half : half + tile_rows, columns]
+            out[rows] = inner[:, tile_cols + index * half : tile_cols + (index + 1) * half]
     for out in side_outs:
         out[2 * half :] = record_ref[:, :half]
 
 
-def meet_kernel(record_ref, keep_ref, swap_ref, rows_out, *corner_outs):
-    total = keep_ref[...].astype(jnp.float32) + swap_ref[...].astype(jnp.float32)
-    total = total.astype(jnp.bfloat16)
-    height = total.shape[0]
-    tile_cols = rows_out.shape[1]
-    rows_out[:height] = total[:, :tile_cols]
-    rows_out[height:] = record_ref[...]
-    for index, out in enumerate(corner_outs):
-        half = out.shape[1]
-        out[:height] = total[:, tile_cols + index * half : tile_cols + (index + 1) * half]
-        out[height:] = record_ref[:, :half]
+def meet_kernel(first_column, record_ref, keep_ref, swap_ref, *outs):
+    at = first_column
+    for out in outs:
+        height, width = keep_ref.shape[0], out.shape[1]
+        columns = slice(at, at + width)
+        total = keep_ref[:, columns].astype(jnp.float32) + swap_ref[:, columns].astype(jnp.float32)
+        out[:height] = total.astype(jnp.bfloat16)
+        out[height:] = record_ref[:, :width]
+        at += width
 
 
 def sum_kernel(sides, slots, z_count, x_count, weight_ref, record_ref, own_ref, rows_ref, *refs):
@@ -452,7 +459,7 @@
     x_count = lax.axis_size("ty")
     m_count = lax.axis_size("mode")
     modes = probe.shape[1]
-    if tile_rows != half or slots != 2 or m_count != 4 or x_count % 2 or modes < 2:
+    if tile_rows != half or slots != 2 or m_count != 4 or z_count % 2 or x_count < 2 or modes < 2:
         raise ValueError("unsupported sizes")
     sides = 1 if x_count == 2 else 2
     axes = ("tx", "ty", "mode")
@@ -484,20 +491,21 @@
         return lax.ppermute(array, "mode", [(m, m ^ flip) for m in range(m_count)])
 
     tables = [jnp.asarray(matrix) for matrix in dft_matrices(side)]
-    probe_low, shared, rest, record, direct, swapped, *packed = pl.pallas_call(
+    probe_low, shared, rest, record, spot, direct, swapped, *packed = pl.pallas_call(
         functools.partial(start_kernel, sides, slots),
         out_shape=[
             jax.ShapeDtypeStruct(probe.shape, jnp.bfloat16),
             jax.ShapeDtypeStruct((side, side), jnp.bfloat16),
             jax.ShapeDtypeStruct((2, modes - 1, side, side), jnp.bfloat16),
             jax.ShapeDtypeStruct((record_rows, tile_cols), jnp.bfloat16),
+            jax.ShapeDtypeStruct((8, 128), jnp.int32),
             jax.ShapeDtypeStruct((2 * side, 2 * side), jnp.bfloat16),
             jax.ShapeDtypeStruct((2 * side, 2 * side), jnp.bfloat16),
             jax.ShapeDtypeStruct(object_field.shape, jnp.bfloat16),
         ]
         + [jax.ShapeDtypeStruct((2, tile_rows, half), jnp.bfloat16)] * sides,
         in_specs=[hbm()] * 5,
-        out_specs=[vmem()] * (7 + sides),
+        out_specs=[vmem()] * (8 + sides),
         scratch_shapes=[
             pltpu.VMEM(object_field.shape, jnp.float32),
             pltpu.VMEM(probe.shape, jnp.float32),
@@ -511,7 +519,7 @@
     probe_core = exchange(probe_low, 1)
     probe_core, rest, live = lax.optimization_barrier((probe_core, rest, live))
     rest = exchange(rest, 2)
-    over_x = lax.ppermute(over_y, "ty", [(x, x ^ 1) for x in range(x_count)])
+    over_z = lax.ppermute(over_y, "tx", [(z, z ^ 1) for z in range(z_count)])
     x_steps = [1] if sides == 1 else [1, -1]
     rows = lax.ppermute(packed[0], axes, zigzag(0))
     corners = [lax.ppermute(edge, axes, zigzag(step)) for step, edge in zip(x_steps, packed[1:])]
@@ -524,12 +532,12 @@
         compiler_params=pltpu.CompilerParams(vmem_limit_bytes=small_bytes),
         name="live",
     )(record, live)
-    rows, record, *levels = lax.optimization_barrier((rows, record, *levels))
+    rows, record = lax.optimization_barrier((rows, record))
+    corners, levels = lax.optimization_barrier((corners, levels))
     pieces = [packed[0], rows, exchange(rows, 1)]
     for at_level, corner in zip(levels, corners):
         pieces += [at_level, corner, exchange(corner, 1)]
     n_pieces = len(pieces)
-    ext_rows = tile_rows + side
     ext_cols = tile_cols + sides * half
 
     def waves(count):
@@ -540,16 +548,15 @@
         ]
 
     patch, *near = pl.pallas_call(
-        functools.partial(near_kernel, sides, slots, z_count, x_count),
+        functools.partial(near_kernel, sides, z_count, x_count),
         out_shape=[jax.ShapeDtypeStruct((2, side, side), jnp.float32)] + waves(2 * modes),
         in_specs=[vmem()] * (n_pieces + 5),
         out_specs=[vmem()] * 4,
-        scratch_shapes=[pltpu.VMEM((2 * ext_rows, ext_cols), jnp.bfloat16)],
         compiler_params=pltpu.CompilerParams(vmem_limit_bytes=wave_bytes),
         name="near",
-    )(record, *in_sent_order(pieces), probe_low, probe_core, direct, swapped)
-    over_x, rest, patch = lax.optimization_barrier((over_x, rest, patch))
-    over_group = (over_y, over_x, rest)
+    )(spot, *in_sent_order(pieces), probe_low, probe_core, direct, swapped)
+    over_z, rest, patch = lax.optimization_barrier((over_z, rest, patch))
+    over_group = (over_y, over_z, rest)
     last_group = [exchange(part, 1) for part in over_group]
     over = pl.pallas_call(
         over_kernel,
@@ -563,19 +570,19 @@
     shapes = [(side, side), (2 * half, tile_cols)] + [(2 * half, ext_cols)] * 2
     shapes += [(piece_rows, half)] * sides
     weight, own, keep, swap, *levels = pl.pallas_call(
-        functools.partial(back_kernel, sides, slots, x_count, tile_rows, tile_cols),
+        functools.partial(back_kernel, sides, slots, tile_cols),
         out_shape=[jax.ShapeDtypeStruct(shape, jnp.bfloat16) for shape in shapes],
-        in_specs=[vmem()] * 19,
+        in_specs=[vmem()] * 20,
         out_specs=[vmem()] * (4 + sides),
         scratch_shapes=[
             pltpu.VMEM((modes, side, 2 * side), jnp.float32),
             pltpu.VMEM((modes, 2 * side, side), jnp.bfloat16),
-            pltpu.VMEM((ext_rows, ext_cols), jnp.bfloat16),
         ],
         compiler_params=pltpu.CompilerParams(vmem_limit_bytes=wave_bytes),
         name="back",
     )(
         record,
+        spot,
         amplitudes,
         patch,
         probe_low,
@@ -589,18 +596,21 @@
     )
     levels = [lax.ppermute(piece, "ty", level(-step)) for piece, step in zip(levels, x_steps)]
     rows, *corners = pl.pallas_call(
-        meet_kernel,
-        out_shape=[jax.ShapeDtypeStruct((piece_rows, tile_cols), jnp.bfloat16)]
-        + [jax.ShapeDtypeStruct((piece_rows, half), jnp.bfloat16)] * sides,
+        functools.partial(meet_kernel, 0),
+        out_shape=[
+            jax.ShapeDtypeStruct((piece_rows, width), jnp.bfloat16)
+            for width in [tile_cols] + [half] * sides
+        ],
         in_specs=[vmem()] * 3,
         out_specs=[vmem()] * (1 + sides),
         compiler_params=pltpu.CompilerParams(vmem_limit_bytes=small_bytes),
         name="meet",
     )(record, keep, exchange(swap, 1))
+    rows = lax.ppermute(rows, axes, zigzag(0))
+    corners, levels = lax.optimization_barrier((corners, levels))
     corners = [
         lax.ppermute(piece, axes, zigzag(-step)) for piece, step in zip(corners, x_steps)
     ]
-    rows = lax.ppermute(rows, axes, zigzag(0))
     summed = pl.pallas_call(
         functools.partial(sum_kernel, sides, slots, z_count, x_count),
         out_shape=jax.ShapeDtypeStruct((3, tile_rows, tile_cols), jnp.bfloat16),

time: 36.2 us -> 34.9 us (0.964)
  waiting for transfers between devices: 8.64 us -> 7.3 us
  starting transfers between devices: 15.6 us -> 16.4 us
  Pallas kernels: 11 us -> 10.4 us
    ppermute x1, starting transfers between devices: 1.29 us -> 2.5 us  [on_device(): lax.ppermute(piece, axes, zigzag(-step))]
    ppermute x1, starting transfers between devices: 2.55 us -> 1.55 us  [on_device(): over_z = lax.ppermute(over_y, 'tx', [(z, z ^ 1) for z in range(z_count)])]
    ppermute x1, starting transfers between devices: 0.89 us -> 1.77 us  [on_device(): rows = lax.ppermute(rows, axes, zigzag(0))]
    ppermute x1, waiting for transfers between devices: 0.81 us -> 0.01 us  [on_device(): lax.ppermute(edge, 'ty', level(step))]
    pallas_call x3, Pallas kernels: 7.13 us -> 6.46 us  [the longest x1 4.34 us: on_device(): pl.pallas_call(functools.partial(back_kernel, sides, slots, tile_cols), o...]
    ppermute x10, waiting for transfers between devices: 4.34 us -> 3.69 us  [exchange(): return lax.ppermute(array, 'mode', [(m, m ^ flip) for m in range(m_count)])]
    ppermute x1, waiting for transfers between devices: 1.43 us -> 1.98 us  [on_device(): lax.ppermute(piece, axes, zigzag(-step))]
    ppermute x1, waiting for transfers between devices: 1.61 us -> 1.13 us  [on_device(): lax.ppermute(piece, 'ty', level(-step))]
  transfers between devices with their start and end apart: 17 -> 17, of which waited for: 9 -> 8; matrix products, arithmetic and copies ran while one was open for 0% -> 0% of each run, Pallas kernels for 9% -> 9%
where the time goes in v10:
time: 34.9 us; the launch traced here: 34.8 us
  starting transfers between devices  16.4 us (47%)
  Pallas kernels  10.4 us (30%)
  waiting for transfers between devices  7.3 us (21%)
  between operations  0.75 us (2%)
    pallas_call x1, Pallas kernels, on_device(): pl.pallas_call(functools.partial(back_kernel, sides, slots, tile_cols), o...  4.34 us
    ppermute x10, waiting for transfers between devices, exchange(): return lax.ppermute(array, 'mode', [(m, m ^ flip) for m in range(m_count)])  3.69 us
    ppermute x10, starting transfers between devices, exchange(): return lax.ppermute(array, 'mode', [(m, m ^ flip) for m in range(m_count)])  3.4 us
    ppermute x1, starting transfers between devices, on_device(): rows = lax.ppermute(packed[0], axes, zigzag(0))  2.6 us
    ppermute x1, starting transfers between devices, on_device(): lax.ppermute(piece, axes, zigzag(-step))  2.5 us
    pallas_call x1, Pallas kernels, on_device(): pl.pallas_call(functools.partial(near_kernel, sides, z_count, x_count), o...  2.07 us
    ppermute x1, waiting for transfers between devices, on_device(): lax.ppermute(piece, axes, zigzag(-step))  1.98 us
    ppermute x1, starting transfers between devices, on_device(): rows = lax.ppermute(rows, axes, zigzag(0))  1.77 us
  transfers between devices with their start and end apart: 17, of which 8 were waited for; matrix products, arithmetic and copies ran while one was open for 0% of the time, Pallas kernels for 9%

profile of v10, /device:TPU:0, one launch (start us, length us, event | category | flops | bytes accessed | tf_op | source)
XLA Modules:
  0.0 34.8 jit_solution(14940399655864718094)
XLA Ops:
  0.0 1.6 %start.1 = (bf16[2,2,256,256]{3,2,1,0:T(8,128)(2,1)S(1)}, bf16[256,256]{1,0:T(8,128)(2,1)S(1)}, bf16[2,1,256,256]{3,2,1,0:T(8,128)(2,1)S(1)}, bf16[16,256]{1,0:T...) custom-call(f32[2,128,256]{2,1,0:T(8,128)} %object_ref.1, ...), custom_call_target="tpu_custom_call" | custom-call | tf_op jit(solution)/shard_map/start/pallas_call | solution.py:494
  1.6 0.5 %collective-permute-start.1 = (bf16[2,2,256,256]{3,2,1,0:T(8,128)(2,1)S(1)}, bf16[2,2,256,256]{3,2,1,0:T(8,128)(2,1)S(1)}, u32[]{:S(2)}, u32[]{:S(2)}) collective-permute-start(bf16[2,2,256,256]{3,2,1,0:T(8,128)(2,1)S(1)} %get-tuple-element.42.refs_6_.refs_2_), channel_id=1, source_target_pairs={{0,1},{1,0},{2,3},{3,2},{4,5},{5,4},{6,7},{7,6},{8,9},{9,8},{10,11... | collective-permute-start | bytes 1572872 | tf_op jit(solution)/shard_map/ppermute | solution.py:491
  2.2 2.6 %collective-permute-start = (bf16[2,128,256]{2,1,0:T(8,128)(2,1)S(1)}, bf16[2,128,256]{2,1,0:T(8,128)(2,1)S(1)}, u32[]{:S(2)}, u32[]{:S(2)}) collective-permute-start(bf16[2,128,256]{2,1,0:T(8,128)(2,1)S(1)} %get-tuple-element.40.refs_0_), channel_id=1, source_target_pairs={{0,8},{1,0},{2,10},{3,2},{4,12},{5,4},{6,14},{7,6},{8,16},{9,1},{1... | collective-permute-start | bytes 393224 | tf_op jit(solution)/shard_map/ppermute | solution.py:524
  4.8 1.5 %collective-permute-start.2 = (bf16[256,256]{1,0:T(8,128)(2,1)S(1)}, bf16[256,256]{1,0:T(8,128)(2,1)S(1)}, u32[]{:S(2)}, u32[]{:S(2)}) collective-permute-start(bf16[256,256]{1,0:T(8,128)(2,1)S(1)} %get-tuple-element.47), channel_id=1, source_target_pairs={{0,2},{1,3},{2,0},{3,1},{4,6},{5,7},{6,4},{7,5},{8,10},{9,11},{10,... | collective-permute-start | bytes 393224 | tf_op jit(solution)/shard_map/ppermute | solution.py:491
  6.3 0.0 collective-permute-done.1.refs_7_.refs_3_
  6.3 0.5 %collective-permute-start.4 = (bf16[2,1,256,256]{3,2,1,0:T(8,128)(2,1)S(1)}, bf16[2,1,256,256]{3,2,1,0:T(8,128)(2,1)S(1)}, u32[]{:S(2)}, u32[]{:S(2)}) collective-permute-start(bf16[2,1,256,256]{3,2,1,0:T(8,128)(2,1)S(1)} %get-tuple-element.48), channel_id=1, source_target_pairs={{0,2},{1,3},{2,0},{3,1},{4,6},{5,7},{6,4},{7,5},{8,10},{9,11},{10,... | collective-permute-start | bytes 786440 | tf_op jit(solution)/shard_map/ppermute | solution.py:491
  6.8 1.5 %collective-permute-start.6 = (bf16[2,128,128]{2,1,0:T(8,128)(2,1)S(1)}, bf16[2,128,128]{2,1,0:T(8,128)(2,1)S(1)}, u32[]{:S(2)}, u32[]{:S(2)}) collective-permute-start(bf16[2,128,128]{2,1,0:T(8,128)(2,1)S(1)} %get-tuple-element.49), channel_id=1, source_target_pairs={{0,4},{4,0},{1,5},{5,1},{2,6},{6,2},{3,7},{7,3},{8,12},{12,8},{9,1... | collective-permute-start | bytes 196616 | tf_op jit(solution)/shard_map/ppermute | solution.py:526
  8.3 1.5 %collective-permute-start.5 = (bf16[2,128,128]{2,1,0:T(8,128)(2,1)S(1)}, bf16[2,128,128]{2,1,0:T(8,128)(2,1)S(1)}, u32[]{:S(2)}, u32[]{:S(2)}) collective-permute-start(bf16[2,128,128]{2,1,0:T(8,128)(2,1)S(1)} %get-tuple-element.49), channel_id=1, source_target_pairs={{0,12},{1,4},{2,14},{3,6},{4,8},{5,0},{6,10},{7,2},{8,20},{9,5},{1... | collective-permute-start | bytes 196616 | tf_op jit(solution)/shard_map/ppermute | solution.py:525
  10.5 0.1 collective-permute-start.8
  10.6 0.5 %collective-permute-done.2.over_y.refs_4_ = bf16[256,256]{1,0:T(8,128)(2,1)S(1)} collective-permute-done((bf16[256,256]{1,0:T(8,128)(2,1)S(1)}, bf16[256,256]{1,0:T(8,128)(2,1)S(1)}, u32[]{:S(2)}, u32[]{:S(2)}) %collective-permute-start.2) | collective-permute-done | bytes 131104 | tf_op jit(solution)/shard_map/ppermute | solution.py:491
  11.1 1.5 %collective-permute-start.3 = (bf16[256,256]{1,0:T(8,128)(2,1)S(1)}, bf16[256,256]{1,0:T(8,128)(2,1)S(1)}, u32[]{:S(2)}, u32[]{:S(2)}) collective-permute-start(bf16[256,256]{1,0:T(8,128)(2,1)S(1)} %collective-permute-done.2.over_y.refs_4_), channel_id=1, source_target_pairs={{0,8},{8,0},{16,24},{24,16},{1,9},{9,1},{17,25},{25,17},{2,10},{10... | collective-permute-start | bytes 393224 | tf_op jit(solution)/shard_map/ppermute | solution.py:522
  12.6 0.0 collective-permute-done.6.refs_5_
  12.7 1.2 %collective-permute-done.7.refs_2_ = bf16[2,128,128]{2,1,0:T(8,128)(2,1)S(1)} collective-permute-done((bf16[2,128,128]{2,1,0:T(8,128)(2,1)S(1)}, bf16[2,128,128]{2,1,0:T(8,128)(2,1)S(1)}, u32[]{:S(2)}, u32[]{:S(2)}) %collective-permute-start.7) | collective-permute-done | bytes 65568 | tf_op jit(solution)/shard_map/ppermute | solution.py:491
  13.9 2.1 %near.1 = (f32[2,256,256]{2,1,0:T(8,128)S(1)}, f32[4,256,512]{2,1,0:T(8,128)S(1)}, bf16[4,512,256]{2,1,0:T(8,128)(2,1)S(1)}, f32[2,256,256]{2,1,0:T(8,128)S(1)}) custom-call(s32[8,128]{1,0:T(8,128)S(1)} %get-tuple-element.46.spot_ref, bf16[2,128,256]{2,1,0:T(8,128)(2,1)S(1)} %get-tuple-element.40.refs_0_, ...), custom_call_target="tpu_custom_call" | custom-call | tf_op jit(solution)/shard_map/near/pallas_call | solution.py:550
  16.0 0.5 %collective-permute-done.3.over_z.refs_5_ = bf16[256,256]{1,0:T(8,128)(2,1)S(1)} collective-permute-done((bf16[256,256]{1,0:T(8,128)(2,1)S(1)}, bf16[256,256]{1,0:T(8,128)(2,1)S(1)}, u32[]{:S(2)}, u32[]{:S(2)}) %collective-permute-start.3) | collective-permute-done | bytes 131104 | tf_op jit(solution)/shard_map/ppermute | solution.py:522
  16.5 0.5 %collective-permute-start.9 = (bf16[256,256]{1,0:T(8,128)(2,1)S(1)}, bf16[256,256]{1,0:T(8,128)(2,1)S(1)}, u32[]{:S(2)}, u32[]{:S(2)}) collective-permute-start(bf16[256,256]{1,0:T(8,128)(2,1)S(1)} %collective-permute-done.2.over_y.refs_4_), channel_id=1, source_target_pairs={{0,1},{1,0},{2,3},{3,2},{4,5},{5,4},{6,7},{7,6},{8,9},{9,8},{10,11... | collective-permute-start | bytes 393224 | tf_op jit(solution)/shard_map/ppermute | solution.py:491
  17.0 0.0 collective-permute-start.10
  17.0 0.9 %over.1 = (f32[2,256,512]{2,1,0:T(8,128)S(1)}, bf16[2,512,256]{2,1,0:T(8,128)(2,1)S(1)}, f32[2,256,256]{2,1,0:T(8,128)S(1)}) custom-call(f32[2,256,256]{2,1,0:T(8,128)S(1)} %get-tuple-element.57.patch_ref.refs_1_, bf16[256,256]{1,0:T(8,128)(2,1)S(1)} %collective-permute-done.2.over_y.refs_4_, bf16[256,256]{1,0:T(8,128)(2,1)S(1)} %collective-permute-done.3.over_z.refs_5_, ...), custom_call_target="tpu_custom_call" | custom-call | tf_op jit(solution)/shard_map/over/pallas_call | solution.py:561
  17.9 0.3 collective-permute-done.9.refs_7_
  18.2 0.2 collective-permute-done.10.refs_8_
  18.4 4.3 %back.1 = (bf16[256,256]{1,0:T(8,128)(2,1)S(1)}, bf16[256,256]{1,0:T(8,128)(2,1)S(1)}, bf16[256,384]{1,0:T(8,128)(2,1)S(1)}, bf16[256,384]{1,0:T(8,128)(2,1)S(1)}, bf16[272,128]{1,0:T(8,128)(2,1)S(1)}) custom-call(bf16[16,256]{1,0:T(8,128)(2,1)S(1)} %live.1.record_ref, s32[8,128]{1,0:T(8,128)S(1)} %get-tuple-element.46.spot_ref, ...), custom_call_target="tpu_custom_call" | custom-call | tf_op jit(solution)/shard_map/back/pallas_call | solution.py:572
  22.8 0.2 collective-permute-start.12
  23.0 1.5 %collective-permute-start.14 = (bf16[272,128]{1,0:T(8,128)(2,1)S(1)}, bf16[272,128]{1,0:T(8,128)(2,1)S(1)}, u32[]{:S(2)}, u32[]{:S(2)}) collective-permute-start(bf16[272,128]{1,0:T(8,128)(2,1)S(1)} %get-tuple-element.72), channel_id=1, source_target_pairs={{0,4},{4,0},{1,5},{5,1},{2,6},{6,2},{3,7},{7,3},{8,12},{12,8},{9,1... | collective-permute-start | bytes 208904 | tf_op jit(solution)/shard_map/ppermute | solution.py:597
  24.5 0.1 meet.1
  24.5 1.8 %collective-permute-start.13 = (bf16[272,256]{1,0:T(8,128)(2,1)S(1)}, bf16[272,256]{1,0:T(8,128)(2,1)S(1)}, u32[]{:S(2)}, u32[]{:S(2)}) collective-permute-start(bf16[272,256]{1,0:T(8,128)(2,1)S(1)} %get-tuple-element.70), channel_id=1, source_target_pairs={{0,8},{1,0},{2,10},{3,2},{4,12},{5,4},{6,14},{7,6},{8,16},{9,1},{1... | collective-permute-start | bytes 417800 | tf_op jit(solution)/shard_map/ppermute | solution.py:609
  26.3 1.1 %collective-permute-done.14.refs_1_ = bf16[272,128]{1,0:T(8,128)(2,1)S(1)} collective-permute-done((bf16[272,128]{1,0:T(8,128)(2,1)S(1)}, bf16[272,128]{1,0:T(8,128)(2,1)S(1)}, u32[]{:S(2)}, u32[]{:S(2)}) %collective-permute-start.14) | collective-permute-done | bytes 69664 | tf_op jit(solution)/shard_map/ppermute | solution.py:597
  27.4 2.5 %collective-permute-start.15 = (bf16[272,128]{1,0:T(8,128)(2,1)S(1)}, bf16[272,128]{1,0:T(8,128)(2,1)S(1)}, u32[]{:S(2)}, u32[]{:S(2)}) collective-permute-start(bf16[272,128]{1,0:T(8,128)(2,1)S(1)} %get-tuple-element.73), channel_id=1, source_target_pairs={{0,12},{1,4},{2,14},{3,6},{4,8},{5,0},{6,10},{7,2},{8,20},{9,5},{1... | collective-permute-start | bytes 208904 | tf_op jit(solution)/shard_map/ppermute | solution.py:612
  29.9 2.0 %collective-permute-done.15.refs_0_ = bf16[272,128]{1,0:T(8,128)(2,1)S(1)} collective-permute-done((bf16[272,128]{1,0:T(8,128)(2,1)S(1)}, bf16[272,128]{1,0:T(8,128)(2,1)S(1)}, u32[]{:S(2)}, u32[]{:S(2)}) %collective-permute-start.15) | collective-permute-done | bytes 69664 | tf_op jit(solution)/shard_map/ppermute | solution.py:612
  31.9 0.6 %sums.1.own_ref = bf16[3,128,256]{2,1,0:T(8,128)(2,1)S(1)} custom-call(bf16[256,256]{1,0:T(8,128)(2,1)S(1)} %get-tuple-element.66.weight_ref, bf16[16,256]{1,0:T(8,128)(2,1)S(1)} %live.1.record_ref, bf16[256,256]{1,0:T(8,128)(2,1)S(1)} %get-tuple-element.67.own_ref, bf16[272,256]{1,0:T(8,128)(2,1)S(1)} %collective-permute-done.13.rows_ref, ...), custom_call_target="tpu_custom_call" | custom-call | tf_op jit(solution)/shard_map/sums/pallas_call | solution.py:614
  32.5 0.1 collective-permute-start.16
  32.6 1.4 %collective-permute-done.16.other_ref = bf16[3,128,256]{2,1,0:T(8,128)(2,1)S(1)} collective-permute-done((bf16[3,128,256]{2,1,0:T(8,128)(2,1)S(1)}, bf16[3,128,256]{2,1,0:T(8,128)(2,1)S(1)}, u32[]{:S(2)}, u32[]{:S(2)}) %collective-permute-start.16) | collective-permute-done | bytes 196640 | tf_op jit(solution)/shard_map/ppermute | solution.py:491
  34.0 0.8 %update.1 = f32[2,128,256]{2,1,0:T(8,128)} custom-call(f32[2,128,256]{2,1,0:T(8,128)S(1)} %copy-done, bf16[3,128,256]{2,1,0:T(8,128)(2,1)S(1)} %sums.1.own_ref, bf16[3,128,256]{2,1,0:T(8,128)(2,1)S(1)} %collective-permute-done.16.other_ref), custom_call_target="tpu_custom_call" | custom-call | tf_op jit(solution)/shard_map/update/pallas_call | solution.py:622
  (14 shorter events, 0.0 us)
Async XLA Ops:
  1.6 4.6 %collective-permute-start.1 = (bf16[2,2,256,256]{3,2,1,0:T(8,128)(2,1)S(1)}, bf16[2,2,256,256]{3,2,1,0:T(8,128)(2,1)S(1)}, u32[]{:S(2)}, u32[]{:S(2)}) collective-permute-start(bf16[2,2,256,256]{3,2,1,0:T(8,128)(2,1)S(1)} %get-tuple-element.42.refs_6_.refs_2_), channel_id=1, source_target_pairs={{0,1},{1,0},{2,3},{3,2},{4,5},{5,4},{6,7},{7,6},{8,9},{9,8},{10,11... | collective-permute-start | bytes 1572872 | tf_op jit(solution)/shard_map/ppermute | solution.py:491
  2.2 8.3 %collective-permute-start = (bf16[2,128,256]{2,1,0:T(8,128)(2,1)S(1)}, bf16[2,128,256]{2,1,0:T(8,128)(2,1)S(1)}, u32[]{:S(2)}, u32[]{:S(2)}) collective-permute-start(bf16[2,128,256]{2,1,0:T(8,128)(2,1)S(1)} %get-tuple-element.40.refs_0_), channel_id=1, source_target_pairs={{0,8},{1,0},{2,10},{3,2},{4,12},{5,4},{6,14},{7,6},{8,16},{9,1},{1... | collective-permute-start | bytes 393224 | tf_op jit(solution)/shard_map/ppermute | solution.py:524
  4.8 6.3 %collective-permute-start.2 = (bf16[256,256]{1,0:T(8,128)(2,1)S(1)}, bf16[256,256]{1,0:T(8,128)(2,1)S(1)}, u32[]{:S(2)}, u32[]{:S(2)}) collective-permute-start(bf16[256,256]{1,0:T(8,128)(2,1)S(1)} %get-tuple-element.47), channel_id=1, source_target_pairs={{0,2},{1,3},{2,0},{3,1},{4,6},{5,7},{6,4},{7,5},{8,10},{9,11},{10,... | collective-permute-start | bytes 393224 | tf_op jit(solution)/shard_map/ppermute | solution.py:491
  6.3 10.2 %collective-permute-start.4 = (bf16[2,1,256,256]{3,2,1,0:T(8,128)(2,1)S(1)}, bf16[2,1,256,256]{3,2,1,0:T(8,128)(2,1)S(1)}, u32[]{:S(2)}, u32[]{:S(2)}) collective-permute-start(bf16[2,1,256,256]{3,2,1,0:T(8,128)(2,1)S(1)} %get-tuple-element.48), channel_id=1, source_target_pairs={{0,2},{1,3},{2,0},{3,1},{4,6},{5,7},{6,4},{7,5},{8,10},{9,11},{10,... | collective-permute-start | bytes 786440 | tf_op jit(solution)/shard_map/ppermute | solution.py:491
  6.8 5.9 %collective-permute-start.6 = (bf16[2,128,128]{2,1,0:T(8,128)(2,1)S(1)}, bf16[2,128,128]{2,1,0:T(8,128)(2,1)S(1)}, u32[]{:S(2)}, u32[]{:S(2)}) collective-permute-start(bf16[2,128,128]{2,1,0:T(8,128)(2,1)S(1)} %get-tuple-element.49), channel_id=1, source_target_pairs={{0,4},{4,0},{1,5},{5,1},{2,6},{6,2},{3,7},{7,3},{8,12},{12,8},{9,1... | collective-permute-start | bytes 196616 | tf_op jit(solution)/shard_map/ppermute | solution.py:526
  8.3 4.4 %collective-permute-start.5 = (bf16[2,128,128]{2,1,0:T(8,128)(2,1)S(1)}, bf16[2,128,128]{2,1,0:T(8,128)(2,1)S(1)}, u32[]{:S(2)}, u32[]{:S(2)}) collective-permute-start(bf16[2,128,128]{2,1,0:T(8,128)(2,1)S(1)} %get-tuple-element.49), channel_id=1, source_target_pairs={{0,12},{1,4},{2,14},{3,6},{4,8},{5,0},{6,10},{7,2},{8,20},{9,5},{1... | collective-permute-start | bytes 196616 | tf_op jit(solution)/shard_map/ppermute | solution.py:525
  10.5 3.4 %collective-permute-start.8 = (bf16[2,128,256]{2,1,0:T(8,128)(2,1)S(1)}, bf16[2,128,256]{2,1,0:T(8,128)(2,1)S(1)}, u32[]{:S(2)}, u32[]{:S(2)}) collective-permute-start(bf16[2,128,256]{2,1,0:T(8,128)(2,1)S(1)} %collective-permute-done.refs_3_), channel_id=1, source_target_pairs={{0,1},{1,0},{2,3},{3,2},{4,5},{5,4},{6,7},{7,6},{8,9},{9,8},{10,11... | collective-permute-start | bytes 393224 | tf_op jit(solution)/shard_map/ppermute | solution.py:491
  11.1 5.4 %collective-permute-start.3 = (bf16[256,256]{1,0:T(8,128)(2,1)S(1)}, bf16[256,256]{1,0:T(8,128)(2,1)S(1)}, u32[]{:S(2)}, u32[]{:S(2)}) collective-permute-start(bf16[256,256]{1,0:T(8,128)(2,1)S(1)} %collective-permute-done.2.over_y.refs_4_), channel_id=1, source_target_pairs={{0,8},{8,0},{16,24},{24,16},{1,9},{9,1},{17,25},{25,17},{2,10},{10... | collective-permute-start | bytes 393224 | tf_op jit(solution)/shard_map/ppermute | solution.py:522
  12.7 1.3 %collective-permute-start.7 = (bf16[2,128,128]{2,1,0:T(8,128)(2,1)S(1)}, bf16[2,128,128]{2,1,0:T(8,128)(2,1)S(1)}, u32[]{:S(2)}, u32[]{:S(2)}) collective-permute-start(bf16[2,128,128]{2,1,0:T(8,128)(2,1)S(1)} %collective-permute-done.5.refs_1_), channel_id=1, source_target_pairs={{0,1},{1,0},{2,3},{3,2},{4,5},{5,4},{6,7},{7,6},{8,9},{9,8},{10,11... | collective-permute-start | bytes 196616 | tf_op jit(solution)/shard_map/ppermute | solution.py:491
  13.9 4.5 %copy-start.1 = (bf16[1,1,2,256,256]{4,3,2,1,0:T(8,128)(2,1)S(1)}, bf16[1,1,2,256,256]{4,3,2,1,0:T(8,128)(2,1)}, u32[]{:S(2)}) copy-start(bf16[1,1,2,256,256]{4,3,2,1,0:T(8,128)(2,1)} %refs_0_.1) | copy-start | bytes 786436
  16.5 1.9 %collective-permute-start.11 = (bf16[2,1,256,256]{3,2,1,0:T(8,128)(2,1)S(1)}, bf16[2,1,256,256]{3,2,1,0:T(8,128)(2,1)S(1)}, u32[]{:S(2)}, u32[]{:S(2)}) collective-permute-start(bf16[2,1,256,256]{3,2,1,0:T(8,128)(2,1)S(1)} %collective-permute-done.4.rest.refs_6_), channel_id=1, source_target_pairs={{0,1},{1,0},{2,3},{3,2},{4,5},{5,4},{6,7},{7,6},{8,9},{9,8},{10,11... | collective-permute-start | bytes 786440 | tf_op jit(solution)/shard_map/ppermute | solution.py:491
  16.5 1.7 %collective-permute-start.9 = (bf16[256,256]{1,0:T(8,128)(2,1)S(1)}, bf16[256,256]{1,0:T(8,128)(2,1)S(1)}, u32[]{:S(2)}, u32[]{:S(2)}) collective-permute-start(bf16[256,256]{1,0:T(8,128)(2,1)S(1)} %collective-permute-done.2.over_y.refs_4_), channel_id=1, source_target_pairs={{0,1},{1,0},{2,3},{3,2},{4,5},{5,4},{6,7},{7,6},{8,9},{9,8},{10,11... | collective-permute-start | bytes 393224 | tf_op jit(solution)/shard_map/ppermute | solution.py:491
  17.0 1.4 %collective-permute-start.10 = (bf16[256,256]{1,0:T(8,128)(2,1)S(1)}, bf16[256,256]{1,0:T(8,128)(2,1)S(1)}, u32[]{:S(2)}, u32[]{:S(2)}) collective-permute-start(bf16[256,256]{1,0:T(8,128)(2,1)S(1)} %collective-permute-done.3.over_z.refs_5_), channel_id=1, source_target_pairs={{0,1},{1,0},{2,3},{3,2},{4,5},{5,4},{6,7},{7,6},{8,9},{9,8},{10,11... | collective-permute-start | bytes 393224 | tf_op jit(solution)/shard_map/ppermute | solution.py:491
  18.4 15.6 %copy-start = (f32[2,128,256]{2,1,0:T(8,128)S(1)}, f32[2,128,256]{2,1,0:T(8,128)}, u32[]{:S(2)}) copy-start(f32[2,128,256]{2,1,0:T(8,128)} %object_ref.1) | copy-start | bytes 786436
  22.8 1.7 %collective-permute-start.12 = (bf16[256,384]{1,0:T(8,128)(2,1)S(1)}, bf16[256,384]{1,0:T(8,128)(2,1)S(1)}, u32[]{:S(2)}, u32[]{:S(2)}) collective-permute-start(bf16[256,384]{1,0:T(8,128)(2,1)S(1)} %get-tuple-element.69), channel_id=1, source_target_pairs={{0,1},{1,0},{2,3},{3,2},{4,5},{5,4},{6,7},{7,6},{8,9},{9,8},{10,11... | collective-permute-start | bytes 589832 | tf_op jit(solution)/shard_map/ppermute | solution.py:491
  23.0 4.5 %collective-permute-start.14 = (bf16[272,128]{1,0:T(8,128)(2,1)S(1)}, bf16[272,128]{1,0:T(8,128)(2,1)S(1)}, u32[]{:S(2)}, u32[]{:S(2)}) collective-permute-start(bf16[272,128]{1,0:T(8,128)(2,1)S(1)} %get-tuple-element.72), channel_id=1, source_target_pairs={{0,4},{4,0},{1,5},{5,1},{2,6},{6,2},{3,7},{7,3},{8,12},{12,8},{9,1... | collective-permute-start | bytes 208904 | tf_op jit(solution)/shard_map/ppermute | solution.py:597
  24.5 7.4 %collective-permute-start.13 = (bf16[272,256]{1,0:T(8,128)(2,1)S(1)}, bf16[272,256]{1,0:T(8,128)(2,1)S(1)}, u32[]{:S(2)}, u32[]{:S(2)}) collective-permute-start(bf16[272,256]{1,0:T(8,128)(2,1)S(1)} %get-tuple-element.70), channel_id=1, source_target_pairs={{0,8},{1,0},{2,10},{3,2},{4,12},{5,4},{6,14},{7,6},{8,16},{9,1},{1... | collective-permute-start | bytes 417800 | tf_op jit(solution)/shard_map/ppermute | solution.py:609
  27.4 4.5 %collective-permute-start.15 = (bf16[272,128]{1,0:T(8,128)(2,1)S(1)}, bf16[272,128]{1,0:T(8,128)(2,1)S(1)}, u32[]{:S(2)}, u32[]{:S(2)}) collective-permute-start(bf16[272,128]{1,0:T(8,128)(2,1)S(1)} %get-tuple-element.73), channel_id=1, source_target_pairs={{0,12},{1,4},{2,14},{3,6},{4,8},{5,0},{6,10},{7,2},{8,20},{9,5},{1... | collective-permute-start | bytes 208904 | tf_op jit(solution)/shard_map/ppermute | solution.py:612
  32.5 1.5 %collective-permute-start.16 = (bf16[3,128,256]{2,1,0:T(8,128)(2,1)S(1)}, bf16[3,128,256]{2,1,0:T(8,128)(2,1)S(1)}, u32[]{:S(2)}, u32[]{:S(2)}) collective-permute-start(bf16[3,128,256]{2,1,0:T(8,128)(2,1)S(1)} %sums.1.own_ref), channel_id=1, source_target_pairs={{0,1},{1,0},{2,3},{3,2},{4,5},{5,4},{6,7},{7,6},{8,9},{9,8},{10,11... | collective-permute-start | bytes 589832 | tf_op jit(solution)/shard_map/ppermute | solution.py:491

commit v11 on v10

--- a/solution.py
+++ b/solution.py
@@ -267,24 +267,23 @@
 def near_kernel(sides, z_count, x_count, spot_ref, *refs):
     n_pieces = 3 + 3 * sides
     pieces = from_sent_order(refs[:n_pieces])
-    own, core, direct, swapped = refs[n_pieces : n_pieces + 4]
-    patch_ref, far_ref, exit_ref, sum_ref = refs[n_pieces + 4 :]
+    own, direct, swapped = refs[n_pieces : n_pieces + 3]
+    patch_ref, far_ref, exit_ref, sum_ref = refs[n_pieces + 3 :]
     side = own.shape[2]
     patch = patch_of(sides, z_count, x_count, side, spot_ref, pieces)
     patch_ref[0], patch_ref[1] = patch
+    sum_ref[0], sum_ref[1] = forward(
+        modes_of(own), patch, direct[...], swapped[...], far_ref, exit_ref, 0
+    )
+
+
+def over_kernel(patch_ref, core, over_y, over_z, rest, direct, swapped, far_ref, exit_ref, sum_ref):
+    patch = (patch_ref[0], patch_ref[1])
     tables = (direct[...], swapped[...], far_ref, exit_ref)
-    first = forward(modes_of(own), patch, *tables, 0)
-    second = forward(modes_of(core), patch, *tables, own.shape[1])
-    sum_ref[0] = first[0] + second[0]
-    sum_ref[1] = first[1] + second[1]
-
-
-def over_kernel(patch_ref, over_y, over_z, rest, direct, swapped, far_ref, exit_ref, sum_ref):
-    patch = (patch_ref[0], patch_ref[1])
-    modes = [shared_mode(over_y, over_z)] + modes_of(rest)
-    sum_ref[0], sum_ref[1] = forward(
-        modes, patch, direct[...], swapped[...], far_ref, exit_ref, 0
-    )
+    modes = modes_of(core)
+    sum_ref[0], sum_ref[1] = forward(modes, patch, *tables, 0)
+    over_modes = [shared_mode(over_y, over_z)] + modes_of(rest)
+    sum_ref[2], sum_ref[3] = forward(over_modes, patch, *tables, len(modes))
 
 
 def back_kernel(sides, slots, tile_cols, record_ref, spot_ref, *refs):
@@ -306,8 +305,8 @@
     swapped = swapped_ref[...]
     patch = (patch_ref[0], patch_ref[1])
     power, weight = forward(last_modes, patch, direct, swapped, last_far, last_exit, 0)
-    power = near_sum[0] + (over_sum[0] + power)
-    weight = near_sum[1] + (over_sum[1] + weight)
+    power = (near_sum[0] + over_sum[0]) + (over_sum[2] + power)
+    weight = (near_sum[1] + over_sum[1]) + (over_sum[3] + weight)
     weight_out[...] = weight.astype(jnp.bfloat16)
     amplitude = amplitude_ref[0, 0, parity].astype(jnp.float32)
     factor = amplitude / jnp.sqrt(power + power_floor)
@@ -315,8 +314,8 @@
     tables = (factor, direct, swapped)
     grads = [
         backward(modes_of(own), *tables, near_far, near_exit, 0),
-        backward(modes_of(core), *tables, near_far, near_exit, modes),
-        backward(over_modes, *tables, over_far, over_exit, 0),
+        backward(modes_of(core), *tables, over_far, over_exit, 0),
+        backward(over_modes, *tables, over_far, over_exit, modes),
         backward(last_modes, *tables, last_far, last_exit, 0),
     ]
     even = parity == 0
@@ -362,68 +361,89 @@
         at += width
 
 
-def sum_kernel(sides, slots, z_count, x_count, weight_ref, record_ref, own_ref, rows_ref, *refs):
-    corners, levels, out_ref = refs[:sides], refs[sides:-1], refs[-1]
-    _, tile_rows, tile_cols = out_ref.shape
-    side = weight_ref.shape[0]
+def placed_weight(weight, position, z_step, x_step, shown, shape):
+    tile_rows, tile_cols = shape
+    side = weight.shape[0]
     half = side // 2
-    z_index, x_index, parity = here()
+    row, col, is_live = position
+    row = jnp.where(is_live & shown, row + (z_step * tile_rows - half), nowhere)
+    col = col + (x_step * tile_cols - half)
+    put_rows = (iota((tile_rows, side), 0) == iota((tile_rows, side), 1) + row).astype(jnp.bfloat16)
+    put_cols = (iota((side, tile_cols), 1) == iota((side, tile_cols), 0) + col).astype(jnp.bfloat16)
+    return dot(dot(put_rows, weight).astype(jnp.bfloat16), put_cols)
+
+
+def beside(sides, x_count):
+    z_index, x_index, _ = here()
+    if sides == 1:
+        return [jnp.where(x_index == 0, 1, -1)], [z_index >= 0]
+    return [1, -1], [x_index < x_count - 1, x_index > 0]
+
+
+def edges_added(inner, edges, sides, shown):
+    _, x_index, _ = here()
+    half = edges[0].shape[1]
+    first = jnp.zeros(edges[0].shape, jnp.float32)
+    last = first
+    for index, edge in enumerate(edges):
+        if sides == 1:
+            first = jnp.where(x_index == 1, edge, 0.0)
+            last = jnp.where(x_index == 0, edge, 0.0)
+        elif index == 0:
+            last = jnp.where(shown[0], edge, 0.0)
+        else:
+            first = jnp.where(shown[1], edge, 0.0)
+    middle = inner.shape[1] - 2 * half
+    parts = [inner[:, :half] + first]
+    if middle:
+        parts.append(inner[:, half : half + middle])
+    parts.append(inner[:, half + middle :] + last)
+    return jnp.concatenate(parts, axis=1)
+
+
+def level_kernel(sides, slots, x_count, weight_ref, record_ref, own_ref, *refs):
+    levels, out_ref = refs[:sides], refs[-1]
+    shape = out_ref.shape[1:]
+    half = levels[0].shape[1]
+    z_index, _, parity = here()
+    x_steps, shown = beside(sides, x_count)
+    weight = weight_ref[...]
+    position = position_of(record_ref, slots, parity)
+    total = placed_weight(weight, position, 0, 0, z_index >= 0, shape)
+    for level, x_step, is_shown in zip(levels, x_steps, shown):
+        position = position_of(level[2 * half :], slots, parity)
+        total = total + placed_weight(weight, position, 0, x_step, is_shown, shape)
+    out_ref[2] = total
+    for channel in range(2):
+        rows = slice(channel * half, (channel + 1) * half)
+        edges = [level[rows].astype(jnp.float32) for level in levels]
+        out_ref[channel] = edges_added(own_ref[rows].astype(jnp.float32), edges, sides, shown)
+
+
+def sum_kernel(sides, slots, z_count, x_count, weight_ref, level_ref, rows_ref, *refs):
+    corners, out_ref = refs[:sides], refs[-1]
+    shape = out_ref.shape[1:]
+    half = corners[0].shape[1]
+    z_index, _, parity = here()
     z_step = jnp.where(parity == 0, -1, 1)
     z_shown = jnp.where(parity == 0, z_index > 0, z_index < z_count - 1)
-    if sides == 1:
-        x_steps = [jnp.where(x_index == 0, 1, -1)]
-        x_shown = [z_index >= 0]
-    else:
-        x_steps = [1, -1]
-        x_shown = [x_index < x_count - 1, x_index > 0]
+    x_steps, shown = beside(sides, x_count)
     weight = weight_ref[...]
-
-    def placed(position, z_step, x_step, shown):
-        row, col, is_live = position
-        row = jnp.where(is_live & shown, row + (z_step * tile_rows - half), nowhere)
-        col = col + (x_step * tile_cols - half)
-        put_rows = (iota((tile_rows, side), 0) == iota((tile_rows, side), 1) + row).astype(
-            jnp.bfloat16
-        )
-        put_cols = (iota((side, tile_cols), 1) == iota((side, tile_cols), 0) + col).astype(
-            jnp.bfloat16
-        )
-        return dot(dot(put_rows, weight).astype(jnp.bfloat16), put_cols)
-
-    total = placed(position_of(record_ref, slots, parity), 0, 0, z_index >= 0)
-    for level, x_step, shown in zip(levels, x_steps, x_shown):
-        record = level[2 * half :]
-        total = total + placed(position_of(record, slots, parity), 0, x_step, shown)
-    for piece, x_step, shown in zip(
-        (rows_ref,) + corners, [0] + x_steps, [z_index >= 0] + x_shown
+    total = level_ref[2]
+    for piece, x_step, is_shown in zip(
+        (rows_ref,) + corners, [0] + x_steps, [z_index >= 0] + shown
     ):
-        record = piece[2 * half :]
         for slot in range(slots):
-            position = position_of(record, slots, slot)
-            total = total + placed(position, z_step, x_step, shown & z_shown)
+            position = position_of(piece[2 * half :], slots, slot)
+            total = total + placed_weight(
+                weight, position, z_step, x_step, is_shown & z_shown, shape
+            )
     out_ref[2] = total.astype(jnp.bfloat16)
-
     for channel in range(2):
-        rows = slice(channel * tile_rows, (channel + 1) * tile_rows)
-
-        def values(ref, rows=rows):
-            return ref[rows].astype(jnp.float32)
-
-        total = values(own_ref) + jnp.where(z_shown, values(rows_ref), 0.0)
-        first = jnp.zeros((tile_rows, half), jnp.float32)
-        last = first
-        for index in range(sides):
-            edge = values(levels[index]) + jnp.where(z_shown, values(corners[index]), 0.0)
-            if sides == 1:
-                first = jnp.where(x_index == 1, edge, 0.0)
-                last = jnp.where(x_index == 0, edge, 0.0)
-            elif index == 0:
-                last = jnp.where(x_shown[0], edge, 0.0)
-            else:
-                first = jnp.where(x_shown[1], edge, 0.0)
-        zero = jnp.zeros((tile_rows, tile_cols - 2 * half), jnp.float32)
-        parts = [first, zero, last] if tile_cols > 2 * half else [first, last]
-        total = total + jnp.concatenate(parts, axis=1)
+        rows = slice(channel * half, (channel + 1) * half)
+        edges = [corner[rows].astype(jnp.float32) for corner in corners]
+        above = edges_added(rows_ref[rows].astype(jnp.float32), edges, sides, shown)
+        total = level_ref[channel] + jnp.where(z_shown, above, 0.0)
         out_ref[channel] = total.astype(jnp.bfloat16)
 
 
@@ -432,6 +452,10 @@
     for channel in range(2):
         gradient = own_ref[channel].astype(jnp.float32) + other_ref[channel].astype(jnp.float32)
         out_ref[channel] = object_ref[channel] + gradient / weight
+
+
+def cost(products):
+    return pl.CostEstimate(flops=products * 2 * 256**3, bytes_accessed=0, transcendentals=0)
 
 
 def in_hbm(array):
@@ -516,56 +540,59 @@
         name="start",
     )(*(in_hbm(array) for array in (object_field, probe, centers, *tables)))
     over_y = exchange(shared, 2)
-    probe_core = exchange(probe_low, 1)
-    probe_core, rest, live = lax.optimization_barrier((probe_core, rest, live))
     rest = exchange(rest, 2)
     over_z = lax.ppermute(over_y, "tx", [(z, z ^ 1) for z in range(z_count)])
     x_steps = [1] if sides == 1 else [1, -1]
     rows = lax.ppermute(packed[0], axes, zigzag(0))
     corners = [lax.ppermute(edge, axes, zigzag(step)) for step, edge in zip(x_steps, packed[1:])]
     levels = [lax.ppermute(edge, "ty", level(step)) for step, edge in zip(x_steps, packed[1:])]
+    probe_core = exchange(probe_low, 1)
+    corners, record = lax.optimization_barrier((corners, record))
     record = pl.pallas_call(
         functools.partial(live_kernel, slots),
         out_shape=jax.ShapeDtypeStruct(record.shape, jnp.bfloat16),
         in_specs=[vmem(), smem()],
         out_specs=vmem(),
         compiler_params=pltpu.CompilerParams(vmem_limit_bytes=small_bytes),
+        cost_estimate=cost(80),
         name="live",
     )(record, live)
-    rows, record = lax.optimization_barrier((rows, record))
-    corners, levels = lax.optimization_barrier((corners, levels))
+    corners, record = lax.optimization_barrier((corners, record))
     pieces = [packed[0], rows, exchange(rows, 1)]
     for at_level, corner in zip(levels, corners):
         pieces += [at_level, corner, exchange(corner, 1)]
     n_pieces = len(pieces)
     ext_cols = tile_cols + sides * half
 
-    def waves(count):
+    def waves(groups):
+        count = groups * modes
         return [
             jax.ShapeDtypeStruct((count, side, 2 * side), jnp.float32),
             jax.ShapeDtypeStruct((count, 2 * side, side), jnp.bfloat16),
-            jax.ShapeDtypeStruct((2, side, side), jnp.float32),
+            jax.ShapeDtypeStruct((2 * groups, side, side), jnp.float32),
         ]
 
     patch, *near = pl.pallas_call(
         functools.partial(near_kernel, sides, z_count, x_count),
-        out_shape=[jax.ShapeDtypeStruct((2, side, side), jnp.float32)] + waves(2 * modes),
-        in_specs=[vmem()] * (n_pieces + 5),
+        out_shape=[jax.ShapeDtypeStruct((2, side, side), jnp.float32)] + waves(1),
+        in_specs=[vmem()] * (n_pieces + 4),
         out_specs=[vmem()] * 4,
         compiler_params=pltpu.CompilerParams(vmem_limit_bytes=wave_bytes),
+        cost_estimate=cost(20),
         name="near",
-    )(spot, *in_sent_order(pieces), probe_low, probe_core, direct, swapped)
+    )(spot, *in_sent_order(pieces), probe_low, direct, swapped)
     over_z, rest, patch = lax.optimization_barrier((over_z, rest, patch))
     over_group = (over_y, over_z, rest)
     last_group = [exchange(part, 1) for part in over_group]
     over = pl.pallas_call(
         over_kernel,
-        out_shape=waves(modes),
-        in_specs=[vmem()] * 6,
+        out_shape=waves(2),
+        in_specs=[vmem()] * 7,
         out_specs=[vmem()] * 3,
         compiler_params=pltpu.CompilerParams(vmem_limit_bytes=wave_bytes),
+        cost_estimate=cost(32),
         name="over",
-    )(patch, *over_group, direct, swapped)
+    )(patch, probe_core, *over_group, direct, swapped)
     piece_rows = 2 * half + record_rows
     shapes = [(side, side), (2 * half, tile_cols)] + [(2 * half, ext_cols)] * 2
     shapes += [(piece_rows, half)] * sides
@@ -579,6 +606,7 @@
             pltpu.VMEM((modes, 2 * side, side), jnp.bfloat16),
         ],
         compiler_params=pltpu.CompilerParams(vmem_limit_bytes=wave_bytes),
+        cost_estimate=cost(80),
         name="back",
     )(
         record,
@@ -607,18 +635,26 @@
         name="meet",
     )(record, keep, exchange(swap, 1))
     rows = lax.ppermute(rows, axes, zigzag(0))
-    corners, levels = lax.optimization_barrier((corners, levels))
     corners = [
         lax.ppermute(piece, axes, zigzag(-step)) for piece, step in zip(corners, x_steps)
     ]
+    leveled = pl.pallas_call(
+        functools.partial(level_kernel, sides, slots, x_count),
+        out_shape=jax.ShapeDtypeStruct((3, tile_rows, tile_cols), jnp.float32),
+        in_specs=[vmem()] * (3 + sides),
+        out_specs=vmem(),
+        compiler_params=pltpu.CompilerParams(vmem_limit_bytes=small_bytes),
+        cost_estimate=cost(80),
+        name="levels",
+    )(weight, record, own, *levels)
     summed = pl.pallas_call(
         functools.partial(sum_kernel, sides, slots, z_count, x_count),
         out_shape=jax.ShapeDtypeStruct((3, tile_rows, tile_cols), jnp.bfloat16),
-        in_specs=[vmem()] * (4 + 2 * sides),
+        in_specs=[vmem()] * (3 + sides),
         out_specs=vmem(),
         compiler_params=pltpu.CompilerParams(vmem_limit_bytes=small_bytes),
         name="sums",
-    )(weight, record, own, rows, *corners, *levels)
+    )(weight, leveled, rows, *corners)
     return pl.pallas_call(
         update_kernel,
         out_shape=jax.ShapeDtypeStruct(object_field.shape, jnp.float32),

time: 34.9 us -> 35 us (level)
  waiting for transfers between devices: 7.3 us -> 5.91 us
  starting transfers between devices: 16.4 us -> 17.6 us
    ppermute x1, waiting for transfers between devices: 0.01 us -> 1.94 us  [on_device(): rows = lax.ppermute(rows, axes, zigzag(0))]
    ppermute x10, starting transfers between devices: 3.4 us -> 5.28 us  [exchange(): return lax.ppermute(array, 'mode', [(m, m ^ flip) for m in range(m_count)])]
    ppermute x1, waiting for transfers between devices: 1.98 us -> 0.23 us  [on_device(): lax.ppermute(piece, axes, zigzag(-step))]
    ppermute x10, waiting for transfers between devices: 3.69 us -> 2.42 us  [exchange(): return lax.ppermute(array, 'mode', [(m, m ^ flip) for m in range(m_count)])]
    ppermute x1, waiting for transfers between devices: 1.13 us -> 0.01 us  [on_device(): lax.ppermute(piece, 'ty', level(-step))]
    ppermute x1, starting transfers between devices: 2.6 us -> 1.58 us  [on_device(): rows = lax.ppermute(packed[0], axes, zigzag(0))]
    ppermute x1, starting transfers between devices: 1.55 us -> 2.5 us  [on_device(): lax.ppermute(edge, axes, zigzag(step))]
    ppermute x1, starting transfers between devices: 1.49 us -> 0.54 us  [on_device(): lax.ppermute(edge, 'ty', level(step))]
  transfers between devices with their start and end apart: 17 -> 17, of which waited for: 8 -> 6; matrix products, arithmetic and copies ran while one was open for 0% -> 0% of each run, Pallas kernels for 9% -> 10%
where the time goes in v11:
time: 35 us; the launch traced here: 34.9 us
  starting transfers between devices  17.6 us (50%)
  Pallas kernels  10.6 us (30%)
  waiting for transfers between devices  5.91 us (17%)
  between operations  0.76 us (2%)
    ppermute x10, starting transfers between devices, exchange(): return lax.ppermute(array, 'mode', [(m, m ^ flip) for m in range(m_count)])  5.28 us
    pallas_call x1, Pallas kernels, on_device(): pl.pallas_call(functools.partial(back_kernel, sides, slots, tile_cols), o...  4.33 us
    ppermute x1, starting transfers between devices, on_device(): lax.ppermute(edge, axes, zigzag(step))  2.5 us
    ppermute x10, waiting for transfers between devices, exchange(): return lax.ppermute(array, 'mode', [(m, m ^ flip) for m in range(m_count)])  2.42 us
    ppermute x1, starting transfers between devices, on_device(): over_z = lax.ppermute(over_y, 'tx', [(z, z ^ 1) for z in range(z_count)])  2.33 us
    ppermute x1, starting transfers between devices, on_device(): lax.ppermute(piece, axes, zigzag(-step))  2.31 us
    ppermute x1, waiting for transfers between devices, on_device(): rows = lax.ppermute(rows, axes, zigzag(0))  1.94 us
    pallas_call x1, Pallas kernels, on_device(): pl.pallas_call(functools.partial(start_kernel, sides, slots), out_shape=[...  1.64 us
  transfers between devices with their start and end apart: 17, of which 6 were waited for; matrix products, arithmetic and copies ran while one was open for 0% of the time, Pallas kernels for 10%

profile of v11, /device:TPU:0, one launch (start us, length us, event | category | flops | bytes accessed | tf_op | source)
XLA Modules:
  0.0 34.9 jit_solution(12626466136698730749)
XLA Ops:
  0.0 1.6 %start.1 = (bf16[2,2,256,256]{3,2,1,0:T(8,128)(2,1)S(1)}, bf16[256,256]{1,0:T(8,128)(2,1)S(1)}, bf16[2,1,256,256]{3,2,1,0:T(8,128)(2,1)S(1)}, bf16[16,256]{1,0:T...) custom-call(f32[2,128,256]{2,1,0:T(8,128)} %object_ref.1, ...), custom_call_target="tpu_custom_call" | custom-call | tf_op jit(solution)/shard_map/start/pallas_call | solution.py:518
  1.6 3.0 %collective-permute-start.1 = (bf16[256,256]{1,0:T(8,128)(2,1)S(1)}, bf16[256,256]{1,0:T(8,128)(2,1)S(1)}, u32[]{:S(2)}, u32[]{:S(2)}) collective-permute-start(bf16[256,256]{1,0:T(8,128)(2,1)S(1)} %get-tuple-element.41), channel_id=1, source_target_pairs={{0,2},{1,3},{2,0},{3,1},{4,6},{5,7},{6,4},{7,5},{8,10},{9,11},{10,... | collective-permute-start | bytes 393224 | tf_op jit(solution)/shard_map/ppermute | solution.py:515
  4.7 1.6 %collective-permute-start.5 = (bf16[2,128,256]{2,1,0:T(8,128)(2,1)S(1)}, bf16[2,128,256]{2,1,0:T(8,128)(2,1)S(1)}, u32[]{:S(2)}, u32[]{:S(2)}) collective-permute-start(bf16[2,128,256]{2,1,0:T(8,128)(2,1)S(1)} %get-tuple-element.43.refs_0_), channel_id=1, source_target_pairs={{0,8},{1,0},{2,10},{3,2},{4,12},{5,4},{6,14},{7,6},{8,16},{9,1},{1... | collective-permute-start | bytes 393224 | tf_op jit(solution)/shard_map/ppermute | solution.py:546
  6.3 2.5 %collective-permute-start = (bf16[2,128,128]{2,1,0:T(8,128)(2,1)S(1)}, bf16[2,128,128]{2,1,0:T(8,128)(2,1)S(1)}, u32[]{:S(2)}, u32[]{:S(2)}) collective-permute-start(bf16[2,128,128]{2,1,0:T(8,128)(2,1)S(1)} %get-tuple-element.35), channel_id=1, source_target_pairs={{0,12},{1,4},{2,14},{3,6},{4,8},{5,0},{6,10},{7,2},{8,20},{9,5},{1... | collective-permute-start | bytes 196616 | tf_op jit(solution)/shard_map/ppermute | solution.py:547
  8.8 0.5 %collective-permute-start.7 = (bf16[2,128,128]{2,1,0:T(8,128)(2,1)S(1)}, bf16[2,128,128]{2,1,0:T(8,128)(2,1)S(1)}, u32[]{:S(2)}, u32[]{:S(2)}) collective-permute-start(bf16[2,128,128]{2,1,0:T(8,128)(2,1)S(1)} %get-tuple-element.35), channel_id=1, source_target_pairs={{0,4},{4,0},{1,5},{5,1},{2,6},{6,2},{3,7},{7,3},{8,12},{12,8},{9,1... | collective-permute-start | bytes 196616 | tf_op jit(solution)/shard_map/ppermute | solution.py:548
  9.3 0.5 %collective-permute-start.3 = (bf16[2,1,256,256]{3,2,1,0:T(8,128)(2,1)S(1)}, bf16[2,1,256,256]{3,2,1,0:T(8,128)(2,1)S(1)}, u32[]{:S(2)}, u32[]{:S(2)}) collective-permute-start(bf16[2,1,256,256]{3,2,1,0:T(8,128)(2,1)S(1)} %get-tuple-element.42), channel_id=1, source_target_pairs={{0,2},{1,3},{2,0},{3,1},{4,6},{5,7},{6,4},{7,5},{8,10},{9,11},{10,... | collective-permute-start | bytes 786440 | tf_op jit(solution)/shard_map/ppermute | solution.py:515
  10.5 0.2 collective-permute-done.refs_1_
  10.7 0.0 collective-permute-start.8
  10.7 0.0 collective-permute-done.1.over_y.refs_4_
  10.7 2.3 %collective-permute-start.2 = (bf16[256,256]{1,0:T(8,128)(2,1)S(1)}, bf16[256,256]{1,0:T(8,128)(2,1)S(1)}, u32[]{:S(2)}, u32[]{:S(2)}) collective-permute-start(bf16[256,256]{1,0:T(8,128)(2,1)S(1)} %collective-permute-done.1.over_y.refs_4_), channel_id=1, source_target_pairs={{0,8},{8,0},{16,24},{24,16},{1,9},{9,1},{17,25},{25,17},{2,10},{10... | collective-permute-start | bytes 393224 | tf_op jit(solution)/shard_map/ppermute | solution.py:544
  13.0 0.2 collective-permute-start.6
  13.2 0.3 %collective-permute-start.4 = (bf16[2,128,128]{2,1,0:T(8,128)(2,1)S(1)}, bf16[2,128,128]{2,1,0:T(8,128)(2,1)S(1)}, u32[]{:S(2)}, u32[]{:S(2)}) collective-permute-start(bf16[2,128,128]{2,1,0:T(8,128)(2,1)S(1)} %collective-permute-done.refs_1_), channel_id=1, source_target_pairs={{0,1},{1,0},{2,3},{3,2},{4,5},{5,4},{6,7},{7,6},{8,9},{9,8},{10,11... | collective-permute-start | bytes 196616 | tf_op jit(solution)/shard_map/ppermute | solution.py:515
  13.6 1.0 %collective-permute-done.4.refs_2_ = bf16[2,128,128]{2,1,0:T(8,128)(2,1)S(1)} collective-permute-done((bf16[2,128,128]{2,1,0:T(8,128)(2,1)S(1)}, bf16[2,128,128]{2,1,0:T(8,128)(2,1)S(1)}, u32[]{:S(2)}, u32[]{:S(2)}) %collective-permute-start.4) | collective-permute-done | bytes 65568 | tf_op jit(solution)/shard_map/ppermute | solution.py:515
  14.6 1.5 %near.1 = (f32[2,256,256]{2,1,0:T(8,128)S(1)}, f32[2,256,512]{2,1,0:T(8,128)S(1)}, bf16[2,512,256]{2,1,0:T(8,128)(2,1)S(1)}, f32[2,256,256]{2,1,0:T(8,128)S(1)}) custom-call(s32[8,128]{1,0:T(8,128)S(1)} %get-tuple-element.40.spot_ref, bf16[2,128,256]{2,1,0:T(8,128)(2,1)S(1)} %get-tuple-element.43.refs_0_, ...), custom_call_target="tpu_custom_call" | custom-call | flops 671088640 | tf_op jit(solution)/shard_map/near/pallas_call | solution.py:575
  16.1 0.0 copy-start.1
  16.1 1.1 %collective-permute-done.2.over_z.refs_5_ = bf16[256,256]{1,0:T(8,128)(2,1)S(1)} collective-permute-done((bf16[256,256]{1,0:T(8,128)(2,1)S(1)}, bf16[256,256]{1,0:T(8,128)(2,1)S(1)}, u32[]{:S(2)}, u32[]{:S(2)}) %collective-permute-start.2) | collective-permute-done | bytes 131104 | tf_op jit(solution)/shard_map/ppermute | solution.py:544
  17.2 0.5 %collective-permute-start.9 = (bf16[256,256]{1,0:T(8,128)(2,1)S(1)}, bf16[256,256]{1,0:T(8,128)(2,1)S(1)}, u32[]{:S(2)}, u32[]{:S(2)}) collective-permute-start(bf16[256,256]{1,0:T(8,128)(2,1)S(1)} %collective-permute-done.1.over_y.refs_4_), channel_id=1, source_target_pairs={{0,1},{1,0},{2,3},{3,2},{4,5},{5,4},{6,7},{7,6},{8,9},{9,8},{10,11... | collective-permute-start | bytes 393224 | tf_op jit(solution)/shard_map/ppermute | solution.py:515
  17.7 0.0 collective-permute-start.10
  17.7 1.4 %over.1 = (f32[4,256,512]{2,1,0:T(8,128)S(1)}, bf16[4,512,256]{2,1,0:T(8,128)(2,1)S(1)}, f32[4,256,256]{2,1,0:T(8,128)S(1)}) custom-call(f32[2,256,256]{2,1,0:T(8,128)S(1)} %get-tuple-element.49.patch_ref.refs_1_, bf16[2,2,256,256]{3,2,1,0:T(8,128)(2,1)S(1)} %collective-permute-done.8.core.refs_3_, ...), custom_call_target="tpu_custom_call" | custom-call | flops 1073741824 | tf_op jit(solution)/shard_map/over/pallas_call | solution.py:587
  19.2 4.3 %back.1 = (bf16[256,256]{1,0:T(8,128)(2,1)S(1)}, bf16[256,256]{1,0:T(8,128)(2,1)S(1)}, bf16[256,384]{1,0:T(8,128)(2,1)S(1)}, bf16[256,384]{1,0:T(8,128)(2,1)S(1)}, bf16[272,128]{1,0:T(8,128)(2,1)S(1)}) custom-call(bf16[16,256]{1,0:T(8,128)(2,1)S(1)} %live.1.record_ref, s32[8,128]{1,0:T(8,128)S(1)} %get-tuple-element.40.spot_ref, ...), custom_call_target="tpu_custom_call" | custom-call | flops 2684354560 | tf_op jit(solution)/shard_map/back/pallas_call | solution.py:599
  23.5 0.6 %collective-permute-start.13 = (bf16[256,384]{1,0:T(8,128)(2,1)S(1)}, bf16[256,384]{1,0:T(8,128)(2,1)S(1)}, u32[]{:S(2)}, u32[]{:S(2)}) collective-permute-start(bf16[256,384]{1,0:T(8,128)(2,1)S(1)} %get-tuple-element.62), channel_id=1, source_target_pairs={{0,1},{1,0},{2,3},{3,2},{4,5},{5,4},{6,7},{7,6},{8,9},{9,8},{10,11... | collective-permute-start | bytes 589832 | tf_op jit(solution)/shard_map/ppermute | solution.py:515
  24.1 1.5 %collective-permute-start.12 = (bf16[272,128]{1,0:T(8,128)(2,1)S(1)}, bf16[272,128]{1,0:T(8,128)(2,1)S(1)}, u32[]{:S(2)}, u32[]{:S(2)}) collective-permute-start(bf16[272,128]{1,0:T(8,128)(2,1)S(1)} %get-tuple-element.60), channel_id=1, source_target_pairs={{0,4},{4,0},{1,5},{5,1},{2,6},{6,2},{3,7},{7,3},{8,12},{12,8},{9,1... | collective-permute-start | bytes 208904 | tf_op jit(solution)/shard_map/ppermute | solution.py:625
  25.6 0.1 meet.1
  25.6 2.3 %collective-permute-start.15 = (bf16[272,128]{1,0:T(8,128)(2,1)S(1)}, bf16[272,128]{1,0:T(8,128)(2,1)S(1)}, u32[]{:S(2)}, u32[]{:S(2)}) collective-permute-start(bf16[272,128]{1,0:T(8,128)(2,1)S(1)} %get-tuple-element.64), channel_id=1, source_target_pairs={{0,12},{1,4},{2,14},{3,6},{4,8},{5,0},{6,10},{7,2},{8,20},{9,5},{1... | collective-permute-start | bytes 208904 | tf_op jit(solution)/shard_map/ppermute | solution.py:639
  27.9 1.6 %collective-permute-start.14 = (bf16[272,256]{1,0:T(8,128)(2,1)S(1)}, bf16[272,256]{1,0:T(8,128)(2,1)S(1)}, u32[]{:S(2)}, u32[]{:S(2)}) collective-permute-start(bf16[272,256]{1,0:T(8,128)(2,1)S(1)} %get-tuple-element.63), channel_id=1, source_target_pairs={{0,8},{1,0},{2,10},{3,2},{4,12},{5,4},{6,14},{7,6},{8,16},{9,1},{1... | collective-permute-start | bytes 417800 | tf_op jit(solution)/shard_map/ppermute | solution.py:637
  29.5 0.4 %levels.1.level_ref = f32[3,128,256]{2,1,0:T(8,128)S(1)} custom-call(bf16[256,256]{1,0:T(8,128)(2,1)S(1)} %get-tuple-element.58.weight_ref, bf16[16,256]{1,0:T(8,128)(2,1)S(1)} %live.1.record_ref, bf16[256,256]{1,0:T(8,128)(2,1)S(1)} %get-tuple-element.59.own_ref, bf16[272,128]{1,0:T(8,128)(2,1)S(1)} %collective-permute-done.12.refs_0_), custom_call_target="tpu_custom_call" | custom-call | flops 2684354560 | tf_op jit(solution)/shard_map/levels/pallas_call | solution.py:641
  29.9 0.2 collective-permute-done.15.refs_0_
  30.2 1.9 %collective-permute-done.14.rows_ref = bf16[272,256]{1,0:T(8,128)(2,1)S(1)} collective-permute-done((bf16[272,256]{1,0:T(8,128)(2,1)S(1)}, bf16[272,256]{1,0:T(8,128)(2,1)S(1)}, u32[]{:S(2)}, u32[]{:S(2)}) %collective-permute-start.14) | collective-permute-done | bytes 139296 | tf_op jit(solution)/shard_map/ppermute | solution.py:637
  32.1 0.5 %sums.1.own_ref = bf16[3,128,256]{2,1,0:T(8,128)(2,1)S(1)} custom-call(bf16[256,256]{1,0:T(8,128)(2,1)S(1)} %get-tuple-element.58.weight_ref, f32[3,128,256]{2,1,0:T(8,128)S(1)} %levels.1.level_ref, bf16[272,256]{1,0:T(8,128)(2,1)S(1)} %collective-permute-done.14.rows_ref, bf16[272,128]{1,0:T(8,128)(2,1)S(1)} %collective-permute-done.15.refs_0_), custom_call_target="tpu_custom_call" | custom-call | tf_op jit(solution)/shard_map/sums/pallas_call | solution.py:650
  32.6 0.1 collective-permute-start.16
  32.7 1.4 %collective-permute-done.16.other_ref = bf16[3,128,256]{2,1,0:T(8,128)(2,1)S(1)} collective-permute-done((bf16[3,128,256]{2,1,0:T(8,128)(2,1)S(1)}, bf16[3,128,256]{2,1,0:T(8,128)(2,1)S(1)}, u32[]{:S(2)}, u32[]{:S(2)}) %collective-permute-start.16) | collective-permute-done | bytes 196640 | tf_op jit(solution)/shard_map/ppermute | solution.py:515
  34.1 0.8 %update.1 = f32[2,128,256]{2,1,0:T(8,128)} custom-call(f32[2,128,256]{2,1,0:T(8,128)S(1)} %copy-done, bf16[3,128,256]{2,1,0:T(8,128)(2,1)S(1)} %sums.1.own_ref, bf16[3,128,256]{2,1,0:T(8,128)(2,1)S(1)} %collective-permute-done.16.other_ref), custom_call_target="tpu_custom_call" | custom-call | tf_op jit(solution)/shard_map/update/pallas_call | solution.py:658
  (15 shorter events, 0.0 us)
Async XLA Ops:
  1.6 9.0 %collective-permute-start.1 = (bf16[256,256]{1,0:T(8,128)(2,1)S(1)}, bf16[256,256]{1,0:T(8,128)(2,1)S(1)}, u32[]{:S(2)}, u32[]{:S(2)}) collective-permute-start(bf16[256,256]{1,0:T(8,128)(2,1)S(1)} %get-tuple-element.41), channel_id=1, source_target_pairs={{0,2},{1,3},{2,0},{3,1},{4,6},{5,7},{6,4},{7,5},{8,10},{9,11},{10,... | collective-permute-start | bytes 393224 | tf_op jit(solution)/shard_map/ppermute | solution.py:515
  4.7 8.3 %collective-permute-start.5 = (bf16[2,128,256]{2,1,0:T(8,128)(2,1)S(1)}, bf16[2,128,256]{2,1,0:T(8,128)(2,1)S(1)}, u32[]{:S(2)}, u32[]{:S(2)}) collective-permute-start(bf16[2,128,256]{2,1,0:T(8,128)(2,1)S(1)} %get-tuple-element.43.refs_0_), channel_id=1, source_target_pairs={{0,8},{1,0},{2,10},{3,2},{4,12},{5,4},{6,14},{7,6},{8,16},{9,1},{1... | collective-permute-start | bytes 393224 | tf_op jit(solution)/shard_map/ppermute | solution.py:546
  6.3 4.4 %collective-permute-start = (bf16[2,128,128]{2,1,0:T(8,128)(2,1)S(1)}, bf16[2,128,128]{2,1,0:T(8,128)(2,1)S(1)}, u32[]{:S(2)}, u32[]{:S(2)}) collective-permute-start(bf16[2,128,128]{2,1,0:T(8,128)(2,1)S(1)} %get-tuple-element.35), channel_id=1, source_target_pairs={{0,12},{1,4},{2,14},{3,6},{4,8},{5,0},{6,10},{7,2},{8,20},{9,5},{1... | collective-permute-start | bytes 196616 | tf_op jit(solution)/shard_map/ppermute | solution.py:547
  8.8 4.5 %collective-permute-start.7 = (bf16[2,128,128]{2,1,0:T(8,128)(2,1)S(1)}, bf16[2,128,128]{2,1,0:T(8,128)(2,1)S(1)}, u32[]{:S(2)}, u32[]{:S(2)}) collective-permute-start(bf16[2,128,128]{2,1,0:T(8,128)(2,1)S(1)} %get-tuple-element.35), channel_id=1, source_target_pairs={{0,4},{4,0},{1,5},{5,1},{2,6},{6,2},{3,7},{7,3},{8,12},{12,8},{9,1... | collective-permute-start | bytes 196616 | tf_op jit(solution)/shard_map/ppermute | solution.py:548
  9.3 7.9 %collective-permute-start.3 = (bf16[2,1,256,256]{3,2,1,0:T(8,128)(2,1)S(1)}, bf16[2,1,256,256]{3,2,1,0:T(8,128)(2,1)S(1)}, u32[]{:S(2)}, u32[]{:S(2)}) collective-permute-start(bf16[2,1,256,256]{3,2,1,0:T(8,128)(2,1)S(1)} %get-tuple-element.42), channel_id=1, source_target_pairs={{0,2},{1,3},{2,0},{3,1},{4,6},{5,7},{6,4},{7,5},{8,10},{9,11},{10,... | collective-permute-start | bytes 786440 | tf_op jit(solution)/shard_map/ppermute | solution.py:515
  10.7 7.0 %collective-permute-start.8 = (bf16[2,2,256,256]{3,2,1,0:T(8,128)(2,1)S(1)}, bf16[2,2,256,256]{3,2,1,0:T(8,128)(2,1)S(1)}, u32[]{:S(2)}, u32[]{:S(2)}) collective-permute-start(bf16[2,2,256,256]{3,2,1,0:T(8,128)(2,1)S(1)} %get-tuple-element.45.refs_6_.refs_2_), channel_id=1, source_target_pairs={{0,1},{1,0},{2,3},{3,2},{4,5},{5,4},{6,7},{7,6},{8,9},{9,8},{10,11... | collective-permute-start | bytes 1572872 | tf_op jit(solution)/shard_map/ppermute | solution.py:515
  10.7 6.5 %collective-permute-start.2 = (bf16[256,256]{1,0:T(8,128)(2,1)S(1)}, bf16[256,256]{1,0:T(8,128)(2,1)S(1)}, u32[]{:S(2)}, u32[]{:S(2)}) collective-permute-start(bf16[256,256]{1,0:T(8,128)(2,1)S(1)} %collective-permute-done.1.over_y.refs_4_), channel_id=1, source_target_pairs={{0,8},{8,0},{16,24},{24,16},{1,9},{9,1},{17,25},{25,17},{2,10},{10... | collective-permute-start | bytes 393224 | tf_op jit(solution)/shard_map/ppermute | solution.py:544
  13.0 1.6 %collective-permute-start.6 = (bf16[2,128,256]{2,1,0:T(8,128)(2,1)S(1)}, bf16[2,128,256]{2,1,0:T(8,128)(2,1)S(1)}, u32[]{:S(2)}, u32[]{:S(2)}) collective-permute-start(bf16[2,128,256]{2,1,0:T(8,128)(2,1)S(1)} %collective-permute-done.5.refs_3_), channel_id=1, source_target_pairs={{0,1},{1,0},{2,3},{3,2},{4,5},{5,4},{6,7},{7,6},{8,9},{9,8},{10,11... | collective-permute-start | bytes 393224 | tf_op jit(solution)/shard_map/ppermute | solution.py:515
  13.2 1.3 %collective-permute-start.4 = (bf16[2,128,128]{2,1,0:T(8,128)(2,1)S(1)}, bf16[2,128,128]{2,1,0:T(8,128)(2,1)S(1)}, u32[]{:S(2)}, u32[]{:S(2)}) collective-permute-start(bf16[2,128,128]{2,1,0:T(8,128)(2,1)S(1)} %collective-permute-done.refs_1_), channel_id=1, source_target_pairs={{0,1},{1,0},{2,3},{3,2},{4,5},{5,4},{6,7},{7,6},{8,9},{9,8},{10,11... | collective-permute-start | bytes 196616 | tf_op jit(solution)/shard_map/ppermute | solution.py:515
  16.1 3.1 %copy-start.1 = (bf16[1,1,2,256,256]{4,3,2,1,0:T(8,128)(2,1)S(1)}, bf16[1,1,2,256,256]{4,3,2,1,0:T(8,128)(2,1)}, u32[]{:S(2)}) copy-start(bf16[1,1,2,256,256]{4,3,2,1,0:T(8,128)(2,1)} %refs_0_.1) | copy-start | bytes 786436
  17.2 2.0 %collective-permute-start.11 = (bf16[2,1,256,256]{3,2,1,0:T(8,128)(2,1)S(1)}, bf16[2,1,256,256]{3,2,1,0:T(8,128)(2,1)S(1)}, u32[]{:S(2)}, u32[]{:S(2)}) collective-permute-start(bf16[2,1,256,256]{3,2,1,0:T(8,128)(2,1)S(1)} %collective-permute-done.3.rest.refs_6_), channel_id=1, source_target_pairs={{0,1},{1,0},{2,3},{3,2},{4,5},{5,4},{6,7},{7,6},{8,9},{9,8},{10,11... | collective-permute-start | bytes 786440 | tf_op jit(solution)/shard_map/ppermute | solution.py:515
  17.2 2.0 %collective-permute-start.9 = (bf16[256,256]{1,0:T(8,128)(2,1)S(1)}, bf16[256,256]{1,0:T(8,128)(2,1)S(1)}, u32[]{:S(2)}, u32[]{:S(2)}) collective-permute-start(bf16[256,256]{1,0:T(8,128)(2,1)S(1)} %collective-permute-done.1.over_y.refs_4_), channel_id=1, source_target_pairs={{0,1},{1,0},{2,3},{3,2},{4,5},{5,4},{6,7},{7,6},{8,9},{9,8},{10,11... | collective-permute-start | bytes 393224 | tf_op jit(solution)/shard_map/ppermute | solution.py:515
  17.7 1.5 %collective-permute-start.10 = (bf16[256,256]{1,0:T(8,128)(2,1)S(1)}, bf16[256,256]{1,0:T(8,128)(2,1)S(1)}, u32[]{:S(2)}, u32[]{:S(2)}) collective-permute-start(bf16[256,256]{1,0:T(8,128)(2,1)S(1)} %collective-permute-done.2.over_z.refs_5_), channel_id=1, source_target_pairs={{0,1},{1,0},{2,3},{3,2},{4,5},{5,4},{6,7},{7,6},{8,9},{9,8},{10,11... | collective-permute-start | bytes 393224 | tf_op jit(solution)/shard_map/ppermute | solution.py:515
  23.5 2.1 %collective-permute-start.13 = (bf16[256,384]{1,0:T(8,128)(2,1)S(1)}, bf16[256,384]{1,0:T(8,128)(2,1)S(1)}, u32[]{:S(2)}, u32[]{:S(2)}) collective-permute-start(bf16[256,384]{1,0:T(8,128)(2,1)S(1)} %get-tuple-element.62), channel_id=1, source_target_pairs={{0,1},{1,0},{2,3},{3,2},{4,5},{5,4},{6,7},{7,6},{8,9},{9,8},{10,11... | collective-permute-start | bytes 589832 | tf_op jit(solution)/shard_map/ppermute | solution.py:515
  24.1 5.4 %collective-permute-start.12 = (bf16[272,128]{1,0:T(8,128)(2,1)S(1)}, bf16[272,128]{1,0:T(8,128)(2,1)S(1)}, u32[]{:S(2)}, u32[]{:S(2)}) collective-permute-start(bf16[272,128]{1,0:T(8,128)(2,1)S(1)} %get-tuple-element.60), channel_id=1, source_target_pairs={{0,4},{4,0},{1,5},{5,1},{2,6},{6,2},{3,7},{7,3},{8,12},{12,8},{9,1... | collective-permute-start | bytes 208904 | tf_op jit(solution)/shard_map/ppermute | solution.py:625
  25.6 4.5 %collective-permute-start.15 = (bf16[272,128]{1,0:T(8,128)(2,1)S(1)}, bf16[272,128]{1,0:T(8,128)(2,1)S(1)}, u32[]{:S(2)}, u32[]{:S(2)}) collective-permute-start(bf16[272,128]{1,0:T(8,128)(2,1)S(1)} %get-tuple-element.64), channel_id=1, source_target_pairs={{0,12},{1,4},{2,14},{3,6},{4,8},{5,0},{6,10},{7,2},{8,20},{9,5},{1... | collective-permute-start | bytes 208904 | tf_op jit(solution)/shard_map/ppermute | solution.py:639
  27.9 4.2 %collective-permute-start.14 = (bf16[272,256]{1,0:T(8,128)(2,1)S(1)}, bf16[272,256]{1,0:T(8,128)(2,1)S(1)}, u32[]{:S(2)}, u32[]{:S(2)}) collective-permute-start(bf16[272,256]{1,0:T(8,128)(2,1)S(1)} %get-tuple-element.63), channel_id=1, source_target_pairs={{0,8},{1,0},{2,10},{3,2},{4,12},{5,4},{6,14},{7,6},{8,16},{9,1},{1... | collective-permute-start | bytes 417800 | tf_op jit(solution)/shard_map/ppermute | solution.py:637
  29.5 4.6 %copy-start = (f32[2,128,256]{2,1,0:T(8,128)S(1)}, f32[2,128,256]{2,1,0:T(8,128)}, u32[]{:S(2)}) copy-start(f32[2,128,256]{2,1,0:T(8,128)} %object_ref.1) | copy-start | bytes 786436
  32.6 1.5 %collective-permute-start.16 = (bf16[3,128,256]{2,1,0:T(8,128)(2,1)S(1)}, bf16[3,128,256]{2,1,0:T(8,128)(2,1)S(1)}, u32[]{:S(2)}, u32[]{:S(2)}) collective-permute-start(bf16[3,128,256]{2,1,0:T(8,128)(2,1)S(1)} %sums.1.own_ref), channel_id=1, source_target_pairs={{0,1},{1,0},{2,3},{3,2},{4,5},{5,4},{6,7},{7,6},{8,9},{9,8},{10,11... | collective-permute-start | bytes 589832 | tf_op jit(solution)/shard_map/ppermute | solution.py:515

commit v12 on v11

--- a/solution.py
+++ b/solution.py
@@ -277,13 +277,17 @@
     )
 
 
-def over_kernel(patch_ref, core, over_y, over_z, rest, direct, swapped, far_ref, exit_ref, sum_ref):
+def core_kernel(patch_ref, core, direct, swapped, far_ref, exit_ref, sum_ref):
     patch = (patch_ref[0], patch_ref[1])
-    tables = (direct[...], swapped[...], far_ref, exit_ref)
-    modes = modes_of(core)
-    sum_ref[0], sum_ref[1] = forward(modes, patch, *tables, 0)
-    over_modes = [shared_mode(over_y, over_z)] + modes_of(rest)
-    sum_ref[2], sum_ref[3] = forward(over_modes, patch, *tables, len(modes))
+    sum_ref[0], sum_ref[1] = forward(
+        modes_of(core), patch, direct[...], swapped[...], far_ref, exit_ref, 0
+    )
+
+
+def over_kernel(patch_ref, over_y, over_z, rest, direct, swapped, far_ref, exit_ref, sum_ref):
+    patch = (patch_ref[0], patch_ref[1])
+    modes = [shared_mode(over_y, over_z)] + modes_of(rest)
+    sum_ref[0], sum_ref[1] = forward(modes, patch, direct[...], swapped[...], far_ref, exit_ref, 0)
 
 
 def back_kernel(sides, slots, tile_cols, record_ref, spot_ref, *refs):
@@ -291,13 +295,13 @@
     over_modes = [shared_mode(*refs[4:6])] + modes_of(refs[6])
     last_modes = [shared_mode(*refs[7:9])] + modes_of(refs[9])
     direct_ref, swapped_ref = refs[10:12]
-    near_far, near_exit, near_sum, over_far, over_exit, over_sum = refs[12:18]
-    weight_out, own_out, keep_out, swap_out = refs[18:22]
-    side_outs = refs[22 : 22 + sides]
-    last_far, last_exit = refs[22 + sides :]
+    near_far, near_exit, near_sum, core_far, core_exit, core_sum = refs[12:18]
+    over_far, over_exit, over_sum = refs[18:21]
+    weight_out, own_out, keep_out, swap_out = refs[21:25]
+    side_outs = refs[25 : 25 + sides]
+    last_far, last_exit = refs[25 + sides :]
     side = own.shape[2]
     half = side // 2
-    modes = own.shape[1]
     _, x_index, parity = here()
     row_at, col_at = spot_ref[0, 0], spot_ref[1, 0]
     _, _, is_live = position_of(record_ref, slots, parity)
@@ -305,8 +309,8 @@
     swapped = swapped_ref[...]
     patch = (patch_ref[0], patch_ref[1])
     power, weight = forward(last_modes, patch, direct, swapped, last_far, last_exit, 0)
-    power = (near_sum[0] + over_sum[0]) + (over_sum[2] + power)
-    weight = (near_sum[1] + over_sum[1]) + (over_sum[3] + weight)
+    power = (near_sum[0] + core_sum[0]) + (over_sum[0] + power)
+    weight = (near_sum[1] + core_sum[1]) + (over_sum[1] + weight)
     weight_out[...] = weight.astype(jnp.bfloat16)
     amplitude = amplitude_ref[0, 0, parity].astype(jnp.float32)
     factor = amplitude / jnp.sqrt(power + power_floor)
@@ -314,8 +318,8 @@
     tables = (factor, direct, swapped)
     grads = [
         backward(modes_of(own), *tables, near_far, near_exit, 0),
-        backward(modes_of(core), *tables, over_far, over_exit, 0),
-        backward(over_modes, *tables, over_far, over_exit, modes),
+        backward(modes_of(core), *tables, core_far, core_exit, 0),
+        backward(over_modes, *tables, over_far, over_exit, 0),
         backward(last_modes, *tables, last_far, last_exit, 0),
     ]
     even = parity == 0
@@ -540,13 +544,14 @@
         name="start",
     )(*(in_hbm(array) for array in (object_field, probe, centers, *tables)))
     over_y = exchange(shared, 2)
+    probe_core = exchange(probe_low, 1)
+    probe_core, rest = lax.optimization_barrier((probe_core, rest))
     rest = exchange(rest, 2)
     over_z = lax.ppermute(over_y, "tx", [(z, z ^ 1) for z in range(z_count)])
     x_steps = [1] if sides == 1 else [1, -1]
     rows = lax.ppermute(packed[0], axes, zigzag(0))
     corners = [lax.ppermute(edge, axes, zigzag(step)) for step, edge in zip(x_steps, packed[1:])]
     levels = [lax.ppermute(edge, "ty", level(step)) for step, edge in zip(x_steps, packed[1:])]
-    probe_core = exchange(probe_low, 1)
     corners, record = lax.optimization_barrier((corners, record))
     record = pl.pallas_call(
         functools.partial(live_kernel, slots),
@@ -554,7 +559,7 @@
         in_specs=[vmem(), smem()],
         out_specs=vmem(),
         compiler_params=pltpu.CompilerParams(vmem_limit_bytes=small_bytes),
-        cost_estimate=cost(80),
+        cost_estimate=cost(40),
         name="live",
     )(record, live)
     corners, record = lax.optimization_barrier((corners, record))
@@ -564,42 +569,49 @@
     n_pieces = len(pieces)
     ext_cols = tile_cols + sides * half
 
-    def waves(groups):
-        count = groups * modes
-        return [
-            jax.ShapeDtypeStruct((count, side, 2 * side), jnp.float32),
-            jax.ShapeDtypeStruct((count, 2 * side, side), jnp.bfloat16),
-            jax.ShapeDtypeStruct((2 * groups, side, side), jnp.float32),
-        ]
-
+    waves = [
+        jax.ShapeDtypeStruct((modes, side, 2 * side), jnp.float32),
+        jax.ShapeDtypeStruct((modes, 2 * side, side), jnp.bfloat16),
+        jax.ShapeDtypeStruct((2, side, side), jnp.float32),
+    ]
     patch, *near = pl.pallas_call(
         functools.partial(near_kernel, sides, z_count, x_count),
-        out_shape=[jax.ShapeDtypeStruct((2, side, side), jnp.float32)] + waves(1),
+        out_shape=[jax.ShapeDtypeStruct((2, side, side), jnp.float32)] + waves,
         in_specs=[vmem()] * (n_pieces + 4),
         out_specs=[vmem()] * 4,
         compiler_params=pltpu.CompilerParams(vmem_limit_bytes=wave_bytes),
-        cost_estimate=cost(20),
+        cost_estimate=cost(1),
         name="near",
     )(spot, *in_sent_order(pieces), probe_low, direct, swapped)
-    over_z, rest, patch = lax.optimization_barrier((over_z, rest, patch))
+    other = pl.pallas_call(
+        core_kernel,
+        out_shape=waves,
+        in_specs=[vmem()] * 4,
+        out_specs=[vmem()] * 3,
+        compiler_params=pltpu.CompilerParams(vmem_limit_bytes=wave_bytes),
+        cost_estimate=cost(1),
+        name="core",
+    )(patch, probe_core, direct, swapped)
+    last_y = exchange(over_y, 1)
+    over_z, rest, other = lax.optimization_barrier((over_z, rest, other))
     over_group = (over_y, over_z, rest)
-    last_group = [exchange(part, 1) for part in over_group]
+    last_group = [last_y, exchange(over_z, 1), exchange(rest, 1)]
     over = pl.pallas_call(
         over_kernel,
-        out_shape=waves(2),
-        in_specs=[vmem()] * 7,
+        out_shape=waves,
+        in_specs=[vmem()] * 6,
         out_specs=[vmem()] * 3,
         compiler_params=pltpu.CompilerParams(vmem_limit_bytes=wave_bytes),
-        cost_estimate=cost(32),
+        cost_estimate=cost(100),
         name="over",
-    )(patch, probe_core, *over_group, direct, swapped)
+    )(patch, *over_group, direct, swapped)
     piece_rows = 2 * half + record_rows
     shapes = [(side, side), (2 * half, tile_cols)] + [(2 * half, ext_cols)] * 2
     shapes += [(piece_rows, half)] * sides
     weight, own, keep, swap, *levels = pl.pallas_call(
         functools.partial(back_kernel, sides, slots, tile_cols),
         out_shape=[jax.ShapeDtypeStruct(shape, jnp.bfloat16) for shape in shapes],
-        in_specs=[vmem()] * 20,
+        in_specs=[vmem()] * 23,
         out_specs=[vmem()] * (4 + sides),
         scratch_shapes=[
             pltpu.VMEM((modes, side, 2 * side), jnp.float32),
@@ -620,6 +632,7 @@
         direct,
         swapped,
         *near,
+        *other,
         *over,
     )
     levels = [lax.ppermute(piece, "ty", level(-step)) for piece, step in zip(levels, x_steps)]

time: 35 us -> 33.9 us (0.969)
  waiting for transfers between devices: 5.91 us -> 5.14 us
  starting transfers between devices: 17.6 us -> 16.9 us
    ppermute x1, waiting for transfers between devices: 1.1 us -> 0.01 us  [on_device(): over_z = lax.ppermute(over_y, 'tx', [(z, z ^ 1) for z in range(z_count)])]
    ppermute x1, starting transfers between devices: 2.31 us -> 1.68 us  [on_device(): lax.ppermute(piece, axes, zigzag(-step))]
    ppermute x1, waiting for transfers between devices: 1.94 us -> 1.42 us  [on_device(): rows = lax.ppermute(rows, axes, zigzag(0))]
    ppermute x1, waiting for transfers between devices: 0.23 us -> 0.75 us  [on_device(): lax.ppermute(piece, axes, zigzag(-step))]
    pallas_call x1 -> x2, Pallas kernels: 1.44 us -> 1.73 us  [the longest x1 0.88 us: on_device(): pl.pallas_call(over_kernel, out_shape=waves, in_specs=[vmem()] * 6, out_s...]
  transfers between devices with their start and end apart: 17 -> 17, of which waited for: 6 -> 6; matrix products, arithmetic and copies ran while one was open for 0% -> 0% of each run, Pallas kernels for 10% -> 11%
where the time goes in v12:
time: 33.9 us; the launch traced here: 33.7 us
  starting transfers between devices  16.9 us (50%)
  Pallas kernels  10.9 us (32%)
  waiting for transfers between devices  5.14 us (15%)
  between operations  0.78 us (2%)
    ppermute x10, starting transfers between devices, exchange(): return lax.ppermute(array, 'mode', [(m, m ^ flip) for m in range(m_count)])  5.08 us
    pallas_call x1, Pallas kernels, on_device(): pl.pallas_call(functools.partial(back_kernel, sides, slots, tile_cols), o...  4.36 us
    ppermute x10, waiting for transfers between devices, exchange(): return lax.ppermute(array, 'mode', [(m, m ^ flip) for m in range(m_count)])  2.74 us
    ppermute x1, starting transfers between devices, on_device(): lax.ppermute(edge, axes, zigzag(step))  2.5 us
    ppermute x1, starting transfers between devices, on_device(): over_z = lax.ppermute(over_y, 'tx', [(z, z ^ 1) for z in range(z_count)])  2.33 us
    ppermute x1, starting transfers between devices, on_device(): lax.ppermute(piece, axes, zigzag(-step))  1.68 us
    ppermute x1, starting transfers between devices, on_device(): rows = lax.ppermute(rows, axes, zigzag(0))  1.68 us
    pallas_call x1, Pallas kernels, on_device(): pl.pallas_call(functools.partial(start_kernel, sides, slots), out_shape=[...  1.64 us
  transfers between devices with their start and end apart: 17, of which 6 were waited for; matrix products, arithmetic and copies ran while one was open for 0% of the time, Pallas kernels for 11%

profile of v12, /device:TPU:0, one launch (start us, length us, event | category | flops | bytes accessed | tf_op | source)
XLA Modules:
  0.0 33.7 jit_solution(1403937124639779340)
XLA Ops:
  0.0 1.6 %start.1 = (bf16[2,2,256,256]{3,2,1,0:T(8,128)(2,1)S(1)}, bf16[256,256]{1,0:T(8,128)(2,1)S(1)}, bf16[2,1,256,256]{3,2,1,0:T(8,128)(2,1)S(1)}, bf16[16,256]{1,0:T...) custom-call(f32[2,128,256]{2,1,0:T(8,128)} %object_ref.1, ...), custom_call_target="tpu_custom_call" | custom-call | tf_op jit(solution)/shard_map/start/pallas_call | solution.py:522
  1.6 0.5 %collective-permute-start.5 = (bf16[2,2,256,256]{3,2,1,0:T(8,128)(2,1)S(1)}, bf16[2,2,256,256]{3,2,1,0:T(8,128)(2,1)S(1)}, u32[]{:S(2)}, u32[]{:S(2)}) collective-permute-start(bf16[2,2,256,256]{3,2,1,0:T(8,128)(2,1)S(1)} %get-tuple-element.50.refs_6_.refs_2_), channel_id=1, source_target_pairs={{0,1},{1,0},{2,3},{3,2},{4,5},{5,4},{6,7},{7,6},{8,9},{9,8},{10,11... | collective-permute-start | bytes 1572872 | tf_op jit(solution)/shard_map/ppermute | solution.py:519
  2.2 2.6 %collective-permute-start.6 = (bf16[256,256]{1,0:T(8,128)(2,1)S(1)}, bf16[256,256]{1,0:T(8,128)(2,1)S(1)}, u32[]{:S(2)}, u32[]{:S(2)}) collective-permute-start(bf16[256,256]{1,0:T(8,128)(2,1)S(1)} %get-tuple-element.56), channel_id=1, source_target_pairs={{0,2},{1,3},{2,0},{3,1},{4,6},{5,7},{6,4},{7,5},{8,10},{9,11},{10,... | collective-permute-start | bytes 393224 | tf_op jit(solution)/shard_map/ppermute | solution.py:519
  4.8 1.6 %collective-permute-start.2 = (bf16[2,128,256]{2,1,0:T(8,128)(2,1)S(1)}, bf16[2,128,256]{2,1,0:T(8,128)(2,1)S(1)}, u32[]{:S(2)}, u32[]{:S(2)}) collective-permute-start(bf16[2,128,256]{2,1,0:T(8,128)(2,1)S(1)} %get-tuple-element.48.refs_0_), channel_id=1, source_target_pairs={{0,8},{1,0},{2,10},{3,2},{4,12},{5,4},{6,14},{7,6},{8,16},{9,1},{1... | collective-permute-start | bytes 393224 | tf_op jit(solution)/shard_map/ppermute | solution.py:552
  6.3 2.5 %collective-permute-start = (bf16[2,128,128]{2,1,0:T(8,128)(2,1)S(1)}, bf16[2,128,128]{2,1,0:T(8,128)(2,1)S(1)}, u32[]{:S(2)}, u32[]{:S(2)}) collective-permute-start(bf16[2,128,128]{2,1,0:T(8,128)(2,1)S(1)} %get-tuple-element.42), channel_id=1, source_target_pairs={{0,12},{1,4},{2,14},{3,6},{4,8},{5,0},{6,10},{7,2},{8,20},{9,5},{1... | collective-permute-start | bytes 196616 | tf_op jit(solution)/shard_map/ppermute | solution.py:553
  8.8 0.5 %collective-permute-start.8 = (bf16[2,1,256,256]{3,2,1,0:T(8,128)(2,1)S(1)}, bf16[2,1,256,256]{3,2,1,0:T(8,128)(2,1)S(1)}, u32[]{:S(2)}, u32[]{:S(2)}) collective-permute-start(bf16[2,1,256,256]{3,2,1,0:T(8,128)(2,1)S(1)} %get-tuple-element.57), channel_id=1, source_target_pairs={{0,2},{1,3},{2,0},{3,1},{4,6},{5,7},{6,4},{7,5},{8,10},{9,11},{10,... | collective-permute-start | bytes 786440 | tf_op jit(solution)/shard_map/ppermute | solution.py:519
  9.3 0.5 %collective-permute-start.4 = (bf16[2,128,128]{2,1,0:T(8,128)(2,1)S(1)}, bf16[2,128,128]{2,1,0:T(8,128)(2,1)S(1)}, u32[]{:S(2)}, u32[]{:S(2)}) collective-permute-start(bf16[2,128,128]{2,1,0:T(8,128)(2,1)S(1)} %get-tuple-element.42), channel_id=1, source_target_pairs={{0,4},{4,0},{1,5},{5,1},{2,6},{6,2},{3,7},{7,3},{8,12},{12,8},{9,1... | collective-permute-start | bytes 196616 | tf_op jit(solution)/shard_map/ppermute | solution.py:554
  10.5 0.2 collective-permute-done.refs_1_
  10.7 2.3 %collective-permute-start.7 = (bf16[256,256]{1,0:T(8,128)(2,1)S(1)}, bf16[256,256]{1,0:T(8,128)(2,1)S(1)}, u32[]{:S(2)}, u32[]{:S(2)}) collective-permute-start(bf16[256,256]{1,0:T(8,128)(2,1)S(1)} %collective-permute-done.6.over_y.refs_4_), channel_id=1, source_target_pairs={{0,8},{8,0},{16,24},{24,16},{1,9},{9,1},{17,25},{25,17},{2,10},{10... | collective-permute-start | bytes 393224 | tf_op jit(solution)/shard_map/ppermute | solution.py:550
  13.1 0.5 %collective-permute-start.1 = (bf16[2,128,128]{2,1,0:T(8,128)(2,1)S(1)}, bf16[2,128,128]{2,1,0:T(8,128)(2,1)S(1)}, u32[]{:S(2)}, u32[]{:S(2)}) collective-permute-start(bf16[2,128,128]{2,1,0:T(8,128)(2,1)S(1)} %collective-permute-done.refs_1_), channel_id=1, source_target_pairs={{0,1},{1,0},{2,3},{3,2},{4,5},{5,4},{6,7},{7,6},{8,9},{9,8},{10,11... | collective-permute-start | bytes 196616 | tf_op jit(solution)/shard_map/ppermute | solution.py:519
  13.6 0.0 collective-permute-done.4.refs_5_
  13.6 0.1 collective-permute-start.9
  13.7 0.8 %collective-permute-done.1.refs_2_ = bf16[2,128,128]{2,1,0:T(8,128)(2,1)S(1)} collective-permute-done((bf16[2,128,128]{2,1,0:T(8,128)(2,1)S(1)}, bf16[2,128,128]{2,1,0:T(8,128)(2,1)S(1)}, u32[]{:S(2)}, u32[]{:S(2)}) %collective-permute-start.1) | collective-permute-done | bytes 65568 | tf_op jit(solution)/shard_map/ppermute | solution.py:519
  14.5 1.5 %near.1 = (f32[2,256,256]{2,1,0:T(8,128)S(1)}, f32[2,256,512]{2,1,0:T(8,128)S(1)}, bf16[2,512,256]{2,1,0:T(8,128)(2,1)S(1)}, f32[2,256,256]{2,1,0:T(8,128)S(1)}) custom-call(s32[8,128]{1,0:T(8,128)S(1)} %get-tuple-element.47.spot_ref, bf16[2,128,256]{2,1,0:T(8,128)(2,1)S(1)} %get-tuple-element.48.refs_0_, ...), custom_call_target="tpu_custom_call" | custom-call | flops 33554432 | tf_op jit(solution)/shard_map/near/pallas_call | solution.py:577
  16.0 0.9 %core.1 = (f32[2,256,512]{2,1,0:T(8,128)S(1)}, bf16[2,512,256]{2,1,0:T(8,128)(2,1)S(1)}, f32[2,256,256]{2,1,0:T(8,128)S(1)}) custom-call(f32[2,256,256]{2,1,0:T(8,128)S(1)} %get-tuple-element.53.patch_ref.refs_1_, bf16[2,2,256,256]{3,2,1,0:T(8,128)(2,1)S(1)} %collective-permute-done.5.core.refs_3_, ...), custom_call_target="tpu_custom_call" | custom-call | flops 33554432 | tf_op jit(solution)/shard_map/core/pallas_call | solution.py:586
  16.9 0.4 %collective-permute-start.10 = (bf16[256,256]{1,0:T(8,128)(2,1)S(1)}, bf16[256,256]{1,0:T(8,128)(2,1)S(1)}, u32[]{:S(2)}, u32[]{:S(2)}) collective-permute-start(bf16[256,256]{1,0:T(8,128)(2,1)S(1)} %collective-permute-done.7.over_z.refs_5_), channel_id=1, source_target_pairs={{0,1},{1,0},{2,3},{3,2},{4,5},{5,4},{6,7},{7,6},{8,9},{9,8},{10,11... | collective-permute-start | bytes 393224 | tf_op jit(solution)/shard_map/ppermute | solution.py:519
  17.3 0.2 collective-permute-start.11
  17.5 0.9 %over.1 = (f32[2,256,512]{2,1,0:T(8,128)S(1)}, bf16[2,512,256]{2,1,0:T(8,128)(2,1)S(1)}, f32[2,256,256]{2,1,0:T(8,128)S(1)}) custom-call(f32[2,256,256]{2,1,0:T(8,128)S(1)} %get-tuple-element.53.patch_ref.refs_1_, bf16[256,256]{1,0:T(8,128)(2,1)S(1)} %collective-permute-done.6.over_y.refs_4_, bf16[256,256]{1,0:T(8,128)(2,1)S(1)} %collective-permute-done.7.over_z.refs_5_, ...), custom_call_target="tpu_custom_call" | custom-call | flops 3355443200 | tf_op jit(solution)/shard_map/over/pallas_call | solution.py:599
  18.4 0.4 %collective-permute-done.11.refs_9_ = bf16[2,1,256,256]{3,2,1,0:T(8,128)(2,1)S(1)} collective-permute-done((bf16[2,1,256,256]{3,2,1,0:T(8,128)(2,1)S(1)}, bf16[2,1,256,256]{3,2,1,0:T(8,128)(2,1)S(1)}, u32[]{:S(2)}, u32[]{:S(2)}) %collective-permute-start.11) | collective-permute-done | bytes 262176 | tf_op jit(solution)/shard_map/ppermute | solution.py:519
  18.8 4.4 %back.1 = (bf16[256,256]{1,0:T(8,128)(2,1)S(1)}, bf16[256,256]{1,0:T(8,128)(2,1)S(1)}, bf16[256,384]{1,0:T(8,128)(2,1)S(1)}, bf16[256,384]{1,0:T(8,128)(2,1)S(1)}, bf16[272,128]{1,0:T(8,128)(2,1)S(1)}) custom-call(bf16[16,256]{1,0:T(8,128)(2,1)S(1)} %live.1.record_ref, s32[8,128]{1,0:T(8,128)S(1)} %get-tuple-element.47.spot_ref, ...), custom_call_target="tpu_custom_call" | custom-call | flops 2684354560 | tf_op jit(solution)/shard_map/back/pallas_call | solution.py:611
  23.2 0.2 collective-permute-start.13
  23.5 1.5 %collective-permute-start.12 = (bf16[272,128]{1,0:T(8,128)(2,1)S(1)}, bf16[272,128]{1,0:T(8,128)(2,1)S(1)}, u32[]{:S(2)}, u32[]{:S(2)}) collective-permute-start(bf16[272,128]{1,0:T(8,128)(2,1)S(1)} %get-tuple-element.74), channel_id=1, source_target_pairs={{0,4},{4,0},{1,5},{5,1},{2,6},{6,2},{3,7},{7,3},{8,12},{12,8},{9,1... | collective-permute-start | bytes 208904 | tf_op jit(solution)/shard_map/ppermute | solution.py:638
  25.0 0.1 meet.1
  25.0 1.7 %collective-permute-start.15 = (bf16[272,128]{1,0:T(8,128)(2,1)S(1)}, bf16[272,128]{1,0:T(8,128)(2,1)S(1)}, u32[]{:S(2)}, u32[]{:S(2)}) collective-permute-start(bf16[272,128]{1,0:T(8,128)(2,1)S(1)} %get-tuple-element.78), channel_id=1, source_target_pairs={{0,12},{1,4},{2,14},{3,6},{4,8},{5,0},{6,10},{7,2},{8,20},{9,5},{1... | collective-permute-start | bytes 208904 | tf_op jit(solution)/shard_map/ppermute | solution.py:652
  26.7 1.7 %collective-permute-start.14 = (bf16[272,256]{1,0:T(8,128)(2,1)S(1)}, bf16[272,256]{1,0:T(8,128)(2,1)S(1)}, u32[]{:S(2)}, u32[]{:S(2)}) collective-permute-start(bf16[272,256]{1,0:T(8,128)(2,1)S(1)} %get-tuple-element.77), channel_id=1, source_target_pairs={{0,8},{1,0},{2,10},{3,2},{4,12},{5,4},{6,14},{7,6},{8,16},{9,1},{1... | collective-permute-start | bytes 417800 | tf_op jit(solution)/shard_map/ppermute | solution.py:650
  28.4 0.4 %levels.1.level_ref = f32[3,128,256]{2,1,0:T(8,128)S(1)} custom-call(bf16[256,256]{1,0:T(8,128)(2,1)S(1)} %get-tuple-element.72.weight_ref, bf16[16,256]{1,0:T(8,128)(2,1)S(1)} %live.1.record_ref, bf16[256,256]{1,0:T(8,128)(2,1)S(1)} %get-tuple-element.73.own_ref, bf16[272,128]{1,0:T(8,128)(2,1)S(1)} %collective-permute-done.12.refs_0_), custom_call_target="tpu_custom_call" | custom-call | flops 2684354560 | tf_op jit(solution)/shard_map/levels/pallas_call | solution.py:654
  28.8 0.7 %collective-permute-done.15.refs_0_ = bf16[272,128]{1,0:T(8,128)(2,1)S(1)} collective-permute-done((bf16[272,128]{1,0:T(8,128)(2,1)S(1)}, bf16[272,128]{1,0:T(8,128)(2,1)S(1)}, u32[]{:S(2)}, u32[]{:S(2)}) %collective-permute-start.15) | collective-permute-done | bytes 69664 | tf_op jit(solution)/shard_map/ppermute | solution.py:652
  29.5 1.4 %collective-permute-done.14.rows_ref = bf16[272,256]{1,0:T(8,128)(2,1)S(1)} collective-permute-done((bf16[272,256]{1,0:T(8,128)(2,1)S(1)}, bf16[272,256]{1,0:T(8,128)(2,1)S(1)}, u32[]{:S(2)}, u32[]{:S(2)}) %collective-permute-start.14) | collective-permute-done | bytes 139296 | tf_op jit(solution)/shard_map/ppermute | solution.py:650
  31.0 0.5 %sums.1.own_ref = bf16[3,128,256]{2,1,0:T(8,128)(2,1)S(1)} custom-call(bf16[256,256]{1,0:T(8,128)(2,1)S(1)} %get-tuple-element.72.weight_ref, f32[3,128,256]{2,1,0:T(8,128)S(1)} %levels.1.level_ref, bf16[272,256]{1,0:T(8,128)(2,1)S(1)} %collective-permute-done.14.rows_ref, bf16[272,128]{1,0:T(8,128)(2,1)S(1)} %collective-permute-done.15.refs_0_), custom_call_target="tpu_custom_call" | custom-call | tf_op jit(solution)/shard_map/sums/pallas_call | solution.py:663
  31.4 0.1 collective-permute-start.16
  31.5 1.4 %collective-permute-done.16.other_ref = bf16[3,128,256]{2,1,0:T(8,128)(2,1)S(1)} collective-permute-done((bf16[3,128,256]{2,1,0:T(8,128)(2,1)S(1)}, bf16[3,128,256]{2,1,0:T(8,128)(2,1)S(1)}, u32[]{:S(2)}, u32[]{:S(2)}) %collective-permute-start.16) | collective-permute-done | bytes 196640 | tf_op jit(solution)/shard_map/ppermute | solution.py:519
  32.9 0.8 %update.1 = f32[2,128,256]{2,1,0:T(8,128)} custom-call(f32[2,128,256]{2,1,0:T(8,128)S(1)} %copy-done, bf16[3,128,256]{2,1,0:T(8,128)(2,1)S(1)} %sums.1.own_ref, bf16[3,128,256]{2,1,0:T(8,128)(2,1)S(1)} %collective-permute-done.16.other_ref), custom_call_target="tpu_custom_call" | custom-call | tf_op jit(solution)/shard_map/update/pallas_call | solution.py:671
  (16 shorter events, 0.0 us)
Async XLA Ops:
  1.6 7.2 %collective-permute-start.5 = (bf16[2,2,256,256]{3,2,1,0:T(8,128)(2,1)S(1)}, bf16[2,2,256,256]{3,2,1,0:T(8,128)(2,1)S(1)}, u32[]{:S(2)}, u32[]{:S(2)}) collective-permute-start(bf16[2,2,256,256]{3,2,1,0:T(8,128)(2,1)S(1)} %get-tuple-element.50.refs_6_.refs_2_), channel_id=1, source_target_pairs={{0,1},{1,0},{2,3},{3,2},{4,5},{5,4},{6,7},{7,6},{8,9},{9,8},{10,11... | collective-permute-start | bytes 1572872 | tf_op jit(solution)/shard_map/ppermute | solution.py:519
  2.2 8.6 %collective-permute-start.6 = (bf16[256,256]{1,0:T(8,128)(2,1)S(1)}, bf16[256,256]{1,0:T(8,128)(2,1)S(1)}, u32[]{:S(2)}, u32[]{:S(2)}) collective-permute-start(bf16[256,256]{1,0:T(8,128)(2,1)S(1)} %get-tuple-element.56), channel_id=1, source_target_pairs={{0,2},{1,3},{2,0},{3,1},{4,6},{5,7},{6,4},{7,5},{8,10},{9,11},{10,... | collective-permute-start | bytes 393224 | tf_op jit(solution)/shard_map/ppermute | solution.py:519
  4.8 8.3 %collective-permute-start.2 = (bf16[2,128,256]{2,1,0:T(8,128)(2,1)S(1)}, bf16[2,128,256]{2,1,0:T(8,128)(2,1)S(1)}, u32[]{:S(2)}, u32[]{:S(2)}) collective-permute-start(bf16[2,128,256]{2,1,0:T(8,128)(2,1)S(1)} %get-tuple-element.48.refs_0_), channel_id=1, source_target_pairs={{0,8},{1,0},{2,10},{3,2},{4,12},{5,4},{6,14},{7,6},{8,16},{9,1},{1... | collective-permute-start | bytes 393224 | tf_op jit(solution)/shard_map/ppermute | solution.py:552
  6.3 4.4 %collective-permute-start = (bf16[2,128,128]{2,1,0:T(8,128)(2,1)S(1)}, bf16[2,128,128]{2,1,0:T(8,128)(2,1)S(1)}, u32[]{:S(2)}, u32[]{:S(2)}) collective-permute-start(bf16[2,128,128]{2,1,0:T(8,128)(2,1)S(1)} %get-tuple-element.42), channel_id=1, source_target_pairs={{0,12},{1,4},{2,14},{3,6},{4,8},{5,0},{6,10},{7,2},{8,20},{9,5},{1... | collective-permute-start | bytes 196616 | tf_op jit(solution)/shard_map/ppermute | solution.py:553
  8.8 8.1 %collective-permute-start.8 = (bf16[2,1,256,256]{3,2,1,0:T(8,128)(2,1)S(1)}, bf16[2,1,256,256]{3,2,1,0:T(8,128)(2,1)S(1)}, u32[]{:S(2)}, u32[]{:S(2)}) collective-permute-start(bf16[2,1,256,256]{3,2,1,0:T(8,128)(2,1)S(1)} %get-tuple-element.57), channel_id=1, source_target_pairs={{0,2},{1,3},{2,0},{3,1},{4,6},{5,7},{6,4},{7,5},{8,10},{9,11},{10,... | collective-permute-start | bytes 786440 | tf_op jit(solution)/shard_map/ppermute | solution.py:519
  9.3 4.3 %collective-permute-start.4 = (bf16[2,128,128]{2,1,0:T(8,128)(2,1)S(1)}, bf16[2,128,128]{2,1,0:T(8,128)(2,1)S(1)}, u32[]{:S(2)}, u32[]{:S(2)}) collective-permute-start(bf16[2,128,128]{2,1,0:T(8,128)(2,1)S(1)} %get-tuple-element.42), channel_id=1, source_target_pairs={{0,4},{4,0},{1,5},{5,1},{2,6},{6,2},{3,7},{7,3},{8,12},{12,8},{9,1... | collective-permute-start | bytes 196616 | tf_op jit(solution)/shard_map/ppermute | solution.py:554
  10.7 6.1 %collective-permute-start.7 = (bf16[256,256]{1,0:T(8,128)(2,1)S(1)}, bf16[256,256]{1,0:T(8,128)(2,1)S(1)}, u32[]{:S(2)}, u32[]{:S(2)}) collective-permute-start(bf16[256,256]{1,0:T(8,128)(2,1)S(1)} %collective-permute-done.6.over_y.refs_4_), channel_id=1, source_target_pairs={{0,8},{8,0},{16,24},{24,16},{1,9},{9,1},{17,25},{25,17},{2,10},{10... | collective-permute-start | bytes 393224 | tf_op jit(solution)/shard_map/ppermute | solution.py:550
  13.1 1.4 %collective-permute-start.3 = (bf16[2,128,256]{2,1,0:T(8,128)(2,1)S(1)}, bf16[2,128,256]{2,1,0:T(8,128)(2,1)S(1)}, u32[]{:S(2)}, u32[]{:S(2)}) collective-permute-start(bf16[2,128,256]{2,1,0:T(8,128)(2,1)S(1)} %collective-permute-done.2.refs_3_), channel_id=1, source_target_pairs={{0,1},{1,0},{2,3},{3,2},{4,5},{5,4},{6,7},{7,6},{8,9},{9,8},{10,11... | collective-permute-start | bytes 393224 | tf_op jit(solution)/shard_map/ppermute | solution.py:519
  13.1 1.4 %collective-permute-start.1 = (bf16[2,128,128]{2,1,0:T(8,128)(2,1)S(1)}, bf16[2,128,128]{2,1,0:T(8,128)(2,1)S(1)}, u32[]{:S(2)}, u32[]{:S(2)}) collective-permute-start(bf16[2,128,128]{2,1,0:T(8,128)(2,1)S(1)} %collective-permute-done.refs_1_), channel_id=1, source_target_pairs={{0,1},{1,0},{2,3},{3,2},{4,5},{5,4},{6,7},{7,6},{8,9},{9,8},{10,11... | collective-permute-start | bytes 196616 | tf_op jit(solution)/shard_map/ppermute | solution.py:519
  13.6 4.8 %collective-permute-start.9 = (bf16[256,256]{1,0:T(8,128)(2,1)S(1)}, bf16[256,256]{1,0:T(8,128)(2,1)S(1)}, u32[]{:S(2)}, u32[]{:S(2)}) collective-permute-start(bf16[256,256]{1,0:T(8,128)(2,1)S(1)} %collective-permute-done.6.over_y.refs_4_), channel_id=1, source_target_pairs={{0,1},{1,0},{2,3},{3,2},{4,5},{5,4},{6,7},{7,6},{8,9},{9,8},{10,11... | collective-permute-start | bytes 393224 | tf_op jit(solution)/shard_map/ppermute | solution.py:519
  16.9 1.9 %copy-start.1 = (bf16[1,1,2,256,256]{4,3,2,1,0:T(8,128)(2,1)S(1)}, bf16[1,1,2,256,256]{4,3,2,1,0:T(8,128)(2,1)}, u32[]{:S(2)}) copy-start(bf16[1,1,2,256,256]{4,3,2,1,0:T(8,128)(2,1)} %refs_0_.1) | copy-start | bytes 786436
  16.9 1.5 %collective-permute-start.10 = (bf16[256,256]{1,0:T(8,128)(2,1)S(1)}, bf16[256,256]{1,0:T(8,128)(2,1)S(1)}, u32[]{:S(2)}, u32[]{:S(2)}) collective-permute-start(bf16[256,256]{1,0:T(8,128)(2,1)S(1)} %collective-permute-done.7.over_z.refs_5_), channel_id=1, source_target_pairs={{0,1},{1,0},{2,3},{3,2},{4,5},{5,4},{6,7},{7,6},{8,9},{9,8},{10,11... | collective-permute-start | bytes 393224 | tf_op jit(solution)/shard_map/ppermute | solution.py:519
  17.3 1.5 %collective-permute-start.11 = (bf16[2,1,256,256]{3,2,1,0:T(8,128)(2,1)S(1)}, bf16[2,1,256,256]{3,2,1,0:T(8,128)(2,1)S(1)}, u32[]{:S(2)}, u32[]{:S(2)}) collective-permute-start(bf16[2,1,256,256]{3,2,1,0:T(8,128)(2,1)S(1)} %collective-permute-done.8.rest.refs_6_), channel_id=1, source_target_pairs={{0,1},{1,0},{2,3},{3,2},{4,5},{5,4},{6,7},{7,6},{8,9},{9,8},{10,11... | collective-permute-start | bytes 786440 | tf_op jit(solution)/shard_map/ppermute | solution.py:519
  23.2 1.7 %collective-permute-start.13 = (bf16[256,384]{1,0:T(8,128)(2,1)S(1)}, bf16[256,384]{1,0:T(8,128)(2,1)S(1)}, u32[]{:S(2)}, u32[]{:S(2)}) collective-permute-start(bf16[256,384]{1,0:T(8,128)(2,1)S(1)} %get-tuple-element.76), channel_id=1, source_target_pairs={{0,1},{1,0},{2,3},{3,2},{4,5},{5,4},{6,7},{7,6},{8,9},{9,8},{10,11... | collective-permute-start | bytes 589832 | tf_op jit(solution)/shard_map/ppermute | solution.py:519
  23.5 4.9 %collective-permute-start.12 = (bf16[272,128]{1,0:T(8,128)(2,1)S(1)}, bf16[272,128]{1,0:T(8,128)(2,1)S(1)}, u32[]{:S(2)}, u32[]{:S(2)}) collective-permute-start(bf16[272,128]{1,0:T(8,128)(2,1)S(1)} %get-tuple-element.74), channel_id=1, source_target_pairs={{0,4},{4,0},{1,5},{5,1},{2,6},{6,2},{3,7},{7,3},{8,12},{12,8},{9,1... | collective-permute-start | bytes 208904 | tf_op jit(solution)/shard_map/ppermute | solution.py:638
  25.0 4.5 %collective-permute-start.15 = (bf16[272,128]{1,0:T(8,128)(2,1)S(1)}, bf16[272,128]{1,0:T(8,128)(2,1)S(1)}, u32[]{:S(2)}, u32[]{:S(2)}) collective-permute-start(bf16[272,128]{1,0:T(8,128)(2,1)S(1)} %get-tuple-element.78), channel_id=1, source_target_pairs={{0,12},{1,4},{2,14},{3,6},{4,8},{5,0},{6,10},{7,2},{8,20},{9,5},{1... | collective-permute-start | bytes 208904 | tf_op jit(solution)/shard_map/ppermute | solution.py:652
  26.7 4.3 %collective-permute-start.14 = (bf16[272,256]{1,0:T(8,128)(2,1)S(1)}, bf16[272,256]{1,0:T(8,128)(2,1)S(1)}, u32[]{:S(2)}, u32[]{:S(2)}) collective-permute-start(bf16[272,256]{1,0:T(8,128)(2,1)S(1)} %get-tuple-element.77), channel_id=1, source_target_pairs={{0,8},{1,0},{2,10},{3,2},{4,12},{5,4},{6,14},{7,6},{8,16},{9,1},{1... | collective-permute-start | bytes 417800 | tf_op jit(solution)/shard_map/ppermute | solution.py:650
  28.8 4.2 %copy-start = (f32[2,128,256]{2,1,0:T(8,128)S(1)}, f32[2,128,256]{2,1,0:T(8,128)}, u32[]{:S(2)}) copy-start(f32[2,128,256]{2,1,0:T(8,128)} %object_ref.1) | copy-start | bytes 786436
  31.4 1.5 %collective-permute-start.16 = (bf16[3,128,256]{2,1,0:T(8,128)(2,1)S(1)}, bf16[3,128,256]{2,1,0:T(8,128)(2,1)S(1)}, u32[]{:S(2)}, u32[]{:S(2)}) collective-permute-start(bf16[3,128,256]{2,1,0:T(8,128)(2,1)S(1)} %sums.1.own_ref), channel_id=1, source_target_pairs={{0,1},{1,0},{2,3},{3,2},{4,5},{5,4},{6,7},{7,6},{8,9},{9,8},{10,11... | collective-permute-start | bytes 589832 | tf_op jit(solution)/shard_map/ppermute | solution.py:519

commit v13 on v12

--- a/solution.py
+++ b/solution.py
@@ -657,7 +657,7 @@
         in_specs=[vmem()] * (3 + sides),
         out_specs=vmem(),
         compiler_params=pltpu.CompilerParams(vmem_limit_bytes=small_bytes),
-        cost_estimate=cost(80),
+        cost_estimate=cost(40),
         name="levels",
     )(weight, record, own, *levels)
     summed = pl.pallas_call(

time: 33.9 us -> 33.3 us (0.982)
  waiting for transfers between devices: 5.14 us -> 4.22 us
    ppermute x1, waiting for transfers between devices: 1.42 us -> 0.01 us  [on_device(): rows = lax.ppermute(rows, axes, zigzag(0))]
    ppermute x1, waiting for transfers between devices: 0.75 us -> 1.51 us  [on_device(): lax.ppermute(piece, axes, zigzag(-step))]
    ppermute x1, starting transfers between devices: 1.68 us -> 1.09 us  [on_device(): rows = lax.ppermute(rows, axes, zigzag(0))]
    ppermute x1, starting transfers between devices: 1.68 us -> 2.23 us  [on_device(): lax.ppermute(piece, axes, zigzag(-step))]
  transfers between devices with their start and end apart: 17 -> 17, of which waited for: 6 -> 5; matrix products, arithmetic and copies ran while one was open for 0% -> 0% of each run, Pallas kernels for 11% -> 11%
where the time goes in v13:
time: 33.3 us; the launch traced here: 33 us
  starting transfers between devices  17.1 us (51%)
  Pallas kernels  10.9 us (33%)
  waiting for transfers between devices  4.22 us (13%)
  between operations  0.77 us (2%)
    ppermute x10, starting transfers between devices, exchange(): return lax.ppermute(array, 'mode', [(m, m ^ flip) for m in range(m_count)])  5.36 us
    pallas_call x1, Pallas kernels, on_device(): pl.pallas_call(functools.partial(back_kernel, sides, slots, tile_cols), o...  4.36 us
    ppermute x1, starting transfers between devices, on_device(): lax.ppermute(edge, axes, zigzag(step))  2.5 us
    ppermute x10, waiting for transfers between devices, exchange(): return lax.ppermute(array, 'mode', [(m, m ^ flip) for m in range(m_count)])  2.47 us
    ppermute x1, starting transfers between devices, on_device(): over_z = lax.ppermute(over_y, 'tx', [(z, z ^ 1) for z in range(z_count)])  2.33 us
    ppermute x1, starting transfers between devices, on_device(): lax.ppermute(piece, axes, zigzag(-step))  2.23 us
    pallas_call x1, Pallas kernels, on_device(): pl.pallas_call(functools.partial(start_kernel, sides, slots), out_shape=[...  1.64 us
    ppermute x1, starting transfers between devices, on_device(): rows = lax.ppermute(packed[0], axes, zigzag(0))  1.58 us
  transfers between devices with their start and end apart: 17, of which 5 were waited for; matrix products, arithmetic and copies ran while one was open for 0% of the time, Pallas kernels for 11%

profile of v13, /device:TPU:0, one launch (start us, length us, event | category | flops | bytes accessed | tf_op | source)
XLA Modules:
  0.0 33.0 jit_solution(15020612694734433565)
XLA Ops:
  0.0 1.6 %start.1 = (bf16[2,2,256,256]{3,2,1,0:T(8,128)(2,1)S(1)}, bf16[256,256]{1,0:T(8,128)(2,1)S(1)}, bf16[2,1,256,256]{3,2,1,0:T(8,128)(2,1)S(1)}, bf16[16,256]{1,0:T...) custom-call(f32[2,128,256]{2,1,0:T(8,128)} %object_ref.1, ...), custom_call_target="tpu_custom_call" | custom-call | tf_op jit(solution)/shard_map/start/pallas_call | solution.py:522
  1.6 0.5 %collective-permute-start.5 = (bf16[2,2,256,256]{3,2,1,0:T(8,128)(2,1)S(1)}, bf16[2,2,256,256]{3,2,1,0:T(8,128)(2,1)S(1)}, u32[]{:S(2)}, u32[]{:S(2)}) collective-permute-start(bf16[2,2,256,256]{3,2,1,0:T(8,128)(2,1)S(1)} %get-tuple-element.50.refs_6_.refs_2_), channel_id=1, source_target_pairs={{0,1},{1,0},{2,3},{3,2},{4,5},{5,4},{6,7},{7,6},{8,9},{9,8},{10,11... | collective-permute-start | bytes 1572872 | tf_op jit(solution)/shard_map/ppermute | solution.py:519
  2.2 2.6 %collective-permute-start.6 = (bf16[256,256]{1,0:T(8,128)(2,1)S(1)}, bf16[256,256]{1,0:T(8,128)(2,1)S(1)}, u32[]{:S(2)}, u32[]{:S(2)}) collective-permute-start(bf16[256,256]{1,0:T(8,128)(2,1)S(1)} %get-tuple-element.56), channel_id=1, source_target_pairs={{0,2},{1,3},{2,0},{3,1},{4,6},{5,7},{6,4},{7,5},{8,10},{9,11},{10,... | collective-permute-start | bytes 393224 | tf_op jit(solution)/shard_map/ppermute | solution.py:519
  4.8 1.6 %collective-permute-start.2 = (bf16[2,128,256]{2,1,0:T(8,128)(2,1)S(1)}, bf16[2,128,256]{2,1,0:T(8,128)(2,1)S(1)}, u32[]{:S(2)}, u32[]{:S(2)}) collective-permute-start(bf16[2,128,256]{2,1,0:T(8,128)(2,1)S(1)} %get-tuple-element.48.refs_0_), channel_id=1, source_target_pairs={{0,8},{1,0},{2,10},{3,2},{4,12},{5,4},{6,14},{7,6},{8,16},{9,1},{1... | collective-permute-start | bytes 393224 | tf_op jit(solution)/shard_map/ppermute | solution.py:552
  6.3 2.5 %collective-permute-start = (bf16[2,128,128]{2,1,0:T(8,128)(2,1)S(1)}, bf16[2,128,128]{2,1,0:T(8,128)(2,1)S(1)}, u32[]{:S(2)}, u32[]{:S(2)}) collective-permute-start(bf16[2,128,128]{2,1,0:T(8,128)(2,1)S(1)} %get-tuple-element.42), channel_id=1, source_target_pairs={{0,12},{1,4},{2,14},{3,6},{4,8},{5,0},{6,10},{7,2},{8,20},{9,5},{1... | collective-permute-start | bytes 196616 | tf_op jit(solution)/shard_map/ppermute | solution.py:553
  8.8 0.5 %collective-permute-start.8 = (bf16[2,1,256,256]{3,2,1,0:T(8,128)(2,1)S(1)}, bf16[2,1,256,256]{3,2,1,0:T(8,128)(2,1)S(1)}, u32[]{:S(2)}, u32[]{:S(2)}) collective-permute-start(bf16[2,1,256,256]{3,2,1,0:T(8,128)(2,1)S(1)} %get-tuple-element.57), channel_id=1, source_target_pairs={{0,2},{1,3},{2,0},{3,1},{4,6},{5,7},{6,4},{7,5},{8,10},{9,11},{10,... | collective-permute-start | bytes 786440 | tf_op jit(solution)/shard_map/ppermute | solution.py:519
  9.3 0.5 %collective-permute-start.4 = (bf16[2,128,128]{2,1,0:T(8,128)(2,1)S(1)}, bf16[2,128,128]{2,1,0:T(8,128)(2,1)S(1)}, u32[]{:S(2)}, u32[]{:S(2)}) collective-permute-start(bf16[2,128,128]{2,1,0:T(8,128)(2,1)S(1)} %get-tuple-element.42), channel_id=1, source_target_pairs={{0,4},{4,0},{1,5},{5,1},{2,6},{6,2},{3,7},{7,3},{8,12},{12,8},{9,1... | collective-permute-start | bytes 196616 | tf_op jit(solution)/shard_map/ppermute | solution.py:554
  10.5 0.2 collective-permute-done.refs_1_
  10.7 2.3 %collective-permute-start.7 = (bf16[256,256]{1,0:T(8,128)(2,1)S(1)}, bf16[256,256]{1,0:T(8,128)(2,1)S(1)}, u32[]{:S(2)}, u32[]{:S(2)}) collective-permute-start(bf16[256,256]{1,0:T(8,128)(2,1)S(1)} %collective-permute-done.6.over_y.refs_4_), channel_id=1, source_target_pairs={{0,8},{8,0},{16,24},{24,16},{1,9},{9,1},{17,25},{25,17},{2,10},{10... | collective-permute-start | bytes 393224 | tf_op jit(solution)/shard_map/ppermute | solution.py:550
  13.1 0.5 %collective-permute-start.1 = (bf16[2,128,128]{2,1,0:T(8,128)(2,1)S(1)}, bf16[2,128,128]{2,1,0:T(8,128)(2,1)S(1)}, u32[]{:S(2)}, u32[]{:S(2)}) collective-permute-start(bf16[2,128,128]{2,1,0:T(8,128)(2,1)S(1)} %collective-permute-done.refs_1_), channel_id=1, source_target_pairs={{0,1},{1,0},{2,3},{3,2},{4,5},{5,4},{6,7},{7,6},{8,9},{9,8},{10,11... | collective-permute-start | bytes 196616 | tf_op jit(solution)/shard_map/ppermute | solution.py:519
  13.6 0.0 collective-permute-done.4.refs_5_
  13.6 0.1 collective-permute-start.9
  13.7 0.8 %collective-permute-done.1.refs_2_ = bf16[2,128,128]{2,1,0:T(8,128)(2,1)S(1)} collective-permute-done((bf16[2,128,128]{2,1,0:T(8,128)(2,1)S(1)}, bf16[2,128,128]{2,1,0:T(8,128)(2,1)S(1)}, u32[]{:S(2)}, u32[]{:S(2)}) %collective-permute-start.1) | collective-permute-done | bytes 65568 | tf_op jit(solution)/shard_map/ppermute | solution.py:519
  14.5 1.5 %near.1 = (f32[2,256,256]{2,1,0:T(8,128)S(1)}, f32[2,256,512]{2,1,0:T(8,128)S(1)}, bf16[2,512,256]{2,1,0:T(8,128)(2,1)S(1)}, f32[2,256,256]{2,1,0:T(8,128)S(1)}) custom-call(s32[8,128]{1,0:T(8,128)S(1)} %get-tuple-element.47.spot_ref, bf16[2,128,256]{2,1,0:T(8,128)(2,1)S(1)} %get-tuple-element.48.refs_0_, ...), custom_call_target="tpu_custom_call" | custom-call | flops 33554432 | tf_op jit(solution)/shard_map/near/pallas_call | solution.py:577
  16.0 0.9 %core.1 = (f32[2,256,512]{2,1,0:T(8,128)S(1)}, bf16[2,512,256]{2,1,0:T(8,128)(2,1)S(1)}, f32[2,256,256]{2,1,0:T(8,128)S(1)}) custom-call(f32[2,256,256]{2,1,0:T(8,128)S(1)} %get-tuple-element.53.patch_ref.refs_1_, bf16[2,2,256,256]{3,2,1,0:T(8,128)(2,1)S(1)} %collective-permute-done.5.core.refs_3_, ...), custom_call_target="tpu_custom_call" | custom-call | flops 33554432 | tf_op jit(solution)/shard_map/core/pallas_call | solution.py:586
  16.9 0.0 copy-start.1
  16.9 0.4 %collective-permute-start.10 = (bf16[256,256]{1,0:T(8,128)(2,1)S(1)}, bf16[256,256]{1,0:T(8,128)(2,1)S(1)}, u32[]{:S(2)}, u32[]{:S(2)}) collective-permute-start(bf16[256,256]{1,0:T(8,128)(2,1)S(1)} %collective-permute-done.7.over_z.refs_5_), channel_id=1, source_target_pairs={{0,1},{1,0},{2,3},{3,2},{4,5},{5,4},{6,7},{7,6},{8,9},{9,8},{10,11... | collective-permute-start | bytes 393224 | tf_op jit(solution)/shard_map/ppermute | solution.py:519
  17.3 0.2 collective-permute-start.11
  17.5 0.9 %over.1 = (f32[2,256,512]{2,1,0:T(8,128)S(1)}, bf16[2,512,256]{2,1,0:T(8,128)(2,1)S(1)}, f32[2,256,256]{2,1,0:T(8,128)S(1)}) custom-call(f32[2,256,256]{2,1,0:T(8,128)S(1)} %get-tuple-element.53.patch_ref.refs_1_, bf16[256,256]{1,0:T(8,128)(2,1)S(1)} %collective-permute-done.6.over_y.refs_4_, bf16[256,256]{1,0:T(8,128)(2,1)S(1)} %collective-permute-done.7.over_z.refs_5_, ...), custom_call_target="tpu_custom_call" | custom-call | flops 3355443200 | tf_op jit(solution)/shard_map/over/pallas_call | solution.py:599
  18.4 0.4 %collective-permute-done.11.refs_9_ = bf16[2,1,256,256]{3,2,1,0:T(8,128)(2,1)S(1)} collective-permute-done((bf16[2,1,256,256]{3,2,1,0:T(8,128)(2,1)S(1)}, bf16[2,1,256,256]{3,2,1,0:T(8,128)(2,1)S(1)}, u32[]{:S(2)}, u32[]{:S(2)}) %collective-permute-start.11) | collective-permute-done | bytes 262176 | tf_op jit(solution)/shard_map/ppermute | solution.py:519
  18.8 4.4 %back.1 = (bf16[256,256]{1,0:T(8,128)(2,1)S(1)}, bf16[256,256]{1,0:T(8,128)(2,1)S(1)}, bf16[256,384]{1,0:T(8,128)(2,1)S(1)}, bf16[256,384]{1,0:T(8,128)(2,1)S(1)}, bf16[272,128]{1,0:T(8,128)(2,1)S(1)}) custom-call(bf16[16,256]{1,0:T(8,128)(2,1)S(1)} %live.1.record_ref, s32[8,128]{1,0:T(8,128)S(1)} %get-tuple-element.47.spot_ref, ...), custom_call_target="tpu_custom_call" | custom-call | flops 2684354560 | tf_op jit(solution)/shard_map/back/pallas_call | solution.py:611
  23.2 0.2 collective-permute-start.13
  23.5 1.5 %collective-permute-start.12 = (bf16[272,128]{1,0:T(8,128)(2,1)S(1)}, bf16[272,128]{1,0:T(8,128)(2,1)S(1)}, u32[]{:S(2)}, u32[]{:S(2)}) collective-permute-start(bf16[272,128]{1,0:T(8,128)(2,1)S(1)} %get-tuple-element.74), channel_id=1, source_target_pairs={{0,4},{4,0},{1,5},{5,1},{2,6},{6,2},{3,7},{7,3},{8,12},{12,8},{9,1... | collective-permute-start | bytes 208904 | tf_op jit(solution)/shard_map/ppermute | solution.py:638
  25.0 0.1 meet.1
  25.0 1.1 %collective-permute-start.14 = (bf16[272,256]{1,0:T(8,128)(2,1)S(1)}, bf16[272,256]{1,0:T(8,128)(2,1)S(1)}, u32[]{:S(2)}, u32[]{:S(2)}) collective-permute-start(bf16[272,256]{1,0:T(8,128)(2,1)S(1)} %get-tuple-element.77), channel_id=1, source_target_pairs={{0,8},{1,0},{2,10},{3,2},{4,12},{5,4},{6,14},{7,6},{8,16},{9,1},{1... | collective-permute-start | bytes 417800 | tf_op jit(solution)/shard_map/ppermute | solution.py:650
  26.1 2.2 %collective-permute-start.15 = (bf16[272,128]{1,0:T(8,128)(2,1)S(1)}, bf16[272,128]{1,0:T(8,128)(2,1)S(1)}, u32[]{:S(2)}, u32[]{:S(2)}) collective-permute-start(bf16[272,128]{1,0:T(8,128)(2,1)S(1)} %get-tuple-element.78), channel_id=1, source_target_pairs={{0,12},{1,4},{2,14},{3,6},{4,8},{5,0},{6,10},{7,2},{8,20},{9,5},{1... | collective-permute-start | bytes 208904 | tf_op jit(solution)/shard_map/ppermute | solution.py:652
  28.3 0.4 %levels.1.level_ref = f32[3,128,256]{2,1,0:T(8,128)S(1)} custom-call(bf16[256,256]{1,0:T(8,128)(2,1)S(1)} %get-tuple-element.72.weight_ref, bf16[16,256]{1,0:T(8,128)(2,1)S(1)} %live.1.record_ref, bf16[256,256]{1,0:T(8,128)(2,1)S(1)} %get-tuple-element.73.own_ref, bf16[272,128]{1,0:T(8,128)(2,1)S(1)} %collective-permute-done.12.refs_0_), custom_call_target="tpu_custom_call" | custom-call | flops 1342177280 | tf_op jit(solution)/shard_map/levels/pallas_call | solution.py:654
  28.8 1.5 %collective-permute-done.15.refs_0_ = bf16[272,128]{1,0:T(8,128)(2,1)S(1)} collective-permute-done((bf16[272,128]{1,0:T(8,128)(2,1)S(1)}, bf16[272,128]{1,0:T(8,128)(2,1)S(1)}, u32[]{:S(2)}, u32[]{:S(2)}) %collective-permute-start.15) | collective-permute-done | bytes 69664 | tf_op jit(solution)/shard_map/ppermute | solution.py:652
  30.3 0.5 %sums.1.own_ref = bf16[3,128,256]{2,1,0:T(8,128)(2,1)S(1)} custom-call(bf16[256,256]{1,0:T(8,128)(2,1)S(1)} %get-tuple-element.72.weight_ref, f32[3,128,256]{2,1,0:T(8,128)S(1)} %levels.1.level_ref, bf16[272,256]{1,0:T(8,128)(2,1)S(1)} %collective-permute-done.14.rows_ref, bf16[272,128]{1,0:T(8,128)(2,1)S(1)} %collective-permute-done.15.refs_0_), custom_call_target="tpu_custom_call" | custom-call | tf_op jit(solution)/shard_map/sums/pallas_call | solution.py:663
  30.7 0.3 %collective-permute-start.16 = (bf16[3,128,256]{2,1,0:T(8,128)(2,1)S(1)}, bf16[3,128,256]{2,1,0:T(8,128)(2,1)S(1)}, u32[]{:S(2)}, u32[]{:S(2)}) collective-permute-start(bf16[3,128,256]{2,1,0:T(8,128)(2,1)S(1)} %sums.1.own_ref), channel_id=1, source_target_pairs={{0,1},{1,0},{2,3},{3,2},{4,5},{5,4},{6,7},{7,6},{8,9},{9,8},{10,11... | collective-permute-start | bytes 589832 | tf_op jit(solution)/shard_map/ppermute | solution.py:519
  31.1 1.2 %collective-permute-done.16.other_ref = bf16[3,128,256]{2,1,0:T(8,128)(2,1)S(1)} collective-permute-done((bf16[3,128,256]{2,1,0:T(8,128)(2,1)S(1)}, bf16[3,128,256]{2,1,0:T(8,128)(2,1)S(1)}, u32[]{:S(2)}, u32[]{:S(2)}) %collective-permute-start.16) | collective-permute-done | bytes 196640 | tf_op jit(solution)/shard_map/ppermute | solution.py:519
  32.3 0.8 %update.1 = f32[2,128,256]{2,1,0:T(8,128)} custom-call(f32[2,128,256]{2,1,0:T(8,128)S(1)} %copy-done, bf16[3,128,256]{2,1,0:T(8,128)(2,1)S(1)} %sums.1.own_ref, bf16[3,128,256]{2,1,0:T(8,128)(2,1)S(1)} %collective-permute-done.16.other_ref), custom_call_target="tpu_custom_call" | custom-call | tf_op jit(solution)/shard_map/update/pallas_call | solution.py:671
  (16 shorter events, 0.0 us)
Async XLA Ops:
  1.6 7.2 %collective-permute-start.5 = (bf16[2,2,256,256]{3,2,1,0:T(8,128)(2,1)S(1)}, bf16[2,2,256,256]{3,2,1,0:T(8,128)(2,1)S(1)}, u32[]{:S(2)}, u32[]{:S(2)}) collective-permute-start(bf16[2,2,256,256]{3,2,1,0:T(8,128)(2,1)S(1)} %get-tuple-element.50.refs_6_.refs_2_), channel_id=1, source_target_pairs={{0,1},{1,0},{2,3},{3,2},{4,5},{5,4},{6,7},{7,6},{8,9},{9,8},{10,11... | collective-permute-start | bytes 1572872 | tf_op jit(solution)/shard_map/ppermute | solution.py:519
  2.2 8.6 %collective-permute-start.6 = (bf16[256,256]{1,0:T(8,128)(2,1)S(1)}, bf16[256,256]{1,0:T(8,128)(2,1)S(1)}, u32[]{:S(2)}, u32[]{:S(2)}) collective-permute-start(bf16[256,256]{1,0:T(8,128)(2,1)S(1)} %get-tuple-element.56), channel_id=1, source_target_pairs={{0,2},{1,3},{2,0},{3,1},{4,6},{5,7},{6,4},{7,5},{8,10},{9,11},{10,... | collective-permute-start | bytes 393224 | tf_op jit(solution)/shard_map/ppermute | solution.py:519
  4.8 8.3 %collective-permute-start.2 = (bf16[2,128,256]{2,1,0:T(8,128)(2,1)S(1)}, bf16[2,128,256]{2,1,0:T(8,128)(2,1)S(1)}, u32[]{:S(2)}, u32[]{:S(2)}) collective-permute-start(bf16[2,128,256]{2,1,0:T(8,128)(2,1)S(1)} %get-tuple-element.48.refs_0_), channel_id=1, source_target_pairs={{0,8},{1,0},{2,10},{3,2},{4,12},{5,4},{6,14},{7,6},{8,16},{9,1},{1... | collective-permute-start | bytes 393224 | tf_op jit(solution)/shard_map/ppermute | solution.py:552
  6.3 4.4 %collective-permute-start = (bf16[2,128,128]{2,1,0:T(8,128)(2,1)S(1)}, bf16[2,128,128]{2,1,0:T(8,128)(2,1)S(1)}, u32[]{:S(2)}, u32[]{:S(2)}) collective-permute-start(bf16[2,128,128]{2,1,0:T(8,128)(2,1)S(1)} %get-tuple-element.42), channel_id=1, source_target_pairs={{0,12},{1,4},{2,14},{3,6},{4,8},{5,0},{6,10},{7,2},{8,20},{9,5},{1... | collective-permute-start | bytes 196616 | tf_op jit(solution)/shard_map/ppermute | solution.py:553
  8.8 8.1 %collective-permute-start.8 = (bf16[2,1,256,256]{3,2,1,0:T(8,128)(2,1)S(1)}, bf16[2,1,256,256]{3,2,1,0:T(8,128)(2,1)S(1)}, u32[]{:S(2)}, u32[]{:S(2)}) collective-permute-start(bf16[2,1,256,256]{3,2,1,0:T(8,128)(2,1)S(1)} %get-tuple-element.57), channel_id=1, source_target_pairs={{0,2},{1,3},{2,0},{3,1},{4,6},{5,7},{6,4},{7,5},{8,10},{9,11},{10,... | collective-permute-start | bytes 786440 | tf_op jit(solution)/shard_map/ppermute | solution.py:519
  9.3 4.3 %collective-permute-start.4 = (bf16[2,128,128]{2,1,0:T(8,128)(2,1)S(1)}, bf16[2,128,128]{2,1,0:T(8,128)(2,1)S(1)}, u32[]{:S(2)}, u32[]{:S(2)}) collective-permute-start(bf16[2,128,128]{2,1,0:T(8,128)(2,1)S(1)} %get-tuple-element.42), channel_id=1, source_target_pairs={{0,4},{4,0},{1,5},{5,1},{2,6},{6,2},{3,7},{7,3},{8,12},{12,8},{9,1... | collective-permute-start | bytes 196616 | tf_op jit(solution)/shard_map/ppermute | solution.py:554
  10.7 6.1 %collective-permute-start.7 = (bf16[256,256]{1,0:T(8,128)(2,1)S(1)}, bf16[256,256]{1,0:T(8,128)(2,1)S(1)}, u32[]{:S(2)}, u32[]{:S(2)}) collective-permute-start(bf16[256,256]{1,0:T(8,128)(2,1)S(1)} %collective-permute-done.6.over_y.refs_4_), channel_id=1, source_target_pairs={{0,8},{8,0},{16,24},{24,16},{1,9},{9,1},{17,25},{25,17},{2,10},{10... | collective-permute-start | bytes 393224 | tf_op jit(solution)/shard_map/ppermute | solution.py:550
  13.1 1.4 %collective-permute-start.3 = (bf16[2,128,256]{2,1,0:T(8,128)(2,1)S(1)}, bf16[2,128,256]{2,1,0:T(8,128)(2,1)S(1)}, u32[]{:S(2)}, u32[]{:S(2)}) collective-permute-start(bf16[2,128,256]{2,1,0:T(8,128)(2,1)S(1)} %collective-permute-done.2.refs_3_), channel_id=1, source_target_pairs={{0,1},{1,0},{2,3},{3,2},{4,5},{5,4},{6,7},{7,6},{8,9},{9,8},{10,11... | collective-permute-start | bytes 393224 | tf_op jit(solution)/shard_map/ppermute | solution.py:519
  13.1 1.4 %collective-permute-start.1 = (bf16[2,128,128]{2,1,0:T(8,128)(2,1)S(1)}, bf16[2,128,128]{2,1,0:T(8,128)(2,1)S(1)}, u32[]{:S(2)}, u32[]{:S(2)}) collective-permute-start(bf16[2,128,128]{2,1,0:T(8,128)(2,1)S(1)} %collective-permute-done.refs_1_), channel_id=1, source_target_pairs={{0,1},{1,0},{2,3},{3,2},{4,5},{5,4},{6,7},{7,6},{8,9},{9,8},{10,11... | collective-permute-start | bytes 196616 | tf_op jit(solution)/shard_map/ppermute | solution.py:519
  13.6 4.8 %collective-permute-start.9 = (bf16[256,256]{1,0:T(8,128)(2,1)S(1)}, bf16[256,256]{1,0:T(8,128)(2,1)S(1)}, u32[]{:S(2)}, u32[]{:S(2)}) collective-permute-start(bf16[256,256]{1,0:T(8,128)(2,1)S(1)} %collective-permute-done.6.over_y.refs_4_), channel_id=1, source_target_pairs={{0,1},{1,0},{2,3},{3,2},{4,5},{5,4},{6,7},{7,6},{8,9},{9,8},{10,11... | collective-permute-start | bytes 393224 | tf_op jit(solution)/shard_map/ppermute | solution.py:519
  16.9 1.9 %copy-start.1 = (bf16[1,1,2,256,256]{4,3,2,1,0:T(8,128)(2,1)S(1)}, bf16[1,1,2,256,256]{4,3,2,1,0:T(8,128)(2,1)}, u32[]{:S(2)}) copy-start(bf16[1,1,2,256,256]{4,3,2,1,0:T(8,128)(2,1)} %refs_0_.1) | copy-start | bytes 786436
  16.9 1.5 %collective-permute-start.10 = (bf16[256,256]{1,0:T(8,128)(2,1)S(1)}, bf16[256,256]{1,0:T(8,128)(2,1)S(1)}, u32[]{:S(2)}, u32[]{:S(2)}) collective-permute-start(bf16[256,256]{1,0:T(8,128)(2,1)S(1)} %collective-permute-done.7.over_z.refs_5_), channel_id=1, source_target_pairs={{0,1},{1,0},{2,3},{3,2},{4,5},{5,4},{6,7},{7,6},{8,9},{9,8},{10,11... | collective-permute-start | bytes 393224 | tf_op jit(solution)/shard_map/ppermute | solution.py:519
  17.3 1.5 %collective-permute-start.11 = (bf16[2,1,256,256]{3,2,1,0:T(8,128)(2,1)S(1)}, bf16[2,1,256,256]{3,2,1,0:T(8,128)(2,1)S(1)}, u32[]{:S(2)}, u32[]{:S(2)}) collective-permute-start(bf16[2,1,256,256]{3,2,1,0:T(8,128)(2,1)S(1)} %collective-permute-done.8.rest.refs_6_), channel_id=1, source_target_pairs={{0,1},{1,0},{2,3},{3,2},{4,5},{5,4},{6,7},{7,6},{8,9},{9,8},{10,11... | collective-permute-start | bytes 786440 | tf_op jit(solution)/shard_map/ppermute | solution.py:519
  23.2 1.7 %collective-permute-start.13 = (bf16[256,384]{1,0:T(8,128)(2,1)S(1)}, bf16[256,384]{1,0:T(8,128)(2,1)S(1)}, u32[]{:S(2)}, u32[]{:S(2)}) collective-permute-start(bf16[256,384]{1,0:T(8,128)(2,1)S(1)} %get-tuple-element.76), channel_id=1, source_target_pairs={{0,1},{1,0},{2,3},{3,2},{4,5},{5,4},{6,7},{7,6},{8,9},{9,8},{10,11... | collective-permute-start | bytes 589832 | tf_op jit(solution)/shard_map/ppermute | solution.py:519
  23.5 4.9 %collective-permute-start.12 = (bf16[272,128]{1,0:T(8,128)(2,1)S(1)}, bf16[272,128]{1,0:T(8,128)(2,1)S(1)}, u32[]{:S(2)}, u32[]{:S(2)}) collective-permute-start(bf16[272,128]{1,0:T(8,128)(2,1)S(1)} %get-tuple-element.74), channel_id=1, source_target_pairs={{0,4},{4,0},{1,5},{5,1},{2,6},{6,2},{3,7},{7,3},{8,12},{12,8},{9,1... | collective-permute-start | bytes 208904 | tf_op jit(solution)/shard_map/ppermute | solution.py:638
  25.0 5.3 %collective-permute-start.14 = (bf16[272,256]{1,0:T(8,128)(2,1)S(1)}, bf16[272,256]{1,0:T(8,128)(2,1)S(1)}, u32[]{:S(2)}, u32[]{:S(2)}) collective-permute-start(bf16[272,256]{1,0:T(8,128)(2,1)S(1)} %get-tuple-element.77), channel_id=1, source_target_pairs={{0,8},{1,0},{2,10},{3,2},{4,12},{5,4},{6,14},{7,6},{8,16},{9,1},{1... | collective-permute-start | bytes 417800 | tf_op jit(solution)/shard_map/ppermute | solution.py:650
  26.1 4.2 %collective-permute-start.15 = (bf16[272,128]{1,0:T(8,128)(2,1)S(1)}, bf16[272,128]{1,0:T(8,128)(2,1)S(1)}, u32[]{:S(2)}, u32[]{:S(2)}) collective-permute-start(bf16[272,128]{1,0:T(8,128)(2,1)S(1)} %get-tuple-element.78), channel_id=1, source_target_pairs={{0,12},{1,4},{2,14},{3,6},{4,8},{5,0},{6,10},{7,2},{8,20},{9,5},{1... | collective-permute-start | bytes 208904 | tf_op jit(solution)/shard_map/ppermute | solution.py:652
  28.7 3.5 %copy-start = (f32[2,128,256]{2,1,0:T(8,128)S(1)}, f32[2,128,256]{2,1,0:T(8,128)}, u32[]{:S(2)}) copy-start(f32[2,128,256]{2,1,0:T(8,128)} %object_ref.1) | copy-start | bytes 786436
  30.7 1.5 %collective-permute-start.16 = (bf16[3,128,256]{2,1,0:T(8,128)(2,1)S(1)}, bf16[3,128,256]{2,1,0:T(8,128)(2,1)S(1)}, u32[]{:S(2)}, u32[]{:S(2)}) collective-permute-start(bf16[3,128,256]{2,1,0:T(8,128)(2,1)S(1)} %sums.1.own_ref), channel_id=1, source_target_pairs={{0,1},{1,0},{2,3},{3,2},{4,5},{5,4},{6,7},{7,6},{8,9},{9,8},{10,11... | collective-permute-start | bytes 589832 | tf_op jit(solution)/shard_map/ppermute | solution.py:519

commit v14 on v13

--- a/solution.py
+++ b/solution.py
@@ -36,20 +36,6 @@
 
 def iota(shape, dim):
     return lax.broadcasted_iota(jnp.int32, shape, dim)
-
-
-def sent_order(sides):
-    corners = [at for index in range(sides) for at in (4 + 3 * index, 5 + 3 * index)]
-    return [0] + corners + [1, 2] + [3 + 3 * index for index in range(sides)]
-
-
-def in_sent_order(pieces):
-    return [pieces[at] for at in sent_order(len(pieces) // 3 - 1)]
-
-
-def from_sent_order(pieces):
-    order = sent_order(len(pieces) // 3 - 1)
-    return [pieces[order.index(at)] for at in range(len(pieces))]
 
 
 def wide(tall):
@@ -155,35 +141,38 @@
     return jnp.where(value == 0, 0, side - value)
 
 
-def patch_of(sides, z_count, x_count, side, spot_ref, pieces):
-    z_index, x_index, parity = here()
-    row_at, col_at = spot_ref[0, 0], spot_ref[1, 0]
-    half = side // 2
+def joined(piece, turn_a, turn_b, channel, z_count, row_at):
+    z_index, _, parity = here()
     even = parity == 0
     low_shown = z_index > 0
     high_shown = z_index < z_count - 1
-
-    def joined(piece, a, b, channel):
-        level = piece[channel].astype(jnp.float32)
-        turn_a = a[channel].astype(jnp.float32)
-        turn_b = b[channel].astype(jnp.float32)
-        low = jnp.where(even & low_shown, turn_a, jnp.where(low_shown, turn_b, 0.0))
-        high = jnp.where(even & high_shown, turn_b, jnp.where(high_shown, turn_a, 0.0))
-        first = jnp.where(iota(low.shape, 0) >= row_at, low, high)
-        return jnp.concatenate([first, level], axis=0)
-
+    level = piece[channel].astype(jnp.float32)
+    first = turn_a[channel].astype(jnp.float32)
+    second = turn_b[channel].astype(jnp.float32)
+    low = jnp.where(even & low_shown, first, jnp.where(low_shown, second, 0.0))
+    high = jnp.where(even & high_shown, second, jnp.where(high_shown, first, 0.0))
+    upper = jnp.where(iota(low.shape, 0) >= row_at, low, high)
+    return jnp.concatenate([upper, level], axis=0)
+
+
+def edge_kernel(z_count, spot_ref, level_ref, turn_a, turn_b, out_ref):
+    for channel in range(2):
+        out_ref[channel] = joined(level_ref, turn_a, turn_b, channel, z_count, spot_ref[0, 0])
+
+
+def patch_of(z_count, x_count, spot_ref, pieces, edges):
+    _, x_index, _ = here()
+    row_at, col_at = spot_ref[0, 0], spot_ref[1, 0]
+    side, half = edges[0].shape[1:]
     out = []
     for channel in range(2):
-        own = joined(*pieces[:3], channel)
-        sides_joined = [
-            joined(*pieces[3 + 3 * index : 6 + 3 * index], channel) for index in range(sides)
-        ]
-        if sides == 1:
-            left = jnp.where(x_index == 1, sides_joined[0], 0.0)
-            right = jnp.where(x_index == 0, sides_joined[0], 0.0)
+        own = joined(*pieces, channel, z_count, row_at)
+        if len(edges) == 1:
+            left = jnp.where(x_index == 1, edges[0][channel], 0.0)
+            right = jnp.where(x_index == 0, edges[0][channel], 0.0)
         else:
-            left = jnp.where(x_index > 0, sides_joined[0], 0.0)
-            right = jnp.where(x_index < x_count - 1, sides_joined[1], 0.0)
+            left = jnp.where(x_index > 0, edges[0][channel], 0.0)
+            right = jnp.where(x_index < x_count - 1, edges[1][channel], 0.0)
         at = iota(left.shape, 1)
         window = jnp.concatenate(
             [
@@ -265,12 +254,9 @@
 
 
 def near_kernel(sides, z_count, x_count, spot_ref, *refs):
-    n_pieces = 3 + 3 * sides
-    pieces = from_sent_order(refs[:n_pieces])
-    own, direct, swapped = refs[n_pieces : n_pieces + 3]
-    patch_ref, far_ref, exit_ref, sum_ref = refs[n_pieces + 3 :]
-    side = own.shape[2]
-    patch = patch_of(sides, z_count, x_count, side, spot_ref, pieces)
+    pieces, edges = refs[:3], refs[3 : 3 + sides]
+    own, direct, swapped, patch_ref, far_ref, exit_ref, sum_ref = refs[3 + sides :]
+    patch = patch_of(z_count, x_count, spot_ref, pieces, edges)
     patch_ref[0], patch_ref[1] = patch
     sum_ref[0], sum_ref[1] = forward(
         modes_of(own), patch, direct[...], swapped[...], far_ref, exit_ref, 0
@@ -559,14 +545,22 @@
         in_specs=[vmem(), smem()],
         out_specs=vmem(),
         compiler_params=pltpu.CompilerParams(vmem_limit_bytes=small_bytes),
-        cost_estimate=cost(40),
+        cost_estimate=cost(1),
         name="live",
     )(record, live)
     corners, record = lax.optimization_barrier((corners, record))
-    pieces = [packed[0], rows, exchange(rows, 1)]
-    for at_level, corner in zip(levels, corners):
-        pieces += [at_level, corner, exchange(corner, 1)]
-    n_pieces = len(pieces)
+    edges = [
+        pl.pallas_call(
+            functools.partial(edge_kernel, z_count),
+            out_shape=jax.ShapeDtypeStruct((2, side, half), jnp.float32),
+            in_specs=[vmem()] * 4,
+            out_specs=vmem(),
+            compiler_params=pltpu.CompilerParams(vmem_limit_bytes=small_bytes),
+            cost_estimate=cost(50),
+            name="edge",
+        )(spot, at_level, corner, exchange(corner, 1))
+        for at_level, corner in zip(levels, corners)
+    ]
     ext_cols = tile_cols + sides * half
 
     waves = [
@@ -577,12 +571,12 @@
     patch, *near = pl.pallas_call(
         functools.partial(near_kernel, sides, z_count, x_count),
         out_shape=[jax.ShapeDtypeStruct((2, side, side), jnp.float32)] + waves,
-        in_specs=[vmem()] * (n_pieces + 4),
+        in_specs=[vmem()] * (7 + sides),
         out_specs=[vmem()] * 4,
         compiler_params=pltpu.CompilerParams(vmem_limit_bytes=wave_bytes),
         cost_estimate=cost(1),
         name="near",
-    )(spot, *in_sent_order(pieces), probe_low, direct, swapped)
+    )(spot, packed[0], rows, exchange(rows, 1), *edges, probe_low, direct, swapped)
     other = pl.pallas_call(
         core_kernel,
         out_shape=waves,
@@ -602,7 +596,7 @@
         in_specs=[vmem()] * 6,
         out_specs=[vmem()] * 3,
         compiler_params=pltpu.CompilerParams(vmem_limit_bytes=wave_bytes),
-        cost_estimate=cost(100),
+        cost_estimate=cost(60),
         name="over",
     )(patch, *over_group, direct, swapped)
     piece_rows = 2 * half + record_rows

time: 33.3 us -> 33.8 us (1.015)
  waiting for transfers between devices: 4.22 us -> 6.41 us
  starting transfers between devices: 17.1 us -> 15.5 us
    ppermute x10, starting transfers between devices: 5.36 us -> 3.63 us  [exchange(): return lax.ppermute(array, 'mode', [(m, m ^ flip) for m in range(m_count)])]
    ppermute x10, waiting for transfers between devices: 2.47 us -> 4.1 us  [exchange(): return lax.ppermute(array, 'mode', [(m, m ^ flip) for m in range(m_count)])]
    ppermute x1, starting transfers between devices: 2.5 us -> 3.57 us  [on_device(): lax.ppermute(edge, axes, zigzag(step))]
    ppermute x1, starting transfers between devices: 1.49 us -> 0.71 us  [on_device(): lax.ppermute(piece, 'ty', level(-step))]
    ppermute x1, waiting for transfers between devices: 1.51 us -> 2.2 us  [on_device(): lax.ppermute(piece, axes, zigzag(-step))]
    ppermute x1, starting transfers between devices: 2.23 us -> 1.75 us  [on_device(): lax.ppermute(piece, axes, zigzag(-step))]
  transfers between devices with their start and end apart: 17 -> 17, of which waited for: 5 -> 8; matrix products, arithmetic and copies ran while one was open for 0% -> 0% of each run, Pallas kernels for 11% -> 11%
where the time goes in v14:
time: 33.8 us; the launch traced here: 33.7 us
  starting transfers between devices  15.5 us (46%)
  Pallas kernels  10.9 us (32%)
  waiting for transfers between devices  6.41 us (19%)
  between operations  0.8 us (2%)
    pallas_call x1, Pallas kernels, on_device(): pl.pallas_call(functools.partial(back_kernel, sides, slots, tile_cols), o...  4.36 us
    ppermute x10, waiting for transfers between devices, exchange(): return lax.ppermute(array, 'mode', [(m, m ^ flip) for m in range(m_count)])  4.1 us
    ppermute x10, starting transfers between devices, exchange(): return lax.ppermute(array, 'mode', [(m, m ^ flip) for m in range(m_count)])  3.63 us
    ppermute x1, starting transfers between devices, on_device(): lax.ppermute(edge, axes, zigzag(step))  3.57 us
    ppermute x1, starting transfers between devices, on_device(): over_z = lax.ppermute(over_y, 'tx', [(z, z ^ 1) for z in range(z_count)])  2.51 us
    ppermute x1, waiting for transfers between devices, on_device(): lax.ppermute(piece, axes, zigzag(-step))  2.2 us
    ppermute x1, starting transfers between devices, on_device(): lax.ppermute(piece, axes, zigzag(-step))  1.75 us
    pallas_call x1, Pallas kernels, on_device(): pl.pallas_call(functools.partial(start_kernel, sides, slots), out_shape=[...  1.64 us
  transfers between devices with their start and end apart: 17, of which 8 were waited for; matrix products, arithmetic and copies ran while one was open for 0% of the time, Pallas kernels for 11%

profile of v14, /device:TPU:0, one launch (start us, length us, event | category | flops | bytes accessed | tf_op | source)
XLA Modules:
  0.0 33.7 jit_solution(4294829783407171960)
XLA Ops:
  0.0 1.6 %start.1 = (bf16[2,2,256,256]{3,2,1,0:T(8,128)(2,1)S(1)}, bf16[256,256]{1,0:T(8,128)(2,1)S(1)}, bf16[2,1,256,256]{3,2,1,0:T(8,128)(2,1)S(1)}, bf16[16,256]{1,0:T...) custom-call(f32[2,128,256]{2,1,0:T(8,128)} %object_ref.1, ...), custom_call_target="tpu_custom_call" | custom-call | tf_op jit(solution)/shard_map/start/pallas_call | solution.py:508
  1.6 0.5 %collective-permute-start.5 = (bf16[2,2,256,256]{3,2,1,0:T(8,128)(2,1)S(1)}, bf16[2,2,256,256]{3,2,1,0:T(8,128)(2,1)S(1)}, u32[]{:S(2)}, u32[]{:S(2)}) collective-permute-start(bf16[2,2,256,256]{3,2,1,0:T(8,128)(2,1)S(1)} %get-tuple-element.50.refs_4_.refs_2_), channel_id=1, source_target_pairs={{0,1},{1,0},{2,3},{3,2},{4,5},{5,4},{6,7},{7,6},{8,9},{9,8},{10,11... | collective-permute-start | bytes 1572872 | tf_op jit(solution)/shard_map/ppermute | solution.py:505
  2.2 3.6 %collective-permute-start = (bf16[2,128,128]{2,1,0:T(8,128)(2,1)S(1)}, bf16[2,128,128]{2,1,0:T(8,128)(2,1)S(1)}, u32[]{:S(2)}, u32[]{:S(2)}) collective-permute-start(bf16[2,128,128]{2,1,0:T(8,128)(2,1)S(1)} %get-tuple-element.42), channel_id=1, source_target_pairs={{0,12},{1,4},{2,14},{3,6},{4,8},{5,0},{6,10},{7,2},{8,20},{9,5},{1... | collective-permute-start | bytes 196616 | tf_op jit(solution)/shard_map/ppermute | solution.py:539
  5.7 1.5 %collective-permute-start.6 = (bf16[256,256]{1,0:T(8,128)(2,1)S(1)}, bf16[256,256]{1,0:T(8,128)(2,1)S(1)}, u32[]{:S(2)}, u32[]{:S(2)}) collective-permute-start(bf16[256,256]{1,0:T(8,128)(2,1)S(1)} %get-tuple-element.56), channel_id=1, source_target_pairs={{0,2},{1,3},{2,0},{3,1},{4,6},{5,7},{6,4},{7,5},{8,10},{9,11},{10,... | collective-permute-start | bytes 393224 | tf_op jit(solution)/shard_map/ppermute | solution.py:505
  7.3 1.6 %collective-permute-start.1 = (bf16[2,128,256]{2,1,0:T(8,128)(2,1)S(1)}, bf16[2,128,256]{2,1,0:T(8,128)(2,1)S(1)}, u32[]{:S(2)}, u32[]{:S(2)}) collective-permute-start(bf16[2,128,256]{2,1,0:T(8,128)(2,1)S(1)} %get-tuple-element.48.refs_0_), channel_id=1, source_target_pairs={{0,8},{1,0},{2,10},{3,2},{4,12},{5,4},{6,14},{7,6},{8,16},{9,1},{1... | collective-permute-start | bytes 393224 | tf_op jit(solution)/shard_map/ppermute | solution.py:538
  8.8 0.5 %collective-permute-start.8 = (bf16[2,1,256,256]{3,2,1,0:T(8,128)(2,1)S(1)}, bf16[2,1,256,256]{3,2,1,0:T(8,128)(2,1)S(1)}, u32[]{:S(2)}, u32[]{:S(2)}) collective-permute-start(bf16[2,1,256,256]{3,2,1,0:T(8,128)(2,1)S(1)} %get-tuple-element.57), channel_id=1, source_target_pairs={{0,2},{1,3},{2,0},{3,1},{4,6},{5,7},{6,4},{7,5},{8,10},{9,11},{10,... | collective-permute-start | bytes 786440 | tf_op jit(solution)/shard_map/ppermute | solution.py:505
  9.3 0.5 %collective-permute-start.3 = (bf16[2,128,128]{2,1,0:T(8,128)(2,1)S(1)}, bf16[2,128,128]{2,1,0:T(8,128)(2,1)S(1)}, u32[]{:S(2)}, u32[]{:S(2)}) collective-permute-start(bf16[2,128,128]{2,1,0:T(8,128)(2,1)S(1)} %get-tuple-element.42), channel_id=1, source_target_pairs={{0,4},{4,0},{1,5},{5,1},{2,6},{6,2},{3,7},{7,3},{8,12},{12,8},{9,1... | collective-permute-start | bytes 196616 | tf_op jit(solution)/shard_map/ppermute | solution.py:540
  10.6 0.1 collective-permute-start.4
  10.6 0.5 %collective-permute-done.6.over_y.refs_4_ = bf16[256,256]{1,0:T(8,128)(2,1)S(1)} collective-permute-done((bf16[256,256]{1,0:T(8,128)(2,1)S(1)}, bf16[256,256]{1,0:T(8,128)(2,1)S(1)}, u32[]{:S(2)}, u32[]{:S(2)}) %collective-permute-start.6) | collective-permute-done | bytes 131104 | tf_op jit(solution)/shard_map/ppermute | solution.py:505
  11.1 2.5 %collective-permute-start.7 = (bf16[256,256]{1,0:T(8,128)(2,1)S(1)}, bf16[256,256]{1,0:T(8,128)(2,1)S(1)}, u32[]{:S(2)}, u32[]{:S(2)}) collective-permute-start(bf16[256,256]{1,0:T(8,128)(2,1)S(1)} %collective-permute-done.6.over_y.refs_4_), channel_id=1, source_target_pairs={{0,8},{8,0},{16,24},{24,16},{1,9},{9,1},{17,25},{25,17},{2,10},{10... | collective-permute-start | bytes 393224 | tf_op jit(solution)/shard_map/ppermute | solution.py:536
  13.6 0.1 edge.1.refs_3_
  13.7 1.2 %collective-permute-done.2.refs_2_ = bf16[2,128,256]{2,1,0:T(8,128)(2,1)S(1)} collective-permute-done((bf16[2,128,256]{2,1,0:T(8,128)(2,1)S(1)}, bf16[2,128,256]{2,1,0:T(8,128)(2,1)S(1)}, u32[]{:S(2)}, u32[]{:S(2)}) %collective-permute-start.2) | collective-permute-done | bytes 131104 | tf_op jit(solution)/shard_map/ppermute | solution.py:505
  15.0 1.4 %near.1 = (f32[2,256,256]{2,1,0:T(8,128)S(1)}, f32[2,256,512]{2,1,0:T(8,128)S(1)}, bf16[2,512,256]{2,1,0:T(8,128)(2,1)S(1)}, f32[2,256,256]{2,1,0:T(8,128)S(1)}) custom-call(s32[8,128]{1,0:T(8,128)S(1)} %get-tuple-element.47.spot_ref, bf16[2,128,256]{2,1,0:T(8,128)(2,1)S(1)} %get-tuple-element.48.refs_0_, ...), custom_call_target="tpu_custom_call" | custom-call | flops 33554432 | tf_op jit(solution)/shard_map/near/pallas_call | solution.py:571
  16.4 0.9 %core.1 = (f32[2,256,512]{2,1,0:T(8,128)S(1)}, bf16[2,512,256]{2,1,0:T(8,128)(2,1)S(1)}, f32[2,256,256]{2,1,0:T(8,128)S(1)}) custom-call(f32[2,256,256]{2,1,0:T(8,128)S(1)} %get-tuple-element.53.patch_ref.refs_1_, bf16[2,2,256,256]{3,2,1,0:T(8,128)(2,1)S(1)} %collective-permute-done.5.core.refs_3_, ...), custom_call_target="tpu_custom_call" | custom-call | flops 33554432 | tf_op jit(solution)/shard_map/core/pallas_call | solution.py:580
  17.3 0.2 collective-permute-start.11
  17.5 0.4 %collective-permute-start.9 = (bf16[256,256]{1,0:T(8,128)(2,1)S(1)}, bf16[256,256]{1,0:T(8,128)(2,1)S(1)}, u32[]{:S(2)}, u32[]{:S(2)}) collective-permute-start(bf16[256,256]{1,0:T(8,128)(2,1)S(1)} %collective-permute-done.6.over_y.refs_4_), channel_id=1, source_target_pairs={{0,1},{1,0},{2,3},{3,2},{4,5},{5,4},{6,7},{7,6},{8,9},{9,8},{10,11... | collective-permute-start | bytes 393224 | tf_op jit(solution)/shard_map/ppermute | solution.py:505
  17.9 0.1 collective-permute-start.10
  18.0 0.9 %over.1 = (f32[2,256,512]{2,1,0:T(8,128)S(1)}, bf16[2,512,256]{2,1,0:T(8,128)(2,1)S(1)}, f32[2,256,256]{2,1,0:T(8,128)S(1)}) custom-call(f32[2,256,256]{2,1,0:T(8,128)S(1)} %get-tuple-element.53.patch_ref.refs_1_, bf16[256,256]{1,0:T(8,128)(2,1)S(1)} %collective-permute-done.6.over_y.refs_4_, bf16[256,256]{1,0:T(8,128)(2,1)S(1)} %collective-permute-done.7.over_z.refs_5_, ...), custom_call_target="tpu_custom_call" | custom-call | flops 2013265920 | tf_op jit(solution)/shard_map/over/pallas_call | solution.py:593
  18.9 0.2 collective-permute-done.9.refs_7_
  19.1 0.2 collective-permute-done.10.refs_8_
  19.3 4.4 %back.1 = (bf16[256,256]{1,0:T(8,128)(2,1)S(1)}, bf16[256,256]{1,0:T(8,128)(2,1)S(1)}, bf16[256,384]{1,0:T(8,128)(2,1)S(1)}, bf16[256,384]{1,0:T(8,128)(2,1)S(1)}, bf16[272,128]{1,0:T(8,128)(2,1)S(1)}) custom-call(bf16[16,256]{1,0:T(8,128)(2,1)S(1)} %live.1.record_ref, s32[8,128]{1,0:T(8,128)S(1)} %get-tuple-element.47.spot_ref, ...), custom_call_target="tpu_custom_call" | custom-call | flops 2684354560 | tf_op jit(solution)/shard_map/back/pallas_call | solution.py:605
  23.6 0.2 collective-permute-start.13
  23.8 0.7 %collective-permute-start.12 = (bf16[272,128]{1,0:T(8,128)(2,1)S(1)}, bf16[272,128]{1,0:T(8,128)(2,1)S(1)}, u32[]{:S(2)}, u32[]{:S(2)}) collective-permute-start(bf16[272,128]{1,0:T(8,128)(2,1)S(1)} %get-tuple-element.74), channel_id=1, source_target_pairs={{0,4},{4,0},{1,5},{5,1},{2,6},{6,2},{3,7},{7,3},{8,12},{12,8},{9,1... | collective-permute-start | bytes 208904 | tf_op jit(solution)/shard_map/ppermute | solution.py:632
  24.5 0.6 %collective-permute-done.13.swap_ref = bf16[256,384]{1,0:T(8,128)(2,1)S(1)} collective-permute-done((bf16[256,384]{1,0:T(8,128)(2,1)S(1)}, bf16[256,384]{1,0:T(8,128)(2,1)S(1)}, u32[]{:S(2)}, u32[]{:S(2)}) %collective-permute-start.13) | collective-permute-done | bytes 196640 | tf_op jit(solution)/shard_map/ppermute | solution.py:505
  25.2 1.2 %collective-permute-start.14 = (bf16[272,256]{1,0:T(8,128)(2,1)S(1)}, bf16[272,256]{1,0:T(8,128)(2,1)S(1)}, u32[]{:S(2)}, u32[]{:S(2)}) collective-permute-start(bf16[272,256]{1,0:T(8,128)(2,1)S(1)} %get-tuple-element.77), channel_id=1, source_target_pairs={{0,8},{1,0},{2,10},{3,2},{4,12},{5,4},{6,14},{7,6},{8,16},{9,1},{1... | collective-permute-start | bytes 417800 | tf_op jit(solution)/shard_map/ppermute | solution.py:644
  26.4 1.8 %collective-permute-start.15 = (bf16[272,128]{1,0:T(8,128)(2,1)S(1)}, bf16[272,128]{1,0:T(8,128)(2,1)S(1)}, u32[]{:S(2)}, u32[]{:S(2)}) collective-permute-start(bf16[272,128]{1,0:T(8,128)(2,1)S(1)} %get-tuple-element.78), channel_id=1, source_target_pairs={{0,12},{1,4},{2,14},{3,6},{4,8},{5,0},{6,10},{7,2},{8,20},{9,5},{1... | collective-permute-start | bytes 208904 | tf_op jit(solution)/shard_map/ppermute | solution.py:646
  28.2 0.1 collective-permute-done.12.refs_0_
  28.3 0.4 %levels.1.level_ref = f32[3,128,256]{2,1,0:T(8,128)S(1)} custom-call(bf16[256,256]{1,0:T(8,128)(2,1)S(1)} %get-tuple-element.72.weight_ref, bf16[16,256]{1,0:T(8,128)(2,1)S(1)} %live.1.record_ref, bf16[256,256]{1,0:T(8,128)(2,1)S(1)} %get-tuple-element.73.own_ref, bf16[272,128]{1,0:T(8,128)(2,1)S(1)} %collective-permute-done.12.refs_0_), custom_call_target="tpu_custom_call" | custom-call | flops 1342177280 | tf_op jit(solution)/shard_map/levels/pallas_call | solution.py:648
  28.7 2.2 %collective-permute-done.15.refs_0_ = bf16[272,128]{1,0:T(8,128)(2,1)S(1)} collective-permute-done((bf16[272,128]{1,0:T(8,128)(2,1)S(1)}, bf16[272,128]{1,0:T(8,128)(2,1)S(1)}, u32[]{:S(2)}, u32[]{:S(2)}) %collective-permute-start.15) | collective-permute-done | bytes 69664 | tf_op jit(solution)/shard_map/ppermute | solution.py:646
  30.9 0.5 %sums.1.own_ref = bf16[3,128,256]{2,1,0:T(8,128)(2,1)S(1)} custom-call(bf16[256,256]{1,0:T(8,128)(2,1)S(1)} %get-tuple-element.72.weight_ref, f32[3,128,256]{2,1,0:T(8,128)S(1)} %levels.1.level_ref, bf16[272,256]{1,0:T(8,128)(2,1)S(1)} %collective-permute-done.14.rows_ref, bf16[272,128]{1,0:T(8,128)(2,1)S(1)} %collective-permute-done.15.refs_0_), custom_call_target="tpu_custom_call" | custom-call | tf_op jit(solution)/shard_map/sums/pallas_call | solution.py:657
  31.5 1.4 %collective-permute-done.16.other_ref = bf16[3,128,256]{2,1,0:T(8,128)(2,1)S(1)} collective-permute-done((bf16[3,128,256]{2,1,0:T(8,128)(2,1)S(1)}, bf16[3,128,256]{2,1,0:T(8,128)(2,1)S(1)}, u32[]{:S(2)}, u32[]{:S(2)}) %collective-permute-start.16) | collective-permute-done | bytes 196640 | tf_op jit(solution)/shard_map/ppermute | solution.py:505
  32.9 0.8 %update.1 = f32[2,128,256]{2,1,0:T(8,128)} custom-call(f32[2,128,256]{2,1,0:T(8,128)S(1)} %copy-done, bf16[3,128,256]{2,1,0:T(8,128)(2,1)S(1)} %sums.1.own_ref, bf16[3,128,256]{2,1,0:T(8,128)(2,1)S(1)} %collective-permute-done.16.other_ref), custom_call_target="tpu_custom_call" | custom-call | tf_op jit(solution)/shard_map/update/pallas_call | solution.py:665
  (17 shorter events, 0.2 us)
Async XLA Ops:
  1.6 7.2 %collective-permute-start.5 = (bf16[2,2,256,256]{3,2,1,0:T(8,128)(2,1)S(1)}, bf16[2,2,256,256]{3,2,1,0:T(8,128)(2,1)S(1)}, u32[]{:S(2)}, u32[]{:S(2)}) collective-permute-start(bf16[2,2,256,256]{3,2,1,0:T(8,128)(2,1)S(1)} %get-tuple-element.50.refs_4_.refs_2_), channel_id=1, source_target_pairs={{0,1},{1,0},{2,3},{3,2},{4,5},{5,4},{6,7},{7,6},{8,9},{9,8},{10,11... | collective-permute-start | bytes 1572872 | tf_op jit(solution)/shard_map/ppermute | solution.py:505
  2.2 8.4 %collective-permute-start = (bf16[2,128,128]{2,1,0:T(8,128)(2,1)S(1)}, bf16[2,128,128]{2,1,0:T(8,128)(2,1)S(1)}, u32[]{:S(2)}, u32[]{:S(2)}) collective-permute-start(bf16[2,128,128]{2,1,0:T(8,128)(2,1)S(1)} %get-tuple-element.42), channel_id=1, source_target_pairs={{0,12},{1,4},{2,14},{3,6},{4,8},{5,0},{6,10},{7,2},{8,20},{9,5},{1... | collective-permute-start | bytes 196616 | tf_op jit(solution)/shard_map/ppermute | solution.py:539
  5.7 5.4 %collective-permute-start.6 = (bf16[256,256]{1,0:T(8,128)(2,1)S(1)}, bf16[256,256]{1,0:T(8,128)(2,1)S(1)}, u32[]{:S(2)}, u32[]{:S(2)}) collective-permute-start(bf16[256,256]{1,0:T(8,128)(2,1)S(1)} %get-tuple-element.56), channel_id=1, source_target_pairs={{0,2},{1,3},{2,0},{3,1},{4,6},{5,7},{6,4},{7,5},{8,10},{9,11},{10,... | collective-permute-start | bytes 393224 | tf_op jit(solution)/shard_map/ppermute | solution.py:505
  7.3 6.4 %collective-permute-start.1 = (bf16[2,128,256]{2,1,0:T(8,128)(2,1)S(1)}, bf16[2,128,256]{2,1,0:T(8,128)(2,1)S(1)}, u32[]{:S(2)}, u32[]{:S(2)}) collective-permute-start(bf16[2,128,256]{2,1,0:T(8,128)(2,1)S(1)} %get-tuple-element.48.refs_0_), channel_id=1, source_target_pairs={{0,8},{1,0},{2,10},{3,2},{4,12},{5,4},{6,14},{7,6},{8,16},{9,1},{1... | collective-permute-start | bytes 393224 | tf_op jit(solution)/shard_map/ppermute | solution.py:538
  8.8 8.4 %collective-permute-start.8 = (bf16[2,1,256,256]{3,2,1,0:T(8,128)(2,1)S(1)}, bf16[2,1,256,256]{3,2,1,0:T(8,128)(2,1)S(1)}, u32[]{:S(2)}, u32[]{:S(2)}) collective-permute-start(bf16[2,1,256,256]{3,2,1,0:T(8,128)(2,1)S(1)} %get-tuple-element.57), channel_id=1, source_target_pairs={{0,2},{1,3},{2,0},{3,1},{4,6},{5,7},{6,4},{7,5},{8,10},{9,11},{10,... | collective-permute-start | bytes 786440 | tf_op jit(solution)/shard_map/ppermute | solution.py:505
  9.3 4.3 %collective-permute-start.3 = (bf16[2,128,128]{2,1,0:T(8,128)(2,1)S(1)}, bf16[2,128,128]{2,1,0:T(8,128)(2,1)S(1)}, u32[]{:S(2)}, u32[]{:S(2)}) collective-permute-start(bf16[2,128,128]{2,1,0:T(8,128)(2,1)S(1)} %get-tuple-element.42), channel_id=1, source_target_pairs={{0,4},{4,0},{1,5},{5,1},{2,6},{6,2},{3,7},{7,3},{8,12},{12,8},{9,1... | collective-permute-start | bytes 196616 | tf_op jit(solution)/shard_map/ppermute | solution.py:540
  10.6 3.1 %collective-permute-start.4 = (bf16[2,128,128]{2,1,0:T(8,128)(2,1)S(1)}, bf16[2,128,128]{2,1,0:T(8,128)(2,1)S(1)}, u32[]{:S(2)}, u32[]{:S(2)}) collective-permute-start(bf16[2,128,128]{2,1,0:T(8,128)(2,1)S(1)} %collective-permute-done.turn_a), channel_id=1, source_target_pairs={{0,1},{1,0},{2,3},{3,2},{4,5},{5,4},{6,7},{7,6},{8,9},{9,8},{10,11... | collective-permute-start | bytes 196616 | tf_op jit(solution)/shard_map/ppermute | solution.py:505
  11.1 6.2 %collective-permute-start.7 = (bf16[256,256]{1,0:T(8,128)(2,1)S(1)}, bf16[256,256]{1,0:T(8,128)(2,1)S(1)}, u32[]{:S(2)}, u32[]{:S(2)}) collective-permute-start(bf16[256,256]{1,0:T(8,128)(2,1)S(1)} %collective-permute-done.6.over_y.refs_4_), channel_id=1, source_target_pairs={{0,8},{8,0},{16,24},{24,16},{1,9},{9,1},{17,25},{25,17},{2,10},{10... | collective-permute-start | bytes 393224 | tf_op jit(solution)/shard_map/ppermute | solution.py:536
  13.6 1.3 %collective-permute-start.2 = (bf16[2,128,256]{2,1,0:T(8,128)(2,1)S(1)}, bf16[2,128,256]{2,1,0:T(8,128)(2,1)S(1)}, u32[]{:S(2)}, u32[]{:S(2)}) collective-permute-start(bf16[2,128,256]{2,1,0:T(8,128)(2,1)S(1)} %collective-permute-done.1.refs_1_), channel_id=1, source_target_pairs={{0,1},{1,0},{2,3},{3,2},{4,5},{5,4},{6,7},{7,6},{8,9},{9,8},{10,11... | collective-permute-start | bytes 393224 | tf_op jit(solution)/shard_map/ppermute | solution.py:505
  17.3 2.0 %copy-start.1 = (bf16[1,1,2,256,256]{4,3,2,1,0:T(8,128)(2,1)S(1)}, bf16[1,1,2,256,256]{4,3,2,1,0:T(8,128)(2,1)}, u32[]{:S(2)}) copy-start(bf16[1,1,2,256,256]{4,3,2,1,0:T(8,128)(2,1)} %refs_0_.1) | copy-start | bytes 786436
  17.3 2.0 %collective-permute-start.11 = (bf16[2,1,256,256]{3,2,1,0:T(8,128)(2,1)S(1)}, bf16[2,1,256,256]{3,2,1,0:T(8,128)(2,1)S(1)}, u32[]{:S(2)}, u32[]{:S(2)}) collective-permute-start(bf16[2,1,256,256]{3,2,1,0:T(8,128)(2,1)S(1)} %collective-permute-done.8.rest.refs_6_), channel_id=1, source_target_pairs={{0,1},{1,0},{2,3},{3,2},{4,5},{5,4},{6,7},{7,6},{8,9},{9,8},{10,11... | collective-permute-start | bytes 786440 | tf_op jit(solution)/shard_map/ppermute | solution.py:505
  17.5 1.6 %collective-permute-start.9 = (bf16[256,256]{1,0:T(8,128)(2,1)S(1)}, bf16[256,256]{1,0:T(8,128)(2,1)S(1)}, u32[]{:S(2)}, u32[]{:S(2)}) collective-permute-start(bf16[256,256]{1,0:T(8,128)(2,1)S(1)} %collective-permute-done.6.over_y.refs_4_), channel_id=1, source_target_pairs={{0,1},{1,0},{2,3},{3,2},{4,5},{5,4},{6,7},{7,6},{8,9},{9,8},{10,11... | collective-permute-start | bytes 393224 | tf_op jit(solution)/shard_map/ppermute | solution.py:505
  17.9 1.4 %collective-permute-start.10 = (bf16[256,256]{1,0:T(8,128)(2,1)S(1)}, bf16[256,256]{1,0:T(8,128)(2,1)S(1)}, u32[]{:S(2)}, u32[]{:S(2)}) collective-permute-start(bf16[256,256]{1,0:T(8,128)(2,1)S(1)} %collective-permute-done.7.over_z.refs_5_), channel_id=1, source_target_pairs={{0,1},{1,0},{2,3},{3,2},{4,5},{5,4},{6,7},{7,6},{8,9},{9,8},{10,11... | collective-permute-start | bytes 393224 | tf_op jit(solution)/shard_map/ppermute | solution.py:505
  23.6 1.5 %collective-permute-start.13 = (bf16[256,384]{1,0:T(8,128)(2,1)S(1)}, bf16[256,384]{1,0:T(8,128)(2,1)S(1)}, u32[]{:S(2)}, u32[]{:S(2)}) collective-permute-start(bf16[256,384]{1,0:T(8,128)(2,1)S(1)} %get-tuple-element.76), channel_id=1, source_target_pairs={{0,1},{1,0},{2,3},{3,2},{4,5},{5,4},{6,7},{7,6},{8,9},{9,8},{10,11... | collective-permute-start | bytes 589832 | tf_op jit(solution)/shard_map/ppermute | solution.py:505
  23.8 4.4 %collective-permute-start.12 = (bf16[272,128]{1,0:T(8,128)(2,1)S(1)}, bf16[272,128]{1,0:T(8,128)(2,1)S(1)}, u32[]{:S(2)}, u32[]{:S(2)}) collective-permute-start(bf16[272,128]{1,0:T(8,128)(2,1)S(1)} %get-tuple-element.74), channel_id=1, source_target_pairs={{0,4},{4,0},{1,5},{5,1},{2,6},{6,2},{3,7},{7,3},{8,12},{12,8},{9,1... | collective-permute-start | bytes 208904 | tf_op jit(solution)/shard_map/ppermute | solution.py:632
  25.2 5.7 %collective-permute-start.14 = (bf16[272,256]{1,0:T(8,128)(2,1)S(1)}, bf16[272,256]{1,0:T(8,128)(2,1)S(1)}, u32[]{:S(2)}, u32[]{:S(2)}) collective-permute-start(bf16[272,256]{1,0:T(8,128)(2,1)S(1)} %get-tuple-element.77), channel_id=1, source_target_pairs={{0,8},{1,0},{2,10},{3,2},{4,12},{5,4},{6,14},{7,6},{8,16},{9,1},{1... | collective-permute-start | bytes 417800 | tf_op jit(solution)/shard_map/ppermute | solution.py:644
  26.4 4.5 %collective-permute-start.15 = (bf16[272,128]{1,0:T(8,128)(2,1)S(1)}, bf16[272,128]{1,0:T(8,128)(2,1)S(1)}, u32[]{:S(2)}, u32[]{:S(2)}) collective-permute-start(bf16[272,128]{1,0:T(8,128)(2,1)S(1)} %get-tuple-element.78), channel_id=1, source_target_pairs={{0,12},{1,4},{2,14},{3,6},{4,8},{5,0},{6,10},{7,2},{8,20},{9,5},{1... | collective-permute-start | bytes 208904 | tf_op jit(solution)/shard_map/ppermute | solution.py:646
  28.7 4.2 %copy-start = (f32[2,128,256]{2,1,0:T(8,128)S(1)}, f32[2,128,256]{2,1,0:T(8,128)}, u32[]{:S(2)}) copy-start(f32[2,128,256]{2,1,0:T(8,128)} %object_ref.1) | copy-start | bytes 786436
  31.4 1.5 %collective-permute-start.16 = (bf16[3,128,256]{2,1,0:T(8,128)(2,1)S(1)}, bf16[3,128,256]{2,1,0:T(8,128)(2,1)S(1)}, u32[]{:S(2)}, u32[]{:S(2)}) collective-permute-start(bf16[3,128,256]{2,1,0:T(8,128)(2,1)S(1)} %sums.1.own_ref), channel_id=1, source_target_pairs={{0,1},{1,0},{2,3},{3,2},{4,5},{5,4},{6,7},{7,6},{8,9},{9,8},{10,11... | collective-permute-start | bytes 589832 | tf_op jit(solution)/shard_map/ppermute | solution.py:505

commit v15 on v13

--- a/solution.py
+++ b/solution.py
@@ -559,7 +559,7 @@
         in_specs=[vmem(), smem()],
         out_specs=vmem(),
         compiler_params=pltpu.CompilerParams(vmem_limit_bytes=small_bytes),
-        cost_estimate=cost(40),
+        cost_estimate=cost(50),
         name="live",
     )(record, live)
     corners, record = lax.optimization_barrier((corners, record))
@@ -583,6 +583,7 @@
         cost_estimate=cost(1),
         name="near",
     )(spot, *in_sent_order(pieces), probe_low, direct, swapped)
+    rest, patch = lax.optimization_barrier((rest, patch))
     other = pl.pallas_call(
         core_kernel,
         out_shape=waves,
@@ -593,7 +594,7 @@
         name="core",
     )(patch, probe_core, direct, swapped)
     last_y = exchange(over_y, 1)
-    over_z, rest, other = lax.optimization_barrier((over_z, rest, other))
+    over_z, other = lax.optimization_barrier((over_z, other))
     over_group = (over_y, over_z, rest)
     last_group = [last_y, exchange(over_z, 1), exchange(rest, 1)]
     over = pl.pallas_call(

time: 33.3 us -> 33.2 us (level)
    ppermute x1, starting transfers between devices: 1.09 us -> 0.68 us  [on_device(): rows = lax.ppermute(rows, axes, zigzag(0))]
  transfers between devices with their start and end apart: 17 -> 17, of which waited for: 5 -> 6; matrix products, arithmetic and copies ran while one was open for 0% -> 0% of each run, Pallas kernels for 11% -> 11%
where the time goes in v15:
time: 33.2 us; the launch traced here: 32.8 us
  starting transfers between devices  17.1 us (52%)
  Pallas kernels  10.9 us (33%)
  waiting for transfers between devices  4.02 us (12%)
  between operations  0.75 us (2%)
    ppermute x10, starting transfers between devices, exchange(): return lax.ppermute(array, 'mode', [(m, m ^ flip) for m in range(m_count)])  5.62 us
    pallas_call x1, Pallas kernels, on_device(): pl.pallas_call(functools.partial(back_kernel, sides, slots, tile_cols), o...  4.36 us
    ppermute x1, starting transfers between devices, on_device(): lax.ppermute(edge, axes, zigzag(step))  2.5 us
    ppermute x1, starting transfers between devices, on_device(): lax.ppermute(piece, axes, zigzag(-step))  2.43 us
    ppermute x1, starting transfers between devices, on_device(): over_z = lax.ppermute(over_y, 'tx', [(z, z ^ 1) for z in range(z_count)])  2.33 us
    ppermute x10, waiting for transfers between devices, exchange(): return lax.ppermute(array, 'mode', [(m, m ^ flip) for m in range(m_count)])  2.27 us
    pallas_call x1, Pallas kernels, on_device(): pl.pallas_call(functools.partial(start_kernel, sides, slots), out_shape=[...  1.64 us
    ppermute x1, starting transfers between devices, on_device(): rows = lax.ppermute(packed[0], axes, zigzag(0))  1.58 us
  transfers between devices with their start and end apart: 17, of which 6 were waited for; matrix products, arithmetic and copies ran while one was open for 0% of the time, Pallas kernels for 11%

profile of v15, /device:TPU:0, one launch (start us, length us, event | category | flops | bytes accessed | tf_op | source)
XLA Modules:
  0.0 32.8 jit_solution(5726652114994187495)
XLA Ops:
  0.0 1.6 %start.1 = (bf16[2,2,256,256]{3,2,1,0:T(8,128)(2,1)S(1)}, bf16[256,256]{1,0:T(8,128)(2,1)S(1)}, bf16[2,1,256,256]{3,2,1,0:T(8,128)(2,1)S(1)}, bf16[16,256]{1,0:T...) custom-call(f32[2,128,256]{2,1,0:T(8,128)} %object_ref.1, ...), custom_call_target="tpu_custom_call" | custom-call | tf_op jit(solution)/shard_map/start/pallas_call | solution.py:522
  1.6 0.5 %collective-permute-start.1 = (bf16[2,2,256,256]{3,2,1,0:T(8,128)(2,1)S(1)}, bf16[2,2,256,256]{3,2,1,0:T(8,128)(2,1)S(1)}, u32[]{:S(2)}, u32[]{:S(2)}) collective-permute-start(bf16[2,2,256,256]{3,2,1,0:T(8,128)(2,1)S(1)} %get-tuple-element.49.refs_6_.refs_2_), channel_id=1, source_target_pairs={{0,1},{1,0},{2,3},{3,2},{4,5},{5,4},{6,7},{7,6},{8,9},{9,8},{10,11... | collective-permute-start | bytes 1572872 | tf_op jit(solution)/shard_map/ppermute | solution.py:519
  2.2 2.6 %collective-permute-start.7 = (bf16[256,256]{1,0:T(8,128)(2,1)S(1)}, bf16[256,256]{1,0:T(8,128)(2,1)S(1)}, u32[]{:S(2)}, u32[]{:S(2)}) collective-permute-start(bf16[256,256]{1,0:T(8,128)(2,1)S(1)} %get-tuple-element.59), channel_id=1, source_target_pairs={{0,2},{1,3},{2,0},{3,1},{4,6},{5,7},{6,4},{7,5},{8,10},{9,11},{10,... | collective-permute-start | bytes 393224 | tf_op jit(solution)/shard_map/ppermute | solution.py:519
  4.8 1.6 %collective-permute-start.4 = (bf16[2,128,256]{2,1,0:T(8,128)(2,1)S(1)}, bf16[2,128,256]{2,1,0:T(8,128)(2,1)S(1)}, u32[]{:S(2)}, u32[]{:S(2)}) collective-permute-start(bf16[2,128,256]{2,1,0:T(8,128)(2,1)S(1)} %get-tuple-element.52.refs_0_), channel_id=1, source_target_pairs={{0,8},{1,0},{2,10},{3,2},{4,12},{5,4},{6,14},{7,6},{8,16},{9,1},{1... | collective-permute-start | bytes 393224 | tf_op jit(solution)/shard_map/ppermute | solution.py:552
  6.3 2.5 %collective-permute-start = (bf16[2,128,128]{2,1,0:T(8,128)(2,1)S(1)}, bf16[2,128,128]{2,1,0:T(8,128)(2,1)S(1)}, u32[]{:S(2)}, u32[]{:S(2)}) collective-permute-start(bf16[2,128,128]{2,1,0:T(8,128)(2,1)S(1)} %get-tuple-element.43), channel_id=1, source_target_pairs={{0,12},{1,4},{2,14},{3,6},{4,8},{5,0},{6,10},{7,2},{8,20},{9,5},{1... | collective-permute-start | bytes 196616 | tf_op jit(solution)/shard_map/ppermute | solution.py:553
  8.8 0.5 %collective-permute-start.2 = (bf16[2,1,256,256]{3,2,1,0:T(8,128)(2,1)S(1)}, bf16[2,1,256,256]{3,2,1,0:T(8,128)(2,1)S(1)}, u32[]{:S(2)}, u32[]{:S(2)}) collective-permute-start(bf16[2,1,256,256]{3,2,1,0:T(8,128)(2,1)S(1)} %get-tuple-element.51), channel_id=1, source_target_pairs={{0,2},{1,3},{2,0},{3,1},{4,6},{5,7},{6,4},{7,5},{8,10},{9,11},{10,... | collective-permute-start | bytes 786440 | tf_op jit(solution)/shard_map/ppermute | solution.py:519
  9.3 0.5 %collective-permute-start.6 = (bf16[2,128,128]{2,1,0:T(8,128)(2,1)S(1)}, bf16[2,128,128]{2,1,0:T(8,128)(2,1)S(1)}, u32[]{:S(2)}, u32[]{:S(2)}) collective-permute-start(bf16[2,128,128]{2,1,0:T(8,128)(2,1)S(1)} %get-tuple-element.43), channel_id=1, source_target_pairs={{0,4},{4,0},{1,5},{5,1},{2,6},{6,2},{3,7},{7,3},{8,12},{12,8},{9,1... | collective-permute-start | bytes 196616 | tf_op jit(solution)/shard_map/ppermute | solution.py:554
  10.5 0.2 collective-permute-done.refs_1_
  10.7 2.3 %collective-permute-start.8 = (bf16[256,256]{1,0:T(8,128)(2,1)S(1)}, bf16[256,256]{1,0:T(8,128)(2,1)S(1)}, u32[]{:S(2)}, u32[]{:S(2)}) collective-permute-start(bf16[256,256]{1,0:T(8,128)(2,1)S(1)} %collective-permute-done.7.over_y.refs_4_), channel_id=1, source_target_pairs={{0,8},{8,0},{16,24},{24,16},{1,9},{9,1},{17,25},{25,17},{2,10},{10... | collective-permute-start | bytes 393224 | tf_op jit(solution)/shard_map/ppermute | solution.py:550
  13.1 0.5 %collective-permute-start.3 = (bf16[2,128,128]{2,1,0:T(8,128)(2,1)S(1)}, bf16[2,128,128]{2,1,0:T(8,128)(2,1)S(1)}, u32[]{:S(2)}, u32[]{:S(2)}) collective-permute-start(bf16[2,128,128]{2,1,0:T(8,128)(2,1)S(1)} %collective-permute-done.refs_1_), channel_id=1, source_target_pairs={{0,1},{1,0},{2,3},{3,2},{4,5},{5,4},{6,7},{7,6},{8,9},{9,8},{10,11... | collective-permute-start | bytes 196616 | tf_op jit(solution)/shard_map/ppermute | solution.py:519
  13.6 0.0 collective-permute-done.6.refs_5_
  13.6 0.1 collective-permute-start.9
  13.7 0.8 %collective-permute-done.3.refs_2_ = bf16[2,128,128]{2,1,0:T(8,128)(2,1)S(1)} collective-permute-done((bf16[2,128,128]{2,1,0:T(8,128)(2,1)S(1)}, bf16[2,128,128]{2,1,0:T(8,128)(2,1)S(1)}, u32[]{:S(2)}, u32[]{:S(2)}) %collective-permute-start.3) | collective-permute-done | bytes 65568 | tf_op jit(solution)/shard_map/ppermute | solution.py:519
  14.5 1.5 %near.1 = (f32[2,256,256]{2,1,0:T(8,128)S(1)}, f32[2,256,512]{2,1,0:T(8,128)S(1)}, bf16[2,512,256]{2,1,0:T(8,128)(2,1)S(1)}, f32[2,256,256]{2,1,0:T(8,128)S(1)}) custom-call(s32[8,128]{1,0:T(8,128)S(1)} %get-tuple-element.48.spot_ref, bf16[2,128,256]{2,1,0:T(8,128)(2,1)S(1)} %get-tuple-element.52.refs_0_, ...), custom_call_target="tpu_custom_call" | custom-call | flops 33554432 | tf_op jit(solution)/shard_map/near/pallas_call | solution.py:577
  16.0 0.1 collective-permute-done.2.rest.refs_6_
  16.2 0.3 collective-permute-start.11
  16.4 0.9 %core.1 = (f32[2,256,512]{2,1,0:T(8,128)S(1)}, bf16[2,512,256]{2,1,0:T(8,128)(2,1)S(1)}, f32[2,256,256]{2,1,0:T(8,128)S(1)}) custom-call(f32[2,256,256]{2,1,0:T(8,128)S(1)} %get-tuple-element.57.patch_ref.refs_1_, bf16[2,2,256,256]{3,2,1,0:T(8,128)(2,1)S(1)} %collective-permute-done.1.core.refs_3_, ...), custom_call_target="tpu_custom_call" | custom-call | flops 33554432 | tf_op jit(solution)/shard_map/core/pallas_call | solution.py:587
  17.3 0.3 collective-permute-start.10
  17.6 0.9 %over.1 = (f32[2,256,512]{2,1,0:T(8,128)S(1)}, bf16[2,512,256]{2,1,0:T(8,128)(2,1)S(1)}, f32[2,256,256]{2,1,0:T(8,128)S(1)}) custom-call(f32[2,256,256]{2,1,0:T(8,128)S(1)} %get-tuple-element.57.patch_ref.refs_1_, bf16[256,256]{1,0:T(8,128)(2,1)S(1)} %collective-permute-done.7.over_y.refs_4_, bf16[256,256]{1,0:T(8,128)(2,1)S(1)} %collective-permute-done.8.over_z.refs_5_, ...), custom_call_target="tpu_custom_call" | custom-call | flops 3355443200 | tf_op jit(solution)/shard_map/over/pallas_call | solution.py:600
  18.5 0.2 collective-permute-done.10.refs_8_
  18.7 4.4 %back.1 = (bf16[256,256]{1,0:T(8,128)(2,1)S(1)}, bf16[256,256]{1,0:T(8,128)(2,1)S(1)}, bf16[256,384]{1,0:T(8,128)(2,1)S(1)}, bf16[256,384]{1,0:T(8,128)(2,1)S(1)}, bf16[272,128]{1,0:T(8,128)(2,1)S(1)}) custom-call(bf16[16,256]{1,0:T(8,128)(2,1)S(1)} %live.1.record_ref, s32[8,128]{1,0:T(8,128)S(1)} %get-tuple-element.48.spot_ref, ...), custom_call_target="tpu_custom_call" | custom-call | flops 2684354560 | tf_op jit(solution)/shard_map/back/pallas_call | solution.py:612
  23.1 0.3 collective-permute-start.13
  23.4 1.4 %collective-permute-start.12 = (bf16[272,128]{1,0:T(8,128)(2,1)S(1)}, bf16[272,128]{1,0:T(8,128)(2,1)S(1)}, u32[]{:S(2)}, u32[]{:S(2)}) collective-permute-start(bf16[272,128]{1,0:T(8,128)(2,1)S(1)} %get-tuple-element.76), channel_id=1, source_target_pairs={{0,4},{4,0},{1,5},{5,1},{2,6},{6,2},{3,7},{7,3},{8,12},{12,8},{9,1... | collective-permute-start | bytes 208904 | tf_op jit(solution)/shard_map/ppermute | solution.py:639
  24.8 0.1 meet.1
  24.9 0.7 %collective-permute-start.14 = (bf16[272,256]{1,0:T(8,128)(2,1)S(1)}, bf16[272,256]{1,0:T(8,128)(2,1)S(1)}, u32[]{:S(2)}, u32[]{:S(2)}) collective-permute-start(bf16[272,256]{1,0:T(8,128)(2,1)S(1)} %get-tuple-element.79), channel_id=1, source_target_pairs={{0,8},{1,0},{2,10},{3,2},{4,12},{5,4},{6,14},{7,6},{8,16},{9,1},{1... | collective-permute-start | bytes 417800 | tf_op jit(solution)/shard_map/ppermute | solution.py:651
  25.6 2.4 %collective-permute-start.15 = (bf16[272,128]{1,0:T(8,128)(2,1)S(1)}, bf16[272,128]{1,0:T(8,128)(2,1)S(1)}, u32[]{:S(2)}, u32[]{:S(2)}) collective-permute-start(bf16[272,128]{1,0:T(8,128)(2,1)S(1)} %get-tuple-element.80), channel_id=1, source_target_pairs={{0,12},{1,4},{2,14},{3,6},{4,8},{5,0},{6,10},{7,2},{8,20},{9,5},{1... | collective-permute-start | bytes 208904 | tf_op jit(solution)/shard_map/ppermute | solution.py:653
  28.0 0.4 %levels.1.level_ref = f32[3,128,256]{2,1,0:T(8,128)S(1)} custom-call(bf16[256,256]{1,0:T(8,128)(2,1)S(1)} %get-tuple-element.74.weight_ref, bf16[16,256]{1,0:T(8,128)(2,1)S(1)} %live.1.record_ref, bf16[256,256]{1,0:T(8,128)(2,1)S(1)} %get-tuple-element.75.own_ref, bf16[272,128]{1,0:T(8,128)(2,1)S(1)} %collective-permute-done.12.refs_0_), custom_call_target="tpu_custom_call" | custom-call | flops 1342177280 | tf_op jit(solution)/shard_map/levels/pallas_call | solution.py:655
  28.4 1.5 %collective-permute-done.15.refs_0_ = bf16[272,128]{1,0:T(8,128)(2,1)S(1)} collective-permute-done((bf16[272,128]{1,0:T(8,128)(2,1)S(1)}, bf16[272,128]{1,0:T(8,128)(2,1)S(1)}, u32[]{:S(2)}, u32[]{:S(2)}) %collective-permute-start.15) | collective-permute-done | bytes 69664 | tf_op jit(solution)/shard_map/ppermute | solution.py:653
  29.9 0.5 %sums.1.own_ref = bf16[3,128,256]{2,1,0:T(8,128)(2,1)S(1)} custom-call(bf16[256,256]{1,0:T(8,128)(2,1)S(1)} %get-tuple-element.74.weight_ref, f32[3,128,256]{2,1,0:T(8,128)S(1)} %levels.1.level_ref, bf16[272,256]{1,0:T(8,128)(2,1)S(1)} %collective-permute-done.14.rows_ref, bf16[272,128]{1,0:T(8,128)(2,1)S(1)} %collective-permute-done.15.refs_0_), custom_call_target="tpu_custom_call" | custom-call | tf_op jit(solution)/shard_map/sums/pallas_call | solution.py:664
  30.4 0.6 %collective-permute-start.16 = (bf16[3,128,256]{2,1,0:T(8,128)(2,1)S(1)}, bf16[3,128,256]{2,1,0:T(8,128)(2,1)S(1)}, u32[]{:S(2)}, u32[]{:S(2)}) collective-permute-start(bf16[3,128,256]{2,1,0:T(8,128)(2,1)S(1)} %sums.1.own_ref), channel_id=1, source_target_pairs={{0,1},{1,0},{2,3},{3,2},{4,5},{5,4},{6,7},{7,6},{8,9},{9,8},{10,11... | collective-permute-start | bytes 589832 | tf_op jit(solution)/shard_map/ppermute | solution.py:519
  31.0 1.1 %collective-permute-done.16.other_ref = bf16[3,128,256]{2,1,0:T(8,128)(2,1)S(1)} collective-permute-done((bf16[3,128,256]{2,1,0:T(8,128)(2,1)S(1)}, bf16[3,128,256]{2,1,0:T(8,128)(2,1)S(1)}, u32[]{:S(2)}, u32[]{:S(2)}) %collective-permute-start.16) | collective-permute-done | bytes 196640 | tf_op jit(solution)/shard_map/ppermute | solution.py:519
  32.0 0.8 %update.1 = f32[2,128,256]{2,1,0:T(8,128)} custom-call(f32[2,128,256]{2,1,0:T(8,128)S(1)} %copy-done, bf16[3,128,256]{2,1,0:T(8,128)(2,1)S(1)} %sums.1.own_ref, bf16[3,128,256]{2,1,0:T(8,128)(2,1)S(1)} %collective-permute-done.16.other_ref), custom_call_target="tpu_custom_call" | custom-call | tf_op jit(solution)/shard_map/update/pallas_call | solution.py:672
  (16 shorter events, 0.0 us)
Async XLA Ops:
  1.6 7.2 %collective-permute-start.1 = (bf16[2,2,256,256]{3,2,1,0:T(8,128)(2,1)S(1)}, bf16[2,2,256,256]{3,2,1,0:T(8,128)(2,1)S(1)}, u32[]{:S(2)}, u32[]{:S(2)}) collective-permute-start(bf16[2,2,256,256]{3,2,1,0:T(8,128)(2,1)S(1)} %get-tuple-element.49.refs_6_.refs_2_), channel_id=1, source_target_pairs={{0,1},{1,0},{2,3},{3,2},{4,5},{5,4},{6,7},{7,6},{8,9},{9,8},{10,11... | collective-permute-start | bytes 1572872 | tf_op jit(solution)/shard_map/ppermute | solution.py:519
  2.2 8.6 %collective-permute-start.7 = (bf16[256,256]{1,0:T(8,128)(2,1)S(1)}, bf16[256,256]{1,0:T(8,128)(2,1)S(1)}, u32[]{:S(2)}, u32[]{:S(2)}) collective-permute-start(bf16[256,256]{1,0:T(8,128)(2,1)S(1)} %get-tuple-element.59), channel_id=1, source_target_pairs={{0,2},{1,3},{2,0},{3,1},{4,6},{5,7},{6,4},{7,5},{8,10},{9,11},{10,... | collective-permute-start | bytes 393224 | tf_op jit(solution)/shard_map/ppermute | solution.py:519
  4.8 8.3 %collective-permute-start.4 = (bf16[2,128,256]{2,1,0:T(8,128)(2,1)S(1)}, bf16[2,128,256]{2,1,0:T(8,128)(2,1)S(1)}, u32[]{:S(2)}, u32[]{:S(2)}) collective-permute-start(bf16[2,128,256]{2,1,0:T(8,128)(2,1)S(1)} %get-tuple-element.52.refs_0_), channel_id=1, source_target_pairs={{0,8},{1,0},{2,10},{3,2},{4,12},{5,4},{6,14},{7,6},{8,16},{9,1},{1... | collective-permute-start | bytes 393224 | tf_op jit(solution)/shard_map/ppermute | solution.py:552
  6.3 4.4 %collective-permute-start = (bf16[2,128,128]{2,1,0:T(8,128)(2,1)S(1)}, bf16[2,128,128]{2,1,0:T(8,128)(2,1)S(1)}, u32[]{:S(2)}, u32[]{:S(2)}) collective-permute-start(bf16[2,128,128]{2,1,0:T(8,128)(2,1)S(1)} %get-tuple-element.43), channel_id=1, source_target_pairs={{0,12},{1,4},{2,14},{3,6},{4,8},{5,0},{6,10},{7,2},{8,20},{9,5},{1... | collective-permute-start | bytes 196616 | tf_op jit(solution)/shard_map/ppermute | solution.py:553
  8.8 7.3 %collective-permute-start.2 = (bf16[2,1,256,256]{3,2,1,0:T(8,128)(2,1)S(1)}, bf16[2,1,256,256]{3,2,1,0:T(8,128)(2,1)S(1)}, u32[]{:S(2)}, u32[]{:S(2)}) collective-permute-start(bf16[2,1,256,256]{3,2,1,0:T(8,128)(2,1)S(1)} %get-tuple-element.51), channel_id=1, source_target_pairs={{0,2},{1,3},{2,0},{3,1},{4,6},{5,7},{6,4},{7,5},{8,10},{9,11},{10,... | collective-permute-start | bytes 786440 | tf_op jit(solution)/shard_map/ppermute | solution.py:519
  9.3 4.3 %collective-permute-start.6 = (bf16[2,128,128]{2,1,0:T(8,128)(2,1)S(1)}, bf16[2,128,128]{2,1,0:T(8,128)(2,1)S(1)}, u32[]{:S(2)}, u32[]{:S(2)}) collective-permute-start(bf16[2,128,128]{2,1,0:T(8,128)(2,1)S(1)} %get-tuple-element.43), channel_id=1, source_target_pairs={{0,4},{4,0},{1,5},{5,1},{2,6},{6,2},{3,7},{7,3},{8,12},{12,8},{9,1... | collective-permute-start | bytes 196616 | tf_op jit(solution)/shard_map/ppermute | solution.py:554
  10.7 6.5 %collective-permute-start.8 = (bf16[256,256]{1,0:T(8,128)(2,1)S(1)}, bf16[256,256]{1,0:T(8,128)(2,1)S(1)}, u32[]{:S(2)}, u32[]{:S(2)}) collective-permute-start(bf16[256,256]{1,0:T(8,128)(2,1)S(1)} %collective-permute-done.7.over_y.refs_4_), channel_id=1, source_target_pairs={{0,8},{8,0},{16,24},{24,16},{1,9},{9,1},{17,25},{25,17},{2,10},{10... | collective-permute-start | bytes 393224 | tf_op jit(solution)/shard_map/ppermute | solution.py:550
  13.1 1.4 %collective-permute-start.5 = (bf16[2,128,256]{2,1,0:T(8,128)(2,1)S(1)}, bf16[2,128,256]{2,1,0:T(8,128)(2,1)S(1)}, u32[]{:S(2)}, u32[]{:S(2)}) collective-permute-start(bf16[2,128,256]{2,1,0:T(8,128)(2,1)S(1)} %collective-permute-done.4.refs_3_), channel_id=1, source_target_pairs={{0,1},{1,0},{2,3},{3,2},{4,5},{5,4},{6,7},{7,6},{8,9},{9,8},{10,11... | collective-permute-start | bytes 393224 | tf_op jit(solution)/shard_map/ppermute | solution.py:519
  13.1 1.4 %collective-permute-start.3 = (bf16[2,128,128]{2,1,0:T(8,128)(2,1)S(1)}, bf16[2,128,128]{2,1,0:T(8,128)(2,1)S(1)}, u32[]{:S(2)}, u32[]{:S(2)}) collective-permute-start(bf16[2,128,128]{2,1,0:T(8,128)(2,1)S(1)} %collective-permute-done.refs_1_), channel_id=1, source_target_pairs={{0,1},{1,0},{2,3},{3,2},{4,5},{5,4},{6,7},{7,6},{8,9},{9,8},{10,11... | collective-permute-start | bytes 196616 | tf_op jit(solution)/shard_map/ppermute | solution.py:519
  13.6 4.9 %collective-permute-start.9 = (bf16[256,256]{1,0:T(8,128)(2,1)S(1)}, bf16[256,256]{1,0:T(8,128)(2,1)S(1)}, u32[]{:S(2)}, u32[]{:S(2)}) collective-permute-start(bf16[256,256]{1,0:T(8,128)(2,1)S(1)} %collective-permute-done.7.over_y.refs_4_), channel_id=1, source_target_pairs={{0,1},{1,0},{2,3},{3,2},{4,5},{5,4},{6,7},{7,6},{8,9},{9,8},{10,11... | collective-permute-start | bytes 393224 | tf_op jit(solution)/shard_map/ppermute | solution.py:519
  16.2 2.6 %collective-permute-start.11 = (bf16[2,1,256,256]{3,2,1,0:T(8,128)(2,1)S(1)}, bf16[2,1,256,256]{3,2,1,0:T(8,128)(2,1)S(1)}, u32[]{:S(2)}, u32[]{:S(2)}) collective-permute-start(bf16[2,1,256,256]{3,2,1,0:T(8,128)(2,1)S(1)} %collective-permute-done.2.rest.refs_6_), channel_id=1, source_target_pairs={{0,1},{1,0},{2,3},{3,2},{4,5},{5,4},{6,7},{7,6},{8,9},{9,8},{10,11... | collective-permute-start | bytes 786440 | tf_op jit(solution)/shard_map/ppermute | solution.py:519
  17.3 1.4 %copy-start.1 = (bf16[1,1,2,256,256]{4,3,2,1,0:T(8,128)(2,1)S(1)}, bf16[1,1,2,256,256]{4,3,2,1,0:T(8,128)(2,1)}, u32[]{:S(2)}) copy-start(bf16[1,1,2,256,256]{4,3,2,1,0:T(8,128)(2,1)} %refs_0_.1) | copy-start | bytes 786436
  17.3 1.4 %collective-permute-start.10 = (bf16[256,256]{1,0:T(8,128)(2,1)S(1)}, bf16[256,256]{1,0:T(8,128)(2,1)S(1)}, u32[]{:S(2)}, u32[]{:S(2)}) collective-permute-start(bf16[256,256]{1,0:T(8,128)(2,1)S(1)} %collective-permute-done.8.over_z.refs_5_), channel_id=1, source_target_pairs={{0,1},{1,0},{2,3},{3,2},{4,5},{5,4},{6,7},{7,6},{8,9},{9,8},{10,11... | collective-permute-start | bytes 393224 | tf_op jit(solution)/shard_map/ppermute | solution.py:519
  23.1 1.7 %collective-permute-start.13 = (bf16[256,384]{1,0:T(8,128)(2,1)S(1)}, bf16[256,384]{1,0:T(8,128)(2,1)S(1)}, u32[]{:S(2)}, u32[]{:S(2)}) collective-permute-start(bf16[256,384]{1,0:T(8,128)(2,1)S(1)} %get-tuple-element.78), channel_id=1, source_target_pairs={{0,1},{1,0},{2,3},{3,2},{4,5},{5,4},{6,7},{7,6},{8,9},{9,8},{10,11... | collective-permute-start | bytes 589832 | tf_op jit(solution)/shard_map/ppermute | solution.py:519
  23.4 4.6 %collective-permute-start.12 = (bf16[272,128]{1,0:T(8,128)(2,1)S(1)}, bf16[272,128]{1,0:T(8,128)(2,1)S(1)}, u32[]{:S(2)}, u32[]{:S(2)}) collective-permute-start(bf16[272,128]{1,0:T(8,128)(2,1)S(1)} %get-tuple-element.76), channel_id=1, source_target_pairs={{0,4},{4,0},{1,5},{5,1},{2,6},{6,2},{3,7},{7,3},{8,12},{12,8},{9,1... | collective-permute-start | bytes 208904 | tf_op jit(solution)/shard_map/ppermute | solution.py:639
  24.9 5.1 %collective-permute-start.14 = (bf16[272,256]{1,0:T(8,128)(2,1)S(1)}, bf16[272,256]{1,0:T(8,128)(2,1)S(1)}, u32[]{:S(2)}, u32[]{:S(2)}) collective-permute-start(bf16[272,256]{1,0:T(8,128)(2,1)S(1)} %get-tuple-element.79), channel_id=1, source_target_pairs={{0,8},{1,0},{2,10},{3,2},{4,12},{5,4},{6,14},{7,6},{8,16},{9,1},{1... | collective-permute-start | bytes 417800 | tf_op jit(solution)/shard_map/ppermute | solution.py:651
  25.6 4.4 %collective-permute-start.15 = (bf16[272,128]{1,0:T(8,128)(2,1)S(1)}, bf16[272,128]{1,0:T(8,128)(2,1)S(1)}, u32[]{:S(2)}, u32[]{:S(2)}) collective-permute-start(bf16[272,128]{1,0:T(8,128)(2,1)S(1)} %get-tuple-element.80), channel_id=1, source_target_pairs={{0,12},{1,4},{2,14},{3,6},{4,8},{5,0},{6,10},{7,2},{8,20},{9,5},{1... | collective-permute-start | bytes 208904 | tf_op jit(solution)/shard_map/ppermute | solution.py:653
  28.4 3.6 %copy-start = (f32[2,128,256]{2,1,0:T(8,128)S(1)}, f32[2,128,256]{2,1,0:T(8,128)}, u32[]{:S(2)}) copy-start(f32[2,128,256]{2,1,0:T(8,128)} %object_ref.1) | copy-start | bytes 786436
  30.4 1.6 %collective-permute-start.16 = (bf16[3,128,256]{2,1,0:T(8,128)(2,1)S(1)}, bf16[3,128,256]{2,1,0:T(8,128)(2,1)S(1)}, u32[]{:S(2)}, u32[]{:S(2)}) collective-permute-start(bf16[3,128,256]{2,1,0:T(8,128)(2,1)S(1)} %sums.1.own_ref), channel_id=1, source_target_pairs={{0,1},{1,0},{2,3},{3,2},{4,5},{5,4},{6,7},{7,6},{8,9},{9,8},{10,11... | collective-permute-start | bytes 589832 | tf_op jit(solution)/shard_map/ppermute | solution.py:519

commit v16 on v15

--- a/solution.py
+++ b/solution.py
@@ -545,12 +545,12 @@
     )(*(in_hbm(array) for array in (object_field, probe, centers, *tables)))
     over_y = exchange(shared, 2)
     probe_core = exchange(probe_low, 1)
-    probe_core, rest = lax.optimization_barrier((probe_core, rest))
     rest = exchange(rest, 2)
     over_z = lax.ppermute(over_y, "tx", [(z, z ^ 1) for z in range(z_count)])
     x_steps = [1] if sides == 1 else [1, -1]
     rows = lax.ppermute(packed[0], axes, zigzag(0))
-    corners = [lax.ppermute(edge, axes, zigzag(step)) for step, edge in zip(x_steps, packed[1:])]
+    probe_core, *corner_edges = lax.optimization_barrier((probe_core, *packed[1:]))
+    corners = [lax.ppermute(edge, axes, zigzag(step)) for step, edge in zip(x_steps, corner_edges)]
     levels = [lax.ppermute(edge, "ty", level(step)) for step, edge in zip(x_steps, packed[1:])]
     corners, record = lax.optimization_barrier((corners, record))
     record = pl.pallas_call(

time: 33.2 us -> 32.9 us (level)
  starting transfers between devices: 17.1 us -> 14.7 us
  waiting for transfers between devices: 4.02 us -> 6.32 us
    ppermute x1, starting transfers between devices: 1.43 us -> 0.59 us  [on_device(): lax.ppermute(piece, 'ty', level(-step))]
    ppermute x1, waiting for transfers between devices: 0.01 us -> 0.84 us  [on_device(): lax.ppermute(edge, 'ty', level(step))]
    ppermute x10, waiting for transfers between devices: 2.27 us -> 3.07 us  [exchange(): return lax.ppermute(array, 'mode', [(m, m ^ flip) for m in range(m_count)])]
    ppermute x1, starting transfers between devices: 2.43 us -> 1.65 us  [on_device(): lax.ppermute(piece, axes, zigzag(-step))]
    ppermute x1, starting transfers between devices: 2.33 us -> 1.64 us  [on_device(): over_z = lax.ppermute(over_y, 'tx', [(z, z ^ 1) for z in range(z_count)])]
    ppermute x1, waiting for transfers between devices: 0.01 us -> 0.53 us  [on_device(): lax.ppermute(piece, 'ty', level(-step))]
    ppermute x10, starting transfers between devices: 5.62 us -> 5.26 us  [exchange(): return lax.ppermute(array, 'mode', [(m, m ^ flip) for m in range(m_count)])]
    ppermute x1, waiting for transfers between devices: 1.51 us -> 1.87 us  [on_device(): lax.ppermute(piece, axes, zigzag(-step))]
  transfers between devices with their start and end apart: 17 -> 17, of which waited for: 6 -> 8; matrix products, arithmetic and copies ran while one was open for 0% -> 0% of each run, Pallas kernels for 11% -> 11%
where the time goes in v16:
time: 32.9 us; the launch traced here: 32.8 us
  starting transfers between devices  14.7 us (45%)
  Pallas kernels  10.9 us (33%)
  waiting for transfers between devices  6.32 us (19%)
  between operations  0.78 us (2%)
    ppermute x10, starting transfers between devices, exchange(): return lax.ppermute(array, 'mode', [(m, m ^ flip) for m in range(m_count)])  5.26 us
    pallas_call x1, Pallas kernels, on_device(): pl.pallas_call(functools.partial(back_kernel, sides, slots, tile_cols), o...  4.36 us
    ppermute x10, waiting for transfers between devices, exchange(): return lax.ppermute(array, 'mode', [(m, m ^ flip) for m in range(m_count)])  3.07 us
    ppermute x1, starting transfers between devices, on_device(): lax.ppermute(edge, axes, zigzag(step))  2.5 us
    ppermute x1, waiting for transfers between devices, on_device(): lax.ppermute(piece, axes, zigzag(-step))  1.87 us
    ppermute x1, starting transfers between devices, on_device(): lax.ppermute(piece, axes, zigzag(-step))  1.65 us
    ppermute x1, starting transfers between devices, on_device(): over_z = lax.ppermute(over_y, 'tx', [(z, z ^ 1) for z in range(z_count)])  1.64 us
    pallas_call x1, Pallas kernels, on_device(): pl.pallas_call(functools.partial(start_kernel, sides, slots), out_shape=[...  1.64 us
  transfers between devices with their start and end apart: 17, of which 8 were waited for; matrix products, arithmetic and copies ran while one was open for 0% of the time, Pallas kernels for 11%

profile of v16, /device:TPU:0, one launch (start us, length us, event | category | flops | bytes accessed | tf_op | source)
XLA Modules:
  0.0 32.8 jit_solution(2279777926984004051)
XLA Ops:
  0.0 1.6 %start.1 = (bf16[2,2,256,256]{3,2,1,0:T(8,128)(2,1)S(1)}, bf16[256,256]{1,0:T(8,128)(2,1)S(1)}, bf16[2,1,256,256]{3,2,1,0:T(8,128)(2,1)S(1)}, bf16[16,256]{1,0:T...) custom-call(f32[2,128,256]{2,1,0:T(8,128)} %object_ref.1, ...), custom_call_target="tpu_custom_call" | custom-call | tf_op jit(solution)/shard_map/start/pallas_call | solution.py:522
  1.6 0.5 %collective-permute-start = (bf16[2,2,256,256]{3,2,1,0:T(8,128)(2,1)S(1)}, bf16[2,2,256,256]{3,2,1,0:T(8,128)(2,1)S(1)}, u32[]{:S(2)}, u32[]{:S(2)}) collective-permute-start(bf16[2,2,256,256]{3,2,1,0:T(8,128)(2,1)S(1)} %get-tuple-element.43.refs_6_.refs_2_), channel_id=1, source_target_pairs={{0,1},{1,0},{2,3},{3,2},{4,5},{5,4},{6,7},{7,6},{8,9},{9,8},{10,11... | collective-permute-start | bytes 1572872 | tf_op jit(solution)/shard_map/ppermute | solution.py:519
  2.2 2.6 %collective-permute-start.7 = (bf16[256,256]{1,0:T(8,128)(2,1)S(1)}, bf16[256,256]{1,0:T(8,128)(2,1)S(1)}, u32[]{:S(2)}, u32[]{:S(2)}) collective-permute-start(bf16[256,256]{1,0:T(8,128)(2,1)S(1)} %get-tuple-element.59), channel_id=1, source_target_pairs={{0,2},{1,3},{2,0},{3,1},{4,6},{5,7},{6,4},{7,5},{8,10},{9,11},{10,... | collective-permute-start | bytes 393224 | tf_op jit(solution)/shard_map/ppermute | solution.py:519
  4.8 1.6 %collective-permute-start.4 = (bf16[2,128,256]{2,1,0:T(8,128)(2,1)S(1)}, bf16[2,128,256]{2,1,0:T(8,128)(2,1)S(1)}, u32[]{:S(2)}, u32[]{:S(2)}) collective-permute-start(bf16[2,128,256]{2,1,0:T(8,128)(2,1)S(1)} %get-tuple-element.52.refs_0_), channel_id=1, source_target_pairs={{0,8},{1,0},{2,10},{3,2},{4,12},{5,4},{6,14},{7,6},{8,16},{9,1},{1... | collective-permute-start | bytes 393224 | tf_op jit(solution)/shard_map/ppermute | solution.py:551
  6.3 2.5 %collective-permute-start.1 = (bf16[2,128,128]{2,1,0:T(8,128)(2,1)S(1)}, bf16[2,128,128]{2,1,0:T(8,128)(2,1)S(1)}, u32[]{:S(2)}, u32[]{:S(2)}) collective-permute-start(bf16[2,128,128]{2,1,0:T(8,128)(2,1)S(1)} %get-tuple-element.45), channel_id=1, source_target_pairs={{0,12},{1,4},{2,14},{3,6},{4,8},{5,0},{6,10},{7,2},{8,20},{9,5},{1... | collective-permute-start | bytes 196616 | tf_op jit(solution)/shard_map/ppermute | solution.py:553
  8.8 0.5 %collective-permute-start.2 = (bf16[2,1,256,256]{3,2,1,0:T(8,128)(2,1)S(1)}, bf16[2,1,256,256]{3,2,1,0:T(8,128)(2,1)S(1)}, u32[]{:S(2)}, u32[]{:S(2)}) collective-permute-start(bf16[2,1,256,256]{3,2,1,0:T(8,128)(2,1)S(1)} %get-tuple-element.51), channel_id=1, source_target_pairs={{0,2},{1,3},{2,0},{3,1},{4,6},{5,7},{6,4},{7,5},{8,10},{9,11},{10,... | collective-permute-start | bytes 786440 | tf_op jit(solution)/shard_map/ppermute | solution.py:519
  9.3 0.5 %collective-permute-start.6 = (bf16[2,128,128]{2,1,0:T(8,128)(2,1)S(1)}, bf16[2,128,128]{2,1,0:T(8,128)(2,1)S(1)}, u32[]{:S(2)}, u32[]{:S(2)}) collective-permute-start(bf16[2,128,128]{2,1,0:T(8,128)(2,1)S(1)} %get-tuple-element.45), channel_id=1, source_target_pairs={{0,4},{4,0},{1,5},{5,1},{2,6},{6,2},{3,7},{7,3},{8,12},{12,8},{9,1... | collective-permute-start | bytes 196616 | tf_op jit(solution)/shard_map/ppermute | solution.py:554
  10.5 1.6 %collective-permute-start.8 = (bf16[256,256]{1,0:T(8,128)(2,1)S(1)}, bf16[256,256]{1,0:T(8,128)(2,1)S(1)}, u32[]{:S(2)}, u32[]{:S(2)}) collective-permute-start(bf16[256,256]{1,0:T(8,128)(2,1)S(1)} %collective-permute-done.7.over_y.refs_4_), channel_id=1, source_target_pairs={{0,8},{8,0},{16,24},{24,16},{1,9},{9,1},{17,25},{25,17},{2,10},{10... | collective-permute-start | bytes 393224 | tf_op jit(solution)/shard_map/ppermute | solution.py:549
  12.2 0.6 %collective-permute-start.3 = (bf16[2,128,128]{2,1,0:T(8,128)(2,1)S(1)}, bf16[2,128,128]{2,1,0:T(8,128)(2,1)S(1)}, u32[]{:S(2)}, u32[]{:S(2)}) collective-permute-start(bf16[2,128,128]{2,1,0:T(8,128)(2,1)S(1)} %collective-permute-done.1.refs_1_), channel_id=1, source_target_pairs={{0,1},{1,0},{2,3},{3,2},{4,5},{5,4},{6,7},{7,6},{8,9},{9,8},{10,11... | collective-permute-start | bytes 196616 | tf_op jit(solution)/shard_map/ppermute | solution.py:519
  12.8 0.8 %collective-permute-done.6.refs_5_ = bf16[2,128,128]{2,1,0:T(8,128)(2,1)S(1)} collective-permute-done((bf16[2,128,128]{2,1,0:T(8,128)(2,1)S(1)}, bf16[2,128,128]{2,1,0:T(8,128)(2,1)S(1)}, u32[]{:S(2)}, u32[]{:S(2)}) %collective-permute-start.6) | collective-permute-done | bytes 65568 | tf_op jit(solution)/shard_map/ppermute | solution.py:554
  13.6 0.1 collective-permute-done.3.refs_2_
  13.7 1.5 %near.1 = (f32[2,256,256]{2,1,0:T(8,128)S(1)}, f32[2,256,512]{2,1,0:T(8,128)S(1)}, bf16[2,512,256]{2,1,0:T(8,128)(2,1)S(1)}, f32[2,256,256]{2,1,0:T(8,128)S(1)}) custom-call(s32[8,128]{1,0:T(8,128)S(1)} %get-tuple-element.50.spot_ref, bf16[2,128,256]{2,1,0:T(8,128)(2,1)S(1)} %get-tuple-element.52.refs_0_, ...), custom_call_target="tpu_custom_call" | custom-call | flops 33554432 | tf_op jit(solution)/shard_map/near/pallas_call | solution.py:577
  15.2 1.0 %collective-permute-done.2.rest.refs_6_ = bf16[2,1,256,256]{3,2,1,0:T(8,128)(2,1)S(1)} collective-permute-done((bf16[2,1,256,256]{3,2,1,0:T(8,128)(2,1)S(1)}, bf16[2,1,256,256]{3,2,1,0:T(8,128)(2,1)S(1)}, u32[]{:S(2)}, u32[]{:S(2)}) %collective-permute-start.2) | collective-permute-done | bytes 262176 | tf_op jit(solution)/shard_map/ppermute | solution.py:519
  16.2 0.9 %core.1 = (f32[2,256,512]{2,1,0:T(8,128)S(1)}, bf16[2,512,256]{2,1,0:T(8,128)(2,1)S(1)}, f32[2,256,256]{2,1,0:T(8,128)S(1)}) custom-call(f32[2,256,256]{2,1,0:T(8,128)S(1)} %get-tuple-element.57.patch_ref.refs_1_, bf16[2,2,256,256]{3,2,1,0:T(8,128)(2,1)S(1)} %collective-permute-done.core.refs_3_, ...), custom_call_target="tpu_custom_call" | custom-call | flops 33554432 | tf_op jit(solution)/shard_map/core/pallas_call | solution.py:587
  17.0 0.0 copy-start.1
  17.0 0.6 %collective-permute-start.10 = (bf16[256,256]{1,0:T(8,128)(2,1)S(1)}, bf16[256,256]{1,0:T(8,128)(2,1)S(1)}, u32[]{:S(2)}, u32[]{:S(2)}) collective-permute-start(bf16[256,256]{1,0:T(8,128)(2,1)S(1)} %collective-permute-done.8.over_z.refs_5_), channel_id=1, source_target_pairs={{0,1},{1,0},{2,3},{3,2},{4,5},{5,4},{6,7},{7,6},{8,9},{9,8},{10,11... | collective-permute-start | bytes 393224 | tf_op jit(solution)/shard_map/ppermute | solution.py:519
  17.6 0.9 %over.1 = (f32[2,256,512]{2,1,0:T(8,128)S(1)}, bf16[2,512,256]{2,1,0:T(8,128)(2,1)S(1)}, f32[2,256,256]{2,1,0:T(8,128)S(1)}) custom-call(f32[2,256,256]{2,1,0:T(8,128)S(1)} %get-tuple-element.57.patch_ref.refs_1_, bf16[256,256]{1,0:T(8,128)(2,1)S(1)} %collective-permute-done.7.over_y.refs_4_, bf16[256,256]{1,0:T(8,128)(2,1)S(1)} %collective-permute-done.8.over_z.refs_5_, ...), custom_call_target="tpu_custom_call" | custom-call | flops 3355443200 | tf_op jit(solution)/shard_map/over/pallas_call | solution.py:600
  18.5 0.1 collective-permute-done.10.refs_8_
  18.6 4.4 %back.1 = (bf16[256,256]{1,0:T(8,128)(2,1)S(1)}, bf16[256,256]{1,0:T(8,128)(2,1)S(1)}, bf16[256,384]{1,0:T(8,128)(2,1)S(1)}, bf16[256,384]{1,0:T(8,128)(2,1)S(1)}, bf16[272,128]{1,0:T(8,128)(2,1)S(1)}) custom-call(bf16[16,256]{1,0:T(8,128)(2,1)S(1)} %live.1.record_ref, s32[8,128]{1,0:T(8,128)S(1)} %get-tuple-element.50.spot_ref, ...), custom_call_target="tpu_custom_call" | custom-call | flops 2684354560 | tf_op jit(solution)/shard_map/back/pallas_call | solution.py:612
  23.0 0.4 %collective-permute-start.13 = (bf16[256,384]{1,0:T(8,128)(2,1)S(1)}, bf16[256,384]{1,0:T(8,128)(2,1)S(1)}, u32[]{:S(2)}, u32[]{:S(2)}) collective-permute-start(bf16[256,384]{1,0:T(8,128)(2,1)S(1)} %get-tuple-element.78), channel_id=1, source_target_pairs={{0,1},{1,0},{2,3},{3,2},{4,5},{5,4},{6,7},{7,6},{8,9},{9,8},{10,11... | collective-permute-start | bytes 589832 | tf_op jit(solution)/shard_map/ppermute | solution.py:519
  23.4 0.6 %collective-permute-start.12 = (bf16[272,128]{1,0:T(8,128)(2,1)S(1)}, bf16[272,128]{1,0:T(8,128)(2,1)S(1)}, u32[]{:S(2)}, u32[]{:S(2)}) collective-permute-start(bf16[272,128]{1,0:T(8,128)(2,1)S(1)} %get-tuple-element.76), channel_id=1, source_target_pairs={{0,4},{4,0},{1,5},{5,1},{2,6},{6,2},{3,7},{7,3},{8,12},{12,8},{9,1... | collective-permute-start | bytes 208904 | tf_op jit(solution)/shard_map/ppermute | solution.py:639
  24.0 0.5 %collective-permute-done.13.swap_ref = bf16[256,384]{1,0:T(8,128)(2,1)S(1)} collective-permute-done((bf16[256,384]{1,0:T(8,128)(2,1)S(1)}, bf16[256,384]{1,0:T(8,128)(2,1)S(1)}, u32[]{:S(2)}, u32[]{:S(2)}) %collective-permute-start.13) | collective-permute-done | bytes 196640 | tf_op jit(solution)/shard_map/ppermute | solution.py:519
  24.5 0.1 meet.1
  24.5 1.0 %collective-permute-start.14 = (bf16[272,256]{1,0:T(8,128)(2,1)S(1)}, bf16[272,256]{1,0:T(8,128)(2,1)S(1)}, u32[]{:S(2)}, u32[]{:S(2)}) collective-permute-start(bf16[272,256]{1,0:T(8,128)(2,1)S(1)} %get-tuple-element.79), channel_id=1, source_target_pairs={{0,8},{1,0},{2,10},{3,2},{4,12},{5,4},{6,14},{7,6},{8,16},{9,1},{1... | collective-permute-start | bytes 417800 | tf_op jit(solution)/shard_map/ppermute | solution.py:651
  25.5 1.7 %collective-permute-start.15 = (bf16[272,128]{1,0:T(8,128)(2,1)S(1)}, bf16[272,128]{1,0:T(8,128)(2,1)S(1)}, u32[]{:S(2)}, u32[]{:S(2)}) collective-permute-start(bf16[272,128]{1,0:T(8,128)(2,1)S(1)} %get-tuple-element.80), channel_id=1, source_target_pairs={{0,12},{1,4},{2,14},{3,6},{4,8},{5,0},{6,10},{7,2},{8,20},{9,5},{1... | collective-permute-start | bytes 208904 | tf_op jit(solution)/shard_map/ppermute | solution.py:653
  27.2 0.5 %collective-permute-done.12.refs_0_ = bf16[272,128]{1,0:T(8,128)(2,1)S(1)} collective-permute-done((bf16[272,128]{1,0:T(8,128)(2,1)S(1)}, bf16[272,128]{1,0:T(8,128)(2,1)S(1)}, u32[]{:S(2)}, u32[]{:S(2)}) %collective-permute-start.12) | collective-permute-done | bytes 69664 | tf_op jit(solution)/shard_map/ppermute | solution.py:639
  27.7 0.4 %levels.1.level_ref = f32[3,128,256]{2,1,0:T(8,128)S(1)} custom-call(bf16[256,256]{1,0:T(8,128)(2,1)S(1)} %get-tuple-element.74.weight_ref, bf16[16,256]{1,0:T(8,128)(2,1)S(1)} %live.1.record_ref, bf16[256,256]{1,0:T(8,128)(2,1)S(1)} %get-tuple-element.75.own_ref, bf16[272,128]{1,0:T(8,128)(2,1)S(1)} %collective-permute-done.12.refs_0_), custom_call_target="tpu_custom_call" | custom-call | flops 1342177280 | tf_op jit(solution)/shard_map/levels/pallas_call | solution.py:655
  28.1 1.9 %collective-permute-done.15.refs_0_ = bf16[272,128]{1,0:T(8,128)(2,1)S(1)} collective-permute-done((bf16[272,128]{1,0:T(8,128)(2,1)S(1)}, bf16[272,128]{1,0:T(8,128)(2,1)S(1)}, u32[]{:S(2)}, u32[]{:S(2)}) %collective-permute-start.15) | collective-permute-done | bytes 69664 | tf_op jit(solution)/shard_map/ppermute | solution.py:653
  30.0 0.5 %sums.1.own_ref = bf16[3,128,256]{2,1,0:T(8,128)(2,1)S(1)} custom-call(bf16[256,256]{1,0:T(8,128)(2,1)S(1)} %get-tuple-element.74.weight_ref, f32[3,128,256]{2,1,0:T(8,128)S(1)} %levels.1.level_ref, bf16[272,256]{1,0:T(8,128)(2,1)S(1)} %collective-permute-done.14.rows_ref, bf16[272,128]{1,0:T(8,128)(2,1)S(1)} %collective-permute-done.15.refs_0_), custom_call_target="tpu_custom_call" | custom-call | tf_op jit(solution)/shard_map/sums/pallas_call | solution.py:664
  30.5 0.1 collective-permute-start.16
  30.6 1.4 %collective-permute-done.16.other_ref = bf16[3,128,256]{2,1,0:T(8,128)(2,1)S(1)} collective-permute-done((bf16[3,128,256]{2,1,0:T(8,128)(2,1)S(1)}, bf16[3,128,256]{2,1,0:T(8,128)(2,1)S(1)}, u32[]{:S(2)}, u32[]{:S(2)}) %collective-permute-start.16) | collective-permute-done | bytes 196640 | tf_op jit(solution)/shard_map/ppermute | solution.py:519
  32.0 0.8 %update.1 = f32[2,128,256]{2,1,0:T(8,128)} custom-call(f32[2,128,256]{2,1,0:T(8,128)S(1)} %copy-done, bf16[3,128,256]{2,1,0:T(8,128)(2,1)S(1)} %sums.1.own_ref, bf16[3,128,256]{2,1,0:T(8,128)(2,1)S(1)} %collective-permute-done.16.other_ref), custom_call_target="tpu_custom_call" | custom-call | tf_op jit(solution)/shard_map/update/pallas_call | solution.py:672
  (16 shorter events, 0.0 us)
Async XLA Ops:
  1.6 4.7 %collective-permute-start = (bf16[2,2,256,256]{3,2,1,0:T(8,128)(2,1)S(1)}, bf16[2,2,256,256]{3,2,1,0:T(8,128)(2,1)S(1)}, u32[]{:S(2)}, u32[]{:S(2)}) collective-permute-start(bf16[2,2,256,256]{3,2,1,0:T(8,128)(2,1)S(1)} %get-tuple-element.43.refs_6_.refs_2_), channel_id=1, source_target_pairs={{0,1},{1,0},{2,3},{3,2},{4,5},{5,4},{6,7},{7,6},{8,9},{9,8},{10,11... | collective-permute-start | bytes 1572872 | tf_op jit(solution)/shard_map/ppermute | solution.py:519
  2.2 8.4 %collective-permute-start.7 = (bf16[256,256]{1,0:T(8,128)(2,1)S(1)}, bf16[256,256]{1,0:T(8,128)(2,1)S(1)}, u32[]{:S(2)}, u32[]{:S(2)}) collective-permute-start(bf16[256,256]{1,0:T(8,128)(2,1)S(1)} %get-tuple-element.59), channel_id=1, source_target_pairs={{0,2},{1,3},{2,0},{3,1},{4,6},{5,7},{6,4},{7,5},{8,10},{9,11},{10,... | collective-permute-start | bytes 393224 | tf_op jit(solution)/shard_map/ppermute | solution.py:519
  4.8 7.4 %collective-permute-start.4 = (bf16[2,128,256]{2,1,0:T(8,128)(2,1)S(1)}, bf16[2,128,256]{2,1,0:T(8,128)(2,1)S(1)}, u32[]{:S(2)}, u32[]{:S(2)}) collective-permute-start(bf16[2,128,256]{2,1,0:T(8,128)(2,1)S(1)} %get-tuple-element.52.refs_0_), channel_id=1, source_target_pairs={{0,8},{1,0},{2,10},{3,2},{4,12},{5,4},{6,14},{7,6},{8,16},{9,1},{1... | collective-permute-start | bytes 393224 | tf_op jit(solution)/shard_map/ppermute | solution.py:551
  6.3 5.9 %collective-permute-start.1 = (bf16[2,128,128]{2,1,0:T(8,128)(2,1)S(1)}, bf16[2,128,128]{2,1,0:T(8,128)(2,1)S(1)}, u32[]{:S(2)}, u32[]{:S(2)}) collective-permute-start(bf16[2,128,128]{2,1,0:T(8,128)(2,1)S(1)} %get-tuple-element.45), channel_id=1, source_target_pairs={{0,12},{1,4},{2,14},{3,6},{4,8},{5,0},{6,10},{7,2},{8,20},{9,5},{1... | collective-permute-start | bytes 196616 | tf_op jit(solution)/shard_map/ppermute | solution.py:553
  8.8 7.3 %collective-permute-start.2 = (bf16[2,1,256,256]{3,2,1,0:T(8,128)(2,1)S(1)}, bf16[2,1,256,256]{3,2,1,0:T(8,128)(2,1)S(1)}, u32[]{:S(2)}, u32[]{:S(2)}) collective-permute-start(bf16[2,1,256,256]{3,2,1,0:T(8,128)(2,1)S(1)} %get-tuple-element.51), channel_id=1, source_target_pairs={{0,2},{1,3},{2,0},{3,1},{4,6},{5,7},{6,4},{7,5},{8,10},{9,11},{10,... | collective-permute-start | bytes 786440 | tf_op jit(solution)/shard_map/ppermute | solution.py:519
  9.3 4.3 %collective-permute-start.6 = (bf16[2,128,128]{2,1,0:T(8,128)(2,1)S(1)}, bf16[2,128,128]{2,1,0:T(8,128)(2,1)S(1)}, u32[]{:S(2)}, u32[]{:S(2)}) collective-permute-start(bf16[2,128,128]{2,1,0:T(8,128)(2,1)S(1)} %get-tuple-element.45), channel_id=1, source_target_pairs={{0,4},{4,0},{1,5},{5,1},{2,6},{6,2},{3,7},{7,3},{8,12},{12,8},{9,1... | collective-permute-start | bytes 196616 | tf_op jit(solution)/shard_map/ppermute | solution.py:554
  10.5 6.5 %collective-permute-start.8 = (bf16[256,256]{1,0:T(8,128)(2,1)S(1)}, bf16[256,256]{1,0:T(8,128)(2,1)S(1)}, u32[]{:S(2)}, u32[]{:S(2)}) collective-permute-start(bf16[256,256]{1,0:T(8,128)(2,1)S(1)} %collective-permute-done.7.over_y.refs_4_), channel_id=1, source_target_pairs={{0,8},{8,0},{16,24},{24,16},{1,9},{9,1},{17,25},{25,17},{2,10},{10... | collective-permute-start | bytes 393224 | tf_op jit(solution)/shard_map/ppermute | solution.py:549
  12.2 1.4 %collective-permute-start.5 = (bf16[2,128,256]{2,1,0:T(8,128)(2,1)S(1)}, bf16[2,128,256]{2,1,0:T(8,128)(2,1)S(1)}, u32[]{:S(2)}, u32[]{:S(2)}) collective-permute-start(bf16[2,128,256]{2,1,0:T(8,128)(2,1)S(1)} %collective-permute-done.4.refs_3_), channel_id=1, source_target_pairs={{0,1},{1,0},{2,3},{3,2},{4,5},{5,4},{6,7},{7,6},{8,9},{9,8},{10,11... | collective-permute-start | bytes 393224 | tf_op jit(solution)/shard_map/ppermute | solution.py:519
  12.2 1.5 %collective-permute-start.3 = (bf16[2,128,128]{2,1,0:T(8,128)(2,1)S(1)}, bf16[2,128,128]{2,1,0:T(8,128)(2,1)S(1)}, u32[]{:S(2)}, u32[]{:S(2)}) collective-permute-start(bf16[2,128,128]{2,1,0:T(8,128)(2,1)S(1)} %collective-permute-done.1.refs_1_), channel_id=1, source_target_pairs={{0,1},{1,0},{2,3},{3,2},{4,5},{5,4},{6,7},{7,6},{8,9},{9,8},{10,11... | collective-permute-start | bytes 196616 | tf_op jit(solution)/shard_map/ppermute | solution.py:519
  13.6 4.9 %collective-permute-start.9 = (bf16[256,256]{1,0:T(8,128)(2,1)S(1)}, bf16[256,256]{1,0:T(8,128)(2,1)S(1)}, u32[]{:S(2)}, u32[]{:S(2)}) collective-permute-start(bf16[256,256]{1,0:T(8,128)(2,1)S(1)} %collective-permute-done.7.over_y.refs_4_), channel_id=1, source_target_pairs={{0,1},{1,0},{2,3},{3,2},{4,5},{5,4},{6,7},{7,6},{8,9},{9,8},{10,11... | collective-permute-start | bytes 393224 | tf_op jit(solution)/shard_map/ppermute | solution.py:519
  16.2 2.4 %collective-permute-start.11 = (bf16[2,1,256,256]{3,2,1,0:T(8,128)(2,1)S(1)}, bf16[2,1,256,256]{3,2,1,0:T(8,128)(2,1)S(1)}, u32[]{:S(2)}, u32[]{:S(2)}) collective-permute-start(bf16[2,1,256,256]{3,2,1,0:T(8,128)(2,1)S(1)} %collective-permute-done.2.rest.refs_6_), channel_id=1, source_target_pairs={{0,1},{1,0},{2,3},{3,2},{4,5},{5,4},{6,7},{7,6},{8,9},{9,8},{10,11... | collective-permute-start | bytes 786440 | tf_op jit(solution)/shard_map/ppermute | solution.py:519
  17.0 1.6 %copy-start.1 = (bf16[1,1,2,256,256]{4,3,2,1,0:T(8,128)(2,1)S(1)}, bf16[1,1,2,256,256]{4,3,2,1,0:T(8,128)(2,1)}, u32[]{:S(2)}) copy-start(bf16[1,1,2,256,256]{4,3,2,1,0:T(8,128)(2,1)} %refs_0_.1) | copy-start | bytes 786436
  17.0 1.6 %collective-permute-start.10 = (bf16[256,256]{1,0:T(8,128)(2,1)S(1)}, bf16[256,256]{1,0:T(8,128)(2,1)S(1)}, u32[]{:S(2)}, u32[]{:S(2)}) collective-permute-start(bf16[256,256]{1,0:T(8,128)(2,1)S(1)} %collective-permute-done.8.over_z.refs_5_), channel_id=1, source_target_pairs={{0,1},{1,0},{2,3},{3,2},{4,5},{5,4},{6,7},{7,6},{8,9},{9,8},{10,11... | collective-permute-start | bytes 393224 | tf_op jit(solution)/shard_map/ppermute | solution.py:519
  23.0 1.5 %collective-permute-start.13 = (bf16[256,384]{1,0:T(8,128)(2,1)S(1)}, bf16[256,384]{1,0:T(8,128)(2,1)S(1)}, u32[]{:S(2)}, u32[]{:S(2)}) collective-permute-start(bf16[256,384]{1,0:T(8,128)(2,1)S(1)} %get-tuple-element.78), channel_id=1, source_target_pairs={{0,1},{1,0},{2,3},{3,2},{4,5},{5,4},{6,7},{7,6},{8,9},{9,8},{10,11... | collective-permute-start | bytes 589832 | tf_op jit(solution)/shard_map/ppermute | solution.py:519
  23.4 4.3 %collective-permute-start.12 = (bf16[272,128]{1,0:T(8,128)(2,1)S(1)}, bf16[272,128]{1,0:T(8,128)(2,1)S(1)}, u32[]{:S(2)}, u32[]{:S(2)}) collective-permute-start(bf16[272,128]{1,0:T(8,128)(2,1)S(1)} %get-tuple-element.76), channel_id=1, source_target_pairs={{0,4},{4,0},{1,5},{5,1},{2,6},{6,2},{3,7},{7,3},{8,12},{12,8},{9,1... | collective-permute-start | bytes 208904 | tf_op jit(solution)/shard_map/ppermute | solution.py:639
  24.5 5.5 %collective-permute-start.14 = (bf16[272,256]{1,0:T(8,128)(2,1)S(1)}, bf16[272,256]{1,0:T(8,128)(2,1)S(1)}, u32[]{:S(2)}, u32[]{:S(2)}) collective-permute-start(bf16[272,256]{1,0:T(8,128)(2,1)S(1)} %get-tuple-element.79), channel_id=1, source_target_pairs={{0,8},{1,0},{2,10},{3,2},{4,12},{5,4},{6,14},{7,6},{8,16},{9,1},{1... | collective-permute-start | bytes 417800 | tf_op jit(solution)/shard_map/ppermute | solution.py:651
  25.5 4.5 %collective-permute-start.15 = (bf16[272,128]{1,0:T(8,128)(2,1)S(1)}, bf16[272,128]{1,0:T(8,128)(2,1)S(1)}, u32[]{:S(2)}, u32[]{:S(2)}) collective-permute-start(bf16[272,128]{1,0:T(8,128)(2,1)S(1)} %get-tuple-element.80), channel_id=1, source_target_pairs={{0,12},{1,4},{2,14},{3,6},{4,8},{5,0},{6,10},{7,2},{8,20},{9,5},{1... | collective-permute-start | bytes 208904 | tf_op jit(solution)/shard_map/ppermute | solution.py:653
  28.1 3.9 %copy-start = (f32[2,128,256]{2,1,0:T(8,128)S(1)}, f32[2,128,256]{2,1,0:T(8,128)}, u32[]{:S(2)}) copy-start(f32[2,128,256]{2,1,0:T(8,128)} %object_ref.1) | copy-start | bytes 786436
  30.5 1.5 %collective-permute-start.16 = (bf16[3,128,256]{2,1,0:T(8,128)(2,1)S(1)}, bf16[3,128,256]{2,1,0:T(8,128)(2,1)S(1)}, u32[]{:S(2)}, u32[]{:S(2)}) collective-permute-start(bf16[3,128,256]{2,1,0:T(8,128)(2,1)S(1)} %sums.1.own_ref), channel_id=1, source_target_pairs={{0,1},{1,0},{2,3},{3,2},{4,5},{5,4},{6,7},{7,6},{8,9},{9,8},{10,11... | collective-permute-start | bytes 589832 | tf_op jit(solution)/shard_map/ppermute | solution.py:519

commit v17 on v16

--- a/solution.py
+++ b/solution.py
@@ -559,7 +559,7 @@
         in_specs=[vmem(), smem()],
         out_specs=vmem(),
         compiler_params=pltpu.CompilerParams(vmem_limit_bytes=small_bytes),
-        cost_estimate=cost(50),
+        cost_estimate=cost(40),
         name="live",
     )(record, live)
     corners, record = lax.optimization_barrier((corners, record))

time: 32.9 us -> 33.3 us (1.012)
  starting transfers between devices: 14.7 us -> 16 us
  waiting for transfers between devices: 6.32 us -> 5.4 us
    ppermute x10, waiting for transfers between devices: 3.07 us -> 1.9 us  [exchange(): return lax.ppermute(array, 'mode', [(m, m ^ flip) for m in range(m_count)])]
    ppermute x1, starting transfers between devices: 0.99 us -> 1.87 us  [on_device(): rows = lax.ppermute(rows, axes, zigzag(0))]
    ppermute x1, starting transfers between devices: 0.59 us -> 1.4 us  [on_device(): lax.ppermute(piece, 'ty', level(-step))]
    ppermute x1, waiting for transfers between devices: 1.87 us -> 2.65 us  [on_device(): lax.ppermute(piece, axes, zigzag(-step))]
    ppermute x1, waiting for transfers between devices: 0.53 us -> 0.01 us  [on_device(): lax.ppermute(piece, 'ty', level(-step))]
  transfers between devices with their start and end apart: 17 -> 17, of which waited for: 8 -> 5; matrix products, arithmetic and copies ran while one was open for 0% -> 0% of each run, Pallas kernels for 11% -> 11%
where the time goes in v17:
time: 33.3 us; the launch traced here: 33.2 us
  starting transfers between devices  16 us (48%)
  Pallas kernels  10.9 us (33%)
  waiting for transfers between devices  5.4 us (16%)
  between operations  0.78 us (2%)
    ppermute x10, starting transfers between devices, exchange(): return lax.ppermute(array, 'mode', [(m, m ^ flip) for m in range(m_count)])  5.11 us
    pallas_call x1, Pallas kernels, on_device(): pl.pallas_call(functools.partial(back_kernel, sides, slots, tile_cols), o...  4.37 us
    ppermute x1, waiting for transfers between devices, on_device(): lax.ppermute(piece, axes, zigzag(-step))  2.65 us
    ppermute x1, starting transfers between devices, on_device(): lax.ppermute(edge, axes, zigzag(step))  2.5 us
    ppermute x10, waiting for transfers between devices, exchange(): return lax.ppermute(array, 'mode', [(m, m ^ flip) for m in range(m_count)])  1.9 us
    ppermute x1, starting transfers between devices, on_device(): rows = lax.ppermute(rows, axes, zigzag(0))  1.87 us
    ppermute x1, starting transfers between devices, on_device(): over_z = lax.ppermute(over_y, 'tx', [(z, z ^ 1) for z in range(z_count)])  1.64 us
    pallas_call x1, Pallas kernels, on_device(): pl.pallas_call(functools.partial(start_kernel, sides, slots), out_shape=[...  1.64 us
  transfers between devices with their start and end apart: 17, of which 5 were waited for; matrix products, arithmetic and copies ran while one was open for 0% of the time, Pallas kernels for 11%

profile of v17, /device:TPU:0, one launch (start us, length us, event | category | flops | bytes accessed | tf_op | source)
XLA Modules:
  0.0 33.2 jit_solution(1131898447584701447)
XLA Ops:
  0.0 1.6 %start.1 = (bf16[2,2,256,256]{3,2,1,0:T(8,128)(2,1)S(1)}, bf16[256,256]{1,0:T(8,128)(2,1)S(1)}, bf16[2,1,256,256]{3,2,1,0:T(8,128)(2,1)S(1)}, bf16[16,256]{1,0:T...) custom-call(f32[2,128,256]{2,1,0:T(8,128)} %object_ref.1, ...), custom_call_target="tpu_custom_call" | custom-call | tf_op jit(solution)/shard_map/start/pallas_call | solution.py:522
  1.6 0.5 %collective-permute-start = (bf16[2,2,256,256]{3,2,1,0:T(8,128)(2,1)S(1)}, bf16[2,2,256,256]{3,2,1,0:T(8,128)(2,1)S(1)}, u32[]{:S(2)}, u32[]{:S(2)}) collective-permute-start(bf16[2,2,256,256]{3,2,1,0:T(8,128)(2,1)S(1)} %get-tuple-element.43.refs_6_.refs_2_), channel_id=1, source_target_pairs={{0,1},{1,0},{2,3},{3,2},{4,5},{5,4},{6,7},{7,6},{8,9},{9,8},{10,11... | collective-permute-start | bytes 1572872 | tf_op jit(solution)/shard_map/ppermute | solution.py:519
  2.2 2.6 %collective-permute-start.7 = (bf16[256,256]{1,0:T(8,128)(2,1)S(1)}, bf16[256,256]{1,0:T(8,128)(2,1)S(1)}, u32[]{:S(2)}, u32[]{:S(2)}) collective-permute-start(bf16[256,256]{1,0:T(8,128)(2,1)S(1)} %get-tuple-element.59), channel_id=1, source_target_pairs={{0,2},{1,3},{2,0},{3,1},{4,6},{5,7},{6,4},{7,5},{8,10},{9,11},{10,... | collective-permute-start | bytes 393224 | tf_op jit(solution)/shard_map/ppermute | solution.py:519
  4.8 1.6 %collective-permute-start.4 = (bf16[2,128,256]{2,1,0:T(8,128)(2,1)S(1)}, bf16[2,128,256]{2,1,0:T(8,128)(2,1)S(1)}, u32[]{:S(2)}, u32[]{:S(2)}) collective-permute-start(bf16[2,128,256]{2,1,0:T(8,128)(2,1)S(1)} %get-tuple-element.52.refs_0_), channel_id=1, source_target_pairs={{0,8},{1,0},{2,10},{3,2},{4,12},{5,4},{6,14},{7,6},{8,16},{9,1},{1... | collective-permute-start | bytes 393224 | tf_op jit(solution)/shard_map/ppermute | solution.py:551
  6.3 0.5 %collective-permute-start.2 = (bf16[2,1,256,256]{3,2,1,0:T(8,128)(2,1)S(1)}, bf16[2,1,256,256]{3,2,1,0:T(8,128)(2,1)S(1)}, u32[]{:S(2)}, u32[]{:S(2)}) collective-permute-start(bf16[2,1,256,256]{3,2,1,0:T(8,128)(2,1)S(1)} %get-tuple-element.51), channel_id=1, source_target_pairs={{0,2},{1,3},{2,0},{3,1},{4,6},{5,7},{6,4},{7,5},{8,10},{9,11},{10,... | collective-permute-start | bytes 786440 | tf_op jit(solution)/shard_map/ppermute | solution.py:519
  6.8 0.0 collective-permute-done.core.refs_3_
  6.8 2.5 %collective-permute-start.1 = (bf16[2,128,128]{2,1,0:T(8,128)(2,1)S(1)}, bf16[2,128,128]{2,1,0:T(8,128)(2,1)S(1)}, u32[]{:S(2)}, u32[]{:S(2)}) collective-permute-start(bf16[2,128,128]{2,1,0:T(8,128)(2,1)S(1)} %get-tuple-element.45), channel_id=1, source_target_pairs={{0,12},{1,4},{2,14},{3,6},{4,8},{5,0},{6,10},{7,2},{8,20},{9,5},{1... | collective-permute-start | bytes 196616 | tf_op jit(solution)/shard_map/ppermute | solution.py:553
  9.3 0.5 %collective-permute-start.6 = (bf16[2,128,128]{2,1,0:T(8,128)(2,1)S(1)}, bf16[2,128,128]{2,1,0:T(8,128)(2,1)S(1)}, u32[]{:S(2)}, u32[]{:S(2)}) collective-permute-start(bf16[2,128,128]{2,1,0:T(8,128)(2,1)S(1)} %get-tuple-element.45), channel_id=1, source_target_pairs={{0,4},{4,0},{1,5},{5,1},{2,6},{6,2},{3,7},{7,3},{8,12},{12,8},{9,1... | collective-permute-start | bytes 196616 | tf_op jit(solution)/shard_map/ppermute | solution.py:554
  10.5 1.6 %collective-permute-start.8 = (bf16[256,256]{1,0:T(8,128)(2,1)S(1)}, bf16[256,256]{1,0:T(8,128)(2,1)S(1)}, u32[]{:S(2)}, u32[]{:S(2)}) collective-permute-start(bf16[256,256]{1,0:T(8,128)(2,1)S(1)} %collective-permute-done.7.over_y.refs_4_), channel_id=1, source_target_pairs={{0,8},{8,0},{16,24},{24,16},{1,9},{9,1},{17,25},{25,17},{2,10},{10... | collective-permute-start | bytes 393224 | tf_op jit(solution)/shard_map/ppermute | solution.py:549
  12.2 0.6 %collective-permute-start.3 = (bf16[2,128,128]{2,1,0:T(8,128)(2,1)S(1)}, bf16[2,128,128]{2,1,0:T(8,128)(2,1)S(1)}, u32[]{:S(2)}, u32[]{:S(2)}) collective-permute-start(bf16[2,128,128]{2,1,0:T(8,128)(2,1)S(1)} %collective-permute-done.1.refs_1_), channel_id=1, source_target_pairs={{0,1},{1,0},{2,3},{3,2},{4,5},{5,4},{6,7},{7,6},{8,9},{9,8},{10,11... | collective-permute-start | bytes 196616 | tf_op jit(solution)/shard_map/ppermute | solution.py:519
  12.8 0.8 %collective-permute-done.6.refs_5_ = bf16[2,128,128]{2,1,0:T(8,128)(2,1)S(1)} collective-permute-done((bf16[2,128,128]{2,1,0:T(8,128)(2,1)S(1)}, bf16[2,128,128]{2,1,0:T(8,128)(2,1)S(1)}, u32[]{:S(2)}, u32[]{:S(2)}) %collective-permute-start.6) | collective-permute-done | bytes 65568 | tf_op jit(solution)/shard_map/ppermute | solution.py:554
  13.6 0.1 collective-permute-done.3.refs_2_
  13.7 1.5 %near.1 = (f32[2,256,256]{2,1,0:T(8,128)S(1)}, f32[2,256,512]{2,1,0:T(8,128)S(1)}, bf16[2,512,256]{2,1,0:T(8,128)(2,1)S(1)}, f32[2,256,256]{2,1,0:T(8,128)S(1)}) custom-call(s32[8,128]{1,0:T(8,128)S(1)} %get-tuple-element.50.spot_ref, bf16[2,128,256]{2,1,0:T(8,128)(2,1)S(1)} %get-tuple-element.52.refs_0_, ...), custom_call_target="tpu_custom_call" | custom-call | flops 33554432 | tf_op jit(solution)/shard_map/near/pallas_call | solution.py:577
  15.2 0.5 %collective-permute-start.11 = (bf16[2,1,256,256]{3,2,1,0:T(8,128)(2,1)S(1)}, bf16[2,1,256,256]{3,2,1,0:T(8,128)(2,1)S(1)}, u32[]{:S(2)}, u32[]{:S(2)}) collective-permute-start(bf16[2,1,256,256]{3,2,1,0:T(8,128)(2,1)S(1)} %collective-permute-done.2.rest.refs_6_), channel_id=1, source_target_pairs={{0,1},{1,0},{2,3},{3,2},{4,5},{5,4},{6,7},{7,6},{8,9},{9,8},{10,11... | collective-permute-start | bytes 786440 | tf_op jit(solution)/shard_map/ppermute | solution.py:519
  15.7 0.9 %core.1 = (f32[2,256,512]{2,1,0:T(8,128)S(1)}, bf16[2,512,256]{2,1,0:T(8,128)(2,1)S(1)}, f32[2,256,256]{2,1,0:T(8,128)S(1)}) custom-call(f32[2,256,256]{2,1,0:T(8,128)S(1)} %get-tuple-element.57.patch_ref.refs_1_, bf16[2,2,256,256]{3,2,1,0:T(8,128)(2,1)S(1)} %collective-permute-done.core.refs_3_, ...), custom_call_target="tpu_custom_call" | custom-call | flops 33554432 | tf_op jit(solution)/shard_map/core/pallas_call | solution.py:587
  16.6 0.0 copy-start.1
  16.6 0.1 collective-permute-start.10
  16.7 0.9 %over.1 = (f32[2,256,512]{2,1,0:T(8,128)S(1)}, bf16[2,512,256]{2,1,0:T(8,128)(2,1)S(1)}, f32[2,256,256]{2,1,0:T(8,128)S(1)}) custom-call(f32[2,256,256]{2,1,0:T(8,128)S(1)} %get-tuple-element.57.patch_ref.refs_1_, bf16[256,256]{1,0:T(8,128)(2,1)S(1)} %collective-permute-done.7.over_y.refs_4_, bf16[256,256]{1,0:T(8,128)(2,1)S(1)} %collective-permute-done.8.over_z.refs_5_, ...), custom_call_target="tpu_custom_call" | custom-call | flops 3355443200 | tf_op jit(solution)/shard_map/over/pallas_call | solution.py:600
  17.6 0.4 %collective-permute-done.10.refs_8_ = bf16[256,256]{1,0:T(8,128)(2,1)S(1)} collective-permute-done((bf16[256,256]{1,0:T(8,128)(2,1)S(1)}, bf16[256,256]{1,0:T(8,128)(2,1)S(1)}, u32[]{:S(2)}, u32[]{:S(2)}) %collective-permute-start.10) | collective-permute-done | bytes 131104 | tf_op jit(solution)/shard_map/ppermute | solution.py:519
  18.0 4.4 %back.1 = (bf16[256,256]{1,0:T(8,128)(2,1)S(1)}, bf16[256,256]{1,0:T(8,128)(2,1)S(1)}, bf16[256,384]{1,0:T(8,128)(2,1)S(1)}, bf16[256,384]{1,0:T(8,128)(2,1)S(1)}, bf16[272,128]{1,0:T(8,128)(2,1)S(1)}) custom-call(bf16[16,256]{1,0:T(8,128)(2,1)S(1)} %live.1.record_ref, s32[8,128]{1,0:T(8,128)S(1)} %get-tuple-element.50.spot_ref, ...), custom_call_target="tpu_custom_call" | custom-call | flops 2684354560 | tf_op jit(solution)/shard_map/back/pallas_call | solution.py:612
  22.4 0.2 collective-permute-start.13
  22.6 1.4 %collective-permute-start.12 = (bf16[272,128]{1,0:T(8,128)(2,1)S(1)}, bf16[272,128]{1,0:T(8,128)(2,1)S(1)}, u32[]{:S(2)}, u32[]{:S(2)}) collective-permute-start(bf16[272,128]{1,0:T(8,128)(2,1)S(1)} %get-tuple-element.76), channel_id=1, source_target_pairs={{0,4},{4,0},{1,5},{5,1},{2,6},{6,2},{3,7},{7,3},{8,12},{12,8},{9,1... | collective-permute-start | bytes 208904 | tf_op jit(solution)/shard_map/ppermute | solution.py:639
  24.0 0.1 meet.1
  24.0 1.9 %collective-permute-start.14 = (bf16[272,256]{1,0:T(8,128)(2,1)S(1)}, bf16[272,256]{1,0:T(8,128)(2,1)S(1)}, u32[]{:S(2)}, u32[]{:S(2)}) collective-permute-start(bf16[272,256]{1,0:T(8,128)(2,1)S(1)} %get-tuple-element.79), channel_id=1, source_target_pairs={{0,8},{1,0},{2,10},{3,2},{4,12},{5,4},{6,14},{7,6},{8,16},{9,1},{1... | collective-permute-start | bytes 417800 | tf_op jit(solution)/shard_map/ppermute | solution.py:651
  25.9 1.4 %collective-permute-start.15 = (bf16[272,128]{1,0:T(8,128)(2,1)S(1)}, bf16[272,128]{1,0:T(8,128)(2,1)S(1)}, u32[]{:S(2)}, u32[]{:S(2)}) collective-permute-start(bf16[272,128]{1,0:T(8,128)(2,1)S(1)} %get-tuple-element.80), channel_id=1, source_target_pairs={{0,12},{1,4},{2,14},{3,6},{4,8},{5,0},{6,10},{7,2},{8,20},{9,5},{1... | collective-permute-start | bytes 208904 | tf_op jit(solution)/shard_map/ppermute | solution.py:653
  27.3 0.4 %levels.1.level_ref = f32[3,128,256]{2,1,0:T(8,128)S(1)} custom-call(bf16[256,256]{1,0:T(8,128)(2,1)S(1)} %get-tuple-element.74.weight_ref, bf16[16,256]{1,0:T(8,128)(2,1)S(1)} %live.1.record_ref, bf16[256,256]{1,0:T(8,128)(2,1)S(1)} %get-tuple-element.75.own_ref, bf16[272,128]{1,0:T(8,128)(2,1)S(1)} %collective-permute-done.12.refs_0_), custom_call_target="tpu_custom_call" | custom-call | flops 1342177280 | tf_op jit(solution)/shard_map/levels/pallas_call | solution.py:655
  27.7 0.0 copy-start
  27.7 2.6 %collective-permute-done.15.refs_0_ = bf16[272,128]{1,0:T(8,128)(2,1)S(1)} collective-permute-done((bf16[272,128]{1,0:T(8,128)(2,1)S(1)}, bf16[272,128]{1,0:T(8,128)(2,1)S(1)}, u32[]{:S(2)}, u32[]{:S(2)}) %collective-permute-start.15) | collective-permute-done | bytes 69664 | tf_op jit(solution)/shard_map/ppermute | solution.py:653
  30.4 0.5 %sums.1.own_ref = bf16[3,128,256]{2,1,0:T(8,128)(2,1)S(1)} custom-call(bf16[256,256]{1,0:T(8,128)(2,1)S(1)} %get-tuple-element.74.weight_ref, f32[3,128,256]{2,1,0:T(8,128)S(1)} %levels.1.level_ref, bf16[272,256]{1,0:T(8,128)(2,1)S(1)} %collective-permute-done.14.rows_ref, bf16[272,128]{1,0:T(8,128)(2,1)S(1)} %collective-permute-done.15.refs_0_), custom_call_target="tpu_custom_call" | custom-call | tf_op jit(solution)/shard_map/sums/pallas_call | solution.py:664
  30.9 0.1 collective-permute-start.16
  30.9 1.4 %collective-permute-done.16.other_ref = bf16[3,128,256]{2,1,0:T(8,128)(2,1)S(1)} collective-permute-done((bf16[3,128,256]{2,1,0:T(8,128)(2,1)S(1)}, bf16[3,128,256]{2,1,0:T(8,128)(2,1)S(1)}, u32[]{:S(2)}, u32[]{:S(2)}) %collective-permute-start.16) | collective-permute-done | bytes 196640 | tf_op jit(solution)/shard_map/ppermute | solution.py:519
  32.4 0.8 %update.1 = f32[2,128,256]{2,1,0:T(8,128)} custom-call(f32[2,128,256]{2,1,0:T(8,128)S(1)} %copy-done, bf16[3,128,256]{2,1,0:T(8,128)(2,1)S(1)} %sums.1.own_ref, bf16[3,128,256]{2,1,0:T(8,128)(2,1)S(1)} %collective-permute-done.16.other_ref), custom_call_target="tpu_custom_call" | custom-call | tf_op jit(solution)/shard_map/update/pallas_call | solution.py:672
  (16 shorter events, 0.0 us)
Async XLA Ops:
  1.6 5.2 %collective-permute-start = (bf16[2,2,256,256]{3,2,1,0:T(8,128)(2,1)S(1)}, bf16[2,2,256,256]{3,2,1,0:T(8,128)(2,1)S(1)}, u32[]{:S(2)}, u32[]{:S(2)}) collective-permute-start(bf16[2,2,256,256]{3,2,1,0:T(8,128)(2,1)S(1)} %get-tuple-element.43.refs_6_.refs_2_), channel_id=1, source_target_pairs={{0,1},{1,0},{2,3},{3,2},{4,5},{5,4},{6,7},{7,6},{8,9},{9,8},{10,11... | collective-permute-start | bytes 1572872 | tf_op jit(solution)/shard_map/ppermute | solution.py:519
  2.2 8.4 %collective-permute-start.7 = (bf16[256,256]{1,0:T(8,128)(2,1)S(1)}, bf16[256,256]{1,0:T(8,128)(2,1)S(1)}, u32[]{:S(2)}, u32[]{:S(2)}) collective-permute-start(bf16[256,256]{1,0:T(8,128)(2,1)S(1)} %get-tuple-element.59), channel_id=1, source_target_pairs={{0,2},{1,3},{2,0},{3,1},{4,6},{5,7},{6,4},{7,5},{8,10},{9,11},{10,... | collective-permute-start | bytes 393224 | tf_op jit(solution)/shard_map/ppermute | solution.py:519
  4.8 7.4 %collective-permute-start.4 = (bf16[2,128,256]{2,1,0:T(8,128)(2,1)S(1)}, bf16[2,128,256]{2,1,0:T(8,128)(2,1)S(1)}, u32[]{:S(2)}, u32[]{:S(2)}) collective-permute-start(bf16[2,128,256]{2,1,0:T(8,128)(2,1)S(1)} %get-tuple-element.52.refs_0_), channel_id=1, source_target_pairs={{0,8},{1,0},{2,10},{3,2},{4,12},{5,4},{6,14},{7,6},{8,16},{9,1},{1... | collective-permute-start | bytes 393224 | tf_op jit(solution)/shard_map/ppermute | solution.py:551
  6.3 8.8 %collective-permute-start.2 = (bf16[2,1,256,256]{3,2,1,0:T(8,128)(2,1)S(1)}, bf16[2,1,256,256]{3,2,1,0:T(8,128)(2,1)S(1)}, u32[]{:S(2)}, u32[]{:S(2)}) collective-permute-start(bf16[2,1,256,256]{3,2,1,0:T(8,128)(2,1)S(1)} %get-tuple-element.51), channel_id=1, source_target_pairs={{0,2},{1,3},{2,0},{3,1},{4,6},{5,7},{6,4},{7,5},{8,10},{9,11},{10,... | collective-permute-start | bytes 786440 | tf_op jit(solution)/shard_map/ppermute | solution.py:519
  6.8 5.4 %collective-permute-start.1 = (bf16[2,128,128]{2,1,0:T(8,128)(2,1)S(1)}, bf16[2,128,128]{2,1,0:T(8,128)(2,1)S(1)}, u32[]{:S(2)}, u32[]{:S(2)}) collective-permute-start(bf16[2,128,128]{2,1,0:T(8,128)(2,1)S(1)} %get-tuple-element.45), channel_id=1, source_target_pairs={{0,12},{1,4},{2,14},{3,6},{4,8},{5,0},{6,10},{7,2},{8,20},{9,5},{1... | collective-permute-start | bytes 196616 | tf_op jit(solution)/shard_map/ppermute | solution.py:553
  9.3 4.3 %collective-permute-start.6 = (bf16[2,128,128]{2,1,0:T(8,128)(2,1)S(1)}, bf16[2,128,128]{2,1,0:T(8,128)(2,1)S(1)}, u32[]{:S(2)}, u32[]{:S(2)}) collective-permute-start(bf16[2,128,128]{2,1,0:T(8,128)(2,1)S(1)} %get-tuple-element.45), channel_id=1, source_target_pairs={{0,4},{4,0},{1,5},{5,1},{2,6},{6,2},{3,7},{7,3},{8,12},{12,8},{9,1... | collective-permute-start | bytes 196616 | tf_op jit(solution)/shard_map/ppermute | solution.py:554
  10.5 6.0 %collective-permute-start.8 = (bf16[256,256]{1,0:T(8,128)(2,1)S(1)}, bf16[256,256]{1,0:T(8,128)(2,1)S(1)}, u32[]{:S(2)}, u32[]{:S(2)}) collective-permute-start(bf16[256,256]{1,0:T(8,128)(2,1)S(1)} %collective-permute-done.7.over_y.refs_4_), channel_id=1, source_target_pairs={{0,8},{8,0},{16,24},{24,16},{1,9},{9,1},{17,25},{25,17},{2,10},{10... | collective-permute-start | bytes 393224 | tf_op jit(solution)/shard_map/ppermute | solution.py:549
  12.2 1.4 %collective-permute-start.5 = (bf16[2,128,256]{2,1,0:T(8,128)(2,1)S(1)}, bf16[2,128,256]{2,1,0:T(8,128)(2,1)S(1)}, u32[]{:S(2)}, u32[]{:S(2)}) collective-permute-start(bf16[2,128,256]{2,1,0:T(8,128)(2,1)S(1)} %collective-permute-done.4.refs_3_), channel_id=1, source_target_pairs={{0,1},{1,0},{2,3},{3,2},{4,5},{5,4},{6,7},{7,6},{8,9},{9,8},{10,11... | collective-permute-start | bytes 393224 | tf_op jit(solution)/shard_map/ppermute | solution.py:519
  12.2 1.5 %collective-permute-start.3 = (bf16[2,128,128]{2,1,0:T(8,128)(2,1)S(1)}, bf16[2,128,128]{2,1,0:T(8,128)(2,1)S(1)}, u32[]{:S(2)}, u32[]{:S(2)}) collective-permute-start(bf16[2,128,128]{2,1,0:T(8,128)(2,1)S(1)} %collective-permute-done.1.refs_1_), channel_id=1, source_target_pairs={{0,1},{1,0},{2,3},{3,2},{4,5},{5,4},{6,7},{7,6},{8,9},{9,8},{10,11... | collective-permute-start | bytes 196616 | tf_op jit(solution)/shard_map/ppermute | solution.py:519
  13.6 4.0 %collective-permute-start.9 = (bf16[256,256]{1,0:T(8,128)(2,1)S(1)}, bf16[256,256]{1,0:T(8,128)(2,1)S(1)}, u32[]{:S(2)}, u32[]{:S(2)}) collective-permute-start(bf16[256,256]{1,0:T(8,128)(2,1)S(1)} %collective-permute-done.7.over_y.refs_4_), channel_id=1, source_target_pairs={{0,1},{1,0},{2,3},{3,2},{4,5},{5,4},{6,7},{7,6},{8,9},{9,8},{10,11... | collective-permute-start | bytes 393224 | tf_op jit(solution)/shard_map/ppermute | solution.py:519
  15.2 2.8 %collective-permute-start.11 = (bf16[2,1,256,256]{3,2,1,0:T(8,128)(2,1)S(1)}, bf16[2,1,256,256]{3,2,1,0:T(8,128)(2,1)S(1)}, u32[]{:S(2)}, u32[]{:S(2)}) collective-permute-start(bf16[2,1,256,256]{3,2,1,0:T(8,128)(2,1)S(1)} %collective-permute-done.2.rest.refs_6_), channel_id=1, source_target_pairs={{0,1},{1,0},{2,3},{3,2},{4,5},{5,4},{6,7},{7,6},{8,9},{9,8},{10,11... | collective-permute-start | bytes 786440 | tf_op jit(solution)/shard_map/ppermute | solution.py:519
  16.6 1.4 %copy-start.1 = (bf16[1,1,2,256,256]{4,3,2,1,0:T(8,128)(2,1)S(1)}, bf16[1,1,2,256,256]{4,3,2,1,0:T(8,128)(2,1)}, u32[]{:S(2)}) copy-start(bf16[1,1,2,256,256]{4,3,2,1,0:T(8,128)(2,1)} %refs_0_.1) | copy-start | bytes 786436
  16.6 1.4 %collective-permute-start.10 = (bf16[256,256]{1,0:T(8,128)(2,1)S(1)}, bf16[256,256]{1,0:T(8,128)(2,1)S(1)}, u32[]{:S(2)}, u32[]{:S(2)}) collective-permute-start(bf16[256,256]{1,0:T(8,128)(2,1)S(1)} %collective-permute-done.8.over_z.refs_5_), channel_id=1, source_target_pairs={{0,1},{1,0},{2,3},{3,2},{4,5},{5,4},{6,7},{7,6},{8,9},{9,8},{10,11... | collective-permute-start | bytes 393224 | tf_op jit(solution)/shard_map/ppermute | solution.py:519
  22.4 1.6 %collective-permute-start.13 = (bf16[256,384]{1,0:T(8,128)(2,1)S(1)}, bf16[256,384]{1,0:T(8,128)(2,1)S(1)}, u32[]{:S(2)}, u32[]{:S(2)}) collective-permute-start(bf16[256,384]{1,0:T(8,128)(2,1)S(1)} %get-tuple-element.78), channel_id=1, source_target_pairs={{0,1},{1,0},{2,3},{3,2},{4,5},{5,4},{6,7},{7,6},{8,9},{9,8},{10,11... | collective-permute-start | bytes 589832 | tf_op jit(solution)/shard_map/ppermute | solution.py:519
  22.6 4.7 %collective-permute-start.12 = (bf16[272,128]{1,0:T(8,128)(2,1)S(1)}, bf16[272,128]{1,0:T(8,128)(2,1)S(1)}, u32[]{:S(2)}, u32[]{:S(2)}) collective-permute-start(bf16[272,128]{1,0:T(8,128)(2,1)S(1)} %get-tuple-element.76), channel_id=1, source_target_pairs={{0,4},{4,0},{1,5},{5,1},{2,6},{6,2},{3,7},{7,3},{8,12},{12,8},{9,1... | collective-permute-start | bytes 208904 | tf_op jit(solution)/shard_map/ppermute | solution.py:639
  24.0 6.4 %collective-permute-start.14 = (bf16[272,256]{1,0:T(8,128)(2,1)S(1)}, bf16[272,256]{1,0:T(8,128)(2,1)S(1)}, u32[]{:S(2)}, u32[]{:S(2)}) collective-permute-start(bf16[272,256]{1,0:T(8,128)(2,1)S(1)} %get-tuple-element.79), channel_id=1, source_target_pairs={{0,8},{1,0},{2,10},{3,2},{4,12},{5,4},{6,14},{7,6},{8,16},{9,1},{1... | collective-permute-start | bytes 417800 | tf_op jit(solution)/shard_map/ppermute | solution.py:651
  25.9 4.5 %collective-permute-start.15 = (bf16[272,128]{1,0:T(8,128)(2,1)S(1)}, bf16[272,128]{1,0:T(8,128)(2,1)S(1)}, u32[]{:S(2)}, u32[]{:S(2)}) collective-permute-start(bf16[272,128]{1,0:T(8,128)(2,1)S(1)} %get-tuple-element.80), channel_id=1, source_target_pairs={{0,12},{1,4},{2,14},{3,6},{4,8},{5,0},{6,10},{7,2},{8,20},{9,5},{1... | collective-permute-start | bytes 208904 | tf_op jit(solution)/shard_map/ppermute | solution.py:653
  27.7 4.6 %copy-start = (f32[2,128,256]{2,1,0:T(8,128)S(1)}, f32[2,128,256]{2,1,0:T(8,128)}, u32[]{:S(2)}) copy-start(f32[2,128,256]{2,1,0:T(8,128)} %object_ref.1) | copy-start | bytes 786436
  30.9 1.5 %collective-permute-start.16 = (bf16[3,128,256]{2,1,0:T(8,128)(2,1)S(1)}, bf16[3,128,256]{2,1,0:T(8,128)(2,1)S(1)}, u32[]{:S(2)}, u32[]{:S(2)}) collective-permute-start(bf16[3,128,256]{2,1,0:T(8,128)(2,1)S(1)} %sums.1.own_ref), channel_id=1, source_target_pairs={{0,1},{1,0},{2,3},{3,2},{4,5},{5,4},{6,7},{7,6},{8,9},{9,8},{10,11... | collective-permute-start | bytes 589832 | tf_op jit(solution)/shard_map/ppermute | solution.py:519

commit v18 on v16

--- a/solution.py
+++ b/solution.py
@@ -17,7 +17,7 @@
 small_bytes = 8 * 1024 * 1024
 
 
-def dft_matrices(side):
+def dft_table(side):
     line = np.arange(side, dtype=np.int32)
     angle = (line[:, None] * line[None, :] % side).astype(np.float32) * np.float32(
         2.0 * math.pi / side
@@ -25,9 +25,7 @@
     scaling = np.float32(1.0 / math.sqrt(side))
     real = (np.cos(angle) * scaling).astype(jnp.bfloat16)
     imag = (-np.sin(angle) * scaling).astype(jnp.bfloat16)
-    direct = np.block([[real, -imag], [imag, real]])
-    swapped = np.block([[real, imag], [-imag, real]])
-    return direct, swapped
+    return np.stack([real, imag])
 
 
 def dot(left, right):
@@ -72,8 +70,7 @@
     object_hbm,
     probe_hbm,
     centers_hbm,
-    direct_hbm,
-    swapped_hbm,
+    table_hbm,
     low_ref,
     shared_ref,
     rest_ref,
@@ -85,7 +82,7 @@
     *refs,
 ):
     edges = refs[:sides]
-    object_ref, probe_ref, centers_ref, sems = refs[sides:]
+    object_ref, probe_ref, centers_ref, table_ref, sems = refs[sides:]
     copies = [
         pltpu.make_async_copy(source, target, sems.at[index])
         for index, (source, target) in enumerate(
@@ -93,8 +90,7 @@
                 (probe_hbm, probe_ref),
                 (object_hbm, object_ref),
                 (centers_hbm, centers_ref),
-                (direct_hbm, direct_ref),
-                (swapped_hbm, swapped_ref),
+                (table_hbm, table_ref),
             )
         )
     ]
@@ -129,7 +125,14 @@
             record = jnp.where(line == 2 * slot + axis, value, record)
     record_ref[...] = record.astype(jnp.bfloat16)
     copies[3].wait()
-    copies[4].wait()
+    real, imag = table_ref[0], table_ref[1]
+    side = real.shape[0]
+    first, last = slice(0, side), slice(side, 2 * side)
+    for matrix_ref, upper, lower in ((direct_ref, -imag, imag), (swapped_ref, imag, -imag)):
+        matrix_ref[first, first] = real
+        matrix_ref[first, last] = upper
+        matrix_ref[last, first] = lower
+        matrix_ref[last, last] = real
 
 
 def live_kernel(slots, record_ref, live_ref, out_ref):
@@ -518,7 +521,7 @@
     def exchange(array, flip):
         return lax.ppermute(array, "mode", [(m, m ^ flip) for m in range(m_count)])
 
-    tables = [jnp.asarray(matrix) for matrix in dft_matrices(side)]
+    table = jnp.asarray(dft_table(side))
     probe_low, shared, rest, record, spot, direct, swapped, *packed = pl.pallas_call(
         functools.partial(start_kernel, sides, slots),
         out_shape=[
@@ -532,17 +535,18 @@
             jax.ShapeDtypeStruct(object_field.shape, jnp.bfloat16),
         ]
         + [jax.ShapeDtypeStruct((2, tile_rows, half), jnp.bfloat16)] * sides,
-        in_specs=[hbm()] * 5,
+        in_specs=[hbm()] * 4,
         out_specs=[vmem()] * (8 + sides),
         scratch_shapes=[
             pltpu.VMEM(object_field.shape, jnp.float32),
             pltpu.VMEM(probe.shape, jnp.float32),
             pltpu.SMEM(centers.shape, jnp.int32),
-            pltpu.SemaphoreType.DMA((5,)),
+            pltpu.VMEM((2, side, side), jnp.bfloat16),
+            pltpu.SemaphoreType.DMA((4,)),
         ],
         compiler_params=pltpu.CompilerParams(vmem_limit_bytes=small_bytes),
         name="start",
-    )(*(in_hbm(array) for array in (object_field, probe, centers, *tables)))
+    )(*(in_hbm(array) for array in (object_field, probe, centers, table)))
     over_y = exchange(shared, 2)
     probe_core = exchange(probe_low, 1)
     rest = exchange(rest, 2)

time: 32.9 us -> 32.7 us (level)
  no operation moved by 1% of the time
where the time goes in v18:
time: 32.7 us; the launch traced here: 32.6 us
  starting transfers between devices  14.7 us (45%)
  Pallas kernels  10.7 us (33%)
  waiting for transfers between devices  6.32 us (19%)
  between operations  0.77 us (2%)
    ppermute x10, starting transfers between devices, exchange(): return lax.ppermute(array, 'mode', [(m, m ^ flip) for m in range(m_count)])  5.27 us
    pallas_call x1, Pallas kernels, on_device(): pl.pallas_call(functools.partial(back_kernel, sides, slots, tile_cols), o...  4.36 us
    ppermute x10, waiting for transfers between devices, exchange(): return lax.ppermute(array, 'mode', [(m, m ^ flip) for m in range(m_count)])  3.08 us
    ppermute x1, starting transfers between devices, on_device(): lax.ppermute(edge, axes, zigzag(step))  2.5 us
    ppermute x1, waiting for transfers between devices, on_device(): lax.ppermute(piece, axes, zigzag(-step))  1.85 us
    ppermute x1, starting transfers between devices, on_device(): lax.ppermute(piece, axes, zigzag(-step))  1.65 us
    ppermute x1, starting transfers between devices, on_device(): over_z = lax.ppermute(over_y, 'tx', [(z, z ^ 1) for z in range(z_count)])  1.64 us
    ppermute x1, starting transfers between devices, on_device(): rows = lax.ppermute(packed[0], axes, zigzag(0))  1.58 us
  transfers between devices with their start and end apart: 17, of which 8 were waited for; matrix products, arithmetic and copies ran while one was open for 0% of the time, Pallas kernels for 11%

profile of v18, /device:TPU:0, one launch (start us, length us, event | category | flops | bytes accessed | tf_op | source)
XLA Modules:
  0.0 32.6 jit_solution(4313033410593101565)
XLA Ops:
  0.0 1.4 %start.1 = (bf16[2,2,256,256]{3,2,1,0:T(8,128)(2,1)S(1)}, bf16[256,256]{1,0:T(8,128)(2,1)S(1)}, bf16[2,1,256,256]{3,2,1,0:T(8,128)(2,1)S(1)}, bf16[16,256]{1,0:T...) custom-call(f32[2,128,256]{2,1,0:T(8,128)} %object_ref.1, ...), custom_call_target="tpu_custom_call" | custom-call | tf_op jit(solution)/shard_map/start/pallas_call | solution.py:525
  1.5 0.5 %collective-permute-start = (bf16[2,2,256,256]{3,2,1,0:T(8,128)(2,1)S(1)}, bf16[2,2,256,256]{3,2,1,0:T(8,128)(2,1)S(1)}, u32[]{:S(2)}, u32[]{:S(2)}) collective-permute-start(bf16[2,2,256,256]{3,2,1,0:T(8,128)(2,1)S(1)} %get-tuple-element.43.refs_6_.refs_2_), channel_id=1, source_target_pairs={{0,1},{1,0},{2,3},{3,2},{4,5},{5,4},{6,7},{7,6},{8,9},{9,8},{10,11... | collective-permute-start | bytes 1572872 | tf_op jit(solution)/shard_map/ppermute | solution.py:522
  2.0 2.6 %collective-permute-start.7 = (bf16[256,256]{1,0:T(8,128)(2,1)S(1)}, bf16[256,256]{1,0:T(8,128)(2,1)S(1)}, u32[]{:S(2)}, u32[]{:S(2)}) collective-permute-start(bf16[256,256]{1,0:T(8,128)(2,1)S(1)} %get-tuple-element.59), channel_id=1, source_target_pairs={{0,2},{1,3},{2,0},{3,1},{4,6},{5,7},{6,4},{7,5},{8,10},{9,11},{10,... | collective-permute-start | bytes 393224 | tf_op jit(solution)/shard_map/ppermute | solution.py:522
  4.6 1.6 %collective-permute-start.4 = (bf16[2,128,256]{2,1,0:T(8,128)(2,1)S(1)}, bf16[2,128,256]{2,1,0:T(8,128)(2,1)S(1)}, u32[]{:S(2)}, u32[]{:S(2)}) collective-permute-start(bf16[2,128,256]{2,1,0:T(8,128)(2,1)S(1)} %get-tuple-element.52.refs_0_), channel_id=1, source_target_pairs={{0,8},{1,0},{2,10},{3,2},{4,12},{5,4},{6,14},{7,6},{8,16},{9,1},{1... | collective-permute-start | bytes 393224 | tf_op jit(solution)/shard_map/ppermute | solution.py:555
  6.1 2.5 %collective-permute-start.1 = (bf16[2,128,128]{2,1,0:T(8,128)(2,1)S(1)}, bf16[2,128,128]{2,1,0:T(8,128)(2,1)S(1)}, u32[]{:S(2)}, u32[]{:S(2)}) collective-permute-start(bf16[2,128,128]{2,1,0:T(8,128)(2,1)S(1)} %get-tuple-element.45), channel_id=1, source_target_pairs={{0,12},{1,4},{2,14},{3,6},{4,8},{5,0},{6,10},{7,2},{8,20},{9,5},{1... | collective-permute-start | bytes 196616 | tf_op jit(solution)/shard_map/ppermute | solution.py:557
  8.7 0.5 %collective-permute-start.2 = (bf16[2,1,256,256]{3,2,1,0:T(8,128)(2,1)S(1)}, bf16[2,1,256,256]{3,2,1,0:T(8,128)(2,1)S(1)}, u32[]{:S(2)}, u32[]{:S(2)}) collective-permute-start(bf16[2,1,256,256]{3,2,1,0:T(8,128)(2,1)S(1)} %get-tuple-element.51), channel_id=1, source_target_pairs={{0,2},{1,3},{2,0},{3,1},{4,6},{5,7},{6,4},{7,5},{8,10},{9,11},{10,... | collective-permute-start | bytes 786440 | tf_op jit(solution)/shard_map/ppermute | solution.py:522
  9.2 0.5 %collective-permute-start.6 = (bf16[2,128,128]{2,1,0:T(8,128)(2,1)S(1)}, bf16[2,128,128]{2,1,0:T(8,128)(2,1)S(1)}, u32[]{:S(2)}, u32[]{:S(2)}) collective-permute-start(bf16[2,128,128]{2,1,0:T(8,128)(2,1)S(1)} %get-tuple-element.45), channel_id=1, source_target_pairs={{0,4},{4,0},{1,5},{5,1},{2,6},{6,2},{3,7},{7,3},{8,12},{12,8},{9,1... | collective-permute-start | bytes 196616 | tf_op jit(solution)/shard_map/ppermute | solution.py:558
  10.4 1.6 %collective-permute-start.8 = (bf16[256,256]{1,0:T(8,128)(2,1)S(1)}, bf16[256,256]{1,0:T(8,128)(2,1)S(1)}, u32[]{:S(2)}, u32[]{:S(2)}) collective-permute-start(bf16[256,256]{1,0:T(8,128)(2,1)S(1)} %collective-permute-done.7.over_y.refs_4_), channel_id=1, source_target_pairs={{0,8},{8,0},{16,24},{24,16},{1,9},{9,1},{17,25},{25,17},{2,10},{10... | collective-permute-start | bytes 393224 | tf_op jit(solution)/shard_map/ppermute | solution.py:553
  12.0 0.6 %collective-permute-start.3 = (bf16[2,128,128]{2,1,0:T(8,128)(2,1)S(1)}, bf16[2,128,128]{2,1,0:T(8,128)(2,1)S(1)}, u32[]{:S(2)}, u32[]{:S(2)}) collective-permute-start(bf16[2,128,128]{2,1,0:T(8,128)(2,1)S(1)} %collective-permute-done.1.refs_1_), channel_id=1, source_target_pairs={{0,1},{1,0},{2,3},{3,2},{4,5},{5,4},{6,7},{7,6},{8,9},{9,8},{10,11... | collective-permute-start | bytes 196616 | tf_op jit(solution)/shard_map/ppermute | solution.py:522
  12.6 0.8 %collective-permute-done.6.refs_5_ = bf16[2,128,128]{2,1,0:T(8,128)(2,1)S(1)} collective-permute-done((bf16[2,128,128]{2,1,0:T(8,128)(2,1)S(1)}, bf16[2,128,128]{2,1,0:T(8,128)(2,1)S(1)}, u32[]{:S(2)}, u32[]{:S(2)}) %collective-permute-start.6) | collective-permute-done | bytes 65568 | tf_op jit(solution)/shard_map/ppermute | solution.py:558
  13.4 0.1 collective-permute-done.3.refs_2_
  13.5 1.5 %near.1 = (f32[2,256,256]{2,1,0:T(8,128)S(1)}, f32[2,256,512]{2,1,0:T(8,128)S(1)}, bf16[2,512,256]{2,1,0:T(8,128)(2,1)S(1)}, f32[2,256,256]{2,1,0:T(8,128)S(1)}) custom-call(s32[8,128]{1,0:T(8,128)S(1)} %get-tuple-element.50.spot_ref, bf16[2,128,256]{2,1,0:T(8,128)(2,1)S(1)} %get-tuple-element.52.refs_0_, ...), custom_call_target="tpu_custom_call" | custom-call | flops 33554432 | tf_op jit(solution)/shard_map/near/pallas_call | solution.py:581
  15.0 1.0 %collective-permute-done.2.rest.refs_6_ = bf16[2,1,256,256]{3,2,1,0:T(8,128)(2,1)S(1)} collective-permute-done((bf16[2,1,256,256]{3,2,1,0:T(8,128)(2,1)S(1)}, bf16[2,1,256,256]{3,2,1,0:T(8,128)(2,1)S(1)}, u32[]{:S(2)}, u32[]{:S(2)}) %collective-permute-start.2) | collective-permute-done | bytes 262176 | tf_op jit(solution)/shard_map/ppermute | solution.py:522
  16.0 0.9 %core.1 = (f32[2,256,512]{2,1,0:T(8,128)S(1)}, bf16[2,512,256]{2,1,0:T(8,128)(2,1)S(1)}, f32[2,256,256]{2,1,0:T(8,128)S(1)}) custom-call(f32[2,256,256]{2,1,0:T(8,128)S(1)} %get-tuple-element.57.patch_ref.refs_1_, bf16[2,2,256,256]{3,2,1,0:T(8,128)(2,1)S(1)} %collective-permute-done.core.refs_3_, ...), custom_call_target="tpu_custom_call" | custom-call | flops 33554432 | tf_op jit(solution)/shard_map/core/pallas_call | solution.py:591
  16.8 0.0 copy-start.1
  16.8 0.6 %collective-permute-start.10 = (bf16[256,256]{1,0:T(8,128)(2,1)S(1)}, bf16[256,256]{1,0:T(8,128)(2,1)S(1)}, u32[]{:S(2)}, u32[]{:S(2)}) collective-permute-start(bf16[256,256]{1,0:T(8,128)(2,1)S(1)} %collective-permute-done.8.over_z.refs_5_), channel_id=1, source_target_pairs={{0,1},{1,0},{2,3},{3,2},{4,5},{5,4},{6,7},{7,6},{8,9},{9,8},{10,11... | collective-permute-start | bytes 393224 | tf_op jit(solution)/shard_map/ppermute | solution.py:522
  17.4 0.9 %over.1 = (f32[2,256,512]{2,1,0:T(8,128)S(1)}, bf16[2,512,256]{2,1,0:T(8,128)(2,1)S(1)}, f32[2,256,256]{2,1,0:T(8,128)S(1)}) custom-call(f32[2,256,256]{2,1,0:T(8,128)S(1)} %get-tuple-element.57.patch_ref.refs_1_, bf16[256,256]{1,0:T(8,128)(2,1)S(1)} %collective-permute-done.7.over_y.refs_4_, bf16[256,256]{1,0:T(8,128)(2,1)S(1)} %collective-permute-done.8.over_z.refs_5_, ...), custom_call_target="tpu_custom_call" | custom-call | flops 3355443200 | tf_op jit(solution)/shard_map/over/pallas_call | solution.py:604
  18.3 0.1 collective-permute-done.10.refs_8_
  18.4 4.4 %back.1 = (bf16[256,256]{1,0:T(8,128)(2,1)S(1)}, bf16[256,256]{1,0:T(8,128)(2,1)S(1)}, bf16[256,384]{1,0:T(8,128)(2,1)S(1)}, bf16[256,384]{1,0:T(8,128)(2,1)S(1)}, bf16[272,128]{1,0:T(8,128)(2,1)S(1)}) custom-call(bf16[16,256]{1,0:T(8,128)(2,1)S(1)} %live.1.record_ref, s32[8,128]{1,0:T(8,128)S(1)} %get-tuple-element.50.spot_ref, ...), custom_call_target="tpu_custom_call" | custom-call | flops 2684354560 | tf_op jit(solution)/shard_map/back/pallas_call | solution.py:616
  22.8 0.4 %collective-permute-start.13 = (bf16[256,384]{1,0:T(8,128)(2,1)S(1)}, bf16[256,384]{1,0:T(8,128)(2,1)S(1)}, u32[]{:S(2)}, u32[]{:S(2)}) collective-permute-start(bf16[256,384]{1,0:T(8,128)(2,1)S(1)} %get-tuple-element.78), channel_id=1, source_target_pairs={{0,1},{1,0},{2,3},{3,2},{4,5},{5,4},{6,7},{7,6},{8,9},{9,8},{10,11... | collective-permute-start | bytes 589832 | tf_op jit(solution)/shard_map/ppermute | solution.py:522
  23.2 0.6 %collective-permute-start.12 = (bf16[272,128]{1,0:T(8,128)(2,1)S(1)}, bf16[272,128]{1,0:T(8,128)(2,1)S(1)}, u32[]{:S(2)}, u32[]{:S(2)}) collective-permute-start(bf16[272,128]{1,0:T(8,128)(2,1)S(1)} %get-tuple-element.76), channel_id=1, source_target_pairs={{0,4},{4,0},{1,5},{5,1},{2,6},{6,2},{3,7},{7,3},{8,12},{12,8},{9,1... | collective-permute-start | bytes 208904 | tf_op jit(solution)/shard_map/ppermute | solution.py:643
  23.8 0.5 %collective-permute-done.13.swap_ref = bf16[256,384]{1,0:T(8,128)(2,1)S(1)} collective-permute-done((bf16[256,384]{1,0:T(8,128)(2,1)S(1)}, bf16[256,384]{1,0:T(8,128)(2,1)S(1)}, u32[]{:S(2)}, u32[]{:S(2)}) %collective-permute-start.13) | collective-permute-done | bytes 196640 | tf_op jit(solution)/shard_map/ppermute | solution.py:522
  24.3 0.1 meet.1
  24.3 1.0 %collective-permute-start.14 = (bf16[272,256]{1,0:T(8,128)(2,1)S(1)}, bf16[272,256]{1,0:T(8,128)(2,1)S(1)}, u32[]{:S(2)}, u32[]{:S(2)}) collective-permute-start(bf16[272,256]{1,0:T(8,128)(2,1)S(1)} %get-tuple-element.79), channel_id=1, source_target_pairs={{0,8},{1,0},{2,10},{3,2},{4,12},{5,4},{6,14},{7,6},{8,16},{9,1},{1... | collective-permute-start | bytes 417800 | tf_op jit(solution)/shard_map/ppermute | solution.py:655
  25.3 1.7 %collective-permute-start.15 = (bf16[272,128]{1,0:T(8,128)(2,1)S(1)}, bf16[272,128]{1,0:T(8,128)(2,1)S(1)}, u32[]{:S(2)}, u32[]{:S(2)}) collective-permute-start(bf16[272,128]{1,0:T(8,128)(2,1)S(1)} %get-tuple-element.80), channel_id=1, source_target_pairs={{0,12},{1,4},{2,14},{3,6},{4,8},{5,0},{6,10},{7,2},{8,20},{9,5},{1... | collective-permute-start | bytes 208904 | tf_op jit(solution)/shard_map/ppermute | solution.py:657
  27.0 0.5 %collective-permute-done.12.refs_0_ = bf16[272,128]{1,0:T(8,128)(2,1)S(1)} collective-permute-done((bf16[272,128]{1,0:T(8,128)(2,1)S(1)}, bf16[272,128]{1,0:T(8,128)(2,1)S(1)}, u32[]{:S(2)}, u32[]{:S(2)}) %collective-permute-start.12) | collective-permute-done | bytes 69664 | tf_op jit(solution)/shard_map/ppermute | solution.py:643
  27.5 0.4 %levels.1.level_ref = f32[3,128,256]{2,1,0:T(8,128)S(1)} custom-call(bf16[256,256]{1,0:T(8,128)(2,1)S(1)} %get-tuple-element.74.weight_ref, bf16[16,256]{1,0:T(8,128)(2,1)S(1)} %live.1.record_ref, bf16[256,256]{1,0:T(8,128)(2,1)S(1)} %get-tuple-element.75.own_ref, bf16[272,128]{1,0:T(8,128)(2,1)S(1)} %collective-permute-done.12.refs_0_), custom_call_target="tpu_custom_call" | custom-call | flops 1342177280 | tf_op jit(solution)/shard_map/levels/pallas_call | solution.py:659
  28.0 1.9 %collective-permute-done.15.refs_0_ = bf16[272,128]{1,0:T(8,128)(2,1)S(1)} collective-permute-done((bf16[272,128]{1,0:T(8,128)(2,1)S(1)}, bf16[272,128]{1,0:T(8,128)(2,1)S(1)}, u32[]{:S(2)}, u32[]{:S(2)}) %collective-permute-start.15) | collective-permute-done | bytes 69664 | tf_op jit(solution)/shard_map/ppermute | solution.py:657
  29.8 0.5 %sums.1.own_ref = bf16[3,128,256]{2,1,0:T(8,128)(2,1)S(1)} custom-call(bf16[256,256]{1,0:T(8,128)(2,1)S(1)} %get-tuple-element.74.weight_ref, f32[3,128,256]{2,1,0:T(8,128)S(1)} %levels.1.level_ref, bf16[272,256]{1,0:T(8,128)(2,1)S(1)} %collective-permute-done.14.rows_ref, bf16[272,128]{1,0:T(8,128)(2,1)S(1)} %collective-permute-done.15.refs_0_), custom_call_target="tpu_custom_call" | custom-call | tf_op jit(solution)/shard_map/sums/pallas_call | solution.py:668
  30.3 0.1 collective-permute-start.16
  30.4 1.4 %collective-permute-done.16.other_ref = bf16[3,128,256]{2,1,0:T(8,128)(2,1)S(1)} collective-permute-done((bf16[3,128,256]{2,1,0:T(8,128)(2,1)S(1)}, bf16[3,128,256]{2,1,0:T(8,128)(2,1)S(1)}, u32[]{:S(2)}, u32[]{:S(2)}) %collective-permute-start.16) | collective-permute-done | bytes 196640 | tf_op jit(solution)/shard_map/ppermute | solution.py:522
  31.8 0.8 %update.1 = f32[2,128,256]{2,1,0:T(8,128)} custom-call(f32[2,128,256]{2,1,0:T(8,128)S(1)} %copy-done, bf16[3,128,256]{2,1,0:T(8,128)(2,1)S(1)} %sums.1.own_ref, bf16[3,128,256]{2,1,0:T(8,128)(2,1)S(1)} %collective-permute-done.16.other_ref), custom_call_target="tpu_custom_call" | custom-call | tf_op jit(solution)/shard_map/update/pallas_call | solution.py:676
  (16 shorter events, 0.0 us)
Async XLA Ops:
  1.5 4.7 %collective-permute-start = (bf16[2,2,256,256]{3,2,1,0:T(8,128)(2,1)S(1)}, bf16[2,2,256,256]{3,2,1,0:T(8,128)(2,1)S(1)}, u32[]{:S(2)}, u32[]{:S(2)}) collective-permute-start(bf16[2,2,256,256]{3,2,1,0:T(8,128)(2,1)S(1)} %get-tuple-element.43.refs_6_.refs_2_), channel_id=1, source_target_pairs={{0,1},{1,0},{2,3},{3,2},{4,5},{5,4},{6,7},{7,6},{8,9},{9,8},{10,11... | collective-permute-start | bytes 1572872 | tf_op jit(solution)/shard_map/ppermute | solution.py:522
  2.0 8.4 %collective-permute-start.7 = (bf16[256,256]{1,0:T(8,128)(2,1)S(1)}, bf16[256,256]{1,0:T(8,128)(2,1)S(1)}, u32[]{:S(2)}, u32[]{:S(2)}) collective-permute-start(bf16[256,256]{1,0:T(8,128)(2,1)S(1)} %get-tuple-element.59), channel_id=1, source_target_pairs={{0,2},{1,3},{2,0},{3,1},{4,6},{5,7},{6,4},{7,5},{8,10},{9,11},{10,... | collective-permute-start | bytes 393224 | tf_op jit(solution)/shard_map/ppermute | solution.py:522
  4.6 7.4 %collective-permute-start.4 = (bf16[2,128,256]{2,1,0:T(8,128)(2,1)S(1)}, bf16[2,128,256]{2,1,0:T(8,128)(2,1)S(1)}, u32[]{:S(2)}, u32[]{:S(2)}) collective-permute-start(bf16[2,128,256]{2,1,0:T(8,128)(2,1)S(1)} %get-tuple-element.52.refs_0_), channel_id=1, source_target_pairs={{0,8},{1,0},{2,10},{3,2},{4,12},{5,4},{6,14},{7,6},{8,16},{9,1},{1... | collective-permute-start | bytes 393224 | tf_op jit(solution)/shard_map/ppermute | solution.py:555
  6.1 5.9 %collective-permute-start.1 = (bf16[2,128,128]{2,1,0:T(8,128)(2,1)S(1)}, bf16[2,128,128]{2,1,0:T(8,128)(2,1)S(1)}, u32[]{:S(2)}, u32[]{:S(2)}) collective-permute-start(bf16[2,128,128]{2,1,0:T(8,128)(2,1)S(1)} %get-tuple-element.45), channel_id=1, source_target_pairs={{0,12},{1,4},{2,14},{3,6},{4,8},{5,0},{6,10},{7,2},{8,20},{9,5},{1... | collective-permute-start | bytes 196616 | tf_op jit(solution)/shard_map/ppermute | solution.py:557
  8.7 7.3 %collective-permute-start.2 = (bf16[2,1,256,256]{3,2,1,0:T(8,128)(2,1)S(1)}, bf16[2,1,256,256]{3,2,1,0:T(8,128)(2,1)S(1)}, u32[]{:S(2)}, u32[]{:S(2)}) collective-permute-start(bf16[2,1,256,256]{3,2,1,0:T(8,128)(2,1)S(1)} %get-tuple-element.51), channel_id=1, source_target_pairs={{0,2},{1,3},{2,0},{3,1},{4,6},{5,7},{6,4},{7,5},{8,10},{9,11},{10,... | collective-permute-start | bytes 786440 | tf_op jit(solution)/shard_map/ppermute | solution.py:522
  9.2 4.3 %collective-permute-start.6 = (bf16[2,128,128]{2,1,0:T(8,128)(2,1)S(1)}, bf16[2,128,128]{2,1,0:T(8,128)(2,1)S(1)}, u32[]{:S(2)}, u32[]{:S(2)}) collective-permute-start(bf16[2,128,128]{2,1,0:T(8,128)(2,1)S(1)} %get-tuple-element.45), channel_id=1, source_target_pairs={{0,4},{4,0},{1,5},{5,1},{2,6},{6,2},{3,7},{7,3},{8,12},{12,8},{9,1... | collective-permute-start | bytes 196616 | tf_op jit(solution)/shard_map/ppermute | solution.py:558
  10.4 6.5 %collective-permute-start.8 = (bf16[256,256]{1,0:T(8,128)(2,1)S(1)}, bf16[256,256]{1,0:T(8,128)(2,1)S(1)}, u32[]{:S(2)}, u32[]{:S(2)}) collective-permute-start(bf16[256,256]{1,0:T(8,128)(2,1)S(1)} %collective-permute-done.7.over_y.refs_4_), channel_id=1, source_target_pairs={{0,8},{8,0},{16,24},{24,16},{1,9},{9,1},{17,25},{25,17},{2,10},{10... | collective-permute-start | bytes 393224 | tf_op jit(solution)/shard_map/ppermute | solution.py:553
  12.0 1.4 %collective-permute-start.5 = (bf16[2,128,256]{2,1,0:T(8,128)(2,1)S(1)}, bf16[2,128,256]{2,1,0:T(8,128)(2,1)S(1)}, u32[]{:S(2)}, u32[]{:S(2)}) collective-permute-start(bf16[2,128,256]{2,1,0:T(8,128)(2,1)S(1)} %collective-permute-done.4.refs_3_), channel_id=1, source_target_pairs={{0,1},{1,0},{2,3},{3,2},{4,5},{5,4},{6,7},{7,6},{8,9},{9,8},{10,11... | collective-permute-start | bytes 393224 | tf_op jit(solution)/shard_map/ppermute | solution.py:522
  12.0 1.5 %collective-permute-start.3 = (bf16[2,128,128]{2,1,0:T(8,128)(2,1)S(1)}, bf16[2,128,128]{2,1,0:T(8,128)(2,1)S(1)}, u32[]{:S(2)}, u32[]{:S(2)}) collective-permute-start(bf16[2,128,128]{2,1,0:T(8,128)(2,1)S(1)} %collective-permute-done.1.refs_1_), channel_id=1, source_target_pairs={{0,1},{1,0},{2,3},{3,2},{4,5},{5,4},{6,7},{7,6},{8,9},{9,8},{10,11... | collective-permute-start | bytes 196616 | tf_op jit(solution)/shard_map/ppermute | solution.py:522
  13.4 4.9 %collective-permute-start.9 = (bf16[256,256]{1,0:T(8,128)(2,1)S(1)}, bf16[256,256]{1,0:T(8,128)(2,1)S(1)}, u32[]{:S(2)}, u32[]{:S(2)}) collective-permute-start(bf16[256,256]{1,0:T(8,128)(2,1)S(1)} %collective-permute-done.7.over_y.refs_4_), channel_id=1, source_target_pairs={{0,1},{1,0},{2,3},{3,2},{4,5},{5,4},{6,7},{7,6},{8,9},{9,8},{10,11... | collective-permute-start | bytes 393224 | tf_op jit(solution)/shard_map/ppermute | solution.py:522
  16.0 2.5 %collective-permute-start.11 = (bf16[2,1,256,256]{3,2,1,0:T(8,128)(2,1)S(1)}, bf16[2,1,256,256]{3,2,1,0:T(8,128)(2,1)S(1)}, u32[]{:S(2)}, u32[]{:S(2)}) collective-permute-start(bf16[2,1,256,256]{3,2,1,0:T(8,128)(2,1)S(1)} %collective-permute-done.2.rest.refs_6_), channel_id=1, source_target_pairs={{0,1},{1,0},{2,3},{3,2},{4,5},{5,4},{6,7},{7,6},{8,9},{9,8},{10,11... | collective-permute-start | bytes 786440 | tf_op jit(solution)/shard_map/ppermute | solution.py:522
  16.8 1.6 %copy-start.1 = (bf16[1,1,2,256,256]{4,3,2,1,0:T(8,128)(2,1)S(1)}, bf16[1,1,2,256,256]{4,3,2,1,0:T(8,128)(2,1)}, u32[]{:S(2)}) copy-start(bf16[1,1,2,256,256]{4,3,2,1,0:T(8,128)(2,1)} %refs_0_.1) | copy-start | bytes 786436
  16.8 1.6 %collective-permute-start.10 = (bf16[256,256]{1,0:T(8,128)(2,1)S(1)}, bf16[256,256]{1,0:T(8,128)(2,1)S(1)}, u32[]{:S(2)}, u32[]{:S(2)}) collective-permute-start(bf16[256,256]{1,0:T(8,128)(2,1)S(1)} %collective-permute-done.8.over_z.refs_5_), channel_id=1, source_target_pairs={{0,1},{1,0},{2,3},{3,2},{4,5},{5,4},{6,7},{7,6},{8,9},{9,8},{10,11... | collective-permute-start | bytes 393224 | tf_op jit(solution)/shard_map/ppermute | solution.py:522
  22.8 1.5 %collective-permute-start.13 = (bf16[256,384]{1,0:T(8,128)(2,1)S(1)}, bf16[256,384]{1,0:T(8,128)(2,1)S(1)}, u32[]{:S(2)}, u32[]{:S(2)}) collective-permute-start(bf16[256,384]{1,0:T(8,128)(2,1)S(1)} %get-tuple-element.78), channel_id=1, source_target_pairs={{0,1},{1,0},{2,3},{3,2},{4,5},{5,4},{6,7},{7,6},{8,9},{9,8},{10,11... | collective-permute-start | bytes 589832 | tf_op jit(solution)/shard_map/ppermute | solution.py:522
  23.2 4.3 %collective-permute-start.12 = (bf16[272,128]{1,0:T(8,128)(2,1)S(1)}, bf16[272,128]{1,0:T(8,128)(2,1)S(1)}, u32[]{:S(2)}, u32[]{:S(2)}) collective-permute-start(bf16[272,128]{1,0:T(8,128)(2,1)S(1)} %get-tuple-element.76), channel_id=1, source_target_pairs={{0,4},{4,0},{1,5},{5,1},{2,6},{6,2},{3,7},{7,3},{8,12},{12,8},{9,1... | collective-permute-start | bytes 208904 | tf_op jit(solution)/shard_map/ppermute | solution.py:643
  24.3 5.5 %collective-permute-start.14 = (bf16[272,256]{1,0:T(8,128)(2,1)S(1)}, bf16[272,256]{1,0:T(8,128)(2,1)S(1)}, u32[]{:S(2)}, u32[]{:S(2)}) collective-permute-start(bf16[272,256]{1,0:T(8,128)(2,1)S(1)} %get-tuple-element.79), channel_id=1, source_target_pairs={{0,8},{1,0},{2,10},{3,2},{4,12},{5,4},{6,14},{7,6},{8,16},{9,1},{1... | collective-permute-start | bytes 417800 | tf_op jit(solution)/shard_map/ppermute | solution.py:655
  25.3 4.5 %collective-permute-start.15 = (bf16[272,128]{1,0:T(8,128)(2,1)S(1)}, bf16[272,128]{1,0:T(8,128)(2,1)S(1)}, u32[]{:S(2)}, u32[]{:S(2)}) collective-permute-start(bf16[272,128]{1,0:T(8,128)(2,1)S(1)} %get-tuple-element.80), channel_id=1, source_target_pairs={{0,12},{1,4},{2,14},{3,6},{4,8},{5,0},{6,10},{7,2},{8,20},{9,5},{1... | collective-permute-start | bytes 208904 | tf_op jit(solution)/shard_map/ppermute | solution.py:657
  27.9 3.8 %copy-start = (f32[2,128,256]{2,1,0:T(8,128)S(1)}, f32[2,128,256]{2,1,0:T(8,128)}, u32[]{:S(2)}) copy-start(f32[2,128,256]{2,1,0:T(8,128)} %object_ref.1) | copy-start | bytes 786436
  30.3 1.5 %collective-permute-start.16 = (bf16[3,128,256]{2,1,0:T(8,128)(2,1)S(1)}, bf16[3,128,256]{2,1,0:T(8,128)(2,1)S(1)}, u32[]{:S(2)}, u32[]{:S(2)}) collective-permute-start(bf16[3,128,256]{2,1,0:T(8,128)(2,1)S(1)} %sums.1.own_ref), channel_id=1, source_target_pairs={{0,1},{1,0},{2,3},{3,2},{4,5},{5,4},{6,7},{7,6},{8,9},{9,8},{10,11... | collective-permute-start | bytes 589832 | tf_op jit(solution)/shard_map/ppermute | solution.py:522

commit v19 on v18

--- a/solution.py
+++ b/solution.py
@@ -563,7 +563,7 @@
         in_specs=[vmem(), smem()],
         out_specs=vmem(),
         compiler_params=pltpu.CompilerParams(vmem_limit_bytes=small_bytes),
-        cost_estimate=cost(50),
+        cost_estimate=cost(20),
         name="live",
     )(record, live)
     corners, record = lax.optimization_barrier((corners, record))

time: 32.7 us -> 32.4 us (level)
  waiting for transfers between devices: 6.32 us -> 4.8 us
  starting transfers between devices: 14.7 us -> 16 us
    ppermute x10, starting transfers between devices: 5.27 us -> 3.85 us  [exchange(): return lax.ppermute(array, 'mode', [(m, m ^ flip) for m in range(m_count)])]
    ppermute x1, starting transfers between devices: 0.57 us -> 1.61 us  [on_device(): lax.ppermute(piece, 'ty', level(-step))]
    ppermute x1, starting transfers between devices: 1.58 us -> 2.6 us  [on_device(): rows = lax.ppermute(packed[0], axes, zigzag(0))]
    ppermute x10, waiting for transfers between devices: 3.08 us -> 2.22 us  [exchange(): return lax.ppermute(array, 'mode', [(m, m ^ flip) for m in range(m_count)])]
    ppermute x1, waiting for transfers between devices: 0.55 us -> 0.01 us  [on_device(): lax.ppermute(piece, 'ty', level(-step))]
    ppermute x1, starting transfers between devices: 1.65 us -> 2.06 us  [on_device(): lax.ppermute(piece, axes, zigzag(-step))]
    ppermute x1, waiting for transfers between devices: 1.85 us -> 1.51 us  [on_device(): lax.ppermute(piece, axes, zigzag(-step))]
  transfers between devices with their start and end apart: 17 -> 17, of which waited for: 8 -> 6; matrix products, arithmetic and copies ran while one was open for 0% -> 0% of each run, Pallas kernels for 11% -> 11%
where the time goes in v19:
time: 32.4 us; the launch traced here: 32.3 us
  starting transfers between devices  16 us (49%)
  Pallas kernels  10.7 us (33%)
  waiting for transfers between devices  4.8 us (15%)
  between operations  0.77 us (2%)
    pallas_call x1, Pallas kernels, on_device(): pl.pallas_call(functools.partial(back_kernel, sides, slots, tile_cols), o...  4.36 us
    ppermute x10, starting transfers between devices, exchange(): return lax.ppermute(array, 'mode', [(m, m ^ flip) for m in range(m_count)])  3.85 us
    ppermute x1, starting transfers between devices, on_device(): rows = lax.ppermute(packed[0], axes, zigzag(0))  2.6 us
    ppermute x1, starting transfers between devices, on_device(): lax.ppermute(edge, axes, zigzag(step))  2.5 us
    ppermute x10, waiting for transfers between devices, exchange(): return lax.ppermute(array, 'mode', [(m, m ^ flip) for m in range(m_count)])  2.22 us
    ppermute x1, starting transfers between devices, on_device(): lax.ppermute(piece, axes, zigzag(-step))  2.06 us
    ppermute x1, starting transfers between devices, on_device(): lax.ppermute(piece, 'ty', level(-step))  1.61 us
    ppermute x1, starting transfers between devices, on_device(): over_z = lax.ppermute(over_y, 'tx', [(z, z ^ 1) for z in range(z_count)])  1.56 us
  transfers between devices with their start and end apart: 17, of which 6 were waited for; matrix products, arithmetic and copies ran while one was open for 0% of the time, Pallas kernels for 11%

profile of v19, /device:TPU:0, one launch (start us, length us, event | category | flops | bytes accessed | tf_op | source)
XLA Modules:
  0.0 32.3 jit_solution(4444201545404084533)
XLA Ops:
  0.0 1.4 %start.1 = (bf16[2,2,256,256]{3,2,1,0:T(8,128)(2,1)S(1)}, bf16[256,256]{1,0:T(8,128)(2,1)S(1)}, bf16[2,1,256,256]{3,2,1,0:T(8,128)(2,1)S(1)}, bf16[16,256]{1,0:T...) custom-call(f32[2,128,256]{2,1,0:T(8,128)} %object_ref.1, ...), custom_call_target="tpu_custom_call" | custom-call | tf_op jit(solution)/shard_map/start/pallas_call | solution.py:525
  1.5 0.5 %collective-permute-start = (bf16[2,2,256,256]{3,2,1,0:T(8,128)(2,1)S(1)}, bf16[2,2,256,256]{3,2,1,0:T(8,128)(2,1)S(1)}, u32[]{:S(2)}, u32[]{:S(2)}) collective-permute-start(bf16[2,2,256,256]{3,2,1,0:T(8,128)(2,1)S(1)} %get-tuple-element.43.refs_6_.refs_2_), channel_id=1, source_target_pairs={{0,1},{1,0},{2,3},{3,2},{4,5},{5,4},{6,7},{7,6},{8,9},{9,8},{10,11... | collective-permute-start | bytes 1572872 | tf_op jit(solution)/shard_map/ppermute | solution.py:522
  2.0 2.6 %collective-permute-start.4 = (bf16[2,128,256]{2,1,0:T(8,128)(2,1)S(1)}, bf16[2,128,256]{2,1,0:T(8,128)(2,1)S(1)}, u32[]{:S(2)}, u32[]{:S(2)}) collective-permute-start(bf16[2,128,256]{2,1,0:T(8,128)(2,1)S(1)} %get-tuple-element.52.refs_0_), channel_id=1, source_target_pairs={{0,8},{1,0},{2,10},{3,2},{4,12},{5,4},{6,14},{7,6},{8,16},{9,1},{1... | collective-permute-start | bytes 393224 | tf_op jit(solution)/shard_map/ppermute | solution.py:555
  4.6 1.5 %collective-permute-start.7 = (bf16[256,256]{1,0:T(8,128)(2,1)S(1)}, bf16[256,256]{1,0:T(8,128)(2,1)S(1)}, u32[]{:S(2)}, u32[]{:S(2)}) collective-permute-start(bf16[256,256]{1,0:T(8,128)(2,1)S(1)} %get-tuple-element.59), channel_id=1, source_target_pairs={{0,2},{1,3},{2,0},{3,1},{4,6},{5,7},{6,4},{7,5},{8,10},{9,11},{10,... | collective-permute-start | bytes 393224 | tf_op jit(solution)/shard_map/ppermute | solution.py:522
  6.1 0.5 %collective-permute-start.2 = (bf16[2,1,256,256]{3,2,1,0:T(8,128)(2,1)S(1)}, bf16[2,1,256,256]{3,2,1,0:T(8,128)(2,1)S(1)}, u32[]{:S(2)}, u32[]{:S(2)}) collective-permute-start(bf16[2,1,256,256]{3,2,1,0:T(8,128)(2,1)S(1)} %get-tuple-element.51), channel_id=1, source_target_pairs={{0,2},{1,3},{2,0},{3,1},{4,6},{5,7},{6,4},{7,5},{8,10},{9,11},{10,... | collective-permute-start | bytes 786440 | tf_op jit(solution)/shard_map/ppermute | solution.py:522
  6.6 2.5 %collective-permute-start.1 = (bf16[2,128,128]{2,1,0:T(8,128)(2,1)S(1)}, bf16[2,128,128]{2,1,0:T(8,128)(2,1)S(1)}, u32[]{:S(2)}, u32[]{:S(2)}) collective-permute-start(bf16[2,128,128]{2,1,0:T(8,128)(2,1)S(1)} %get-tuple-element.45), channel_id=1, source_target_pairs={{0,12},{1,4},{2,14},{3,6},{4,8},{5,0},{6,10},{7,2},{8,20},{9,5},{1... | collective-permute-start | bytes 196616 | tf_op jit(solution)/shard_map/ppermute | solution.py:557
  9.1 0.5 %collective-permute-start.6 = (bf16[2,128,128]{2,1,0:T(8,128)(2,1)S(1)}, bf16[2,128,128]{2,1,0:T(8,128)(2,1)S(1)}, u32[]{:S(2)}, u32[]{:S(2)}) collective-permute-start(bf16[2,128,128]{2,1,0:T(8,128)(2,1)S(1)} %get-tuple-element.45), channel_id=1, source_target_pairs={{0,4},{4,0},{1,5},{5,1},{2,6},{6,2},{3,7},{7,3},{8,12},{12,8},{9,1... | collective-permute-start | bytes 196616 | tf_op jit(solution)/shard_map/ppermute | solution.py:558
  10.3 0.6 %collective-permute-done.7.over_y.refs_4_ = bf16[256,256]{1,0:T(8,128)(2,1)S(1)} collective-permute-done((bf16[256,256]{1,0:T(8,128)(2,1)S(1)}, bf16[256,256]{1,0:T(8,128)(2,1)S(1)}, u32[]{:S(2)}, u32[]{:S(2)}) %collective-permute-start.7) | collective-permute-done | bytes 131104 | tf_op jit(solution)/shard_map/ppermute | solution.py:522
  10.9 1.6 %collective-permute-start.8 = (bf16[256,256]{1,0:T(8,128)(2,1)S(1)}, bf16[256,256]{1,0:T(8,128)(2,1)S(1)}, u32[]{:S(2)}, u32[]{:S(2)}) collective-permute-start(bf16[256,256]{1,0:T(8,128)(2,1)S(1)} %collective-permute-done.7.over_y.refs_4_), channel_id=1, source_target_pairs={{0,8},{8,0},{16,24},{24,16},{1,9},{9,1},{17,25},{25,17},{2,10},{10... | collective-permute-start | bytes 393224 | tf_op jit(solution)/shard_map/ppermute | solution.py:553
  12.5 0.1 collective-permute-start.3
  12.6 1.1 %collective-permute-done.6.refs_5_ = bf16[2,128,128]{2,1,0:T(8,128)(2,1)S(1)} collective-permute-done((bf16[2,128,128]{2,1,0:T(8,128)(2,1)S(1)}, bf16[2,128,128]{2,1,0:T(8,128)(2,1)S(1)}, u32[]{:S(2)}, u32[]{:S(2)}) %collective-permute-start.6) | collective-permute-done | bytes 65568 | tf_op jit(solution)/shard_map/ppermute | solution.py:558
  13.6 0.2 collective-permute-done.3.refs_2_
  13.8 1.5 %near.1 = (f32[2,256,256]{2,1,0:T(8,128)S(1)}, f32[2,256,512]{2,1,0:T(8,128)S(1)}, bf16[2,512,256]{2,1,0:T(8,128)(2,1)S(1)}, f32[2,256,256]{2,1,0:T(8,128)S(1)}) custom-call(s32[8,128]{1,0:T(8,128)S(1)} %get-tuple-element.50.spot_ref, bf16[2,128,256]{2,1,0:T(8,128)(2,1)S(1)} %get-tuple-element.52.refs_0_, ...), custom_call_target="tpu_custom_call" | custom-call | flops 33554432 | tf_op jit(solution)/shard_map/near/pallas_call | solution.py:581
  15.3 0.4 %collective-permute-start.11 = (bf16[2,1,256,256]{3,2,1,0:T(8,128)(2,1)S(1)}, bf16[2,1,256,256]{3,2,1,0:T(8,128)(2,1)S(1)}, u32[]{:S(2)}, u32[]{:S(2)}) collective-permute-start(bf16[2,1,256,256]{3,2,1,0:T(8,128)(2,1)S(1)} %collective-permute-done.2.rest.refs_6_), channel_id=1, source_target_pairs={{0,1},{1,0},{2,3},{3,2},{4,5},{5,4},{6,7},{7,6},{8,9},{9,8},{10,11... | collective-permute-start | bytes 786440 | tf_op jit(solution)/shard_map/ppermute | solution.py:522
  15.7 0.9 %core.1 = (f32[2,256,512]{2,1,0:T(8,128)S(1)}, bf16[2,512,256]{2,1,0:T(8,128)(2,1)S(1)}, f32[2,256,256]{2,1,0:T(8,128)S(1)}) custom-call(f32[2,256,256]{2,1,0:T(8,128)S(1)} %get-tuple-element.57.patch_ref.refs_1_, bf16[2,2,256,256]{3,2,1,0:T(8,128)(2,1)S(1)} %collective-permute-done.core.refs_3_, ...), custom_call_target="tpu_custom_call" | custom-call | flops 33554432 | tf_op jit(solution)/shard_map/core/pallas_call | solution.py:591
  16.6 0.0 copy-start.1
  16.6 0.2 collective-permute-start.10
  16.8 0.9 %over.1 = (f32[2,256,512]{2,1,0:T(8,128)S(1)}, bf16[2,512,256]{2,1,0:T(8,128)(2,1)S(1)}, f32[2,256,256]{2,1,0:T(8,128)S(1)}) custom-call(f32[2,256,256]{2,1,0:T(8,128)S(1)} %get-tuple-element.57.patch_ref.refs_1_, bf16[256,256]{1,0:T(8,128)(2,1)S(1)} %collective-permute-done.7.over_y.refs_4_, bf16[256,256]{1,0:T(8,128)(2,1)S(1)} %collective-permute-done.8.over_z.refs_5_, ...), custom_call_target="tpu_custom_call" | custom-call | flops 3355443200 | tf_op jit(solution)/shard_map/over/pallas_call | solution.py:604
  17.7 0.3 collective-permute-done.10.refs_8_
  18.0 4.4 %back.1 = (bf16[256,256]{1,0:T(8,128)(2,1)S(1)}, bf16[256,256]{1,0:T(8,128)(2,1)S(1)}, bf16[256,384]{1,0:T(8,128)(2,1)S(1)}, bf16[256,384]{1,0:T(8,128)(2,1)S(1)}, bf16[272,128]{1,0:T(8,128)(2,1)S(1)}) custom-call(bf16[16,256]{1,0:T(8,128)(2,1)S(1)} %live.1.record_ref, s32[8,128]{1,0:T(8,128)S(1)} %get-tuple-element.50.spot_ref, ...), custom_call_target="tpu_custom_call" | custom-call | flops 2684354560 | tf_op jit(solution)/shard_map/back/pallas_call | solution.py:616
  22.4 0.2 collective-permute-start.13
  22.6 1.6 %collective-permute-start.12 = (bf16[272,128]{1,0:T(8,128)(2,1)S(1)}, bf16[272,128]{1,0:T(8,128)(2,1)S(1)}, u32[]{:S(2)}, u32[]{:S(2)}) collective-permute-start(bf16[272,128]{1,0:T(8,128)(2,1)S(1)} %get-tuple-element.76), channel_id=1, source_target_pairs={{0,4},{4,0},{1,5},{5,1},{2,6},{6,2},{3,7},{7,3},{8,12},{12,8},{9,1... | collective-permute-start | bytes 208904 | tf_op jit(solution)/shard_map/ppermute | solution.py:643
  24.2 0.1 meet.1
  24.3 1.3 %collective-permute-start.14 = (bf16[272,256]{1,0:T(8,128)(2,1)S(1)}, bf16[272,256]{1,0:T(8,128)(2,1)S(1)}, u32[]{:S(2)}, u32[]{:S(2)}) collective-permute-start(bf16[272,256]{1,0:T(8,128)(2,1)S(1)} %get-tuple-element.79), channel_id=1, source_target_pairs={{0,8},{1,0},{2,10},{3,2},{4,12},{5,4},{6,14},{7,6},{8,16},{9,1},{1... | collective-permute-start | bytes 417800 | tf_op jit(solution)/shard_map/ppermute | solution.py:655
  25.5 2.1 %collective-permute-start.15 = (bf16[272,128]{1,0:T(8,128)(2,1)S(1)}, bf16[272,128]{1,0:T(8,128)(2,1)S(1)}, u32[]{:S(2)}, u32[]{:S(2)}) collective-permute-start(bf16[272,128]{1,0:T(8,128)(2,1)S(1)} %get-tuple-element.80), channel_id=1, source_target_pairs={{0,12},{1,4},{2,14},{3,6},{4,8},{5,0},{6,10},{7,2},{8,20},{9,5},{1... | collective-permute-start | bytes 208904 | tf_op jit(solution)/shard_map/ppermute | solution.py:657
  27.6 0.4 %levels.1.level_ref = f32[3,128,256]{2,1,0:T(8,128)S(1)} custom-call(bf16[256,256]{1,0:T(8,128)(2,1)S(1)} %get-tuple-element.74.weight_ref, bf16[16,256]{1,0:T(8,128)(2,1)S(1)} %live.1.record_ref, bf16[256,256]{1,0:T(8,128)(2,1)S(1)} %get-tuple-element.75.own_ref, bf16[272,128]{1,0:T(8,128)(2,1)S(1)} %collective-permute-done.12.refs_0_), custom_call_target="tpu_custom_call" | custom-call | flops 1342177280 | tf_op jit(solution)/shard_map/levels/pallas_call | solution.py:659
  28.0 0.0 copy-start
  28.0 1.5 %collective-permute-done.15.refs_0_ = bf16[272,128]{1,0:T(8,128)(2,1)S(1)} collective-permute-done((bf16[272,128]{1,0:T(8,128)(2,1)S(1)}, bf16[272,128]{1,0:T(8,128)(2,1)S(1)}, u32[]{:S(2)}, u32[]{:S(2)}) %collective-permute-start.15) | collective-permute-done | bytes 69664 | tf_op jit(solution)/shard_map/ppermute | solution.py:657
  29.5 0.5 %sums.1.own_ref = bf16[3,128,256]{2,1,0:T(8,128)(2,1)S(1)} custom-call(bf16[256,256]{1,0:T(8,128)(2,1)S(1)} %get-tuple-element.74.weight_ref, f32[3,128,256]{2,1,0:T(8,128)S(1)} %levels.1.level_ref, bf16[272,256]{1,0:T(8,128)(2,1)S(1)} %collective-permute-done.14.rows_ref, bf16[272,128]{1,0:T(8,128)(2,1)S(1)} %collective-permute-done.15.refs_0_), custom_call_target="tpu_custom_call" | custom-call | tf_op jit(solution)/shard_map/sums/pallas_call | solution.py:668
  30.0 0.4 %collective-permute-start.16 = (bf16[3,128,256]{2,1,0:T(8,128)(2,1)S(1)}, bf16[3,128,256]{2,1,0:T(8,128)(2,1)S(1)}, u32[]{:S(2)}, u32[]{:S(2)}) collective-permute-start(bf16[3,128,256]{2,1,0:T(8,128)(2,1)S(1)} %sums.1.own_ref), channel_id=1, source_target_pairs={{0,1},{1,0},{2,3},{3,2},{4,5},{5,4},{6,7},{7,6},{8,9},{9,8},{10,11... | collective-permute-start | bytes 589832 | tf_op jit(solution)/shard_map/ppermute | solution.py:522
  30.4 1.1 %collective-permute-done.16.other_ref = bf16[3,128,256]{2,1,0:T(8,128)(2,1)S(1)} collective-permute-done((bf16[3,128,256]{2,1,0:T(8,128)(2,1)S(1)}, bf16[3,128,256]{2,1,0:T(8,128)(2,1)S(1)}, u32[]{:S(2)}, u32[]{:S(2)}) %collective-permute-start.16) | collective-permute-done | bytes 196640 | tf_op jit(solution)/shard_map/ppermute | solution.py:522
  31.5 0.8 %update.1 = f32[2,128,256]{2,1,0:T(8,128)} custom-call(f32[2,128,256]{2,1,0:T(8,128)S(1)} %copy-done, bf16[3,128,256]{2,1,0:T(8,128)(2,1)S(1)} %sums.1.own_ref, bf16[3,128,256]{2,1,0:T(8,128)(2,1)S(1)} %collective-permute-done.16.other_ref), custom_call_target="tpu_custom_call" | custom-call | tf_op jit(solution)/shard_map/update/pallas_call | solution.py:676
  (16 shorter events, 0.0 us)
Async XLA Ops:
  1.5 5.1 %collective-permute-start = (bf16[2,2,256,256]{3,2,1,0:T(8,128)(2,1)S(1)}, bf16[2,2,256,256]{3,2,1,0:T(8,128)(2,1)S(1)}, u32[]{:S(2)}, u32[]{:S(2)}) collective-permute-start(bf16[2,2,256,256]{3,2,1,0:T(8,128)(2,1)S(1)} %get-tuple-element.43.refs_6_.refs_2_), channel_id=1, source_target_pairs={{0,1},{1,0},{2,3},{3,2},{4,5},{5,4},{6,7},{7,6},{8,9},{9,8},{10,11... | collective-permute-start | bytes 1572872 | tf_op jit(solution)/shard_map/ppermute | solution.py:522
  2.0 7.1 %collective-permute-start.4 = (bf16[2,128,256]{2,1,0:T(8,128)(2,1)S(1)}, bf16[2,128,256]{2,1,0:T(8,128)(2,1)S(1)}, u32[]{:S(2)}, u32[]{:S(2)}) collective-permute-start(bf16[2,128,256]{2,1,0:T(8,128)(2,1)S(1)} %get-tuple-element.52.refs_0_), channel_id=1, source_target_pairs={{0,8},{1,0},{2,10},{3,2},{4,12},{5,4},{6,14},{7,6},{8,16},{9,1},{1... | collective-permute-start | bytes 393224 | tf_op jit(solution)/shard_map/ppermute | solution.py:555
  4.6 6.3 %collective-permute-start.7 = (bf16[256,256]{1,0:T(8,128)(2,1)S(1)}, bf16[256,256]{1,0:T(8,128)(2,1)S(1)}, u32[]{:S(2)}, u32[]{:S(2)}) collective-permute-start(bf16[256,256]{1,0:T(8,128)(2,1)S(1)} %get-tuple-element.59), channel_id=1, source_target_pairs={{0,2},{1,3},{2,0},{3,1},{4,6},{5,7},{6,4},{7,5},{8,10},{9,11},{10,... | collective-permute-start | bytes 393224 | tf_op jit(solution)/shard_map/ppermute | solution.py:522
  6.1 9.2 %collective-permute-start.2 = (bf16[2,1,256,256]{3,2,1,0:T(8,128)(2,1)S(1)}, bf16[2,1,256,256]{3,2,1,0:T(8,128)(2,1)S(1)}, u32[]{:S(2)}, u32[]{:S(2)}) collective-permute-start(bf16[2,1,256,256]{3,2,1,0:T(8,128)(2,1)S(1)} %get-tuple-element.51), channel_id=1, source_target_pairs={{0,2},{1,3},{2,0},{3,1},{4,6},{5,7},{6,4},{7,5},{8,10},{9,11},{10,... | collective-permute-start | bytes 786440 | tf_op jit(solution)/shard_map/ppermute | solution.py:522
  6.6 5.9 %collective-permute-start.1 = (bf16[2,128,128]{2,1,0:T(8,128)(2,1)S(1)}, bf16[2,128,128]{2,1,0:T(8,128)(2,1)S(1)}, u32[]{:S(2)}, u32[]{:S(2)}) collective-permute-start(bf16[2,128,128]{2,1,0:T(8,128)(2,1)S(1)} %get-tuple-element.45), channel_id=1, source_target_pairs={{0,12},{1,4},{2,14},{3,6},{4,8},{5,0},{6,10},{7,2},{8,20},{9,5},{1... | collective-permute-start | bytes 196616 | tf_op jit(solution)/shard_map/ppermute | solution.py:557
  9.1 4.5 %collective-permute-start.5 = (bf16[2,128,256]{2,1,0:T(8,128)(2,1)S(1)}, bf16[2,128,256]{2,1,0:T(8,128)(2,1)S(1)}, u32[]{:S(2)}, u32[]{:S(2)}) collective-permute-start(bf16[2,128,256]{2,1,0:T(8,128)(2,1)S(1)} %collective-permute-done.4.refs_3_), channel_id=1, source_target_pairs={{0,1},{1,0},{2,3},{3,2},{4,5},{5,4},{6,7},{7,6},{8,9},{9,8},{10,11... | collective-permute-start | bytes 393224 | tf_op jit(solution)/shard_map/ppermute | solution.py:522
  9.1 4.5 %collective-permute-start.6 = (bf16[2,128,128]{2,1,0:T(8,128)(2,1)S(1)}, bf16[2,128,128]{2,1,0:T(8,128)(2,1)S(1)}, u32[]{:S(2)}, u32[]{:S(2)}) collective-permute-start(bf16[2,128,128]{2,1,0:T(8,128)(2,1)S(1)} %get-tuple-element.45), channel_id=1, source_target_pairs={{0,4},{4,0},{1,5},{5,1},{2,6},{6,2},{3,7},{7,3},{8,12},{12,8},{9,1... | collective-permute-start | bytes 196616 | tf_op jit(solution)/shard_map/ppermute | solution.py:558
  10.9 5.7 %collective-permute-start.8 = (bf16[256,256]{1,0:T(8,128)(2,1)S(1)}, bf16[256,256]{1,0:T(8,128)(2,1)S(1)}, u32[]{:S(2)}, u32[]{:S(2)}) collective-permute-start(bf16[256,256]{1,0:T(8,128)(2,1)S(1)} %collective-permute-done.7.over_y.refs_4_), channel_id=1, source_target_pairs={{0,8},{8,0},{16,24},{24,16},{1,9},{9,1},{17,25},{25,17},{2,10},{10... | collective-permute-start | bytes 393224 | tf_op jit(solution)/shard_map/ppermute | solution.py:553
  12.5 1.3 %collective-permute-start.3 = (bf16[2,128,128]{2,1,0:T(8,128)(2,1)S(1)}, bf16[2,128,128]{2,1,0:T(8,128)(2,1)S(1)}, u32[]{:S(2)}, u32[]{:S(2)}) collective-permute-start(bf16[2,128,128]{2,1,0:T(8,128)(2,1)S(1)} %collective-permute-done.1.refs_1_), channel_id=1, source_target_pairs={{0,1},{1,0},{2,3},{3,2},{4,5},{5,4},{6,7},{7,6},{8,9},{9,8},{10,11... | collective-permute-start | bytes 196616 | tf_op jit(solution)/shard_map/ppermute | solution.py:522
  13.6 4.1 %collective-permute-start.9 = (bf16[256,256]{1,0:T(8,128)(2,1)S(1)}, bf16[256,256]{1,0:T(8,128)(2,1)S(1)}, u32[]{:S(2)}, u32[]{:S(2)}) collective-permute-start(bf16[256,256]{1,0:T(8,128)(2,1)S(1)} %collective-permute-done.7.over_y.refs_4_), channel_id=1, source_target_pairs={{0,1},{1,0},{2,3},{3,2},{4,5},{5,4},{6,7},{7,6},{8,9},{9,8},{10,11... | collective-permute-start | bytes 393224 | tf_op jit(solution)/shard_map/ppermute | solution.py:522
  15.3 2.7 %collective-permute-start.11 = (bf16[2,1,256,256]{3,2,1,0:T(8,128)(2,1)S(1)}, bf16[2,1,256,256]{3,2,1,0:T(8,128)(2,1)S(1)}, u32[]{:S(2)}, u32[]{:S(2)}) collective-permute-start(bf16[2,1,256,256]{3,2,1,0:T(8,128)(2,1)S(1)} %collective-permute-done.2.rest.refs_6_), channel_id=1, source_target_pairs={{0,1},{1,0},{2,3},{3,2},{4,5},{5,4},{6,7},{7,6},{8,9},{9,8},{10,11... | collective-permute-start | bytes 786440 | tf_op jit(solution)/shard_map/ppermute | solution.py:522
  16.6 1.4 %copy-start.1 = (bf16[1,1,2,256,256]{4,3,2,1,0:T(8,128)(2,1)S(1)}, bf16[1,1,2,256,256]{4,3,2,1,0:T(8,128)(2,1)}, u32[]{:S(2)}) copy-start(bf16[1,1,2,256,256]{4,3,2,1,0:T(8,128)(2,1)} %refs_0_.1) | copy-start | bytes 786436
  16.6 1.4 %collective-permute-start.10 = (bf16[256,256]{1,0:T(8,128)(2,1)S(1)}, bf16[256,256]{1,0:T(8,128)(2,1)S(1)}, u32[]{:S(2)}, u32[]{:S(2)}) collective-permute-start(bf16[256,256]{1,0:T(8,128)(2,1)S(1)} %collective-permute-done.8.over_z.refs_5_), channel_id=1, source_target_pairs={{0,1},{1,0},{2,3},{3,2},{4,5},{5,4},{6,7},{7,6},{8,9},{9,8},{10,11... | collective-permute-start | bytes 393224 | tf_op jit(solution)/shard_map/ppermute | solution.py:522
  22.4 1.8 %collective-permute-start.13 = (bf16[256,384]{1,0:T(8,128)(2,1)S(1)}, bf16[256,384]{1,0:T(8,128)(2,1)S(1)}, u32[]{:S(2)}, u32[]{:S(2)}) collective-permute-start(bf16[256,384]{1,0:T(8,128)(2,1)S(1)} %get-tuple-element.78), channel_id=1, source_target_pairs={{0,1},{1,0},{2,3},{3,2},{4,5},{5,4},{6,7},{7,6},{8,9},{9,8},{10,11... | collective-permute-start | bytes 589832 | tf_op jit(solution)/shard_map/ppermute | solution.py:522
  22.6 5.0 %collective-permute-start.12 = (bf16[272,128]{1,0:T(8,128)(2,1)S(1)}, bf16[272,128]{1,0:T(8,128)(2,1)S(1)}, u32[]{:S(2)}, u32[]{:S(2)}) collective-permute-start(bf16[272,128]{1,0:T(8,128)(2,1)S(1)} %get-tuple-element.76), channel_id=1, source_target_pairs={{0,4},{4,0},{1,5},{5,1},{2,6},{6,2},{3,7},{7,3},{8,12},{12,8},{9,1... | collective-permute-start | bytes 208904 | tf_op jit(solution)/shard_map/ppermute | solution.py:643
  24.3 5.3 %collective-permute-start.14 = (bf16[272,256]{1,0:T(8,128)(2,1)S(1)}, bf16[272,256]{1,0:T(8,128)(2,1)S(1)}, u32[]{:S(2)}, u32[]{:S(2)}) collective-permute-start(bf16[272,256]{1,0:T(8,128)(2,1)S(1)} %get-tuple-element.79), channel_id=1, source_target_pairs={{0,8},{1,0},{2,10},{3,2},{4,12},{5,4},{6,14},{7,6},{8,16},{9,1},{1... | collective-permute-start | bytes 417800 | tf_op jit(solution)/shard_map/ppermute | solution.py:655
  25.5 4.0 %collective-permute-start.15 = (bf16[272,128]{1,0:T(8,128)(2,1)S(1)}, bf16[272,128]{1,0:T(8,128)(2,1)S(1)}, u32[]{:S(2)}, u32[]{:S(2)}) collective-permute-start(bf16[272,128]{1,0:T(8,128)(2,1)S(1)} %get-tuple-element.80), channel_id=1, source_target_pairs={{0,12},{1,4},{2,14},{3,6},{4,8},{5,0},{6,10},{7,2},{8,20},{9,5},{1... | collective-permute-start | bytes 208904 | tf_op jit(solution)/shard_map/ppermute | solution.py:657
  28.0 3.5 %copy-start = (f32[2,128,256]{2,1,0:T(8,128)S(1)}, f32[2,128,256]{2,1,0:T(8,128)}, u32[]{:S(2)}) copy-start(f32[2,128,256]{2,1,0:T(8,128)} %object_ref.1) | copy-start | bytes 786436
  30.0 1.5 %collective-permute-start.16 = (bf16[3,128,256]{2,1,0:T(8,128)(2,1)S(1)}, bf16[3,128,256]{2,1,0:T(8,128)(2,1)S(1)}, u32[]{:S(2)}, u32[]{:S(2)}) collective-permute-start(bf16[3,128,256]{2,1,0:T(8,128)(2,1)S(1)} %sums.1.own_ref), channel_id=1, source_target_pairs={{0,1},{1,0},{2,3},{3,2},{4,5},{5,4},{6,7},{7,6},{8,9},{9,8},{10,11... | collective-permute-start | bytes 589832 | tf_op jit(solution)/shard_map/ppermute | solution.py:522

commit v20 on v19

--- a/solution.py
+++ b/solution.py
@@ -556,6 +556,7 @@
     probe_core, *corner_edges = lax.optimization_barrier((probe_core, *packed[1:]))
     corners = [lax.ppermute(edge, axes, zigzag(step)) for step, edge in zip(x_steps, corner_edges)]
     levels = [lax.ppermute(edge, "ty", level(step)) for step, edge in zip(x_steps, packed[1:])]
+    rows, levels = lax.optimization_barrier((rows, levels))
     corners, record = lax.optimization_barrier((corners, record))
     record = pl.pallas_call(
         functools.partial(live_kernel, slots),

time: 32.4 us -> 33.7 us (1.040)
  starting transfers between devices: 16 us -> 16.8 us
  waiting for transfers between devices: 4.8 us -> 5.31 us
    ppermute x1, starting transfers between devices: 2.5 us -> 1.55 us  [on_device(): lax.ppermute(edge, axes, zigzag(step))]
    ppermute x1, starting transfers between devices: 0.54 us -> 1.49 us  [on_device(): lax.ppermute(edge, 'ty', level(step))]
    ppermute x1, waiting for transfers between devices: 1.06 us -> 1.44 us  [on_device(): lax.ppermute(edge, 'ty', level(step))]
    ppermute x10, starting transfers between devices: 3.85 us -> 4.22 us  [exchange(): return lax.ppermute(array, 'mode', [(m, m ^ flip) for m in range(m_count)])]
where the time goes in v20:
time: 33.7 us; the launch traced here: 33.6 us
  starting transfers between devices  16.8 us (50%)
  Pallas kernels  10.7 us (32%)
  waiting for transfers between devices  5.31 us (16%)
  between operations  0.76 us (2%)
    pallas_call x1, Pallas kernels, on_device(): pl.pallas_call(functools.partial(back_kernel, sides, slots, tile_cols), o...  4.36 us
    ppermute x10, starting transfers between devices, exchange(): return lax.ppermute(array, 'mode', [(m, m ^ flip) for m in range(m_count)])  4.22 us
    ppermute x1, starting transfers between devices, on_device(): rows = lax.ppermute(packed[0], axes, zigzag(0))  2.6 us
    ppermute x1, starting transfers between devices, on_device(): lax.ppermute(piece, axes, zigzag(-step))  2.15 us
    ppermute x10, waiting for transfers between devices, exchange(): return lax.ppermute(array, 'mode', [(m, m ^ flip) for m in range(m_count)])  2.13 us
    ppermute x1, starting transfers between devices, on_device(): lax.ppermute(piece, 'ty', level(-step))  1.94 us
    ppermute x1, starting transfers between devices, on_device(): over_z = lax.ppermute(over_y, 'tx', [(z, z ^ 1) for z in range(z_count)])  1.78 us
    ppermute x1, starting transfers between devices, on_device(): lax.ppermute(edge, axes, zigzag(step))  1.55 us
  transfers between devices with their start and end apart: 17, of which 6 were waited for; matrix products, arithmetic and copies ran while one was open for 0% of the time, Pallas kernels for 11%

profile of v20, /device:TPU:0, one launch (start us, length us, event | category | flops | bytes accessed | tf_op | source)
XLA Modules:
  0.0 33.6 jit_solution(3656750000057935631)
XLA Ops:
  0.0 1.4 %start.1 = (bf16[2,2,256,256]{3,2,1,0:T(8,128)(2,1)S(1)}, bf16[256,256]{1,0:T(8,128)(2,1)S(1)}, bf16[2,1,256,256]{3,2,1,0:T(8,128)(2,1)S(1)}, bf16[16,256]{1,0:T...) custom-call(f32[2,128,256]{2,1,0:T(8,128)} %object_ref.1, ...), custom_call_target="tpu_custom_call" | custom-call | tf_op jit(solution)/shard_map/start/pallas_call | solution.py:525
  1.5 0.5 %collective-permute-start = (bf16[2,2,256,256]{3,2,1,0:T(8,128)(2,1)S(1)}, bf16[2,2,256,256]{3,2,1,0:T(8,128)(2,1)S(1)}, u32[]{:S(2)}, u32[]{:S(2)}) collective-permute-start(bf16[2,2,256,256]{3,2,1,0:T(8,128)(2,1)S(1)} %get-tuple-element.45.refs_6_.refs_2_), channel_id=1, source_target_pairs={{0,1},{1,0},{2,3},{3,2},{4,5},{5,4},{6,7},{7,6},{8,9},{9,8},{10,11... | collective-permute-start | bytes 1572872 | tf_op jit(solution)/shard_map/ppermute | solution.py:522
  2.0 2.6 %collective-permute-start.4 = (bf16[2,128,256]{2,1,0:T(8,128)(2,1)S(1)}, bf16[2,128,256]{2,1,0:T(8,128)(2,1)S(1)}, u32[]{:S(2)}, u32[]{:S(2)}) collective-permute-start(bf16[2,128,256]{2,1,0:T(8,128)(2,1)S(1)} %get-tuple-element.54.refs_0_), channel_id=1, source_target_pairs={{0,8},{1,0},{2,10},{3,2},{4,12},{5,4},{6,14},{7,6},{8,16},{9,1},{1... | collective-permute-start | bytes 393224 | tf_op jit(solution)/shard_map/ppermute | solution.py:555
  4.6 1.5 %collective-permute-start.7 = (bf16[256,256]{1,0:T(8,128)(2,1)S(1)}, bf16[256,256]{1,0:T(8,128)(2,1)S(1)}, u32[]{:S(2)}, u32[]{:S(2)}) collective-permute-start(bf16[256,256]{1,0:T(8,128)(2,1)S(1)} %get-tuple-element.63), channel_id=1, source_target_pairs={{0,2},{1,3},{2,0},{3,1},{4,6},{5,7},{6,4},{7,5},{8,10},{9,11},{10,... | collective-permute-start | bytes 393224 | tf_op jit(solution)/shard_map/ppermute | solution.py:522
  6.1 0.5 %collective-permute-start.2 = (bf16[2,1,256,256]{3,2,1,0:T(8,128)(2,1)S(1)}, bf16[2,1,256,256]{3,2,1,0:T(8,128)(2,1)S(1)}, u32[]{:S(2)}, u32[]{:S(2)}) collective-permute-start(bf16[2,1,256,256]{3,2,1,0:T(8,128)(2,1)S(1)} %get-tuple-element.53), channel_id=1, source_target_pairs={{0,2},{1,3},{2,0},{3,1},{4,6},{5,7},{6,4},{7,5},{8,10},{9,11},{10,... | collective-permute-start | bytes 786440 | tf_op jit(solution)/shard_map/ppermute | solution.py:522
  6.6 1.5 %collective-permute-start.5 = (bf16[2,128,128]{2,1,0:T(8,128)(2,1)S(1)}, bf16[2,128,128]{2,1,0:T(8,128)(2,1)S(1)}, u32[]{:S(2)}, u32[]{:S(2)}) collective-permute-start(bf16[2,128,128]{2,1,0:T(8,128)(2,1)S(1)} %get-tuple-element.47), channel_id=1, source_target_pairs={{0,4},{4,0},{1,5},{5,1},{2,6},{6,2},{3,7},{7,3},{8,12},{12,8},{9,1... | collective-permute-start | bytes 196616 | tf_op jit(solution)/shard_map/ppermute | solution.py:558
  8.1 1.5 %collective-permute-start.1 = (bf16[2,128,128]{2,1,0:T(8,128)(2,1)S(1)}, bf16[2,128,128]{2,1,0:T(8,128)(2,1)S(1)}, u32[]{:S(2)}, u32[]{:S(2)}) collective-permute-start(bf16[2,128,128]{2,1,0:T(8,128)(2,1)S(1)} %get-tuple-element.47), channel_id=1, source_target_pairs={{0,12},{1,4},{2,14},{3,6},{4,8},{5,0},{6,10},{7,2},{8,20},{9,5},{1... | collective-permute-start | bytes 196616 | tf_op jit(solution)/shard_map/ppermute | solution.py:557
  9.6 1.4 %collective-permute-done.5.refs_5_ = bf16[2,128,128]{2,1,0:T(8,128)(2,1)S(1)} collective-permute-done((bf16[2,128,128]{2,1,0:T(8,128)(2,1)S(1)}, bf16[2,128,128]{2,1,0:T(8,128)(2,1)S(1)}, u32[]{:S(2)}, u32[]{:S(2)}) %collective-permute-start.5) | collective-permute-done | bytes 65568 | tf_op jit(solution)/shard_map/ppermute | solution.py:558
  11.8 1.8 %collective-permute-start.8 = (bf16[256,256]{1,0:T(8,128)(2,1)S(1)}, bf16[256,256]{1,0:T(8,128)(2,1)S(1)}, u32[]{:S(2)}, u32[]{:S(2)}) collective-permute-start(bf16[256,256]{1,0:T(8,128)(2,1)S(1)} %collective-permute-done.7.over_y.refs_4_), channel_id=1, source_target_pairs={{0,8},{8,0},{16,24},{24,16},{1,9},{9,1},{17,25},{25,17},{2,10},{10... | collective-permute-start | bytes 393224 | tf_op jit(solution)/shard_map/ppermute | solution.py:553
  13.5 0.3 collective-permute-start.3
  13.8 0.3 collective-permute-start.9
  14.1 0.7 %collective-permute-done.3.refs_2_ = bf16[2,128,128]{2,1,0:T(8,128)(2,1)S(1)} collective-permute-done((bf16[2,128,128]{2,1,0:T(8,128)(2,1)S(1)}, bf16[2,128,128]{2,1,0:T(8,128)(2,1)S(1)}, u32[]{:S(2)}, u32[]{:S(2)}) %collective-permute-start.3) | collective-permute-done | bytes 65568 | tf_op jit(solution)/shard_map/ppermute | solution.py:522
  14.9 1.5 %near.1 = (f32[2,256,256]{2,1,0:T(8,128)S(1)}, f32[2,256,512]{2,1,0:T(8,128)S(1)}, bf16[2,512,256]{2,1,0:T(8,128)(2,1)S(1)}, f32[2,256,256]{2,1,0:T(8,128)S(1)}) custom-call(s32[8,128]{1,0:T(8,128)S(1)} %get-tuple-element.52.spot_ref, bf16[2,128,256]{2,1,0:T(8,128)(2,1)S(1)} %get-tuple-element.54.refs_0_, ...), custom_call_target="tpu_custom_call" | custom-call | flops 33554432 | tf_op jit(solution)/shard_map/near/pallas_call | solution.py:582
  16.4 0.3 collective-permute-start.11
  16.7 0.9 %core.1 = (f32[2,256,512]{2,1,0:T(8,128)S(1)}, bf16[2,512,256]{2,1,0:T(8,128)(2,1)S(1)}, f32[2,256,256]{2,1,0:T(8,128)S(1)}) custom-call(f32[2,256,256]{2,1,0:T(8,128)S(1)} %get-tuple-element.61.patch_ref.refs_1_, bf16[2,2,256,256]{3,2,1,0:T(8,128)(2,1)S(1)} %collective-permute-done.core.refs_3_, ...), custom_call_target="tpu_custom_call" | custom-call | flops 33554432 | tf_op jit(solution)/shard_map/core/pallas_call | solution.py:592
  17.5 0.2 collective-permute-done.8.over_z.refs_5_
  17.7 0.2 collective-permute-start.10
  17.9 0.9 %over.1 = (f32[2,256,512]{2,1,0:T(8,128)S(1)}, bf16[2,512,256]{2,1,0:T(8,128)(2,1)S(1)}, f32[2,256,256]{2,1,0:T(8,128)S(1)}) custom-call(f32[2,256,256]{2,1,0:T(8,128)S(1)} %get-tuple-element.61.patch_ref.refs_1_, bf16[256,256]{1,0:T(8,128)(2,1)S(1)} %collective-permute-done.7.over_y.refs_4_, bf16[256,256]{1,0:T(8,128)(2,1)S(1)} %collective-permute-done.8.over_z.refs_5_, ...), custom_call_target="tpu_custom_call" | custom-call | flops 3355443200 | tf_op jit(solution)/shard_map/over/pallas_call | solution.py:605
  18.8 0.3 collective-permute-done.10.refs_8_
  19.1 4.4 %back.1 = (bf16[256,256]{1,0:T(8,128)(2,1)S(1)}, bf16[256,256]{1,0:T(8,128)(2,1)S(1)}, bf16[256,384]{1,0:T(8,128)(2,1)S(1)}, bf16[256,384]{1,0:T(8,128)(2,1)S(1)}, bf16[272,128]{1,0:T(8,128)(2,1)S(1)}) custom-call(bf16[16,256]{1,0:T(8,128)(2,1)S(1)} %live.1.record_ref, s32[8,128]{1,0:T(8,128)S(1)} %get-tuple-element.52.spot_ref, ...), custom_call_target="tpu_custom_call" | custom-call | flops 2684354560 | tf_op jit(solution)/shard_map/back/pallas_call | solution.py:617
  23.5 0.2 collective-permute-start.13
  23.7 1.9 %collective-permute-start.12 = (bf16[272,128]{1,0:T(8,128)(2,1)S(1)}, bf16[272,128]{1,0:T(8,128)(2,1)S(1)}, u32[]{:S(2)}, u32[]{:S(2)}) collective-permute-start(bf16[272,128]{1,0:T(8,128)(2,1)S(1)} %get-tuple-element.80), channel_id=1, source_target_pairs={{0,4},{4,0},{1,5},{5,1},{2,6},{6,2},{3,7},{7,3},{8,12},{12,8},{9,1... | collective-permute-start | bytes 208904 | tf_op jit(solution)/shard_map/ppermute | solution.py:644
  25.6 0.1 meet.1
  25.7 1.1 %collective-permute-start.14 = (bf16[272,256]{1,0:T(8,128)(2,1)S(1)}, bf16[272,256]{1,0:T(8,128)(2,1)S(1)}, u32[]{:S(2)}, u32[]{:S(2)}) collective-permute-start(bf16[272,256]{1,0:T(8,128)(2,1)S(1)} %get-tuple-element.83), channel_id=1, source_target_pairs={{0,8},{1,0},{2,10},{3,2},{4,12},{5,4},{6,14},{7,6},{8,16},{9,1},{1... | collective-permute-start | bytes 417800 | tf_op jit(solution)/shard_map/ppermute | solution.py:656
  26.7 2.1 %collective-permute-start.15 = (bf16[272,128]{1,0:T(8,128)(2,1)S(1)}, bf16[272,128]{1,0:T(8,128)(2,1)S(1)}, u32[]{:S(2)}, u32[]{:S(2)}) collective-permute-start(bf16[272,128]{1,0:T(8,128)(2,1)S(1)} %get-tuple-element.84), channel_id=1, source_target_pairs={{0,12},{1,4},{2,14},{3,6},{4,8},{5,0},{6,10},{7,2},{8,20},{9,5},{1... | collective-permute-start | bytes 208904 | tf_op jit(solution)/shard_map/ppermute | solution.py:658
  28.9 0.4 %levels.1.level_ref = f32[3,128,256]{2,1,0:T(8,128)S(1)} custom-call(bf16[256,256]{1,0:T(8,128)(2,1)S(1)} %get-tuple-element.78.weight_ref, bf16[16,256]{1,0:T(8,128)(2,1)S(1)} %live.1.record_ref, bf16[256,256]{1,0:T(8,128)(2,1)S(1)} %get-tuple-element.79.own_ref, bf16[272,128]{1,0:T(8,128)(2,1)S(1)} %collective-permute-done.12.refs_0_), custom_call_target="tpu_custom_call" | custom-call | flops 1342177280 | tf_op jit(solution)/shard_map/levels/pallas_call | solution.py:660
  29.3 0.0 copy-start
  29.3 1.5 %collective-permute-done.15.refs_0_ = bf16[272,128]{1,0:T(8,128)(2,1)S(1)} collective-permute-done((bf16[272,128]{1,0:T(8,128)(2,1)S(1)}, bf16[272,128]{1,0:T(8,128)(2,1)S(1)}, u32[]{:S(2)}, u32[]{:S(2)}) %collective-permute-start.15) | collective-permute-done | bytes 69664 | tf_op jit(solution)/shard_map/ppermute | solution.py:658
  30.8 0.5 %sums.1.own_ref = bf16[3,128,256]{2,1,0:T(8,128)(2,1)S(1)} custom-call(bf16[256,256]{1,0:T(8,128)(2,1)S(1)} %get-tuple-element.78.weight_ref, f32[3,128,256]{2,1,0:T(8,128)S(1)} %levels.1.level_ref, bf16[272,256]{1,0:T(8,128)(2,1)S(1)} %collective-permute-done.14.rows_ref, bf16[272,128]{1,0:T(8,128)(2,1)S(1)} %collective-permute-done.15.refs_0_), custom_call_target="tpu_custom_call" | custom-call | tf_op jit(solution)/shard_map/sums/pallas_call | solution.py:669
  31.3 0.4 %collective-permute-start.16 = (bf16[3,128,256]{2,1,0:T(8,128)(2,1)S(1)}, bf16[3,128,256]{2,1,0:T(8,128)(2,1)S(1)}, u32[]{:S(2)}, u32[]{:S(2)}) collective-permute-start(bf16[3,128,256]{2,1,0:T(8,128)(2,1)S(1)} %sums.1.own_ref), channel_id=1, source_target_pairs={{0,1},{1,0},{2,3},{3,2},{4,5},{5,4},{6,7},{7,6},{8,9},{9,8},{10,11... | collective-permute-start | bytes 589832 | tf_op jit(solution)/shard_map/ppermute | solution.py:522
  31.7 1.1 %collective-permute-done.16.other_ref = bf16[3,128,256]{2,1,0:T(8,128)(2,1)S(1)} collective-permute-done((bf16[3,128,256]{2,1,0:T(8,128)(2,1)S(1)}, bf16[3,128,256]{2,1,0:T(8,128)(2,1)S(1)}, u32[]{:S(2)}, u32[]{:S(2)}) %collective-permute-start.16) | collective-permute-done | bytes 196640 | tf_op jit(solution)/shard_map/ppermute | solution.py:522
  32.8 0.8 %update.1 = f32[2,128,256]{2,1,0:T(8,128)} custom-call(f32[2,128,256]{2,1,0:T(8,128)S(1)} %copy-done, bf16[3,128,256]{2,1,0:T(8,128)(2,1)S(1)} %sums.1.own_ref, bf16[3,128,256]{2,1,0:T(8,128)(2,1)S(1)} %collective-permute-done.16.other_ref), custom_call_target="tpu_custom_call" | custom-call | tf_op jit(solution)/shard_map/update/pallas_call | solution.py:677
  (16 shorter events, 0.0 us)
Async XLA Ops:
  1.5 6.6 %collective-permute-start = (bf16[2,2,256,256]{3,2,1,0:T(8,128)(2,1)S(1)}, bf16[2,2,256,256]{3,2,1,0:T(8,128)(2,1)S(1)}, u32[]{:S(2)}, u32[]{:S(2)}) collective-permute-start(bf16[2,2,256,256]{3,2,1,0:T(8,128)(2,1)S(1)} %get-tuple-element.45.refs_6_.refs_2_), channel_id=1, source_target_pairs={{0,1},{1,0},{2,3},{3,2},{4,5},{5,4},{6,7},{7,6},{8,9},{9,8},{10,11... | collective-permute-start | bytes 1572872 | tf_op jit(solution)/shard_map/ppermute | solution.py:522
  2.0 9.1 %collective-permute-start.4 = (bf16[2,128,256]{2,1,0:T(8,128)(2,1)S(1)}, bf16[2,128,256]{2,1,0:T(8,128)(2,1)S(1)}, u32[]{:S(2)}, u32[]{:S(2)}) collective-permute-start(bf16[2,128,256]{2,1,0:T(8,128)(2,1)S(1)} %get-tuple-element.54.refs_0_), channel_id=1, source_target_pairs={{0,8},{1,0},{2,10},{3,2},{4,12},{5,4},{6,14},{7,6},{8,16},{9,1},{1... | collective-permute-start | bytes 393224 | tf_op jit(solution)/shard_map/ppermute | solution.py:555
  4.6 7.2 %collective-permute-start.7 = (bf16[256,256]{1,0:T(8,128)(2,1)S(1)}, bf16[256,256]{1,0:T(8,128)(2,1)S(1)}, u32[]{:S(2)}, u32[]{:S(2)}) collective-permute-start(bf16[256,256]{1,0:T(8,128)(2,1)S(1)} %get-tuple-element.63), channel_id=1, source_target_pairs={{0,2},{1,3},{2,0},{3,1},{4,6},{5,7},{6,4},{7,5},{8,10},{9,11},{10,... | collective-permute-start | bytes 393224 | tf_op jit(solution)/shard_map/ppermute | solution.py:522
  6.1 10.3 %collective-permute-start.2 = (bf16[2,1,256,256]{3,2,1,0:T(8,128)(2,1)S(1)}, bf16[2,1,256,256]{3,2,1,0:T(8,128)(2,1)S(1)}, u32[]{:S(2)}, u32[]{:S(2)}) collective-permute-start(bf16[2,1,256,256]{3,2,1,0:T(8,128)(2,1)S(1)} %get-tuple-element.53), channel_id=1, source_target_pairs={{0,2},{1,3},{2,0},{3,1},{4,6},{5,7},{6,4},{7,5},{8,10},{9,11},{10,... | collective-permute-start | bytes 786440 | tf_op jit(solution)/shard_map/ppermute | solution.py:522
  6.6 4.5 %collective-permute-start.5 = (bf16[2,128,128]{2,1,0:T(8,128)(2,1)S(1)}, bf16[2,128,128]{2,1,0:T(8,128)(2,1)S(1)}, u32[]{:S(2)}, u32[]{:S(2)}) collective-permute-start(bf16[2,128,128]{2,1,0:T(8,128)(2,1)S(1)} %get-tuple-element.47), channel_id=1, source_target_pairs={{0,4},{4,0},{1,5},{5,1},{2,6},{6,2},{3,7},{7,3},{8,12},{12,8},{9,1... | collective-permute-start | bytes 196616 | tf_op jit(solution)/shard_map/ppermute | solution.py:558
  8.1 5.4 %collective-permute-start.1 = (bf16[2,128,128]{2,1,0:T(8,128)(2,1)S(1)}, bf16[2,128,128]{2,1,0:T(8,128)(2,1)S(1)}, u32[]{:S(2)}, u32[]{:S(2)}) collective-permute-start(bf16[2,128,128]{2,1,0:T(8,128)(2,1)S(1)} %get-tuple-element.47), channel_id=1, source_target_pairs={{0,12},{1,4},{2,14},{3,6},{4,8},{5,0},{6,10},{7,2},{8,20},{9,5},{1... | collective-permute-start | bytes 196616 | tf_op jit(solution)/shard_map/ppermute | solution.py:557
  11.1 3.0 %collective-permute-start.6 = (bf16[2,128,256]{2,1,0:T(8,128)(2,1)S(1)}, bf16[2,128,256]{2,1,0:T(8,128)(2,1)S(1)}, u32[]{:S(2)}, u32[]{:S(2)}) collective-permute-start(bf16[2,128,256]{2,1,0:T(8,128)(2,1)S(1)} %collective-permute-done.4.refs_3_), channel_id=1, source_target_pairs={{0,1},{1,0},{2,3},{3,2},{4,5},{5,4},{6,7},{7,6},{8,9},{9,8},{10,11... | collective-permute-start | bytes 393224 | tf_op jit(solution)/shard_map/ppermute | solution.py:522
  11.8 6.0 %collective-permute-start.8 = (bf16[256,256]{1,0:T(8,128)(2,1)S(1)}, bf16[256,256]{1,0:T(8,128)(2,1)S(1)}, u32[]{:S(2)}, u32[]{:S(2)}) collective-permute-start(bf16[256,256]{1,0:T(8,128)(2,1)S(1)} %collective-permute-done.7.over_y.refs_4_), channel_id=1, source_target_pairs={{0,8},{8,0},{16,24},{24,16},{1,9},{9,1},{17,25},{25,17},{2,10},{10... | collective-permute-start | bytes 393224 | tf_op jit(solution)/shard_map/ppermute | solution.py:553
  13.5 1.3 %collective-permute-start.3 = (bf16[2,128,128]{2,1,0:T(8,128)(2,1)S(1)}, bf16[2,128,128]{2,1,0:T(8,128)(2,1)S(1)}, u32[]{:S(2)}, u32[]{:S(2)}) collective-permute-start(bf16[2,128,128]{2,1,0:T(8,128)(2,1)S(1)} %collective-permute-done.1.refs_1_), channel_id=1, source_target_pairs={{0,1},{1,0},{2,3},{3,2},{4,5},{5,4},{6,7},{7,6},{8,9},{9,8},{10,11... | collective-permute-start | bytes 196616 | tf_op jit(solution)/shard_map/ppermute | solution.py:522
  13.8 4.9 %collective-permute-start.9 = (bf16[256,256]{1,0:T(8,128)(2,1)S(1)}, bf16[256,256]{1,0:T(8,128)(2,1)S(1)}, u32[]{:S(2)}, u32[]{:S(2)}) collective-permute-start(bf16[256,256]{1,0:T(8,128)(2,1)S(1)} %collective-permute-done.7.over_y.refs_4_), channel_id=1, source_target_pairs={{0,1},{1,0},{2,3},{3,2},{4,5},{5,4},{6,7},{7,6},{8,9},{9,8},{10,11... | collective-permute-start | bytes 393224 | tf_op jit(solution)/shard_map/ppermute | solution.py:522
  16.4 2.7 %collective-permute-start.11 = (bf16[2,1,256,256]{3,2,1,0:T(8,128)(2,1)S(1)}, bf16[2,1,256,256]{3,2,1,0:T(8,128)(2,1)S(1)}, u32[]{:S(2)}, u32[]{:S(2)}) collective-permute-start(bf16[2,1,256,256]{3,2,1,0:T(8,128)(2,1)S(1)} %collective-permute-done.2.rest.refs_6_), channel_id=1, source_target_pairs={{0,1},{1,0},{2,3},{3,2},{4,5},{5,4},{6,7},{7,6},{8,9},{9,8},{10,11... | collective-permute-start | bytes 786440 | tf_op jit(solution)/shard_map/ppermute | solution.py:522
  17.7 1.4 %copy-start.1 = (bf16[1,1,2,256,256]{4,3,2,1,0:T(8,128)(2,1)S(1)}, bf16[1,1,2,256,256]{4,3,2,1,0:T(8,128)(2,1)}, u32[]{:S(2)}) copy-start(bf16[1,1,2,256,256]{4,3,2,1,0:T(8,128)(2,1)} %refs_0_.1) | copy-start | bytes 786436
  17.7 1.3 %collective-permute-start.10 = (bf16[256,256]{1,0:T(8,128)(2,1)S(1)}, bf16[256,256]{1,0:T(8,128)(2,1)S(1)}, u32[]{:S(2)}, u32[]{:S(2)}) collective-permute-start(bf16[256,256]{1,0:T(8,128)(2,1)S(1)} %collective-permute-done.8.over_z.refs_5_), channel_id=1, source_target_pairs={{0,1},{1,0},{2,3},{3,2},{4,5},{5,4},{6,7},{7,6},{8,9},{9,8},{10,11... | collective-permute-start | bytes 393224 | tf_op jit(solution)/shard_map/ppermute | solution.py:522
  23.5 2.2 %collective-permute-start.13 = (bf16[256,384]{1,0:T(8,128)(2,1)S(1)}, bf16[256,384]{1,0:T(8,128)(2,1)S(1)}, u32[]{:S(2)}, u32[]{:S(2)}) collective-permute-start(bf16[256,384]{1,0:T(8,128)(2,1)S(1)} %get-tuple-element.82), channel_id=1, source_target_pairs={{0,1},{1,0},{2,3},{3,2},{4,5},{5,4},{6,7},{7,6},{8,9},{9,8},{10,11... | collective-permute-start | bytes 589832 | tf_op jit(solution)/shard_map/ppermute | solution.py:522
  23.7 5.2 %collective-permute-start.12 = (bf16[272,128]{1,0:T(8,128)(2,1)S(1)}, bf16[272,128]{1,0:T(8,128)(2,1)S(1)}, u32[]{:S(2)}, u32[]{:S(2)}) collective-permute-start(bf16[272,128]{1,0:T(8,128)(2,1)S(1)} %get-tuple-element.80), channel_id=1, source_target_pairs={{0,4},{4,0},{1,5},{5,1},{2,6},{6,2},{3,7},{7,3},{8,12},{12,8},{9,1... | collective-permute-start | bytes 208904 | tf_op jit(solution)/shard_map/ppermute | solution.py:644
  25.7 5.2 %collective-permute-start.14 = (bf16[272,256]{1,0:T(8,128)(2,1)S(1)}, bf16[272,256]{1,0:T(8,128)(2,1)S(1)}, u32[]{:S(2)}, u32[]{:S(2)}) collective-permute-start(bf16[272,256]{1,0:T(8,128)(2,1)S(1)} %get-tuple-element.83), channel_id=1, source_target_pairs={{0,8},{1,0},{2,10},{3,2},{4,12},{5,4},{6,14},{7,6},{8,16},{9,1},{1... | collective-permute-start | bytes 417800 | tf_op jit(solution)/shard_map/ppermute | solution.py:656
  26.7 4.1 %collective-permute-start.15 = (bf16[272,128]{1,0:T(8,128)(2,1)S(1)}, bf16[272,128]{1,0:T(8,128)(2,1)S(1)}, u32[]{:S(2)}, u32[]{:S(2)}) collective-permute-start(bf16[272,128]{1,0:T(8,128)(2,1)S(1)} %get-tuple-element.84), channel_id=1, source_target_pairs={{0,12},{1,4},{2,14},{3,6},{4,8},{5,0},{6,10},{7,2},{8,20},{9,5},{1... | collective-permute-start | bytes 208904 | tf_op jit(solution)/shard_map/ppermute | solution.py:658
  29.3 3.5 %copy-start = (f32[2,128,256]{2,1,0:T(8,128)S(1)}, f32[2,128,256]{2,1,0:T(8,128)}, u32[]{:S(2)}) copy-start(f32[2,128,256]{2,1,0:T(8,128)} %object_ref.1) | copy-start | bytes 786436
  31.3 1.5 %collective-permute-start.16 = (bf16[3,128,256]{2,1,0:T(8,128)(2,1)S(1)}, bf16[3,128,256]{2,1,0:T(8,128)(2,1)S(1)}, u32[]{:S(2)}, u32[]{:S(2)}) collective-permute-start(bf16[3,128,256]{2,1,0:T(8,128)(2,1)S(1)} %sums.1.own_ref), channel_id=1, source_target_pairs={{0,1},{1,0},{2,3},{3,2},{4,5},{5,4},{6,7},{7,6},{8,9},{9,8},{10,11... | collective-permute-start | bytes 589832 | tf_op jit(solution)/shard_map/ppermute | solution.py:522
